TPU v7x, 512 devices: a whole 4x8x8 slice. The times are simulated.
512 devices in a mesh: aux: 64 (over x, z, core), pair: 8 (over y).
Axes of the slice: x: 4, y: 8, z: 8, core: 2. Of those that a mesh axis runs over, the one named last changes fastest.
Arguments:
- three_index: bfloat16 [57344, 2048], P('aux', 'pair'), may hold values from -0.1875 to 0.1875
- occupied_energy: float32 [64], replicated, may hold values from -2 to -0.3
- virtual_energy: float32 [20096], replicated, may hold values from 0.5 to 4
- tile_occupied: int32 [16], replicated, may hold values from 0 to 63
- tile_virtual: int32 [16], replicated, may hold values from 0 to 156
- tile_exponent: int32 [16], replicated, may hold values from -1 to 1
Outputs:
- gamma_terms: bfloat16 [57344, 2048], P('aux', 'pair')
All inputs are finite; a program needn't handle non-finite values.
Results may differ from a plain program's by a relative error of at most 0.0048.
Values may be sent and summed in bfloat16 or wider, within the bound.
No kernel may reach another device: no remote copies, remote signals or barrier semaphores. Data moves between devices by JAX's collectives and lax.ppermute only.
A program may use at most 64 MiB of HBM per device.

v0:
```python
import jax
import jax.numpy as jnp
from jax import lax
from jax.sharding import PartitionSpec as P

TS = 128
VT = 157


def column_scale(tile_exponent):
    factor = jnp.where(tile_exponent == -1, 0.5, jnp.where(tile_exponent == 1, 2.0, 1.0)).astype(
        jnp.float32
    )
    return jnp.repeat(factor, TS)


def column_energy(occupied_energy, virtual_energy, tile_occupied, tile_virtual):
    virtual_cols = virtual_energy.reshape(VT, TS)[tile_virtual].reshape(-1)
    occupied_cols = jnp.repeat(occupied_energy[tile_occupied], TS)
    return virtual_cols - occupied_cols


def make_amplitude(coulomb, row_energy, row_scale, own_energy, own_scale):
    return (
        coulomb
        * (row_scale * row_scale)[:, None]
        * own_scale[None, :]
        / (row_energy[:, None] + own_energy[None, :])
    ).astype(jnp.bfloat16)


def body(three_index, occupied_energy, virtual_energy, tile_occupied, tile_virtual, tile_exponent):
    width_local = three_index.shape[1]
    col_scale = column_scale(tile_exponent)
    col_energy = column_energy(occupied_energy, virtual_energy, tile_occupied, tile_virtual)
    offset = lax.axis_index("pair") * width_local
    own_energy = lax.dynamic_slice_in_dim(col_energy, offset, width_local)
    own_scale = lax.dynamic_slice_in_dim(col_scale, offset, width_local)
    contract = (((0,), (0,)), ((), ()))
    gathered = lax.all_gather(three_index, "pair", axis=1, tiled=True)
    coulomb = lax.dot_general(gathered, three_index, contract, preferred_element_type=jnp.float32)
    summed = lax.psum(coulomb, "aux")
    amplitude = make_amplitude(summed, col_energy, col_scale, own_energy, own_scale)
    result = jnp.dot(gathered, amplitude, preferred_element_type=jnp.float32)
    return result.astype(jnp.bfloat16)


def solution(mesh):
    placed = (P("aux", "pair"), P(), P(), P(), P(), P())
    return jax.shard_map(
        body, mesh=mesh, in_specs=placed, out_specs=P("aux", "pair"), check_vma=False
    )
```

profile of v0, /device:TPU:1, one launch (start us, length us, event | category | flops | bytes accessed | tf_op | source)
XLA Modules:
  0.0 291.6 jit_solution(8254626462926114139)
XLA Ops:
  6.5 0.0 copy-start
  6.5 0.0 all-gather.2.cloned.1.call-start
  6.5 0.7 all-gather.2.cloned.1.call-update
  7.3 0.0 all-reduce.2.cloned.1.call-start
  7.3 0.7 compare_select_fusion.1
  8.0 0.7 compare_select_fusion
  8.6 64.9 %all-gather.2.cloned.1.call-done = bf16[896,2048]{1,0:T(8,128)(2,1)} async-done(((bf16[896,256]{1,0:T(8,128)(2,1)}), bf16[896,2048]{1,0:T(8,128)(2,1)}) %all-gather.2.cloned.1.call-update) | async-done | bytes 3670032 | tf_op jit(solution)/shard_map/all_gather | solution.py:40
  73.6 4.7 %fusion.5 = f32[2048,256]{1,0:T(8,128)} fusion(bf16[896,2048]{1,0:T(8,128)(2,1)} %all-gather.2.cloned.1.call-done, bf16[896,256]{1,0:T(8,128)(2,1)} %param.6), kind=kOutput, calls=%fused_computation.18 | convolution fusion | flops 939524096 | bytes 6225920 | tf_op jit(solution)/shard_map/dot_general | solution.py:41
  78.3 0.0 copy-start.1
  78.3 0.0 copy-start.2
  78.3 0.0 all-reduce.2.cloned.1.call-update
  78.3 0.0 copy-done
  78.3 0.6 gather_fusion
  78.9 0.0 copy-done.1
  78.9 0.7 gather_fusion.1
  79.6 0.1 subtract_bitcast_fusion
  79.7 0.1 dynamic_slice.7
  79.8 0.0 copy-done.2
  79.8 0.1 broadcast_bitcast_fusion
  79.8 0.1 dynamic_slice.6
  79.9 0.1 bitcast_multiply_fusion
  80.0 199.2 %all-reduce.2.cloned.1.call-done = f32[2048,256]{1,0:T(8,128)} async-done(((f32[2048,256]{1,0:T(8,128)}), f32[2048,256]{1,0:T(8,128)}) %all-reduce.2.cloned.1.call-update) | async-done | bytes 2097168 | tf_op jit(solution)/shard_map/psum | solution.py:42
  279.2 4.6 %fusion = bf16[896,256]{0,1:T(8,128)(2,1)S(1)} fusion(bf16[896,2048]{1,0:T(8,128)(2,1)} %all-gather.2.cloned.1.call-done, f32[2048,256]{1,0:T(8,128)} %all-reduce.2.cloned.1.call-done, f32[256]{0:T(256)S(1)} %dynamic_slice.7, f32[2048]{0:T(1024)S(1)} %subtract_bitcast_fusion, f32[256]{0:T(256)S(1)} %dynamic_slice.6, f32[2048]{0:T(1024)S(1)} %bitcast_multiply_fusion), kind=kOutput, calls=%fused_computation.4 | convolution fusion | flops 942374912 | bytes 6244352 | tf_op jit(solution)/shard_map/dot_general | solution.py:44
  283.8 1.0 copy.8
  (3 shorter events, 0.0 us)
Async XLA Ops:
  6.5 71.8 %copy-start = (f32[20096]{0:T(1024)S(1)}, f32[20096]{0:T(1024)}, u32[]{:S(2)}) copy-start(f32[20096]{0:T(1024)} %param.8) | copy-start | bytes 241156
  6.5 67.0 %all-gather.2.cloned.1.call-start = ((), (), s32[]{:S(2)}) async-start(), calls=%async_computation | async-start | bytes 4128768 | tf_op jit(solution)/shard_map/all_gather | solution.py:40
  7.3 271.9 %all-reduce.2.cloned.1.call-start = ((), (), s32[]{:S(2)}) async-start(), calls=%async_computation.1 | async-start | bytes 4194304 | tf_op jit(solution)/shard_map/psum | solution.py:42
  78.3 0.7 copy-start.1
  78.3 1.5 copy-start.2
Sparse Core Ops, SparseCore 0:
  9.4 64.1 all-gather.1
  78.4 200.7 all-reduce.1
where the time goes:
time: 292 us
  waiting for transfers between devices  265 us (91%)
  between operations  13.4 us (5%)
  matrix products  9.29 us (3%)
    psum x1, waiting for transfers between devices, body(): summed = lax.psum(coulomb, 'aux')  199 us
    all_gather x1, waiting for transfers between devices, body(): gathered = lax.all_gather(three_index, 'pair', axis=1, tiled=True)  64.9 us
  transfers between devices with their start and end apart: 2, of which 2 were waited for; matrix products, arithmetic and copies ran while one was open for 1% of the time, Pallas kernels for 0%

commit v1 on v0

v1 whole, which is shorter than its diff:
```python
import jax
import jax.numpy as jnp
from jax import lax
from jax.sharding import Mesh, PartitionSpec as P

TS = 128
VT = 157
NX, NZ, NCORE, NPAIR = 4, 8, 2, 8
NXZ = NX * NZ
AUX = ("x", "z", "core")
PAIRS = ((0, 0), (0, 1), (-1, 1), (-1, 2), (-2, 2))
PIECE = len(PAIRS) * 2 * TS // NXZ


def ring(size, step):
    return [(i, (i + step) % size) for i in range(size)]


def tile_scale(tile_exponent):
    return jnp.where(tile_exponent == -1, 0.5, jnp.where(tile_exponent == 1, 2.0, 1.0)).astype(
        jnp.float32
    )


def tile_energy(occupied_energy, virtual_energy, tile_occupied, tile_virtual):
    return virtual_energy.reshape(VT, TS)[tile_virtual] - occupied_energy[tile_occupied][:, None]


def full_block(tiles):
    return tiles.transpose(0, 2, 1, 3).reshape(2 * TS, 2 * TS)


def body(three_index, occupied_energy, virtual_energy, tile_occupied, tile_virtual, tile_exponent):
    bf16, f32 = jnp.bfloat16, jnp.float32
    me = lax.axis_index("pair")
    core = lax.axis_index("core")
    slot = lax.axis_index(("x", "z"))

    block = {0: three_index}
    for d in (1, 2, 3):
        block[-d] = lax.ppermute(block[1 - d], "pair", ring(NPAIR, 1))
        block[d] = lax.ppermute(block[d - 1], "pair", ring(NPAIR, -1))
    half = three_index.shape[0] // 2
    block[4] = jnp.concatenate(
        [
            lax.ppermute(block[-3][:half], "pair", ring(NPAIR, 1)),
            lax.ppermute(block[3][half:], "pair", ring(NPAIR, -1)),
        ]
    )

    energy = tile_energy(occupied_energy, virtual_energy, tile_occupied, tile_virtual)
    scale = tile_scale(tile_exponent)

    def tile_of(relative, part):
        return 2 * ((me + relative + NPAIR) % NPAIR) + part

    partial = []
    for r, c in PAIRS:
        product = lax.dot_general(
            block[r], block[c], (((0,), (0,)), ((), ())), preferred_element_type=f32
        )
        partial.append(product.reshape(2, TS, 2, TS).transpose(0, 2, 1, 3))
    partial = jnp.stack(partial, axis=1)
    own = jnp.where(core == 0, partial[0], partial[1])
    other = jnp.where(core == 0, partial[1], partial[0]).astype(bf16)
    summed = own + lax.ppermute(other, "core", ring(NCORE, 1)).astype(f32)
    pieces = lax.all_to_all(
        summed.astype(bf16).reshape(NXZ, PIECE, TS), ("x", "z"), 0, 0
    )
    coulomb = jnp.sum(pieces.astype(f32), axis=0)

    denominator = jnp.stack(
        [
            jnp.stack(
                [energy[tile_of(r, core)][:, None] + energy[tile_of(c, h)][None, :] for h in (0, 1)]
            )
            for r, c in PAIRS
        ]
    ).reshape(-1, TS)
    factor = jnp.stack(
        [jnp.stack([scale[tile_of(r, core)] * scale[tile_of(c, h)] for h in (0, 1)]) for r, c in PAIRS]
    ).reshape(-1)
    factor = jnp.repeat(factor, TS)[:, None]
    own_denominator = lax.dynamic_slice_in_dim(denominator, slot * PIECE, PIECE)
    own_factor = lax.dynamic_slice_in_dim(factor, slot * PIECE, PIECE)
    amplitude = (coulomb * own_factor / own_denominator).astype(bf16)
    halves = lax.all_to_all(
        jnp.broadcast_to(amplitude[None], (NXZ, PIECE, TS)), ("x", "z"), 0, 0
    ).reshape(-1, TS)

    width = 2 * TS
    lower1 = lax.ppermute(halves[1 * width : 3 * width], "pair", ring(NPAIR, 1))
    upper1 = lax.ppermute(halves[2 * width : 4 * width], "pair", ring(NPAIR, -1))
    lower2 = lax.ppermute(halves[3 * width : 5 * width], "pair", ring(NPAIR, 2))
    mine = jnp.concatenate([halves[: 2 * width], lower1, upper1, lower2])
    tiles = lax.all_gather(mine, "core").reshape(2, 8, 2, TS, TS)

    order = ((0, False), (1, True), (-1, False), (-2, False), (2, True), (3, True), (-3, False), (4, False))
    total = None
    for n, (q, transposed) in enumerate(order):
        matrix = full_block(tiles[:, n])
        row_scale = jnp.repeat(jnp.stack([scale[tile_of(q, 0)], scale[tile_of(q, 1)]]), TS).astype(bf16)
        if transposed:
            matrix = matrix * row_scale[None, :]
            dims = (((1,), (1,)), ((), ()))
        else:
            matrix = matrix * row_scale[:, None]
            dims = (((1,), (0,)), ((), ()))
        term = lax.dot_general(block[q], matrix, dims, preferred_element_type=f32)
        total = term if total is None else total + term
    return total.astype(bf16)


def solution(mesh):
    grid = Mesh(mesh.devices.reshape(NX, NZ, NCORE, NPAIR), AUX + ("pair",))
    placed = (P(AUX, "pair"), P(), P(), P(), P(), P())
    return jax.shard_map(
        body, mesh=grid, in_specs=placed, out_specs=P(AUX, "pair"), check_vma=False
    )
```

time: 292 us -> 174 us (0.60)
  the two profiles are of different devices: /device:TPU:1 before, /device:TPU:68 now
where the time goes in v1:
time: 174 us; the launch traced here: 173 us
  starting transfers between devices  58.8 us (34%)
  waiting for transfers between devices  44.6 us (26%)
  between operations  30 us (17%)
  local copies, waits for them, and re-layouts  14.7 us (8%)
  other arithmetic  14.5 us (8%)
  matrix products  10.5 us (6%)
    ppermute x3, starting transfers between devices, body(): block[d] = lax.ppermute(block[d - 1], 'pair', ring(NPAIR, -1))  15.8 us
    ppermute x3, waiting for transfers between devices, body(): block[d] = lax.ppermute(block[d - 1], 'pair', ring(NPAIR, -1))  13.3 us
    all_to_all x1, starting transfers between devices, body(): lax.all_to_all(summed.astype(bf16).reshape(NXZ, PIECE, TS), ('x', 'z'), 0...  12.5 us
    all_to_all x1, waiting for transfers between devices, body(): lax.all_to_all(jnp.broadcast_to(amplitude[None], (NXZ, PIECE, TS)), ('x',...  11.6 us
    all_to_all x1, waiting for transfers between devices, body(): lax.all_to_all(summed.astype(bf16).reshape(NXZ, PIECE, TS), ('x', 'z'), 0...  9.58 us
    another operation x8, other arithmetic, body(): jnp.stack([scale[tile_of(q, 0)], scale[tile_of(q, 1)]])  7.07 us
    all_to_all x1, starting transfers between devices, body(): lax.all_to_all(jnp.broadcast_to(amplitude[None], (NXZ, PIECE, TS)), ('x',...  6.32 us
    ppermute x3, starting transfers between devices, body(): block[-d] = lax.ppermute(block[1 - d], 'pair', ring(NPAIR, 1))  5.75 us
  transfers between devices with their start and end apart: 15, of which 7 were waited for; matrix products, arithmetic and copies ran while one was open for 15% of the time, Pallas kernels for 0%

profile of v1, /device:TPU:68, one launch (start us, length us, event | category | flops | bytes accessed | tf_op | source)
XLA Modules:
  0.0 173.1 jit_solution(190722931667045878)
XLA Ops:
  6.5 5.5 %collective-permute-start = (bf16[896,256]{1,0:T(8,128)(2,1)}, bf16[896,256]{1,0:T(8,128)(2,1)S(1)}, u32[]{:S(2)}, u32[]{:S(2)}) collective-permute-start(bf16[896,256]{1,0:T(8,128)(2,1)} %param.6), channel_id=1, source_target_pairs={{0,7},{1,0},{2,1},{3,2},{4,3},{5,4},{6,5},{7,6},{8,15},{9,8},{10,9... | collective-permute-start | bytes 1376264 | tf_op jit(solution)/shard_map/ppermute | solution.py:42
  12.1 1.9 %collective-permute-start.1 = (bf16[896,256]{1,0:T(8,128)(2,1)}, bf16[896,256]{1,0:T(8,128)(2,1)S(1)}, u32[]{:S(2)}, u32[]{:S(2)}) collective-permute-start(bf16[896,256]{1,0:T(8,128)(2,1)} %param.6), channel_id=1, source_target_pairs={{0,1},{1,2},{2,3},{3,4},{4,5},{5,6},{6,7},{7,0},{8,9},{9,10},{10,1... | collective-permute-start | bytes 1376264 | tf_op jit(solution)/shard_map/ppermute | solution.py:41
  14.1 0.7 compare_select_fusion.3
  14.7 0.7 fusion.48
  25.2 1.6 fusion.49
  33.5 0.6 gather_fusion
  34.1 0.7 gather_fusion.1
  35.3 0.7 fusion.47
  36.0 1.0 broadcast_add_fusion.1
  37.0 0.3 fusion.51
  37.5 0.3 fusion.50
  37.8 0.8 reshape.654
  38.7 5.1 %collective-permute-start.2 = (bf16[896,256]{1,0:T(8,128)(2,1)S(1)}, bf16[896,256]{1,0:T(8,128)(2,1)S(1)}, u32[]{:S(2)}, u32[]{:S(2)}) collective-permute-start(bf16[896,256]{1,0:T(8,128)(2,1)S(1)} %collective-permute-done), channel_id=1, source_target_pairs={{0,7},{1,0},{2,1},{3,2},{4,3},{5,4},{6,5},{7,6},{8,15},{9,8},{10,9... | collective-permute-start | bytes 1376264 | tf_op jit(solution)/shard_map/ppermute | solution.py:42
  43.8 1.9 %collective-permute-start.3 = (bf16[896,256]{1,0:T(8,128)(2,1)S(1)}, bf16[896,256]{1,0:T(8,128)(2,1)}, u32[]{:S(2)}, u32[]{:S(2)}) collective-permute-start(bf16[896,256]{1,0:T(8,128)(2,1)S(1)} %collective-permute-done.1), channel_id=1, source_target_pairs={{0,1},{1,2},{2,3},{3,4},{4,5},{5,6},{6,7},{7,0},{8,9},{9,10},{10,1... | collective-permute-start | bytes 1376264 | tf_op jit(solution)/shard_map/ppermute | solution.py:41
  45.7 1.0 bitcast_dynamic-update-slice_fusion.3
  46.7 6.3 %collective-permute-done.2 = bf16[896,256]{1,0:T(8,128)(2,1)S(1)} collective-permute-done((bf16[896,256]{1,0:T(8,128)(2,1)S(1)}, bf16[896,256]{1,0:T(8,128)(2,1)S(1)}, u32[]{:S(2)}, u32[]{:S(2)}) %collective-permute-start.2) | collective-permute-done | bytes 458784 | tf_op jit(solution)/shard_map/ppermute | solution.py:42
  53.0 1.0 fusion.52
  54.0 1.1 reshape.656
  55.1 3.3 %collective-permute-done.3 = bf16[896,256]{1,0:T(8,128)(2,1)} collective-permute-done((bf16[896,256]{1,0:T(8,128)(2,1)S(1)}, bf16[896,256]{1,0:T(8,128)(2,1)}, u32[]{:S(2)}, u32[]{:S(2)}) %collective-permute-start.3) | collective-permute-done | bytes 458784 | tf_op jit(solution)/shard_map/ppermute | solution.py:41
  58.4 2.1 %fusion.53 = f32[256,256]{1,0:T(8,128)} fusion(bf16[896,256]{1,0:T(8,128)(2,1)} %collective-permute-done.3, bf16[896,256]{1,0:T(8,128)(2,1)S(1)} %collective-permute-done.2), kind=kOutput, calls=%fused_computation.140 | convolution fusion | flops 117440512 | bytes 1179648 | tf_op jit(solution)/shard_map/dot_general | solution.py:59
  60.5 1.8 %reshape.657 = f32[2,128,2,128]{3,2,1,0:T(2,128)} reshape(f32[256,256]{1,0:T(8,128)} %fusion.53) | data formatting | bytes 524288 | tf_op jit(solution)/shard_map/reshape | solution.py:62
  62.3 1.0 bitcast_dynamic-update-slice_fusion
  63.4 1.9 %collective-permute-start.4 = (bf16[5,2,128,128]{3,2,1,0:T(8,128)(2,1)S(1)}, bf16[5,2,128,128]{3,2,1,0:T(8,128)(2,1)S(1)}, u32[]{:S(2)}, u32[]{:S(2)}) collective-permute-start(bf16[5,2,128,128]{3,2,1,0:T(8,128)(2,1)S(1)} %fusion.10), channel_id=1, source_target_pairs={{0,8},{8,0},{1,9},{9,1},{2,10},{10,2},{3,11},{11,3},{4,12},{12,4},... | collective-permute-start | bytes 983048 | tf_op jit(solution)/shard_map/ppermute | solution.py:66
  65.3 1.3 pad_maximum_fusion.3
  66.7 0.8 copy-done.11
  67.6 0.8 fusion.5
  68.4 12.5 %all-to-all-start = ((bf16[32,40,128]{2,1,0:T(8,128)(2,1)}), bf16[32,40,128]{2,1,0:T(8,128)(2,1)S(1)}, u32[]{:S(2)}, u32[]{:S(2)}) async-start(bf16[32,40,128]{2,1,0:T(8,128)(2,1)} %bitcast.12), calls=%async_computation | async-start | bytes 655360 | tf_op jit(solution)/shard_map/all_to_all | solution.py:67
  81.0 1.5 fusion.24
  82.6 0.7 fusion.25
  83.2 0.7 fusion.26
  84.0 9.6 %all-to-all-done = bf16[32,40,128]{2,1,0:T(8,128)(2,1)S(1)} async-done(((bf16[32,40,128]{2,1,0:T(8,128)(2,1)}), bf16[32,40,128]{2,1,0:T(8,128)(2,1)S(1)}, u32[]{:S(2)}, u32[]{:S(2)}) %all-to-all-start) | async-done | bytes 327712 | tf_op jit(solution)/shard_map/all_to_all | solution.py:67
  93.6 0.8 divide_convert_fusion
  94.4 0.8 broadcast_in_dim.66
  95.2 6.3 %all-to-all-start.1 = ((bf16[32,40,128]{2,1,0:T(8,128)(2,1)}), bf16[32,40,128]{2,1,0:T(8,128)(2,1)S(1)}, u32[]{:S(2)}, u32[]{:S(2)}) async-start(bf16[32,40,128]{2,1,0:T(8,128)(2,1)} %broadcast_in_dim.66), calls=%async_computation.1 | async-start | bytes 655360 | tf_op jit(solution)/shard_map/all_to_all | solution.py:87
  101.8 11.6 %all-to-all-done.1 = bf16[32,40,128]{2,1,0:T(8,128)(2,1)S(1)} async-done(((bf16[32,40,128]{2,1,0:T(8,128)(2,1)}), bf16[32,40,128]{2,1,0:T(8,128)(2,1)S(1)}, u32[]{:S(2)}, u32[]{:S(2)}) %all-to-all-start.1) | async-done | bytes 327712 | tf_op jit(solution)/shard_map/all_to_all | solution.py:87
  113.4 1.9 %collective-permute-start.5 = (bf16[512,128]{1,0:T(8,128)(2,1)S(1)}, bf16[512,128]{1,0:T(8,128)(2,1)S(1)}, u32[]{:S(2)}, u32[]{:S(2)}) collective-permute-start(bf16[512,128]{1,0:T(8,128)(2,1)S(1)} %get-tuple-element.16), channel_id=1, source_target_pairs={{0,1},{1,2},{2,3},{3,4},{4,5},{5,6},{6,7},{7,0},{8,9},{9,10},{10,1... | collective-permute-start | bytes 393224 | tf_op jit(solution)/shard_map/ppermute | solution.py:92
  115.4 5.1 %collective-permute-start.6 = (bf16[512,128]{1,0:T(8,128)(2,1)S(1)}, bf16[512,128]{1,0:T(8,128)(2,1)S(1)}, u32[]{:S(2)}, u32[]{:S(2)}) collective-permute-start(bf16[512,128]{1,0:T(8,128)(2,1)S(1)} %get-tuple-element.15), channel_id=1, source_target_pairs={{0,7},{1,0},{2,1},{3,2},{4,3},{5,4},{6,5},{7,6},{8,15},{9,8},{10,9... | collective-permute-start | bytes 393224 | tf_op jit(solution)/shard_map/ppermute | solution.py:93
  120.5 1.9 %collective-permute-start.7 = (bf16[512,128]{1,0:T(8,128)(2,1)S(1)}, bf16[512,128]{1,0:T(8,128)(2,1)S(1)}, u32[]{:S(2)}, u32[]{:S(2)}) collective-permute-start(bf16[512,128]{1,0:T(8,128)(2,1)S(1)} %get-tuple-element.14), channel_id=1, source_target_pairs={{0,2},{1,3},{2,4},{3,5},{4,6},{5,7},{6,0},{7,1},{8,10},{9,11},{10,... | collective-permute-start | bytes 393224 | tf_op jit(solution)/shard_map/ppermute | solution.py:94
  122.4 1.3 pad_maximum_fusion.4
  123.7 1.4 pad_maximum_fusion.7
  125.1 5.5 %collective-permute-done.7 = bf16[512,128]{1,0:T(8,128)(2,1)S(1)} collective-permute-done((bf16[512,128]{1,0:T(8,128)(2,1)S(1)}, bf16[512,128]{1,0:T(8,128)(2,1)S(1)}, u32[]{:S(2)}, u32[]{:S(2)}) %collective-permute-start.7) | collective-permute-done | bytes 131104 | tf_op jit(solution)/shard_map/ppermute | solution.py:94
  130.6 0.8 pad_maximum_fusion
  131.5 1.4 pad_maximum_fusion.8
  133.0 1.9 %collective-permute-start.9 = (bf16[896,256]{1,0:T(8,128)(2,1)}, bf16[896,256]{1,0:T(8,128)(2,1)S(1)}, u32[]{:S(2)}, u32[]{:S(2)}) collective-permute-start(bf16[896,256]{1,0:T(8,128)(2,1)} %collective-permute-done.3), channel_id=1, source_target_pairs={{0,1},{1,2},{2,3},{3,4},{4,5},{5,6},{6,7},{7,0},{8,9},{9,10},{10,1... | collective-permute-start | bytes 1376264 | tf_op jit(solution)/shard_map/ppermute | solution.py:41
  134.9 5.1 %collective-permute-start.8 = (bf16[896,256]{1,0:T(8,128)(2,1)S(1)}, bf16[896,256]{1,0:T(8,128)(2,1)S(1)}, u32[]{:S(2)}, u32[]{:S(2)}) collective-permute-start(bf16[896,256]{1,0:T(8,128)(2,1)S(1)} %collective-permute-done.2), channel_id=1, source_target_pairs={{0,7},{1,0},{2,1},{3,2},{4,3},{5,4},{6,5},{7,6},{8,15},{9,8},{10,9... | collective-permute-start | bytes 1376264 | tf_op jit(solution)/shard_map/ppermute | solution.py:42
  140.0 1.5 pad_maximum_fusion.6
  141.6 7.0 %collective-permute-done.8 = bf16[896,256]{1,0:T(8,128)(2,1)S(1)} collective-permute-done((bf16[896,256]{1,0:T(8,128)(2,1)S(1)}, bf16[896,256]{1,0:T(8,128)(2,1)S(1)}, u32[]{:S(2)}, u32[]{:S(2)}) %collective-permute-start.8) | collective-permute-done | bytes 458784 | tf_op jit(solution)/shard_map/ppermute | solution.py:42
  148.7 5.6 %collective-permute-start.11 = (bf16[448,256]{1,0:T(8,128)(2,1)S(1)}, bf16[448,256]{1,0:T(8,128)(2,1)S(1)}, u32[]{:S(2)}, u32[]{:S(2)}) collective-permute-start(bf16[448,256]{1,0:T(8,128)(2,1)S(1)} %slice.84), channel_id=1, source_target_pairs={{0,7},{1,0},{2,1},{3,2},{4,3},{5,4},{6,5},{7,6},{8,15},{9,8},{10,9... | collective-permute-start | bytes 688136 | tf_op jit(solution)/shard_map/ppermute | solution.py:47
  154.3 1.9 %collective-permute-start.10 = (bf16[448,256]{1,0:T(8,128)(2,1)S(1)}, bf16[448,256]{1,0:T(8,128)(2,1)}, u32[]{:S(2)}, u32[]{:S(2)}) collective-permute-start(bf16[448,256]{1,0:T(8,128)(2,1)S(1)} %slice.83), channel_id=1, source_target_pairs={{0,1},{1,2},{2,3},{3,4},{4,5},{5,6},{6,7},{7,0},{8,9},{9,10},{10,1... | collective-permute-start | bytes 688136 | tf_op jit(solution)/shard_map/ppermute | solution.py:46
  156.3 1.4 slice_bitcast_fusion.2
  157.7 0.1 copy.61
  157.8 0.1 copy.62
  158.0 0.1 copy.63
  158.1 0.1 copy.65
  158.9 0.4 fusion.20
  159.3 0.3 fusion.15
  159.6 0.3 convolution_add_fusion.3
  160.0 0.4 convolution_add_fusion.2
  160.4 1.5 fusion.3
  161.9 0.4 fusion.12
  162.3 1.3 collective-permute-done.10
  163.6 1.4 fusion.6
  164.9 0.4 fusion.4
  165.3 1.0 copy.70
  (77 shorter events, 2.7 us)
Async XLA Ops:
  6.5 27.0 %copy-start = (f32[20096]{0:T(1024)S(1)}, f32[20096]{0:T(1024)}, u32[]{:S(2)}) copy-start(f32[20096]{0:T(1024)} %param.8) | copy-start | bytes 241156
  6.5 26.9 %copy-start.13 = (s32[16]{0:T(128)S(1)}, s32[16]{0:T(128)}, u32[]{:S(2)}) copy-start(s32[16]{0:T(128)} %param.10) | copy-start | bytes 196
  6.5 26.9 %copy-start.12 = (s32[16]{0:T(128)S(1)}, s32[16]{0:T(128)}, u32[]{:S(2)}) copy-start(s32[16]{0:T(128)} %param.9) | copy-start | bytes 196
  6.5 27.6 %copy-start.1 = (f32[64]{0:T(128)S(1)}, f32[64]{0:T(128)}, u32[]{:S(2)}) copy-start(f32[64]{0:T(128)} %param.7) | copy-start | bytes 772
  6.5 30.4 %collective-permute-start = (bf16[896,256]{1,0:T(8,128)(2,1)}, bf16[896,256]{1,0:T(8,128)(2,1)S(1)}, u32[]{:S(2)}, u32[]{:S(2)}) collective-permute-start(bf16[896,256]{1,0:T(8,128)(2,1)} %param.6), channel_id=1, source_target_pairs={{0,7},{1,0},{2,1},{3,2},{4,3},{5,4},{6,5},{7,6},{8,15},{9,8},{10,9... | collective-permute-start | bytes 1376264 | tf_op jit(solution)/shard_map/ppermute | solution.py:42
  12.1 24.9 %collective-permute-start.1 = (bf16[896,256]{1,0:T(8,128)(2,1)}, bf16[896,256]{1,0:T(8,128)(2,1)S(1)}, u32[]{:S(2)}, u32[]{:S(2)}) collective-permute-start(bf16[896,256]{1,0:T(8,128)(2,1)} %param.6), channel_id=1, source_target_pairs={{0,1},{1,2},{2,3},{3,4},{4,5},{5,6},{6,7},{7,0},{8,9},{9,10},{10,1... | collective-permute-start | bytes 1376264 | tf_op jit(solution)/shard_map/ppermute | solution.py:41
  36.0 1.5 copy-start.2
  38.7 14.3 %collective-permute-start.2 = (bf16[896,256]{1,0:T(8,128)(2,1)S(1)}, bf16[896,256]{1,0:T(8,128)(2,1)S(1)}, u32[]{:S(2)}, u32[]{:S(2)}) collective-permute-start(bf16[896,256]{1,0:T(8,128)(2,1)S(1)} %collective-permute-done), channel_id=1, source_target_pairs={{0,7},{1,0},{2,1},{3,2},{4,3},{5,4},{6,5},{7,6},{8,15},{9,8},{10,9... | collective-permute-start | bytes 1376264 | tf_op jit(solution)/shard_map/ppermute | solution.py:42
  43.8 14.6 %collective-permute-start.3 = (bf16[896,256]{1,0:T(8,128)(2,1)S(1)}, bf16[896,256]{1,0:T(8,128)(2,1)}, u32[]{:S(2)}, u32[]{:S(2)}) collective-permute-start(bf16[896,256]{1,0:T(8,128)(2,1)S(1)} %collective-permute-done.1), channel_id=1, source_target_pairs={{0,1},{1,2},{2,3},{3,4},{4,5},{5,6},{6,7},{7,0},{8,9},{9,10},{10,1... | collective-permute-start | bytes 1376264 | tf_op jit(solution)/shard_map/ppermute | solution.py:41
  62.3 4.4 %copy-start.9 = (f32[1,128,128]{2,1,0:T(8,128)S(1)}, f32[1,128,128]{2,1,0:T(8,128)}, u32[]{:S(2)}) copy-start(f32[1,128,128]{2,1,0:T(8,128)} %get-tuple-element.51) | copy-start | bytes 196612
  62.3 4.4 %copy-start.10 = (f32[1,128,128]{2,1,0:T(8,128)S(1)}, f32[1,128,128]{2,1,0:T(8,128)}, u32[]{:S(2)}) copy-start(f32[1,128,128]{2,1,0:T(8,128)} %get-tuple-element.52) | copy-start | bytes 196612
  62.3 4.4 %copy-start.7 = (f32[1,128,128]{2,1,0:T(8,128)S(1)}, f32[1,128,128]{2,1,0:T(8,128)}, u32[]{:S(2)}) copy-start(f32[1,128,128]{2,1,0:T(8,128)} %get-tuple-element.48) | copy-start | bytes 196612
  62.3 4.4 %copy-start.8 = (f32[1,128,128]{2,1,0:T(8,128)S(1)}, f32[1,128,128]{2,1,0:T(8,128)}, u32[]{:S(2)}) copy-start(f32[1,128,128]{2,1,0:T(8,128)} %get-tuple-element.49) | copy-start | bytes 196612
  63.4 4.2 %collective-permute-start.4 = (bf16[5,2,128,128]{3,2,1,0:T(8,128)(2,1)S(1)}, bf16[5,2,128,128]{3,2,1,0:T(8,128)(2,1)S(1)}, u32[]{:S(2)}, u32[]{:S(2)}) collective-permute-start(bf16[5,2,128,128]{3,2,1,0:T(8,128)(2,1)S(1)} %fusion.10), channel_id=1, source_target_pairs={{0,8},{8,0},{1,9},{9,1},{2,10},{10,2},{3,11},{11,3},{4,12},{12,4},... | collective-permute-start | bytes 983048 | tf_op jit(solution)/shard_map/ppermute | solution.py:66
  66.7 0.9 copy-start.11
  67.5 15.0 %copy-start.5 = (f32[1,128,128]{2,1,0:T(8,128)S(1)}, f32[1,128,128]{2,1,0:T(8,128)}, u32[]{:S(2)}) copy-start(f32[1,128,128]{2,1,0:T(8,128)} %get-tuple-element.46) | copy-start | bytes 196612
  67.5 15.0 %copy-start.6 = (f32[1,128,128]{2,1,0:T(8,128)S(1)}, f32[1,128,128]{2,1,0:T(8,128)}, u32[]{:S(2)}) copy-start(f32[1,128,128]{2,1,0:T(8,128)} %get-tuple-element.53) | copy-start | bytes 196612
  67.6 15.7 %copy-start.3 = (f32[1,128,128]{2,1,0:T(8,128)S(1)}, f32[1,128,128]{2,1,0:T(8,128)}, u32[]{:S(2)}) copy-start(f32[1,128,128]{2,1,0:T(8,128)} %get-tuple-element.45) | copy-start | bytes 196612
  67.6 15.7 %copy-start.4 = (f32[1,128,128]{2,1,0:T(8,128)S(1)}, f32[1,128,128]{2,1,0:T(8,128)}, u32[]{:S(2)}) copy-start(f32[1,128,128]{2,1,0:T(8,128)} %get-tuple-element.54) | copy-start | bytes 196612
  68.4 25.1 %all-to-all-start = ((bf16[32,40,128]{2,1,0:T(8,128)(2,1)}), bf16[32,40,128]{2,1,0:T(8,128)(2,1)S(1)}, u32[]{:S(2)}, u32[]{:S(2)}) async-start(bf16[32,40,128]{2,1,0:T(8,128)(2,1)} %bitcast.12), calls=%async_computation | async-start | bytes 655360 | tf_op jit(solution)/shard_map/all_to_all | solution.py:67
  95.2 18.2 %all-to-all-start.1 = ((bf16[32,40,128]{2,1,0:T(8,128)(2,1)}), bf16[32,40,128]{2,1,0:T(8,128)(2,1)S(1)}, u32[]{:S(2)}, u32[]{:S(2)}) async-start(bf16[32,40,128]{2,1,0:T(8,128)(2,1)} %broadcast_in_dim.66), calls=%async_computation.1 | async-start | bytes 655360 | tf_op jit(solution)/shard_map/all_to_all | solution.py:87
  101.5 54.8 %all-gather.3.cloned.1.call-start = ((), (), s32[]{:S(2)}) async-start(), calls=%async_computation.2 | async-start | bytes 1572864 | tf_op jit(solution)/shard_map/all_gather | solution.py:96
  113.4 11.7 %collective-permute-start.5 = (bf16[512,128]{1,0:T(8,128)(2,1)S(1)}, bf16[512,128]{1,0:T(8,128)(2,1)S(1)}, u32[]{:S(2)}, u32[]{:S(2)}) collective-permute-start(bf16[512,128]{1,0:T(8,128)(2,1)S(1)} %get-tuple-element.16), channel_id=1, source_target_pairs={{0,1},{1,2},{2,3},{3,4},{4,5},{5,6},{6,7},{7,0},{8,9},{9,10},{10,1... | collective-permute-start | bytes 393224 | tf_op jit(solution)/shard_map/ppermute | solution.py:92
  115.4 9.8 %collective-permute-start.6 = (bf16[512,128]{1,0:T(8,128)(2,1)S(1)}, bf16[512,128]{1,0:T(8,128)(2,1)S(1)}, u32[]{:S(2)}, u32[]{:S(2)}) collective-permute-start(bf16[512,128]{1,0:T(8,128)(2,1)S(1)} %get-tuple-element.15), channel_id=1, source_target_pairs={{0,7},{1,0},{2,1},{3,2},{4,3},{5,4},{6,5},{7,6},{8,15},{9,8},{10,9... | collective-permute-start | bytes 393224 | tf_op jit(solution)/shard_map/ppermute | solution.py:93
  120.5 10.1 %collective-permute-start.7 = (bf16[512,128]{1,0:T(8,128)(2,1)S(1)}, bf16[512,128]{1,0:T(8,128)(2,1)S(1)}, u32[]{:S(2)}, u32[]{:S(2)}) collective-permute-start(bf16[512,128]{1,0:T(8,128)(2,1)S(1)} %get-tuple-element.14), channel_id=1, source_target_pairs={{0,2},{1,3},{2,4},{3,5},{4,6},{5,7},{6,0},{7,1},{8,10},{9,11},{10,... | collective-permute-start | bytes 393224 | tf_op jit(solution)/shard_map/ppermute | solution.py:94
  133.0 21.3 %collective-permute-start.9 = (bf16[896,256]{1,0:T(8,128)(2,1)}, bf16[896,256]{1,0:T(8,128)(2,1)S(1)}, u32[]{:S(2)}, u32[]{:S(2)}) collective-permute-start(bf16[896,256]{1,0:T(8,128)(2,1)} %collective-permute-done.3), channel_id=1, source_target_pairs={{0,1},{1,2},{2,3},{3,4},{4,5},{5,6},{6,7},{7,0},{8,9},{9,10},{10,1... | collective-permute-start | bytes 1376264 | tf_op jit(solution)/shard_map/ppermute | solution.py:41
  134.9 13.8 %collective-permute-start.8 = (bf16[896,256]{1,0:T(8,128)(2,1)S(1)}, bf16[896,256]{1,0:T(8,128)(2,1)S(1)}, u32[]{:S(2)}, u32[]{:S(2)}) collective-permute-start(bf16[896,256]{1,0:T(8,128)(2,1)S(1)} %collective-permute-done.2), channel_id=1, source_target_pairs={{0,7},{1,0},{2,1},{3,2},{4,3},{5,4},{6,5},{7,6},{8,15},{9,8},{10,9... | collective-permute-start | bytes 1376264 | tf_op jit(solution)/shard_map/ppermute | solution.py:42
  148.7 13.6 %collective-permute-start.11 = (bf16[448,256]{1,0:T(8,128)(2,1)S(1)}, bf16[448,256]{1,0:T(8,128)(2,1)S(1)}, u32[]{:S(2)}, u32[]{:S(2)}) collective-permute-start(bf16[448,256]{1,0:T(8,128)(2,1)S(1)} %slice.84), channel_id=1, source_target_pairs={{0,7},{1,0},{2,1},{3,2},{4,3},{5,4},{6,5},{7,6},{8,15},{9,8},{10,9... | collective-permute-start | bytes 688136 | tf_op jit(solution)/shard_map/ppermute | solution.py:47
  154.3 9.2 %collective-permute-start.10 = (bf16[448,256]{1,0:T(8,128)(2,1)S(1)}, bf16[448,256]{1,0:T(8,128)(2,1)}, u32[]{:S(2)}, u32[]{:S(2)}) collective-permute-start(bf16[448,256]{1,0:T(8,128)(2,1)S(1)} %slice.83), channel_id=1, source_target_pairs={{0,1},{1,2},{2,3},{3,4},{4,5},{5,6},{6,7},{7,0},{8,9},{9,10},{10,1... | collective-permute-start | bytes 688136 | tf_op jit(solution)/shard_map/ppermute | solution.py:46
Sparse Core Ops, SparseCore 0:
  131.6 11.6 all-gather.2

commit v2 on v0

v2 whole, which is shorter than its diff:
```python
import jax
import jax.numpy as jnp
from jax import lax
from jax.experimental import pallas as pl
from jax.experimental.pallas import tpu as pltpu
from jax.sharding import Mesh, PartitionSpec as P

TS = 128
VT = 157
NT = 16
NX, NZ, NCORE, NPAIR = 4, 8, 2, 8
NXZ = NX * NZ
AUX = ("x", "z", "core")
EARLY = ((0, 0), (0, 1), (-1, 1))
LATE = ((-1, 2), (-2, 2))
PAIRS = EARLY + LATE
WIDTH = 2 * TS
PIECE = len(PAIRS) * WIDTH // NXZ
ORDER = (
    (0, False, 0, 0),
    (1, True, 0, 1),
    (-1, False, 1, 0),
    (-2, False, 1, 1),
    (2, True, 2, 0),
    (3, True, 2, 1),
    (-3, False, 3, 0),
    (4, False, 3, 1),
)
ROWS = 128
VMEM_LIMIT = 48 * 1024 * 1024
bf16, f32 = jnp.bfloat16, jnp.float32
in_vmem = pl.BlockSpec(memory_space=pltpu.VMEM)
in_smem = pl.BlockSpec(memory_space=pltpu.SMEM)


def ring(size, step):
    return [(i, (i + step) % size) for i in range(size)]


def coulomb_pairs(blocks, pairs):
    names = sorted({d for pair in pairs for d in pair})

    def kernel(*refs):
        block = dict(zip(names, refs))
        own, other = refs[len(names) :]
        core = lax.axis_index("core")
        for k, (r, c) in enumerate(pairs):
            for out, part in ((own, core), (other, 1 - core)):
                left = block[r][:, pl.ds(pl.multiple_of(part * TS, TS), TS)]
                product = lax.dot_general(
                    left, block[c][...], (((0,), (0,)), ((), ())), preferred_element_type=f32
                )
                for h in (0, 1):
                    out[k, h] = product[:, h * TS : (h + 1) * TS].astype(out.dtype)

    shape = (len(pairs), 2, TS, TS)
    return pl.pallas_call(
        kernel,
        out_shape=(jax.ShapeDtypeStruct(shape, f32), jax.ShapeDtypeStruct(shape, bf16)),
        in_specs=[in_vmem] * len(names),
        out_specs=(in_vmem, in_vmem),
        compiler_params=pltpu.CompilerParams(vmem_limit_bytes=VMEM_LIMIT),
        name="coulomb_pairs",
    )(*[blocks[d] for d in names])


def sum_cores(own, received):
    def kernel(*refs):
        out = refs[-1]
        n = 0
        for mine, theirs in zip(refs[: len(own)], refs[len(own) : -1]):
            size = mine.shape[0]
            out[n : n + size] = (mine[...] + theirs[...].astype(f32)).astype(bf16)
            n += size

    total = sum(a.shape[0] for a in own)
    return pl.pallas_call(
        kernel,
        out_shape=jax.ShapeDtypeStruct((total,) + own[0].shape[1:], bf16),
        in_specs=[in_vmem] * (2 * len(own)),
        out_specs=in_vmem,
        compiler_params=pltpu.CompilerParams(vmem_limit_bytes=VMEM_LIMIT),
        name="sum_cores",
    )(*own, *received)


def amplitude_piece(pieces, denominator):
    def kernel(pieces_ref, denominator_ref, out):
        total = jnp.sum(pieces_ref[...].astype(f32), axis=0)
        out[...] = jnp.broadcast_to((total / denominator_ref[...]).astype(bf16)[None], out.shape)

    return pl.pallas_call(
        kernel,
        out_shape=jax.ShapeDtypeStruct(pieces.shape, bf16),
        in_specs=[in_vmem, in_vmem],
        out_specs=in_vmem,
        compiler_params=pltpu.CompilerParams(vmem_limit_bytes=VMEM_LIMIT),
        name="amplitude_piece",
    )(pieces, denominator)


def gamma_rows(blocks, last, mine, theirs, tile_exponent):
    rows, width = blocks[0].shape
    names = [q for q, *_ in ORDER if q != 4]
    steps = rows // ROWS

    def kernel(*refs):
        block = dict(zip(names, refs))
        block[4] = refs[len(names)]
        n = len(names) + 1
        own, other = refs[n : n + 4], refs[n + 4 : n + 8]
        exponent, out, matrix = refs[n + 8 :]
        me = lax.axis_index("pair")
        core = lax.axis_index("core")

        @pl.when(pl.program_id(0) == 0)
        def _():
            for i, (q, transposed, array, k) in enumerate(ORDER):
                for source, part in ((own, core), (other, 1 - core)):
                    for h in (0, 1):
                        tile = 2 * lax.rem(me + q + NPAIR, NPAIR) + (h if transposed else part)
                        level = exponent[tile]
                        scale = jnp.where(level == -1, 0.5, jnp.where(level == 1, 2.0, 1.0))
                        values = source[array][k, h].astype(f32) * scale.astype(f32)
                        row = pl.multiple_of(part * TS, TS)
                        matrix[i, pl.ds(row, TS), h * TS : (h + 1) * TS] = values.astype(bf16)

        total = None
        for i, (q, transposed, _, _) in enumerate(ORDER):
            dims = (((1,), (1 if transposed else 0,)), ((), ()))
            term = lax.dot_general(block[q][...], matrix[i], dims, preferred_element_type=f32)
            total = term if total is None else total + term
        out[...] = total.astype(bf16)

    row_block = pl.BlockSpec((ROWS, width), lambda i: (i, 0))
    return pl.pallas_call(
        kernel,
        grid=(steps,),
        out_shape=jax.ShapeDtypeStruct((rows, width), bf16),
        in_specs=[row_block] * 8 + [in_vmem] * 8 + [in_smem],
        out_specs=row_block,
        scratch_shapes=[pltpu.VMEM((len(ORDER), WIDTH, WIDTH), bf16)],
        compiler_params=pltpu.CompilerParams(vmem_limit_bytes=VMEM_LIMIT),
        name="gamma_rows",
    )(*[blocks[q] for q in names], last, *mine, *theirs, tile_exponent)


def body(three_index, occupied_energy, virtual_energy, tile_occupied, tile_virtual, tile_exponent):
    me = lax.axis_index("pair")
    core = lax.axis_index("core")
    slot = lax.axis_index(("x", "z"))
    up, down = ring(NPAIR, 1), ring(NPAIR, -1)
    swap = ring(NCORE, 1)

    block = {0: three_index}
    for d in (1, 2):
        block[-d] = lax.ppermute(block[1 - d], "pair", up)
        block[d] = lax.ppermute(block[d - 1], "pair", down)

    energy = virtual_energy.reshape(VT, TS)[tile_virtual] - occupied_energy[tile_occupied][:, None]
    scale = jnp.where(tile_exponent == -1, 0.5, jnp.where(tile_exponent == 1, 2.0, 1.0)).astype(f32)
    table = jnp.concatenate([energy, jnp.broadcast_to(scale[:, None], (NT, TS))], axis=1)
    table = jnp.concatenate([table, table, table])
    near = lax.dynamic_slice_in_dim(table, 2 * me + NT - 4, 10).reshape(5, 2, 2 * TS)
    row = lax.dynamic_index_in_dim(near, core, 1, keepdims=False)
    row_of = jnp.stack([row[r + 2] for r, _ in PAIRS])
    column_of = jnp.stack([near[c + 2] for _, c in PAIRS])
    denominator = (
        (row_of[:, None, :TS, None] + column_of[:, :, None, :TS])
        / (row_of[:, None, TS:, None] * column_of[:, :, None, TS:])
    ).reshape(-1, TS)
    own_denominator = lax.dynamic_slice_in_dim(denominator, slot * PIECE, PIECE)

    own_early, other_early = coulomb_pairs(block, EARLY)
    got_early = lax.ppermute(other_early, "core", swap)
    own_late, other_late = coulomb_pairs(block, LATE)
    got_late = lax.ppermute(other_late, "core", swap)
    summed = sum_cores((own_early, own_late), (got_early, got_late))

    block[-3] = lax.ppermute(block[-2], "pair", up)
    block[3] = lax.ppermute(block[2], "pair", down)
    pieces = lax.all_to_all(summed.reshape(NXZ, PIECE, TS), ("x", "z"), 0, 0)
    pieces, block[-3], block[3], own_denominator = lax.optimization_barrier(
        (pieces, block[-3], block[3], own_denominator)
    )

    half = three_index.shape[0] // 2
    last_upper = lax.ppermute(block[-3][:half], "pair", up)
    last_lower = lax.ppermute(block[3][half:], "pair", down)
    halves = lax.all_to_all(amplitude_piece(pieces, own_denominator), ("x", "z"), 0, 0)
    halves, last_upper, last_lower = lax.optimization_barrier((halves, last_upper, last_lower))
    last = jnp.concatenate([last_upper, last_lower])

    halves = halves.reshape(len(PAIRS), 2, TS, TS)
    mine = (
        halves[0:2],
        lax.ppermute(halves[1:3], "pair", up),
        lax.ppermute(halves[2:4], "pair", down),
        lax.ppermute(halves[3:5], "pair", ring(NPAIR, 2)),
    )
    theirs = lax.ppermute(jnp.concatenate(mine), "core", swap)
    theirs = tuple(theirs[2 * i : 2 * i + 2] for i in range(4))
    return gamma_rows(block, last, mine, theirs, tile_exponent)


def solution(mesh):
    grid = Mesh(mesh.devices.reshape(NX, NZ, NCORE, NPAIR), AUX + ("pair",))
    placed = (P(AUX, "pair"), P(), P(), P(), P(), P())
    return jax.shard_map(
        body, mesh=grid, in_specs=placed, out_specs=P(AUX, "pair"), check_vma=False
    )
```

time: 292 us -> 118 us (0.40)
  waiting for transfers between devices: 265 us -> 20.1 us
  starting transfers between devices: 0.04 us -> 81 us
  between operations: 13.4 us -> 0.36 us
  matrix products: 9.29 us -> 0 us
  Pallas kernels: 0 us -> 8.51 us
    psum x1 -> x0, waiting for transfers between devices: 199 us -> none  [body(): summed = lax.psum(coulomb, 'aux')]
    all_gather x1 -> x0, waiting for transfers between devices: 64.9 us -> none  [body(): gathered = lax.all_gather(three_index, 'pair', axis=1, tiled=True)]
    ppermute x0 -> x14, starting transfers between devices: none -> 59.2 us  [the longest x2 9.15 us: body(): block[-d] = lax.ppermute(block[1 - d], 'pair', up)]
    all_to_all x0 -> x2, starting transfers between devices: none -> 21.8 us  [the longest x1 14.4 us: body(): pieces = lax.all_to_all(summed.reshape(NXZ, PIECE, TS), ('x', 'z'), 0, 0)]
    all_to_all x0 -> x2, waiting for transfers between devices: none -> 10.1 us  [the longest x1 10.1 us: body(): pieces = lax.all_to_all(summed.reshape(NXZ, PIECE, TS), ('x', 'z'), 0, 0)]
    ppermute x0 -> x14, waiting for transfers between devices: none -> 9.97 us  [the longest x1 3.31 us: body(): lax.ppermute(halves[1:3], 'pair', up)]
    dot_general x2 -> x0, matrix products: 9.29 us -> none  [the longest x1 4.73 us: body(): lax.dot_general(gathered, three_index, contract, preferred_element_type=j...]
    pallas_call x0 -> x5, Pallas kernels: none -> 8.51 us  [the longest x1 5.83 us: gamma_rows(): pl.pallas_call(kernel, grid=(steps,), out_shape=jax.ShapeDtypeStruct((row...]
  transfers between devices with their start and end apart: 2 -> 16, of which waited for: 2 -> 8; matrix products, arithmetic and copies ran while one was open for 1% -> 5% of each run, Pallas kernels for 0% -> 2%
where the time goes in v2:
time: 118 us; the launch traced here: 117 us
  starting transfers between devices  81 us (69%)
  waiting for transfers between devices  20.1 us (17%)
  Pallas kernels  8.51 us (7%)
  local copies, waits for them, and re-layouts  4.08 us (3%)
  other arithmetic  2.56 us (2%)
    all_to_all x1, starting transfers between devices, body(): pieces = lax.all_to_all(summed.reshape(NXZ, PIECE, TS), ('x', 'z'), 0, 0)  14.4 us
    all_to_all x1, waiting for transfers between devices, body(): pieces = lax.all_to_all(summed.reshape(NXZ, PIECE, TS), ('x', 'z'), 0, 0)  10.1 us
    ppermute x2, starting transfers between devices, body(): block[-d] = lax.ppermute(block[1 - d], 'pair', up)  9.15 us
    ppermute x2, starting transfers between devices, body(): block[d] = lax.ppermute(block[d - 1], 'pair', down)  8.15 us
    all_to_all x1, starting transfers between devices, body(): lax.all_to_all(amplitude_piece(pieces, own_denominator), ('x', 'z'), 0, 0)  7.43 us
    ppermute x1, starting transfers between devices, body(): got_early = lax.ppermute(other_early, 'core', swap)  6.29 us
    ppermute x1, starting transfers between devices, body(): theirs = lax.ppermute(jnp.concatenate(mine), 'core', swap)  6.02 us
    pallas_call x1, Pallas kernels, gamma_rows(): pl.pallas_call(kernel, grid=(steps,), out_shape=jax.ShapeDtypeStruct((row...  5.83 us
  transfers between devices with their start and end apart: 16, of which 8 were waited for; matrix products, arithmetic and copies ran while one was open for 5% of the time, Pallas kernels for 2%

profile of v2, /device:TPU:1, one launch (start us, length us, event | category | flops | bytes accessed | tf_op | source)
XLA Modules:
  0.0 116.7 jit_solution(11621724586946750505)
XLA Ops:
  0.0 0.0 copy-start
  0.0 0.0 copy-start.1
  0.0 4.2 %collective-permute-start.1 = (bf16[896,256]{1,0:T(8,128)(2,1)}, bf16[896,256]{1,0:T(8,128)(2,1)S(1)}, u32[]{:S(2)}, u32[]{:S(2)}) collective-permute-start(bf16[896,256]{1,0:T(8,128)(2,1)} %refs_0_.1), channel_id=1, source_target_pairs={{0,1},{1,2},{2,3},{3,4},{4,5},{5,6},{6,7},{7,0},{8,9},{9,10},{10,1... | collective-permute-start | bytes 1376264 | tf_op jit(solution)/shard_map/ppermute | solution.py:157
  4.2 3.8 %collective-permute-start = (bf16[896,256]{1,0:T(8,128)(2,1)}, bf16[896,256]{1,0:T(8,128)(2,1)S(1)}, u32[]{:S(2)}, u32[]{:S(2)}) collective-permute-start(bf16[896,256]{1,0:T(8,128)(2,1)} %refs_0_.1), channel_id=1, source_target_pairs={{0,7},{1,0},{2,1},{3,2},{4,3},{5,4},{6,5},{7,6},{8,15},{9,8},{10,9... | collective-permute-start | bytes 1376264 | tf_op jit(solution)/shard_map/ppermute | solution.py:158
  8.0 0.7 compare_select_fusion.3
  8.7 0.7 compare_select_fusion
  9.3 1.3 %gather_fusion.1 = f32[16]{0:T(128)S(1)} fusion(f32[64]{0:T(128)} %param.7, s32[1024]{0:T(1024)S(1)} %pad_clamp_fusion), kind=kCustom, calls=%fused_computation.1 | custom fusion | bytes 192 | tf_op jit(solution)/shard_map/gather | solution.py:160
  10.7 0.0 copy-done
  10.7 0.6 gather_fusion
  11.2 0.1 broadcast_subtract_fusion
  11.3 0.1 broadcast_in_dim.34
  11.4 0.7 collective-permute-done.1.refs_0_.refs_1_.refs_2_
  12.1 5.0 %collective-permute-start.2 = (bf16[896,256]{1,0:T(8,128)(2,1)S(1)}, bf16[896,256]{1,0:T(8,128)(2,1)S(1)}, u32[]{:S(2)}, u32[]{:S(2)}) collective-permute-start(bf16[896,256]{1,0:T(8,128)(2,1)S(1)} %collective-permute-done.1.refs_0_.refs_1_.refs_2_), channel_id=1, source_target_pairs={{0,1},{1,2},{2,3},{3,4},{4,5},{5,6},{6,7},{7,0},{8,9},{9,10},{10,1... | collective-permute-start | bytes 1376264 | tf_op jit(solution)/shard_map/ppermute | solution.py:157
  17.1 0.0 collective-permute-done.refs_2_.refs_1_
  17.1 4.3 %collective-permute-start.3 = (bf16[896,256]{1,0:T(8,128)(2,1)S(1)}, bf16[896,256]{1,0:T(8,128)(2,1)S(1)}, u32[]{:S(2)}, u32[]{:S(2)}) collective-permute-start(bf16[896,256]{1,0:T(8,128)(2,1)S(1)} %collective-permute-done.refs_2_.refs_1_), channel_id=1, source_target_pairs={{0,7},{1,0},{2,1},{3,2},{4,3},{5,4},{6,5},{7,6},{8,15},{9,8},{10,9... | collective-permute-start | bytes 1376264 | tf_op jit(solution)/shard_map/ppermute | solution.py:158
  21.5 0.0 copy-done.1
  21.6 0.6 coulomb_pairs.2
  22.2 6.3 %collective-permute-start.4 = (bf16[3,2,128,128]{3,2,1,0:T(8,128)(2,1)S(1)}, bf16[3,2,128,128]{3,2,1,0:T(8,128)(2,1)S(1)}, u32[]{:S(2)}, u32[]{:S(2)}) collective-permute-start(bf16[3,2,128,128]{3,2,1,0:T(8,128)(2,1)S(1)} %get-tuple-element.18), channel_id=1, source_target_pairs={{0,8},{8,0},{1,9},{9,1},{2,10},{10,2},{3,11},{11,3},{4,12},{12,4},... | collective-permute-start | bytes 589832 | tf_op jit(solution)/shard_map/ppermute | solution.py:175
  28.5 0.0 collective-permute-done.2.refs_0_.refs_3_
  28.5 0.2 collective-permute-done.3.refs_2_.refs_4_
  28.7 0.5 coulomb_pairs.3
  29.2 5.8 %collective-permute-start.5 = (bf16[2,2,128,128]{3,2,1,0:T(8,128)(2,1)S(1)}, bf16[2,2,128,128]{3,2,1,0:T(8,128)(2,1)S(1)}, u32[]{:S(2)}, u32[]{:S(2)}) collective-permute-start(bf16[2,2,128,128]{3,2,1,0:T(8,128)(2,1)S(1)} %get-tuple-element.19), channel_id=1, source_target_pairs={{0,8},{8,0},{1,9},{9,1},{2,10},{10,2},{3,11},{11,3},{4,12},{12,4},... | collective-permute-start | bytes 393224 | tf_op jit(solution)/shard_map/ppermute | solution.py:177
  35.0 4.0 %collective-permute-start.6 = (bf16[896,256]{1,0:T(8,128)(2,1)S(1)}, bf16[896,256]{1,0:T(8,128)(2,1)S(1)}, u32[]{:S(2)}, u32[]{:S(2)}) collective-permute-start(bf16[896,256]{1,0:T(8,128)(2,1)S(1)} %collective-permute-done.2.refs_0_.refs_3_), channel_id=1, source_target_pairs={{0,1},{1,2},{2,3},{3,4},{4,5},{5,6},{6,7},{7,0},{8,9},{9,10},{10,1... | collective-permute-start | bytes 1376264 | tf_op jit(solution)/shard_map/ppermute | solution.py:180
  39.0 2.9 %collective-permute-start.7 = (bf16[896,256]{1,0:T(8,128)(2,1)S(1)}, bf16[896,256]{1,0:T(8,128)(2,1)}, u32[]{:S(2)}, u32[]{:S(2)}) collective-permute-start(bf16[896,256]{1,0:T(8,128)(2,1)S(1)} %collective-permute-done.3.refs_2_.refs_4_), channel_id=1, source_target_pairs={{0,7},{1,0},{2,1},{3,2},{4,3},{5,4},{6,5},{7,6},{8,15},{9,8},{10,9... | collective-permute-start | bytes 1376264 | tf_op jit(solution)/shard_map/ppermute | solution.py:181
  41.9 0.0 collective-permute-done.4.refs_2_
  41.9 0.0 collective-permute-done.5.refs_3_
  41.9 0.8 sum_cores.1
  42.7 14.4 %all-to-all-start = ((bf16[32,40,128]{2,1,0:T(8,128)(2,1)}), bf16[32,40,128]{2,1,0:T(8,128)(2,1)S(1)}, u32[]{:S(2)}, u32[]{:S(2)}) async-start(bf16[32,40,128]{2,1,0:T(8,128)(2,1)} %bitcast), calls=%async_computation | async-start | bytes 655360 | tf_op jit(solution)/shard_map/all_to_all | solution.py:182
  57.2 0.1 dynamic-slice.3
  57.2 0.1 dynamic-slice.4
  57.4 0.1 fusion.denominator_ref
  57.5 0.0 collective-permute-done.6.refs_6_
  57.5 0.0 collective-permute-done.7.refs_5_
  57.5 10.1 %all-to-all-done.pieces_ref = bf16[32,40,128]{2,1,0:T(8,128)(2,1)S(1)} async-done(((bf16[32,40,128]{2,1,0:T(8,128)(2,1)}), bf16[32,40,128]{2,1,0:T(8,128)(2,1)S(1)}, u32[]{:S(2)}, u32[]{:S(2)}) %all-to-all-start) | async-done | bytes 327712 | tf_op jit(solution)/shard_map/all_to_all | solution.py:182
  67.7 0.8 amplitude_piece.1
  68.5 7.4 %all-to-all-start.1 = ((bf16[32,40,128]{2,1,0:T(8,128)(2,1)}), bf16[32,40,128]{2,1,0:T(8,128)(2,1)S(1)}, u32[]{:S(2)}, u32[]{:S(2)}) async-start(bf16[32,40,128]{2,1,0:T(8,128)(2,1)} %amplitude_piece.1), calls=%async_computation.1 | async-start | bytes 655360 | tf_op jit(solution)/shard_map/all_to_all | solution.py:190
  75.9 1.0 slice.99
  76.9 2.1 %collective-permute-start.8 = (bf16[448,256]{1,0:T(8,128)(2,1)S(1)}, bf16[448,256]{1,0:T(8,128)(2,1)S(1)}, u32[]{:S(2)}, u32[]{:S(2)}) collective-permute-start(bf16[448,256]{1,0:T(8,128)(2,1)S(1)} %slice.98), channel_id=1, source_target_pairs={{0,1},{1,2},{2,3},{3,4},{4,5},{5,6},{6,7},{7,0},{8,9},{9,10},{10,1... | collective-permute-start | bytes 688136 | tf_op jit(solution)/shard_map/ppermute | solution.py:188
  79.0 4.4 %collective-permute-start.9 = (bf16[448,256]{1,0:T(8,128)(2,1)S(1)}, bf16[448,256]{1,0:T(8,128)(2,1)}, u32[]{:S(2)}, u32[]{:S(2)}) collective-permute-start(bf16[448,256]{1,0:T(8,128)(2,1)S(1)} %slice.99), channel_id=1, source_target_pairs={{0,7},{1,0},{2,1},{3,2},{4,3},{5,4},{6,5},{7,6},{8,15},{9,8},{10,9... | collective-permute-start | bytes 688136 | tf_op jit(solution)/shard_map/ppermute | solution.py:189
  83.4 2.5 %collective-permute-done.8 = bf16[448,256]{1,0:T(8,128)(2,1)S(1)} collective-permute-done((bf16[448,256]{1,0:T(8,128)(2,1)S(1)}, bf16[448,256]{1,0:T(8,128)(2,1)S(1)}, u32[]{:S(2)}, u32[]{:S(2)}) %collective-permute-start.8) | collective-permute-done | bytes 229408 | tf_op jit(solution)/shard_map/ppermute | solution.py:188
  85.9 2.2 %collective-permute-done.9 = bf16[448,256]{1,0:T(8,128)(2,1)} collective-permute-done((bf16[448,256]{1,0:T(8,128)(2,1)S(1)}, bf16[448,256]{1,0:T(8,128)(2,1)}, u32[]{:S(2)}, u32[]{:S(2)}) %collective-permute-start.9) | collective-permute-done | bytes 229408 | tf_op jit(solution)/shard_map/ppermute | solution.py:189
  88.1 0.0 all-to-all-done.1
  88.1 0.1 fusion.10
  88.2 3.8 %collective-permute-start.12 = (bf16[2,2,128,128]{3,2,1,0:T(8,128)(2,1)S(1)}, bf16[2,2,128,128]{3,2,1,0:T(8,128)(2,1)S(1)}, u32[]{:S(2)}, u32[]{:S(2)}) collective-permute-start(bf16[2,2,128,128]{3,2,1,0:T(8,128)(2,1)S(1)} %get-tuple-element.31), channel_id=1, source_target_pairs={{0,2},{1,3},{2,4},{3,5},{4,6},{5,7},{6,0},{7,1},{8,10},{9,11},{10,... | collective-permute-start | bytes 393224 | tf_op jit(solution)/shard_map/ppermute | solution.py:199
  92.1 3.5 %collective-permute-start.11 = (bf16[2,2,128,128]{3,2,1,0:T(8,128)(2,1)S(1)}, bf16[2,2,128,128]{3,2,1,0:T(8,128)(2,1)S(1)}, u32[]{:S(2)}, u32[]{:S(2)}) collective-permute-start(bf16[2,2,128,128]{3,2,1,0:T(8,128)(2,1)S(1)} %get-tuple-element.32), channel_id=1, source_target_pairs={{0,7},{1,0},{2,1},{3,2},{4,3},{5,4},{6,5},{7,6},{8,15},{9,8},{10,9... | collective-permute-start | bytes 393224 | tf_op jit(solution)/shard_map/ppermute | solution.py:198
  95.6 3.1 %collective-permute-start.10 = (bf16[2,2,128,128]{3,2,1,0:T(8,128)(2,1)S(1)}, bf16[2,2,128,128]{3,2,1,0:T(8,128)(2,1)S(1)}, u32[]{:S(2)}, u32[]{:S(2)}) collective-permute-start(bf16[2,2,128,128]{3,2,1,0:T(8,128)(2,1)S(1)} %get-tuple-element.33), channel_id=1, source_target_pairs={{0,1},{1,2},{2,3},{3,4},{4,5},{5,6},{6,7},{7,0},{8,9},{9,10},{10,1... | collective-permute-start | bytes 393224 | tf_op jit(solution)/shard_map/ppermute | solution.py:197
  98.8 0.0 collective-permute-done.12.refs_11_
  98.8 0.5 collective-permute-done.11.refs_10_
  99.2 3.3 %collective-permute-done.10.refs_9_ = bf16[2,2,128,128]{3,2,1,0:T(8,128)(2,1)S(1)} collective-permute-done((bf16[2,2,128,128]{3,2,1,0:T(8,128)(2,1)S(1)}, bf16[2,2,128,128]{3,2,1,0:T(8,128)(2,1)S(1)}, u32[]{:S(2)}, u32[]{:S(2)}) %collective-permute-start.10) | collective-permute-done | bytes 131104 | tf_op jit(solution)/shard_map/ppermute | solution.py:197
  102.5 0.1 pad_maximum_fusion
  102.6 6.0 %collective-permute-start.13 = (bf16[8,2,128,128]{3,2,1,0:T(8,128)(2,1)S(1)}, bf16[8,2,128,128]{3,2,1,0:T(8,128)(2,1)S(1)}, u32[]{:S(2)}, u32[]{:S(2)}) collective-permute-start(bf16[8,2,128,128]{3,2,1,0:T(8,128)(2,1)S(1)} %pad_maximum_fusion), channel_id=1, source_target_pairs={{0,8},{8,0},{1,9},{9,1},{2,10},{10,2},{3,11},{11,3},{4,12},{12,4},... | collective-permute-start | bytes 1572872 | tf_op jit(solution)/shard_map/ppermute | solution.py:201
  108.6 1.0 pad_maximum_fusion.1.refs_7_
  109.6 0.5 collective-permute-done.13
  110.2 0.0 copy-start.2
  110.2 0.6 copy-done.2
  110.9 5.8 %gamma_rows.1 = bf16[896,256]{1,0:T(8,128)(2,1)} custom-call(bf16[896,256]{1,0:T(8,128)(2,1)S(1)} %copy-done.1, bf16[896,256]{1,0:T(8,128)(2,1)S(1)} %collective-permute-done.refs_2_.refs_1_, bf16[896,256]{1,0:T(8,128)(2,1)S(1)} %collective-permute-done.1.refs_0_.refs_1_.refs_2_, bf16[896,256]{1,0:T(8,128)(2,1)S(1)} %collective-permute-done.2.refs_0_.refs_3_, ...), custom_call_target="tpu_custom_call" | custom-call | tf_op jit(solution)/shard_map/gamma_rows/pallas_call | solution.py:136
  (21 shorter events, 0.3 us)
Async XLA Ops:
  0.0 10.7 %copy-start = (f32[20096]{0:T(1024)S(1)}, f32[20096]{0:T(1024)}, u32[]{:S(2)}) copy-start(f32[20096]{0:T(1024)} %param.8) | copy-start | bytes 241156
  0.0 21.5 %copy-start.1 = (bf16[896,256]{1,0:T(8,128)(2,1)S(1)}, bf16[896,256]{1,0:T(8,128)(2,1)}, u32[]{:S(2)}) copy-start(bf16[896,256]{1,0:T(8,128)(2,1)} %refs_0_.1) | copy-start | bytes 1376260
  0.0 12.1 %collective-permute-start.1 = (bf16[896,256]{1,0:T(8,128)(2,1)}, bf16[896,256]{1,0:T(8,128)(2,1)S(1)}, u32[]{:S(2)}, u32[]{:S(2)}) collective-permute-start(bf16[896,256]{1,0:T(8,128)(2,1)} %refs_0_.1), channel_id=1, source_target_pairs={{0,1},{1,2},{2,3},{3,4},{4,5},{5,6},{6,7},{7,0},{8,9},{9,10},{10,1... | collective-permute-start | bytes 1376264 | tf_op jit(solution)/shard_map/ppermute | solution.py:157
  4.2 13.0 %collective-permute-start = (bf16[896,256]{1,0:T(8,128)(2,1)}, bf16[896,256]{1,0:T(8,128)(2,1)S(1)}, u32[]{:S(2)}, u32[]{:S(2)}) collective-permute-start(bf16[896,256]{1,0:T(8,128)(2,1)} %refs_0_.1), channel_id=1, source_target_pairs={{0,7},{1,0},{2,1},{3,2},{4,3},{5,4},{6,5},{7,6},{8,15},{9,8},{10,9... | collective-permute-start | bytes 1376264 | tf_op jit(solution)/shard_map/ppermute | solution.py:158
  12.1 16.4 %collective-permute-start.2 = (bf16[896,256]{1,0:T(8,128)(2,1)S(1)}, bf16[896,256]{1,0:T(8,128)(2,1)S(1)}, u32[]{:S(2)}, u32[]{:S(2)}) collective-permute-start(bf16[896,256]{1,0:T(8,128)(2,1)S(1)} %collective-permute-done.1.refs_0_.refs_1_.refs_2_), channel_id=1, source_target_pairs={{0,1},{1,2},{2,3},{3,4},{4,5},{5,6},{6,7},{7,0},{8,9},{9,10},{10,1... | collective-permute-start | bytes 1376264 | tf_op jit(solution)/shard_map/ppermute | solution.py:157
  17.1 11.6 %collective-permute-start.3 = (bf16[896,256]{1,0:T(8,128)(2,1)S(1)}, bf16[896,256]{1,0:T(8,128)(2,1)S(1)}, u32[]{:S(2)}, u32[]{:S(2)}) collective-permute-start(bf16[896,256]{1,0:T(8,128)(2,1)S(1)} %collective-permute-done.refs_2_.refs_1_), channel_id=1, source_target_pairs={{0,7},{1,0},{2,1},{3,2},{4,3},{5,4},{6,5},{7,6},{8,15},{9,8},{10,9... | collective-permute-start | bytes 1376264 | tf_op jit(solution)/shard_map/ppermute | solution.py:158
  22.2 19.7 %collective-permute-start.4 = (bf16[3,2,128,128]{3,2,1,0:T(8,128)(2,1)S(1)}, bf16[3,2,128,128]{3,2,1,0:T(8,128)(2,1)S(1)}, u32[]{:S(2)}, u32[]{:S(2)}) collective-permute-start(bf16[3,2,128,128]{3,2,1,0:T(8,128)(2,1)S(1)} %get-tuple-element.18), channel_id=1, source_target_pairs={{0,8},{8,0},{1,9},{9,1},{2,10},{10,2},{3,11},{11,3},{4,12},{12,4},... | collective-permute-start | bytes 589832 | tf_op jit(solution)/shard_map/ppermute | solution.py:175
  29.2 12.6 %collective-permute-start.5 = (bf16[2,2,128,128]{3,2,1,0:T(8,128)(2,1)S(1)}, bf16[2,2,128,128]{3,2,1,0:T(8,128)(2,1)S(1)}, u32[]{:S(2)}, u32[]{:S(2)}) collective-permute-start(bf16[2,2,128,128]{3,2,1,0:T(8,128)(2,1)S(1)} %get-tuple-element.19), channel_id=1, source_target_pairs={{0,8},{8,0},{1,9},{9,1},{2,10},{10,2},{3,11},{11,3},{4,12},{12,4},... | collective-permute-start | bytes 393224 | tf_op jit(solution)/shard_map/ppermute | solution.py:177
  35.0 22.5 %collective-permute-start.6 = (bf16[896,256]{1,0:T(8,128)(2,1)S(1)}, bf16[896,256]{1,0:T(8,128)(2,1)S(1)}, u32[]{:S(2)}, u32[]{:S(2)}) collective-permute-start(bf16[896,256]{1,0:T(8,128)(2,1)S(1)} %collective-permute-done.2.refs_0_.refs_3_), channel_id=1, source_target_pairs={{0,1},{1,2},{2,3},{3,4},{4,5},{5,6},{6,7},{7,0},{8,9},{9,10},{10,1... | collective-permute-start | bytes 1376264 | tf_op jit(solution)/shard_map/ppermute | solution.py:180
  39.0 18.5 %collective-permute-start.7 = (bf16[896,256]{1,0:T(8,128)(2,1)S(1)}, bf16[896,256]{1,0:T(8,128)(2,1)}, u32[]{:S(2)}, u32[]{:S(2)}) collective-permute-start(bf16[896,256]{1,0:T(8,128)(2,1)S(1)} %collective-permute-done.3.refs_2_.refs_4_), channel_id=1, source_target_pairs={{0,7},{1,0},{2,1},{3,2},{4,3},{5,4},{6,5},{7,6},{8,15},{9,8},{10,9... | collective-permute-start | bytes 1376264 | tf_op jit(solution)/shard_map/ppermute | solution.py:181
  42.7 25.0 %all-to-all-start = ((bf16[32,40,128]{2,1,0:T(8,128)(2,1)}), bf16[32,40,128]{2,1,0:T(8,128)(2,1)S(1)}, u32[]{:S(2)}, u32[]{:S(2)}) async-start(bf16[32,40,128]{2,1,0:T(8,128)(2,1)} %bitcast), calls=%async_computation | async-start | bytes 655360 | tf_op jit(solution)/shard_map/all_to_all | solution.py:182
  68.5 19.7 %all-to-all-start.1 = ((bf16[32,40,128]{2,1,0:T(8,128)(2,1)}), bf16[32,40,128]{2,1,0:T(8,128)(2,1)S(1)}, u32[]{:S(2)}, u32[]{:S(2)}) async-start(bf16[32,40,128]{2,1,0:T(8,128)(2,1)} %amplitude_piece.1), calls=%async_computation.1 | async-start | bytes 655360 | tf_op jit(solution)/shard_map/all_to_all | solution.py:190
  76.9 9.0 %collective-permute-start.8 = (bf16[448,256]{1,0:T(8,128)(2,1)S(1)}, bf16[448,256]{1,0:T(8,128)(2,1)S(1)}, u32[]{:S(2)}, u32[]{:S(2)}) collective-permute-start(bf16[448,256]{1,0:T(8,128)(2,1)S(1)} %slice.98), channel_id=1, source_target_pairs={{0,1},{1,2},{2,3},{3,4},{4,5},{5,6},{6,7},{7,0},{8,9},{9,10},{10,1... | collective-permute-start | bytes 688136 | tf_op jit(solution)/shard_map/ppermute | solution.py:188
  79.0 9.1 %collective-permute-start.9 = (bf16[448,256]{1,0:T(8,128)(2,1)S(1)}, bf16[448,256]{1,0:T(8,128)(2,1)}, u32[]{:S(2)}, u32[]{:S(2)}) collective-permute-start(bf16[448,256]{1,0:T(8,128)(2,1)S(1)} %slice.99), channel_id=1, source_target_pairs={{0,7},{1,0},{2,1},{3,2},{4,3},{5,4},{6,5},{7,6},{8,15},{9,8},{10,9... | collective-permute-start | bytes 688136 | tf_op jit(solution)/shard_map/ppermute | solution.py:189
  88.2 10.5 %collective-permute-start.12 = (bf16[2,2,128,128]{3,2,1,0:T(8,128)(2,1)S(1)}, bf16[2,2,128,128]{3,2,1,0:T(8,128)(2,1)S(1)}, u32[]{:S(2)}, u32[]{:S(2)}) collective-permute-start(bf16[2,2,128,128]{3,2,1,0:T(8,128)(2,1)S(1)} %get-tuple-element.31), channel_id=1, source_target_pairs={{0,2},{1,3},{2,4},{3,5},{4,6},{5,7},{6,0},{7,1},{8,10},{9,11},{10,... | collective-permute-start | bytes 393224 | tf_op jit(solution)/shard_map/ppermute | solution.py:199
  92.1 7.2 %collective-permute-start.11 = (bf16[2,2,128,128]{3,2,1,0:T(8,128)(2,1)S(1)}, bf16[2,2,128,128]{3,2,1,0:T(8,128)(2,1)S(1)}, u32[]{:S(2)}, u32[]{:S(2)}) collective-permute-start(bf16[2,2,128,128]{3,2,1,0:T(8,128)(2,1)S(1)} %get-tuple-element.32), channel_id=1, source_target_pairs={{0,7},{1,0},{2,1},{3,2},{4,3},{5,4},{6,5},{7,6},{8,15},{9,8},{10,9... | collective-permute-start | bytes 393224 | tf_op jit(solution)/shard_map/ppermute | solution.py:198
  95.6 6.9 %collective-permute-start.10 = (bf16[2,2,128,128]{3,2,1,0:T(8,128)(2,1)S(1)}, bf16[2,2,128,128]{3,2,1,0:T(8,128)(2,1)S(1)}, u32[]{:S(2)}, u32[]{:S(2)}) collective-permute-start(bf16[2,2,128,128]{3,2,1,0:T(8,128)(2,1)S(1)} %get-tuple-element.33), channel_id=1, source_target_pairs={{0,1},{1,2},{2,3},{3,4},{4,5},{5,6},{6,7},{7,0},{8,9},{9,10},{10,1... | collective-permute-start | bytes 393224 | tf_op jit(solution)/shard_map/ppermute | solution.py:197
  102.6 7.5 %collective-permute-start.13 = (bf16[8,2,128,128]{3,2,1,0:T(8,128)(2,1)S(1)}, bf16[8,2,128,128]{3,2,1,0:T(8,128)(2,1)S(1)}, u32[]{:S(2)}, u32[]{:S(2)}) collective-permute-start(bf16[8,2,128,128]{3,2,1,0:T(8,128)(2,1)S(1)} %pad_maximum_fusion), channel_id=1, source_target_pairs={{0,8},{8,0},{1,9},{9,1},{2,10},{10,2},{3,11},{11,3},{4,12},{12,4},... | collective-permute-start | bytes 1572872 | tf_op jit(solution)/shard_map/ppermute | solution.py:201
  110.2 0.7 copy-start.2

commit v3 on v2

--- a/solution.py
+++ b/solution.py
@@ -26,11 +26,10 @@
     (-3, False, 3, 0),
     (4, False, 3, 1),
 )
-ROWS = 128
+ROWS = 224
 VMEM_LIMIT = 48 * 1024 * 1024
 bf16, f32 = jnp.bfloat16, jnp.float32
 in_vmem = pl.BlockSpec(memory_space=pltpu.VMEM)
-in_smem = pl.BlockSpec(memory_space=pltpu.SMEM)
 
 
 def ring(size, step):
@@ -99,50 +98,54 @@
     )(pieces, denominator)
 
 
-def gamma_rows(blocks, last, mine, theirs, tile_exponent):
+def gamma_rows(blocks, last, mine, theirs, scales):
     rows, width = blocks[0].shape
     names = [q for q, *_ in ORDER if q != 4]
-    steps = rows // ROWS
+    half = rows // len(last)
 
     def kernel(*refs):
         block = dict(zip(names, refs))
-        block[4] = refs[len(names)]
-        n = len(names) + 1
-        own, other = refs[n : n + 4], refs[n + 4 : n + 8]
-        exponent, out, matrix = refs[n + 8 :]
-        me = lax.axis_index("pair")
+        n = len(names)
+        last_refs, refs = refs[n : n + len(last)], refs[n + len(last) :]
+        own, other, scale, out, matrix = refs[:4], refs[4], refs[5], refs[6], refs[7]
         core = lax.axis_index("core")
-
-        @pl.when(pl.program_id(0) == 0)
-        def _():
-            for i, (q, transposed, array, k) in enumerate(ORDER):
-                for source, part in ((own, core), (other, 1 - core)):
-                    for h in (0, 1):
-                        tile = 2 * lax.rem(me + q + NPAIR, NPAIR) + (h if transposed else part)
-                        level = exponent[tile]
-                        scale = jnp.where(level == -1, 0.5, jnp.where(level == 1, 2.0, 1.0))
-                        values = source[array][k, h].astype(f32) * scale.astype(f32)
-                        row = pl.multiple_of(part * TS, TS)
-                        matrix[i, pl.ds(row, TS), h * TS : (h + 1) * TS] = values.astype(bf16)
-
-        total = None
-        for i, (q, transposed, _, _) in enumerate(ORDER):
-            dims = (((1,), (1 if transposed else 0,)), ((), ()))
-            term = lax.dot_general(block[q][...], matrix[i], dims, preferred_element_type=f32)
-            total = term if total is None else total + term
-        out[...] = total.astype(bf16)
-
-    row_block = pl.BlockSpec((ROWS, width), lambda i: (i, 0))
-    return pl.pallas_call(
-        kernel,
-        grid=(steps,),
+        for i, (q, transposed, array, k) in enumerate(ORDER):
+            for part, values in ((core, own[array].at[k]), (1 - core, other.at[2 * array + k])):
+                place = pl.ds(pl.multiple_of(part * TS, TS), TS)
+                for h in (0, 1):
+                    tile = values[h].astype(f32)
+                    if transposed:
+                        tile = tile.T * scale[2 * i + h : 2 * i + h + 1]
+                        matrix[i, h * TS : (h + 1) * TS, place] = tile.astype(bf16)
+                    else:
+                        tile = tile * scale[pl.ds(2 * i + part, 1)]
+                        matrix[i, place, h * TS : (h + 1) * TS] = tile.astype(bf16)
+
+        for start in range(0, rows, ROWS):
+            total = None
+            for i, (q, *_) in enumerate(ORDER):
+                if q == 4:
+                    left = [
+                        last_refs[j][max(start - j * half, 0) : start + ROWS - j * half]
+                        for j in range(len(last))
+                        if start < (j + 1) * half and start + ROWS > j * half
+                    ]
+                    left = left[0] if len(left) == 1 else jnp.concatenate(left)
+                else:
+                    left = block[q][start : start + ROWS]
+                term = jnp.dot(left, matrix[i], preferred_element_type=f32)
+                total = term if total is None else total + term
+            out[start : start + ROWS] = total.astype(bf16)
+
+    return pl.pallas_call(
+        kernel,
         out_shape=jax.ShapeDtypeStruct((rows, width), bf16),
-        in_specs=[row_block] * 8 + [in_vmem] * 8 + [in_smem],
-        out_specs=row_block,
+        in_specs=[in_vmem] * (len(names) + len(last) + 6),
+        out_specs=in_vmem,
         scratch_shapes=[pltpu.VMEM((len(ORDER), WIDTH, WIDTH), bf16)],
         compiler_params=pltpu.CompilerParams(vmem_limit_bytes=VMEM_LIMIT),
         name="gamma_rows",
-    )(*[blocks[q] for q in names], last, *mine, *theirs, tile_exponent)
+    )(*[blocks[q] for q in names], *last, *mine, theirs, scales)
 
 
 def body(three_index, occupied_energy, virtual_energy, tile_occupied, tile_virtual, tile_exponent):
@@ -170,6 +173,8 @@
         / (row_of[:, None, TS:, None] * column_of[:, :, None, TS:])
     ).reshape(-1, TS)
     own_denominator = lax.dynamic_slice_in_dim(denominator, slot * PIECE, PIECE)
+    turned = lax.dynamic_slice_in_dim(table[:, TS:], 2 * me, NT).reshape(NPAIR, 2, TS)
+    scales = jnp.concatenate([turned[q % NPAIR] for q, *_ in ORDER])
 
     own_early, other_early = coulomb_pairs(block, EARLY)
     got_early = lax.ppermute(other_early, "core", swap)
@@ -177,6 +182,9 @@
     got_late = lax.ppermute(other_late, "core", swap)
     summed = sum_cores((own_early, own_late), (got_early, got_late))
 
+    summed, block[-2], block[2], scales = lax.optimization_barrier(
+        (summed, block[-2], block[2], scales)
+    )
     block[-3] = lax.ppermute(block[-2], "pair", up)
     block[3] = lax.ppermute(block[2], "pair", down)
     pieces = lax.all_to_all(summed.reshape(NXZ, PIECE, TS), ("x", "z"), 0, 0)
@@ -189,7 +197,6 @@
     last_lower = lax.ppermute(block[3][half:], "pair", down)
     halves = lax.all_to_all(amplitude_piece(pieces, own_denominator), ("x", "z"), 0, 0)
     halves, last_upper, last_lower = lax.optimization_barrier((halves, last_upper, last_lower))
-    last = jnp.concatenate([last_upper, last_lower])
 
     halves = halves.reshape(len(PAIRS), 2, TS, TS)
     mine = (
@@ -199,8 +206,7 @@
         lax.ppermute(halves[3:5], "pair", ring(NPAIR, 2)),
     )
     theirs = lax.ppermute(jnp.concatenate(mine), "core", swap)
-    theirs = tuple(theirs[2 * i : 2 * i + 2] for i in range(4))
-    return gamma_rows(block, last, mine, theirs, tile_exponent)
+    return gamma_rows(block, (last_upper, last_lower), mine, theirs, scales)
 
 
 def solution(mesh):

time: 118 us -> 121 us (1.025)
  local copies, waits for them, and re-layouts: 4.08 us -> 12 us
  other arithmetic: 2.56 us -> 0.25 us
  Pallas kernels: 8.51 us -> 6.51 us
    all_to_all x1, waiting for transfers between devices: 10.1 us -> 0.01 us  [body(): pieces = lax.all_to_all(summed.reshape(NXZ, PIECE, TS), ('x', 'z'), 0, 0)]
    ppermute x1, waiting for transfers between devices: 0.01 us -> 7.04 us  [body(): block[-3] = lax.ppermute(block[-2], 'pair', up)]
    unnamed x10 -> x20, local copies, waits for them, and re-layouts: 0.69 us -> 4.25 us
    pallas_call x1, Pallas kernels: 5.83 us -> 3.16 us  [gamma_rows(): pl.pallas_call(kernel, out_shape=jax.ShapeDtypeStruct((rows, width), bf16...]
    ppermute x1, starting transfers between devices: 4.38 us -> 1.92 us  [body(): last_lower = lax.ppermute(block[3][half:], 'pair', down)]
    ppermute x1, starting transfers between devices: 2.12 us -> 4.57 us  [body(): last_upper = lax.ppermute(block[-3][:half], 'pair', up)]
    ppermute x1, starting transfers between devices: 5.77 us -> 3.58 us  [body(): got_late = lax.ppermute(other_late, 'core', swap)]
    ppermute x1, waiting for transfers between devices: 0.01 us -> 1.91 us  [body(): block[3] = lax.ppermute(block[2], 'pair', down)]
  transfers between devices with their start and end apart: 16 -> 16, of which waited for: 8 -> 8; matrix products, arithmetic and copies ran while one was open for 5% -> 8% of each run, Pallas kernels for 2% -> 1%
where the time goes in v3:
time: 121 us
  starting transfers between devices  80.2 us (66%)
  waiting for transfers between devices  21.3 us (18%)
  local copies, waits for them, and re-layouts  12 us (10%)
  Pallas kernels  6.51 us (5%)
    all_to_all x1, starting transfers between devices, body(): pieces = lax.all_to_all(summed.reshape(NXZ, PIECE, TS), ('x', 'z'), 0, 0)  14 us
    ppermute x2, starting transfers between devices, body(): block[-d] = lax.ppermute(block[1 - d], 'pair', up)  9.15 us
    all_to_all x1, starting transfers between devices, body(): lax.all_to_all(amplitude_piece(pieces, own_denominator), ('x', 'z'), 0, 0)  9.02 us
    ppermute x2, starting transfers between devices, body(): block[d] = lax.ppermute(block[d - 1], 'pair', down)  8.15 us
    ppermute x1, waiting for transfers between devices, body(): block[-3] = lax.ppermute(block[-2], 'pair', up)  7.04 us
    ppermute x1, starting transfers between devices, body(): theirs = lax.ppermute(jnp.concatenate(mine), 'core', swap)  6.7 us
    ppermute x1, starting transfers between devices, body(): got_early = lax.ppermute(other_early, 'core', swap)  6.29 us
    ppermute x1, starting transfers between devices, body(): last_upper = lax.ppermute(block[-3][:half], 'pair', up)  4.57 us
  transfers between devices with their start and end apart: 16, of which 8 were waited for; matrix products, arithmetic and copies ran while one was open for 8% of the time, Pallas kernels for 1%

profile of v3, /device:TPU:1, one launch (start us, length us, event | category | flops | bytes accessed | tf_op | source)
XLA Modules:
  0.0 120.5 jit_solution(6160047136210032744)
XLA Ops:
  0.0 0.0 copy-start
  0.0 4.2 %collective-permute-start.1 = (bf16[896,256]{1,0:T(8,128)(2,1)}, bf16[896,256]{1,0:T(8,128)(2,1)S(1)}, u32[]{:S(2)}, u32[]{:S(2)}) collective-permute-start(bf16[896,256]{1,0:T(8,128)(2,1)} %refs_0_.1), channel_id=1, source_target_pairs={{0,1},{1,2},{2,3},{3,4},{4,5},{5,6},{6,7},{7,0},{8,9},{9,10},{10,1... | collective-permute-start | bytes 1376264 | tf_op jit(solution)/shard_map/ppermute | solution.py:160
  4.2 3.8 %collective-permute-start = (bf16[896,256]{1,0:T(8,128)(2,1)}, bf16[896,256]{1,0:T(8,128)(2,1)S(1)}, u32[]{:S(2)}, u32[]{:S(2)}) collective-permute-start(bf16[896,256]{1,0:T(8,128)(2,1)} %refs_0_.1), channel_id=1, source_target_pairs={{0,7},{1,0},{2,1},{3,2},{4,3},{5,4},{6,5},{7,6},{8,15},{9,8},{10,9... | collective-permute-start | bytes 1376264 | tf_op jit(solution)/shard_map/ppermute | solution.py:161
  8.0 0.6 copy-done.5
  8.7 0.0 copy-done.6
  8.7 0.0 copy-start.4
  8.7 0.0 copy-start.1
  8.7 0.6 copy-done.4
  9.3 0.7 gather_fusion.1
  10.0 0.6 gather_fusion
  10.6 0.0 copy-start.7
  10.6 0.1 broadcast_subtract_fusion
  10.7 0.6 copy-done.7
  11.2 0.1 broadcast_in_dim.34
  11.4 0.8 collective-permute-done.1.refs_0_.refs_1_.refs_2_
  12.1 5.0 %collective-permute-start.2 = (bf16[896,256]{1,0:T(8,128)(2,1)S(1)}, bf16[896,256]{1,0:T(8,128)(2,1)S(1)}, u32[]{:S(2)}, u32[]{:S(2)}) collective-permute-start(bf16[896,256]{1,0:T(8,128)(2,1)S(1)} %collective-permute-done.1.refs_0_.refs_1_.refs_2_), channel_id=1, source_target_pairs={{0,1},{1,2},{2,3},{3,4},{4,5},{5,6},{6,7},{7,0},{8,9},{9,10},{10,1... | collective-permute-start | bytes 1376264 | tf_op jit(solution)/shard_map/ppermute | solution.py:160
  17.1 0.0 collective-permute-done.refs_2_.refs_1_
  17.1 4.3 %collective-permute-start.3 = (bf16[896,256]{1,0:T(8,128)(2,1)S(1)}, bf16[896,256]{1,0:T(8,128)(2,1)S(1)}, u32[]{:S(2)}, u32[]{:S(2)}) collective-permute-start(bf16[896,256]{1,0:T(8,128)(2,1)S(1)} %collective-permute-done.refs_2_.refs_1_), channel_id=1, source_target_pairs={{0,7},{1,0},{2,1},{3,2},{4,3},{5,4},{6,5},{7,6},{8,15},{9,8},{10,9... | collective-permute-start | bytes 1376264 | tf_op jit(solution)/shard_map/ppermute | solution.py:161
  21.5 0.6 constant_dynamic-update-slice_fusion.4
  22.1 0.6 constant_dynamic-slice_fusion.6
  22.7 0.6 constant_dynamic-slice_fusion.12
  23.3 1.3 %coulomb_pairs.2 = (f32[3,2,128,128]{3,2,1,0:T(8,128)S(1)}, bf16[3,2,128,128]{3,2,1,0:T(8,128)(2,1)}) custom-call(bf16[896,256]{1,0:T(8,128)(2,1)S(1)} %collective-permute-done.1.refs_0_.refs_1_.refs_2_, bf16[896,256]{1,0:T(8,128)(2,1)S(1)} %copy-done.1, bf16[896,256]{1,0:T(8,128)(2,1)S(1)} %collective-permute-done.refs_2_.refs_1_), custom_call_target="tpu_custom_call" | custom-call | tf_op jit(solution)/shard_map/coulomb_pairs/pallas_call | solution.py:56
  24.6 6.3 %collective-permute-start.4 = (bf16[3,2,128,128]{3,2,1,0:T(8,128)(2,1)}, bf16[3,2,128,128]{3,2,1,0:T(8,128)(2,1)S(1)}, u32[]{:S(2)}, u32[]{:S(2)}) collective-permute-start(bf16[3,2,128,128]{3,2,1,0:T(8,128)(2,1)} %get-tuple-element.22), channel_id=1, source_target_pairs={{0,8},{8,0},{1,9},{9,1},{2,10},{10,2},{3,11},{11,3},{4,12},{12,4},... | collective-permute-start | bytes 589832 | tf_op jit(solution)/shard_map/ppermute | solution.py:180
  30.9 0.0 collective-permute-done.2.refs_0_.refs_3_
  30.9 0.0 collective-permute-done.3.refs_2_.refs_4_
  30.9 0.5 coulomb_pairs.3
  31.4 3.6 %collective-permute-start.5 = (bf16[2,2,128,128]{3,2,1,0:T(8,128)(2,1)S(1)}, bf16[2,2,128,128]{3,2,1,0:T(8,128)(2,1)S(1)}, u32[]{:S(2)}, u32[]{:S(2)}) collective-permute-start(bf16[2,2,128,128]{3,2,1,0:T(8,128)(2,1)S(1)} %get-tuple-element.23), channel_id=1, source_target_pairs={{0,8},{8,0},{1,9},{9,1},{2,10},{10,2},{3,11},{11,3},{4,12},{12,4},... | collective-permute-start | bytes 393224 | tf_op jit(solution)/shard_map/ppermute | solution.py:182
  35.0 0.6 constant_dynamic-update-slice_fusion.3
  35.6 1.4 %concatenate.15.refs_14_ = f32[16,128]{1,0:T(8,128)S(1)} concatenate(f32[4,128]{1,0:T(4,128)} %get-tuple-element.44, f32[2,128]{1,0:T(2,128)} %get-tuple-element.42, f32[2,128]{1,0:T(2,128)} %get-tuple-element.41, f32[4,128]{1,0:T(4,128)} %get-tuple-element.43, f32[2,128]{1,0:T(2,128)} %get-tuple-element.40, f32[2,128]{1,0:T(2,128)} %get-tuple-element.39), dimensions={0} | concatenate | bytes 16384 | tf_op jit(solution)/shard_map/concatenate | solution.py:177
  37.0 0.6 constant_dynamic-update-slice_fusion.2
  37.6 0.0 collective-permute-done.4.refs_2_
  37.6 0.0 collective-permute-done.5.refs_3_
  37.6 0.8 sum_cores.1
  38.4 14.0 %all-to-all-start = ((bf16[32,40,128]{2,1,0:T(8,128)(2,1)}), bf16[32,40,128]{2,1,0:T(8,128)(2,1)S(1)}, u32[]{:S(2)}, u32[]{:S(2)}) async-start(bf16[32,40,128]{2,1,0:T(8,128)(2,1)} %bitcast.1), calls=%async_computation | async-start | bytes 655360 | tf_op jit(solution)/shard_map/all_to_all | solution.py:190
  52.4 0.6 constant_dynamic-update-slice_fusion.1
  53.0 2.8 %collective-permute-start.6 = (bf16[896,256]{1,0:T(8,128)(2,1)S(1)}, bf16[896,256]{1,0:T(8,128)(2,1)S(1)}, u32[]{:S(2)}, u32[]{:S(2)}) collective-permute-start(bf16[896,256]{1,0:T(8,128)(2,1)S(1)} %collective-permute-done.2.refs_0_.refs_3_), channel_id=1, source_target_pairs={{0,1},{1,2},{2,3},{3,4},{4,5},{5,6},{6,7},{7,0},{8,9},{9,10},{10,1... | collective-permute-start | bytes 1376264 | tf_op jit(solution)/shard_map/ppermute | solution.py:188
  55.8 4.4 %collective-permute-start.7 = (bf16[896,256]{1,0:T(8,128)(2,1)S(1)}, bf16[896,256]{1,0:T(8,128)(2,1)}, u32[]{:S(2)}, u32[]{:S(2)}) collective-permute-start(bf16[896,256]{1,0:T(8,128)(2,1)S(1)} %collective-permute-done.3.refs_2_.refs_4_), channel_id=1, source_target_pairs={{0,7},{1,0},{2,1},{3,2},{4,3},{5,4},{6,5},{7,6},{8,15},{9,8},{10,9... | collective-permute-start | bytes 1376264 | tf_op jit(solution)/shard_map/ppermute | solution.py:189
  60.2 0.6 constant_dynamic-update-slice_fusion
  60.9 0.1 dynamic-slice.12
  60.9 0.1 dynamic-slice.13
  61.0 0.7 fusion.8
  61.8 0.1 fusion.denominator_ref
  61.9 7.0 %collective-permute-done.6.refs_6_ = bf16[896,256]{1,0:T(8,128)(2,1)S(1)} collective-permute-done((bf16[896,256]{1,0:T(8,128)(2,1)S(1)}, bf16[896,256]{1,0:T(8,128)(2,1)S(1)}, u32[]{:S(2)}, u32[]{:S(2)}) %collective-permute-start.6) | collective-permute-done | bytes 458784 | tf_op jit(solution)/shard_map/ppermute | solution.py:188
  68.9 1.9 %collective-permute-done.7.refs_5_ = bf16[896,256]{1,0:T(8,128)(2,1)} collective-permute-done((bf16[896,256]{1,0:T(8,128)(2,1)S(1)}, bf16[896,256]{1,0:T(8,128)(2,1)}, u32[]{:S(2)}, u32[]{:S(2)}) %collective-permute-start.7) | collective-permute-done | bytes 458784 | tf_op jit(solution)/shard_map/ppermute | solution.py:189
  70.9 0.0 all-to-all-done.pieces_ref
  70.9 0.8 amplitude_piece.1
  71.7 9.0 %all-to-all-start.1 = ((bf16[32,40,128]{2,1,0:T(8,128)(2,1)}), bf16[32,40,128]{2,1,0:T(8,128)(2,1)}, u32[]{:S(2)}, u32[]{:S(2)}) async-start(bf16[32,40,128]{2,1,0:T(8,128)(2,1)} %amplitude_piece.1), calls=%async_computation.1 | async-start | bytes 655360 | tf_op jit(solution)/shard_map/all_to_all | solution.py:198
  80.7 1.0 slice.127
  81.7 4.6 %collective-permute-start.8 = (bf16[448,256]{1,0:T(8,128)(2,1)S(1)}, bf16[448,256]{1,0:T(8,128)(2,1)S(1)}, u32[]{:S(2)}, u32[]{:S(2)}) collective-permute-start(bf16[448,256]{1,0:T(8,128)(2,1)S(1)} %slice.126), channel_id=1, source_target_pairs={{0,1},{1,2},{2,3},{3,4},{4,5},{5,6},{6,7},{7,0},{8,9},{9,10},{10,1... | collective-permute-start | bytes 688136 | tf_op jit(solution)/shard_map/ppermute | solution.py:196
  86.2 1.9 %collective-permute-start.9 = (bf16[448,256]{1,0:T(8,128)(2,1)S(1)}, bf16[448,256]{1,0:T(8,128)(2,1)S(1)}, u32[]{:S(2)}, u32[]{:S(2)}) collective-permute-start(bf16[448,256]{1,0:T(8,128)(2,1)S(1)} %slice.127), channel_id=1, source_target_pairs={{0,7},{1,0},{2,1},{3,2},{4,3},{5,4},{6,5},{7,6},{8,15},{9,8},{10,9... | collective-permute-start | bytes 688136 | tf_op jit(solution)/shard_map/ppermute | solution.py:197
  88.2 2.1 %collective-permute-done.8.refs_7_ = bf16[448,256]{1,0:T(8,128)(2,1)S(1)} collective-permute-done((bf16[448,256]{1,0:T(8,128)(2,1)S(1)}, bf16[448,256]{1,0:T(8,128)(2,1)S(1)}, u32[]{:S(2)}, u32[]{:S(2)}) %collective-permute-start.8) | collective-permute-done | bytes 229408 | tf_op jit(solution)/shard_map/ppermute | solution.py:196
  90.3 3.1 %collective-permute-done.9.refs_8_ = bf16[448,256]{1,0:T(8,128)(2,1)S(1)} collective-permute-done((bf16[448,256]{1,0:T(8,128)(2,1)S(1)}, bf16[448,256]{1,0:T(8,128)(2,1)S(1)}, u32[]{:S(2)}, u32[]{:S(2)}) %collective-permute-start.9) | collective-permute-done | bytes 229408 | tf_op jit(solution)/shard_map/ppermute | solution.py:197
  93.4 0.0 all-to-all-done.1
  93.4 1.2 %fusion.7 = (bf16[2,2,128,128]{3,2,1,0:T(8,128)(2,1)S(1)}, bf16[2,2,128,128]{3,2,1,0:T(8,128)(2,1)S(1)}, bf16[2,2,128,128]{3,2,1,0:T(8,128)(2,1)S(1)}, bf16[2,2,128,128]{3,2,1,0:T(8,128)(2,1)S(1)}) fusion(bf16[5,2,128,128]{3,2,1,0:T(8,128)(2,1)} %bitcast.10), kind=kLoop, calls=%fused_computation.38 | loop fusion | bytes 1048576 | tf_op jit(solution)/shard_map/slice | solution.py:206
  94.7 4.3 %collective-permute-start.12 = (bf16[2,2,128,128]{3,2,1,0:T(8,128)(2,1)S(1)}, bf16[2,2,128,128]{3,2,1,0:T(8,128)(2,1)S(1)}, u32[]{:S(2)}, u32[]{:S(2)}) collective-permute-start(bf16[2,2,128,128]{3,2,1,0:T(8,128)(2,1)S(1)} %get-tuple-element.35), channel_id=1, source_target_pairs={{0,2},{1,3},{2,4},{3,5},{4,6},{5,7},{6,0},{7,1},{8,10},{9,11},{10,... | collective-permute-start | bytes 393224 | tf_op jit(solution)/shard_map/ppermute | solution.py:206
  99.0 3.1 %collective-permute-start.11 = (bf16[2,2,128,128]{3,2,1,0:T(8,128)(2,1)S(1)}, bf16[2,2,128,128]{3,2,1,0:T(8,128)(2,1)S(1)}, u32[]{:S(2)}, u32[]{:S(2)}) collective-permute-start(bf16[2,2,128,128]{3,2,1,0:T(8,128)(2,1)S(1)} %get-tuple-element.36), channel_id=1, source_target_pairs={{0,7},{1,0},{2,1},{3,2},{4,3},{5,4},{6,5},{7,6},{8,15},{9,8},{10,9... | collective-permute-start | bytes 393224 | tf_op jit(solution)/shard_map/ppermute | solution.py:205
  102.1 2.2 %collective-permute-start.10 = (bf16[2,2,128,128]{3,2,1,0:T(8,128)(2,1)S(1)}, bf16[2,2,128,128]{3,2,1,0:T(8,128)(2,1)S(1)}, u32[]{:S(2)}, u32[]{:S(2)}) collective-permute-start(bf16[2,2,128,128]{3,2,1,0:T(8,128)(2,1)S(1)} %get-tuple-element.37), channel_id=1, source_target_pairs={{0,1},{1,2},{2,3},{3,4},{4,5},{5,6},{6,7},{7,0},{8,9},{9,10},{10,1... | collective-permute-start | bytes 393224 | tf_op jit(solution)/shard_map/ppermute | solution.py:204
  104.3 0.0 collective-permute-done.12.refs_12_
  104.3 0.7 collective-permute-done.11.refs_11_
  105.0 4.1 %collective-permute-done.10.refs_10_ = bf16[2,2,128,128]{3,2,1,0:T(8,128)(2,1)S(1)} collective-permute-done((bf16[2,2,128,128]{3,2,1,0:T(8,128)(2,1)S(1)}, bf16[2,2,128,128]{3,2,1,0:T(8,128)(2,1)S(1)}, u32[]{:S(2)}, u32[]{:S(2)}) %collective-permute-start.10) | collective-permute-done | bytes 131104 | tf_op jit(solution)/shard_map/ppermute | solution.py:204
  109.1 0.1 pad_maximum_fusion
  109.1 6.7 %collective-permute-start.13 = (bf16[8,2,128,128]{3,2,1,0:T(8,128)(2,1)S(1)}, bf16[8,2,128,128]{3,2,1,0:T(8,128)(2,1)S(1)}, u32[]{:S(2)}, u32[]{:S(2)}) collective-permute-start(bf16[8,2,128,128]{3,2,1,0:T(8,128)(2,1)S(1)} %pad_maximum_fusion), channel_id=1, source_target_pairs={{0,8},{8,0},{1,9},{9,1},{2,10},{10,2},{3,11},{11,3},{4,12},{12,4},... | collective-permute-start | bytes 1572872 | tf_op jit(solution)/shard_map/ppermute | solution.py:208
  115.8 1.5 %collective-permute-done.13.refs_13_ = bf16[8,2,128,128]{3,2,1,0:T(8,128)(2,1)S(1)} collective-permute-done((bf16[8,2,128,128]{3,2,1,0:T(8,128)(2,1)S(1)}, bf16[8,2,128,128]{3,2,1,0:T(8,128)(2,1)S(1)}, u32[]{:S(2)}, u32[]{:S(2)}) %collective-permute-start.13) | collective-permute-done | bytes 524320 | tf_op jit(solution)/shard_map/ppermute | solution.py:208
  117.4 3.2 %gamma_rows.1 = bf16[896,256]{1,0:T(8,128)(2,1)} custom-call(bf16[896,256]{1,0:T(8,128)(2,1)S(1)} %copy-done.1, bf16[896,256]{1,0:T(8,128)(2,1)S(1)} %collective-permute-done.refs_2_.refs_1_, bf16[896,256]{1,0:T(8,128)(2,1)S(1)} %collective-permute-done.1.refs_0_.refs_1_.refs_2_, bf16[896,256]{1,0:T(8,128)(2,1)S(1)} %collective-permute-done.2.refs_0_.refs_3_, ...), custom_call_target="tpu_custom_call" | custom-call | tf_op jit(solution)/shard_map/gamma_rows/pallas_call | solution.py:140
  (26 shorter events, 0.2 us)
Async XLA Ops:
  0.0 10.0 %copy-start = (f32[20096]{0:T(1024)S(1)}, f32[20096]{0:T(1024)}, u32[]{:S(2)}) copy-start(f32[20096]{0:T(1024)} %param.8) | copy-start | bytes 241156
  0.0 12.1 %collective-permute-start.1 = (bf16[896,256]{1,0:T(8,128)(2,1)}, bf16[896,256]{1,0:T(8,128)(2,1)S(1)}, u32[]{:S(2)}, u32[]{:S(2)}) collective-permute-start(bf16[896,256]{1,0:T(8,128)(2,1)} %refs_0_.1), channel_id=1, source_target_pairs={{0,1},{1,2},{2,3},{3,4},{4,5},{5,6},{6,7},{7,0},{8,9},{9,10},{10,1... | collective-permute-start | bytes 1376264 | tf_op jit(solution)/shard_map/ppermute | solution.py:160
  4.2 13.0 %collective-permute-start = (bf16[896,256]{1,0:T(8,128)(2,1)}, bf16[896,256]{1,0:T(8,128)(2,1)S(1)}, u32[]{:S(2)}, u32[]{:S(2)}) collective-permute-start(bf16[896,256]{1,0:T(8,128)(2,1)} %refs_0_.1), channel_id=1, source_target_pairs={{0,7},{1,0},{2,1},{3,2},{4,3},{5,4},{6,5},{7,6},{8,15},{9,8},{10,9... | collective-permute-start | bytes 1376264 | tf_op jit(solution)/shard_map/ppermute | solution.py:161
  8.0 0.7 copy-start.5
  8.0 0.7 copy-start.6
  8.7 0.7 copy-start.4
  8.7 14.6 %copy-start.1 = (bf16[896,256]{1,0:T(8,128)(2,1)S(1)}, bf16[896,256]{1,0:T(8,128)(2,1)}, u32[]{:S(2)}) copy-start(bf16[896,256]{1,0:T(8,128)(2,1)} %refs_0_.1) | copy-start | bytes 1376260
  10.6 0.7 copy-start.7
  12.1 18.8 %collective-permute-start.2 = (bf16[896,256]{1,0:T(8,128)(2,1)S(1)}, bf16[896,256]{1,0:T(8,128)(2,1)S(1)}, u32[]{:S(2)}, u32[]{:S(2)}) collective-permute-start(bf16[896,256]{1,0:T(8,128)(2,1)S(1)} %collective-permute-done.1.refs_0_.refs_1_.refs_2_), channel_id=1, source_target_pairs={{0,1},{1,2},{2,3},{3,4},{4,5},{5,6},{6,7},{7,0},{8,9},{9,10},{10,1... | collective-permute-start | bytes 1376264 | tf_op jit(solution)/shard_map/ppermute | solution.py:160
  17.1 13.8 %collective-permute-start.3 = (bf16[896,256]{1,0:T(8,128)(2,1)S(1)}, bf16[896,256]{1,0:T(8,128)(2,1)S(1)}, u32[]{:S(2)}, u32[]{:S(2)}) collective-permute-start(bf16[896,256]{1,0:T(8,128)(2,1)S(1)} %collective-permute-done.refs_2_.refs_1_), channel_id=1, source_target_pairs={{0,7},{1,0},{2,1},{3,2},{4,3},{5,4},{6,5},{7,6},{8,15},{9,8},{10,9... | collective-permute-start | bytes 1376264 | tf_op jit(solution)/shard_map/ppermute | solution.py:161
  24.6 13.0 %collective-permute-start.4 = (bf16[3,2,128,128]{3,2,1,0:T(8,128)(2,1)}, bf16[3,2,128,128]{3,2,1,0:T(8,128)(2,1)S(1)}, u32[]{:S(2)}, u32[]{:S(2)}) collective-permute-start(bf16[3,2,128,128]{3,2,1,0:T(8,128)(2,1)} %get-tuple-element.22), channel_id=1, source_target_pairs={{0,8},{8,0},{1,9},{9,1},{2,10},{10,2},{3,11},{11,3},{4,12},{12,4},... | collective-permute-start | bytes 589832 | tf_op jit(solution)/shard_map/ppermute | solution.py:180
  31.4 6.2 %collective-permute-start.5 = (bf16[2,2,128,128]{3,2,1,0:T(8,128)(2,1)S(1)}, bf16[2,2,128,128]{3,2,1,0:T(8,128)(2,1)S(1)}, u32[]{:S(2)}, u32[]{:S(2)}) collective-permute-start(bf16[2,2,128,128]{3,2,1,0:T(8,128)(2,1)S(1)} %get-tuple-element.23), channel_id=1, source_target_pairs={{0,8},{8,0},{1,9},{9,1},{2,10},{10,2},{3,11},{11,3},{4,12},{12,4},... | collective-permute-start | bytes 393224 | tf_op jit(solution)/shard_map/ppermute | solution.py:182
  38.4 32.5 %all-to-all-start = ((bf16[32,40,128]{2,1,0:T(8,128)(2,1)}), bf16[32,40,128]{2,1,0:T(8,128)(2,1)S(1)}, u32[]{:S(2)}, u32[]{:S(2)}) async-start(bf16[32,40,128]{2,1,0:T(8,128)(2,1)} %bitcast.1), calls=%async_computation | async-start | bytes 655360 | tf_op jit(solution)/shard_map/all_to_all | solution.py:190
  53.0 16.0 %collective-permute-start.6 = (bf16[896,256]{1,0:T(8,128)(2,1)S(1)}, bf16[896,256]{1,0:T(8,128)(2,1)S(1)}, u32[]{:S(2)}, u32[]{:S(2)}) collective-permute-start(bf16[896,256]{1,0:T(8,128)(2,1)S(1)} %collective-permute-done.2.refs_0_.refs_3_), channel_id=1, source_target_pairs={{0,1},{1,2},{2,3},{3,4},{4,5},{5,6},{6,7},{7,0},{8,9},{9,10},{10,1... | collective-permute-start | bytes 1376264 | tf_op jit(solution)/shard_map/ppermute | solution.py:188
  55.8 15.0 %collective-permute-start.7 = (bf16[896,256]{1,0:T(8,128)(2,1)S(1)}, bf16[896,256]{1,0:T(8,128)(2,1)}, u32[]{:S(2)}, u32[]{:S(2)}) collective-permute-start(bf16[896,256]{1,0:T(8,128)(2,1)S(1)} %collective-permute-done.3.refs_2_.refs_4_), channel_id=1, source_target_pairs={{0,7},{1,0},{2,1},{3,2},{4,3},{5,4},{6,5},{7,6},{8,15},{9,8},{10,9... | collective-permute-start | bytes 1376264 | tf_op jit(solution)/shard_map/ppermute | solution.py:189
  71.7 21.8 %all-to-all-start.1 = ((bf16[32,40,128]{2,1,0:T(8,128)(2,1)}), bf16[32,40,128]{2,1,0:T(8,128)(2,1)}, u32[]{:S(2)}, u32[]{:S(2)}) async-start(bf16[32,40,128]{2,1,0:T(8,128)(2,1)} %amplitude_piece.1), calls=%async_computation.1 | async-start | bytes 655360 | tf_op jit(solution)/shard_map/all_to_all | solution.py:198
  81.7 8.6 %collective-permute-start.8 = (bf16[448,256]{1,0:T(8,128)(2,1)S(1)}, bf16[448,256]{1,0:T(8,128)(2,1)S(1)}, u32[]{:S(2)}, u32[]{:S(2)}) collective-permute-start(bf16[448,256]{1,0:T(8,128)(2,1)S(1)} %slice.126), channel_id=1, source_target_pairs={{0,1},{1,2},{2,3},{3,4},{4,5},{5,6},{6,7},{7,0},{8,9},{9,10},{10,1... | collective-permute-start | bytes 688136 | tf_op jit(solution)/shard_map/ppermute | solution.py:196
  86.2 7.2 %collective-permute-start.9 = (bf16[448,256]{1,0:T(8,128)(2,1)S(1)}, bf16[448,256]{1,0:T(8,128)(2,1)S(1)}, u32[]{:S(2)}, u32[]{:S(2)}) collective-permute-start(bf16[448,256]{1,0:T(8,128)(2,1)S(1)} %slice.127), channel_id=1, source_target_pairs={{0,7},{1,0},{2,1},{3,2},{4,3},{5,4},{6,5},{7,6},{8,15},{9,8},{10,9... | collective-permute-start | bytes 688136 | tf_op jit(solution)/shard_map/ppermute | solution.py:197
  93.4 1.2 %copy-start.2 = (bf16[448,256]{1,0:T(8,128)(2,1)}, bf16[448,256]{1,0:T(8,128)(2,1)S(1)}, u32[]{:S(2)}) copy-start(bf16[448,256]{1,0:T(8,128)(2,1)S(1)} %collective-permute-done.9.refs_8_) | copy-start | bytes 688132
  94.7 9.6 %collective-permute-start.12 = (bf16[2,2,128,128]{3,2,1,0:T(8,128)(2,1)S(1)}, bf16[2,2,128,128]{3,2,1,0:T(8,128)(2,1)S(1)}, u32[]{:S(2)}, u32[]{:S(2)}) collective-permute-start(bf16[2,2,128,128]{3,2,1,0:T(8,128)(2,1)S(1)} %get-tuple-element.35), channel_id=1, source_target_pairs={{0,2},{1,3},{2,4},{3,5},{4,6},{5,7},{6,0},{7,1},{8,10},{9,11},{10,... | collective-permute-start | bytes 393224 | tf_op jit(solution)/shard_map/ppermute | solution.py:206
  99.0 6.0 %collective-permute-start.11 = (bf16[2,2,128,128]{3,2,1,0:T(8,128)(2,1)S(1)}, bf16[2,2,128,128]{3,2,1,0:T(8,128)(2,1)S(1)}, u32[]{:S(2)}, u32[]{:S(2)}) collective-permute-start(bf16[2,2,128,128]{3,2,1,0:T(8,128)(2,1)S(1)} %get-tuple-element.36), channel_id=1, source_target_pairs={{0,7},{1,0},{2,1},{3,2},{4,3},{5,4},{6,5},{7,6},{8,15},{9,8},{10,9... | collective-permute-start | bytes 393224 | tf_op jit(solution)/shard_map/ppermute | solution.py:205
  102.1 6.9 %collective-permute-start.10 = (bf16[2,2,128,128]{3,2,1,0:T(8,128)(2,1)S(1)}, bf16[2,2,128,128]{3,2,1,0:T(8,128)(2,1)S(1)}, u32[]{:S(2)}, u32[]{:S(2)}) collective-permute-start(bf16[2,2,128,128]{3,2,1,0:T(8,128)(2,1)S(1)} %get-tuple-element.37), channel_id=1, source_target_pairs={{0,1},{1,2},{2,3},{3,4},{4,5},{5,6},{6,7},{7,0},{8,9},{9,10},{10,1... | collective-permute-start | bytes 393224 | tf_op jit(solution)/shard_map/ppermute | solution.py:204
  109.1 8.3 %copy-start.3 = (bf16[448,256]{1,0:T(8,128)(2,1)S(1)}, bf16[448,256]{1,0:T(8,128)(2,1)}, u32[]{:S(2)}) copy-start(bf16[448,256]{1,0:T(8,128)(2,1)} %copy-done.2) | copy-start | bytes 688132
  109.1 8.2 %collective-permute-start.13 = (bf16[8,2,128,128]{3,2,1,0:T(8,128)(2,1)S(1)}, bf16[8,2,128,128]{3,2,1,0:T(8,128)(2,1)S(1)}, u32[]{:S(2)}, u32[]{:S(2)}) collective-permute-start(bf16[8,2,128,128]{3,2,1,0:T(8,128)(2,1)S(1)} %pad_maximum_fusion), channel_id=1, source_target_pairs={{0,8},{8,0},{1,9},{9,1},{2,10},{10,2},{3,11},{11,3},{4,12},{12,4},... | collective-permute-start | bytes 1572872 | tf_op jit(solution)/shard_map/ppermute | solution.py:208

commit v4 on v3

v4 whole, which is shorter than its diff:
```python
import jax
import jax.numpy as jnp
from jax import lax
from jax.experimental import pallas as pl
from jax.experimental.pallas import tpu as pltpu
from jax.sharding import Mesh, PartitionSpec as P

TS = 128
VT = 157
NT = 16
NX, NZ, NCORE, NPAIR = 4, 8, 2, 8
NXZ = NX * NZ
AUX = ("x", "z", "core")
EARLY = ((0, 0), (0, 1), (-1, 1))
LATE = ((-1, 2), (-2, 2))
PAIRS = EARLY + LATE
WIDTH = 2 * TS
PIECE = WIDTH // NXZ
ORDER = (
    (0, False),
    (1, True),
    (-1, False),
    (-2, False),
    (2, True),
    (3, True),
    (-3, False),
    (4, False),
)
ROWS = 224
VMEM_LIMIT = 48 * 1024 * 1024
bf16, f32 = jnp.bfloat16, jnp.float32
in_vmem = pl.BlockSpec(memory_space=pltpu.VMEM)


def ring(size, step):
    return [(i, (i + step) % size) for i in range(size)]


def coulomb_pairs(blocks, pairs):
    names = sorted({d for pair in pairs for d in pair})

    def kernel(*refs):
        block = dict(zip(names, refs))
        own, other = refs[len(names) :]
        core = lax.axis_index("core")
        for k, (r, c) in enumerate(pairs):
            for out, part in ((own, core), (other, 1 - core)):
                left = block[r][:, pl.ds(pl.multiple_of(part * TS, TS), TS)]
                product = lax.dot_general(
                    left, block[c][...], (((0,), (0,)), ((), ())), preferred_element_type=f32
                )
                for h in (0, 1):
                    out[k, h] = product[:, h * TS : (h + 1) * TS].astype(out.dtype)

    shape = (len(pairs), 2, TS, TS)
    return pl.pallas_call(
        kernel,
        out_shape=(jax.ShapeDtypeStruct(shape, f32), jax.ShapeDtypeStruct(shape, bf16)),
        in_specs=[in_vmem] * len(names),
        out_specs=(in_vmem, in_vmem),
        compiler_params=pltpu.CompilerParams(vmem_limit_bytes=VMEM_LIMIT),
        name="coulomb_pairs",
    )(*[blocks[d] for d in names])


def sum_cores(own, received):
    pairs = own.shape[0]

    def kernel(mine, theirs, out):
        total = (mine[...] + theirs[...].astype(f32)).reshape(pairs, NXZ, PIECE, TS)
        out[...] = jnp.concatenate([total[k] for k in range(pairs)], axis=1).astype(bf16)

    return pl.pallas_call(
        kernel,
        out_shape=jax.ShapeDtypeStruct((NXZ, pairs * PIECE, TS), bf16),
        in_specs=[in_vmem] * 2,
        out_specs=in_vmem,
        compiler_params=pltpu.CompilerParams(vmem_limit_bytes=VMEM_LIMIT),
        name="sum_cores",
    )(own, received)


def early_piece(pieces, denominator):
    def kernel(pieces_ref, denominator_ref, kept, sent, second):
        total = jnp.sum(pieces_ref[...].astype(f32), axis=0) / denominator_ref[...]
        kept[...] = total[: 2 * PIECE].astype(bf16)
        sent[...] = total[PIECE:].astype(bf16)
        second[...] = total[2 * PIECE :]

    shape = jax.ShapeDtypeStruct((2 * PIECE, TS), bf16)
    return pl.pallas_call(
        kernel,
        out_shape=(shape, shape, jax.ShapeDtypeStruct((PIECE, TS), f32)),
        in_specs=[in_vmem] * 2,
        out_specs=(in_vmem,) * 3,
        compiler_params=pltpu.CompilerParams(vmem_limit_bytes=VMEM_LIMIT),
        name="early_piece",
    )(pieces, denominator)


def late_piece(pieces, denominator, second):
    def kernel(pieces_ref, denominator_ref, second_ref, down, up):
        total = jnp.sum(pieces_ref[...].astype(f32), axis=0) / denominator_ref[...]
        up[...] = total.astype(bf16)
        down[...] = jnp.concatenate([second_ref[...], total[:PIECE]]).astype(bf16)

    shape = jax.ShapeDtypeStruct((2 * PIECE, TS), bf16)
    return pl.pallas_call(
        kernel,
        out_shape=(shape, shape),
        in_specs=[in_vmem] * 3,
        out_specs=(in_vmem,) * 2,
        compiler_params=pltpu.CompilerParams(vmem_limit_bytes=VMEM_LIMIT),
        name="late_piece",
    )(pieces, denominator, second)


def spread(*pieces):
    rows = len(pieces) * 2 * PIECE

    def kernel(*refs):
        whole = jnp.concatenate([ref[...] for ref in refs[:-1]])
        refs[-1][...] = jnp.broadcast_to(whole[None], (NXZ, rows, TS))

    return pl.pallas_call(
        kernel,
        out_shape=jax.ShapeDtypeStruct((NXZ, rows, TS), bf16),
        in_specs=[in_vmem] * len(pieces),
        out_specs=in_vmem,
        compiler_params=pltpu.CompilerParams(vmem_limit_bytes=VMEM_LIMIT),
        name="spread",
    )(*pieces)


def gamma_rows(blocks, last, mine, theirs, scales):
    rows, width = blocks[0].shape
    names = [q for q, *_ in ORDER if q != 4]
    half = rows // len(last)

    def kernel(*refs):
        block = dict(zip(names, refs))
        n = len(names)
        last_refs, refs = refs[n : n + len(last)], refs[n + len(last) :]
        own, other, scale, out, matrix = refs
        core = lax.axis_index("core")
        for pair in range(0, len(ORDER), 2):
            for part, source in ((core, own), (1 - core, other)):
                place = pl.ds(pl.multiple_of(part * TS, TS), TS)
                both = source[:, pair * PIECE : (pair + 2) * PIECE].astype(f32)
                for k in (0, 1):
                    i = pair + k
                    tiles = both[:, k * PIECE : (k + 1) * PIECE].reshape(2, TS, TS)
                    for h in (0, 1):
                        if ORDER[i][1]:
                            tile = tiles[h].T * scale[2 * i + h : 2 * i + h + 1]
                            matrix[i, h * TS : (h + 1) * TS, place] = tile.astype(bf16)
                        else:
                            tile = tiles[h] * scale[pl.ds(2 * i + part, 1)]
                            matrix[i, place, h * TS : (h + 1) * TS] = tile.astype(bf16)

        for start in range(0, rows, ROWS):
            total = None
            for i, (q, *_) in enumerate(ORDER):
                if q == 4:
                    left = [
                        last_refs[j][max(start - j * half, 0) : start + ROWS - j * half]
                        for j in range(len(last))
                        if start < (j + 1) * half and start + ROWS > j * half
                    ]
                    left = left[0] if len(left) == 1 else jnp.concatenate(left)
                else:
                    left = block[q][start : start + ROWS]
                term = jnp.dot(left, matrix[i], preferred_element_type=f32)
                total = term if total is None else total + term
            out[start : start + ROWS] = total.astype(bf16)

    return pl.pallas_call(
        kernel,
        out_shape=jax.ShapeDtypeStruct((rows, width), bf16),
        in_specs=[in_vmem] * (len(names) + len(last) + 3),
        out_specs=in_vmem,
        scratch_shapes=[pltpu.VMEM((len(ORDER), WIDTH, WIDTH), bf16)],
        compiler_params=pltpu.CompilerParams(vmem_limit_bytes=VMEM_LIMIT),
        name="gamma_rows",
    )(*[blocks[q] for q in names], *last, mine, theirs, scales)


def body(three_index, occupied_energy, virtual_energy, tile_occupied, tile_virtual, tile_exponent):
    me = lax.axis_index("pair")
    core = lax.axis_index("core")
    slot = lax.axis_index(("x", "z"))
    up, down = ring(NPAIR, 1), ring(NPAIR, -1)
    swap = ring(NCORE, 1)

    block = {0: three_index}
    for d in (1, 2):
        block[-d] = lax.ppermute(block[1 - d], "pair", up)
        block[d] = lax.ppermute(block[d - 1], "pair", down)

    energy = virtual_energy.reshape(VT, TS)[tile_virtual] - occupied_energy[tile_occupied][:, None]
    scale = jnp.where(tile_exponent == -1, 0.5, jnp.where(tile_exponent == 1, 2.0, 1.0)).astype(f32)
    table = jnp.concatenate([energy, jnp.broadcast_to(scale[:, None], (NT, TS))], axis=1)
    table = jnp.concatenate([table, table, table])
    near = lax.dynamic_slice_in_dim(table, 2 * me + NT - 4, 10).reshape(5, 2, 2 * TS)
    row = lax.dynamic_index_in_dim(near, core, 1, keepdims=False)
    row_of = jnp.stack([row[r + 2] for r, _ in PAIRS])
    column_of = jnp.stack([near[c + 2] for _, c in PAIRS])
    denominator = (
        (row_of[:, None, :TS, None] + column_of[:, :, None, :TS])
        / (row_of[:, None, TS:, None] * column_of[:, :, None, TS:])
    ).reshape(len(PAIRS), NXZ, PIECE, TS)
    denominator = lax.dynamic_index_in_dim(denominator, slot, 1, keepdims=False).reshape(-1, TS)
    split = len(EARLY) * PIECE
    turned = lax.dynamic_slice_in_dim(table[:, TS:], 2 * me, NT).reshape(NPAIR, 2, TS)
    scales = jnp.concatenate([turned[q % NPAIR] for q, *_ in ORDER])

    own, other = coulomb_pairs(block, EARLY)
    early = sum_cores(own, lax.ppermute(other, "core", swap))
    early = lax.all_to_all(early, ("x", "z"), 0, 0)
    own, other = coulomb_pairs(block, LATE)
    late = sum_cores(own, lax.ppermute(other, "core", swap))
    late, block[-2], block[2] = lax.optimization_barrier((late, block[-2], block[2]))
    late = lax.all_to_all(late, ("x", "z"), 0, 0)
    block[-3] = lax.ppermute(block[-2], "pair", up)
    block[3] = lax.ppermute(block[2], "pair", down)

    kept, sent, second = early_piece(early, denominator[:split])
    lower1 = lax.ppermute(sent, "pair", up)
    sent, sent2 = late_piece(late, denominator[split:], second)
    upper1 = lax.ppermute(sent, "pair", down)
    lower2 = lax.ppermute(sent2, "pair", ring(NPAIR, 2))
    copies = spread(kept, lower1, upper1, lower2)
    copies, block[-3], block[3], scales = lax.optimization_barrier(
        (copies, block[-3], block[3], scales)
    )

    half = three_index.shape[0] // 2
    last_upper = lax.ppermute(block[-3][:half], "pair", up)
    last_lower = lax.ppermute(block[3][half:], "pair", down)
    mine = lax.all_to_all(copies, ("x", "z"), 0, 0)
    mine, last_upper, last_lower = lax.optimization_barrier((mine, last_upper, last_lower))
    theirs = lax.ppermute(mine, "core", swap)
    return gamma_rows(block, (last_upper, last_lower), mine, theirs, scales)


def solution(mesh):
    grid = Mesh(mesh.devices.reshape(NX, NZ, NCORE, NPAIR), AUX + ("pair",))
    placed = (P(AUX, "pair"), P(), P(), P(), P(), P())
    return jax.shard_map(
        body, mesh=grid, in_specs=placed, out_specs=P(AUX, "pair"), check_vma=False
    )
```

time: 121 us -> 117 us (0.967)
  waiting for transfers between devices: 21.3 us -> 16.8 us
    ppermute x1, waiting for transfers between devices: 7.04 us -> 0.01 us  [body(): block[-3] = lax.ppermute(block[-2], 'pair', up)]
    all_to_all x2 -> x3, waiting for transfers between devices: 0.01 us -> 7 us  [the longest x1 6.35 us: body(): late = lax.all_to_all(late, ('x', 'z'), 0, 0)]
    all_to_all x2 -> x3, starting transfers between devices: 23 us -> 26.8 us  [the longest x1 11.8 us: body(): early = lax.all_to_all(early, ('x', 'z'), 0, 0)]
    ppermute x6, starting transfers between devices: 26.2 us -> 22.5 us  [the longest x1 7.81 us: body(): theirs = lax.ppermute(mine, 'core', swap)]
    unnamed x20 -> x34, local copies, waits for them, and re-layouts: 4.25 us -> 7.72 us
    ppermute x1, waiting for transfers between devices: 3.15 us -> 0.49 us  [body(): last_lower = lax.ppermute(block[3][half:], 'pair', down)]
    ppermute x1, starting transfers between devices: 1.92 us -> 4.57 us  [body(): last_lower = lax.ppermute(block[3][half:], 'pair', down)]
    ppermute x1, starting transfers between devices: 4.57 us -> 1.92 us  [body(): last_upper = lax.ppermute(block[-3][:half], 'pair', up)]
  transfers between devices with their start and end apart: 16 -> 17, of which waited for: 8 -> 9; matrix products, arithmetic and copies ran while one was open for 8% -> 5% of each run, Pallas kernels for 1% -> 3%
where the time goes in v4:
time: 117 us; the launch traced here: 116 us
  starting transfers between devices  79.6 us (68%)
  waiting for transfers between devices  16.8 us (14%)
  local copies, waits for them, and re-layouts  12.8 us (11%)
  Pallas kernels  5.95 us (5%)
    all_to_all x1, starting transfers between devices, body(): early = lax.all_to_all(early, ('x', 'z'), 0, 0)  11.8 us
    all_to_all x1, starting transfers between devices, body(): late = lax.all_to_all(late, ('x', 'z'), 0, 0)  9.63 us
    ppermute x2, starting transfers between devices, body(): block[-d] = lax.ppermute(block[1 - d], 'pair', up)  9.15 us
    ppermute x2, starting transfers between devices, body(): block[d] = lax.ppermute(block[d - 1], 'pair', down)  8.15 us
    ppermute x1, starting transfers between devices, body(): theirs = lax.ppermute(mine, 'core', swap)  7.81 us
    unnamed x34, local copies, waits for them, and re-layouts  7.72 us
    all_to_all x1, waiting for transfers between devices, body(): late = lax.all_to_all(late, ('x', 'z'), 0, 0)  6.35 us
    ppermute x1, starting transfers between devices, body(): early = sum_cores(own, lax.ppermute(other, 'core', swap))  6.29 us
  transfers between devices with their start and end apart: 17, of which 9 were waited for; matrix products, arithmetic and copies ran while one was open for 5% of the time, Pallas kernels for 3%

profile of v4, /device:TPU:1, one launch (start us, length us, event | category | flops | bytes accessed | tf_op | source)
XLA Modules:
  0.0 115.8 jit_solution(12138946638714355316)
XLA Ops:
  0.0 4.2 %collective-permute-start.1 = (bf16[896,256]{1,0:T(8,128)(2,1)}, bf16[896,256]{1,0:T(8,128)(2,1)S(1)}, u32[]{:S(2)}, u32[]{:S(2)}) collective-permute-start(bf16[896,256]{1,0:T(8,128)(2,1)} %refs_0_.1), channel_id=1, source_target_pairs={{0,1},{1,2},{2,3},{3,4},{4,5},{5,6},{6,7},{7,0},{8,9},{9,10},{10,1... | collective-permute-start | bytes 1376264 | tf_op jit(solution)/shard_map/ppermute | solution.py:197
  4.2 3.8 %collective-permute-start = (bf16[896,256]{1,0:T(8,128)(2,1)}, bf16[896,256]{1,0:T(8,128)(2,1)S(1)}, u32[]{:S(2)}, u32[]{:S(2)}) collective-permute-start(bf16[896,256]{1,0:T(8,128)(2,1)} %refs_0_.1), channel_id=1, source_target_pairs={{0,7},{1,0},{2,1},{3,2},{4,3},{5,4},{6,5},{7,6},{8,15},{9,8},{10,9... | collective-permute-start | bytes 1376264 | tf_op jit(solution)/shard_map/ppermute | solution.py:198
  8.0 0.6 copy-done.14
  8.7 0.6 copy-done.12
  9.3 0.0 copy-done.13
  9.3 0.0 copy-start.9
  9.4 0.6 copy-done.9
  10.0 0.7 gather_fusion.1
  10.7 0.6 gather_fusion
  11.2 0.1 broadcast_subtract_fusion
  11.3 0.1 broadcast_in_dim.34
  11.6 0.5 collective-permute-done.1.refs_1_.refs_0_.refs_2_
  12.1 5.0 %collective-permute-start.2 = (bf16[896,256]{1,0:T(8,128)(2,1)S(1)}, bf16[896,256]{1,0:T(8,128)(2,1)S(1)}, u32[]{:S(2)}, u32[]{:S(2)}) collective-permute-start(bf16[896,256]{1,0:T(8,128)(2,1)S(1)} %collective-permute-done.1.refs_1_.refs_0_.refs_2_), channel_id=1, source_target_pairs={{0,1},{1,2},{2,3},{3,4},{4,5},{5,6},{6,7},{7,0},{8,9},{9,10},{10,1... | collective-permute-start | bytes 1376264 | tf_op jit(solution)/shard_map/ppermute | solution.py:197
  17.1 0.0 collective-permute-done.refs_2_.refs_1_
  17.1 4.3 %collective-permute-start.3 = (bf16[896,256]{1,0:T(8,128)(2,1)S(1)}, bf16[896,256]{1,0:T(8,128)(2,1)S(1)}, u32[]{:S(2)}, u32[]{:S(2)}) collective-permute-start(bf16[896,256]{1,0:T(8,128)(2,1)S(1)} %collective-permute-done.refs_2_.refs_1_), channel_id=1, source_target_pairs={{0,7},{1,0},{2,1},{3,2},{4,3},{5,4},{6,5},{7,6},{8,15},{9,8},{10,9... | collective-permute-start | bytes 1376264 | tf_op jit(solution)/shard_map/ppermute | solution.py:198
  21.5 0.1 mul.31
  21.6 0.1 copy.11
  21.7 0.1 add.56
  21.8 0.1 copy.9
  21.9 0.6 coulomb_pairs.3
  22.6 6.3 %collective-permute-start.5 = (bf16[3,2,128,128]{3,2,1,0:T(8,128)(2,1)S(1)}, bf16[3,2,128,128]{3,2,1,0:T(8,128)(2,1)S(1)}, u32[]{:S(2)}, u32[]{:S(2)}) collective-permute-start(bf16[3,2,128,128]{3,2,1,0:T(8,128)(2,1)S(1)} %get-tuple-element.29), channel_id=1, source_target_pairs={{0,8},{8,0},{1,9},{9,1},{2,10},{10,2},{3,11},{11,3},{4,12},{12,4},... | collective-permute-start | bytes 589832 | tf_op jit(solution)/shard_map/ppermute | solution.py:218
  28.9 1.0 collective-permute-done.5.theirs
  29.9 0.7 sum_cores.3
  30.6 11.8 %all-to-all-start = ((bf16[32,24,128]{2,1,0:T(8,128)(2,1)}), bf16[32,24,128]{2,1,0:T(8,128)(2,1)S(1)}, u32[]{:S(2)}, u32[]{:S(2)}) async-start(bf16[32,24,128]{2,1,0:T(8,128)(2,1)} %sum_cores.3), calls=%async_computation | async-start | bytes 393216 | tf_op jit(solution)/shard_map/all_to_all | solution.py:219
  42.4 0.0 collective-permute-done.2.refs_0_.refs_3_
  42.5 0.0 collective-permute-done.3.refs_2_.refs_4_
  42.5 0.5 coulomb_pairs.2
  43.0 2.6 %collective-permute-start.4 = (bf16[2,2,128,128]{3,2,1,0:T(8,128)(2,1)S(1)}, bf16[2,2,128,128]{3,2,1,0:T(8,128)(2,1)S(1)}, u32[]{:S(2)}, u32[]{:S(2)}) collective-permute-start(bf16[2,2,128,128]{3,2,1,0:T(8,128)(2,1)S(1)} %get-tuple-element.25), channel_id=1, source_target_pairs={{0,8},{8,0},{1,9},{9,1},{2,10},{10,2},{3,11},{11,3},{4,12},{12,4},... | collective-permute-start | bytes 393224 | tf_op jit(solution)/shard_map/ppermute | solution.py:221
  45.5 0.1 multiply_divide_fusion
  45.6 0.9 collective-permute-done.4.theirs
  46.5 0.6 copy-done.4
  47.2 1.9 %collective-permute-start.9 = (bf16[896,256]{1,0:T(8,128)(2,1)S(1)}, bf16[896,256]{1,0:T(8,128)(2,1)S(1)}, u32[]{:S(2)}, u32[]{:S(2)}) collective-permute-start(bf16[896,256]{1,0:T(8,128)(2,1)S(1)} %collective-permute-done.2.refs_0_.refs_3_), channel_id=1, source_target_pairs={{0,1},{1,2},{2,3},{3,4},{4,5},{5,6},{6,7},{7,0},{8,9},{9,10},{10,1... | collective-permute-start | bytes 1376264 | tf_op jit(solution)/shard_map/ppermute | solution.py:224
  49.1 4.6 %collective-permute-start.10 = (bf16[896,256]{1,0:T(8,128)(2,1)S(1)}, bf16[896,256]{1,0:T(8,128)(2,1)S(1)}, u32[]{:S(2)}, u32[]{:S(2)}) collective-permute-start(bf16[896,256]{1,0:T(8,128)(2,1)S(1)} %collective-permute-done.3.refs_2_.refs_4_), channel_id=1, source_target_pairs={{0,7},{1,0},{2,1},{3,2},{4,3},{5,4},{6,5},{7,6},{8,15},{9,8},{10,9... | collective-permute-start | bytes 1376264 | tf_op jit(solution)/shard_map/ppermute | solution.py:225
  53.7 0.6 slice.142
  54.3 0.0 all-to-all-done.pieces_ref
  54.3 9.6 %all-to-all-start.1 = ((bf16[32,16,128]{2,1,0:T(8,128)(2,1)}), bf16[32,16,128]{2,1,0:T(8,128)(2,1)}, u32[]{:S(2)}, u32[]{:S(2)}) async-start(bf16[32,16,128]{2,1,0:T(8,128)(2,1)} %copy-done.4), calls=%async_computation.1 | async-start | bytes 262144 | tf_op jit(solution)/shard_map/all_to_all | solution.py:223
  64.0 0.8 constant_dynamic-slice_fusion.1
  64.8 1.9 %collective-permute-start.6 = (bf16[16,128]{1,0:T(8,128)(2,1)S(1)}, bf16[16,128]{1,0:T(8,128)(2,1)S(1)}, u32[]{:S(2)}, u32[]{:S(2)}) collective-permute-start(bf16[16,128]{1,0:T(8,128)(2,1)S(1)} %get-tuple-element.31), channel_id=1, source_target_pairs={{0,1},{1,2},{2,3},{3,4},{4,5},{5,6},{6,7},{7,0},{8,9},{9,10},{10,1... | collective-permute-start | bytes 12296 | tf_op jit(solution)/shard_map/ppermute | solution.py:228
  66.7 6.3 %all-to-all-done.1.pieces_ref = bf16[32,16,128]{2,1,0:T(8,128)(2,1)} async-done(((bf16[32,16,128]{2,1,0:T(8,128)(2,1)}), bf16[32,16,128]{2,1,0:T(8,128)(2,1)}, u32[]{:S(2)}, u32[]{:S(2)}) %all-to-all-start.1) | async-done | bytes 131104 | tf_op jit(solution)/shard_map/all_to_all | solution.py:223
  73.1 0.9 late_piece.1
  74.0 2.0 %collective-permute-start.7 = (bf16[16,128]{1,0:T(8,128)(2,1)S(1)}, bf16[16,128]{1,0:T(8,128)(2,1)S(1)}, u32[]{:S(2)}, u32[]{:S(2)}) collective-permute-start(bf16[16,128]{1,0:T(8,128)(2,1)S(1)} %get-tuple-element.34), channel_id=1, source_target_pairs={{0,7},{1,0},{2,1},{3,2},{4,3},{5,4},{6,5},{7,6},{8,15},{9,8},{10,9... | collective-permute-start | bytes 12296 | tf_op jit(solution)/shard_map/ppermute | solution.py:230
  76.0 1.9 %collective-permute-start.8 = (bf16[16,128]{1,0:T(8,128)(2,1)S(1)}, bf16[16,128]{1,0:T(8,128)(2,1)S(1)}, u32[]{:S(2)}, u32[]{:S(2)}) collective-permute-start(bf16[16,128]{1,0:T(8,128)(2,1)S(1)} %get-tuple-element.35), channel_id=1, source_target_pairs={{0,2},{1,3},{2,4},{3,5},{4,6},{5,7},{6,0},{7,1},{8,10},{9,11},{10,... | collective-permute-start | bytes 12296 | tf_op jit(solution)/shard_map/ppermute | solution.py:231
  78.0 0.8 constant_dynamic-slice_fusion.13
  78.9 0.0 collective-permute-done.6.refs_1_
  78.9 0.0 collective-permute-done.7.refs_2_
  78.9 3.6 %collective-permute-done.8.refs_3_ = bf16[16,128]{1,0:T(8,128)(2,1)S(1)} collective-permute-done((bf16[16,128]{1,0:T(8,128)(2,1)S(1)}, bf16[16,128]{1,0:T(8,128)(2,1)S(1)}, u32[]{:S(2)}, u32[]{:S(2)}) %collective-permute-start.8) | collective-permute-done | bytes 4128 | tf_op jit(solution)/shard_map/ppermute | solution.py:231
  82.5 0.9 spread.1
  83.4 0.0 collective-permute-done.9.refs_6_
  83.4 0.8 copy-done.2
  84.2 5.4 %all-to-all-start.2 = ((bf16[32,64,128]{2,1,0:T(8,128)(2,1)}), bf16[32,64,128]{2,1,0:T(8,128)(2,1)S(1)}, u32[]{:S(2)}, u32[]{:S(2)}) async-start(bf16[32,64,128]{2,1,0:T(8,128)(2,1)} %spread.1), calls=%async_computation.2 | async-start | bytes 1048576 | tf_op jit(solution)/shard_map/all_to_all | solution.py:240
  89.6 1.0 slice.131
  90.6 1.9 %collective-permute-start.11 = (bf16[448,256]{1,0:T(8,128)(2,1)S(1)}, bf16[448,256]{1,0:T(8,128)(2,1)S(1)}, u32[]{:S(2)}, u32[]{:S(2)}) collective-permute-start(bf16[448,256]{1,0:T(8,128)(2,1)S(1)} %slice.130), channel_id=1, source_target_pairs={{0,1},{1,2},{2,3},{3,4},{4,5},{5,6},{6,7},{7,0},{8,9},{9,10},{10,1... | collective-permute-start | bytes 688136 | tf_op jit(solution)/shard_map/ppermute | solution.py:238
  92.5 4.6 %collective-permute-start.12 = (bf16[448,256]{1,0:T(8,128)(2,1)S(1)}, bf16[448,256]{1,0:T(8,128)(2,1)S(1)}, u32[]{:S(2)}, u32[]{:S(2)}) collective-permute-start(bf16[448,256]{1,0:T(8,128)(2,1)S(1)} %slice.131), channel_id=1, source_target_pairs={{0,7},{1,0},{2,1},{3,2},{4,3},{5,4},{6,5},{7,6},{8,15},{9,8},{10,9... | collective-permute-start | bytes 688136 | tf_op jit(solution)/shard_map/ppermute | solution.py:239
  97.1 1.8 %collective-permute-done.11.refs_7_ = bf16[448,256]{1,0:T(8,128)(2,1)S(1)} collective-permute-done((bf16[448,256]{1,0:T(8,128)(2,1)S(1)}, bf16[448,256]{1,0:T(8,128)(2,1)S(1)}, u32[]{:S(2)}, u32[]{:S(2)}) %collective-permute-start.11) | collective-permute-done | bytes 229408 | tf_op jit(solution)/shard_map/ppermute | solution.py:238
  98.8 0.7 copy-done.5
  99.5 0.5 collective-permute-done.12.refs_8_
  100.0 0.7 copy-done.7
  100.7 0.7 all-to-all-done.2.refs_9_
  101.4 7.8 %collective-permute-start.13 = (bf16[32,64,128]{2,1,0:T(8,128)(2,1)S(1)}, bf16[32,64,128]{2,1,0:T(8,128)(2,1)S(1)}, u32[]{:S(2)}, u32[]{:S(2)}) collective-permute-start(bf16[32,64,128]{2,1,0:T(8,128)(2,1)S(1)} %all-to-all-done.2.refs_9_), channel_id=1, source_target_pairs={{0,8},{8,0},{1,9},{9,1},{2,10},{10,2},{3,11},{11,3},{4,12},{12,4},... | collective-permute-start | bytes 1572872 | tf_op jit(solution)/shard_map/ppermute | solution.py:242
  109.2 1.5 %collective-permute-done.13.refs_10_ = bf16[32,64,128]{2,1,0:T(8,128)(2,1)S(1)} collective-permute-done((bf16[32,64,128]{2,1,0:T(8,128)(2,1)S(1)}, bf16[32,64,128]{2,1,0:T(8,128)(2,1)S(1)}, u32[]{:S(2)}, u32[]{:S(2)}) %collective-permute-start.13) | collective-permute-done | bytes 524320 | tf_op jit(solution)/shard_map/ppermute | solution.py:242
  110.7 1.0 copy-done.3
  111.7 0.9 copy-done.6
  112.6 0.9 copy-done.8
  113.6 2.2 %gamma_rows.1 = bf16[896,256]{1,0:T(8,128)(2,1)} custom-call(bf16[896,256]{1,0:T(8,128)(2,1)S(1)} %copy-done.1, bf16[896,256]{1,0:T(8,128)(2,1)S(1)} %collective-permute-done.refs_2_.refs_1_, bf16[896,256]{1,0:T(8,128)(2,1)S(1)} %collective-permute-done.1.refs_1_.refs_0_.refs_2_, bf16[896,256]{1,0:T(8,128)(2,1)S(1)} %collective-permute-done.2.refs_0_.refs_3_, ...), custom_call_target="tpu_custom_call" | custom-call | tf_op jit(solution)/shard_map/gamma_rows/pallas_call | solution.py:177
  (51 shorter events, 0.4 us)
Async XLA Ops:
  0.0 10.7 %copy-start = (f32[20096]{0:T(1024)S(1)}, f32[20096]{0:T(1024)}, u32[]{:S(2)}) copy-start(f32[20096]{0:T(1024)} %param.8) | copy-start | bytes 241156
  0.0 12.1 %collective-permute-start.1 = (bf16[896,256]{1,0:T(8,128)(2,1)}, bf16[896,256]{1,0:T(8,128)(2,1)S(1)}, u32[]{:S(2)}, u32[]{:S(2)}) collective-permute-start(bf16[896,256]{1,0:T(8,128)(2,1)} %refs_0_.1), channel_id=1, source_target_pairs={{0,1},{1,2},{2,3},{3,4},{4,5},{5,6},{6,7},{7,0},{8,9},{9,10},{10,1... | collective-permute-start | bytes 1376264 | tf_op jit(solution)/shard_map/ppermute | solution.py:197
  4.2 13.0 %collective-permute-start = (bf16[896,256]{1,0:T(8,128)(2,1)}, bf16[896,256]{1,0:T(8,128)(2,1)S(1)}, u32[]{:S(2)}, u32[]{:S(2)}) collective-permute-start(bf16[896,256]{1,0:T(8,128)(2,1)} %refs_0_.1), channel_id=1, source_target_pairs={{0,7},{1,0},{2,1},{3,2},{4,3},{5,4},{6,5},{7,6},{8,15},{9,8},{10,9... | collective-permute-start | bytes 1376264 | tf_op jit(solution)/shard_map/ppermute | solution.py:198
  8.0 0.7 copy-start.14
  8.7 0.7 copy-start.12
  8.7 0.7 copy-start.13
  9.3 0.7 copy-start.9
  11.3 10.6 %copy-start.1 = (bf16[896,256]{1,0:T(8,128)(2,1)S(1)}, bf16[896,256]{1,0:T(8,128)(2,1)}, u32[]{:S(2)}) copy-start(bf16[896,256]{1,0:T(8,128)(2,1)} %refs_0_.1) | copy-start | bytes 1376260
  12.1 30.3 %collective-permute-start.2 = (bf16[896,256]{1,0:T(8,128)(2,1)S(1)}, bf16[896,256]{1,0:T(8,128)(2,1)S(1)}, u32[]{:S(2)}, u32[]{:S(2)}) collective-permute-start(bf16[896,256]{1,0:T(8,128)(2,1)S(1)} %collective-permute-done.1.refs_1_.refs_0_.refs_2_), channel_id=1, source_target_pairs={{0,1},{1,2},{2,3},{3,4},{4,5},{5,6},{6,7},{7,0},{8,9},{9,10},{10,1... | collective-permute-start | bytes 1376264 | tf_op jit(solution)/shard_map/ppermute | solution.py:197
  17.1 25.3 %collective-permute-start.3 = (bf16[896,256]{1,0:T(8,128)(2,1)S(1)}, bf16[896,256]{1,0:T(8,128)(2,1)S(1)}, u32[]{:S(2)}, u32[]{:S(2)}) collective-permute-start(bf16[896,256]{1,0:T(8,128)(2,1)S(1)} %collective-permute-done.refs_2_.refs_1_), channel_id=1, source_target_pairs={{0,7},{1,0},{2,1},{3,2},{4,3},{5,4},{6,5},{7,6},{8,15},{9,8},{10,9... | collective-permute-start | bytes 1376264 | tf_op jit(solution)/shard_map/ppermute | solution.py:198
  22.6 7.3 %collective-permute-start.5 = (bf16[3,2,128,128]{3,2,1,0:T(8,128)(2,1)S(1)}, bf16[3,2,128,128]{3,2,1,0:T(8,128)(2,1)S(1)}, u32[]{:S(2)}, u32[]{:S(2)}) collective-permute-start(bf16[3,2,128,128]{3,2,1,0:T(8,128)(2,1)S(1)} %get-tuple-element.29), channel_id=1, source_target_pairs={{0,8},{8,0},{1,9},{9,1},{2,10},{10,2},{3,11},{11,3},{4,12},{12,4},... | collective-permute-start | bytes 589832 | tf_op jit(solution)/shard_map/ppermute | solution.py:218
  30.6 23.7 %all-to-all-start = ((bf16[32,24,128]{2,1,0:T(8,128)(2,1)}), bf16[32,24,128]{2,1,0:T(8,128)(2,1)S(1)}, u32[]{:S(2)}, u32[]{:S(2)}) async-start(bf16[32,24,128]{2,1,0:T(8,128)(2,1)} %sum_cores.3), calls=%async_computation | async-start | bytes 393216 | tf_op jit(solution)/shard_map/all_to_all | solution.py:219
  43.0 3.5 %collective-permute-start.4 = (bf16[2,2,128,128]{3,2,1,0:T(8,128)(2,1)S(1)}, bf16[2,2,128,128]{3,2,1,0:T(8,128)(2,1)S(1)}, u32[]{:S(2)}, u32[]{:S(2)}) collective-permute-start(bf16[2,2,128,128]{3,2,1,0:T(8,128)(2,1)S(1)} %get-tuple-element.25), channel_id=1, source_target_pairs={{0,8},{8,0},{1,9},{9,1},{2,10},{10,2},{3,11},{11,3},{4,12},{12,4},... | collective-permute-start | bytes 393224 | tf_op jit(solution)/shard_map/ppermute | solution.py:221
  45.6 8.1 %copy-start.10 = (f32[5,1,8,128]{3,2,0,1:T(8,128)}, f32[5,1,8,128]{3,2,0,1:T(8,128)S(1)}, u32[]{:S(2)}) copy-start(f32[5,1,8,128]{3,2,0,1:T(8,128)S(1)} %multiply_divide_fusion) | copy-start | bytes 61444
  46.5 0.7 copy-start.4
  47.2 36.3 %collective-permute-start.9 = (bf16[896,256]{1,0:T(8,128)(2,1)S(1)}, bf16[896,256]{1,0:T(8,128)(2,1)S(1)}, u32[]{:S(2)}, u32[]{:S(2)}) collective-permute-start(bf16[896,256]{1,0:T(8,128)(2,1)S(1)} %collective-permute-done.2.refs_0_.refs_3_), channel_id=1, source_target_pairs={{0,1},{1,2},{2,3},{3,4},{4,5},{5,6},{6,7},{7,0},{8,9},{9,10},{10,1... | collective-permute-start | bytes 1376264 | tf_op jit(solution)/shard_map/ppermute | solution.py:224
  49.1 34.3 %collective-permute-start.10 = (bf16[896,256]{1,0:T(8,128)(2,1)S(1)}, bf16[896,256]{1,0:T(8,128)(2,1)S(1)}, u32[]{:S(2)}, u32[]{:S(2)}) collective-permute-start(bf16[896,256]{1,0:T(8,128)(2,1)S(1)} %collective-permute-done.3.refs_2_.refs_4_), channel_id=1, source_target_pairs={{0,7},{1,0},{2,1},{3,2},{4,3},{5,4},{6,5},{7,6},{8,15},{9,8},{10,9... | collective-permute-start | bytes 1376264 | tf_op jit(solution)/shard_map/ppermute | solution.py:225
  54.3 18.8 %all-to-all-start.1 = ((bf16[32,16,128]{2,1,0:T(8,128)(2,1)}), bf16[32,16,128]{2,1,0:T(8,128)(2,1)}, u32[]{:S(2)}, u32[]{:S(2)}) async-start(bf16[32,16,128]{2,1,0:T(8,128)(2,1)} %copy-done.4), calls=%async_computation.1 | async-start | bytes 262144 | tf_op jit(solution)/shard_map/all_to_all | solution.py:223
  63.9 0.8 copy-start.11
  64.8 14.1 %collective-permute-start.6 = (bf16[16,128]{1,0:T(8,128)(2,1)S(1)}, bf16[16,128]{1,0:T(8,128)(2,1)S(1)}, u32[]{:S(2)}, u32[]{:S(2)}) collective-permute-start(bf16[16,128]{1,0:T(8,128)(2,1)S(1)} %get-tuple-element.31), channel_id=1, source_target_pairs={{0,1},{1,2},{2,3},{3,4},{4,5},{5,6},{6,7},{7,0},{8,9},{9,10},{10,1... | collective-permute-start | bytes 12296 | tf_op jit(solution)/shard_map/ppermute | solution.py:228
  74.0 4.8 %collective-permute-start.7 = (bf16[16,128]{1,0:T(8,128)(2,1)S(1)}, bf16[16,128]{1,0:T(8,128)(2,1)S(1)}, u32[]{:S(2)}, u32[]{:S(2)}) collective-permute-start(bf16[16,128]{1,0:T(8,128)(2,1)S(1)} %get-tuple-element.34), channel_id=1, source_target_pairs={{0,7},{1,0},{2,1},{3,2},{4,3},{5,4},{6,5},{7,6},{8,15},{9,8},{10,9... | collective-permute-start | bytes 12296 | tf_op jit(solution)/shard_map/ppermute | solution.py:230
  76.0 6.5 %collective-permute-start.8 = (bf16[16,128]{1,0:T(8,128)(2,1)S(1)}, bf16[16,128]{1,0:T(8,128)(2,1)S(1)}, u32[]{:S(2)}, u32[]{:S(2)}) collective-permute-start(bf16[16,128]{1,0:T(8,128)(2,1)S(1)} %get-tuple-element.35), channel_id=1, source_target_pairs={{0,2},{1,3},{2,4},{3,5},{4,6},{5,7},{6,0},{7,1},{8,10},{9,11},{10,... | collective-permute-start | bytes 12296 | tf_op jit(solution)/shard_map/ppermute | solution.py:231
  83.4 0.8 copy-start.2
  84.2 17.2 %all-to-all-start.2 = ((bf16[32,64,128]{2,1,0:T(8,128)(2,1)}), bf16[32,64,128]{2,1,0:T(8,128)(2,1)S(1)}, u32[]{:S(2)}, u32[]{:S(2)}) async-start(bf16[32,64,128]{2,1,0:T(8,128)(2,1)} %spread.1), calls=%async_computation.2 | async-start | bytes 1048576 | tf_op jit(solution)/shard_map/all_to_all | solution.py:240
  90.6 8.3 %collective-permute-start.11 = (bf16[448,256]{1,0:T(8,128)(2,1)S(1)}, bf16[448,256]{1,0:T(8,128)(2,1)S(1)}, u32[]{:S(2)}, u32[]{:S(2)}) collective-permute-start(bf16[448,256]{1,0:T(8,128)(2,1)S(1)} %slice.130), channel_id=1, source_target_pairs={{0,1},{1,2},{2,3},{3,4},{4,5},{5,6},{6,7},{7,0},{8,9},{9,10},{10,1... | collective-permute-start | bytes 688136 | tf_op jit(solution)/shard_map/ppermute | solution.py:238
  92.5 7.5 %collective-permute-start.12 = (bf16[448,256]{1,0:T(8,128)(2,1)S(1)}, bf16[448,256]{1,0:T(8,128)(2,1)S(1)}, u32[]{:S(2)}, u32[]{:S(2)}) collective-permute-start(bf16[448,256]{1,0:T(8,128)(2,1)S(1)} %slice.131), channel_id=1, source_target_pairs={{0,7},{1,0},{2,1},{3,2},{4,3},{5,4},{6,5},{7,6},{8,15},{9,8},{10,9... | collective-permute-start | bytes 688136 | tf_op jit(solution)/shard_map/ppermute | solution.py:239
  98.8 0.7 copy-start.5
  100.0 0.7 copy-start.7
  101.4 9.3 %collective-permute-start.13 = (bf16[32,64,128]{2,1,0:T(8,128)(2,1)S(1)}, bf16[32,64,128]{2,1,0:T(8,128)(2,1)S(1)}, u32[]{:S(2)}, u32[]{:S(2)}) collective-permute-start(bf16[32,64,128]{2,1,0:T(8,128)(2,1)S(1)} %all-to-all-done.2.refs_9_), channel_id=1, source_target_pairs={{0,8},{8,0},{1,9},{9,1},{2,10},{10,2},{3,11},{11,3},{4,12},{12,4},... | collective-permute-start | bytes 1572872 | tf_op jit(solution)/shard_map/ppermute | solution.py:242
  110.7 1.0 copy-start.3
  111.7 0.9 copy-start.6
  112.6 0.9 copy-start.8

commit v5 on v4

v5 whole, which is shorter than its diff:
```python
import jax
import jax.numpy as jnp
from jax import lax
from jax.experimental import pallas as pl
from jax.experimental.pallas import tpu as pltpu
from jax.sharding import Mesh, PartitionSpec as P

TS = 128
VT = 157
NT = 16
NX, NZ, NCORE, NPAIR = 4, 8, 2, 8
NXZ = NX * NZ
AUX = ("x", "z", "core")
EARLY = ((0, 0), (0, 1), (-1, 1))
LATE = ((-1, 2), (-2, 2))
PAIRS = EARLY + LATE
WIDTH = 2 * TS
PIECE = WIDTH // NXZ
ORDER = (
    (0, False),
    (1, True),
    (-1, False),
    (-2, False),
    (2, True),
    (3, True),
    (-3, False),
    (4, False),
)
ROWS = 224
VMEM_LIMIT = 12 * 1024 * 1024
bf16, f32 = jnp.bfloat16, jnp.float32
in_vmem = pl.BlockSpec(memory_space=pltpu.VMEM)
in_smem = pl.BlockSpec(memory_space=pltpu.SMEM)


def ring(size, step):
    return [(i, (i + step) % size) for i in range(size)]


def tables(occupied_energy, virtual_energy, tile_occupied, tile_virtual, tile_exponent):
    def kernel(occupied, virtual, occupied_of, virtual_of, exponent, denominator, scales):
        me = lax.axis_index("pair")
        core = lax.axis_index("core")
        slot = lax.axis_index("x") * NZ + lax.axis_index("z")
        half, first = slot // (NXZ // 2), (slot % (NXZ // 2)) * PIECE

        def tile_of(relative, part):
            return lax.rem(2 * (me + relative + NPAIR) + part, NT)

        def energy(tile):
            return virtual[pl.ds(virtual_of[tile], 1)] - occupied[occupied_of[tile]]

        def scale(tile):
            level = exponent[tile]
            return jnp.where(level == -1, 0.5, jnp.where(level == 1, 2.0, 1.0)).astype(f32)

        lane = lax.broadcasted_iota(jnp.int32, (PIECE, TS), 1)
        chosen = lane == first + lax.broadcasted_iota(jnp.int32, (PIECE, TS), 0)
        for k, (r, c) in enumerate(PAIRS):
            row, column = tile_of(r, core), tile_of(c, half)
            of_row = jnp.sum(jnp.where(chosen, energy(row), 0.0), axis=1, keepdims=True)
            level = jnp.full((PIECE, TS), scale(row) * scale(column), f32)
            denominator[k * PIECE : (k + 1) * PIECE] = (of_row + energy(column)) / level
        for i, (q, _) in enumerate(ORDER):
            for part in (0, 1):
                n = 2 * i + part
                scales[n : n + 1] = jnp.full((1, TS), scale(tile_of(q, part)), f32)

    return pl.pallas_call(
        kernel,
        out_shape=(
            jax.ShapeDtypeStruct((len(PAIRS) * PIECE, TS), f32),
            jax.ShapeDtypeStruct((2 * len(ORDER), TS), f32),
        ),
        in_specs=[in_smem, in_vmem, in_smem, in_smem, in_smem],
        out_specs=(in_vmem, in_vmem),
        compiler_params=pltpu.CompilerParams(vmem_limit_bytes=VMEM_LIMIT),
        name="tables",
    )(occupied_energy, virtual_energy.reshape(VT, TS), tile_occupied, tile_virtual, tile_exponent)


def coulomb_pairs(blocks, pairs):
    names = sorted({d for pair in pairs for d in pair})

    def kernel(*refs):
        block = dict(zip(names, refs))
        own, other = refs[len(names) :]
        core = lax.axis_index("core")
        for k, (r, c) in enumerate(pairs):
            for out, part in ((own, core), (other, 1 - core)):
                left = block[r][:, pl.ds(pl.multiple_of(part * TS, TS), TS)]
                product = lax.dot_general(
                    left, block[c][...], (((0,), (0,)), ((), ())), preferred_element_type=f32
                )
                for h in (0, 1):
                    out[k, h] = product[:, h * TS : (h + 1) * TS].astype(out.dtype)

    shape = (len(pairs), 2, TS, TS)
    return pl.pallas_call(
        kernel,
        out_shape=(jax.ShapeDtypeStruct(shape, f32), jax.ShapeDtypeStruct(shape, bf16)),
        in_specs=[in_vmem] * len(names),
        out_specs=(in_vmem, in_vmem),
        compiler_params=pltpu.CompilerParams(vmem_limit_bytes=VMEM_LIMIT),
        name="coulomb_pairs",
    )(*[blocks[d] for d in names])


def sum_cores(own, received):
    pairs = sum(a.shape[0] for a in own)

    def kernel(*refs):
        parts = []
        for mine, theirs in zip(refs[: len(own)], refs[len(own) : -1]):
            count = mine.shape[0]
            total = (mine[...] + theirs[...].astype(f32)).reshape(count, NXZ, PIECE, TS)
            parts += [total[k] for k in range(count)]
        refs[-1][...] = jnp.concatenate(parts, axis=1).astype(bf16)

    return pl.pallas_call(
        kernel,
        out_shape=jax.ShapeDtypeStruct((NXZ, pairs * PIECE, TS), bf16),
        in_specs=[in_vmem] * (2 * len(own)),
        out_specs=in_vmem,
        compiler_params=pltpu.CompilerParams(vmem_limit_bytes=VMEM_LIMIT),
        name="sum_cores",
    )(*own, *received)


def amplitude_pieces(pieces, denominator):
    def kernel(pieces_ref, denominator_ref, *outs):
        total = jnp.sum(pieces_ref[...].astype(f32), axis=0) / denominator_ref[...]
        for k, out in enumerate(outs):
            out[...] = total[k * PIECE : (k + 2) * PIECE].astype(bf16)

    shape = jax.ShapeDtypeStruct((2 * PIECE, TS), bf16)
    return pl.pallas_call(
        kernel,
        out_shape=(shape,) * 4,
        in_specs=[in_vmem] * 2,
        out_specs=(in_vmem,) * 4,
        compiler_params=pltpu.CompilerParams(vmem_limit_bytes=VMEM_LIMIT),
        name="amplitude_pieces",
    )(pieces, denominator)


def spread(*pieces):
    rows = len(pieces) * 2 * PIECE

    def kernel(*refs):
        whole = jnp.concatenate([ref[...] for ref in refs[:-1]])
        refs[-1][...] = jnp.broadcast_to(whole[None], (NXZ, rows, TS))

    return pl.pallas_call(
        kernel,
        out_shape=jax.ShapeDtypeStruct((NXZ, rows, TS), bf16),
        in_specs=[in_vmem] * len(pieces),
        out_specs=in_vmem,
        compiler_params=pltpu.CompilerParams(vmem_limit_bytes=VMEM_LIMIT),
        name="spread",
    )(*pieces)


def gamma_rows(blocks, mine, theirs, scales):
    rows, width = blocks[0].shape
    names = [q for q, _ in ORDER]

    def kernel(*refs):
        block = dict(zip(names, refs))
        own, other, scale, out, matrix = refs[len(names) :]
        core = lax.axis_index("core")
        for pair in range(0, len(ORDER), 2):
            for part, source in ((core, own), (1 - core, other)):
                place = pl.ds(pl.multiple_of(part * TS, TS), TS)
                both = source[:, pair * PIECE : (pair + 2) * PIECE].astype(f32)
                for k in (0, 1):
                    i = pair + k
                    tiles = both[:, k * PIECE : (k + 1) * PIECE].reshape(2, TS, TS)
                    for h in (0, 1):
                        if ORDER[i][1]:
                            tile = tiles[h].T * scale[2 * i + h : 2 * i + h + 1]
                            matrix[i, h * TS : (h + 1) * TS, place] = tile.astype(bf16)
                        else:
                            tile = tiles[h] * scale[pl.ds(2 * i + part, 1)]
                            matrix[i, place, h * TS : (h + 1) * TS] = tile.astype(bf16)

        for start in range(0, rows, ROWS):
            total = None
            for i, (q, *_) in enumerate(ORDER):
                left = block[q][start : start + ROWS]
                term = jnp.dot(left, matrix[i], preferred_element_type=f32)
                total = term if total is None else total + term
            out[start : start + ROWS] = total.astype(bf16)

    return pl.pallas_call(
        kernel,
        out_shape=jax.ShapeDtypeStruct((rows, width), bf16),
        in_specs=[in_vmem] * (len(names) + 3),
        out_specs=in_vmem,
        scratch_shapes=[pltpu.VMEM((len(ORDER), WIDTH, WIDTH), bf16)],
        compiler_params=pltpu.CompilerParams(vmem_limit_bytes=VMEM_LIMIT),
        name="gamma_rows",
    )(*[blocks[q] for q in names], mine, theirs, scales)


def body(three_index, *energies):
    up, down = ring(NPAIR, 1), ring(NPAIR, -1)
    swap = ring(NCORE, 1)

    block = {0: three_index}
    block[-1] = lax.ppermute(block[0], "pair", up)
    block[1] = lax.ppermute(block[0], "pair", down)
    denominator, scales = tables(*energies)
    block[-1], denominator, scales = lax.optimization_barrier((block[-1], denominator, scales))
    block[-2] = lax.ppermute(block[-1], "pair", up)
    block[2] = lax.ppermute(block[1], "pair", down)

    early, other_early = coulomb_pairs(block, EARLY)
    got_early = lax.ppermute(other_early, "core", swap)
    late, other_late = coulomb_pairs(block, LATE)
    got_late = lax.ppermute(other_late, "core", swap)
    summed = sum_cores((early, late), (got_early, got_late))

    summed, block[-2] = lax.optimization_barrier((summed, block[-2]))
    block[-3] = lax.ppermute(block[-2], "pair", up)
    pieces = lax.all_to_all(summed, ("x", "z"), 0, 0)
    pieces, block[-3] = lax.optimization_barrier((pieces, block[-3]))

    kept, send_up, send_down, send_far = amplitude_pieces(pieces, denominator)
    lower2 = lax.ppermute(send_far, "pair", ring(NPAIR, 2))
    lower1 = lax.ppermute(send_up, "pair", up)
    upper1 = lax.ppermute(send_down, "pair", down)
    copies = spread(kept, lower1, upper1, lower2)

    copies, block[-3], block[2] = lax.optimization_barrier((copies, block[-3], block[2]))
    block[4] = lax.ppermute(block[-3], "pair", up)
    block[3] = lax.ppermute(block[2], "pair", down)
    mine = lax.all_to_all(copies, ("x", "z"), 0, 0)
    mine, block[3], block[4] = lax.optimization_barrier((mine, block[3], block[4]))
    theirs = lax.ppermute(mine, "core", swap)
    return gamma_rows(block, mine, theirs, scales)


def solution(mesh):
    grid = Mesh(mesh.devices.reshape(NX, NZ, NCORE, NPAIR), AUX + ("pair",))
    placed = (P(AUX, "pair"), P(), P(), P(), P(), P())
    return jax.shard_map(
        body, mesh=grid, in_specs=placed, out_specs=P(AUX, "pair"), check_vma=False
    )
```

time: 117 us -> 117 us (level)
  waiting for transfers between devices: 16.8 us -> 28 us
  local copies, waits for them, and re-layouts: 12.8 us -> 6.15 us
  starting transfers between devices: 79.6 us -> 75.6 us
    ppermute x1, waiting for transfers between devices: 0.01 us -> 12.7 us  [body(): block[-3] = lax.ppermute(block[-2], 'pair', up)]
    all_to_all x2 -> x1, starting transfers between devices: 21.5 us -> 14 us  [body(): pieces = lax.all_to_all(summed, ('x', 'z'), 0, 0)]
    all_to_all x2 -> x1, waiting for transfers between devices: 6.35 us -> 0.01 us  [body(): pieces = lax.all_to_all(summed, ('x', 'z'), 0, 0)]
    ppermute x1, waiting for transfers between devices: 0.01 us -> 5.11 us  [body(): block[3] = lax.ppermute(block[2], 'pair', down)]
    all_to_all x1, starting transfers between devices: 5.37 us -> 9.04 us  [body(): mine = lax.all_to_all(copies, ('x', 'z'), 0, 0)]
    slice x12 -> x0, local copies, waits for them, and re-layouts: 3.26 us -> none  [the longest x2 1.64 us: body(): scales = jnp.concatenate([turned[q % NPAIR] for q, *_ in ORDER])]
    ppermute x11 -> x10, starting transfers between devices: 38.5 us -> 41.5 us  [the longest x1 6.28 us: body(): got_early = lax.ppermute(other_early, 'core', swap)]
    ppermute x1, starting transfers between devices: 4.57 us -> 1.92 us  [body(): block[3] = lax.ppermute(block[2], 'pair', down)]
  transfers between devices with their start and end apart: 17 -> 15, of which waited for: 9 -> 7; matrix products, arithmetic and copies ran while one was open for 5% -> 0% of each run, Pallas kernels for 3% -> 2%
where the time goes in v5:
time: 117 us; the launch traced here: 116 us
  starting transfers between devices  75.6 us (65%)
  waiting for transfers between devices  28 us (24%)
  local copies, waits for them, and re-layouts  6.15 us (5%)
  Pallas kernels  5.82 us (5%)
    all_to_all x1, starting transfers between devices, body(): pieces = lax.all_to_all(summed, ('x', 'z'), 0, 0)  14 us
    ppermute x1, waiting for transfers between devices, body(): block[-3] = lax.ppermute(block[-2], 'pair', up)  12.7 us
    all_to_all x1, starting transfers between devices, body(): mine = lax.all_to_all(copies, ('x', 'z'), 0, 0)  9.04 us
    ppermute x1, starting transfers between devices, body(): theirs = lax.ppermute(mine, 'core', swap)  6.32 us
    ppermute x1, starting transfers between devices, body(): got_early = lax.ppermute(other_early, 'core', swap)  6.28 us
    unnamed x22, local copies, waits for them, and re-layouts  6.15 us
    ppermute x1, waiting for transfers between devices, body(): block[3] = lax.ppermute(block[2], 'pair', down)  5.11 us
    ppermute x1, starting transfers between devices, body(): got_late = lax.ppermute(other_late, 'core', swap)  5.07 us
  transfers between devices with their start and end apart: 15, of which 7 were waited for; matrix products, arithmetic and copies ran while one was open for 0% of the time, Pallas kernels for 2%

profile of v5, /device:TPU:1, one launch (start us, length us, event | category | flops | bytes accessed | tf_op | source)
XLA Modules:
  0.0 115.8 jit_solution(12687588777916148005)
XLA Ops:
  0.0 0.0 copy-start.9
  0.0 0.0 copy-start.8
  0.0 0.0 copy-start.7
  0.0 4.2 %collective-permute-start.1 = (bf16[896,256]{1,0:T(8,128)(2,1)}, bf16[896,256]{1,0:T(8,128)(2,1)S(1)}, u32[]{:S(2)}, u32[]{:S(2)}) collective-permute-start(bf16[896,256]{1,0:T(8,128)(2,1)} %refs_0_.1), channel_id=1, source_target_pairs={{0,1},{1,2},{2,3},{3,4},{4,5},{5,6},{6,7},{7,0},{8,9},{9,10},{10,1... | collective-permute-start | bytes 1376264 | tf_op jit(solution)/shard_map/ppermute | solution.py:211
  4.2 3.8 %collective-permute-start = (bf16[896,256]{1,0:T(8,128)(2,1)}, bf16[896,256]{1,0:T(8,128)(2,1)S(1)}, u32[]{:S(2)}, u32[]{:S(2)}) collective-permute-start(bf16[896,256]{1,0:T(8,128)(2,1)} %refs_0_.1), channel_id=1, source_target_pairs={{0,7},{1,0},{2,1},{3,2},{4,3},{5,4},{6,5},{7,6},{8,15},{9,8},{10,9... | collective-permute-start | bytes 1376264 | tf_op jit(solution)/shard_map/ppermute | solution.py:212
  8.0 0.0 copy-done.9
  8.0 0.0 copy-done.8
  8.0 0.0 copy-done.7
  8.0 0.0 copy-start.6
  8.0 0.9 copy-done.6
  8.9 0.0 copy-start.10
  8.9 0.7 copy-done.10
  9.6 0.7 tables.1
  10.3 1.9 %collective-permute-done.1.refs_0_.refs_1_.refs_2_ = bf16[896,256]{1,0:T(8,128)(2,1)S(1)} collective-permute-done((bf16[896,256]{1,0:T(8,128)(2,1)}, bf16[896,256]{1,0:T(8,128)(2,1)S(1)}, u32[]{:S(2)}, u32[]{:S(2)}) %collective-permute-start.1) | collective-permute-done | bytes 458784 | tf_op jit(solution)/shard_map/ppermute | solution.py:211
  12.1 5.0 %collective-permute-start.2 = (bf16[896,256]{1,0:T(8,128)(2,1)S(1)}, bf16[896,256]{1,0:T(8,128)(2,1)S(1)}, u32[]{:S(2)}, u32[]{:S(2)}) collective-permute-start(bf16[896,256]{1,0:T(8,128)(2,1)S(1)} %collective-permute-done.1.refs_0_.refs_1_.refs_2_), channel_id=1, source_target_pairs={{0,1},{1,2},{2,3},{3,4},{4,5},{5,6},{6,7},{7,0},{8,9},{9,10},{10,1... | collective-permute-start | bytes 1376264 | tf_op jit(solution)/shard_map/ppermute | solution.py:215
  17.1 0.0 collective-permute-done.refs_2_.refs_1_
  17.1 4.3 %collective-permute-start.3 = (bf16[896,256]{1,0:T(8,128)(2,1)S(1)}, bf16[896,256]{1,0:T(8,128)(2,1)S(1)}, u32[]{:S(2)}, u32[]{:S(2)}) collective-permute-start(bf16[896,256]{1,0:T(8,128)(2,1)S(1)} %collective-permute-done.refs_2_.refs_1_), channel_id=1, source_target_pairs={{0,7},{1,0},{2,1},{3,2},{4,3},{5,4},{6,5},{7,6},{8,15},{9,8},{10,9... | collective-permute-start | bytes 1376264 | tf_op jit(solution)/shard_map/ppermute | solution.py:216
  21.5 0.0 copy-start
  21.5 1.0 copy-done
  22.5 0.6 coulomb_pairs.2
  23.1 6.3 %collective-permute-start.4 = (bf16[3,2,128,128]{3,2,1,0:T(8,128)(2,1)S(1)}, bf16[3,2,128,128]{3,2,1,0:T(8,128)(2,1)S(1)}, u32[]{:S(2)}, u32[]{:S(2)}) collective-permute-start(bf16[3,2,128,128]{3,2,1,0:T(8,128)(2,1)S(1)} %get-tuple-element.33), channel_id=1, source_target_pairs={{0,8},{8,0},{1,9},{9,1},{2,10},{10,2},{3,11},{11,3},{4,12},{12,4},... | collective-permute-start | bytes 589832 | tf_op jit(solution)/shard_map/ppermute | solution.py:219
  29.4 0.0 collective-permute-done.2.refs_0_.refs_3_
  29.4 0.0 collective-permute-done.3.refs_2_.refs_4_
  29.5 0.5 coulomb_pairs.3
  29.9 5.1 %collective-permute-start.5 = (bf16[2,2,128,128]{3,2,1,0:T(8,128)(2,1)S(1)}, bf16[2,2,128,128]{3,2,1,0:T(8,128)(2,1)S(1)}, u32[]{:S(2)}, u32[]{:S(2)}) collective-permute-start(bf16[2,2,128,128]{3,2,1,0:T(8,128)(2,1)S(1)} %get-tuple-element.34), channel_id=1, source_target_pairs={{0,8},{8,0},{1,9},{9,1},{2,10},{10,2},{3,11},{11,3},{4,12},{12,4},... | collective-permute-start | bytes 393224 | tf_op jit(solution)/shard_map/ppermute | solution.py:221
  35.0 0.0 collective-permute-done.4.refs_2_
  35.0 1.0 collective-permute-done.5.refs_3_
  36.0 0.8 sum_cores.1
  36.8 14.0 %all-to-all-start = ((bf16[32,40,128]{2,1,0:T(8,128)(2,1)}), bf16[32,40,128]{2,1,0:T(8,128)(2,1)S(1)}, u32[]{:S(2)}, u32[]{:S(2)}) async-start(bf16[32,40,128]{2,1,0:T(8,128)(2,1)} %sum_cores.1), calls=%async_computation | async-start | bytes 655360 | tf_op jit(solution)/shard_map/all_to_all | solution.py:226
  50.8 2.9 %collective-permute-start.6 = (bf16[896,256]{1,0:T(8,128)(2,1)S(1)}, bf16[896,256]{1,0:T(8,128)(2,1)S(1)}, u32[]{:S(2)}, u32[]{:S(2)}) collective-permute-start(bf16[896,256]{1,0:T(8,128)(2,1)S(1)} %collective-permute-done.2.refs_0_.refs_3_), channel_id=1, source_target_pairs={{0,1},{1,2},{2,3},{3,4},{4,5},{5,6},{6,7},{7,0},{8,9},{9,10},{10,1... | collective-permute-start | bytes 1376264 | tf_op jit(solution)/shard_map/ppermute | solution.py:225
  53.6 12.7 %collective-permute-done.6.refs_6_ = bf16[896,256]{1,0:T(8,128)(2,1)S(1)} collective-permute-done((bf16[896,256]{1,0:T(8,128)(2,1)S(1)}, bf16[896,256]{1,0:T(8,128)(2,1)S(1)}, u32[]{:S(2)}, u32[]{:S(2)}) %collective-permute-start.6) | collective-permute-done | bytes 458784 | tf_op jit(solution)/shard_map/ppermute | solution.py:225
  66.4 0.0 all-to-all-done.pieces_ref
  66.4 0.1 amplitude_pieces.1
  66.4 1.9 %collective-permute-start.7 = (bf16[16,128]{1,0:T(8,128)(2,1)S(1)}, bf16[16,128]{1,0:T(8,128)(2,1)S(1)}, u32[]{:S(2)}, u32[]{:S(2)}) collective-permute-start(bf16[16,128]{1,0:T(8,128)(2,1)S(1)} %get-tuple-element.40), channel_id=1, source_target_pairs={{0,1},{1,2},{2,3},{3,4},{4,5},{5,6},{6,7},{7,0},{8,9},{9,10},{10,1... | collective-permute-start | bytes 12296 | tf_op jit(solution)/shard_map/ppermute | solution.py:231
  68.4 4.6 %collective-permute-start.8 = (bf16[16,128]{1,0:T(8,128)(2,1)S(1)}, bf16[16,128]{1,0:T(8,128)(2,1)S(1)}, u32[]{:S(2)}, u32[]{:S(2)}) collective-permute-start(bf16[16,128]{1,0:T(8,128)(2,1)S(1)} %get-tuple-element.41), channel_id=1, source_target_pairs={{0,7},{1,0},{2,1},{3,2},{4,3},{5,4},{6,5},{7,6},{8,15},{9,8},{10,9... | collective-permute-start | bytes 12296 | tf_op jit(solution)/shard_map/ppermute | solution.py:232
  72.9 3.0 %collective-permute-start.9 = (bf16[16,128]{1,0:T(8,128)(2,1)S(1)}, bf16[16,128]{1,0:T(8,128)(2,1)S(1)}, u32[]{:S(2)}, u32[]{:S(2)}) collective-permute-start(bf16[16,128]{1,0:T(8,128)(2,1)S(1)} %get-tuple-element.42), channel_id=1, source_target_pairs={{0,2},{1,3},{2,4},{3,5},{4,6},{5,7},{6,0},{7,1},{8,10},{9,11},{10,... | collective-permute-start | bytes 12296 | tf_op jit(solution)/shard_map/ppermute | solution.py:230
  75.9 0.0 collective-permute-done.7.refs_1_
  75.9 0.0 collective-permute-done.8.refs_2_
  75.9 3.5 %collective-permute-done.9.refs_3_ = bf16[16,128]{1,0:T(8,128)(2,1)S(1)} collective-permute-done((bf16[16,128]{1,0:T(8,128)(2,1)S(1)}, bf16[16,128]{1,0:T(8,128)(2,1)S(1)}, u32[]{:S(2)}, u32[]{:S(2)}) %collective-permute-start.9) | collective-permute-done | bytes 4128 | tf_op jit(solution)/shard_map/ppermute | solution.py:230
  79.4 0.9 spread.1
  80.3 0.0 copy-start.1
  80.3 9.0 %all-to-all-start.1 = ((bf16[32,64,128]{2,1,0:T(8,128)(2,1)}), bf16[32,64,128]{2,1,0:T(8,128)(2,1)S(1)}, u32[]{:S(2)}, u32[]{:S(2)}) async-start(bf16[32,64,128]{2,1,0:T(8,128)(2,1)} %spread.1), calls=%async_computation.1 | async-start | bytes 1048576 | tf_op jit(solution)/shard_map/all_to_all | solution.py:238
  89.4 1.9 %collective-permute-start.10 = (bf16[896,256]{1,0:T(8,128)(2,1)S(1)}, bf16[896,256]{1,0:T(8,128)(2,1)S(1)}, u32[]{:S(2)}, u32[]{:S(2)}) collective-permute-start(bf16[896,256]{1,0:T(8,128)(2,1)S(1)} %collective-permute-done.3.refs_2_.refs_4_), channel_id=1, source_target_pairs={{0,7},{1,0},{2,1},{3,2},{4,3},{5,4},{6,5},{7,6},{8,15},{9,8},{10,9... | collective-permute-start | bytes 1376264 | tf_op jit(solution)/shard_map/ppermute | solution.py:237
  91.3 3.4 %collective-permute-start.11 = (bf16[896,256]{1,0:T(8,128)(2,1)S(1)}, bf16[896,256]{1,0:T(8,128)(2,1)S(1)}, u32[]{:S(2)}, u32[]{:S(2)}) collective-permute-start(bf16[896,256]{1,0:T(8,128)(2,1)S(1)} %collective-permute-done.6.refs_6_), channel_id=1, source_target_pairs={{0,1},{1,2},{2,3},{3,4},{4,5},{5,6},{6,7},{7,0},{8,9},{9,10},{10,1... | collective-permute-start | bytes 1376264 | tf_op jit(solution)/shard_map/ppermute | solution.py:236
  94.7 5.1 %collective-permute-done.10.refs_5_ = bf16[896,256]{1,0:T(8,128)(2,1)S(1)} collective-permute-done((bf16[896,256]{1,0:T(8,128)(2,1)S(1)}, bf16[896,256]{1,0:T(8,128)(2,1)S(1)}, u32[]{:S(2)}, u32[]{:S(2)}) %collective-permute-start.10) | collective-permute-done | bytes 458784 | tf_op jit(solution)/shard_map/ppermute | solution.py:237
  99.8 0.0 copy-start.2
  99.8 0.8 copy-done.2
  100.6 2.4 %collective-permute-done.11.refs_7_ = bf16[896,256]{1,0:T(8,128)(2,1)S(1)} collective-permute-done((bf16[896,256]{1,0:T(8,128)(2,1)S(1)}, bf16[896,256]{1,0:T(8,128)(2,1)S(1)}, u32[]{:S(2)}, u32[]{:S(2)}) %collective-permute-start.11) | collective-permute-done | bytes 458784 | tf_op jit(solution)/shard_map/ppermute | solution.py:236
  102.9 0.0 copy-start.4
  102.9 0.8 copy-done.4
  103.7 0.0 all-to-all-done.1.refs_8_
  103.7 6.3 %collective-permute-start.12 = (bf16[32,64,128]{2,1,0:T(8,128)(2,1)S(1)}, bf16[32,64,128]{2,1,0:T(8,128)(2,1)S(1)}, u32[]{:S(2)}, u32[]{:S(2)}) collective-permute-start(bf16[32,64,128]{2,1,0:T(8,128)(2,1)S(1)} %all-to-all-done.1.refs_8_), channel_id=1, source_target_pairs={{0,8},{8,0},{1,9},{9,1},{2,10},{10,2},{3,11},{11,3},{4,12},{12,4},... | collective-permute-start | bytes 1572872 | tf_op jit(solution)/shard_map/ppermute | solution.py:240
  110.0 1.5 %collective-permute-done.12.refs_9_ = bf16[32,64,128]{2,1,0:T(8,128)(2,1)S(1)} collective-permute-done((bf16[32,64,128]{2,1,0:T(8,128)(2,1)S(1)}, bf16[32,64,128]{2,1,0:T(8,128)(2,1)S(1)}, u32[]{:S(2)}, u32[]{:S(2)}) %collective-permute-start.12) | collective-permute-done | bytes 524320 | tf_op jit(solution)/shard_map/ppermute | solution.py:240
  111.6 0.0 copy-done.1
  111.6 0.0 copy-start.3
  111.6 1.0 copy-done.3
  112.6 0.0 copy-start.5
  112.6 1.0 copy-done.5
  113.6 2.2 %gamma_rows.1 = bf16[896,256]{1,0:T(8,128)(2,1)} custom-call(bf16[896,256]{1,0:T(8,128)(2,1)S(1)} %copy-done.1, bf16[896,256]{1,0:T(8,128)(2,1)S(1)} %collective-permute-done.refs_2_.refs_1_, bf16[896,256]{1,0:T(8,128)(2,1)S(1)} %collective-permute-done.1.refs_0_.refs_1_.refs_2_, bf16[896,256]{1,0:T(8,128)(2,1)S(1)} %collective-permute-done.2.refs_0_.refs_3_, ...), custom_call_target="tpu_custom_call" | custom-call | tf_op jit(solution)/shard_map/gamma_rows/pallas_call | solution.py:195
Async XLA Ops:
  0.0 8.0 %copy-start.9 = (s32[16]{0:T(128)S(1)}, s32[16]{0:T(128)}, u32[]{:S(2)}) copy-start(s32[16]{0:T(128)} %virtual_of.1) | copy-start | bytes 196
  0.0 8.0 %copy-start.8 = (s32[16]{0:T(128)S(1)}, s32[16]{0:T(128)}, u32[]{:S(2)}) copy-start(s32[16]{0:T(128)} %occupied_of.1) | copy-start | bytes 196
  0.0 8.0 %copy-start.7 = (f32[64]{0:T(128)S(1)}, f32[64]{0:T(128)}, u32[]{:S(2)}) copy-start(f32[64]{0:T(128)} %occupied.1) | copy-start | bytes 772
  0.0 12.1 %collective-permute-start.1 = (bf16[896,256]{1,0:T(8,128)(2,1)}, bf16[896,256]{1,0:T(8,128)(2,1)S(1)}, u32[]{:S(2)}, u32[]{:S(2)}) collective-permute-start(bf16[896,256]{1,0:T(8,128)(2,1)} %refs_0_.1), channel_id=1, source_target_pairs={{0,1},{1,2},{2,3},{3,4},{4,5},{5,6},{6,7},{7,0},{8,9},{9,10},{10,1... | collective-permute-start | bytes 1376264 | tf_op jit(solution)/shard_map/ppermute | solution.py:211
  4.2 12.9 %collective-permute-start = (bf16[896,256]{1,0:T(8,128)(2,1)}, bf16[896,256]{1,0:T(8,128)(2,1)S(1)}, u32[]{:S(2)}, u32[]{:S(2)}) collective-permute-start(bf16[896,256]{1,0:T(8,128)(2,1)} %refs_0_.1), channel_id=1, source_target_pairs={{0,7},{1,0},{2,1},{3,2},{4,3},{5,4},{6,5},{7,6},{8,15},{9,8},{10,9... | collective-permute-start | bytes 1376264 | tf_op jit(solution)/shard_map/ppermute | solution.py:212
  8.0 0.9 copy-start.6
  8.9 0.7 copy-start.10
  12.1 17.3 %collective-permute-start.2 = (bf16[896,256]{1,0:T(8,128)(2,1)S(1)}, bf16[896,256]{1,0:T(8,128)(2,1)S(1)}, u32[]{:S(2)}, u32[]{:S(2)}) collective-permute-start(bf16[896,256]{1,0:T(8,128)(2,1)S(1)} %collective-permute-done.1.refs_0_.refs_1_.refs_2_), channel_id=1, source_target_pairs={{0,1},{1,2},{2,3},{3,4},{4,5},{5,6},{6,7},{7,0},{8,9},{9,10},{10,1... | collective-permute-start | bytes 1376264 | tf_op jit(solution)/shard_map/ppermute | solution.py:215
  17.1 12.3 %collective-permute-start.3 = (bf16[896,256]{1,0:T(8,128)(2,1)S(1)}, bf16[896,256]{1,0:T(8,128)(2,1)S(1)}, u32[]{:S(2)}, u32[]{:S(2)}) collective-permute-start(bf16[896,256]{1,0:T(8,128)(2,1)S(1)} %collective-permute-done.refs_2_.refs_1_), channel_id=1, source_target_pairs={{0,7},{1,0},{2,1},{3,2},{4,3},{5,4},{6,5},{7,6},{8,15},{9,8},{10,9... | collective-permute-start | bytes 1376264 | tf_op jit(solution)/shard_map/ppermute | solution.py:216
  21.5 1.0 copy-start
  23.1 11.9 %collective-permute-start.4 = (bf16[3,2,128,128]{3,2,1,0:T(8,128)(2,1)S(1)}, bf16[3,2,128,128]{3,2,1,0:T(8,128)(2,1)S(1)}, u32[]{:S(2)}, u32[]{:S(2)}) collective-permute-start(bf16[3,2,128,128]{3,2,1,0:T(8,128)(2,1)S(1)} %get-tuple-element.33), channel_id=1, source_target_pairs={{0,8},{8,0},{1,9},{9,1},{2,10},{10,2},{3,11},{11,3},{4,12},{12,4},... | collective-permute-start | bytes 589832 | tf_op jit(solution)/shard_map/ppermute | solution.py:219
  29.9 6.0 %collective-permute-start.5 = (bf16[2,2,128,128]{3,2,1,0:T(8,128)(2,1)S(1)}, bf16[2,2,128,128]{3,2,1,0:T(8,128)(2,1)S(1)}, u32[]{:S(2)}, u32[]{:S(2)}) collective-permute-start(bf16[2,2,128,128]{3,2,1,0:T(8,128)(2,1)S(1)} %get-tuple-element.34), channel_id=1, source_target_pairs={{0,8},{8,0},{1,9},{9,1},{2,10},{10,2},{3,11},{11,3},{4,12},{12,4},... | collective-permute-start | bytes 393224 | tf_op jit(solution)/shard_map/ppermute | solution.py:221
  36.8 29.6 %all-to-all-start = ((bf16[32,40,128]{2,1,0:T(8,128)(2,1)}), bf16[32,40,128]{2,1,0:T(8,128)(2,1)S(1)}, u32[]{:S(2)}, u32[]{:S(2)}) async-start(bf16[32,40,128]{2,1,0:T(8,128)(2,1)} %sum_cores.1), calls=%async_computation | async-start | bytes 655360 | tf_op jit(solution)/shard_map/all_to_all | solution.py:226
  50.8 15.6 %collective-permute-start.6 = (bf16[896,256]{1,0:T(8,128)(2,1)S(1)}, bf16[896,256]{1,0:T(8,128)(2,1)S(1)}, u32[]{:S(2)}, u32[]{:S(2)}) collective-permute-start(bf16[896,256]{1,0:T(8,128)(2,1)S(1)} %collective-permute-done.2.refs_0_.refs_3_), channel_id=1, source_target_pairs={{0,1},{1,2},{2,3},{3,4},{4,5},{5,6},{6,7},{7,0},{8,9},{9,10},{10,1... | collective-permute-start | bytes 1376264 | tf_op jit(solution)/shard_map/ppermute | solution.py:225
  66.4 9.5 %collective-permute-start.7 = (bf16[16,128]{1,0:T(8,128)(2,1)S(1)}, bf16[16,128]{1,0:T(8,128)(2,1)S(1)}, u32[]{:S(2)}, u32[]{:S(2)}) collective-permute-start(bf16[16,128]{1,0:T(8,128)(2,1)S(1)} %get-tuple-element.40), channel_id=1, source_target_pairs={{0,1},{1,2},{2,3},{3,4},{4,5},{5,6},{6,7},{7,0},{8,9},{9,10},{10,1... | collective-permute-start | bytes 12296 | tf_op jit(solution)/shard_map/ppermute | solution.py:231
  68.4 7.6 %collective-permute-start.8 = (bf16[16,128]{1,0:T(8,128)(2,1)S(1)}, bf16[16,128]{1,0:T(8,128)(2,1)S(1)}, u32[]{:S(2)}, u32[]{:S(2)}) collective-permute-start(bf16[16,128]{1,0:T(8,128)(2,1)S(1)} %get-tuple-element.41), channel_id=1, source_target_pairs={{0,7},{1,0},{2,1},{3,2},{4,3},{5,4},{6,5},{7,6},{8,15},{9,8},{10,9... | collective-permute-start | bytes 12296 | tf_op jit(solution)/shard_map/ppermute | solution.py:232
  72.9 6.5 %collective-permute-start.9 = (bf16[16,128]{1,0:T(8,128)(2,1)S(1)}, bf16[16,128]{1,0:T(8,128)(2,1)S(1)}, u32[]{:S(2)}, u32[]{:S(2)}) collective-permute-start(bf16[16,128]{1,0:T(8,128)(2,1)S(1)} %get-tuple-element.42), channel_id=1, source_target_pairs={{0,2},{1,3},{2,4},{3,5},{4,6},{5,7},{6,0},{7,1},{8,10},{9,11},{10,... | collective-permute-start | bytes 12296 | tf_op jit(solution)/shard_map/ppermute | solution.py:230
  80.3 31.2 %copy-start.1 = (bf16[896,256]{1,0:T(8,128)(2,1)S(1)}, bf16[896,256]{1,0:T(8,128)(2,1)}, u32[]{:S(2)}) copy-start(bf16[896,256]{1,0:T(8,128)(2,1)} %refs_0_.1) | copy-start | bytes 1376260
  80.3 23.4 %all-to-all-start.1 = ((bf16[32,64,128]{2,1,0:T(8,128)(2,1)}), bf16[32,64,128]{2,1,0:T(8,128)(2,1)S(1)}, u32[]{:S(2)}, u32[]{:S(2)}) async-start(bf16[32,64,128]{2,1,0:T(8,128)(2,1)} %spread.1), calls=%async_computation.1 | async-start | bytes 1048576 | tf_op jit(solution)/shard_map/all_to_all | solution.py:238
  89.4 10.4 %collective-permute-start.10 = (bf16[896,256]{1,0:T(8,128)(2,1)S(1)}, bf16[896,256]{1,0:T(8,128)(2,1)S(1)}, u32[]{:S(2)}, u32[]{:S(2)}) collective-permute-start(bf16[896,256]{1,0:T(8,128)(2,1)S(1)} %collective-permute-done.3.refs_2_.refs_4_), channel_id=1, source_target_pairs={{0,7},{1,0},{2,1},{3,2},{4,3},{5,4},{6,5},{7,6},{8,15},{9,8},{10,9... | collective-permute-start | bytes 1376264 | tf_op jit(solution)/shard_map/ppermute | solution.py:237
  91.3 11.6 %collective-permute-start.11 = (bf16[896,256]{1,0:T(8,128)(2,1)S(1)}, bf16[896,256]{1,0:T(8,128)(2,1)S(1)}, u32[]{:S(2)}, u32[]{:S(2)}) collective-permute-start(bf16[896,256]{1,0:T(8,128)(2,1)S(1)} %collective-permute-done.6.refs_6_), channel_id=1, source_target_pairs={{0,1},{1,2},{2,3},{3,4},{4,5},{5,6},{6,7},{7,0},{8,9},{9,10},{10,1... | collective-permute-start | bytes 1376264 | tf_op jit(solution)/shard_map/ppermute | solution.py:236
  99.8 0.8 copy-start.2
  102.9 0.8 copy-start.4
  103.7 7.8 %collective-permute-start.12 = (bf16[32,64,128]{2,1,0:T(8,128)(2,1)S(1)}, bf16[32,64,128]{2,1,0:T(8,128)(2,1)S(1)}, u32[]{:S(2)}, u32[]{:S(2)}) collective-permute-start(bf16[32,64,128]{2,1,0:T(8,128)(2,1)S(1)} %all-to-all-done.1.refs_8_), channel_id=1, source_target_pairs={{0,8},{8,0},{1,9},{9,1},{2,10},{10,2},{3,11},{11,3},{4,12},{12,4},... | collective-permute-start | bytes 1572872 | tf_op jit(solution)/shard_map/ppermute | solution.py:240
  111.6 1.0 copy-start.3
  112.6 1.0 copy-start.5

commit v6 on v5

--- a/solution.py
+++ b/solution.py
@@ -221,22 +221,20 @@
     got_late = lax.ppermute(other_late, "core", swap)
     summed = sum_cores((early, late), (got_early, got_late))
 
-    summed, block[-2] = lax.optimization_barrier((summed, block[-2]))
+    summed, block[-2], block[2] = lax.optimization_barrier((summed, block[-2], block[2]))
     block[-3] = lax.ppermute(block[-2], "pair", up)
+    block[3] = lax.ppermute(block[2], "pair", down)
     pieces = lax.all_to_all(summed, ("x", "z"), 0, 0)
     pieces, block[-3] = lax.optimization_barrier((pieces, block[-3]))
 
     kept, send_up, send_down, send_far = amplitude_pieces(pieces, denominator)
+    block[4] = lax.ppermute(block[-3], "pair", up)
     lower2 = lax.ppermute(send_far, "pair", ring(NPAIR, 2))
     lower1 = lax.ppermute(send_up, "pair", up)
     upper1 = lax.ppermute(send_down, "pair", down)
     copies = spread(kept, lower1, upper1, lower2)
-
-    copies, block[-3], block[2] = lax.optimization_barrier((copies, block[-3], block[2]))
-    block[4] = lax.ppermute(block[-3], "pair", up)
-    block[3] = lax.ppermute(block[2], "pair", down)
+    copies, block[3], block[4] = lax.optimization_barrier((copies, block[3], block[4]))
     mine = lax.all_to_all(copies, ("x", "z"), 0, 0)
-    mine, block[3], block[4] = lax.optimization_barrier((mine, block[3], block[4]))
     theirs = lax.ppermute(mine, "core", swap)
     return gamma_rows(block, mine, theirs, scales)
 

time: 117 us -> 114 us (0.974)
  blocking collectives: 0 us -> 20.7 us
  waiting for transfers between devices: 28 us -> 14.8 us
  starting transfers between devices: 75.6 us -> 70.6 us
  local copies, waits for them, and re-layouts: 6.15 us -> 2.57 us
    all_to_all x0 -> x1, blocking collectives: none -> 20.7 us  [body(): mine = lax.all_to_all(copies, ('x', 'z'), 0, 0)]
    all_to_all x1 -> x0, starting transfers between devices: 9.04 us -> none  [body(): mine = lax.all_to_all(copies, ('x', 'z'), 0, 0)]
    ppermute x1, waiting for transfers between devices: 5.11 us -> 0.01 us  [body(): block[3] = lax.ppermute(block[2], 'pair', down)]
    ppermute x1, waiting for transfers between devices: 12.7 us -> 8.34 us  [body(): block[-3] = lax.ppermute(block[-2], 'pair', up)]
    unnamed x22 -> x14, local copies, waits for them, and re-layouts: 6.15 us -> 2.57 us
    ppermute x1, starting transfers between devices: 1.92 us -> 4.38 us  [body(): block[3] = lax.ppermute(block[2], 'pair', down)]
    ppermute x1, waiting for transfers between devices: 3.46 us -> 1.08 us  [body(): lower2 = lax.ppermute(send_far, 'pair', ring(NPAIR, 2))]
    ppermute x1, waiting for transfers between devices: 2.37 us -> 0.01 us  [body(): block[4] = lax.ppermute(block[-3], 'pair', up)]
  transfers between devices with their start and end apart: 15 -> 14, of which waited for: 7 -> 6; matrix products, arithmetic and copies ran while one was open for 0% -> 0% of each run, Pallas kernels for 2% -> 2%
where the time goes in v6:
time: 114 us
  starting transfers between devices  70.6 us (62%)
  blocking collectives  20.7 us (18%)
  waiting for transfers between devices  14.8 us (13%)
  Pallas kernels  4.98 us (4%)
  local copies, waits for them, and re-layouts  2.57 us (2%)
    all_to_all x1, blocking collectives, body(): mine = lax.all_to_all(copies, ('x', 'z'), 0, 0)  20.7 us
    all_to_all x1, starting transfers between devices, body(): pieces = lax.all_to_all(summed, ('x', 'z'), 0, 0)  14 us
    ppermute x1, waiting for transfers between devices, body(): block[-3] = lax.ppermute(block[-2], 'pair', up)  8.34 us
    ppermute x1, starting transfers between devices, body(): theirs = lax.ppermute(mine, 'core', swap)  7.76 us
    ppermute x1, starting transfers between devices, body(): got_early = lax.ppermute(other_early, 'core', swap)  6.28 us
    ppermute x1, starting transfers between devices, body(): got_late = lax.ppermute(other_late, 'core', swap)  5.07 us
    ppermute x1, starting transfers between devices, body(): block[-2] = lax.ppermute(block[-1], 'pair', up)  4.98 us
    ppermute x1, starting transfers between devices, body(): lower2 = lax.ppermute(send_far, 'pair', ring(NPAIR, 2))  4.5 us
  transfers between devices with their start and end apart: 14, of which 6 were waited for; matrix products, arithmetic and copies ran while one was open for 0% of the time, Pallas kernels for 2%

profile of v6, /device:TPU:1, one launch (start us, length us, event | category | flops | bytes accessed | tf_op | source)
XLA Modules:
  0.0 113.8 jit_solution(8797476387151454050)
XLA Ops:
  0.0 0.0 copy-start.5
  0.0 0.0 copy-start.4
  0.0 0.0 copy-start.3
  0.0 4.2 %collective-permute-start.1 = (bf16[896,256]{1,0:T(8,128)(2,1)}, bf16[896,256]{1,0:T(8,128)(2,1)S(1)}, u32[]{:S(2)}, u32[]{:S(2)}) collective-permute-start(bf16[896,256]{1,0:T(8,128)(2,1)} %refs_0_.1), channel_id=1, source_target_pairs={{0,1},{1,2},{2,3},{3,4},{4,5},{5,6},{6,7},{7,0},{8,9},{9,10},{10,1... | collective-permute-start | bytes 1376264 | tf_op jit(solution)/shard_map/ppermute | solution.py:211
  4.2 3.8 %collective-permute-start = (bf16[896,256]{1,0:T(8,128)(2,1)}, bf16[896,256]{1,0:T(8,128)(2,1)S(1)}, u32[]{:S(2)}, u32[]{:S(2)}) collective-permute-start(bf16[896,256]{1,0:T(8,128)(2,1)} %refs_0_.1), channel_id=1, source_target_pairs={{0,7},{1,0},{2,1},{3,2},{4,3},{5,4},{6,5},{7,6},{8,15},{9,8},{10,9... | collective-permute-start | bytes 1376264 | tf_op jit(solution)/shard_map/ppermute | solution.py:212
  8.0 0.0 copy-done.5
  8.0 0.0 copy-done.4
  8.0 0.0 copy-done.3
  8.0 0.0 copy-start.2
  8.0 0.9 copy-done.2
  8.9 0.0 copy-start.6
  8.9 0.7 copy-done.6
  9.6 0.7 tables.1
  10.3 1.9 %collective-permute-done.1.refs_0_.refs_1_.refs_2_ = bf16[896,256]{1,0:T(8,128)(2,1)S(1)} collective-permute-done((bf16[896,256]{1,0:T(8,128)(2,1)}, bf16[896,256]{1,0:T(8,128)(2,1)S(1)}, u32[]{:S(2)}, u32[]{:S(2)}) %collective-permute-start.1) | collective-permute-done | bytes 458784 | tf_op jit(solution)/shard_map/ppermute | solution.py:211
  12.1 5.0 %collective-permute-start.2 = (bf16[896,256]{1,0:T(8,128)(2,1)S(1)}, bf16[896,256]{1,0:T(8,128)(2,1)S(1)}, u32[]{:S(2)}, u32[]{:S(2)}) collective-permute-start(bf16[896,256]{1,0:T(8,128)(2,1)S(1)} %collective-permute-done.1.refs_0_.refs_1_.refs_2_), channel_id=1, source_target_pairs={{0,1},{1,2},{2,3},{3,4},{4,5},{5,6},{6,7},{7,0},{8,9},{9,10},{10,1... | collective-permute-start | bytes 1376264 | tf_op jit(solution)/shard_map/ppermute | solution.py:215
  17.1 0.0 collective-permute-done.refs_2_.refs_1_
  17.1 4.3 %collective-permute-start.3 = (bf16[896,256]{1,0:T(8,128)(2,1)S(1)}, bf16[896,256]{1,0:T(8,128)(2,1)S(1)}, u32[]{:S(2)}, u32[]{:S(2)}) collective-permute-start(bf16[896,256]{1,0:T(8,128)(2,1)S(1)} %collective-permute-done.refs_2_.refs_1_), channel_id=1, source_target_pairs={{0,7},{1,0},{2,1},{3,2},{4,3},{5,4},{6,5},{7,6},{8,15},{9,8},{10,9... | collective-permute-start | bytes 1376264 | tf_op jit(solution)/shard_map/ppermute | solution.py:216
  21.5 0.0 copy-start
  21.5 1.0 copy-done
  22.5 0.6 coulomb_pairs.2
  23.1 6.3 %collective-permute-start.4 = (bf16[3,2,128,128]{3,2,1,0:T(8,128)(2,1)S(1)}, bf16[3,2,128,128]{3,2,1,0:T(8,128)(2,1)S(1)}, u32[]{:S(2)}, u32[]{:S(2)}) collective-permute-start(bf16[3,2,128,128]{3,2,1,0:T(8,128)(2,1)S(1)} %get-tuple-element.31), channel_id=1, source_target_pairs={{0,8},{8,0},{1,9},{9,1},{2,10},{10,2},{3,11},{11,3},{4,12},{12,4},... | collective-permute-start | bytes 589832 | tf_op jit(solution)/shard_map/ppermute | solution.py:219
  29.4 0.0 collective-permute-done.2.refs_0_.refs_3_
  29.4 0.0 collective-permute-done.3.refs_2_.refs_4_
  29.5 0.5 coulomb_pairs.3
  29.9 5.1 %collective-permute-start.5 = (bf16[2,2,128,128]{3,2,1,0:T(8,128)(2,1)S(1)}, bf16[2,2,128,128]{3,2,1,0:T(8,128)(2,1)S(1)}, u32[]{:S(2)}, u32[]{:S(2)}) collective-permute-start(bf16[2,2,128,128]{3,2,1,0:T(8,128)(2,1)S(1)} %get-tuple-element.32), channel_id=1, source_target_pairs={{0,8},{8,0},{1,9},{9,1},{2,10},{10,2},{3,11},{11,3},{4,12},{12,4},... | collective-permute-start | bytes 393224 | tf_op jit(solution)/shard_map/ppermute | solution.py:221
  35.0 0.0 collective-permute-done.4.refs_2_
  35.0 1.0 collective-permute-done.5.refs_3_
  36.0 0.8 sum_cores.1
  36.8 14.0 %all-to-all-start = ((bf16[32,40,128]{2,1,0:T(8,128)(2,1)}), bf16[32,40,128]{2,1,0:T(8,128)(2,1)S(1)}, u32[]{:S(2)}, u32[]{:S(2)}) async-start(bf16[32,40,128]{2,1,0:T(8,128)(2,1)} %sum_cores.1), calls=%async_computation | async-start | bytes 655360 | tf_op jit(solution)/shard_map/all_to_all | solution.py:227
  50.8 2.9 %collective-permute-start.6 = (bf16[896,256]{1,0:T(8,128)(2,1)S(1)}, bf16[896,256]{1,0:T(8,128)(2,1)S(1)}, u32[]{:S(2)}, u32[]{:S(2)}) collective-permute-start(bf16[896,256]{1,0:T(8,128)(2,1)S(1)} %collective-permute-done.2.refs_0_.refs_3_), channel_id=1, source_target_pairs={{0,1},{1,2},{2,3},{3,4},{4,5},{5,6},{6,7},{7,0},{8,9},{9,10},{10,1... | collective-permute-start | bytes 1376264 | tf_op jit(solution)/shard_map/ppermute | solution.py:225
  53.6 4.4 %collective-permute-start.10 = (bf16[896,256]{1,0:T(8,128)(2,1)S(1)}, bf16[896,256]{1,0:T(8,128)(2,1)S(1)}, u32[]{:S(2)}, u32[]{:S(2)}) collective-permute-start(bf16[896,256]{1,0:T(8,128)(2,1)S(1)} %collective-permute-done.3.refs_2_.refs_4_), channel_id=1, source_target_pairs={{0,7},{1,0},{2,1},{3,2},{4,3},{5,4},{6,5},{7,6},{8,15},{9,8},{10,9... | collective-permute-start | bytes 1376264 | tf_op jit(solution)/shard_map/ppermute | solution.py:226
  58.0 8.3 %collective-permute-done.6.refs_6_ = bf16[896,256]{1,0:T(8,128)(2,1)S(1)} collective-permute-done((bf16[896,256]{1,0:T(8,128)(2,1)S(1)}, bf16[896,256]{1,0:T(8,128)(2,1)S(1)}, u32[]{:S(2)}, u32[]{:S(2)}) %collective-permute-start.6) | collective-permute-done | bytes 458784 | tf_op jit(solution)/shard_map/ppermute | solution.py:225
  66.4 0.0 all-to-all-done.pieces_ref
  66.4 1.9 %collective-permute-start.11 = (bf16[896,256]{1,0:T(8,128)(2,1)S(1)}, bf16[896,256]{1,0:T(8,128)(2,1)S(1)}, u32[]{:S(2)}, u32[]{:S(2)}) collective-permute-start(bf16[896,256]{1,0:T(8,128)(2,1)S(1)} %collective-permute-done.6.refs_6_), channel_id=1, source_target_pairs={{0,1},{1,2},{2,3},{3,4},{4,5},{5,6},{6,7},{7,0},{8,9},{9,10},{10,1... | collective-permute-start | bytes 1376264 | tf_op jit(solution)/shard_map/ppermute | solution.py:231
  68.3 0.1 amplitude_pieces.1
  68.4 3.7 %collective-permute-start.7 = (bf16[16,128]{1,0:T(8,128)(2,1)S(1)}, bf16[16,128]{1,0:T(8,128)(2,1)S(1)}, u32[]{:S(2)}, u32[]{:S(2)}) collective-permute-start(bf16[16,128]{1,0:T(8,128)(2,1)S(1)} %get-tuple-element.39), channel_id=1, source_target_pairs={{0,1},{1,2},{2,3},{3,4},{4,5},{5,6},{6,7},{7,0},{8,9},{9,10},{10,1... | collective-permute-start | bytes 12296 | tf_op jit(solution)/shard_map/ppermute | solution.py:233
  72.1 2.8 %collective-permute-start.8 = (bf16[16,128]{1,0:T(8,128)(2,1)S(1)}, bf16[16,128]{1,0:T(8,128)(2,1)S(1)}, u32[]{:S(2)}, u32[]{:S(2)}) collective-permute-start(bf16[16,128]{1,0:T(8,128)(2,1)S(1)} %get-tuple-element.40), channel_id=1, source_target_pairs={{0,7},{1,0},{2,1},{3,2},{4,3},{5,4},{6,5},{7,6},{8,15},{9,8},{10,9... | collective-permute-start | bytes 12296 | tf_op jit(solution)/shard_map/ppermute | solution.py:234
  74.9 4.5 %collective-permute-start.9 = (bf16[16,128]{1,0:T(8,128)(2,1)S(1)}, bf16[16,128]{1,0:T(8,128)(2,1)S(1)}, u32[]{:S(2)}, u32[]{:S(2)}) collective-permute-start(bf16[16,128]{1,0:T(8,128)(2,1)S(1)} %get-tuple-element.41), channel_id=1, source_target_pairs={{0,2},{1,3},{2,4},{3,5},{4,6},{5,7},{6,0},{7,1},{8,10},{9,11},{10,... | collective-permute-start | bytes 12296 | tf_op jit(solution)/shard_map/ppermute | solution.py:232
  79.4 1.0 collective-permute-done.7.refs_1_
  80.4 0.0 collective-permute-done.8.refs_2_
  80.4 1.1 collective-permute-done.9.refs_3_
  81.5 0.1 spread.1
  81.6 0.0 copy-start.1
  81.6 0.0 collective-permute-done.10.refs_5_
  81.6 0.0 collective-permute-done.11.refs_7_
  81.6 20.7 %all_to_all.10.refs_8_ = bf16[32,64,128]{2,1,0:T(8,128)(2,1)S(1)} all-to-all(bf16[32,64,128]{2,1,0:T(8,128)(2,1)S(1)} %spread.1), channel_id=1, replica_groups=mesh['x'=4,'z'=8,'core'=2,'pair'=8] {'x','z'}, dimensions={0} | all-to-all | bytes 1048576 | tf_op jit(solution)/shard_map/all_to_all | solution.py:237
  102.3 7.8 %collective-permute-start.12 = (bf16[32,64,128]{2,1,0:T(8,128)(2,1)S(1)}, bf16[32,64,128]{2,1,0:T(8,128)(2,1)S(1)}, u32[]{:S(2)}, u32[]{:S(2)}) collective-permute-start(bf16[32,64,128]{2,1,0:T(8,128)(2,1)S(1)} %all_to_all.10.refs_8_), channel_id=1, source_target_pairs={{0,8},{8,0},{1,9},{9,1},{2,10},{10,2},{3,11},{11,3},{4,12},{12,4},... | collective-permute-start | bytes 1572872 | tf_op jit(solution)/shard_map/ppermute | solution.py:238
  110.1 1.5 %collective-permute-done.12.refs_9_ = bf16[32,64,128]{2,1,0:T(8,128)(2,1)S(1)} collective-permute-done((bf16[32,64,128]{2,1,0:T(8,128)(2,1)S(1)}, bf16[32,64,128]{2,1,0:T(8,128)(2,1)S(1)}, u32[]{:S(2)}, u32[]{:S(2)}) %collective-permute-start.12) | collective-permute-done | bytes 524320 | tf_op jit(solution)/shard_map/ppermute | solution.py:238
  111.6 0.0 copy-done.1
  111.6 2.2 %gamma_rows.1 = bf16[896,256]{1,0:T(8,128)(2,1)} custom-call(bf16[896,256]{1,0:T(8,128)(2,1)S(1)} %copy-done.1, bf16[896,256]{1,0:T(8,128)(2,1)S(1)} %collective-permute-done.refs_2_.refs_1_, bf16[896,256]{1,0:T(8,128)(2,1)S(1)} %collective-permute-done.1.refs_0_.refs_1_.refs_2_, bf16[896,256]{1,0:T(8,128)(2,1)S(1)} %collective-permute-done.2.refs_0_.refs_3_, ...), custom_call_target="tpu_custom_call" | custom-call | tf_op jit(solution)/shard_map/gamma_rows/pallas_call | solution.py:195
Async XLA Ops:
  0.0 8.0 %copy-start.5 = (s32[16]{0:T(128)S(1)}, s32[16]{0:T(128)}, u32[]{:S(2)}) copy-start(s32[16]{0:T(128)} %virtual_of.1) | copy-start | bytes 196
  0.0 8.0 %copy-start.4 = (s32[16]{0:T(128)S(1)}, s32[16]{0:T(128)}, u32[]{:S(2)}) copy-start(s32[16]{0:T(128)} %occupied_of.1) | copy-start | bytes 196
  0.0 8.0 %copy-start.3 = (f32[64]{0:T(128)S(1)}, f32[64]{0:T(128)}, u32[]{:S(2)}) copy-start(f32[64]{0:T(128)} %occupied.1) | copy-start | bytes 772
  0.0 12.1 %collective-permute-start.1 = (bf16[896,256]{1,0:T(8,128)(2,1)}, bf16[896,256]{1,0:T(8,128)(2,1)S(1)}, u32[]{:S(2)}, u32[]{:S(2)}) collective-permute-start(bf16[896,256]{1,0:T(8,128)(2,1)} %refs_0_.1), channel_id=1, source_target_pairs={{0,1},{1,2},{2,3},{3,4},{4,5},{5,6},{6,7},{7,0},{8,9},{9,10},{10,1... | collective-permute-start | bytes 1376264 | tf_op jit(solution)/shard_map/ppermute | solution.py:211
  4.2 12.9 %collective-permute-start = (bf16[896,256]{1,0:T(8,128)(2,1)}, bf16[896,256]{1,0:T(8,128)(2,1)S(1)}, u32[]{:S(2)}, u32[]{:S(2)}) collective-permute-start(bf16[896,256]{1,0:T(8,128)(2,1)} %refs_0_.1), channel_id=1, source_target_pairs={{0,7},{1,0},{2,1},{3,2},{4,3},{5,4},{6,5},{7,6},{8,15},{9,8},{10,9... | collective-permute-start | bytes 1376264 | tf_op jit(solution)/shard_map/ppermute | solution.py:212
  8.0 0.9 copy-start.2
  8.9 0.7 copy-start.6
  12.1 17.3 %collective-permute-start.2 = (bf16[896,256]{1,0:T(8,128)(2,1)S(1)}, bf16[896,256]{1,0:T(8,128)(2,1)S(1)}, u32[]{:S(2)}, u32[]{:S(2)}) collective-permute-start(bf16[896,256]{1,0:T(8,128)(2,1)S(1)} %collective-permute-done.1.refs_0_.refs_1_.refs_2_), channel_id=1, source_target_pairs={{0,1},{1,2},{2,3},{3,4},{4,5},{5,6},{6,7},{7,0},{8,9},{9,10},{10,1... | collective-permute-start | bytes 1376264 | tf_op jit(solution)/shard_map/ppermute | solution.py:215
  17.1 12.3 %collective-permute-start.3 = (bf16[896,256]{1,0:T(8,128)(2,1)S(1)}, bf16[896,256]{1,0:T(8,128)(2,1)S(1)}, u32[]{:S(2)}, u32[]{:S(2)}) collective-permute-start(bf16[896,256]{1,0:T(8,128)(2,1)S(1)} %collective-permute-done.refs_2_.refs_1_), channel_id=1, source_target_pairs={{0,7},{1,0},{2,1},{3,2},{4,3},{5,4},{6,5},{7,6},{8,15},{9,8},{10,9... | collective-permute-start | bytes 1376264 | tf_op jit(solution)/shard_map/ppermute | solution.py:216
  21.5 1.0 copy-start
  23.1 11.9 %collective-permute-start.4 = (bf16[3,2,128,128]{3,2,1,0:T(8,128)(2,1)S(1)}, bf16[3,2,128,128]{3,2,1,0:T(8,128)(2,1)S(1)}, u32[]{:S(2)}, u32[]{:S(2)}) collective-permute-start(bf16[3,2,128,128]{3,2,1,0:T(8,128)(2,1)S(1)} %get-tuple-element.31), channel_id=1, source_target_pairs={{0,8},{8,0},{1,9},{9,1},{2,10},{10,2},{3,11},{11,3},{4,12},{12,4},... | collective-permute-start | bytes 589832 | tf_op jit(solution)/shard_map/ppermute | solution.py:219
  29.9 6.0 %collective-permute-start.5 = (bf16[2,2,128,128]{3,2,1,0:T(8,128)(2,1)S(1)}, bf16[2,2,128,128]{3,2,1,0:T(8,128)(2,1)S(1)}, u32[]{:S(2)}, u32[]{:S(2)}) collective-permute-start(bf16[2,2,128,128]{3,2,1,0:T(8,128)(2,1)S(1)} %get-tuple-element.32), channel_id=1, source_target_pairs={{0,8},{8,0},{1,9},{9,1},{2,10},{10,2},{3,11},{11,3},{4,12},{12,4},... | collective-permute-start | bytes 393224 | tf_op jit(solution)/shard_map/ppermute | solution.py:221
  36.8 29.6 %all-to-all-start = ((bf16[32,40,128]{2,1,0:T(8,128)(2,1)}), bf16[32,40,128]{2,1,0:T(8,128)(2,1)S(1)}, u32[]{:S(2)}, u32[]{:S(2)}) async-start(bf16[32,40,128]{2,1,0:T(8,128)(2,1)} %sum_cores.1), calls=%async_computation | async-start | bytes 655360 | tf_op jit(solution)/shard_map/all_to_all | solution.py:227
  50.8 15.6 %collective-permute-start.6 = (bf16[896,256]{1,0:T(8,128)(2,1)S(1)}, bf16[896,256]{1,0:T(8,128)(2,1)S(1)}, u32[]{:S(2)}, u32[]{:S(2)}) collective-permute-start(bf16[896,256]{1,0:T(8,128)(2,1)S(1)} %collective-permute-done.2.refs_0_.refs_3_), channel_id=1, source_target_pairs={{0,1},{1,2},{2,3},{3,4},{4,5},{5,6},{6,7},{7,0},{8,9},{9,10},{10,1... | collective-permute-start | bytes 1376264 | tf_op jit(solution)/shard_map/ppermute | solution.py:225
  53.6 28.0 %collective-permute-start.10 = (bf16[896,256]{1,0:T(8,128)(2,1)S(1)}, bf16[896,256]{1,0:T(8,128)(2,1)S(1)}, u32[]{:S(2)}, u32[]{:S(2)}) collective-permute-start(bf16[896,256]{1,0:T(8,128)(2,1)S(1)} %collective-permute-done.3.refs_2_.refs_4_), channel_id=1, source_target_pairs={{0,7},{1,0},{2,1},{3,2},{4,3},{5,4},{6,5},{7,6},{8,15},{9,8},{10,9... | collective-permute-start | bytes 1376264 | tf_op jit(solution)/shard_map/ppermute | solution.py:226
  66.4 15.2 %collective-permute-start.11 = (bf16[896,256]{1,0:T(8,128)(2,1)S(1)}, bf16[896,256]{1,0:T(8,128)(2,1)S(1)}, u32[]{:S(2)}, u32[]{:S(2)}) collective-permute-start(bf16[896,256]{1,0:T(8,128)(2,1)S(1)} %collective-permute-done.6.refs_6_), channel_id=1, source_target_pairs={{0,1},{1,2},{2,3},{3,4},{4,5},{5,6},{6,7},{7,0},{8,9},{9,10},{10,1... | collective-permute-start | bytes 1376264 | tf_op jit(solution)/shard_map/ppermute | solution.py:231
  68.4 12.0 %collective-permute-start.7 = (bf16[16,128]{1,0:T(8,128)(2,1)S(1)}, bf16[16,128]{1,0:T(8,128)(2,1)S(1)}, u32[]{:S(2)}, u32[]{:S(2)}) collective-permute-start(bf16[16,128]{1,0:T(8,128)(2,1)S(1)} %get-tuple-element.39), channel_id=1, source_target_pairs={{0,1},{1,2},{2,3},{3,4},{4,5},{5,6},{6,7},{7,0},{8,9},{9,10},{10,1... | collective-permute-start | bytes 12296 | tf_op jit(solution)/shard_map/ppermute | solution.py:233
  72.1 8.3 %collective-permute-start.8 = (bf16[16,128]{1,0:T(8,128)(2,1)S(1)}, bf16[16,128]{1,0:T(8,128)(2,1)S(1)}, u32[]{:S(2)}, u32[]{:S(2)}) collective-permute-start(bf16[16,128]{1,0:T(8,128)(2,1)S(1)} %get-tuple-element.40), channel_id=1, source_target_pairs={{0,7},{1,0},{2,1},{3,2},{4,3},{5,4},{6,5},{7,6},{8,15},{9,8},{10,9... | collective-permute-start | bytes 12296 | tf_op jit(solution)/shard_map/ppermute | solution.py:234
  74.9 6.6 %collective-permute-start.9 = (bf16[16,128]{1,0:T(8,128)(2,1)S(1)}, bf16[16,128]{1,0:T(8,128)(2,1)S(1)}, u32[]{:S(2)}, u32[]{:S(2)}) collective-permute-start(bf16[16,128]{1,0:T(8,128)(2,1)S(1)} %get-tuple-element.41), channel_id=1, source_target_pairs={{0,2},{1,3},{2,4},{3,5},{4,6},{5,7},{6,0},{7,1},{8,10},{9,11},{10,... | collective-permute-start | bytes 12296 | tf_op jit(solution)/shard_map/ppermute | solution.py:232
  81.6 30.0 %copy-start.1 = (bf16[896,256]{1,0:T(8,128)(2,1)S(1)}, bf16[896,256]{1,0:T(8,128)(2,1)}, u32[]{:S(2)}) copy-start(bf16[896,256]{1,0:T(8,128)(2,1)} %refs_0_.1) | copy-start | bytes 1376260
  102.3 9.3 %collective-permute-start.12 = (bf16[32,64,128]{2,1,0:T(8,128)(2,1)S(1)}, bf16[32,64,128]{2,1,0:T(8,128)(2,1)S(1)}, u32[]{:S(2)}, u32[]{:S(2)}) collective-permute-start(bf16[32,64,128]{2,1,0:T(8,128)(2,1)S(1)} %all_to_all.10.refs_8_), channel_id=1, source_target_pairs={{0,8},{8,0},{1,9},{9,1},{2,10},{10,2},{3,11},{11,3},{4,12},{12,4},... | collective-permute-start | bytes 1572872 | tf_op jit(solution)/shard_map/ppermute | solution.py:238

commit v7 on v6

--- a/solution.py
+++ b/solution.py
@@ -16,16 +16,9 @@
 PAIRS = EARLY + LATE
 WIDTH = 2 * TS
 PIECE = WIDTH // NXZ
-ORDER = (
-    (0, False),
-    (1, True),
-    (-1, False),
-    (-2, False),
-    (2, True),
-    (3, True),
-    (-3, False),
-    (4, False),
-)
+SENDS = ((0, (0, 1)), (1, (1, 2)), (-1, (2, 3)), (2, (3, 4)))
+GETS = tuple((PAIRS[k][0] - d, PAIRS[k][1] - d) for d, pairs in SENDS for k in pairs)
+ORDER = tuple((r, False) if c == 0 else (c, True) for r, c in GETS)
 ROWS = 224
 VMEM_LIMIT = 12 * 1024 * 1024
 bf16, f32 = jnp.bfloat16, jnp.float32
@@ -41,7 +34,7 @@
     def kernel(occupied, virtual, occupied_of, virtual_of, exponent, denominator, scales):
         me = lax.axis_index("pair")
         core = lax.axis_index("core")
-        slot = lax.axis_index("x") * NZ + lax.axis_index("z")
+        slot = lax.axis_index("z") * NX + lax.axis_index("x")
         half, first = slot // (NXZ // 2), (slot % (NXZ // 2)) * PIECE
 
         def tile_of(relative, part):
@@ -56,7 +49,7 @@
 
         lane = lax.broadcasted_iota(jnp.int32, (PIECE, TS), 1)
         chosen = lane == first + lax.broadcasted_iota(jnp.int32, (PIECE, TS), 0)
-        for k, (r, c) in enumerate(PAIRS):
+        for k, (r, c) in enumerate(GETS):
             row, column = tile_of(r, core), tile_of(c, half)
             of_row = jnp.sum(jnp.where(chosen, energy(row), 0.0), axis=1, keepdims=True)
             level = jnp.full((PIECE, TS), scale(row) * scale(column), f32)
@@ -69,7 +62,7 @@
     return pl.pallas_call(
         kernel,
         out_shape=(
-            jax.ShapeDtypeStruct((len(PAIRS) * PIECE, TS), f32),
+            jax.ShapeDtypeStruct((len(GETS) * PIECE, TS), f32),
             jax.ShapeDtypeStruct((2 * len(ORDER), TS), f32),
         ),
         in_specs=[in_smem, in_vmem, in_smem, in_smem, in_smem],
@@ -108,18 +101,21 @@
 
 def sum_cores(own, received):
     pairs = sum(a.shape[0] for a in own)
+    rows = WIDTH // NZ
 
     def kernel(*refs):
-        parts = []
+        out = refs[-1]
+        n = 0
         for mine, theirs in zip(refs[: len(own)], refs[len(own) : -1]):
             count = mine.shape[0]
-            total = (mine[...] + theirs[...].astype(f32)).reshape(count, NXZ, PIECE, TS)
-            parts += [total[k] for k in range(count)]
-        refs[-1][...] = jnp.concatenate(parts, axis=1).astype(bf16)
-
-    return pl.pallas_call(
-        kernel,
-        out_shape=jax.ShapeDtypeStruct((NXZ, pairs * PIECE, TS), bf16),
+            total = (mine[...] + theirs[...].astype(f32)).astype(bf16).reshape(count, NZ, rows, TS)
+            for k in range(count):
+                out[:, (n + k) * rows : (n + k + 1) * rows] = total[k]
+            n += count
+
+    return pl.pallas_call(
+        kernel,
+        out_shape=jax.ShapeDtypeStruct((NZ, pairs * rows, TS), bf16),
         in_specs=[in_vmem] * (2 * len(own)),
         out_specs=in_vmem,
         compiler_params=pltpu.CompilerParams(vmem_limit_bytes=VMEM_LIMIT),
@@ -127,47 +123,57 @@
     )(*own, *received)
 
 
-def amplitude_pieces(pieces, denominator):
-    def kernel(pieces_ref, denominator_ref, *outs):
-        total = jnp.sum(pieces_ref[...].astype(f32), axis=0) / denominator_ref[...]
-        for k, out in enumerate(outs):
-            out[...] = total[k * PIECE : (k + 2) * PIECE].astype(bf16)
-
-    shape = jax.ShapeDtypeStruct((2 * PIECE, TS), bf16)
-    return pl.pallas_call(
-        kernel,
-        out_shape=(shape,) * 4,
+def sum_z(parts):
+    def kernel(parts_ref, out):
+        me = lax.axis_index("pair")
+        total = jnp.sum(parts_ref[...].astype(f32), axis=0).reshape(len(PAIRS), NX, PIECE, TS)
+        out[...] = jnp.zeros_like(out)
+        for d, (first, second) in SENDS:
+            both = jnp.concatenate([total[first], total[second]], axis=1)
+            out[pl.ds(NX * lax.rem(me + d + NPAIR, NPAIR), NX)] = both.astype(bf16)
+
+    return pl.pallas_call(
+        kernel,
+        out_shape=jax.ShapeDtypeStruct((NPAIR * NX, 2 * PIECE, TS), bf16),
+        in_specs=[in_vmem],
+        out_specs=in_vmem,
+        compiler_params=pltpu.CompilerParams(vmem_limit_bytes=VMEM_LIMIT),
+        name="sum_z",
+    )(parts)
+
+
+def amplitude_copies(parts, denominator):
+    rows = len(GETS) * PIECE
+
+    def kernel(parts_ref, denominator_ref, out):
+        me = lax.axis_index("pair")
+        total = jnp.concatenate(
+            [
+                jnp.sum(parts_ref[pl.ds(NX * lax.rem(me - d + NPAIR, NPAIR), NX)].astype(f32), axis=0)
+                for d, _ in SENDS
+            ]
+        )
+        amplitude = (total / denominator_ref[...]).astype(bf16)
+        out[...] = jnp.broadcast_to(amplitude[None], out.shape)
+
+    return pl.pallas_call(
+        kernel,
+        out_shape=jax.ShapeDtypeStruct((NXZ, rows, TS), bf16),
         in_specs=[in_vmem] * 2,
-        out_specs=(in_vmem,) * 4,
-        compiler_params=pltpu.CompilerParams(vmem_limit_bytes=VMEM_LIMIT),
-        name="amplitude_pieces",
-    )(pieces, denominator)
-
-
-def spread(*pieces):
-    rows = len(pieces) * 2 * PIECE
-
-    def kernel(*refs):
-        whole = jnp.concatenate([ref[...] for ref in refs[:-1]])
-        refs[-1][...] = jnp.broadcast_to(whole[None], (NXZ, rows, TS))
-
-    return pl.pallas_call(
-        kernel,
-        out_shape=jax.ShapeDtypeStruct((NXZ, rows, TS), bf16),
-        in_specs=[in_vmem] * len(pieces),
-        out_specs=in_vmem,
-        compiler_params=pltpu.CompilerParams(vmem_limit_bytes=VMEM_LIMIT),
-        name="spread",
-    )(*pieces)
-
-
-def gamma_rows(blocks, mine, theirs, scales):
+        out_specs=in_vmem,
+        compiler_params=pltpu.CompilerParams(vmem_limit_bytes=VMEM_LIMIT),
+        name="amplitude_copies",
+    )(parts, denominator)
+
+
+def gamma_rows(blocks, last, mine, theirs, scales):
     rows, width = blocks[0].shape
-    names = [q for q, _ in ORDER]
+    names = [q for q, _ in ORDER[:-1]]
 
     def kernel(*refs):
         block = dict(zip(names, refs))
-        own, other, scale, out, matrix = refs[len(names) :]
+        n = len(names)
+        own, other, scale, out, matrix = refs[n + len(last) :]
         core = lax.axis_index("core")
         for pair in range(0, len(ORDER), 2):
             for part, source in ((core, own), (1 - core, other)):
@@ -184,23 +190,25 @@
                             tile = tiles[h] * scale[pl.ds(2 * i + part, 1)]
                             matrix[i, place, h * TS : (h + 1) * TS] = tile.astype(bf16)
 
+        height = rows // len(last)
         for start in range(0, rows, ROWS):
-            total = None
-            for i, (q, *_) in enumerate(ORDER):
-                left = block[q][start : start + ROWS]
-                term = jnp.dot(left, matrix[i], preferred_element_type=f32)
-                total = term if total is None else total + term
+            part, offset = divmod(start, height)
+            total = jnp.dot(
+                refs[n + part][offset : offset + ROWS], matrix[n], preferred_element_type=f32
+            )
+            for i, q in enumerate(names):
+                total += jnp.dot(block[q][start : start + ROWS], matrix[i], preferred_element_type=f32)
             out[start : start + ROWS] = total.astype(bf16)
 
     return pl.pallas_call(
         kernel,
         out_shape=jax.ShapeDtypeStruct((rows, width), bf16),
-        in_specs=[in_vmem] * (len(names) + 3),
+        in_specs=[in_vmem] * (len(names) + len(last) + 3),
         out_specs=in_vmem,
         scratch_shapes=[pltpu.VMEM((len(ORDER), WIDTH, WIDTH), bf16)],
         compiler_params=pltpu.CompilerParams(vmem_limit_bytes=VMEM_LIMIT),
         name="gamma_rows",
-    )(*[blocks[q] for q in names], mine, theirs, scales)
+    )(*[blocks[q] for q in names], *last, mine, theirs, scales)
 
 
 def body(three_index, *energies):
@@ -224,19 +232,16 @@
     summed, block[-2], block[2] = lax.optimization_barrier((summed, block[-2], block[2]))
     block[-3] = lax.ppermute(block[-2], "pair", up)
     block[3] = lax.ppermute(block[2], "pair", down)
-    pieces = lax.all_to_all(summed, ("x", "z"), 0, 0)
-    pieces, block[-3] = lax.optimization_barrier((pieces, block[-3]))
-
-    kept, send_up, send_down, send_far = amplitude_pieces(pieces, denominator)
-    block[4] = lax.ppermute(block[-3], "pair", up)
-    lower2 = lax.ppermute(send_far, "pair", ring(NPAIR, 2))
-    lower1 = lax.ppermute(send_up, "pair", up)
-    upper1 = lax.ppermute(send_down, "pair", down)
-    copies = spread(kept, lower1, upper1, lower2)
-    copies, block[3], block[4] = lax.optimization_barrier((copies, block[3], block[4]))
-    mine = lax.all_to_all(copies, ("x", "z"), 0, 0)
+    parts = lax.all_to_all(summed, "z", 0, 0)
+    parts = lax.all_to_all(sum_z(parts), ("pair", "x"), 0, 0)
+    copies = amplitude_copies(parts, denominator)
+
+    copies, block[-3], block[3] = lax.optimization_barrier((copies, block[-3], block[3]))
+    last = (lax.ppermute(block[-3], "pair", up),)
+    mine = lax.all_to_all(copies, ("z", "x"), 0, 0)
+    mine, last = lax.optimization_barrier((mine, last))
     theirs = lax.ppermute(mine, "core", swap)
-    return gamma_rows(block, mine, theirs, scales)
+    return gamma_rows(block, last, mine, theirs, scales)
 
 
 def solution(mesh):

time: 114 us -> 113 us (level)
  starting transfers between devices: 70.6 us -> 60.2 us
  waiting for transfers between devices: 14.8 us -> 21.9 us
  local copies, waits for them, and re-layouts: 2.57 us -> 4.35 us
  Pallas kernels: 4.98 us -> 6.75 us
  blocking collectives: 20.7 us -> 19 us
    ppermute x4 -> x1, starting transfers between devices: 12.9 us -> 2.73 us  [body(): last = (lax.ppermute(block[-3], 'pair', up),)]
    ppermute x1, waiting for transfers between devices: 8.34 us -> 0.01 us  [body(): block[-3] = lax.ppermute(block[-2], 'pair', up)]
    ppermute x4 -> x1, waiting for transfers between devices: 2.1 us -> 10.3 us  [body(): last = (lax.ppermute(block[-3], 'pair', up),)]
    all_to_all x1 -> x2, waiting for transfers between devices: 0.01 us -> 7.26 us  [the longest x1 6.39 us: body(): parts = lax.all_to_all(summed, 'z', 0, 0)]
    unnamed x14 -> x18, local copies, waits for them, and re-layouts: 2.57 us -> 4.35 us
    all_to_all x1, blocking collectives: 20.7 us -> 19 us  [body(): parts = lax.all_to_all(sum_z(parts), ('pair', 'x'), 0, 0)]
    ppermute x1, starting transfers between devices: 7.76 us -> 6.41 us  [body(): theirs = lax.ppermute(mine, 'core', swap)]
    all_to_all x1 -> x2, starting transfers between devices: 14 us -> 15.2 us  [the longest x1 11.2 us: body(): parts = lax.all_to_all(summed, 'z', 0, 0)]
  transfers between devices with their start and end apart: 14 -> 12, of which waited for: 6 -> 6; matrix products, arithmetic and copies ran while one was open for 0% -> 0% of each run, Pallas kernels for 2% -> 2%
where the time goes in v7:
time: 113 us; the launch traced here: 112 us
  starting transfers between devices  60.2 us (53%)
  waiting for transfers between devices  21.9 us (19%)
  blocking collectives  19 us (17%)
  Pallas kernels  6.75 us (6%)
  local copies, waits for them, and re-layouts  4.35 us (4%)
    all_to_all x1, blocking collectives, body(): parts = lax.all_to_all(sum_z(parts), ('pair', 'x'), 0, 0)  19 us
    all_to_all x1, starting transfers between devices, body(): parts = lax.all_to_all(summed, 'z', 0, 0)  11.2 us
    ppermute x1, waiting for transfers between devices, body(): last = (lax.ppermute(block[-3], 'pair', up),)  10.3 us
    ppermute x1, starting transfers between devices, body(): theirs = lax.ppermute(mine, 'core', swap)  6.41 us
    all_to_all x1, waiting for transfers between devices, body(): parts = lax.all_to_all(summed, 'z', 0, 0)  6.39 us
    ppermute x1, starting transfers between devices, body(): got_early = lax.ppermute(other_early, 'core', swap)  6.28 us
    ppermute x1, starting transfers between devices, body(): got_late = lax.ppermute(other_late, 'core', swap)  5.07 us
    ppermute x1, starting transfers between devices, body(): block[-2] = lax.ppermute(block[-1], 'pair', up)  4.98 us
  transfers between devices with their start and end apart: 12, of which 6 were waited for; matrix products, arithmetic and copies ran while one was open for 0% of the time, Pallas kernels for 2%

profile of v7, /device:TPU:1, one launch (start us, length us, event | category | flops | bytes accessed | tf_op | source)
XLA Modules:
  0.0 112.4 jit_solution(2082191043679309130)
XLA Ops:
  0.0 0.0 copy-start.7
  0.0 0.0 copy-start.6
  0.0 0.0 copy-start.5
  0.0 4.2 %collective-permute-start.1 = (bf16[896,256]{1,0:T(8,128)(2,1)}, bf16[896,256]{1,0:T(8,128)(2,1)S(1)}, u32[]{:S(2)}, u32[]{:S(2)}) collective-permute-start(bf16[896,256]{1,0:T(8,128)(2,1)} %refs_0_.1), channel_id=1, source_target_pairs={{0,1},{1,2},{2,3},{3,4},{4,5},{5,6},{6,7},{7,0},{8,9},{9,10},{10,1... | collective-permute-start | bytes 1376264 | tf_op jit(solution)/shard_map/ppermute | solution.py:219
  4.2 3.8 %collective-permute-start = (bf16[896,256]{1,0:T(8,128)(2,1)}, bf16[896,256]{1,0:T(8,128)(2,1)S(1)}, u32[]{:S(2)}, u32[]{:S(2)}) collective-permute-start(bf16[896,256]{1,0:T(8,128)(2,1)} %refs_0_.1), channel_id=1, source_target_pairs={{0,7},{1,0},{2,1},{3,2},{4,3},{5,4},{6,5},{7,6},{8,15},{9,8},{10,9... | collective-permute-start | bytes 1376264 | tf_op jit(solution)/shard_map/ppermute | solution.py:220
  8.0 0.0 copy-done.7
  8.0 0.0 copy-done.6
  8.0 0.0 copy-done.5
  8.0 0.0 copy-start.4
  8.0 0.9 copy-done.4
  8.9 0.0 copy-start.8
  8.9 0.7 copy-done.8
  9.6 0.7 tables.1
  10.3 1.8 %collective-permute-done.1.refs_0_.refs_1_.refs_2_ = bf16[896,256]{1,0:T(8,128)(2,1)S(1)} collective-permute-done((bf16[896,256]{1,0:T(8,128)(2,1)}, bf16[896,256]{1,0:T(8,128)(2,1)S(1)}, u32[]{:S(2)}, u32[]{:S(2)}) %collective-permute-start.1) | collective-permute-done | bytes 458784 | tf_op jit(solution)/shard_map/ppermute | solution.py:219
  12.1 5.0 %collective-permute-start.2 = (bf16[896,256]{1,0:T(8,128)(2,1)S(1)}, bf16[896,256]{1,0:T(8,128)(2,1)S(1)}, u32[]{:S(2)}, u32[]{:S(2)}) collective-permute-start(bf16[896,256]{1,0:T(8,128)(2,1)S(1)} %collective-permute-done.1.refs_0_.refs_1_.refs_2_), channel_id=1, source_target_pairs={{0,1},{1,2},{2,3},{3,4},{4,5},{5,6},{6,7},{7,0},{8,9},{9,10},{10,1... | collective-permute-start | bytes 1376264 | tf_op jit(solution)/shard_map/ppermute | solution.py:223
  17.1 0.0 collective-permute-done.refs_2_.refs_1_
  17.1 4.3 %collective-permute-start.3 = (bf16[896,256]{1,0:T(8,128)(2,1)S(1)}, bf16[896,256]{1,0:T(8,128)(2,1)S(1)}, u32[]{:S(2)}, u32[]{:S(2)}) collective-permute-start(bf16[896,256]{1,0:T(8,128)(2,1)S(1)} %collective-permute-done.refs_2_.refs_1_), channel_id=1, source_target_pairs={{0,7},{1,0},{2,1},{3,2},{4,3},{5,4},{6,5},{7,6},{8,15},{9,8},{10,9... | collective-permute-start | bytes 1376264 | tf_op jit(solution)/shard_map/ppermute | solution.py:224
  21.5 0.0 copy-start
  21.5 1.0 copy-done
  22.5 0.6 coulomb_pairs.2
  23.1 6.3 %collective-permute-start.4 = (bf16[3,2,128,128]{3,2,1,0:T(8,128)(2,1)S(1)}, bf16[3,2,128,128]{3,2,1,0:T(8,128)(2,1)S(1)}, u32[]{:S(2)}, u32[]{:S(2)}) collective-permute-start(bf16[3,2,128,128]{3,2,1,0:T(8,128)(2,1)S(1)} %get-tuple-element.27), channel_id=1, source_target_pairs={{0,8},{8,0},{1,9},{9,1},{2,10},{10,2},{3,11},{11,3},{4,12},{12,4},... | collective-permute-start | bytes 589832 | tf_op jit(solution)/shard_map/ppermute | solution.py:227
  29.4 0.0 collective-permute-done.2.refs_0_.refs_3_
  29.4 0.0 collective-permute-done.3.refs_2_.refs_4_
  29.5 0.5 coulomb_pairs.3
  29.9 5.1 %collective-permute-start.5 = (bf16[2,2,128,128]{3,2,1,0:T(8,128)(2,1)S(1)}, bf16[2,2,128,128]{3,2,1,0:T(8,128)(2,1)S(1)}, u32[]{:S(2)}, u32[]{:S(2)}) collective-permute-start(bf16[2,2,128,128]{3,2,1,0:T(8,128)(2,1)S(1)} %get-tuple-element.28), channel_id=1, source_target_pairs={{0,8},{8,0},{1,9},{9,1},{2,10},{10,2},{3,11},{11,3},{4,12},{12,4},... | collective-permute-start | bytes 393224 | tf_op jit(solution)/shard_map/ppermute | solution.py:229
  35.0 0.0 collective-permute-done.4.refs_2_
  35.0 1.0 collective-permute-done.5.refs_3_
  36.0 0.8 sum_cores.1
  36.8 11.2 %all-to-all-start = ((bf16[8,160,128]{2,1,0:T(8,128)(2,1)}), bf16[8,160,128]{2,1,0:T(8,128)(2,1)S(1)}, u32[]{:S(2)}, u32[]{:S(2)}) async-start(bf16[8,160,128]{2,1,0:T(8,128)(2,1)} %sum_cores.1), calls=%async_computation | async-start | bytes 655360 | tf_op jit(solution)/shard_map/all_to_all | solution.py:235
  47.9 2.9 %collective-permute-start.6 = (bf16[896,256]{1,0:T(8,128)(2,1)S(1)}, bf16[896,256]{1,0:T(8,128)(2,1)S(1)}, u32[]{:S(2)}, u32[]{:S(2)}) collective-permute-start(bf16[896,256]{1,0:T(8,128)(2,1)S(1)} %collective-permute-done.2.refs_0_.refs_3_), channel_id=1, source_target_pairs={{0,1},{1,2},{2,3},{3,4},{4,5},{5,6},{6,7},{7,0},{8,9},{9,10},{10,1... | collective-permute-start | bytes 1376264 | tf_op jit(solution)/shard_map/ppermute | solution.py:233
  50.8 4.4 %collective-permute-start.7 = (bf16[896,256]{1,0:T(8,128)(2,1)S(1)}, bf16[896,256]{1,0:T(8,128)(2,1)}, u32[]{:S(2)}, u32[]{:S(2)}) collective-permute-start(bf16[896,256]{1,0:T(8,128)(2,1)S(1)} %collective-permute-done.3.refs_2_.refs_4_), channel_id=1, source_target_pairs={{0,7},{1,0},{2,1},{3,2},{4,3},{5,4},{6,5},{7,6},{8,15},{9,8},{10,9... | collective-permute-start | bytes 1376264 | tf_op jit(solution)/shard_map/ppermute | solution.py:234
  55.2 6.4 %all-to-all-done.parts_ref = bf16[8,160,128]{2,1,0:T(8,128)(2,1)S(1)} async-done(((bf16[8,160,128]{2,1,0:T(8,128)(2,1)}), bf16[8,160,128]{2,1,0:T(8,128)(2,1)S(1)}, u32[]{:S(2)}, u32[]{:S(2)}) %all-to-all-start) | async-done | bytes 327712 | tf_op jit(solution)/shard_map/all_to_all | solution.py:235
  61.5 0.1 sum_z.1
  61.6 19.0 %all_to_all.15.parts_ref = bf16[32,16,128]{2,1,0:T(8,128)(2,1)S(1)} all-to-all(bf16[32,16,128]{2,1,0:T(8,128)(2,1)S(1)} %sum_z.1), channel_id=1, replica_groups=mesh['x'=4,'z'=8,'core'=2,'pair'=8] {'pair','x'}, dimensions={0} | all-to-all | bytes 262144 | tf_op jit(solution)/shard_map/all_to_all | solution.py:236
  80.6 0.9 amplitude_copies.1
  81.5 0.0 copy-start.1
  81.5 0.0 collective-permute-done.6.refs_6_
  81.5 0.0 collective-permute-done.7.refs_5_
  81.5 4.0 %all-to-all-start.2 = ((bf16[32,64,128]{2,1,0:T(8,128)(2,1)}), bf16[32,64,128]{2,1,0:T(8,128)(2,1)S(1)}, u32[]{:S(2)}, u32[]{:S(2)}) async-start(bf16[32,64,128]{2,1,0:T(8,128)(2,1)} %amplitude_copies.1), calls=%async_computation.2 | async-start | bytes 1048576 | tf_op jit(solution)/shard_map/all_to_all | solution.py:241
  85.5 2.7 %collective-permute-start.8 = (bf16[896,256]{1,0:T(8,128)(2,1)S(1)}, bf16[896,256]{1,0:T(8,128)(2,1)S(1)}, u32[]{:S(2)}, u32[]{:S(2)}) collective-permute-start(bf16[896,256]{1,0:T(8,128)(2,1)S(1)} %collective-permute-done.6.refs_6_), channel_id=1, source_target_pairs={{0,1},{1,2},{2,3},{3,4},{4,5},{5,6},{6,7},{7,0},{8,9},{9,10},{10,1... | collective-permute-start | bytes 1376264 | tf_op jit(solution)/shard_map/ppermute | solution.py:240
  88.3 10.3 %collective-permute-done.8.refs_7_ = bf16[896,256]{1,0:T(8,128)(2,1)S(1)} collective-permute-done((bf16[896,256]{1,0:T(8,128)(2,1)S(1)}, bf16[896,256]{1,0:T(8,128)(2,1)S(1)}, u32[]{:S(2)}, u32[]{:S(2)}) %collective-permute-start.8) | collective-permute-done | bytes 458784 | tf_op jit(solution)/shard_map/ppermute | solution.py:240
  98.6 0.0 copy-start.2
  98.6 0.8 copy-done.2
  99.3 0.9 all-to-all-done.2.refs_8_
  100.2 6.4 %collective-permute-start.9 = (bf16[32,64,128]{2,1,0:T(8,128)(2,1)S(1)}, bf16[32,64,128]{2,1,0:T(8,128)(2,1)S(1)}, u32[]{:S(2)}, u32[]{:S(2)}) collective-permute-start(bf16[32,64,128]{2,1,0:T(8,128)(2,1)S(1)} %all-to-all-done.2.refs_8_), channel_id=1, source_target_pairs={{0,8},{8,0},{1,9},{9,1},{2,10},{10,2},{3,11},{11,3},{4,12},{12,4},... | collective-permute-start | bytes 1572872 | tf_op jit(solution)/shard_map/ppermute | solution.py:243
  106.6 1.5 %collective-permute-done.9.refs_9_ = bf16[32,64,128]{2,1,0:T(8,128)(2,1)S(1)} collective-permute-done((bf16[32,64,128]{2,1,0:T(8,128)(2,1)S(1)}, bf16[32,64,128]{2,1,0:T(8,128)(2,1)S(1)}, u32[]{:S(2)}, u32[]{:S(2)}) %collective-permute-start.9) | collective-permute-done | bytes 524320 | tf_op jit(solution)/shard_map/ppermute | solution.py:243
  108.1 0.0 copy-done.1
  108.1 0.0 copy-start.3
  108.2 1.0 copy-done.3
  109.2 3.2 %gamma_rows.1 = bf16[896,256]{1,0:T(8,128)(2,1)} custom-call(bf16[896,256]{1,0:T(8,128)(2,1)S(1)} %copy-done.1, bf16[896,256]{1,0:T(8,128)(2,1)S(1)} %collective-permute-done.refs_2_.refs_1_, bf16[896,256]{1,0:T(8,128)(2,1)S(1)} %collective-permute-done.1.refs_0_.refs_1_.refs_2_, bf16[896,256]{1,0:T(8,128)(2,1)S(1)} %collective-permute-done.2.refs_0_.refs_3_, ...), custom_call_target="tpu_custom_call" | custom-call | tf_op jit(solution)/shard_map/gamma_rows/pallas_call | solution.py:203
Async XLA Ops:
  0.0 8.0 %copy-start.7 = (s32[16]{0:T(128)S(1)}, s32[16]{0:T(128)}, u32[]{:S(2)}) copy-start(s32[16]{0:T(128)} %virtual_of.1) | copy-start | bytes 196
  0.0 8.0 %copy-start.6 = (s32[16]{0:T(128)S(1)}, s32[16]{0:T(128)}, u32[]{:S(2)}) copy-start(s32[16]{0:T(128)} %occupied_of.1) | copy-start | bytes 196
  0.0 8.0 %copy-start.5 = (f32[64]{0:T(128)S(1)}, f32[64]{0:T(128)}, u32[]{:S(2)}) copy-start(f32[64]{0:T(128)} %occupied.1) | copy-start | bytes 772
  0.0 12.1 %collective-permute-start.1 = (bf16[896,256]{1,0:T(8,128)(2,1)}, bf16[896,256]{1,0:T(8,128)(2,1)S(1)}, u32[]{:S(2)}, u32[]{:S(2)}) collective-permute-start(bf16[896,256]{1,0:T(8,128)(2,1)} %refs_0_.1), channel_id=1, source_target_pairs={{0,1},{1,2},{2,3},{3,4},{4,5},{5,6},{6,7},{7,0},{8,9},{9,10},{10,1... | collective-permute-start | bytes 1376264 | tf_op jit(solution)/shard_map/ppermute | solution.py:219
  4.2 12.9 %collective-permute-start = (bf16[896,256]{1,0:T(8,128)(2,1)}, bf16[896,256]{1,0:T(8,128)(2,1)S(1)}, u32[]{:S(2)}, u32[]{:S(2)}) collective-permute-start(bf16[896,256]{1,0:T(8,128)(2,1)} %refs_0_.1), channel_id=1, source_target_pairs={{0,7},{1,0},{2,1},{3,2},{4,3},{5,4},{6,5},{7,6},{8,15},{9,8},{10,9... | collective-permute-start | bytes 1376264 | tf_op jit(solution)/shard_map/ppermute | solution.py:220
  8.0 0.9 copy-start.4
  8.9 0.7 copy-start.8
  12.1 17.3 %collective-permute-start.2 = (bf16[896,256]{1,0:T(8,128)(2,1)S(1)}, bf16[896,256]{1,0:T(8,128)(2,1)S(1)}, u32[]{:S(2)}, u32[]{:S(2)}) collective-permute-start(bf16[896,256]{1,0:T(8,128)(2,1)S(1)} %collective-permute-done.1.refs_0_.refs_1_.refs_2_), channel_id=1, source_target_pairs={{0,1},{1,2},{2,3},{3,4},{4,5},{5,6},{6,7},{7,0},{8,9},{9,10},{10,1... | collective-permute-start | bytes 1376264 | tf_op jit(solution)/shard_map/ppermute | solution.py:223
  17.1 12.3 %collective-permute-start.3 = (bf16[896,256]{1,0:T(8,128)(2,1)S(1)}, bf16[896,256]{1,0:T(8,128)(2,1)S(1)}, u32[]{:S(2)}, u32[]{:S(2)}) collective-permute-start(bf16[896,256]{1,0:T(8,128)(2,1)S(1)} %collective-permute-done.refs_2_.refs_1_), channel_id=1, source_target_pairs={{0,7},{1,0},{2,1},{3,2},{4,3},{5,4},{6,5},{7,6},{8,15},{9,8},{10,9... | collective-permute-start | bytes 1376264 | tf_op jit(solution)/shard_map/ppermute | solution.py:224
  21.5 1.0 copy-start
  23.1 11.9 %collective-permute-start.4 = (bf16[3,2,128,128]{3,2,1,0:T(8,128)(2,1)S(1)}, bf16[3,2,128,128]{3,2,1,0:T(8,128)(2,1)S(1)}, u32[]{:S(2)}, u32[]{:S(2)}) collective-permute-start(bf16[3,2,128,128]{3,2,1,0:T(8,128)(2,1)S(1)} %get-tuple-element.27), channel_id=1, source_target_pairs={{0,8},{8,0},{1,9},{9,1},{2,10},{10,2},{3,11},{11,3},{4,12},{12,4},... | collective-permute-start | bytes 589832 | tf_op jit(solution)/shard_map/ppermute | solution.py:227
  29.9 6.0 %collective-permute-start.5 = (bf16[2,2,128,128]{3,2,1,0:T(8,128)(2,1)S(1)}, bf16[2,2,128,128]{3,2,1,0:T(8,128)(2,1)S(1)}, u32[]{:S(2)}, u32[]{:S(2)}) collective-permute-start(bf16[2,2,128,128]{3,2,1,0:T(8,128)(2,1)S(1)} %get-tuple-element.28), channel_id=1, source_target_pairs={{0,8},{8,0},{1,9},{9,1},{2,10},{10,2},{3,11},{11,3},{4,12},{12,4},... | collective-permute-start | bytes 393224 | tf_op jit(solution)/shard_map/ppermute | solution.py:229
  36.8 24.8 %all-to-all-start = ((bf16[8,160,128]{2,1,0:T(8,128)(2,1)}), bf16[8,160,128]{2,1,0:T(8,128)(2,1)S(1)}, u32[]{:S(2)}, u32[]{:S(2)}) async-start(bf16[8,160,128]{2,1,0:T(8,128)(2,1)} %sum_cores.1), calls=%async_computation | async-start | bytes 655360 | tf_op jit(solution)/shard_map/all_to_all | solution.py:235
  47.9 33.6 %collective-permute-start.6 = (bf16[896,256]{1,0:T(8,128)(2,1)S(1)}, bf16[896,256]{1,0:T(8,128)(2,1)S(1)}, u32[]{:S(2)}, u32[]{:S(2)}) collective-permute-start(bf16[896,256]{1,0:T(8,128)(2,1)S(1)} %collective-permute-done.2.refs_0_.refs_3_), channel_id=1, source_target_pairs={{0,1},{1,2},{2,3},{3,4},{4,5},{5,6},{6,7},{7,0},{8,9},{9,10},{10,1... | collective-permute-start | bytes 1376264 | tf_op jit(solution)/shard_map/ppermute | solution.py:233
  50.8 30.7 %collective-permute-start.7 = (bf16[896,256]{1,0:T(8,128)(2,1)S(1)}, bf16[896,256]{1,0:T(8,128)(2,1)}, u32[]{:S(2)}, u32[]{:S(2)}) collective-permute-start(bf16[896,256]{1,0:T(8,128)(2,1)S(1)} %collective-permute-done.3.refs_2_.refs_4_), channel_id=1, source_target_pairs={{0,7},{1,0},{2,1},{3,2},{4,3},{5,4},{6,5},{7,6},{8,15},{9,8},{10,9... | collective-permute-start | bytes 1376264 | tf_op jit(solution)/shard_map/ppermute | solution.py:234
  81.5 26.7 %copy-start.1 = (bf16[896,256]{1,0:T(8,128)(2,1)S(1)}, bf16[896,256]{1,0:T(8,128)(2,1)}, u32[]{:S(2)}) copy-start(bf16[896,256]{1,0:T(8,128)(2,1)} %refs_0_.1) | copy-start | bytes 1376260
  81.5 18.7 %all-to-all-start.2 = ((bf16[32,64,128]{2,1,0:T(8,128)(2,1)}), bf16[32,64,128]{2,1,0:T(8,128)(2,1)S(1)}, u32[]{:S(2)}, u32[]{:S(2)}) async-start(bf16[32,64,128]{2,1,0:T(8,128)(2,1)} %amplitude_copies.1), calls=%async_computation.2 | async-start | bytes 1048576 | tf_op jit(solution)/shard_map/all_to_all | solution.py:241
  85.5 13.0 %collective-permute-start.8 = (bf16[896,256]{1,0:T(8,128)(2,1)S(1)}, bf16[896,256]{1,0:T(8,128)(2,1)S(1)}, u32[]{:S(2)}, u32[]{:S(2)}) collective-permute-start(bf16[896,256]{1,0:T(8,128)(2,1)S(1)} %collective-permute-done.6.refs_6_), channel_id=1, source_target_pairs={{0,1},{1,2},{2,3},{3,4},{4,5},{5,6},{6,7},{7,0},{8,9},{9,10},{10,1... | collective-permute-start | bytes 1376264 | tf_op jit(solution)/shard_map/ppermute | solution.py:240
  98.6 0.8 copy-start.2
  100.2 7.9 %collective-permute-start.9 = (bf16[32,64,128]{2,1,0:T(8,128)(2,1)S(1)}, bf16[32,64,128]{2,1,0:T(8,128)(2,1)S(1)}, u32[]{:S(2)}, u32[]{:S(2)}) collective-permute-start(bf16[32,64,128]{2,1,0:T(8,128)(2,1)S(1)} %all-to-all-done.2.refs_8_), channel_id=1, source_target_pairs={{0,8},{8,0},{1,9},{9,1},{2,10},{10,2},{3,11},{11,3},{4,12},{12,4},... | collective-permute-start | bytes 1572872 | tf_op jit(solution)/shard_map/ppermute | solution.py:243
  108.1 1.0 copy-start.3

commit v8 on v7

--- a/solution.py
+++ b/solution.py
@@ -166,14 +166,13 @@
     )(parts, denominator)
 
 
-def gamma_rows(blocks, last, mine, theirs, scales):
+def gamma_rows(blocks, mine, theirs, scales):
     rows, width = blocks[0].shape
-    names = [q for q, _ in ORDER[:-1]]
+    names = [q for q, _ in ORDER]
 
     def kernel(*refs):
-        block = dict(zip(names, refs))
-        n = len(names)
-        own, other, scale, out, matrix = refs[n + len(last) :]
+        block = refs[: len(names)]
+        own, other, scale, out, matrix = refs[len(names) :]
         core = lax.axis_index("core")
         for pair in range(0, len(ORDER), 2):
             for part, source in ((core, own), (1 - core, other)):
@@ -190,25 +189,22 @@
                             tile = tiles[h] * scale[pl.ds(2 * i + part, 1)]
                             matrix[i, place, h * TS : (h + 1) * TS] = tile.astype(bf16)
 
-        height = rows // len(last)
         for start in range(0, rows, ROWS):
-            part, offset = divmod(start, height)
-            total = jnp.dot(
-                refs[n + part][offset : offset + ROWS], matrix[n], preferred_element_type=f32
-            )
-            for i, q in enumerate(names):
-                total += jnp.dot(block[q][start : start + ROWS], matrix[i], preferred_element_type=f32)
+            total = None
+            for i, ref in enumerate(block):
+                term = jnp.dot(ref[start : start + ROWS], matrix[i], preferred_element_type=f32)
+                total = term if total is None else total + term
             out[start : start + ROWS] = total.astype(bf16)
 
     return pl.pallas_call(
         kernel,
         out_shape=jax.ShapeDtypeStruct((rows, width), bf16),
-        in_specs=[in_vmem] * (len(names) + len(last) + 3),
+        in_specs=[in_vmem] * (len(names) + 3),
         out_specs=in_vmem,
         scratch_shapes=[pltpu.VMEM((len(ORDER), WIDTH, WIDTH), bf16)],
         compiler_params=pltpu.CompilerParams(vmem_limit_bytes=VMEM_LIMIT),
         name="gamma_rows",
-    )(*[blocks[q] for q in names], *last, mine, theirs, scales)
+    )(*[blocks[q] for q in names], mine, theirs, scales)
 
 
 def body(three_index, *energies):
@@ -232,16 +228,16 @@
     summed, block[-2], block[2] = lax.optimization_barrier((summed, block[-2], block[2]))
     block[-3] = lax.ppermute(block[-2], "pair", up)
     block[3] = lax.ppermute(block[2], "pair", down)
+    block[-4] = lax.ppermute(block[-2], "pair", ring(NPAIR, 2))
     parts = lax.all_to_all(summed, "z", 0, 0)
     parts = lax.all_to_all(sum_z(parts), ("pair", "x"), 0, 0)
     copies = amplitude_copies(parts, denominator)
-
-    copies, block[-3], block[3] = lax.optimization_barrier((copies, block[-3], block[3]))
-    last = (lax.ppermute(block[-3], "pair", up),)
+    copies, block[-3], block[3], block[-4] = lax.optimization_barrier(
+        (copies, block[-3], block[3], block[-4])
+    )
     mine = lax.all_to_all(copies, ("z", "x"), 0, 0)
-    mine, last = lax.optimization_barrier((mine, last))
     theirs = lax.ppermute(mine, "core", swap)
-    return gamma_rows(block, last, mine, theirs, scales)
+    return gamma_rows(block, mine, theirs, scales)
 
 
 def solution(mesh):

time: 113 us -> 127 us (1.12)
  blocking collectives: 19 us -> 55.5 us
  waiting for transfers between devices: 21.9 us -> 5.6 us
  starting transfers between devices: 60.2 us -> 56.9 us
  Pallas kernels: 6.75 us -> 4.94 us
    all_to_all x0 -> x1, blocking collectives: none -> 23.1 us  [body(): mine = lax.all_to_all(copies, ('z', 'x'), 0, 0)]
    all_to_all x1, blocking collectives: 19 us -> 32.4 us  [body(): parts = lax.all_to_all(sum_z(parts), ('pair', 'x'), 0, 0)]
    ppermute x1, waiting for transfers between devices: 10.3 us -> 0.01 us  [body(): block[-4] = lax.ppermute(block[-2], 'pair', ring(NPAIR, 2))]
    all_to_all x1, waiting for transfers between devices: 6.39 us -> 1.87 us  [body(): parts = lax.all_to_all(summed, 'z', 0, 0)]
    all_to_all x1 -> x0, starting transfers between devices: 4.03 us -> none  [body(): mine = lax.all_to_all(copies, ('z', 'x'), 0, 0)]
    ppermute x1, starting transfers between devices: 2.85 us -> 4.51 us  [body(): block[-3] = lax.ppermute(block[-2], 'pair', up)]
  transfers between devices with their start and end apart: 12 -> 11, of which waited for: 6 -> 4; matrix products, arithmetic and copies ran while one was open for 0% -> 0% of each run, Pallas kernels for 2% -> 2%
where the time goes in v8:
time: 127 us; the launch traced here: 126 us
  starting transfers between devices  56.9 us (45%)
  blocking collectives  55.5 us (44%)
  waiting for transfers between devices  5.6 us (4%)
  Pallas kernels  4.94 us (4%)
  local copies, waits for them, and re-layouts  3.16 us (2%)
    all_to_all x1, blocking collectives, body(): parts = lax.all_to_all(sum_z(parts), ('pair', 'x'), 0, 0)  32.4 us
    all_to_all x1, blocking collectives, body(): mine = lax.all_to_all(copies, ('z', 'x'), 0, 0)  23.1 us
    all_to_all x1, starting transfers between devices, body(): parts = lax.all_to_all(summed, 'z', 0, 0)  11.2 us
    ppermute x1, starting transfers between devices, body(): got_early = lax.ppermute(other_early, 'core', swap)  6.28 us
    ppermute x1, starting transfers between devices, body(): theirs = lax.ppermute(mine, 'core', swap)  5.36 us
    ppermute x1, starting transfers between devices, body(): block[3] = lax.ppermute(block[2], 'pair', down)  5.31 us
    ppermute x1, starting transfers between devices, body(): got_late = lax.ppermute(other_late, 'core', swap)  5.07 us
    ppermute x1, starting transfers between devices, body(): block[-2] = lax.ppermute(block[-1], 'pair', up)  4.98 us
  transfers between devices with their start and end apart: 11, of which 4 were waited for; matrix products, arithmetic and copies ran while one was open for 0% of the time, Pallas kernels for 2%

profile of v8, /device:TPU:1, one launch (start us, length us, event | category | flops | bytes accessed | tf_op | source)
XLA Modules:
  0.0 126.4 jit_solution(8204746788519290012)
XLA Ops:
  0.0 0.0 copy-start.7
  0.0 0.0 copy-start.6
  0.0 0.0 copy-start.5
  0.0 4.2 %collective-permute-start.1 = (bf16[896,256]{1,0:T(8,128)(2,1)}, bf16[896,256]{1,0:T(8,128)(2,1)S(1)}, u32[]{:S(2)}, u32[]{:S(2)}) collective-permute-start(bf16[896,256]{1,0:T(8,128)(2,1)} %refs_0_.1), channel_id=1, source_target_pairs={{0,1},{1,2},{2,3},{3,4},{4,5},{5,6},{6,7},{7,0},{8,9},{9,10},{10,1... | collective-permute-start | bytes 1376264 | tf_op jit(solution)/shard_map/ppermute | solution.py:215
  4.2 3.8 %collective-permute-start = (bf16[896,256]{1,0:T(8,128)(2,1)}, bf16[896,256]{1,0:T(8,128)(2,1)S(1)}, u32[]{:S(2)}, u32[]{:S(2)}) collective-permute-start(bf16[896,256]{1,0:T(8,128)(2,1)} %refs_0_.1), channel_id=1, source_target_pairs={{0,7},{1,0},{2,1},{3,2},{4,3},{5,4},{6,5},{7,6},{8,15},{9,8},{10,9... | collective-permute-start | bytes 1376264 | tf_op jit(solution)/shard_map/ppermute | solution.py:216
  8.0 0.0 copy-done.7
  8.0 0.0 copy-done.6
  8.0 0.0 copy-done.5
  8.0 0.0 copy-start.2
  8.0 0.9 copy-done.2
  8.9 0.0 copy-start.8
  8.9 0.7 copy-done.8
  9.6 0.7 tables.1
  10.3 0.0 copy-start.3
  10.3 0.6 copy-done.3
  10.9 1.2 collective-permute-done.1.refs_0_.refs_1_.refs_2_
  12.1 5.0 %collective-permute-start.2 = (bf16[896,256]{1,0:T(8,128)(2,1)S(1)}, bf16[896,256]{1,0:T(8,128)(2,1)S(1)}, u32[]{:S(2)}, u32[]{:S(2)}) collective-permute-start(bf16[896,256]{1,0:T(8,128)(2,1)S(1)} %collective-permute-done.1.refs_0_.refs_1_.refs_2_), channel_id=1, source_target_pairs={{0,1},{1,2},{2,3},{3,4},{4,5},{5,6},{6,7},{7,0},{8,9},{9,10},{10,1... | collective-permute-start | bytes 1376264 | tf_op jit(solution)/shard_map/ppermute | solution.py:219
  17.1 0.0 collective-permute-done.refs_2_.refs_1_
  17.1 4.3 %collective-permute-start.3 = (bf16[896,256]{1,0:T(8,128)(2,1)S(1)}, bf16[896,256]{1,0:T(8,128)(2,1)S(1)}, u32[]{:S(2)}, u32[]{:S(2)}) collective-permute-start(bf16[896,256]{1,0:T(8,128)(2,1)S(1)} %collective-permute-done.refs_2_.refs_1_), channel_id=1, source_target_pairs={{0,7},{1,0},{2,1},{3,2},{4,3},{5,4},{6,5},{7,6},{8,15},{9,8},{10,9... | collective-permute-start | bytes 1376264 | tf_op jit(solution)/shard_map/ppermute | solution.py:220
  21.5 0.0 copy-start
  21.5 1.0 copy-done
  22.5 0.6 coulomb_pairs.2
  23.1 6.3 %collective-permute-start.4 = (bf16[3,2,128,128]{3,2,1,0:T(8,128)(2,1)S(1)}, bf16[3,2,128,128]{3,2,1,0:T(8,128)(2,1)S(1)}, u32[]{:S(2)}, u32[]{:S(2)}) collective-permute-start(bf16[3,2,128,128]{3,2,1,0:T(8,128)(2,1)S(1)} %get-tuple-element.26), channel_id=1, source_target_pairs={{0,8},{8,0},{1,9},{9,1},{2,10},{10,2},{3,11},{11,3},{4,12},{12,4},... | collective-permute-start | bytes 589832 | tf_op jit(solution)/shard_map/ppermute | solution.py:223
  29.4 0.0 collective-permute-done.2.refs_0_.refs_3_
  29.4 0.0 collective-permute-done.3.refs_2_.refs_4_
  29.5 0.5 coulomb_pairs.3
  29.9 5.1 %collective-permute-start.5 = (bf16[2,2,128,128]{3,2,1,0:T(8,128)(2,1)S(1)}, bf16[2,2,128,128]{3,2,1,0:T(8,128)(2,1)S(1)}, u32[]{:S(2)}, u32[]{:S(2)}) collective-permute-start(bf16[2,2,128,128]{3,2,1,0:T(8,128)(2,1)S(1)} %get-tuple-element.27), channel_id=1, source_target_pairs={{0,8},{8,0},{1,9},{9,1},{2,10},{10,2},{3,11},{11,3},{4,12},{12,4},... | collective-permute-start | bytes 393224 | tf_op jit(solution)/shard_map/ppermute | solution.py:225
  35.0 0.0 collective-permute-done.4.refs_2_
  35.0 1.0 collective-permute-done.5.refs_3_
  36.0 0.8 sum_cores.1
  36.8 11.2 %all-to-all-start = ((bf16[8,160,128]{2,1,0:T(8,128)(2,1)}), bf16[8,160,128]{2,1,0:T(8,128)(2,1)S(1)}, u32[]{:S(2)}, u32[]{:S(2)}) async-start(bf16[8,160,128]{2,1,0:T(8,128)(2,1)} %sum_cores.1), calls=%async_computation | async-start | bytes 655360 | tf_op jit(solution)/shard_map/all_to_all | solution.py:232
  47.9 5.3 %collective-permute-start.7 = (bf16[896,256]{1,0:T(8,128)(2,1)S(1)}, bf16[896,256]{1,0:T(8,128)(2,1)S(1)}, u32[]{:S(2)}, u32[]{:S(2)}) collective-permute-start(bf16[896,256]{1,0:T(8,128)(2,1)S(1)} %collective-permute-done.3.refs_2_.refs_4_), channel_id=1, source_target_pairs={{0,7},{1,0},{2,1},{3,2},{4,3},{5,4},{6,5},{7,6},{8,15},{9,8},{10,9... | collective-permute-start | bytes 1376264 | tf_op jit(solution)/shard_map/ppermute | solution.py:230
  53.2 1.9 %collective-permute-start.8 = (bf16[896,256]{1,0:T(8,128)(2,1)S(1)}, bf16[896,256]{1,0:T(8,128)(2,1)S(1)}, u32[]{:S(2)}, u32[]{:S(2)}) collective-permute-start(bf16[896,256]{1,0:T(8,128)(2,1)S(1)} %collective-permute-done.2.refs_0_.refs_3_), channel_id=1, source_target_pairs={{0,2},{1,3},{2,4},{3,5},{4,6},{5,7},{6,0},{7,1},{8,10},{9,11},{10,... | collective-permute-start | bytes 1376264 | tf_op jit(solution)/shard_map/ppermute | solution.py:231
  55.2 4.5 %collective-permute-start.6 = (bf16[896,256]{1,0:T(8,128)(2,1)S(1)}, bf16[896,256]{1,0:T(8,128)(2,1)S(1)}, u32[]{:S(2)}, u32[]{:S(2)}) collective-permute-start(bf16[896,256]{1,0:T(8,128)(2,1)S(1)} %collective-permute-done.2.refs_0_.refs_3_), channel_id=1, source_target_pairs={{0,1},{1,2},{2,3},{3,4},{4,5},{5,6},{6,7},{7,0},{8,9},{9,10},{10,1... | collective-permute-start | bytes 1376264 | tf_op jit(solution)/shard_map/ppermute | solution.py:229
  59.7 1.9 %all-to-all-done.parts_ref = bf16[8,160,128]{2,1,0:T(8,128)(2,1)S(1)} async-done(((bf16[8,160,128]{2,1,0:T(8,128)(2,1)}), bf16[8,160,128]{2,1,0:T(8,128)(2,1)S(1)}, u32[]{:S(2)}, u32[]{:S(2)}) %all-to-all-start) | async-done | bytes 327712 | tf_op jit(solution)/shard_map/all_to_all | solution.py:232
  61.5 0.1 sum_z.1
  61.6 0.0 copy-start.4
  61.6 32.4 %all_to_all.15.parts_ref = bf16[32,16,128]{2,1,0:T(8,128)(2,1)S(1)} all-to-all(bf16[32,16,128]{2,1,0:T(8,128)(2,1)S(1)} %sum_z.1), channel_id=1, replica_groups=mesh['x'=4,'z'=8,'core'=2,'pair'=8] {'pair','x'}, dimensions={0} | all-to-all | bytes 262144 | tf_op jit(solution)/shard_map/all_to_all | solution.py:233
  94.1 0.0 copy-done.4
  94.1 0.1 amplitude_copies.1
  94.1 0.0 copy-start.1
  94.2 0.0 collective-permute-done.7.refs_5_
  94.2 0.0 collective-permute-done.8.refs_7_
  94.2 0.0 collective-permute-done.6.refs_6_
  94.2 23.1 %all_to_all.16.refs_8_ = bf16[32,64,128]{2,1,0:T(8,128)(2,1)S(1)} all-to-all(bf16[32,64,128]{2,1,0:T(8,128)(2,1)S(1)} %amplitude_copies.1), channel_id=1, replica_groups=mesh['x'=4,'z'=8,'core'=2,'pair'=8] {'z','x'}, dimensions={0} | all-to-all | bytes 1048576 | tf_op jit(solution)/shard_map/all_to_all | solution.py:238
  117.3 5.4 %collective-permute-start.9 = (bf16[32,64,128]{2,1,0:T(8,128)(2,1)S(1)}, bf16[32,64,128]{2,1,0:T(8,128)(2,1)S(1)}, u32[]{:S(2)}, u32[]{:S(2)}) collective-permute-start(bf16[32,64,128]{2,1,0:T(8,128)(2,1)S(1)} %all_to_all.16.refs_8_), channel_id=1, source_target_pairs={{0,8},{8,0},{1,9},{9,1},{2,10},{10,2},{3,11},{11,3},{4,12},{12,4},... | collective-permute-start | bytes 1572872 | tf_op jit(solution)/shard_map/ppermute | solution.py:239
  122.6 1.5 %collective-permute-done.9.refs_9_ = bf16[32,64,128]{2,1,0:T(8,128)(2,1)S(1)} collective-permute-done((bf16[32,64,128]{2,1,0:T(8,128)(2,1)S(1)}, bf16[32,64,128]{2,1,0:T(8,128)(2,1)S(1)}, u32[]{:S(2)}, u32[]{:S(2)}) %collective-permute-start.9) | collective-permute-done | bytes 524320 | tf_op jit(solution)/shard_map/ppermute | solution.py:239
  124.2 0.0 copy-done.1
  124.2 2.2 %gamma_rows.1 = bf16[896,256]{1,0:T(8,128)(2,1)} custom-call(bf16[896,256]{1,0:T(8,128)(2,1)S(1)} %copy-done.1, bf16[896,256]{1,0:T(8,128)(2,1)S(1)} %collective-permute-done.refs_2_.refs_1_, bf16[896,256]{1,0:T(8,128)(2,1)S(1)} %collective-permute-done.1.refs_0_.refs_1_.refs_2_, bf16[896,256]{1,0:T(8,128)(2,1)S(1)} %collective-permute-done.2.refs_0_.refs_3_, ...), custom_call_target="tpu_custom_call" | custom-call | tf_op jit(solution)/shard_map/gamma_rows/pallas_call | solution.py:199
Async XLA Ops:
  0.0 8.0 %copy-start.7 = (s32[16]{0:T(128)S(1)}, s32[16]{0:T(128)}, u32[]{:S(2)}) copy-start(s32[16]{0:T(128)} %virtual_of.1) | copy-start | bytes 196
  0.0 8.0 %copy-start.6 = (s32[16]{0:T(128)S(1)}, s32[16]{0:T(128)}, u32[]{:S(2)}) copy-start(s32[16]{0:T(128)} %occupied_of.1) | copy-start | bytes 196
  0.0 8.0 %copy-start.5 = (f32[64]{0:T(128)S(1)}, f32[64]{0:T(128)}, u32[]{:S(2)}) copy-start(f32[64]{0:T(128)} %occupied.1) | copy-start | bytes 772
  0.0 12.1 %collective-permute-start.1 = (bf16[896,256]{1,0:T(8,128)(2,1)}, bf16[896,256]{1,0:T(8,128)(2,1)S(1)}, u32[]{:S(2)}, u32[]{:S(2)}) collective-permute-start(bf16[896,256]{1,0:T(8,128)(2,1)} %refs_0_.1), channel_id=1, source_target_pairs={{0,1},{1,2},{2,3},{3,4},{4,5},{5,6},{6,7},{7,0},{8,9},{9,10},{10,1... | collective-permute-start | bytes 1376264 | tf_op jit(solution)/shard_map/ppermute | solution.py:215
  4.2 12.9 %collective-permute-start = (bf16[896,256]{1,0:T(8,128)(2,1)}, bf16[896,256]{1,0:T(8,128)(2,1)S(1)}, u32[]{:S(2)}, u32[]{:S(2)}) collective-permute-start(bf16[896,256]{1,0:T(8,128)(2,1)} %refs_0_.1), channel_id=1, source_target_pairs={{0,7},{1,0},{2,1},{3,2},{4,3},{5,4},{6,5},{7,6},{8,15},{9,8},{10,9... | collective-permute-start | bytes 1376264 | tf_op jit(solution)/shard_map/ppermute | solution.py:216
  8.0 0.9 copy-start.2
  8.9 0.7 copy-start.8
  10.3 0.6 copy-start.3
  12.1 17.3 %collective-permute-start.2 = (bf16[896,256]{1,0:T(8,128)(2,1)S(1)}, bf16[896,256]{1,0:T(8,128)(2,1)S(1)}, u32[]{:S(2)}, u32[]{:S(2)}) collective-permute-start(bf16[896,256]{1,0:T(8,128)(2,1)S(1)} %collective-permute-done.1.refs_0_.refs_1_.refs_2_), channel_id=1, source_target_pairs={{0,1},{1,2},{2,3},{3,4},{4,5},{5,6},{6,7},{7,0},{8,9},{9,10},{10,1... | collective-permute-start | bytes 1376264 | tf_op jit(solution)/shard_map/ppermute | solution.py:219
  17.1 12.3 %collective-permute-start.3 = (bf16[896,256]{1,0:T(8,128)(2,1)S(1)}, bf16[896,256]{1,0:T(8,128)(2,1)S(1)}, u32[]{:S(2)}, u32[]{:S(2)}) collective-permute-start(bf16[896,256]{1,0:T(8,128)(2,1)S(1)} %collective-permute-done.refs_2_.refs_1_), channel_id=1, source_target_pairs={{0,7},{1,0},{2,1},{3,2},{4,3},{5,4},{6,5},{7,6},{8,15},{9,8},{10,9... | collective-permute-start | bytes 1376264 | tf_op jit(solution)/shard_map/ppermute | solution.py:220
  21.5 1.0 copy-start
  23.1 11.9 %collective-permute-start.4 = (bf16[3,2,128,128]{3,2,1,0:T(8,128)(2,1)S(1)}, bf16[3,2,128,128]{3,2,1,0:T(8,128)(2,1)S(1)}, u32[]{:S(2)}, u32[]{:S(2)}) collective-permute-start(bf16[3,2,128,128]{3,2,1,0:T(8,128)(2,1)S(1)} %get-tuple-element.26), channel_id=1, source_target_pairs={{0,8},{8,0},{1,9},{9,1},{2,10},{10,2},{3,11},{11,3},{4,12},{12,4},... | collective-permute-start | bytes 589832 | tf_op jit(solution)/shard_map/ppermute | solution.py:223
  29.9 6.0 %collective-permute-start.5 = (bf16[2,2,128,128]{3,2,1,0:T(8,128)(2,1)S(1)}, bf16[2,2,128,128]{3,2,1,0:T(8,128)(2,1)S(1)}, u32[]{:S(2)}, u32[]{:S(2)}) collective-permute-start(bf16[2,2,128,128]{3,2,1,0:T(8,128)(2,1)S(1)} %get-tuple-element.27), channel_id=1, source_target_pairs={{0,8},{8,0},{1,9},{9,1},{2,10},{10,2},{3,11},{11,3},{4,12},{12,4},... | collective-permute-start | bytes 393224 | tf_op jit(solution)/shard_map/ppermute | solution.py:225
  36.8 24.8 %all-to-all-start = ((bf16[8,160,128]{2,1,0:T(8,128)(2,1)}), bf16[8,160,128]{2,1,0:T(8,128)(2,1)S(1)}, u32[]{:S(2)}, u32[]{:S(2)}) async-start(bf16[8,160,128]{2,1,0:T(8,128)(2,1)} %sum_cores.1), calls=%async_computation | async-start | bytes 655360 | tf_op jit(solution)/shard_map/all_to_all | solution.py:232
  47.9 46.2 %collective-permute-start.7 = (bf16[896,256]{1,0:T(8,128)(2,1)S(1)}, bf16[896,256]{1,0:T(8,128)(2,1)S(1)}, u32[]{:S(2)}, u32[]{:S(2)}) collective-permute-start(bf16[896,256]{1,0:T(8,128)(2,1)S(1)} %collective-permute-done.3.refs_2_.refs_4_), channel_id=1, source_target_pairs={{0,7},{1,0},{2,1},{3,2},{4,3},{5,4},{6,5},{7,6},{8,15},{9,8},{10,9... | collective-permute-start | bytes 1376264 | tf_op jit(solution)/shard_map/ppermute | solution.py:230
  53.2 40.9 %collective-permute-start.8 = (bf16[896,256]{1,0:T(8,128)(2,1)S(1)}, bf16[896,256]{1,0:T(8,128)(2,1)S(1)}, u32[]{:S(2)}, u32[]{:S(2)}) collective-permute-start(bf16[896,256]{1,0:T(8,128)(2,1)S(1)} %collective-permute-done.2.refs_0_.refs_3_), channel_id=1, source_target_pairs={{0,2},{1,3},{2,4},{3,5},{4,6},{5,7},{6,0},{7,1},{8,10},{9,11},{10,... | collective-permute-start | bytes 1376264 | tf_op jit(solution)/shard_map/ppermute | solution.py:231
  55.2 39.0 %collective-permute-start.6 = (bf16[896,256]{1,0:T(8,128)(2,1)S(1)}, bf16[896,256]{1,0:T(8,128)(2,1)S(1)}, u32[]{:S(2)}, u32[]{:S(2)}) collective-permute-start(bf16[896,256]{1,0:T(8,128)(2,1)S(1)} %collective-permute-done.2.refs_0_.refs_3_), channel_id=1, source_target_pairs={{0,1},{1,2},{2,3},{3,4},{4,5},{5,6},{6,7},{7,0},{8,9},{9,10},{10,1... | collective-permute-start | bytes 1376264 | tf_op jit(solution)/shard_map/ppermute | solution.py:229
  61.6 32.5 %copy-start.4 = (f32[64,128]{1,0:T(8,128)S(1)}, f32[64,128]{1,0:T(8,128)}, u32[]{:S(2)}) copy-start(f32[64,128]{1,0:T(8,128)} %copy-done.3) | copy-start | bytes 98308
  94.1 30.0 %copy-start.1 = (bf16[896,256]{1,0:T(8,128)(2,1)S(1)}, bf16[896,256]{1,0:T(8,128)(2,1)}, u32[]{:S(2)}) copy-start(bf16[896,256]{1,0:T(8,128)(2,1)} %refs_0_.1) | copy-start | bytes 1376260
  117.3 6.9 %collective-permute-start.9 = (bf16[32,64,128]{2,1,0:T(8,128)(2,1)S(1)}, bf16[32,64,128]{2,1,0:T(8,128)(2,1)S(1)}, u32[]{:S(2)}, u32[]{:S(2)}) collective-permute-start(bf16[32,64,128]{2,1,0:T(8,128)(2,1)S(1)} %all_to_all.16.refs_8_), channel_id=1, source_target_pairs={{0,8},{8,0},{1,9},{9,1},{2,10},{10,2},{3,11},{11,3},{4,12},{12,4},... | collective-permute-start | bytes 1572872 | tf_op jit(solution)/shard_map/ppermute | solution.py:239

commit v9 on v8

--- a/solution.py
+++ b/solution.py
@@ -26,8 +26,18 @@
 in_smem = pl.BlockSpec(memory_space=pltpu.SMEM)
 
 
-def ring(size, step):
-    return [(i, (i + step) % size) for i in range(size)]
+SWAP_A = [(i, i ^ 1) for i in range(NPAIR)]
+SWAP_B = [(i, (i + (-1 if i % 2 == 0 else 1)) % NPAIR) for i in range(NPAIR)]
+SWAP_CORES = [(0, 1), (1, 0)]
+HELD = (0, ("A", 1), ("B", 1), ("A", 2), ("B", 2), ("A", 3), ("B", 3), ("B", 4))
+
+
+def held_name(relative, parity):
+    if relative == 0:
+        return 0
+    if abs(relative) == 4:
+        return ("B", 4)
+    return ("A" if (relative > 0) == (parity == 0) else "B", abs(relative))
 
 
 def tables(occupied_energy, virtual_energy, tile_occupied, tile_virtual, tile_exponent):
@@ -73,20 +83,28 @@
 
 
 def coulomb_pairs(blocks, pairs):
-    names = sorted({d for pair in pairs for d in pair})
+    names = [
+        n for n in HELD if n in {held_name(d, parity) for pair in pairs for d in pair for parity in (0, 1)}
+    ]
 
     def kernel(*refs):
         block = dict(zip(names, refs))
         own, other = refs[len(names) :]
         core = lax.axis_index("core")
-        for k, (r, c) in enumerate(pairs):
-            for out, part in ((own, core), (other, 1 - core)):
-                left = block[r][:, pl.ds(pl.multiple_of(part * TS, TS), TS)]
-                product = lax.dot_general(
-                    left, block[c][...], (((0,), (0,)), ((), ())), preferred_element_type=f32
-                )
-                for h in (0, 1):
-                    out[k, h] = product[:, h * TS : (h + 1) * TS].astype(out.dtype)
+        me = lax.axis_index("pair")
+        for parity in (0, 1):
+
+            @pl.when(lax.rem(me, 2) == parity)
+            def _(parity=parity):
+                for k, (r, c) in enumerate(pairs):
+                    rows, columns = block[held_name(r, parity)], block[held_name(c, parity)]
+                    for out, part in ((own, core), (other, 1 - core)):
+                        left = rows[:, pl.ds(pl.multiple_of(part * TS, TS), TS)]
+                        product = lax.dot_general(
+                            left, columns[...], (((0,), (0,)), ((), ())), preferred_element_type=f32
+                        )
+                        for h in (0, 1):
+                            out[k, h] = product[:, h * TS : (h + 1) * TS].astype(out.dtype)
 
     shape = (len(pairs), 2, TS, TS)
     return pl.pallas_call(
@@ -96,7 +114,7 @@
         out_specs=(in_vmem, in_vmem),
         compiler_params=pltpu.CompilerParams(vmem_limit_bytes=VMEM_LIMIT),
         name="coulomb_pairs",
-    )(*[blocks[d] for d in names])
+    )(*[blocks[n] for n in names])
 
 
 def sum_cores(own, received):
@@ -168,26 +186,28 @@
 
 def gamma_rows(blocks, mine, theirs, scales):
     rows, width = blocks[0].shape
-    names = [q for q, _ in ORDER]
 
     def kernel(*refs):
-        block = refs[: len(names)]
-        own, other, scale, out, matrix = refs[len(names) :]
+        block = refs[: len(HELD)]
+        own, other, scale, out, matrix = refs[len(HELD) :]
         core = lax.axis_index("core")
+        even = lax.rem(lax.axis_index("pair"), 2) == 0
         for pair in range(0, len(ORDER), 2):
             for part, source in ((core, own), (1 - core, other)):
                 place = pl.ds(pl.multiple_of(part * TS, TS), TS)
                 both = source[:, pair * PIECE : (pair + 2) * PIECE].astype(f32)
                 for k in (0, 1):
                     i = pair + k
+                    q, transposed = ORDER[i]
+                    held = jnp.where(even, HELD.index(held_name(q, 0)), HELD.index(held_name(q, 1)))
                     tiles = both[:, k * PIECE : (k + 1) * PIECE].reshape(2, TS, TS)
                     for h in (0, 1):
-                        if ORDER[i][1]:
+                        if transposed:
                             tile = tiles[h].T * scale[2 * i + h : 2 * i + h + 1]
-                            matrix[i, h * TS : (h + 1) * TS, place] = tile.astype(bf16)
+                            matrix[held, h * TS : (h + 1) * TS, place] = tile.astype(bf16)
                         else:
                             tile = tiles[h] * scale[pl.ds(2 * i + part, 1)]
-                            matrix[i, place, h * TS : (h + 1) * TS] = tile.astype(bf16)
+                            matrix[held, place, h * TS : (h + 1) * TS] = tile.astype(bf16)
 
         for start in range(0, rows, ROWS):
             total = None
@@ -199,45 +219,56 @@
     return pl.pallas_call(
         kernel,
         out_shape=jax.ShapeDtypeStruct((rows, width), bf16),
-        in_specs=[in_vmem] * (len(names) + 3),
-        out_specs=in_vmem,
-        scratch_shapes=[pltpu.VMEM((len(ORDER), WIDTH, WIDTH), bf16)],
+        in_specs=[in_vmem] * (len(HELD) + 3),
+        out_specs=in_vmem,
+        scratch_shapes=[pltpu.VMEM((len(HELD), WIDTH, WIDTH), bf16)],
         compiler_params=pltpu.CompilerParams(vmem_limit_bytes=VMEM_LIMIT),
         name="gamma_rows",
-    )(*[blocks[q] for q in names], mine, theirs, scales)
+    )(*[blocks[n] for n in HELD], mine, theirs, scales)
 
 
 def body(three_index, *energies):
-    up, down = ring(NPAIR, 1), ring(NPAIR, -1)
-    swap = ring(NCORE, 1)
+    def swap_a(x):
+        return lax.ppermute(x, "pair", SWAP_A)
+
+    def swap_b(x):
+        return lax.ppermute(x, "pair", SWAP_B)
+
+    def swap_cores(x):
+        return lax.ppermute(x, "core", SWAP_CORES)
 
     block = {0: three_index}
-    block[-1] = lax.ppermute(block[0], "pair", up)
-    block[1] = lax.ppermute(block[0], "pair", down)
+    block["A", 1] = swap_a(block[0])
+    block["B", 1] = swap_b(block[0])
     denominator, scales = tables(*energies)
-    block[-1], denominator, scales = lax.optimization_barrier((block[-1], denominator, scales))
-    block[-2] = lax.ppermute(block[-1], "pair", up)
-    block[2] = lax.ppermute(block[1], "pair", down)
+    block["B", 1], denominator, scales = lax.optimization_barrier(
+        (block["B", 1], denominator, scales)
+    )
+    block["B", 2] = swap_b(block["A", 1])
+    block["A", 2] = swap_a(block["B", 1])
 
     early, other_early = coulomb_pairs(block, EARLY)
-    got_early = lax.ppermute(other_early, "core", swap)
+    got_early = swap_cores(other_early)
     late, other_late = coulomb_pairs(block, LATE)
-    got_late = lax.ppermute(other_late, "core", swap)
+    got_late = swap_cores(other_late)
     summed = sum_cores((early, late), (got_early, got_late))
 
-    summed, block[-2], block[2] = lax.optimization_barrier((summed, block[-2], block[2]))
-    block[-3] = lax.ppermute(block[-2], "pair", up)
-    block[3] = lax.ppermute(block[2], "pair", down)
-    block[-4] = lax.ppermute(block[-2], "pair", ring(NPAIR, 2))
+    summed, block["A", 2], block["B", 2] = lax.optimization_barrier(
+        (summed, block["A", 2], block["B", 2])
+    )
+    block["A", 3] = swap_a(block["B", 2])
+    block["B", 3] = swap_b(block["A", 2])
     parts = lax.all_to_all(summed, "z", 0, 0)
     parts = lax.all_to_all(sum_z(parts), ("pair", "x"), 0, 0)
     copies = amplitude_copies(parts, denominator)
-    copies, block[-3], block[3], block[-4] = lax.optimization_barrier(
-        (copies, block[-3], block[3], block[-4])
-    )
+
+    copies, block["A", 3], block["B", 3] = lax.optimization_barrier(
+        (copies, block["A", 3], block["B", 3])
+    )
+    block["B", 4] = swap_b(block["A", 3])
     mine = lax.all_to_all(copies, ("z", "x"), 0, 0)
-    theirs = lax.ppermute(mine, "core", swap)
-    return gamma_rows(block, mine, theirs, scales)
+    mine, block["B", 4] = lax.optimization_barrier((mine, block["B", 4]))
+    return gamma_rows(block, mine, swap_cores(mine), scales)
 
 
 def solution(mesh):

time: 127 us -> 113 us (0.89)
  blocking collectives: 55.5 us -> 17.2 us
  waiting for transfers between devices: 5.6 us -> 27.4 us
  Pallas kernels: 4.94 us -> 6.69 us
    all_to_all x1 -> x0, blocking collectives: 23.1 us -> none  [body(): mine = lax.all_to_all(copies, ('z', 'x'), 0, 0)]
    all_to_all x1, blocking collectives: 32.4 us -> 17.2 us  [body(): parts = lax.all_to_all(sum_z(parts), ('pair', 'x'), 0, 0)]
    ppermute x10, waiting for transfers between devices: 3.73 us -> 18.4 us  [the longest x4 16 us: swap_b(): return lax.ppermute(x, 'pair', SWAP_B)]
    all_to_all x1, waiting for transfers between devices: 1.87 us -> 8.26 us  [body(): parts = lax.all_to_all(summed, 'z', 0, 0)]
    ppermute x10, starting transfers between devices: 45.7 us -> 41.4 us  [the longest x4 17 us: swap_b(): return lax.ppermute(x, 'pair', SWAP_B)]
    all_to_all x0 -> x1, starting transfers between devices: none -> 4.03 us  [body(): mine = lax.all_to_all(copies, ('z', 'x'), 0, 0)]
  transfers between devices with their start and end apart: 11 -> 12, of which waited for: 4 -> 7; matrix products, arithmetic and copies ran while one was open for 0% -> 0% of each run, Pallas kernels for 2% -> 2%
where the time goes in v9:
time: 113 us; the launch traced here: 112 us
  starting transfers between devices  56.3 us (50%)
  waiting for transfers between devices  27.4 us (24%)
  blocking collectives  17.2 us (15%)
  Pallas kernels  6.69 us (6%)
  local copies, waits for them, and re-layouts  4.35 us (4%)
    all_to_all x1, blocking collectives, body(): parts = lax.all_to_all(sum_z(parts), ('pair', 'x'), 0, 0)  17.2 us
    ppermute x4, starting transfers between devices, swap_b(): return lax.ppermute(x, 'pair', SWAP_B)  17 us
    ppermute x3, starting transfers between devices, swap_cores(): return lax.ppermute(x, 'core', SWAP_CORES)  16.5 us
    ppermute x4, waiting for transfers between devices, swap_b(): return lax.ppermute(x, 'pair', SWAP_B)  16 us
    all_to_all x1, starting transfers between devices, body(): parts = lax.all_to_all(summed, 'z', 0, 0)  10.9 us
    all_to_all x1, waiting for transfers between devices, body(): parts = lax.all_to_all(summed, 'z', 0, 0)  8.26 us
    ppermute x3, starting transfers between devices, swap_a(): return lax.ppermute(x, 'pair', SWAP_A)  7.9 us
    unnamed x18, local copies, waits for them, and re-layouts  4.35 us
  transfers between devices with their start and end apart: 12, of which 7 were waited for; matrix products, arithmetic and copies ran while one was open for 0% of the time, Pallas kernels for 2%

profile of v9, /device:TPU:1, one launch (start us, length us, event | category | flops | bytes accessed | tf_op | source)
XLA Modules:
  0.0 112.1 jit_solution(7284927811721908850)
XLA Ops:
  0.0 0.0 copy-start.7
  0.0 0.0 copy-start.6
  0.0 0.0 copy-start.5
  0.0 6.1 %collective-permute-start.1 = (bf16[896,256]{1,0:T(8,128)(2,1)}, bf16[896,256]{1,0:T(8,128)(2,1)S(1)}, u32[]{:S(2)}, u32[]{:S(2)}) collective-permute-start(bf16[896,256]{1,0:T(8,128)(2,1)} %refs_0_.3), channel_id=1, source_target_pairs={{0,7},{1,2},{2,1},{3,4},{4,3},{5,6},{6,5},{7,0},{8,15},{9,10},{10,... | collective-permute-start | bytes 1376264 | tf_op jit(solution)/shard_map/ppermute | solution.py:235
  6.1 1.9 %collective-permute-start = (bf16[896,256]{1,0:T(8,128)(2,1)}, bf16[896,256]{1,0:T(8,128)(2,1)S(1)}, u32[]{:S(2)}, u32[]{:S(2)}) collective-permute-start(bf16[896,256]{1,0:T(8,128)(2,1)} %refs_0_.3), channel_id=1, source_target_pairs={{0,1},{1,0},{2,3},{3,2},{4,5},{5,4},{6,7},{7,6},{8,9},{9,8},{10,11... | collective-permute-start | bytes 1376264 | tf_op jit(solution)/shard_map/ppermute | solution.py:232
  8.0 0.0 copy-done.7
  8.0 0.0 copy-done.6
  8.0 0.0 copy-done.5
  8.0 0.0 copy-start.4
  8.0 0.9 copy-done.4
  8.9 0.0 copy-start.8
  8.9 0.7 copy-done.8
  9.6 0.7 tables.1
  10.3 3.3 %collective-permute-done.1.refs_2_.refs_1_ = bf16[896,256]{1,0:T(8,128)(2,1)S(1)} collective-permute-done((bf16[896,256]{1,0:T(8,128)(2,1)}, bf16[896,256]{1,0:T(8,128)(2,1)S(1)}, u32[]{:S(2)}, u32[]{:S(2)}) %collective-permute-start.1) | collective-permute-done | bytes 458784 | tf_op jit(solution)/shard_map/ppermute | solution.py:235
  13.6 4.1 %collective-permute-start.2 = (bf16[896,256]{1,0:T(8,128)(2,1)S(1)}, bf16[896,256]{1,0:T(8,128)(2,1)S(1)}, u32[]{:S(2)}, u32[]{:S(2)}) collective-permute-start(bf16[896,256]{1,0:T(8,128)(2,1)S(1)} %collective-permute-done.1.refs_2_.refs_1_), channel_id=1, source_target_pairs={{0,1},{1,0},{2,3},{3,2},{4,5},{5,4},{6,7},{7,6},{8,9},{9,8},{10,11... | collective-permute-start | bytes 1376264 | tf_op jit(solution)/shard_map/ppermute | solution.py:232
  17.7 0.0 collective-permute-done.refs_1_.refs_0_
  17.7 4.9 %collective-permute-start.3 = (bf16[896,256]{1,0:T(8,128)(2,1)S(1)}, bf16[896,256]{1,0:T(8,128)(2,1)S(1)}, u32[]{:S(2)}, u32[]{:S(2)}) collective-permute-start(bf16[896,256]{1,0:T(8,128)(2,1)S(1)} %collective-permute-done.refs_1_.refs_0_), channel_id=1, source_target_pairs={{0,7},{1,2},{2,1},{3,4},{4,3},{5,6},{6,5},{7,0},{8,15},{9,10},{10,... | collective-permute-start | bytes 1376264 | tf_op jit(solution)/shard_map/ppermute | solution.py:235
  22.6 0.0 copy-start
  22.6 1.0 copy-done
  23.6 0.6 coulomb_pairs.2
  24.2 4.2 %collective-permute-start.4 = (bf16[3,2,128,128]{3,2,1,0:T(8,128)(2,1)S(1)}, bf16[3,2,128,128]{3,2,1,0:T(8,128)(2,1)S(1)}, u32[]{:S(2)}, u32[]{:S(2)}) collective-permute-start(bf16[3,2,128,128]{3,2,1,0:T(8,128)(2,1)S(1)} %get-tuple-element.27), channel_id=1, source_target_pairs={{0,8},{8,0},{1,9},{9,1},{2,10},{10,2},{3,11},{11,3},{4,12},{12,4},... | collective-permute-start | bytes 589832 | tf_op jit(solution)/shard_map/ppermute | solution.py:238
  28.4 0.0 collective-permute-done.2.refs_2_.refs_3_
  28.4 2.0 %collective-permute-done.3.refs_3_.refs_4_ = bf16[896,256]{1,0:T(8,128)(2,1)S(1)} collective-permute-done((bf16[896,256]{1,0:T(8,128)(2,1)S(1)}, bf16[896,256]{1,0:T(8,128)(2,1)S(1)}, u32[]{:S(2)}, u32[]{:S(2)}) %collective-permute-start.3) | collective-permute-done | bytes 458784 | tf_op jit(solution)/shard_map/ppermute | solution.py:235
  30.4 0.5 coulomb_pairs.3
  30.9 6.0 %collective-permute-start.5 = (bf16[2,2,128,128]{3,2,1,0:T(8,128)(2,1)S(1)}, bf16[2,2,128,128]{3,2,1,0:T(8,128)(2,1)S(1)}, u32[]{:S(2)}, u32[]{:S(2)}) collective-permute-start(bf16[2,2,128,128]{3,2,1,0:T(8,128)(2,1)S(1)} %get-tuple-element.28), channel_id=1, source_target_pairs={{0,8},{8,0},{1,9},{9,1},{2,10},{10,2},{3,11},{11,3},{4,12},{12,4},... | collective-permute-start | bytes 393224 | tf_op jit(solution)/shard_map/ppermute | solution.py:238
  36.8 0.0 collective-permute-done.4.refs_2_
  36.9 1.0 collective-permute-done.5.refs_3_
  37.8 0.8 sum_cores.1
  38.6 10.9 %all-to-all-start = ((bf16[8,160,128]{2,1,0:T(8,128)(2,1)}), bf16[8,160,128]{2,1,0:T(8,128)(2,1)S(1)}, u32[]{:S(2)}, u32[]{:S(2)}) async-start(bf16[8,160,128]{2,1,0:T(8,128)(2,1)} %sum_cores.1), calls=%async_computation | async-start | bytes 655360 | tf_op jit(solution)/shard_map/all_to_all | solution.py:261
  49.5 3.4 %collective-permute-start.7 = (bf16[896,256]{1,0:T(8,128)(2,1)S(1)}, bf16[896,256]{1,0:T(8,128)(2,1)S(1)}, u32[]{:S(2)}, u32[]{:S(2)}) collective-permute-start(bf16[896,256]{1,0:T(8,128)(2,1)S(1)} %collective-permute-done.2.refs_2_.refs_3_), channel_id=1, source_target_pairs={{0,7},{1,2},{2,1},{3,4},{4,3},{5,6},{6,5},{7,0},{8,15},{9,10},{10,... | collective-permute-start | bytes 1376264 | tf_op jit(solution)/shard_map/ppermute | solution.py:235
  52.9 1.9 %collective-permute-start.6 = (bf16[896,256]{1,0:T(8,128)(2,1)S(1)}, bf16[896,256]{1,0:T(8,128)(2,1)}, u32[]{:S(2)}, u32[]{:S(2)}) collective-permute-start(bf16[896,256]{1,0:T(8,128)(2,1)S(1)} %collective-permute-done.3.refs_3_.refs_4_), channel_id=1, source_target_pairs={{0,1},{1,0},{2,3},{3,2},{4,5},{5,4},{6,7},{7,6},{8,9},{9,8},{10,11... | collective-permute-start | bytes 1376264 | tf_op jit(solution)/shard_map/ppermute | solution.py:232
  54.8 8.3 %all-to-all-done.parts_ref = bf16[8,160,128]{2,1,0:T(8,128)(2,1)S(1)} async-done(((bf16[8,160,128]{2,1,0:T(8,128)(2,1)}), bf16[8,160,128]{2,1,0:T(8,128)(2,1)S(1)}, u32[]{:S(2)}, u32[]{:S(2)}) %all-to-all-start) | async-done | bytes 327712 | tf_op jit(solution)/shard_map/all_to_all | solution.py:261
  63.1 0.1 sum_z.1
  63.2 17.2 %all_to_all.15.parts_ref = bf16[32,16,128]{2,1,0:T(8,128)(2,1)S(1)} all-to-all(bf16[32,16,128]{2,1,0:T(8,128)(2,1)S(1)} %sum_z.1), channel_id=1, replica_groups=mesh['x'=4,'z'=8,'core'=2,'pair'=8] {'pair','x'}, dimensions={0} | all-to-all | bytes 262144 | tf_op jit(solution)/shard_map/all_to_all | solution.py:262
  80.3 0.9 amplitude_copies.1
  81.2 0.0 copy-start.1
  81.2 0.0 collective-permute-done.7.refs_6_
  81.2 0.0 collective-permute-done.6.refs_5_
  81.2 4.0 %all-to-all-start.2 = ((bf16[32,64,128]{2,1,0:T(8,128)(2,1)}), bf16[32,64,128]{2,1,0:T(8,128)(2,1)S(1)}, u32[]{:S(2)}, u32[]{:S(2)}) async-start(bf16[32,64,128]{2,1,0:T(8,128)(2,1)} %amplitude_copies.1), calls=%async_computation.2 | async-start | bytes 1048576 | tf_op jit(solution)/shard_map/all_to_all | solution.py:269
  85.3 2.6 %collective-permute-start.8 = (bf16[896,256]{1,0:T(8,128)(2,1)}, bf16[896,256]{1,0:T(8,128)(2,1)S(1)}, u32[]{:S(2)}, u32[]{:S(2)}) collective-permute-start(bf16[896,256]{1,0:T(8,128)(2,1)} %collective-permute-done.6.refs_5_), channel_id=1, source_target_pairs={{0,7},{1,2},{2,1},{3,4},{4,3},{5,6},{6,5},{7,0},{8,15},{9,10},{10,... | collective-permute-start | bytes 1376264 | tf_op jit(solution)/shard_map/ppermute | solution.py:235
  87.9 10.6 %collective-permute-done.8.refs_7_ = bf16[896,256]{1,0:T(8,128)(2,1)S(1)} collective-permute-done((bf16[896,256]{1,0:T(8,128)(2,1)}, bf16[896,256]{1,0:T(8,128)(2,1)S(1)}, u32[]{:S(2)}, u32[]{:S(2)}) %collective-permute-start.8) | collective-permute-done | bytes 458784 | tf_op jit(solution)/shard_map/ppermute | solution.py:235
  98.5 0.0 copy-start.2
  98.5 0.8 copy-done.2
  99.3 0.7 all-to-all-done.2.refs_8_
  99.9 6.4 %collective-permute-start.9 = (bf16[32,64,128]{2,1,0:T(8,128)(2,1)S(1)}, bf16[32,64,128]{2,1,0:T(8,128)(2,1)S(1)}, u32[]{:S(2)}, u32[]{:S(2)}) collective-permute-start(bf16[32,64,128]{2,1,0:T(8,128)(2,1)S(1)} %all-to-all-done.2.refs_8_), channel_id=1, source_target_pairs={{0,8},{8,0},{1,9},{9,1},{2,10},{10,2},{3,11},{11,3},{4,12},{12,4},... | collective-permute-start | bytes 1572872 | tf_op jit(solution)/shard_map/ppermute | solution.py:238
  106.4 1.5 %collective-permute-done.9.refs_9_ = bf16[32,64,128]{2,1,0:T(8,128)(2,1)S(1)} collective-permute-done((bf16[32,64,128]{2,1,0:T(8,128)(2,1)S(1)}, bf16[32,64,128]{2,1,0:T(8,128)(2,1)S(1)}, u32[]{:S(2)}, u32[]{:S(2)}) %collective-permute-start.9) | collective-permute-done | bytes 524320 | tf_op jit(solution)/shard_map/ppermute | solution.py:238
  107.9 0.0 copy-done.1
  107.9 0.0 copy-start.3
  107.9 1.0 copy-done.3
  108.9 3.2 %gamma_rows.1 = bf16[896,256]{1,0:T(8,128)(2,1)} custom-call(bf16[896,256]{1,0:T(8,128)(2,1)S(1)} %copy-done.1, bf16[896,256]{1,0:T(8,128)(2,1)S(1)} %collective-permute-done.refs_1_.refs_0_, bf16[896,256]{1,0:T(8,128)(2,1)S(1)} %collective-permute-done.1.refs_2_.refs_1_, bf16[896,256]{1,0:T(8,128)(2,1)S(1)} %collective-permute-done.2.refs_2_.refs_3_, ...), custom_call_target="tpu_custom_call" | custom-call | tf_op jit(solution)/shard_map/gamma_rows/pallas_call | solution.py:219
Async XLA Ops:
  0.0 8.0 %copy-start.7 = (s32[16]{0:T(128)S(1)}, s32[16]{0:T(128)}, u32[]{:S(2)}) copy-start(s32[16]{0:T(128)} %virtual_of.1) | copy-start | bytes 196
  0.0 8.0 %copy-start.6 = (s32[16]{0:T(128)S(1)}, s32[16]{0:T(128)}, u32[]{:S(2)}) copy-start(s32[16]{0:T(128)} %occupied_of.1) | copy-start | bytes 196
  0.0 8.0 %copy-start.5 = (f32[64]{0:T(128)S(1)}, f32[64]{0:T(128)}, u32[]{:S(2)}) copy-start(f32[64]{0:T(128)} %occupied.1) | copy-start | bytes 772
  0.0 13.6 %collective-permute-start.1 = (bf16[896,256]{1,0:T(8,128)(2,1)}, bf16[896,256]{1,0:T(8,128)(2,1)S(1)}, u32[]{:S(2)}, u32[]{:S(2)}) collective-permute-start(bf16[896,256]{1,0:T(8,128)(2,1)} %refs_0_.3), channel_id=1, source_target_pairs={{0,7},{1,2},{2,1},{3,4},{4,3},{5,6},{6,5},{7,0},{8,15},{9,10},{10,... | collective-permute-start | bytes 1376264 | tf_op jit(solution)/shard_map/ppermute | solution.py:235
  6.1 11.6 %collective-permute-start = (bf16[896,256]{1,0:T(8,128)(2,1)}, bf16[896,256]{1,0:T(8,128)(2,1)S(1)}, u32[]{:S(2)}, u32[]{:S(2)}) collective-permute-start(bf16[896,256]{1,0:T(8,128)(2,1)} %refs_0_.3), channel_id=1, source_target_pairs={{0,1},{1,0},{2,3},{3,2},{4,5},{5,4},{6,7},{7,6},{8,9},{9,8},{10,11... | collective-permute-start | bytes 1376264 | tf_op jit(solution)/shard_map/ppermute | solution.py:232
  8.0 0.9 copy-start.4
  8.9 0.7 copy-start.8
  13.6 14.8 %collective-permute-start.2 = (bf16[896,256]{1,0:T(8,128)(2,1)S(1)}, bf16[896,256]{1,0:T(8,128)(2,1)S(1)}, u32[]{:S(2)}, u32[]{:S(2)}) collective-permute-start(bf16[896,256]{1,0:T(8,128)(2,1)S(1)} %collective-permute-done.1.refs_2_.refs_1_), channel_id=1, source_target_pairs={{0,1},{1,0},{2,3},{3,2},{4,5},{5,4},{6,7},{7,6},{8,9},{9,8},{10,11... | collective-permute-start | bytes 1376264 | tf_op jit(solution)/shard_map/ppermute | solution.py:232
  17.7 12.7 %collective-permute-start.3 = (bf16[896,256]{1,0:T(8,128)(2,1)S(1)}, bf16[896,256]{1,0:T(8,128)(2,1)S(1)}, u32[]{:S(2)}, u32[]{:S(2)}) collective-permute-start(bf16[896,256]{1,0:T(8,128)(2,1)S(1)} %collective-permute-done.refs_1_.refs_0_), channel_id=1, source_target_pairs={{0,7},{1,2},{2,1},{3,4},{4,3},{5,6},{6,5},{7,0},{8,15},{9,10},{10,... | collective-permute-start | bytes 1376264 | tf_op jit(solution)/shard_map/ppermute | solution.py:235
  22.6 1.0 copy-start
  24.2 12.7 %collective-permute-start.4 = (bf16[3,2,128,128]{3,2,1,0:T(8,128)(2,1)S(1)}, bf16[3,2,128,128]{3,2,1,0:T(8,128)(2,1)S(1)}, u32[]{:S(2)}, u32[]{:S(2)}) collective-permute-start(bf16[3,2,128,128]{3,2,1,0:T(8,128)(2,1)S(1)} %get-tuple-element.27), channel_id=1, source_target_pairs={{0,8},{8,0},{1,9},{9,1},{2,10},{10,2},{3,11},{11,3},{4,12},{12,4},... | collective-permute-start | bytes 589832 | tf_op jit(solution)/shard_map/ppermute | solution.py:238
  30.9 6.9 %collective-permute-start.5 = (bf16[2,2,128,128]{3,2,1,0:T(8,128)(2,1)S(1)}, bf16[2,2,128,128]{3,2,1,0:T(8,128)(2,1)S(1)}, u32[]{:S(2)}, u32[]{:S(2)}) collective-permute-start(bf16[2,2,128,128]{3,2,1,0:T(8,128)(2,1)S(1)} %get-tuple-element.28), channel_id=1, source_target_pairs={{0,8},{8,0},{1,9},{9,1},{2,10},{10,2},{3,11},{11,3},{4,12},{12,4},... | collective-permute-start | bytes 393224 | tf_op jit(solution)/shard_map/ppermute | solution.py:238
  38.6 24.5 %all-to-all-start = ((bf16[8,160,128]{2,1,0:T(8,128)(2,1)}), bf16[8,160,128]{2,1,0:T(8,128)(2,1)S(1)}, u32[]{:S(2)}, u32[]{:S(2)}) async-start(bf16[8,160,128]{2,1,0:T(8,128)(2,1)} %sum_cores.1), calls=%async_computation | async-start | bytes 655360 | tf_op jit(solution)/shard_map/all_to_all | solution.py:261
  49.5 31.8 %collective-permute-start.7 = (bf16[896,256]{1,0:T(8,128)(2,1)S(1)}, bf16[896,256]{1,0:T(8,128)(2,1)S(1)}, u32[]{:S(2)}, u32[]{:S(2)}) collective-permute-start(bf16[896,256]{1,0:T(8,128)(2,1)S(1)} %collective-permute-done.2.refs_2_.refs_3_), channel_id=1, source_target_pairs={{0,7},{1,2},{2,1},{3,4},{4,3},{5,6},{6,5},{7,0},{8,15},{9,10},{10,... | collective-permute-start | bytes 1376264 | tf_op jit(solution)/shard_map/ppermute | solution.py:235
  52.9 28.3 %collective-permute-start.6 = (bf16[896,256]{1,0:T(8,128)(2,1)S(1)}, bf16[896,256]{1,0:T(8,128)(2,1)}, u32[]{:S(2)}, u32[]{:S(2)}) collective-permute-start(bf16[896,256]{1,0:T(8,128)(2,1)S(1)} %collective-permute-done.3.refs_3_.refs_4_), channel_id=1, source_target_pairs={{0,1},{1,0},{2,3},{3,2},{4,5},{5,4},{6,7},{7,6},{8,9},{9,8},{10,11... | collective-permute-start | bytes 1376264 | tf_op jit(solution)/shard_map/ppermute | solution.py:232
  81.2 26.7 %copy-start.1 = (bf16[896,256]{1,0:T(8,128)(2,1)S(1)}, bf16[896,256]{1,0:T(8,128)(2,1)}, u32[]{:S(2)}) copy-start(bf16[896,256]{1,0:T(8,128)(2,1)} %refs_0_.3) | copy-start | bytes 1376260
  81.2 18.7 %all-to-all-start.2 = ((bf16[32,64,128]{2,1,0:T(8,128)(2,1)}), bf16[32,64,128]{2,1,0:T(8,128)(2,1)S(1)}, u32[]{:S(2)}, u32[]{:S(2)}) async-start(bf16[32,64,128]{2,1,0:T(8,128)(2,1)} %amplitude_copies.1), calls=%async_computation.2 | async-start | bytes 1048576 | tf_op jit(solution)/shard_map/all_to_all | solution.py:269
  85.3 13.2 %collective-permute-start.8 = (bf16[896,256]{1,0:T(8,128)(2,1)}, bf16[896,256]{1,0:T(8,128)(2,1)S(1)}, u32[]{:S(2)}, u32[]{:S(2)}) collective-permute-start(bf16[896,256]{1,0:T(8,128)(2,1)} %collective-permute-done.6.refs_5_), channel_id=1, source_target_pairs={{0,7},{1,2},{2,1},{3,4},{4,3},{5,6},{6,5},{7,0},{8,15},{9,10},{10,... | collective-permute-start | bytes 1376264 | tf_op jit(solution)/shard_map/ppermute | solution.py:235
  98.5 0.8 copy-start.2
  99.9 7.9 %collective-permute-start.9 = (bf16[32,64,128]{2,1,0:T(8,128)(2,1)S(1)}, bf16[32,64,128]{2,1,0:T(8,128)(2,1)S(1)}, u32[]{:S(2)}, u32[]{:S(2)}) collective-permute-start(bf16[32,64,128]{2,1,0:T(8,128)(2,1)S(1)} %all-to-all-done.2.refs_8_), channel_id=1, source_target_pairs={{0,8},{8,0},{1,9},{9,1},{2,10},{10,2},{3,11},{11,3},{4,12},{12,4},... | collective-permute-start | bytes 1572872 | tf_op jit(solution)/shard_map/ppermute | solution.py:238
  107.9 1.0 copy-start.3

commit v10 on v7

--- a/solution.py
+++ b/solution.py
@@ -229,17 +229,16 @@
     got_late = lax.ppermute(other_late, "core", swap)
     summed = sum_cores((early, late), (got_early, got_late))
 
-    summed, block[-2], block[2] = lax.optimization_barrier((summed, block[-2], block[2]))
     block[-3] = lax.ppermute(block[-2], "pair", up)
-    block[3] = lax.ppermute(block[2], "pair", down)
     parts = lax.all_to_all(summed, "z", 0, 0)
+    parts, block[-3], block[2] = lax.optimization_barrier((parts, block[-3], block[2]))
     parts = lax.all_to_all(sum_z(parts), ("pair", "x"), 0, 0)
     copies = amplitude_copies(parts, denominator)
-
-    copies, block[-3], block[3] = lax.optimization_barrier((copies, block[-3], block[3]))
+    copies, block[-3], block[2] = lax.optimization_barrier((copies, block[-3], block[2]))
+    block[3] = lax.ppermute(block[2], "pair", down)
     last = (lax.ppermute(block[-3], "pair", up),)
     mine = lax.all_to_all(copies, ("z", "x"), 0, 0)
-    mine, last = lax.optimization_barrier((mine, last))
+    mine, last, block[3] = lax.optimization_barrier((mine, last, block[3]))
     theirs = lax.ppermute(mine, "core", swap)
     return gamma_rows(block, last, mine, theirs, scales)
 

time: 113 us -> 118 us (1.044)
  waiting for transfers between devices: 21.9 us -> 24.3 us
  starting transfers between devices: 60.2 us -> 62.6 us
  local copies, waits for them, and re-layouts: 4.35 us -> 6.14 us
    ppermute x1, waiting for transfers between devices: 0.01 us -> 12.7 us  [body(): block[-3] = lax.ppermute(block[-2], 'pair', up)]
    ppermute x1, waiting for transfers between devices: 10.3 us -> 1.76 us  [body(): last = (lax.ppermute(block[-3], 'pair', up),)]
    all_to_all x1, waiting for transfers between devices: 6.39 us -> 0.01 us  [body(): parts = lax.all_to_all(summed, 'z', 0, 0)]
    ppermute x1, waiting for transfers between devices: 0.01 us -> 5.48 us  [body(): block[3] = lax.ppermute(block[2], 'pair', down)]
    all_to_all x1, starting transfers between devices: 4.03 us -> 7.79 us  [body(): mine = lax.all_to_all(copies, ('z', 'x'), 0, 0)]
    ppermute x1, starting transfers between devices: 4.38 us -> 1.92 us  [body(): block[3] = lax.ppermute(block[2], 'pair', down)]
    unnamed x18 -> x22, local copies, waits for them, and re-layouts: 4.35 us -> 6.14 us
where the time goes in v10:
time: 118 us; the launch traced here: 117 us
  starting transfers between devices  62.6 us (53%)
  waiting for transfers between devices  24.3 us (21%)
  blocking collectives  18 us (15%)
  local copies, waits for them, and re-layouts  6.14 us (5%)
  Pallas kernels  5.75 us (5%)
    all_to_all x1, blocking collectives, body(): parts = lax.all_to_all(sum_z(parts), ('pair', 'x'), 0, 0)  18 us
    ppermute x1, waiting for transfers between devices, body(): block[-3] = lax.ppermute(block[-2], 'pair', up)  12.7 us
    all_to_all x1, starting transfers between devices, body(): parts = lax.all_to_all(summed, 'z', 0, 0)  11.2 us
    all_to_all x1, starting transfers between devices, body(): mine = lax.all_to_all(copies, ('z', 'x'), 0, 0)  7.79 us
    ppermute x1, starting transfers between devices, body(): theirs = lax.ppermute(mine, 'core', swap)  6.81 us
    ppermute x1, starting transfers between devices, body(): got_early = lax.ppermute(other_early, 'core', swap)  6.28 us
    unnamed x22, local copies, waits for them, and re-layouts  6.14 us
    ppermute x1, waiting for transfers between devices, body(): block[3] = lax.ppermute(block[2], 'pair', down)  5.48 us
  transfers between devices with their start and end apart: 12, of which 6 were waited for; matrix products, arithmetic and copies ran while one was open for 0% of the time, Pallas kernels for 2%

profile of v10, /device:TPU:1, one launch (start us, length us, event | category | flops | bytes accessed | tf_op | source)
XLA Modules:
  0.0 116.9 jit_solution(2347205185366023410)
XLA Ops:
  0.0 0.0 copy-start.9
  0.0 0.0 copy-start.8
  0.0 0.0 copy-start.7
  0.0 4.2 %collective-permute-start.1 = (bf16[896,256]{1,0:T(8,128)(2,1)}, bf16[896,256]{1,0:T(8,128)(2,1)S(1)}, u32[]{:S(2)}, u32[]{:S(2)}) collective-permute-start(bf16[896,256]{1,0:T(8,128)(2,1)} %refs_0_.1), channel_id=1, source_target_pairs={{0,1},{1,2},{2,3},{3,4},{4,5},{5,6},{6,7},{7,0},{8,9},{9,10},{10,1... | collective-permute-start | bytes 1376264 | tf_op jit(solution)/shard_map/ppermute | solution.py:219
  4.2 3.8 %collective-permute-start = (bf16[896,256]{1,0:T(8,128)(2,1)}, bf16[896,256]{1,0:T(8,128)(2,1)S(1)}, u32[]{:S(2)}, u32[]{:S(2)}) collective-permute-start(bf16[896,256]{1,0:T(8,128)(2,1)} %refs_0_.1), channel_id=1, source_target_pairs={{0,7},{1,0},{2,1},{3,2},{4,3},{5,4},{6,5},{7,6},{8,15},{9,8},{10,9... | collective-permute-start | bytes 1376264 | tf_op jit(solution)/shard_map/ppermute | solution.py:220
  8.0 0.0 copy-done.9
  8.0 0.0 copy-done.8
  8.0 0.0 copy-done.7
  8.0 0.0 copy-start.6
  8.0 0.9 copy-done.6
  8.9 0.0 copy-start.10
  8.9 0.7 copy-done.10
  9.6 0.7 tables.1
  10.3 1.8 %collective-permute-done.1.refs_0_.refs_1_.refs_2_ = bf16[896,256]{1,0:T(8,128)(2,1)S(1)} collective-permute-done((bf16[896,256]{1,0:T(8,128)(2,1)}, bf16[896,256]{1,0:T(8,128)(2,1)S(1)}, u32[]{:S(2)}, u32[]{:S(2)}) %collective-permute-start.1) | collective-permute-done | bytes 458784 | tf_op jit(solution)/shard_map/ppermute | solution.py:219
  12.1 5.0 %collective-permute-start.2 = (bf16[896,256]{1,0:T(8,128)(2,1)S(1)}, bf16[896,256]{1,0:T(8,128)(2,1)S(1)}, u32[]{:S(2)}, u32[]{:S(2)}) collective-permute-start(bf16[896,256]{1,0:T(8,128)(2,1)S(1)} %collective-permute-done.1.refs_0_.refs_1_.refs_2_), channel_id=1, source_target_pairs={{0,1},{1,2},{2,3},{3,4},{4,5},{5,6},{6,7},{7,0},{8,9},{9,10},{10,1... | collective-permute-start | bytes 1376264 | tf_op jit(solution)/shard_map/ppermute | solution.py:223
  17.1 0.0 collective-permute-done.refs_2_.refs_1_
  17.1 4.3 %collective-permute-start.3 = (bf16[896,256]{1,0:T(8,128)(2,1)S(1)}, bf16[896,256]{1,0:T(8,128)(2,1)S(1)}, u32[]{:S(2)}, u32[]{:S(2)}) collective-permute-start(bf16[896,256]{1,0:T(8,128)(2,1)S(1)} %collective-permute-done.refs_2_.refs_1_), channel_id=1, source_target_pairs={{0,7},{1,0},{2,1},{3,2},{4,3},{5,4},{6,5},{7,6},{8,15},{9,8},{10,9... | collective-permute-start | bytes 1376264 | tf_op jit(solution)/shard_map/ppermute | solution.py:224
  21.5 0.0 copy-start
  21.5 1.0 copy-done
  22.5 0.6 coulomb_pairs.2
  23.1 6.3 %collective-permute-start.4 = (bf16[3,2,128,128]{3,2,1,0:T(8,128)(2,1)S(1)}, bf16[3,2,128,128]{3,2,1,0:T(8,128)(2,1)S(1)}, u32[]{:S(2)}, u32[]{:S(2)}) collective-permute-start(bf16[3,2,128,128]{3,2,1,0:T(8,128)(2,1)S(1)} %get-tuple-element.28), channel_id=1, source_target_pairs={{0,8},{8,0},{1,9},{9,1},{2,10},{10,2},{3,11},{11,3},{4,12},{12,4},... | collective-permute-start | bytes 589832 | tf_op jit(solution)/shard_map/ppermute | solution.py:227
  29.4 0.0 collective-permute-done.2.refs_0_.refs_3_
  29.4 0.0 collective-permute-done.3.refs_2_.refs_4_
  29.5 0.5 coulomb_pairs.3
  29.9 5.1 %collective-permute-start.5 = (bf16[2,2,128,128]{3,2,1,0:T(8,128)(2,1)S(1)}, bf16[2,2,128,128]{3,2,1,0:T(8,128)(2,1)S(1)}, u32[]{:S(2)}, u32[]{:S(2)}) collective-permute-start(bf16[2,2,128,128]{3,2,1,0:T(8,128)(2,1)S(1)} %get-tuple-element.29), channel_id=1, source_target_pairs={{0,8},{8,0},{1,9},{9,1},{2,10},{10,2},{3,11},{11,3},{4,12},{12,4},... | collective-permute-start | bytes 393224 | tf_op jit(solution)/shard_map/ppermute | solution.py:229
  35.0 0.0 collective-permute-done.4.refs_2_
  35.0 1.0 collective-permute-done.5.refs_3_
  36.0 0.8 sum_cores.1
  36.8 11.2 %all-to-all-start = ((bf16[8,160,128]{2,1,0:T(8,128)(2,1)}), bf16[8,160,128]{2,1,0:T(8,128)(2,1)S(1)}, u32[]{:S(2)}, u32[]{:S(2)}) async-start(bf16[8,160,128]{2,1,0:T(8,128)(2,1)} %sum_cores.1), calls=%async_computation | async-start | bytes 655360 | tf_op jit(solution)/shard_map/all_to_all | solution.py:233
  47.9 2.9 %collective-permute-start.6 = (bf16[896,256]{1,0:T(8,128)(2,1)S(1)}, bf16[896,256]{1,0:T(8,128)(2,1)S(1)}, u32[]{:S(2)}, u32[]{:S(2)}) collective-permute-start(bf16[896,256]{1,0:T(8,128)(2,1)S(1)} %collective-permute-done.2.refs_0_.refs_3_), channel_id=1, source_target_pairs={{0,1},{1,2},{2,3},{3,4},{4,5},{5,6},{6,7},{7,0},{8,9},{9,10},{10,1... | collective-permute-start | bytes 1376264 | tf_op jit(solution)/shard_map/ppermute | solution.py:232
  50.8 12.7 %collective-permute-done.6.refs_6_ = bf16[896,256]{1,0:T(8,128)(2,1)S(1)} collective-permute-done((bf16[896,256]{1,0:T(8,128)(2,1)S(1)}, bf16[896,256]{1,0:T(8,128)(2,1)S(1)}, u32[]{:S(2)}, u32[]{:S(2)}) %collective-permute-start.6) | collective-permute-done | bytes 458784 | tf_op jit(solution)/shard_map/ppermute | solution.py:232
  63.5 0.0 all-to-all-done.parts_ref
  63.5 0.1 sum_z.1
  63.6 18.0 %all_to_all.15.parts_ref = bf16[32,16,128]{2,1,0:T(8,128)(2,1)S(1)} all-to-all(bf16[32,16,128]{2,1,0:T(8,128)(2,1)S(1)} %sum_z.1), channel_id=1, replica_groups=mesh['x'=4,'z'=8,'core'=2,'pair'=8] {'pair','x'}, dimensions={0} | all-to-all | bytes 262144 | tf_op jit(solution)/shard_map/all_to_all | solution.py:235
  81.5 0.9 amplitude_copies.1
  82.4 0.0 copy-start.1
  82.4 7.8 %all-to-all-start.2 = ((bf16[32,64,128]{2,1,0:T(8,128)(2,1)}), bf16[32,64,128]{2,1,0:T(8,128)(2,1)S(1)}, u32[]{:S(2)}, u32[]{:S(2)}) async-start(bf16[32,64,128]{2,1,0:T(8,128)(2,1)} %amplitude_copies.1), calls=%async_computation.2 | async-start | bytes 1048576 | tf_op jit(solution)/shard_map/all_to_all | solution.py:240
  90.2 1.9 %collective-permute-start.8 = (bf16[896,256]{1,0:T(8,128)(2,1)S(1)}, bf16[896,256]{1,0:T(8,128)(2,1)S(1)}, u32[]{:S(2)}, u32[]{:S(2)}) collective-permute-start(bf16[896,256]{1,0:T(8,128)(2,1)S(1)} %collective-permute-done.3.refs_2_.refs_4_), channel_id=1, source_target_pairs={{0,7},{1,0},{2,1},{3,2},{4,3},{5,4},{6,5},{7,6},{8,15},{9,8},{10,9... | collective-permute-start | bytes 1376264 | tf_op jit(solution)/shard_map/ppermute | solution.py:238
  92.2 3.4 %collective-permute-start.7 = (bf16[896,256]{1,0:T(8,128)(2,1)S(1)}, bf16[896,256]{1,0:T(8,128)(2,1)S(1)}, u32[]{:S(2)}, u32[]{:S(2)}) collective-permute-start(bf16[896,256]{1,0:T(8,128)(2,1)S(1)} %collective-permute-done.6.refs_6_), channel_id=1, source_target_pairs={{0,1},{1,2},{2,3},{3,4},{4,5},{5,6},{6,7},{7,0},{8,9},{9,10},{10,1... | collective-permute-start | bytes 1376264 | tf_op jit(solution)/shard_map/ppermute | solution.py:239
  95.5 5.5 %collective-permute-done.8.refs_5_ = bf16[896,256]{1,0:T(8,128)(2,1)S(1)} collective-permute-done((bf16[896,256]{1,0:T(8,128)(2,1)S(1)}, bf16[896,256]{1,0:T(8,128)(2,1)S(1)}, u32[]{:S(2)}, u32[]{:S(2)}) %collective-permute-start.8) | collective-permute-done | bytes 458784 | tf_op jit(solution)/shard_map/ppermute | solution.py:238
  101.0 0.0 copy-start.2
  101.0 0.8 copy-done.2
  101.8 1.8 %collective-permute-done.7.refs_7_ = bf16[896,256]{1,0:T(8,128)(2,1)S(1)} collective-permute-done((bf16[896,256]{1,0:T(8,128)(2,1)S(1)}, bf16[896,256]{1,0:T(8,128)(2,1)S(1)}, u32[]{:S(2)}, u32[]{:S(2)}) %collective-permute-start.7) | collective-permute-done | bytes 458784 | tf_op jit(solution)/shard_map/ppermute | solution.py:239
  103.5 0.0 copy-start.4
  103.5 0.8 copy-done.4
  104.3 0.0 all-to-all-done.2.refs_8_
  104.3 6.8 %collective-permute-start.9 = (bf16[32,64,128]{2,1,0:T(8,128)(2,1)S(1)}, bf16[32,64,128]{2,1,0:T(8,128)(2,1)S(1)}, u32[]{:S(2)}, u32[]{:S(2)}) collective-permute-start(bf16[32,64,128]{2,1,0:T(8,128)(2,1)S(1)} %all-to-all-done.2.refs_8_), channel_id=1, source_target_pairs={{0,8},{8,0},{1,9},{9,1},{2,10},{10,2},{3,11},{11,3},{4,12},{12,4},... | collective-permute-start | bytes 1572872 | tf_op jit(solution)/shard_map/ppermute | solution.py:242
  111.1 1.5 %collective-permute-done.9.refs_9_ = bf16[32,64,128]{2,1,0:T(8,128)(2,1)S(1)} collective-permute-done((bf16[32,64,128]{2,1,0:T(8,128)(2,1)S(1)}, bf16[32,64,128]{2,1,0:T(8,128)(2,1)S(1)}, u32[]{:S(2)}, u32[]{:S(2)}) %collective-permute-start.9) | collective-permute-done | bytes 524320 | tf_op jit(solution)/shard_map/ppermute | solution.py:242
  112.6 0.0 copy-done.1
  112.6 0.0 copy-start.3
  112.6 1.0 copy-done.3
  113.7 0.0 copy-start.5
  113.7 1.0 copy-done.5
  114.7 2.2 %gamma_rows.1 = bf16[896,256]{1,0:T(8,128)(2,1)} custom-call(bf16[896,256]{1,0:T(8,128)(2,1)S(1)} %copy-done.1, bf16[896,256]{1,0:T(8,128)(2,1)S(1)} %collective-permute-done.refs_2_.refs_1_, bf16[896,256]{1,0:T(8,128)(2,1)S(1)} %collective-permute-done.1.refs_0_.refs_1_.refs_2_, bf16[896,256]{1,0:T(8,128)(2,1)S(1)} %collective-permute-done.2.refs_0_.refs_3_, ...), custom_call_target="tpu_custom_call" | custom-call | tf_op jit(solution)/shard_map/gamma_rows/pallas_call | solution.py:203
Async XLA Ops:
  0.0 8.0 %copy-start.9 = (s32[16]{0:T(128)S(1)}, s32[16]{0:T(128)}, u32[]{:S(2)}) copy-start(s32[16]{0:T(128)} %virtual_of.1) | copy-start | bytes 196
  0.0 8.0 %copy-start.8 = (s32[16]{0:T(128)S(1)}, s32[16]{0:T(128)}, u32[]{:S(2)}) copy-start(s32[16]{0:T(128)} %occupied_of.1) | copy-start | bytes 196
  0.0 8.0 %copy-start.7 = (f32[64]{0:T(128)S(1)}, f32[64]{0:T(128)}, u32[]{:S(2)}) copy-start(f32[64]{0:T(128)} %occupied.1) | copy-start | bytes 772
  0.0 12.1 %collective-permute-start.1 = (bf16[896,256]{1,0:T(8,128)(2,1)}, bf16[896,256]{1,0:T(8,128)(2,1)S(1)}, u32[]{:S(2)}, u32[]{:S(2)}) collective-permute-start(bf16[896,256]{1,0:T(8,128)(2,1)} %refs_0_.1), channel_id=1, source_target_pairs={{0,1},{1,2},{2,3},{3,4},{4,5},{5,6},{6,7},{7,0},{8,9},{9,10},{10,1... | collective-permute-start | bytes 1376264 | tf_op jit(solution)/shard_map/ppermute | solution.py:219
  4.2 12.9 %collective-permute-start = (bf16[896,256]{1,0:T(8,128)(2,1)}, bf16[896,256]{1,0:T(8,128)(2,1)S(1)}, u32[]{:S(2)}, u32[]{:S(2)}) collective-permute-start(bf16[896,256]{1,0:T(8,128)(2,1)} %refs_0_.1), channel_id=1, source_target_pairs={{0,7},{1,0},{2,1},{3,2},{4,3},{5,4},{6,5},{7,6},{8,15},{9,8},{10,9... | collective-permute-start | bytes 1376264 | tf_op jit(solution)/shard_map/ppermute | solution.py:220
  8.0 0.9 copy-start.6
  8.9 0.7 copy-start.10
  12.1 17.3 %collective-permute-start.2 = (bf16[896,256]{1,0:T(8,128)(2,1)S(1)}, bf16[896,256]{1,0:T(8,128)(2,1)S(1)}, u32[]{:S(2)}, u32[]{:S(2)}) collective-permute-start(bf16[896,256]{1,0:T(8,128)(2,1)S(1)} %collective-permute-done.1.refs_0_.refs_1_.refs_2_), channel_id=1, source_target_pairs={{0,1},{1,2},{2,3},{3,4},{4,5},{5,6},{6,7},{7,0},{8,9},{9,10},{10,1... | collective-permute-start | bytes 1376264 | tf_op jit(solution)/shard_map/ppermute | solution.py:223
  17.1 12.3 %collective-permute-start.3 = (bf16[896,256]{1,0:T(8,128)(2,1)S(1)}, bf16[896,256]{1,0:T(8,128)(2,1)S(1)}, u32[]{:S(2)}, u32[]{:S(2)}) collective-permute-start(bf16[896,256]{1,0:T(8,128)(2,1)S(1)} %collective-permute-done.refs_2_.refs_1_), channel_id=1, source_target_pairs={{0,7},{1,0},{2,1},{3,2},{4,3},{5,4},{6,5},{7,6},{8,15},{9,8},{10,9... | collective-permute-start | bytes 1376264 | tf_op jit(solution)/shard_map/ppermute | solution.py:224
  21.5 1.0 copy-start
  23.1 11.9 %collective-permute-start.4 = (bf16[3,2,128,128]{3,2,1,0:T(8,128)(2,1)S(1)}, bf16[3,2,128,128]{3,2,1,0:T(8,128)(2,1)S(1)}, u32[]{:S(2)}, u32[]{:S(2)}) collective-permute-start(bf16[3,2,128,128]{3,2,1,0:T(8,128)(2,1)S(1)} %get-tuple-element.28), channel_id=1, source_target_pairs={{0,8},{8,0},{1,9},{9,1},{2,10},{10,2},{3,11},{11,3},{4,12},{12,4},... | collective-permute-start | bytes 589832 | tf_op jit(solution)/shard_map/ppermute | solution.py:227
  29.9 6.0 %collective-permute-start.5 = (bf16[2,2,128,128]{3,2,1,0:T(8,128)(2,1)S(1)}, bf16[2,2,128,128]{3,2,1,0:T(8,128)(2,1)S(1)}, u32[]{:S(2)}, u32[]{:S(2)}) collective-permute-start(bf16[2,2,128,128]{3,2,1,0:T(8,128)(2,1)S(1)} %get-tuple-element.29), channel_id=1, source_target_pairs={{0,8},{8,0},{1,9},{9,1},{2,10},{10,2},{3,11},{11,3},{4,12},{12,4},... | collective-permute-start | bytes 393224 | tf_op jit(solution)/shard_map/ppermute | solution.py:229
  36.8 26.7 %all-to-all-start = ((bf16[8,160,128]{2,1,0:T(8,128)(2,1)}), bf16[8,160,128]{2,1,0:T(8,128)(2,1)S(1)}, u32[]{:S(2)}, u32[]{:S(2)}) async-start(bf16[8,160,128]{2,1,0:T(8,128)(2,1)} %sum_cores.1), calls=%async_computation | async-start | bytes 655360 | tf_op jit(solution)/shard_map/all_to_all | solution.py:233
  47.9 15.6 %collective-permute-start.6 = (bf16[896,256]{1,0:T(8,128)(2,1)S(1)}, bf16[896,256]{1,0:T(8,128)(2,1)S(1)}, u32[]{:S(2)}, u32[]{:S(2)}) collective-permute-start(bf16[896,256]{1,0:T(8,128)(2,1)S(1)} %collective-permute-done.2.refs_0_.refs_3_), channel_id=1, source_target_pairs={{0,1},{1,2},{2,3},{3,4},{4,5},{5,6},{6,7},{7,0},{8,9},{9,10},{10,1... | collective-permute-start | bytes 1376264 | tf_op jit(solution)/shard_map/ppermute | solution.py:232
  82.4 30.2 %copy-start.1 = (bf16[896,256]{1,0:T(8,128)(2,1)S(1)}, bf16[896,256]{1,0:T(8,128)(2,1)}, u32[]{:S(2)}) copy-start(bf16[896,256]{1,0:T(8,128)(2,1)} %refs_0_.1) | copy-start | bytes 1376260
  82.4 21.9 %all-to-all-start.2 = ((bf16[32,64,128]{2,1,0:T(8,128)(2,1)}), bf16[32,64,128]{2,1,0:T(8,128)(2,1)S(1)}, u32[]{:S(2)}, u32[]{:S(2)}) async-start(bf16[32,64,128]{2,1,0:T(8,128)(2,1)} %amplitude_copies.1), calls=%async_computation.2 | async-start | bytes 1048576 | tf_op jit(solution)/shard_map/all_to_all | solution.py:240
  90.2 10.8 %collective-permute-start.8 = (bf16[896,256]{1,0:T(8,128)(2,1)S(1)}, bf16[896,256]{1,0:T(8,128)(2,1)S(1)}, u32[]{:S(2)}, u32[]{:S(2)}) collective-permute-start(bf16[896,256]{1,0:T(8,128)(2,1)S(1)} %collective-permute-done.3.refs_2_.refs_4_), channel_id=1, source_target_pairs={{0,7},{1,0},{2,1},{3,2},{4,3},{5,4},{6,5},{7,6},{8,15},{9,8},{10,9... | collective-permute-start | bytes 1376264 | tf_op jit(solution)/shard_map/ppermute | solution.py:238
  92.2 11.4 %collective-permute-start.7 = (bf16[896,256]{1,0:T(8,128)(2,1)S(1)}, bf16[896,256]{1,0:T(8,128)(2,1)S(1)}, u32[]{:S(2)}, u32[]{:S(2)}) collective-permute-start(bf16[896,256]{1,0:T(8,128)(2,1)S(1)} %collective-permute-done.6.refs_6_), channel_id=1, source_target_pairs={{0,1},{1,2},{2,3},{3,4},{4,5},{5,6},{6,7},{7,0},{8,9},{9,10},{10,1... | collective-permute-start | bytes 1376264 | tf_op jit(solution)/shard_map/ppermute | solution.py:239
  101.0 0.8 copy-start.2
  103.5 0.8 copy-start.4
  104.3 8.3 %collective-permute-start.9 = (bf16[32,64,128]{2,1,0:T(8,128)(2,1)S(1)}, bf16[32,64,128]{2,1,0:T(8,128)(2,1)S(1)}, u32[]{:S(2)}, u32[]{:S(2)}) collective-permute-start(bf16[32,64,128]{2,1,0:T(8,128)(2,1)S(1)} %all-to-all-done.2.refs_8_), channel_id=1, source_target_pairs={{0,8},{8,0},{1,9},{9,1},{2,10},{10,2},{3,11},{11,3},{4,12},{12,4},... | collective-permute-start | bytes 1572872 | tf_op jit(solution)/shard_map/ppermute | solution.py:242
  112.6 1.0 copy-start.3
  113.7 1.0 copy-start.5

commit v11 on v0

v11 whole, which is shorter than its diff:
```python
import jax
import jax.numpy as jnp
from jax import lax
from jax.experimental import pallas as pl
from jax.experimental.pallas import tpu as pltpu
from jax.sharding import Mesh, PartitionSpec as P

TS = 128
VT = 157
NT = 16
NX, NZ, NCORE, NPAIR = 4, 8, 2, 8
NXZ = NX * NZ
AUX = ("x", "z", "core")
WIDTH = 2 * TS
PIECE = WIDTH // NXZ
CHUNKS = 2
SWAP_A = [(i, i ^ 1) for i in range(NPAIR)]
SWAP_B = [(i, (i + (-1 if i % 2 == 0 else 1)) % NPAIR) for i in range(NPAIR)]
SWAP_CORES = [(0, 1), (1, 0)]
HELD = (0, 1, -1, 2, -2, 3, -3, 4)
EARLY = 5
ROWS = 224
VMEM_LIMIT = 12 * 1024 * 1024
bf16, f32 = jnp.bfloat16, jnp.float32
in_vmem = pl.BlockSpec(memory_space=pltpu.VMEM)
in_smem = pl.BlockSpec(memory_space=pltpu.SMEM)
PARAMS = pltpu.CompilerParams(vmem_limit_bytes=VMEM_LIMIT)


def denominators(occupied_energy, virtual_energy, tile_occupied, tile_virtual, tile_exponent):
    def kernel(occupied, virtual, occupied_of, virtual_of, exponent, out):
        me = lax.axis_index("pair")
        core = lax.axis_index("core")
        side = 1 - 2 * lax.rem(me, 2)
        slot = lax.axis_index("z") * NX + lax.axis_index("x")
        half, first = slot // (NXZ // 2), (slot % (NXZ // 2)) * PIECE

        def tile_of(relative, part):
            return lax.rem(2 * (me + relative + NPAIR) + part, NT)

        def energy(tile):
            return virtual[pl.ds(virtual_of[tile], 1)] - occupied[occupied_of[tile]]

        def scale(tile):
            level = exponent[tile]
            return jnp.where(level == -1, 0.5, jnp.where(level == 1, 2.0, 1.0)).astype(f32)

        lane = lax.broadcasted_iota(jnp.int32, (PIECE, TS), 1)
        chosen = lane == first + lax.broadcasted_iota(jnp.int32, (PIECE, TS), 0)
        column = tile_of(0, half)
        for k, distance in enumerate(HELD):
            row = tile_of(side * distance, core)
            of_row = jnp.sum(jnp.where(chosen, energy(row), 0.0), axis=1, keepdims=True)
            level = jnp.full((PIECE, TS), scale(row) * scale(row) * scale(column), f32)
            out[k * PIECE : (k + 1) * PIECE] = (of_row + energy(column)) / level

    return pl.pallas_call(
        kernel,
        out_shape=jax.ShapeDtypeStruct((len(HELD) * PIECE, TS), f32),
        in_specs=[in_smem, in_vmem, in_smem, in_smem, in_smem],
        out_specs=in_vmem,
        compiler_params=PARAMS,
        name="denominators",
    )(occupied_energy, virtual_energy.reshape(VT, TS), tile_occupied, tile_virtual, tile_exponent)


def coulomb_blocks(own, blocks):
    height = own.shape[0] // CHUNKS
    given = [block for block in blocks if block is not None]

    def kernel(own_ref, *refs):
        mine, other = refs[-2:]
        core = lax.axis_index("core")
        n = 0
        for k, block in enumerate(blocks):
            if block is None:
                parts = [own_ref.at[i * height : (i + 1) * height] for i in range(CHUNKS)]
            else:
                parts = refs[n : n + CHUNKS]
                n += CHUNKS
            for out, part in ((mine, core), (other, 1 - core)):
                total = None
                for i, rows in enumerate(parts):
                    left = rows[:, pl.ds(pl.multiple_of(part * TS, TS), TS)]
                    right = own_ref[i * height : (i + 1) * height]
                    term = lax.dot_general(left, right, (((0,), (0,)), ((), ())), preferred_element_type=f32)
                    total = term if total is None else total + term
                for h in (0, 1):
                    out[k, h] = total[:, h * TS : (h + 1) * TS].astype(out.dtype)

    shape = (len(blocks), 2, TS, TS)
    return pl.pallas_call(
        kernel,
        out_shape=(jax.ShapeDtypeStruct(shape, f32), jax.ShapeDtypeStruct(shape, bf16)),
        in_specs=[in_vmem] * (1 + CHUNKS * len(given)),
        out_specs=(in_vmem, in_vmem),
        compiler_params=PARAMS,
        name="coulomb_blocks",
    )(own, *[part for block in given for part in block])


def sum_cores(own, received):
    count = sum(a.shape[0] for a in own)

    def kernel(*refs):
        parts = []
        for mine, theirs in zip(refs[: len(own)], refs[len(own) : -1]):
            total = (mine[...] + theirs[...].astype(f32)).reshape(-1, NXZ, PIECE, TS)
            parts += [total[k] for k in range(total.shape[0])]
        refs[-1][...] = jnp.concatenate(parts, axis=1).astype(bf16)

    return pl.pallas_call(
        kernel,
        out_shape=jax.ShapeDtypeStruct((NXZ, count * PIECE, TS), bf16),
        in_specs=[in_vmem] * (2 * len(own)),
        out_specs=in_vmem,
        compiler_params=PARAMS,
        name="sum_cores",
    )(*own, *received)


def amplitude_copies(parts, denominator):
    def kernel(parts_ref, denominator_ref, out):
        total = jnp.sum(parts_ref[...].astype(f32), axis=0)
        out[...] = jnp.broadcast_to((total / denominator_ref[...]).astype(bf16)[None], out.shape)

    return pl.pallas_call(
        kernel,
        out_shape=jax.ShapeDtypeStruct(parts.shape, bf16),
        in_specs=[in_vmem] * 2,
        out_specs=in_vmem,
        compiler_params=PARAMS,
        name="amplitude_copies",
    )(parts, denominator)


def gamma_rows(own, blocks, mine, theirs):
    rows, width = own.shape
    height = rows // CHUNKS

    def kernel(own_ref, *refs):
        block = refs[: CHUNKS * len(blocks)]
        mine_ref, theirs_ref, out, matrix = refs[CHUNKS * len(blocks) :]
        core = lax.axis_index("core")
        for pair in range(0, len(HELD), 2):
            for part, source in ((core, mine_ref), (1 - core, theirs_ref)):
                place = pl.ds(pl.multiple_of(part * TS, TS), TS)
                both = source[:, pair * PIECE : (pair + 2) * PIECE].astype(f32)
                for k in (0, 1):
                    tiles = both[:, k * PIECE : (k + 1) * PIECE].reshape(2, TS, TS).astype(bf16)
                    for h in (0, 1):
                        matrix[pair + k, place, h * TS : (h + 1) * TS] = tiles[h]

        for start in range(0, rows, ROWS):
            part, offset = divmod(start, height)
            total = jnp.dot(own_ref[start : start + ROWS], matrix[0], preferred_element_type=f32)
            for k in range(len(blocks)):
                left = block[CHUNKS * k + part][offset : offset + ROWS]
                total += jnp.dot(left, matrix[k + 1], preferred_element_type=f32)
            out[start : start + ROWS] = total.astype(bf16)

    return pl.pallas_call(
        kernel,
        out_shape=jax.ShapeDtypeStruct((rows, width), bf16),
        in_specs=[in_vmem] * (3 + CHUNKS * len(blocks)),
        out_specs=in_vmem,
        scratch_shapes=[pltpu.VMEM((len(HELD), WIDTH, WIDTH), bf16)],
        compiler_params=PARAMS,
        name="gamma_rows",
    )(own, *[part for block in blocks for part in block], mine, theirs)


def body(three_index, *energies):
    def swap_a(x):
        return lax.ppermute(x, "pair", SWAP_A)

    def swap_b(x):
        return lax.ppermute(x, "pair", SWAP_B)

    def swap_cores(x):
        return lax.ppermute(x, "core", SWAP_CORES)

    height = three_index.shape[0] // CHUNKS
    own = [three_index[i * height : (i + 1) * height] for i in range(CHUNKS)]
    a1, b1, a2, b2, a3, b3 = ([None] * CHUNKS for _ in range(6))
    for i in range(CHUNKS):
        a1[i], b1[i] = swap_a(own[i]), swap_b(own[i])
    denominator = denominators(*energies)
    a1[0], denominator = lax.optimization_barrier((a1[0], denominator))
    for i in range(CHUNKS):
        b2[i], a2[i] = swap_b(a1[i]), swap_a(b1[i])
    for i in range(CHUNKS):
        a3[i], b3[i] = swap_a(b2[i]), swap_b(a2[i])
    opposite = [swap_b(a3[0]), swap_a(b3[1])]
    blocks = [a1, b1, a2, b2, a3, b3, opposite]

    early, other_early = coulomb_blocks(three_index, [None] + blocks[: EARLY - 1])
    got_early = swap_cores(other_early)
    late, other_late = coulomb_blocks(three_index, blocks[EARLY - 1 :])
    got_late = swap_cores(other_late)
    parts = lax.all_to_all(sum_cores((early, late), (got_early, got_late)), ("z", "x"), 0, 0)
    mine = lax.all_to_all(amplitude_copies(parts, denominator), ("z", "x"), 0, 0)
    return gamma_rows(three_index, blocks, mine, swap_cores(mine))


def solution(mesh):
    grid = Mesh(mesh.devices.reshape(NX, NZ, NCORE, NPAIR), AUX + ("pair",))
    placed = (P(AUX, "pair"), P(), P(), P(), P(), P())
    return jax.shard_map(
        body, mesh=grid, in_specs=placed, out_specs=P(AUX, "pair"), check_vma=False
    )
```

time: 292 us -> 118 us (0.40)
  waiting for transfers between devices: 265 us -> 2.59 us
  starting transfers between devices: 0.04 us -> 61.2 us
  blocking collectives: 0 us -> 47.6 us
  between operations: 13.4 us -> 0.36 us
  matrix products: 9.29 us -> 0 us
  Pallas kernels: 0 us -> 4.41 us
    psum x1 -> x0, waiting for transfers between devices: 199 us -> none  [body(): summed = lax.psum(coulomb, 'aux')]
    all_gather x1 -> x0, waiting for transfers between devices: 64.9 us -> none  [body(): gathered = lax.all_gather(three_index, 'pair', axis=1, tiled=True)]
    ppermute x0 -> x17, starting transfers between devices: none -> 61.2 us  [the longest x7 24.1 us: swap_b(): return lax.ppermute(x, 'pair', SWAP_B)]
    all_to_all x0 -> x2, blocking collectives: none -> 47.6 us  [the longest x1 27.6 us: body(): lax.all_to_all(sum_cores((early, late), (got_early, got_late)), ('z', 'x'...]
    dot_general x2 -> x0, matrix products: 9.29 us -> none  [the longest x1 4.73 us: body(): lax.dot_general(gathered, three_index, contract, preferred_element_type=j...]
    pallas_call x0 -> x6, Pallas kernels: none -> 4.41 us  [the longest x1 1.95 us: gamma_rows(): pl.pallas_call(kernel, out_shape=jax.ShapeDtypeStruct((rows, width), bf16...]
  transfers between devices with their start and end apart: 2 -> 17, of which waited for: 2 -> 2; matrix products, arithmetic and copies ran while one was open for 1% -> 0% of each run, Pallas kernels for 0% -> 2%
where the time goes in v11:
time: 118 us; the launch traced here: 117 us
  starting transfers between devices  61.2 us (52%)
  blocking collectives  47.6 us (40%)
  Pallas kernels  4.41 us (4%)
  waiting for transfers between devices  2.59 us (2%)
    all_to_all x1, blocking collectives, body(): lax.all_to_all(sum_cores((early, late), (got_early, got_late)), ('z', 'x'...  27.6 us
    ppermute x7, starting transfers between devices, swap_b(): return lax.ppermute(x, 'pair', SWAP_B)  24.1 us
    all_to_all x1, blocking collectives, body(): lax.all_to_all(amplitude_copies(parts, denominator), ('z', 'x'), 0, 0)  20.1 us
    ppermute x3, starting transfers between devices, swap_cores(): return lax.ppermute(x, 'core', SWAP_CORES)  19.4 us
    ppermute x7, starting transfers between devices, swap_a(): return lax.ppermute(x, 'pair', SWAP_A)  17.6 us
    ppermute x3, waiting for transfers between devices, swap_cores(): return lax.ppermute(x, 'core', SWAP_CORES)  2.56 us
  transfers between devices with their start and end apart: 17, of which 2 were waited for; matrix products, arithmetic and copies ran while one was open for 0% of the time, Pallas kernels for 2%

profile of v11, /device:TPU:1, one launch (start us, length us, event | category | flops | bytes accessed | tf_op | source)
XLA Modules:
  0.0 117.3 jit_solution(3905758597530421790)
XLA Ops:
  0.0 0.0 copy-start
  0.0 0.0 copy-start.1
  0.0 1.1 fusion
  1.1 4.0 %collective-permute-start = (bf16[448,256]{1,0:T(8,128)(2,1)S(1)}, bf16[448,256]{1,0:T(8,128)(2,1)S(1)}, u32[]{:S(2)}, u32[]{:S(2)}) collective-permute-start(bf16[448,256]{1,0:T(8,128)(2,1)S(1)} %get-tuple-element.18), channel_id=1, source_target_pairs={{0,1},{1,0},{2,3},{3,2},{4,5},{5,4},{6,7},{7,6},{8,9},{9,8},{10,11... | collective-permute-start | bytes 688136 | tf_op jit(solution)/shard_map/ppermute | solution.py:175
  5.2 0.0 copy-start.5
  5.2 0.0 copy-start.2
  5.2 0.0 copy-start.3
  5.2 0.0 copy-start.4
  5.2 5.0 %collective-permute-start.3 = (bf16[448,256]{1,0:T(8,128)(2,1)S(1)}, bf16[448,256]{1,0:T(8,128)(2,1)S(1)}, u32[]{:S(2)}, u32[]{:S(2)}) collective-permute-start(bf16[448,256]{1,0:T(8,128)(2,1)S(1)} %get-tuple-element.17), channel_id=1, source_target_pairs={{0,7},{1,2},{2,1},{3,4},{4,3},{5,6},{6,5},{7,0},{8,15},{9,10},{10,... | collective-permute-start | bytes 688136 | tf_op jit(solution)/shard_map/ppermute | solution.py:178
  10.2 1.9 %collective-permute-start.1 = (bf16[448,256]{1,0:T(8,128)(2,1)S(1)}, bf16[448,256]{1,0:T(8,128)(2,1)S(1)}, u32[]{:S(2)}, u32[]{:S(2)}) collective-permute-start(bf16[448,256]{1,0:T(8,128)(2,1)S(1)} %get-tuple-element.17), channel_id=1, source_target_pairs={{0,1},{1,0},{2,3},{3,2},{4,5},{5,4},{6,7},{7,6},{8,9},{9,8},{10,11... | collective-permute-start | bytes 688136 | tf_op jit(solution)/shard_map/ppermute | solution.py:175
  12.2 4.0 %collective-permute-start.2 = (bf16[448,256]{1,0:T(8,128)(2,1)S(1)}, bf16[448,256]{1,0:T(8,128)(2,1)S(1)}, u32[]{:S(2)}, u32[]{:S(2)}) collective-permute-start(bf16[448,256]{1,0:T(8,128)(2,1)S(1)} %get-tuple-element.18), channel_id=1, source_target_pairs={{0,7},{1,2},{2,1},{3,4},{4,3},{5,6},{6,5},{7,0},{8,15},{9,10},{10,... | collective-permute-start | bytes 688136 | tf_op jit(solution)/shard_map/ppermute | solution.py:178
  16.2 0.0 copy-done.1
  16.2 0.0 copy-done.5
  16.2 0.0 copy-done.2
  16.2 0.0 copy-done.3
  16.3 0.0 copy-done.4
  16.3 0.7 denominators.1.denominator_ref
  17.0 0.0 collective-permute-done.refs_0_
  17.0 0.0 collective-permute-done.3.refs_3_
  17.0 2.3 %collective-permute-start.5 = (bf16[448,256]{1,0:T(8,128)(2,1)S(1)}, bf16[448,256]{1,0:T(8,128)(2,1)S(1)}, u32[]{:S(2)}, u32[]{:S(2)}) collective-permute-start(bf16[448,256]{1,0:T(8,128)(2,1)S(1)} %collective-permute-done.3.refs_3_), channel_id=1, source_target_pairs={{0,1},{1,0},{2,3},{3,2},{4,5},{5,4},{6,7},{7,6},{8,9},{9,8},{10,11... | collective-permute-start | bytes 688136 | tf_op jit(solution)/shard_map/ppermute | solution.py:175
  19.3 2.1 %collective-permute-start.6 = (bf16[448,256]{1,0:T(8,128)(2,1)S(1)}, bf16[448,256]{1,0:T(8,128)(2,1)S(1)}, u32[]{:S(2)}, u32[]{:S(2)}) collective-permute-start(bf16[448,256]{1,0:T(8,128)(2,1)S(1)} %collective-permute-done.refs_0_), channel_id=1, source_target_pairs={{0,7},{1,2},{2,1},{3,4},{4,3},{5,6},{6,5},{7,0},{8,15},{9,10},{10,... | collective-permute-start | bytes 688136 | tf_op jit(solution)/shard_map/ppermute | solution.py:178
  21.4 0.0 collective-permute-done.1.refs_1_
  21.4 4.4 %collective-permute-start.7 = (bf16[448,256]{1,0:T(8,128)(2,1)S(1)}, bf16[448,256]{1,0:T(8,128)(2,1)S(1)}, u32[]{:S(2)}, u32[]{:S(2)}) collective-permute-start(bf16[448,256]{1,0:T(8,128)(2,1)S(1)} %collective-permute-done.1.refs_1_), channel_id=1, source_target_pairs={{0,7},{1,2},{2,1},{3,4},{4,3},{5,6},{6,5},{7,0},{8,15},{9,10},{10,... | collective-permute-start | bytes 688136 | tf_op jit(solution)/shard_map/ppermute | solution.py:178
  25.8 0.0 collective-permute-done.2.refs_2_
  25.8 1.9 %collective-permute-start.4 = (bf16[448,256]{1,0:T(8,128)(2,1)S(1)}, bf16[448,256]{1,0:T(8,128)(2,1)S(1)}, u32[]{:S(2)}, u32[]{:S(2)}) collective-permute-start(bf16[448,256]{1,0:T(8,128)(2,1)S(1)} %collective-permute-done.2.refs_2_), channel_id=1, source_target_pairs={{0,1},{1,0},{2,3},{3,2},{4,5},{5,4},{6,7},{7,6},{8,9},{9,8},{10,11... | collective-permute-start | bytes 688136 | tf_op jit(solution)/shard_map/ppermute | solution.py:175
  27.8 0.0 collective-permute-done.5.refs_5_
  27.8 2.3 %collective-permute-start.11 = (bf16[448,256]{1,0:T(8,128)(2,1)S(1)}, bf16[448,256]{1,0:T(8,128)(2,1)S(1)}, u32[]{:S(2)}, u32[]{:S(2)}) collective-permute-start(bf16[448,256]{1,0:T(8,128)(2,1)S(1)} %collective-permute-done.5.refs_5_), channel_id=1, source_target_pairs={{0,7},{1,2},{2,1},{3,4},{4,3},{5,6},{6,5},{7,0},{8,15},{9,10},{10,... | collective-permute-start | bytes 688136 | tf_op jit(solution)/shard_map/ppermute | solution.py:178
  30.1 0.0 collective-permute-done.6.refs_6_
  30.1 3.4 %collective-permute-start.8 = (bf16[448,256]{1,0:T(8,128)(2,1)S(1)}, bf16[448,256]{1,0:T(8,128)(2,1)S(1)}, u32[]{:S(2)}, u32[]{:S(2)}) collective-permute-start(bf16[448,256]{1,0:T(8,128)(2,1)S(1)} %collective-permute-done.6.refs_6_), channel_id=1, source_target_pairs={{0,1},{1,0},{2,3},{3,2},{4,5},{5,4},{6,7},{7,6},{8,9},{9,8},{10,11... | collective-permute-start | bytes 688136 | tf_op jit(solution)/shard_map/ppermute | solution.py:175
  33.5 0.0 collective-permute-done.7.refs_7_
  33.5 1.9 %collective-permute-start.9 = (bf16[448,256]{1,0:T(8,128)(2,1)S(1)}, bf16[448,256]{1,0:T(8,128)(2,1)S(1)}, u32[]{:S(2)}, u32[]{:S(2)}) collective-permute-start(bf16[448,256]{1,0:T(8,128)(2,1)S(1)} %collective-permute-done.7.refs_7_), channel_id=1, source_target_pairs={{0,1},{1,0},{2,3},{3,2},{4,5},{5,4},{6,7},{7,6},{8,9},{9,8},{10,11... | collective-permute-start | bytes 688136 | tf_op jit(solution)/shard_map/ppermute | solution.py:175
  35.4 0.0 collective-permute-done.4.refs_4_
  35.4 4.2 %collective-permute-start.10 = (bf16[448,256]{1,0:T(8,128)(2,1)S(1)}, bf16[448,256]{1,0:T(8,128)(2,1)S(1)}, u32[]{:S(2)}, u32[]{:S(2)}) collective-permute-start(bf16[448,256]{1,0:T(8,128)(2,1)S(1)} %collective-permute-done.4.refs_4_), channel_id=1, source_target_pairs={{0,7},{1,2},{2,1},{3,4},{4,3},{5,6},{6,5},{7,0},{8,15},{9,10},{10,... | collective-permute-start | bytes 688136 | tf_op jit(solution)/shard_map/ppermute | solution.py:178
  39.6 0.0 collective-permute-done.11.refs_3_.refs_11_
  39.6 2.2 %collective-permute-start.13 = (bf16[448,256]{1,0:T(8,128)(2,1)S(1)}, bf16[448,256]{1,0:T(8,128)(2,1)S(1)}, u32[]{:S(2)}, u32[]{:S(2)}) collective-permute-start(bf16[448,256]{1,0:T(8,128)(2,1)S(1)} %collective-permute-done.11.refs_3_.refs_11_), channel_id=1, source_target_pairs={{0,1},{1,0},{2,3},{3,2},{4,5},{5,4},{6,7},{7,6},{8,9},{9,8},{10,11... | collective-permute-start | bytes 688136 | tf_op jit(solution)/shard_map/ppermute | solution.py:175
  41.8 0.0 collective-permute-done.8.refs_0_.refs_8_
  41.8 2.1 %collective-permute-start.12 = (bf16[448,256]{1,0:T(8,128)(2,1)S(1)}, bf16[448,256]{1,0:T(8,128)(2,1)S(1)}, u32[]{:S(2)}, u32[]{:S(2)}) collective-permute-start(bf16[448,256]{1,0:T(8,128)(2,1)S(1)} %collective-permute-done.8.refs_0_.refs_8_), channel_id=1, source_target_pairs={{0,7},{1,2},{2,1},{3,4},{4,3},{5,6},{6,5},{7,0},{8,15},{9,10},{10,... | collective-permute-start | bytes 688136 | tf_op jit(solution)/shard_map/ppermute | solution.py:178
  43.9 0.0 copy-done
  43.9 0.9 coulomb_blocks.2
  44.8 8.5 %collective-permute-start.14 = (bf16[5,2,128,128]{3,2,1,0:T(8,128)(2,1)S(1)}, bf16[5,2,128,128]{3,2,1,0:T(8,128)(2,1)S(1)}, u32[]{:S(2)}, u32[]{:S(2)}) collective-permute-start(bf16[5,2,128,128]{3,2,1,0:T(8,128)(2,1)S(1)} %get-tuple-element.14), channel_id=1, source_target_pairs={{0,8},{8,0},{1,9},{9,1},{2,10},{10,2},{3,11},{11,3},{4,12},{12,4},... | collective-permute-start | bytes 983048 | tf_op jit(solution)/shard_map/ppermute | solution.py:181
  53.3 0.0 collective-permute-done.9.refs_1_.refs_9_
  53.3 0.0 collective-permute-done.10.refs_2_.refs_10_
  53.3 0.0 collective-permute-done.13.refs_5_.refs_13_
  53.4 0.0 collective-permute-done.12.refs_4_.refs_12_
  53.4 0.6 coulomb_blocks.3
  54.0 5.5 %collective-permute-start.15 = (bf16[3,2,128,128]{3,2,1,0:T(8,128)(2,1)S(1)}, bf16[3,2,128,128]{3,2,1,0:T(8,128)(2,1)S(1)}, u32[]{:S(2)}, u32[]{:S(2)}) collective-permute-start(bf16[3,2,128,128]{3,2,1,0:T(8,128)(2,1)S(1)} %get-tuple-element.15), channel_id=1, source_target_pairs={{0,8},{8,0},{1,9},{9,1},{2,10},{10,2},{3,11},{11,3},{4,12},{12,4},... | collective-permute-start | bytes 589832 | tf_op jit(solution)/shard_map/ppermute | solution.py:181
  59.5 0.0 collective-permute-done.14.refs_2_
  59.5 1.0 collective-permute-done.15.refs_3_
  60.5 0.1 sum_cores.1
  60.6 27.6 %all_to_all.10.parts_ref = bf16[32,64,128]{2,1,0:T(8,128)(2,1)S(1)} all-to-all(bf16[32,64,128]{2,1,0:T(8,128)(2,1)S(1)} %sum_cores.1), channel_id=1, replica_groups=mesh['x'=4,'z'=8,'core'=2,'pair'=8] {'z','x'}, dimensions={0} | all-to-all | bytes 1048576 | tf_op jit(solution)/shard_map/all_to_all | solution.py:201
  88.2 0.1 amplitude_copies.1
  88.3 20.1 %all_to_all.11.refs_14_ = bf16[32,64,128]{2,1,0:T(8,128)(2,1)S(1)} all-to-all(bf16[32,64,128]{2,1,0:T(8,128)(2,1)S(1)} %amplitude_copies.1), channel_id=1, replica_groups=mesh['x'=4,'z'=8,'core'=2,'pair'=8] {'z','x'}, dimensions={0} | all-to-all | bytes 1048576 | tf_op jit(solution)/shard_map/all_to_all | solution.py:202
  108.4 5.5 %collective-permute-start.16 = (bf16[32,64,128]{2,1,0:T(8,128)(2,1)S(1)}, bf16[32,64,128]{2,1,0:T(8,128)(2,1)S(1)}, u32[]{:S(2)}, u32[]{:S(2)}) collective-permute-start(bf16[32,64,128]{2,1,0:T(8,128)(2,1)S(1)} %all_to_all.11.refs_14_), channel_id=1, source_target_pairs={{0,8},{8,0},{1,9},{9,1},{2,10},{10,2},{3,11},{11,3},{4,12},{12,4},... | collective-permute-start | bytes 1572872 | tf_op jit(solution)/shard_map/ppermute | solution.py:181
  113.8 1.5 %collective-permute-done.16.refs_15_ = bf16[32,64,128]{2,1,0:T(8,128)(2,1)S(1)} collective-permute-done((bf16[32,64,128]{2,1,0:T(8,128)(2,1)S(1)}, bf16[32,64,128]{2,1,0:T(8,128)(2,1)S(1)}, u32[]{:S(2)}, u32[]{:S(2)}) %collective-permute-start.16) | collective-permute-done | bytes 524320 | tf_op jit(solution)/shard_map/ppermute | solution.py:181
  115.4 2.0 %gamma_rows.1 = bf16[896,256]{1,0:T(8,128)(2,1)} custom-call(bf16[896,256]{1,0:T(8,128)(2,1)S(1)} %copy-done, bf16[448,256]{1,0:T(8,128)(2,1)S(1)} %collective-permute-done.refs_0_, bf16[448,256]{1,0:T(8,128)(2,1)S(1)} %collective-permute-done.1.refs_1_, bf16[448,256]{1,0:T(8,128)(2,1)S(1)} %collective-permute-done.2.refs_2_, ...), custom_call_target="tpu_custom_call" | custom-call | tf_op jit(solution)/shard_map/gamma_rows/pallas_call | solution.py:162
Async XLA Ops:
  0.0 43.9 %copy-start = (bf16[896,256]{1,0:T(8,128)(2,1)S(1)}, bf16[896,256]{1,0:T(8,128)(2,1)}, u32[]{:S(2)}) copy-start(bf16[896,256]{1,0:T(8,128)(2,1)} %own_ref.5) | copy-start | bytes 1376260
  0.0 16.2 %copy-start.1 = (f32[20096]{0:T(1024)S(1)}, f32[20096]{0:T(1024)}, u32[]{:S(2)}) copy-start(f32[20096]{0:T(1024)} %param.8) | copy-start | bytes 241156
  1.1 15.8 %collective-permute-start = (bf16[448,256]{1,0:T(8,128)(2,1)S(1)}, bf16[448,256]{1,0:T(8,128)(2,1)S(1)}, u32[]{:S(2)}, u32[]{:S(2)}) collective-permute-start(bf16[448,256]{1,0:T(8,128)(2,1)S(1)} %get-tuple-element.18), channel_id=1, source_target_pairs={{0,1},{1,0},{2,3},{3,2},{4,5},{5,4},{6,7},{7,6},{8,9},{9,8},{10,11... | collective-permute-start | bytes 688136 | tf_op jit(solution)/shard_map/ppermute | solution.py:175
  5.2 11.0 %copy-start.5 = (s32[16]{0:T(128)S(1)}, s32[16]{0:T(128)}, u32[]{:S(2)}) copy-start(s32[16]{0:T(128)} %exponent.1) | copy-start | bytes 196
  5.2 11.0 %copy-start.2 = (f32[64]{0:T(128)S(1)}, f32[64]{0:T(128)}, u32[]{:S(2)}) copy-start(f32[64]{0:T(128)} %occupied.1) | copy-start | bytes 772
  5.2 11.0 %copy-start.3 = (s32[16]{0:T(128)S(1)}, s32[16]{0:T(128)}, u32[]{:S(2)}) copy-start(s32[16]{0:T(128)} %occupied_of.1) | copy-start | bytes 196
  5.2 11.0 %copy-start.4 = (s32[16]{0:T(128)S(1)}, s32[16]{0:T(128)}, u32[]{:S(2)}) copy-start(s32[16]{0:T(128)} %virtual_of.1) | copy-start | bytes 196
  5.2 11.7 %collective-permute-start.3 = (bf16[448,256]{1,0:T(8,128)(2,1)S(1)}, bf16[448,256]{1,0:T(8,128)(2,1)S(1)}, u32[]{:S(2)}, u32[]{:S(2)}) collective-permute-start(bf16[448,256]{1,0:T(8,128)(2,1)S(1)} %get-tuple-element.17), channel_id=1, source_target_pairs={{0,7},{1,2},{2,1},{3,4},{4,3},{5,6},{6,5},{7,0},{8,15},{9,10},{10,... | collective-permute-start | bytes 688136 | tf_op jit(solution)/shard_map/ppermute | solution.py:178
  10.2 11.1 %collective-permute-start.1 = (bf16[448,256]{1,0:T(8,128)(2,1)S(1)}, bf16[448,256]{1,0:T(8,128)(2,1)S(1)}, u32[]{:S(2)}, u32[]{:S(2)}) collective-permute-start(bf16[448,256]{1,0:T(8,128)(2,1)S(1)} %get-tuple-element.17), channel_id=1, source_target_pairs={{0,1},{1,0},{2,3},{3,2},{4,5},{5,4},{6,7},{7,6},{8,9},{9,8},{10,11... | collective-permute-start | bytes 688136 | tf_op jit(solution)/shard_map/ppermute | solution.py:175
  12.2 13.6 %collective-permute-start.2 = (bf16[448,256]{1,0:T(8,128)(2,1)S(1)}, bf16[448,256]{1,0:T(8,128)(2,1)S(1)}, u32[]{:S(2)}, u32[]{:S(2)}) collective-permute-start(bf16[448,256]{1,0:T(8,128)(2,1)S(1)} %get-tuple-element.18), channel_id=1, source_target_pairs={{0,7},{1,2},{2,1},{3,4},{4,3},{5,6},{6,5},{7,0},{8,15},{9,10},{10,... | collective-permute-start | bytes 688136 | tf_op jit(solution)/shard_map/ppermute | solution.py:178
  17.0 10.8 %collective-permute-start.5 = (bf16[448,256]{1,0:T(8,128)(2,1)S(1)}, bf16[448,256]{1,0:T(8,128)(2,1)S(1)}, u32[]{:S(2)}, u32[]{:S(2)}) collective-permute-start(bf16[448,256]{1,0:T(8,128)(2,1)S(1)} %collective-permute-done.3.refs_3_), channel_id=1, source_target_pairs={{0,1},{1,0},{2,3},{3,2},{4,5},{5,4},{6,7},{7,6},{8,9},{9,8},{10,11... | collective-permute-start | bytes 688136 | tf_op jit(solution)/shard_map/ppermute | solution.py:175
  19.3 10.8 %collective-permute-start.6 = (bf16[448,256]{1,0:T(8,128)(2,1)S(1)}, bf16[448,256]{1,0:T(8,128)(2,1)S(1)}, u32[]{:S(2)}, u32[]{:S(2)}) collective-permute-start(bf16[448,256]{1,0:T(8,128)(2,1)S(1)} %collective-permute-done.refs_0_), channel_id=1, source_target_pairs={{0,7},{1,2},{2,1},{3,4},{4,3},{5,6},{6,5},{7,0},{8,15},{9,10},{10,... | collective-permute-start | bytes 688136 | tf_op jit(solution)/shard_map/ppermute | solution.py:178
  21.4 12.1 %collective-permute-start.7 = (bf16[448,256]{1,0:T(8,128)(2,1)S(1)}, bf16[448,256]{1,0:T(8,128)(2,1)S(1)}, u32[]{:S(2)}, u32[]{:S(2)}) collective-permute-start(bf16[448,256]{1,0:T(8,128)(2,1)S(1)} %collective-permute-done.1.refs_1_), channel_id=1, source_target_pairs={{0,7},{1,2},{2,1},{3,4},{4,3},{5,6},{6,5},{7,0},{8,15},{9,10},{10,... | collective-permute-start | bytes 688136 | tf_op jit(solution)/shard_map/ppermute | solution.py:178
  25.8 9.6 %collective-permute-start.4 = (bf16[448,256]{1,0:T(8,128)(2,1)S(1)}, bf16[448,256]{1,0:T(8,128)(2,1)S(1)}, u32[]{:S(2)}, u32[]{:S(2)}) collective-permute-start(bf16[448,256]{1,0:T(8,128)(2,1)S(1)} %collective-permute-done.2.refs_2_), channel_id=1, source_target_pairs={{0,1},{1,0},{2,3},{3,2},{4,5},{5,4},{6,7},{7,6},{8,9},{9,8},{10,11... | collective-permute-start | bytes 688136 | tf_op jit(solution)/shard_map/ppermute | solution.py:175
  27.8 11.8 %collective-permute-start.11 = (bf16[448,256]{1,0:T(8,128)(2,1)S(1)}, bf16[448,256]{1,0:T(8,128)(2,1)S(1)}, u32[]{:S(2)}, u32[]{:S(2)}) collective-permute-start(bf16[448,256]{1,0:T(8,128)(2,1)S(1)} %collective-permute-done.5.refs_5_), channel_id=1, source_target_pairs={{0,7},{1,2},{2,1},{3,4},{4,3},{5,6},{6,5},{7,0},{8,15},{9,10},{10,... | collective-permute-start | bytes 688136 | tf_op jit(solution)/shard_map/ppermute | solution.py:178
  30.1 11.7 %collective-permute-start.8 = (bf16[448,256]{1,0:T(8,128)(2,1)S(1)}, bf16[448,256]{1,0:T(8,128)(2,1)S(1)}, u32[]{:S(2)}, u32[]{:S(2)}) collective-permute-start(bf16[448,256]{1,0:T(8,128)(2,1)S(1)} %collective-permute-done.6.refs_6_), channel_id=1, source_target_pairs={{0,1},{1,0},{2,3},{3,2},{4,5},{5,4},{6,7},{7,6},{8,9},{9,8},{10,11... | collective-permute-start | bytes 688136 | tf_op jit(solution)/shard_map/ppermute | solution.py:175
  33.5 19.9 %collective-permute-start.9 = (bf16[448,256]{1,0:T(8,128)(2,1)S(1)}, bf16[448,256]{1,0:T(8,128)(2,1)S(1)}, u32[]{:S(2)}, u32[]{:S(2)}) collective-permute-start(bf16[448,256]{1,0:T(8,128)(2,1)S(1)} %collective-permute-done.7.refs_7_), channel_id=1, source_target_pairs={{0,1},{1,0},{2,3},{3,2},{4,5},{5,4},{6,7},{7,6},{8,9},{9,8},{10,11... | collective-permute-start | bytes 688136 | tf_op jit(solution)/shard_map/ppermute | solution.py:175
  35.4 17.9 %collective-permute-start.10 = (bf16[448,256]{1,0:T(8,128)(2,1)S(1)}, bf16[448,256]{1,0:T(8,128)(2,1)S(1)}, u32[]{:S(2)}, u32[]{:S(2)}) collective-permute-start(bf16[448,256]{1,0:T(8,128)(2,1)S(1)} %collective-permute-done.4.refs_4_), channel_id=1, source_target_pairs={{0,7},{1,2},{2,1},{3,4},{4,3},{5,6},{6,5},{7,0},{8,15},{9,10},{10,... | collective-permute-start | bytes 688136 | tf_op jit(solution)/shard_map/ppermute | solution.py:178
  39.6 13.7 %collective-permute-start.13 = (bf16[448,256]{1,0:T(8,128)(2,1)S(1)}, bf16[448,256]{1,0:T(8,128)(2,1)S(1)}, u32[]{:S(2)}, u32[]{:S(2)}) collective-permute-start(bf16[448,256]{1,0:T(8,128)(2,1)S(1)} %collective-permute-done.11.refs_3_.refs_11_), channel_id=1, source_target_pairs={{0,1},{1,0},{2,3},{3,2},{4,5},{5,4},{6,7},{7,6},{8,9},{9,8},{10,11... | collective-permute-start | bytes 688136 | tf_op jit(solution)/shard_map/ppermute | solution.py:175
  41.8 11.6 %collective-permute-start.12 = (bf16[448,256]{1,0:T(8,128)(2,1)S(1)}, bf16[448,256]{1,0:T(8,128)(2,1)S(1)}, u32[]{:S(2)}, u32[]{:S(2)}) collective-permute-start(bf16[448,256]{1,0:T(8,128)(2,1)S(1)} %collective-permute-done.8.refs_0_.refs_8_), channel_id=1, source_target_pairs={{0,7},{1,2},{2,1},{3,4},{4,3},{5,6},{6,5},{7,0},{8,15},{9,10},{10,... | collective-permute-start | bytes 688136 | tf_op jit(solution)/shard_map/ppermute | solution.py:178
  44.8 14.7 %collective-permute-start.14 = (bf16[5,2,128,128]{3,2,1,0:T(8,128)(2,1)S(1)}, bf16[5,2,128,128]{3,2,1,0:T(8,128)(2,1)S(1)}, u32[]{:S(2)}, u32[]{:S(2)}) collective-permute-start(bf16[5,2,128,128]{3,2,1,0:T(8,128)(2,1)S(1)} %get-tuple-element.14), channel_id=1, source_target_pairs={{0,8},{8,0},{1,9},{9,1},{2,10},{10,2},{3,11},{11,3},{4,12},{12,4},... | collective-permute-start | bytes 983048 | tf_op jit(solution)/shard_map/ppermute | solution.py:181
  54.0 6.5 %collective-permute-start.15 = (bf16[3,2,128,128]{3,2,1,0:T(8,128)(2,1)S(1)}, bf16[3,2,128,128]{3,2,1,0:T(8,128)(2,1)S(1)}, u32[]{:S(2)}, u32[]{:S(2)}) collective-permute-start(bf16[3,2,128,128]{3,2,1,0:T(8,128)(2,1)S(1)} %get-tuple-element.15), channel_id=1, source_target_pairs={{0,8},{8,0},{1,9},{9,1},{2,10},{10,2},{3,11},{11,3},{4,12},{12,4},... | collective-permute-start | bytes 589832 | tf_op jit(solution)/shard_map/ppermute | solution.py:181
  108.4 7.0 %collective-permute-start.16 = (bf16[32,64,128]{2,1,0:T(8,128)(2,1)S(1)}, bf16[32,64,128]{2,1,0:T(8,128)(2,1)S(1)}, u32[]{:S(2)}, u32[]{:S(2)}) collective-permute-start(bf16[32,64,128]{2,1,0:T(8,128)(2,1)S(1)} %all_to_all.11.refs_14_), channel_id=1, source_target_pairs={{0,8},{8,0},{1,9},{9,1},{2,10},{10,2},{3,11},{11,3},{4,12},{12,4},... | collective-permute-start | bytes 1572872 | tf_op jit(solution)/shard_map/ppermute | solution.py:181

commit v12 on v9

--- a/solution.py
+++ b/solution.py
@@ -59,7 +59,7 @@
 
         lane = lax.broadcasted_iota(jnp.int32, (PIECE, TS), 1)
         chosen = lane == first + lax.broadcasted_iota(jnp.int32, (PIECE, TS), 0)
-        for k, (r, c) in enumerate(GETS):
+        for k, (r, c) in enumerate(PAIRS):
             row, column = tile_of(r, core), tile_of(c, half)
             of_row = jnp.sum(jnp.where(chosen, energy(row), 0.0), axis=1, keepdims=True)
             level = jnp.full((PIECE, TS), scale(row) * scale(column), f32)
@@ -72,7 +72,7 @@
     return pl.pallas_call(
         kernel,
         out_shape=(
-            jax.ShapeDtypeStruct((len(GETS) * PIECE, TS), f32),
+            jax.ShapeDtypeStruct((len(PAIRS) * PIECE, TS), f32),
             jax.ShapeDtypeStruct((2 * len(ORDER), TS), f32),
         ),
         in_specs=[in_smem, in_vmem, in_smem, in_smem, in_smem],
@@ -118,22 +118,18 @@
 
 
 def sum_cores(own, received):
-    pairs = sum(a.shape[0] for a in own)
-    rows = WIDTH // NZ
+    count = sum(a.shape[0] for a in own)
 
     def kernel(*refs):
-        out = refs[-1]
-        n = 0
+        parts = []
         for mine, theirs in zip(refs[: len(own)], refs[len(own) : -1]):
-            count = mine.shape[0]
-            total = (mine[...] + theirs[...].astype(f32)).astype(bf16).reshape(count, NZ, rows, TS)
-            for k in range(count):
-                out[:, (n + k) * rows : (n + k + 1) * rows] = total[k]
-            n += count
-
-    return pl.pallas_call(
-        kernel,
-        out_shape=jax.ShapeDtypeStruct((NZ, pairs * rows, TS), bf16),
+            total = (mine[...] + theirs[...].astype(f32)).reshape(-1, NXZ, PIECE, TS)
+            parts += [total[k] for k in range(total.shape[0])]
+        refs[-1][...] = jnp.concatenate(parts, axis=1).astype(bf16)
+
+    return pl.pallas_call(
+        kernel,
+        out_shape=jax.ShapeDtypeStruct((NXZ, count * PIECE, TS), bf16),
         in_specs=[in_vmem] * (2 * len(own)),
         out_specs=in_vmem,
         compiler_params=pltpu.CompilerParams(vmem_limit_bytes=VMEM_LIMIT),
@@ -141,47 +137,41 @@
     )(*own, *received)
 
 
-def sum_z(parts):
-    def kernel(parts_ref, out):
-        me = lax.axis_index("pair")
-        total = jnp.sum(parts_ref[...].astype(f32), axis=0).reshape(len(PAIRS), NX, PIECE, TS)
+def amplitude_sends(parts, denominator):
+    def kernel(parts_ref, denominator_ref, out):
+        me = lax.axis_index("pair")
+        total = jnp.sum(parts_ref[...].astype(f32), axis=0) / denominator_ref[...]
         out[...] = jnp.zeros_like(out)
         for d, (first, second) in SENDS:
-            both = jnp.concatenate([total[first], total[second]], axis=1)
-            out[pl.ds(NX * lax.rem(me + d + NPAIR, NPAIR), NX)] = both.astype(bf16)
-
-    return pl.pallas_call(
-        kernel,
-        out_shape=jax.ShapeDtypeStruct((NPAIR * NX, 2 * PIECE, TS), bf16),
+            both = total[first * PIECE : (second + 1) * PIECE]
+            out[lax.rem(me + d + NPAIR, NPAIR)] = both.astype(bf16)
+
+    return pl.pallas_call(
+        kernel,
+        out_shape=jax.ShapeDtypeStruct((NPAIR, 2 * PIECE, TS), bf16),
+        in_specs=[in_vmem] * 2,
+        out_specs=in_vmem,
+        compiler_params=pltpu.CompilerParams(vmem_limit_bytes=VMEM_LIMIT),
+        name="amplitude_sends",
+    )(parts, denominator)
+
+
+def amplitude_copies(received):
+    rows = len(GETS) * PIECE
+
+    def kernel(received_ref, out):
+        me = lax.axis_index("pair")
+        pieces = [received_ref[lax.rem(me - d + NPAIR, NPAIR)] for d, _ in SENDS]
+        out[...] = jnp.broadcast_to(jnp.concatenate(pieces)[None], out.shape)
+
+    return pl.pallas_call(
+        kernel,
+        out_shape=jax.ShapeDtypeStruct((NXZ, rows, TS), bf16),
         in_specs=[in_vmem],
         out_specs=in_vmem,
         compiler_params=pltpu.CompilerParams(vmem_limit_bytes=VMEM_LIMIT),
-        name="sum_z",
-    )(parts)
-
-
-def amplitude_copies(parts, denominator):
-    rows = len(GETS) * PIECE
-
-    def kernel(parts_ref, denominator_ref, out):
-        me = lax.axis_index("pair")
-        total = jnp.concatenate(
-            [
-                jnp.sum(parts_ref[pl.ds(NX * lax.rem(me - d + NPAIR, NPAIR), NX)].astype(f32), axis=0)
-                for d, _ in SENDS
-            ]
-        )
-        amplitude = (total / denominator_ref[...]).astype(bf16)
-        out[...] = jnp.broadcast_to(amplitude[None], out.shape)
-
-    return pl.pallas_call(
-        kernel,
-        out_shape=jax.ShapeDtypeStruct((NXZ, rows, TS), bf16),
-        in_specs=[in_vmem] * 2,
-        out_specs=in_vmem,
-        compiler_params=pltpu.CompilerParams(vmem_limit_bytes=VMEM_LIMIT),
         name="amplitude_copies",
-    )(parts, denominator)
+    )(received)
 
 
 def gamma_rows(blocks, mine, theirs, scales):
@@ -258,16 +248,12 @@
     )
     block["A", 3] = swap_a(block["B", 2])
     block["B", 3] = swap_b(block["A", 2])
-    parts = lax.all_to_all(summed, "z", 0, 0)
-    parts = lax.all_to_all(sum_z(parts), ("pair", "x"), 0, 0)
-    copies = amplitude_copies(parts, denominator)
-
-    copies, block["A", 3], block["B", 3] = lax.optimization_barrier(
-        (copies, block["A", 3], block["B", 3])
-    )
+    parts = lax.all_to_all(summed, ("z", "x"), 0, 0)
     block["B", 4] = swap_b(block["A", 3])
+    received = lax.all_to_all(amplitude_sends(parts, denominator), "pair", 0, 0)
+    copies = amplitude_copies(received)
+    copies, block["B", 3], block["B", 4] = lax.optimization_barrier((copies, block["B", 3], block["B", 4]))
     mine = lax.all_to_all(copies, ("z", "x"), 0, 0)
-    mine, block["B", 4] = lax.optimization_barrier((mine, block["B", 4]))
     return gamma_rows(block, mine, swap_cores(mine), scales)
 
 

time: 113 us -> 115 us (1.018)
  blocking collectives: 17.2 us -> 35.8 us
  waiting for transfers between devices: 27.4 us -> 13.5 us
  Pallas kernels: 6.69 us -> 4.91 us
    all_to_all x1 -> x2, blocking collectives: 17.2 us -> 35.8 us  [the longest x1 23.5 us: body(): mine = lax.all_to_all(copies, ('z', 'x'), 0, 0)]
    ppermute x4, waiting for transfers between devices: 16 us -> 4.74 us  [swap_b(): return lax.ppermute(x, 'pair', SWAP_B)]
    all_to_all x2 -> x1, waiting for transfers between devices: 8.92 us -> 6.24 us  [body(): parts = lax.all_to_all(summed, ('z', 'x'), 0, 0)]
    all_to_all x2 -> x1, starting transfers between devices: 14.9 us -> 13.3 us  [body(): parts = lax.all_to_all(summed, ('z', 'x'), 0, 0)]
  transfers between devices with their start and end apart: 12 -> 11, of which waited for: 7 -> 5; matrix products, arithmetic and copies ran while one was open for 0% -> 0% of each run, Pallas kernels for 2% -> 2%
where the time goes in v12:
time: 115 us; the launch traced here: 114 us
  starting transfers between devices  55.6 us (48%)
  blocking collectives  35.8 us (31%)
  waiting for transfers between devices  13.5 us (12%)
  Pallas kernels  4.91 us (4%)
  local copies, waits for them, and re-layouts  3.89 us (3%)
    all_to_all x1, blocking collectives, body(): mine = lax.all_to_all(copies, ('z', 'x'), 0, 0)  23.5 us
    ppermute x4, starting transfers between devices, swap_b(): return lax.ppermute(x, 'pair', SWAP_B)  17.4 us
    ppermute x3, starting transfers between devices, swap_cores(): return lax.ppermute(x, 'core', SWAP_CORES)  16.5 us
    all_to_all x1, starting transfers between devices, body(): parts = lax.all_to_all(summed, ('z', 'x'), 0, 0)  13.3 us
    all_to_all x1, blocking collectives, body(): received = lax.all_to_all(amplitude_sends(parts, denominator), 'pair', 0, 0)  12.3 us
    ppermute x3, starting transfers between devices, swap_a(): return lax.ppermute(x, 'pair', SWAP_A)  8.27 us
    all_to_all x1, waiting for transfers between devices, body(): parts = lax.all_to_all(summed, ('z', 'x'), 0, 0)  6.24 us
    ppermute x4, waiting for transfers between devices, swap_b(): return lax.ppermute(x, 'pair', SWAP_B)  4.74 us
  transfers between devices with their start and end apart: 11, of which 5 were waited for; matrix products, arithmetic and copies ran while one was open for 0% of the time, Pallas kernels for 2%

profile of v12, /device:TPU:1, one launch (start us, length us, event | category | flops | bytes accessed | tf_op | source)
XLA Modules:
  0.0 113.8 jit_solution(17323191123888664908)
XLA Ops:
  0.0 0.0 copy-start.7
  0.0 0.0 copy-start.6
  0.0 0.0 copy-start.5
  0.0 6.1 %collective-permute-start.1 = (bf16[896,256]{1,0:T(8,128)(2,1)}, bf16[896,256]{1,0:T(8,128)(2,1)S(1)}, u32[]{:S(2)}, u32[]{:S(2)}) collective-permute-start(bf16[896,256]{1,0:T(8,128)(2,1)} %refs_0_.3), channel_id=1, source_target_pairs={{0,7},{1,2},{2,1},{3,4},{4,3},{5,6},{6,5},{7,0},{8,15},{9,10},{10,... | collective-permute-start | bytes 1376264 | tf_op jit(solution)/shard_map/ppermute | solution.py:225
  6.1 1.9 %collective-permute-start = (bf16[896,256]{1,0:T(8,128)(2,1)}, bf16[896,256]{1,0:T(8,128)(2,1)S(1)}, u32[]{:S(2)}, u32[]{:S(2)}) collective-permute-start(bf16[896,256]{1,0:T(8,128)(2,1)} %refs_0_.3), channel_id=1, source_target_pairs={{0,1},{1,0},{2,3},{3,2},{4,5},{5,4},{6,7},{7,6},{8,9},{9,8},{10,11... | collective-permute-start | bytes 1376264 | tf_op jit(solution)/shard_map/ppermute | solution.py:222
  8.0 0.0 copy-done.7
  8.0 0.0 copy-done.6
  8.0 0.0 copy-done.5
  8.0 0.0 copy-start.2
  8.0 0.9 copy-done.2
  8.9 0.0 copy-start.8
  8.9 0.7 copy-done.8
  9.6 0.7 tables.1
  10.3 0.0 copy-start.3
  10.3 0.6 copy-done.3
  10.9 2.7 %collective-permute-done.1.refs_2_.refs_1_ = bf16[896,256]{1,0:T(8,128)(2,1)S(1)} collective-permute-done((bf16[896,256]{1,0:T(8,128)(2,1)}, bf16[896,256]{1,0:T(8,128)(2,1)S(1)}, u32[]{:S(2)}, u32[]{:S(2)}) %collective-permute-start.1) | collective-permute-done | bytes 458784 | tf_op jit(solution)/shard_map/ppermute | solution.py:225
  13.6 4.1 %collective-permute-start.2 = (bf16[896,256]{1,0:T(8,128)(2,1)S(1)}, bf16[896,256]{1,0:T(8,128)(2,1)S(1)}, u32[]{:S(2)}, u32[]{:S(2)}) collective-permute-start(bf16[896,256]{1,0:T(8,128)(2,1)S(1)} %collective-permute-done.1.refs_2_.refs_1_), channel_id=1, source_target_pairs={{0,1},{1,0},{2,3},{3,2},{4,5},{5,4},{6,7},{7,6},{8,9},{9,8},{10,11... | collective-permute-start | bytes 1376264 | tf_op jit(solution)/shard_map/ppermute | solution.py:222
  17.7 0.0 collective-permute-done.refs_1_.refs_0_
  17.7 4.9 %collective-permute-start.3 = (bf16[896,256]{1,0:T(8,128)(2,1)S(1)}, bf16[896,256]{1,0:T(8,128)(2,1)S(1)}, u32[]{:S(2)}, u32[]{:S(2)}) collective-permute-start(bf16[896,256]{1,0:T(8,128)(2,1)S(1)} %collective-permute-done.refs_1_.refs_0_), channel_id=1, source_target_pairs={{0,7},{1,2},{2,1},{3,4},{4,3},{5,6},{6,5},{7,0},{8,15},{9,10},{10,... | collective-permute-start | bytes 1376264 | tf_op jit(solution)/shard_map/ppermute | solution.py:225
  22.6 0.0 copy-start
  22.6 1.0 copy-done
  23.6 0.6 coulomb_pairs.2
  24.2 4.2 %collective-permute-start.4 = (bf16[3,2,128,128]{3,2,1,0:T(8,128)(2,1)S(1)}, bf16[3,2,128,128]{3,2,1,0:T(8,128)(2,1)S(1)}, u32[]{:S(2)}, u32[]{:S(2)}) collective-permute-start(bf16[3,2,128,128]{3,2,1,0:T(8,128)(2,1)S(1)} %get-tuple-element.25), channel_id=1, source_target_pairs={{0,8},{8,0},{1,9},{9,1},{2,10},{10,2},{3,11},{11,3},{4,12},{12,4},... | collective-permute-start | bytes 589832 | tf_op jit(solution)/shard_map/ppermute | solution.py:228
  28.4 0.0 collective-permute-done.2.refs_2_.refs_3_
  28.4 2.0 %collective-permute-done.3.refs_3_.refs_4_ = bf16[896,256]{1,0:T(8,128)(2,1)S(1)} collective-permute-done((bf16[896,256]{1,0:T(8,128)(2,1)S(1)}, bf16[896,256]{1,0:T(8,128)(2,1)S(1)}, u32[]{:S(2)}, u32[]{:S(2)}) %collective-permute-start.3) | collective-permute-done | bytes 458784 | tf_op jit(solution)/shard_map/ppermute | solution.py:225
  30.4 0.5 coulomb_pairs.3
  30.9 6.0 %collective-permute-start.5 = (bf16[2,2,128,128]{3,2,1,0:T(8,128)(2,1)S(1)}, bf16[2,2,128,128]{3,2,1,0:T(8,128)(2,1)S(1)}, u32[]{:S(2)}, u32[]{:S(2)}) collective-permute-start(bf16[2,2,128,128]{3,2,1,0:T(8,128)(2,1)S(1)} %get-tuple-element.26), channel_id=1, source_target_pairs={{0,8},{8,0},{1,9},{9,1},{2,10},{10,2},{3,11},{11,3},{4,12},{12,4},... | collective-permute-start | bytes 393224 | tf_op jit(solution)/shard_map/ppermute | solution.py:228
  36.8 0.0 collective-permute-done.4.refs_2_
  36.9 1.0 collective-permute-done.5.refs_3_
  37.8 0.8 sum_cores.1
  38.6 2.3 %collective-permute-start.6 = (bf16[896,256]{1,0:T(8,128)(2,1)S(1)}, bf16[896,256]{1,0:T(8,128)(2,1)S(1)}, u32[]{:S(2)}, u32[]{:S(2)}) collective-permute-start(bf16[896,256]{1,0:T(8,128)(2,1)S(1)} %collective-permute-done.3.refs_3_.refs_4_), channel_id=1, source_target_pairs={{0,1},{1,0},{2,3},{3,2},{4,5},{5,4},{6,7},{7,6},{8,9},{9,8},{10,11... | collective-permute-start | bytes 1376264 | tf_op jit(solution)/shard_map/ppermute | solution.py:222
  40.9 13.3 %all-to-all-start = ((bf16[32,40,128]{2,1,0:T(8,128)(2,1)}), bf16[32,40,128]{2,1,0:T(8,128)(2,1)S(1)}, u32[]{:S(2)}, u32[]{:S(2)}) async-start(bf16[32,40,128]{2,1,0:T(8,128)(2,1)} %sum_cores.1), calls=%async_computation | async-start | bytes 655360 | tf_op jit(solution)/shard_map/all_to_all | solution.py:251
  54.2 4.0 %collective-permute-start.7 = (bf16[896,256]{1,0:T(8,128)(2,1)S(1)}, bf16[896,256]{1,0:T(8,128)(2,1)S(1)}, u32[]{:S(2)}, u32[]{:S(2)}) collective-permute-start(bf16[896,256]{1,0:T(8,128)(2,1)S(1)} %collective-permute-done.2.refs_2_.refs_3_), channel_id=1, source_target_pairs={{0,7},{1,2},{2,1},{3,4},{4,3},{5,6},{6,5},{7,0},{8,15},{9,10},{10,... | collective-permute-start | bytes 1376264 | tf_op jit(solution)/shard_map/ppermute | solution.py:225
  58.2 0.0 collective-permute-done.6.refs_5_
  58.2 2.5 %collective-permute-start.8 = (bf16[896,256]{1,0:T(8,128)(2,1)S(1)}, bf16[896,256]{1,0:T(8,128)(2,1)S(1)}, u32[]{:S(2)}, u32[]{:S(2)}) collective-permute-start(bf16[896,256]{1,0:T(8,128)(2,1)S(1)} %collective-permute-done.6.refs_5_), channel_id=1, source_target_pairs={{0,7},{1,2},{2,1},{3,4},{4,3},{5,6},{6,5},{7,0},{8,15},{9,10},{10,... | collective-permute-start | bytes 1376264 | tf_op jit(solution)/shard_map/ppermute | solution.py:225
  60.8 6.2 %all-to-all-done.parts_ref = bf16[32,40,128]{2,1,0:T(8,128)(2,1)S(1)} async-done(((bf16[32,40,128]{2,1,0:T(8,128)(2,1)}), bf16[32,40,128]{2,1,0:T(8,128)(2,1)S(1)}, u32[]{:S(2)}, u32[]{:S(2)}) %all-to-all-start) | async-done | bytes 327712 | tf_op jit(solution)/shard_map/all_to_all | solution.py:251
  67.0 0.0 copy-start.4
  67.0 0.7 copy-done.4
  67.8 12.3 %all_to_all.15.received_ref = bf16[8,16,128]{2,1,0:T(8,128)(2,1)S(1)} all-to-all(bf16[8,16,128]{2,1,0:T(8,128)(2,1)S(1)} %amplitude_sends.1), channel_id=1, replica_groups=mesh['x'=4,'z'=8,'core'=2,'pair'=8] {'pair'}, dimensions={0} | all-to-all | bytes 65536 | tf_op jit(solution)/shard_map/all_to_all | solution.py:253
  80.1 0.1 amplitude_copies.1
  80.2 0.0 copy-start.1
  80.2 0.0 collective-permute-done.7.refs_6_
  80.2 0.0 collective-permute-done.8.refs_7_
  80.2 23.5 %all_to_all.16.refs_8_ = bf16[32,64,128]{2,1,0:T(8,128)(2,1)S(1)} all-to-all(bf16[32,64,128]{2,1,0:T(8,128)(2,1)S(1)} %amplitude_copies.1), channel_id=1, replica_groups=mesh['x'=4,'z'=8,'core'=2,'pair'=8] {'z','x'}, dimensions={0} | all-to-all | bytes 1048576 | tf_op jit(solution)/shard_map/all_to_all | solution.py:256
  103.7 6.4 %collective-permute-start.9 = (bf16[32,64,128]{2,1,0:T(8,128)(2,1)S(1)}, bf16[32,64,128]{2,1,0:T(8,128)(2,1)S(1)}, u32[]{:S(2)}, u32[]{:S(2)}) collective-permute-start(bf16[32,64,128]{2,1,0:T(8,128)(2,1)S(1)} %all_to_all.16.refs_8_), channel_id=1, source_target_pairs={{0,8},{8,0},{1,9},{9,1},{2,10},{10,2},{3,11},{11,3},{4,12},{12,4},... | collective-permute-start | bytes 1572872 | tf_op jit(solution)/shard_map/ppermute | solution.py:228
  110.1 1.5 %collective-permute-done.9.refs_9_ = bf16[32,64,128]{2,1,0:T(8,128)(2,1)S(1)} collective-permute-done((bf16[32,64,128]{2,1,0:T(8,128)(2,1)S(1)}, bf16[32,64,128]{2,1,0:T(8,128)(2,1)S(1)}, u32[]{:S(2)}, u32[]{:S(2)}) %collective-permute-start.9) | collective-permute-done | bytes 524320 | tf_op jit(solution)/shard_map/ppermute | solution.py:228
  111.7 0.0 copy-done.1
  111.7 2.2 %gamma_rows.1 = bf16[896,256]{1,0:T(8,128)(2,1)} custom-call(bf16[896,256]{1,0:T(8,128)(2,1)S(1)} %copy-done.1, bf16[896,256]{1,0:T(8,128)(2,1)S(1)} %collective-permute-done.refs_1_.refs_0_, bf16[896,256]{1,0:T(8,128)(2,1)S(1)} %collective-permute-done.1.refs_2_.refs_1_, bf16[896,256]{1,0:T(8,128)(2,1)S(1)} %collective-permute-done.2.refs_2_.refs_3_, ...), custom_call_target="tpu_custom_call" | custom-call | tf_op jit(solution)/shard_map/gamma_rows/pallas_call | solution.py:209
  (1 shorter events, 0.0 us)
Async XLA Ops:
  0.0 8.0 %copy-start.7 = (s32[16]{0:T(128)S(1)}, s32[16]{0:T(128)}, u32[]{:S(2)}) copy-start(s32[16]{0:T(128)} %virtual_of.1) | copy-start | bytes 196
  0.0 8.0 %copy-start.6 = (s32[16]{0:T(128)S(1)}, s32[16]{0:T(128)}, u32[]{:S(2)}) copy-start(s32[16]{0:T(128)} %occupied_of.1) | copy-start | bytes 196
  0.0 8.0 %copy-start.5 = (f32[64]{0:T(128)S(1)}, f32[64]{0:T(128)}, u32[]{:S(2)}) copy-start(f32[64]{0:T(128)} %occupied.1) | copy-start | bytes 772
  0.0 13.6 %collective-permute-start.1 = (bf16[896,256]{1,0:T(8,128)(2,1)}, bf16[896,256]{1,0:T(8,128)(2,1)S(1)}, u32[]{:S(2)}, u32[]{:S(2)}) collective-permute-start(bf16[896,256]{1,0:T(8,128)(2,1)} %refs_0_.3), channel_id=1, source_target_pairs={{0,7},{1,2},{2,1},{3,4},{4,3},{5,6},{6,5},{7,0},{8,15},{9,10},{10,... | collective-permute-start | bytes 1376264 | tf_op jit(solution)/shard_map/ppermute | solution.py:225
  6.1 11.6 %collective-permute-start = (bf16[896,256]{1,0:T(8,128)(2,1)}, bf16[896,256]{1,0:T(8,128)(2,1)S(1)}, u32[]{:S(2)}, u32[]{:S(2)}) collective-permute-start(bf16[896,256]{1,0:T(8,128)(2,1)} %refs_0_.3), channel_id=1, source_target_pairs={{0,1},{1,0},{2,3},{3,2},{4,5},{5,4},{6,7},{7,6},{8,9},{9,8},{10,11... | collective-permute-start | bytes 1376264 | tf_op jit(solution)/shard_map/ppermute | solution.py:222
  8.0 0.9 copy-start.2
  8.9 0.7 copy-start.8
  10.3 0.6 copy-start.3
  13.6 14.8 %collective-permute-start.2 = (bf16[896,256]{1,0:T(8,128)(2,1)S(1)}, bf16[896,256]{1,0:T(8,128)(2,1)S(1)}, u32[]{:S(2)}, u32[]{:S(2)}) collective-permute-start(bf16[896,256]{1,0:T(8,128)(2,1)S(1)} %collective-permute-done.1.refs_2_.refs_1_), channel_id=1, source_target_pairs={{0,1},{1,0},{2,3},{3,2},{4,5},{5,4},{6,7},{7,6},{8,9},{9,8},{10,11... | collective-permute-start | bytes 1376264 | tf_op jit(solution)/shard_map/ppermute | solution.py:222
  17.7 12.7 %collective-permute-start.3 = (bf16[896,256]{1,0:T(8,128)(2,1)S(1)}, bf16[896,256]{1,0:T(8,128)(2,1)S(1)}, u32[]{:S(2)}, u32[]{:S(2)}) collective-permute-start(bf16[896,256]{1,0:T(8,128)(2,1)S(1)} %collective-permute-done.refs_1_.refs_0_), channel_id=1, source_target_pairs={{0,7},{1,2},{2,1},{3,4},{4,3},{5,6},{6,5},{7,0},{8,15},{9,10},{10,... | collective-permute-start | bytes 1376264 | tf_op jit(solution)/shard_map/ppermute | solution.py:225
  22.6 1.0 copy-start
  24.2 12.7 %collective-permute-start.4 = (bf16[3,2,128,128]{3,2,1,0:T(8,128)(2,1)S(1)}, bf16[3,2,128,128]{3,2,1,0:T(8,128)(2,1)S(1)}, u32[]{:S(2)}, u32[]{:S(2)}) collective-permute-start(bf16[3,2,128,128]{3,2,1,0:T(8,128)(2,1)S(1)} %get-tuple-element.25), channel_id=1, source_target_pairs={{0,8},{8,0},{1,9},{9,1},{2,10},{10,2},{3,11},{11,3},{4,12},{12,4},... | collective-permute-start | bytes 589832 | tf_op jit(solution)/shard_map/ppermute | solution.py:228
  30.9 6.9 %collective-permute-start.5 = (bf16[2,2,128,128]{3,2,1,0:T(8,128)(2,1)S(1)}, bf16[2,2,128,128]{3,2,1,0:T(8,128)(2,1)S(1)}, u32[]{:S(2)}, u32[]{:S(2)}) collective-permute-start(bf16[2,2,128,128]{3,2,1,0:T(8,128)(2,1)S(1)} %get-tuple-element.26), channel_id=1, source_target_pairs={{0,8},{8,0},{1,9},{9,1},{2,10},{10,2},{3,11},{11,3},{4,12},{12,4},... | collective-permute-start | bytes 393224 | tf_op jit(solution)/shard_map/ppermute | solution.py:228
  38.6 19.6 %collective-permute-start.6 = (bf16[896,256]{1,0:T(8,128)(2,1)S(1)}, bf16[896,256]{1,0:T(8,128)(2,1)S(1)}, u32[]{:S(2)}, u32[]{:S(2)}) collective-permute-start(bf16[896,256]{1,0:T(8,128)(2,1)S(1)} %collective-permute-done.3.refs_3_.refs_4_), channel_id=1, source_target_pairs={{0,1},{1,0},{2,3},{3,2},{4,5},{5,4},{6,7},{7,6},{8,9},{9,8},{10,11... | collective-permute-start | bytes 1376264 | tf_op jit(solution)/shard_map/ppermute | solution.py:222
  40.9 26.1 %all-to-all-start = ((bf16[32,40,128]{2,1,0:T(8,128)(2,1)}), bf16[32,40,128]{2,1,0:T(8,128)(2,1)S(1)}, u32[]{:S(2)}, u32[]{:S(2)}) async-start(bf16[32,40,128]{2,1,0:T(8,128)(2,1)} %sum_cores.1), calls=%async_computation | async-start | bytes 655360 | tf_op jit(solution)/shard_map/all_to_all | solution.py:251
  54.2 26.0 %collective-permute-start.7 = (bf16[896,256]{1,0:T(8,128)(2,1)S(1)}, bf16[896,256]{1,0:T(8,128)(2,1)S(1)}, u32[]{:S(2)}, u32[]{:S(2)}) collective-permute-start(bf16[896,256]{1,0:T(8,128)(2,1)S(1)} %collective-permute-done.2.refs_2_.refs_3_), channel_id=1, source_target_pairs={{0,7},{1,2},{2,1},{3,4},{4,3},{5,6},{6,5},{7,0},{8,15},{9,10},{10,... | collective-permute-start | bytes 1376264 | tf_op jit(solution)/shard_map/ppermute | solution.py:225
  58.2 22.0 %collective-permute-start.8 = (bf16[896,256]{1,0:T(8,128)(2,1)S(1)}, bf16[896,256]{1,0:T(8,128)(2,1)S(1)}, u32[]{:S(2)}, u32[]{:S(2)}) collective-permute-start(bf16[896,256]{1,0:T(8,128)(2,1)S(1)} %collective-permute-done.6.refs_5_), channel_id=1, source_target_pairs={{0,7},{1,2},{2,1},{3,4},{4,3},{5,6},{6,5},{7,0},{8,15},{9,10},{10,... | collective-permute-start | bytes 1376264 | tf_op jit(solution)/shard_map/ppermute | solution.py:225
  67.0 0.7 copy-start.4
  80.2 31.5 %copy-start.1 = (bf16[896,256]{1,0:T(8,128)(2,1)S(1)}, bf16[896,256]{1,0:T(8,128)(2,1)}, u32[]{:S(2)}) copy-start(bf16[896,256]{1,0:T(8,128)(2,1)} %refs_0_.3) | copy-start | bytes 1376260
  103.7 7.9 %collective-permute-start.9 = (bf16[32,64,128]{2,1,0:T(8,128)(2,1)S(1)}, bf16[32,64,128]{2,1,0:T(8,128)(2,1)S(1)}, u32[]{:S(2)}, u32[]{:S(2)}) collective-permute-start(bf16[32,64,128]{2,1,0:T(8,128)(2,1)S(1)} %all_to_all.16.refs_8_), channel_id=1, source_target_pairs={{0,8},{8,0},{1,9},{9,1},{2,10},{10,2},{3,11},{11,3},{4,12},{12,4},... | collective-permute-start | bytes 1572872 | tf_op jit(solution)/shard_map/ppermute | solution.py:228

commit v13 on v9

--- a/solution.py
+++ b/solution.py
@@ -259,15 +259,12 @@
     block["A", 3] = swap_a(block["B", 2])
     block["B", 3] = swap_b(block["A", 2])
     parts = lax.all_to_all(summed, "z", 0, 0)
-    parts = lax.all_to_all(sum_z(parts), ("pair", "x"), 0, 0)
+    slots = sum_z(parts)
+    parts = lax.all_to_all(slots, ("pair", "x"), 0, 0)
+    block["B", 4] = swap_b(block["A", 3])
     copies = amplitude_copies(parts, denominator)
-
-    copies, block["A", 3], block["B", 3] = lax.optimization_barrier(
-        (copies, block["A", 3], block["B", 3])
-    )
-    block["B", 4] = swap_b(block["A", 3])
+    copies, block["B", 3], block["B", 4] = lax.optimization_barrier((copies, block["B", 3], block["B", 4]))
     mine = lax.all_to_all(copies, ("z", "x"), 0, 0)
-    mine, block["B", 4] = lax.optimization_barrier((mine, block["B", 4]))
     return gamma_rows(block, mine, swap_cores(mine), scales)
 
 

time: 113 us -> 114 us (level)
  blocking collectives: 17.2 us -> 37.2 us
  waiting for transfers between devices: 27.4 us -> 14.3 us
  starting transfers between devices: 56.3 us -> 53.2 us
  Pallas kernels: 6.69 us -> 4.87 us
  local copies, waits for them, and re-layouts: 4.35 us -> 3.16 us
    all_to_all x1 -> x2, blocking collectives: 17.2 us -> 37.2 us  [the longest x1 21.6 us: body(): mine = lax.all_to_all(copies, ('z', 'x'), 0, 0)]
    ppermute x4, waiting for transfers between devices: 16 us -> 4.73 us  [swap_b(): return lax.ppermute(x, 'pair', SWAP_B)]
    all_to_all x1 -> x0, starting transfers between devices: 4.03 us -> none  [body(): mine = lax.all_to_all(copies, ('z', 'x'), 0, 0)]
    unnamed x18, local copies, waits for them, and re-layouts: 4.35 us -> 3.16 us
  transfers between devices with their start and end apart: 12 -> 11, of which waited for: 7 -> 5; matrix products, arithmetic and copies ran while one was open for 0% -> 0% of each run, Pallas kernels for 2% -> 2%
where the time goes in v13:
time: 114 us; the launch traced here: 113 us
  starting transfers between devices  53.2 us (47%)
  blocking collectives  37.2 us (33%)
  waiting for transfers between devices  14.3 us (13%)
  Pallas kernels  4.87 us (4%)
  local copies, waits for them, and re-layouts  3.16 us (3%)
    all_to_all x1, blocking collectives, body(): mine = lax.all_to_all(copies, ('z', 'x'), 0, 0)  21.6 us
    ppermute x4, starting transfers between devices, swap_b(): return lax.ppermute(x, 'pair', SWAP_B)  17.4 us
    ppermute x3, starting transfers between devices, swap_cores(): return lax.ppermute(x, 'core', SWAP_CORES)  17.1 us
    all_to_all x1, blocking collectives, body(): parts = lax.all_to_all(slots, ('pair', 'x'), 0, 0)  15.6 us
    all_to_all x1, starting transfers between devices, body(): parts = lax.all_to_all(summed, 'z', 0, 0)  10.5 us
    ppermute x3, starting transfers between devices, swap_a(): return lax.ppermute(x, 'pair', SWAP_A)  8.27 us
    all_to_all x1, waiting for transfers between devices, body(): parts = lax.all_to_all(summed, 'z', 0, 0)  7.13 us
    ppermute x4, waiting for transfers between devices, swap_b(): return lax.ppermute(x, 'pair', SWAP_B)  4.73 us
  transfers between devices with their start and end apart: 11, of which 5 were waited for; matrix products, arithmetic and copies ran while one was open for 0% of the time, Pallas kernels for 2%

profile of v13, /device:TPU:1, one launch (start us, length us, event | category | flops | bytes accessed | tf_op | source)
XLA Modules:
  0.0 113.1 jit_solution(6268689544736526942)
XLA Ops:
  0.0 0.0 copy-start.7
  0.0 0.0 copy-start.6
  0.0 0.0 copy-start.5
  0.0 6.1 %collective-permute-start.1 = (bf16[896,256]{1,0:T(8,128)(2,1)}, bf16[896,256]{1,0:T(8,128)(2,1)S(1)}, u32[]{:S(2)}, u32[]{:S(2)}) collective-permute-start(bf16[896,256]{1,0:T(8,128)(2,1)} %refs_0_.3), channel_id=1, source_target_pairs={{0,7},{1,2},{2,1},{3,4},{4,3},{5,6},{6,5},{7,0},{8,15},{9,10},{10,... | collective-permute-start | bytes 1376264 | tf_op jit(solution)/shard_map/ppermute | solution.py:235
  6.1 1.9 %collective-permute-start = (bf16[896,256]{1,0:T(8,128)(2,1)}, bf16[896,256]{1,0:T(8,128)(2,1)S(1)}, u32[]{:S(2)}, u32[]{:S(2)}) collective-permute-start(bf16[896,256]{1,0:T(8,128)(2,1)} %refs_0_.3), channel_id=1, source_target_pairs={{0,1},{1,0},{2,3},{3,2},{4,5},{5,4},{6,7},{7,6},{8,9},{9,8},{10,11... | collective-permute-start | bytes 1376264 | tf_op jit(solution)/shard_map/ppermute | solution.py:232
  8.0 0.0 copy-done.7
  8.0 0.0 copy-done.6
  8.0 0.0 copy-done.5
  8.0 0.0 copy-start.2
  8.0 0.9 copy-done.2
  8.9 0.0 copy-start.8
  8.9 0.7 copy-done.8
  9.6 0.7 tables.1
  10.3 0.0 copy-start.3
  10.3 0.6 copy-done.3
  10.9 2.7 %collective-permute-done.1.refs_2_.refs_1_ = bf16[896,256]{1,0:T(8,128)(2,1)S(1)} collective-permute-done((bf16[896,256]{1,0:T(8,128)(2,1)}, bf16[896,256]{1,0:T(8,128)(2,1)S(1)}, u32[]{:S(2)}, u32[]{:S(2)}) %collective-permute-start.1) | collective-permute-done | bytes 458784 | tf_op jit(solution)/shard_map/ppermute | solution.py:235
  13.6 4.1 %collective-permute-start.2 = (bf16[896,256]{1,0:T(8,128)(2,1)S(1)}, bf16[896,256]{1,0:T(8,128)(2,1)S(1)}, u32[]{:S(2)}, u32[]{:S(2)}) collective-permute-start(bf16[896,256]{1,0:T(8,128)(2,1)S(1)} %collective-permute-done.1.refs_2_.refs_1_), channel_id=1, source_target_pairs={{0,1},{1,0},{2,3},{3,2},{4,5},{5,4},{6,7},{7,6},{8,9},{9,8},{10,11... | collective-permute-start | bytes 1376264 | tf_op jit(solution)/shard_map/ppermute | solution.py:232
  17.7 0.0 collective-permute-done.refs_1_.refs_0_
  17.7 4.9 %collective-permute-start.3 = (bf16[896,256]{1,0:T(8,128)(2,1)S(1)}, bf16[896,256]{1,0:T(8,128)(2,1)S(1)}, u32[]{:S(2)}, u32[]{:S(2)}) collective-permute-start(bf16[896,256]{1,0:T(8,128)(2,1)S(1)} %collective-permute-done.refs_1_.refs_0_), channel_id=1, source_target_pairs={{0,7},{1,2},{2,1},{3,4},{4,3},{5,6},{6,5},{7,0},{8,15},{9,10},{10,... | collective-permute-start | bytes 1376264 | tf_op jit(solution)/shard_map/ppermute | solution.py:235
  22.6 0.0 copy-start
  22.6 1.0 copy-done
  23.6 0.6 coulomb_pairs.2
  24.2 4.2 %collective-permute-start.4 = (bf16[3,2,128,128]{3,2,1,0:T(8,128)(2,1)S(1)}, bf16[3,2,128,128]{3,2,1,0:T(8,128)(2,1)S(1)}, u32[]{:S(2)}, u32[]{:S(2)}) collective-permute-start(bf16[3,2,128,128]{3,2,1,0:T(8,128)(2,1)S(1)} %get-tuple-element.25), channel_id=1, source_target_pairs={{0,8},{8,0},{1,9},{9,1},{2,10},{10,2},{3,11},{11,3},{4,12},{12,4},... | collective-permute-start | bytes 589832 | tf_op jit(solution)/shard_map/ppermute | solution.py:238
  28.4 0.0 collective-permute-done.2.refs_2_.refs_3_
  28.4 2.0 %collective-permute-done.3.refs_3_.refs_4_ = bf16[896,256]{1,0:T(8,128)(2,1)S(1)} collective-permute-done((bf16[896,256]{1,0:T(8,128)(2,1)S(1)}, bf16[896,256]{1,0:T(8,128)(2,1)S(1)}, u32[]{:S(2)}, u32[]{:S(2)}) %collective-permute-start.3) | collective-permute-done | bytes 458784 | tf_op jit(solution)/shard_map/ppermute | solution.py:235
  30.4 0.5 coulomb_pairs.3
  30.9 6.0 %collective-permute-start.5 = (bf16[2,2,128,128]{3,2,1,0:T(8,128)(2,1)S(1)}, bf16[2,2,128,128]{3,2,1,0:T(8,128)(2,1)S(1)}, u32[]{:S(2)}, u32[]{:S(2)}) collective-permute-start(bf16[2,2,128,128]{3,2,1,0:T(8,128)(2,1)S(1)} %get-tuple-element.26), channel_id=1, source_target_pairs={{0,8},{8,0},{1,9},{9,1},{2,10},{10,2},{3,11},{11,3},{4,12},{12,4},... | collective-permute-start | bytes 393224 | tf_op jit(solution)/shard_map/ppermute | solution.py:238
  36.8 0.0 collective-permute-done.4.refs_2_
  36.9 1.0 collective-permute-done.5.refs_3_
  37.8 0.8 sum_cores.1
  38.6 2.3 %collective-permute-start.6 = (bf16[896,256]{1,0:T(8,128)(2,1)S(1)}, bf16[896,256]{1,0:T(8,128)(2,1)S(1)}, u32[]{:S(2)}, u32[]{:S(2)}) collective-permute-start(bf16[896,256]{1,0:T(8,128)(2,1)S(1)} %collective-permute-done.3.refs_3_.refs_4_), channel_id=1, source_target_pairs={{0,1},{1,0},{2,3},{3,2},{4,5},{5,4},{6,7},{7,6},{8,9},{9,8},{10,11... | collective-permute-start | bytes 1376264 | tf_op jit(solution)/shard_map/ppermute | solution.py:232
  40.9 10.5 %all-to-all-start = ((bf16[8,160,128]{2,1,0:T(8,128)(2,1)}), bf16[8,160,128]{2,1,0:T(8,128)(2,1)S(1)}, u32[]{:S(2)}, u32[]{:S(2)}) async-start(bf16[8,160,128]{2,1,0:T(8,128)(2,1)} %sum_cores.1), calls=%async_computation | async-start | bytes 655360 | tf_op jit(solution)/shard_map/all_to_all | solution.py:261
  51.4 4.0 %collective-permute-start.7 = (bf16[896,256]{1,0:T(8,128)(2,1)S(1)}, bf16[896,256]{1,0:T(8,128)(2,1)S(1)}, u32[]{:S(2)}, u32[]{:S(2)}) collective-permute-start(bf16[896,256]{1,0:T(8,128)(2,1)S(1)} %collective-permute-done.2.refs_2_.refs_3_), channel_id=1, source_target_pairs={{0,7},{1,2},{2,1},{3,4},{4,3},{5,6},{6,5},{7,0},{8,15},{9,10},{10,... | collective-permute-start | bytes 1376264 | tf_op jit(solution)/shard_map/ppermute | solution.py:235
  55.4 0.0 collective-permute-done.6.refs_5_
  55.4 2.5 %collective-permute-start.8 = (bf16[896,256]{1,0:T(8,128)(2,1)S(1)}, bf16[896,256]{1,0:T(8,128)(2,1)S(1)}, u32[]{:S(2)}, u32[]{:S(2)}) collective-permute-start(bf16[896,256]{1,0:T(8,128)(2,1)S(1)} %collective-permute-done.6.refs_5_), channel_id=1, source_target_pairs={{0,7},{1,2},{2,1},{3,4},{4,3},{5,6},{6,5},{7,0},{8,15},{9,10},{10,... | collective-permute-start | bytes 1376264 | tf_op jit(solution)/shard_map/ppermute | solution.py:235
  57.9 7.1 %all-to-all-done.parts_ref = bf16[8,160,128]{2,1,0:T(8,128)(2,1)S(1)} async-done(((bf16[8,160,128]{2,1,0:T(8,128)(2,1)}), bf16[8,160,128]{2,1,0:T(8,128)(2,1)S(1)}, u32[]{:S(2)}, u32[]{:S(2)}) %all-to-all-start) | async-done | bytes 327712 | tf_op jit(solution)/shard_map/all_to_all | solution.py:261
  65.0 0.1 sum_z.1
  65.1 0.0 copy-start.4
  65.1 15.6 %all_to_all.15.parts_ref = bf16[32,16,128]{2,1,0:T(8,128)(2,1)S(1)} all-to-all(bf16[32,16,128]{2,1,0:T(8,128)(2,1)S(1)} %sum_z.1), channel_id=1, replica_groups=mesh['x'=4,'z'=8,'core'=2,'pair'=8] {'pair','x'}, dimensions={0} | all-to-all | bytes 262144 | tf_op jit(solution)/shard_map/all_to_all | solution.py:263
  80.7 0.0 copy-done.4
  80.7 0.1 amplitude_copies.1
  80.8 0.0 copy-start.1
  80.8 0.0 collective-permute-done.7.refs_6_
  80.8 0.0 collective-permute-done.8.refs_7_
  80.8 21.6 %all_to_all.16.refs_8_ = bf16[32,64,128]{2,1,0:T(8,128)(2,1)S(1)} all-to-all(bf16[32,64,128]{2,1,0:T(8,128)(2,1)S(1)} %amplitude_copies.1), channel_id=1, replica_groups=mesh['x'=4,'z'=8,'core'=2,'pair'=8] {'z','x'}, dimensions={0} | all-to-all | bytes 1048576 | tf_op jit(solution)/shard_map/all_to_all | solution.py:267
  102.4 6.9 %collective-permute-start.9 = (bf16[32,64,128]{2,1,0:T(8,128)(2,1)S(1)}, bf16[32,64,128]{2,1,0:T(8,128)(2,1)S(1)}, u32[]{:S(2)}, u32[]{:S(2)}) collective-permute-start(bf16[32,64,128]{2,1,0:T(8,128)(2,1)S(1)} %all_to_all.16.refs_8_), channel_id=1, source_target_pairs={{0,8},{8,0},{1,9},{9,1},{2,10},{10,2},{3,11},{11,3},{4,12},{12,4},... | collective-permute-start | bytes 1572872 | tf_op jit(solution)/shard_map/ppermute | solution.py:238
  109.4 1.5 %collective-permute-done.9.refs_9_ = bf16[32,64,128]{2,1,0:T(8,128)(2,1)S(1)} collective-permute-done((bf16[32,64,128]{2,1,0:T(8,128)(2,1)S(1)}, bf16[32,64,128]{2,1,0:T(8,128)(2,1)S(1)}, u32[]{:S(2)}, u32[]{:S(2)}) %collective-permute-start.9) | collective-permute-done | bytes 524320 | tf_op jit(solution)/shard_map/ppermute | solution.py:238
  110.9 0.0 copy-done.1
  110.9 2.2 %gamma_rows.1 = bf16[896,256]{1,0:T(8,128)(2,1)} custom-call(bf16[896,256]{1,0:T(8,128)(2,1)S(1)} %copy-done.1, bf16[896,256]{1,0:T(8,128)(2,1)S(1)} %collective-permute-done.refs_1_.refs_0_, bf16[896,256]{1,0:T(8,128)(2,1)S(1)} %collective-permute-done.1.refs_2_.refs_1_, bf16[896,256]{1,0:T(8,128)(2,1)S(1)} %collective-permute-done.2.refs_2_.refs_3_, ...), custom_call_target="tpu_custom_call" | custom-call | tf_op jit(solution)/shard_map/gamma_rows/pallas_call | solution.py:219
Async XLA Ops:
  0.0 8.0 %copy-start.7 = (s32[16]{0:T(128)S(1)}, s32[16]{0:T(128)}, u32[]{:S(2)}) copy-start(s32[16]{0:T(128)} %virtual_of.1) | copy-start | bytes 196
  0.0 8.0 %copy-start.6 = (s32[16]{0:T(128)S(1)}, s32[16]{0:T(128)}, u32[]{:S(2)}) copy-start(s32[16]{0:T(128)} %occupied_of.1) | copy-start | bytes 196
  0.0 8.0 %copy-start.5 = (f32[64]{0:T(128)S(1)}, f32[64]{0:T(128)}, u32[]{:S(2)}) copy-start(f32[64]{0:T(128)} %occupied.1) | copy-start | bytes 772
  0.0 13.6 %collective-permute-start.1 = (bf16[896,256]{1,0:T(8,128)(2,1)}, bf16[896,256]{1,0:T(8,128)(2,1)S(1)}, u32[]{:S(2)}, u32[]{:S(2)}) collective-permute-start(bf16[896,256]{1,0:T(8,128)(2,1)} %refs_0_.3), channel_id=1, source_target_pairs={{0,7},{1,2},{2,1},{3,4},{4,3},{5,6},{6,5},{7,0},{8,15},{9,10},{10,... | collective-permute-start | bytes 1376264 | tf_op jit(solution)/shard_map/ppermute | solution.py:235
  6.1 11.6 %collective-permute-start = (bf16[896,256]{1,0:T(8,128)(2,1)}, bf16[896,256]{1,0:T(8,128)(2,1)S(1)}, u32[]{:S(2)}, u32[]{:S(2)}) collective-permute-start(bf16[896,256]{1,0:T(8,128)(2,1)} %refs_0_.3), channel_id=1, source_target_pairs={{0,1},{1,0},{2,3},{3,2},{4,5},{5,4},{6,7},{7,6},{8,9},{9,8},{10,11... | collective-permute-start | bytes 1376264 | tf_op jit(solution)/shard_map/ppermute | solution.py:232
  8.0 0.9 copy-start.2
  8.9 0.7 copy-start.8
  10.3 0.6 copy-start.3
  13.6 14.8 %collective-permute-start.2 = (bf16[896,256]{1,0:T(8,128)(2,1)S(1)}, bf16[896,256]{1,0:T(8,128)(2,1)S(1)}, u32[]{:S(2)}, u32[]{:S(2)}) collective-permute-start(bf16[896,256]{1,0:T(8,128)(2,1)S(1)} %collective-permute-done.1.refs_2_.refs_1_), channel_id=1, source_target_pairs={{0,1},{1,0},{2,3},{3,2},{4,5},{5,4},{6,7},{7,6},{8,9},{9,8},{10,11... | collective-permute-start | bytes 1376264 | tf_op jit(solution)/shard_map/ppermute | solution.py:232
  17.7 12.7 %collective-permute-start.3 = (bf16[896,256]{1,0:T(8,128)(2,1)S(1)}, bf16[896,256]{1,0:T(8,128)(2,1)S(1)}, u32[]{:S(2)}, u32[]{:S(2)}) collective-permute-start(bf16[896,256]{1,0:T(8,128)(2,1)S(1)} %collective-permute-done.refs_1_.refs_0_), channel_id=1, source_target_pairs={{0,7},{1,2},{2,1},{3,4},{4,3},{5,6},{6,5},{7,0},{8,15},{9,10},{10,... | collective-permute-start | bytes 1376264 | tf_op jit(solution)/shard_map/ppermute | solution.py:235
  22.6 1.0 copy-start
  24.2 12.7 %collective-permute-start.4 = (bf16[3,2,128,128]{3,2,1,0:T(8,128)(2,1)S(1)}, bf16[3,2,128,128]{3,2,1,0:T(8,128)(2,1)S(1)}, u32[]{:S(2)}, u32[]{:S(2)}) collective-permute-start(bf16[3,2,128,128]{3,2,1,0:T(8,128)(2,1)S(1)} %get-tuple-element.25), channel_id=1, source_target_pairs={{0,8},{8,0},{1,9},{9,1},{2,10},{10,2},{3,11},{11,3},{4,12},{12,4},... | collective-permute-start | bytes 589832 | tf_op jit(solution)/shard_map/ppermute | solution.py:238
  30.9 6.9 %collective-permute-start.5 = (bf16[2,2,128,128]{3,2,1,0:T(8,128)(2,1)S(1)}, bf16[2,2,128,128]{3,2,1,0:T(8,128)(2,1)S(1)}, u32[]{:S(2)}, u32[]{:S(2)}) collective-permute-start(bf16[2,2,128,128]{3,2,1,0:T(8,128)(2,1)S(1)} %get-tuple-element.26), channel_id=1, source_target_pairs={{0,8},{8,0},{1,9},{9,1},{2,10},{10,2},{3,11},{11,3},{4,12},{12,4},... | collective-permute-start | bytes 393224 | tf_op jit(solution)/shard_map/ppermute | solution.py:238
  38.6 16.8 %collective-permute-start.6 = (bf16[896,256]{1,0:T(8,128)(2,1)S(1)}, bf16[896,256]{1,0:T(8,128)(2,1)S(1)}, u32[]{:S(2)}, u32[]{:S(2)}) collective-permute-start(bf16[896,256]{1,0:T(8,128)(2,1)S(1)} %collective-permute-done.3.refs_3_.refs_4_), channel_id=1, source_target_pairs={{0,1},{1,0},{2,3},{3,2},{4,5},{5,4},{6,7},{7,6},{8,9},{9,8},{10,11... | collective-permute-start | bytes 1376264 | tf_op jit(solution)/shard_map/ppermute | solution.py:232
  40.9 24.1 %all-to-all-start = ((bf16[8,160,128]{2,1,0:T(8,128)(2,1)}), bf16[8,160,128]{2,1,0:T(8,128)(2,1)S(1)}, u32[]{:S(2)}, u32[]{:S(2)}) async-start(bf16[8,160,128]{2,1,0:T(8,128)(2,1)} %sum_cores.1), calls=%async_computation | async-start | bytes 655360 | tf_op jit(solution)/shard_map/all_to_all | solution.py:261
  51.4 29.4 %collective-permute-start.7 = (bf16[896,256]{1,0:T(8,128)(2,1)S(1)}, bf16[896,256]{1,0:T(8,128)(2,1)S(1)}, u32[]{:S(2)}, u32[]{:S(2)}) collective-permute-start(bf16[896,256]{1,0:T(8,128)(2,1)S(1)} %collective-permute-done.2.refs_2_.refs_3_), channel_id=1, source_target_pairs={{0,7},{1,2},{2,1},{3,4},{4,3},{5,6},{6,5},{7,0},{8,15},{9,10},{10,... | collective-permute-start | bytes 1376264 | tf_op jit(solution)/shard_map/ppermute | solution.py:235
  55.4 25.5 %collective-permute-start.8 = (bf16[896,256]{1,0:T(8,128)(2,1)S(1)}, bf16[896,256]{1,0:T(8,128)(2,1)S(1)}, u32[]{:S(2)}, u32[]{:S(2)}) collective-permute-start(bf16[896,256]{1,0:T(8,128)(2,1)S(1)} %collective-permute-done.6.refs_5_), channel_id=1, source_target_pairs={{0,7},{1,2},{2,1},{3,4},{4,3},{5,6},{6,5},{7,0},{8,15},{9,10},{10,... | collective-permute-start | bytes 1376264 | tf_op jit(solution)/shard_map/ppermute | solution.py:235
  65.1 15.7 %copy-start.4 = (f32[64,128]{1,0:T(8,128)S(1)}, f32[64,128]{1,0:T(8,128)}, u32[]{:S(2)}) copy-start(f32[64,128]{1,0:T(8,128)} %copy-done.3) | copy-start | bytes 98308
  80.8 30.1 %copy-start.1 = (bf16[896,256]{1,0:T(8,128)(2,1)S(1)}, bf16[896,256]{1,0:T(8,128)(2,1)}, u32[]{:S(2)}) copy-start(bf16[896,256]{1,0:T(8,128)(2,1)} %refs_0_.3) | copy-start | bytes 1376260
  102.4 8.5 %collective-permute-start.9 = (bf16[32,64,128]{2,1,0:T(8,128)(2,1)S(1)}, bf16[32,64,128]{2,1,0:T(8,128)(2,1)S(1)}, u32[]{:S(2)}, u32[]{:S(2)}) collective-permute-start(bf16[32,64,128]{2,1,0:T(8,128)(2,1)S(1)} %all_to_all.16.refs_8_), channel_id=1, source_target_pairs={{0,8},{8,0},{1,9},{9,1},{2,10},{10,2},{3,11},{11,3},{4,12},{12,4},... | collective-permute-start | bytes 1572872 | tf_op jit(solution)/shard_map/ppermute | solution.py:238

commit v14 on v13

--- a/solution.py
+++ b/solution.py
@@ -82,14 +82,24 @@
     )(occupied_energy, virtual_energy.reshape(VT, TS), tile_occupied, tile_virtual, tile_exponent)
 
 
-def coulomb_pairs(blocks, pairs):
+def coulomb_pairs(blocks, pairs, joined=None):
     names = [
         n for n in HELD if n in {held_name(d, parity) for pair in pairs for d in pair for parity in (0, 1)}
     ]
+    counts = [len(blocks[n]) for n in names]
+    rows = sum(part.shape[0] for part in blocks[names[0]])
+    most = max(counts)
+    height = rows // most
 
     def kernel(*refs):
-        block = dict(zip(names, refs))
-        own, other = refs[len(names) :]
+        parts = {}
+        given = list(refs[: sum(counts)])
+        for n, count in zip(names, counts):
+            mine, given = given[:count], given[count:]
+            parts[n] = mine if count == most else [
+                mine[0].at[i * height : (i + 1) * height] for i in range(most)
+            ]
+        own, other, *whole = refs[sum(counts) :]
         core = lax.axis_index("core")
         me = lax.axis_index("pair")
         for parity in (0, 1):
@@ -97,24 +107,33 @@
             @pl.when(lax.rem(me, 2) == parity)
             def _(parity=parity):
                 for k, (r, c) in enumerate(pairs):
-                    rows, columns = block[held_name(r, parity)], block[held_name(c, parity)]
                     for out, part in ((own, core), (other, 1 - core)):
-                        left = rows[:, pl.ds(pl.multiple_of(part * TS, TS), TS)]
-                        product = lax.dot_general(
-                            left, columns[...], (((0,), (0,)), ((), ())), preferred_element_type=f32
-                        )
+                        place = pl.ds(pl.multiple_of(part * TS, TS), TS)
+                        total = None
+                        for left, right in zip(parts[held_name(r, parity)], parts[held_name(c, parity)]):
+                            term = lax.dot_general(
+                                left[:, place], right[...], (((0,), (0,)), ((), ())), preferred_element_type=f32
+                            )
+                            total = term if total is None else total + term
                         for h in (0, 1):
-                            out[k, h] = product[:, h * TS : (h + 1) * TS].astype(out.dtype)
+                            out[k, h] = total[:, h * TS : (h + 1) * TS].astype(out.dtype)
+
+        for ref in whole:
+            for i, part in enumerate(parts[joined]):
+                ref[i * height : (i + 1) * height] = part[...]
 
     shape = (len(pairs), 2, TS, TS)
-    return pl.pallas_call(
-        kernel,
-        out_shape=(jax.ShapeDtypeStruct(shape, f32), jax.ShapeDtypeStruct(shape, bf16)),
-        in_specs=[in_vmem] * len(names),
-        out_specs=(in_vmem, in_vmem),
+    out_shape = [jax.ShapeDtypeStruct(shape, f32), jax.ShapeDtypeStruct(shape, bf16)]
+    if joined is not None:
+        out_shape.append(jax.ShapeDtypeStruct((rows, WIDTH), bf16))
+    return pl.pallas_call(
+        kernel,
+        out_shape=out_shape,
+        in_specs=[in_vmem] * sum(counts),
+        out_specs=[in_vmem] * len(out_shape),
         compiler_params=pltpu.CompilerParams(vmem_limit_bytes=VMEM_LIMIT),
         name="coulomb_pairs",
-    )(*[blocks[n] for n in names])
+    )(*[part for n in names for part in blocks[n]])
 
 
 def sum_cores(own, received):
@@ -185,11 +204,16 @@
 
 
 def gamma_rows(blocks, mine, theirs, scales):
-    rows, width = blocks[0].shape
+    rows, width = blocks[0][0].shape
+    counts = [len(blocks[n]) for n in HELD]
 
     def kernel(*refs):
-        block = refs[: len(HELD)]
-        own, other, scale, out, matrix = refs[len(HELD) :]
+        given = list(refs[: sum(counts)])
+        block = []
+        for count in counts:
+            block.append(given[:count])
+            given = given[count:]
+        own, other, scale, out, matrix = refs[sum(counts) :]
         core = lax.axis_index("core")
         even = lax.rem(lax.axis_index("pair"), 2) == 0
         for pair in range(0, len(ORDER), 2):
@@ -211,20 +235,22 @@
 
         for start in range(0, rows, ROWS):
             total = None
-            for i, ref in enumerate(block):
-                term = jnp.dot(ref[start : start + ROWS], matrix[i], preferred_element_type=f32)
+            for i, parts in enumerate(block):
+                part, offset = divmod(start, rows // len(parts))
+                left = parts[part][offset : offset + ROWS]
+                term = jnp.dot(left, matrix[i], preferred_element_type=f32)
                 total = term if total is None else total + term
             out[start : start + ROWS] = total.astype(bf16)
 
     return pl.pallas_call(
         kernel,
         out_shape=jax.ShapeDtypeStruct((rows, width), bf16),
-        in_specs=[in_vmem] * (len(HELD) + 3),
+        in_specs=[in_vmem] * (sum(counts) + 3),
         out_specs=in_vmem,
         scratch_shapes=[pltpu.VMEM((len(HELD), WIDTH, WIDTH), bf16)],
         compiler_params=pltpu.CompilerParams(vmem_limit_bytes=VMEM_LIMIT),
         name="gamma_rows",
-    )(*[blocks[n] for n in HELD], mine, theirs, scales)
+    )(*[part for n in HELD for part in blocks[n]], mine, theirs, scales)
 
 
 def body(three_index, *energies):
@@ -237,34 +263,36 @@
     def swap_cores(x):
         return lax.ppermute(x, "core", SWAP_CORES)
 
-    block = {0: three_index}
-    block["A", 1] = swap_a(block[0])
-    block["B", 1] = swap_b(block[0])
+    half = three_index.shape[0] // 2
+    block = {0: [three_index]}
+    block["A", 1] = [swap_a(three_index)]
+    block["B", 1] = [swap_b(three_index[:half]), swap_b(three_index[half:])]
     denominator, scales = tables(*energies)
-    block["B", 1], denominator, scales = lax.optimization_barrier(
-        (block["B", 1], denominator, scales)
+    block["B", 1][1], denominator, scales = lax.optimization_barrier(
+        (block["B", 1][1], denominator, scales)
     )
-    block["B", 2] = swap_b(block["A", 1])
-    block["A", 2] = swap_a(block["B", 1])
+    block["B", 2] = [swap_b(block["A", 1][0])]
+    block["A", 2] = [swap_a(part) for part in block["B", 1]]
 
     early, other_early = coulomb_pairs(block, EARLY)
     got_early = swap_cores(other_early)
-    late, other_late = coulomb_pairs(block, LATE)
+    late, other_late, joined = coulomb_pairs(block, LATE, ("A", 2))
     got_late = swap_cores(other_late)
     summed = sum_cores((early, late), (got_early, got_late))
-
-    summed, block["A", 2], block["B", 2] = lax.optimization_barrier(
-        (summed, block["A", 2], block["B", 2])
-    )
-    block["A", 3] = swap_a(block["B", 2])
-    block["B", 3] = swap_b(block["A", 2])
+    block["A", 2] = [joined]
+
+    b2, a2 = block["B", 2][0], joined
+    summed, b2, a2 = lax.optimization_barrier((summed, b2, a2))
+    a3, b3 = swap_a(b2), swap_b(a2)
     parts = lax.all_to_all(summed, "z", 0, 0)
-    slots = sum_z(parts)
-    parts = lax.all_to_all(slots, ("pair", "x"), 0, 0)
-    block["B", 4] = swap_b(block["A", 3])
+    parts = lax.all_to_all(sum_z(parts), ("pair", "x"), 0, 0)
     copies = amplitude_copies(parts, denominator)
-    copies, block["B", 3], block["B", 4] = lax.optimization_barrier((copies, block["B", 3], block["B", 4]))
+
+    copies, a3, b3 = lax.optimization_barrier((copies, a3, b3))
+    b4 = swap_b(a3)
     mine = lax.all_to_all(copies, ("z", "x"), 0, 0)
+    mine, b4 = lax.optimization_barrier((mine, b4))
+    block.update({("B", 2): [b2], ("A", 2): [a2], ("A", 3): [a3], ("B", 3): [b3], ("B", 4): [b4]})
     return gamma_rows(block, mine, swap_cores(mine), scales)
 
 

time: 114 us -> 111 us (0.974)
  blocking collectives: 37.2 us -> 15.9 us
  waiting for transfers between devices: 14.3 us -> 23.2 us
  starting transfers between devices: 53.2 us -> 61.5 us
  Pallas kernels: 4.87 us -> 6.76 us
    all_to_all x2 -> x1, blocking collectives: 37.2 us -> 15.9 us  [body(): parts = lax.all_to_all(sum_z(parts), ('pair', 'x'), 0, 0)]
    ppermute x4 -> x5, waiting for transfers between devices: 4.73 us -> 10.6 us  [swap_b(): return lax.ppermute(x, 'pair', SWAP_B)]
    ppermute x3 -> x4, starting transfers between devices: 8.27 us -> 12.4 us  [swap_a(): return lax.ppermute(x, 'pair', SWAP_A)]
    all_to_all x0 -> x1, starting transfers between devices: none -> 3.89 us  [body(): mine = lax.all_to_all(copies, ('z', 'x'), 0, 0)]
    ppermute x4 -> x5, starting transfers between devices: 17.4 us -> 19.4 us  [swap_b(): return lax.ppermute(x, 'pair', SWAP_B)]
    ppermute x3 -> x4, waiting for transfers between devices: 0.01 us -> 1.4 us  [swap_a(): return lax.ppermute(x, 'pair', SWAP_A)]
    unnamed x18 -> x16, local copies, waits for them, and re-layouts: 3.16 us -> 1.82 us
    ppermute x3, starting transfers between devices: 17.1 us -> 15.8 us  [swap_cores(): return lax.ppermute(x, 'core', SWAP_CORES)]
  transfers between devices with their start and end apart: 11 -> 14, of which waited for: 5 -> 6; matrix products, arithmetic and copies ran while one was open for 0% -> 1% of each run, Pallas kernels for 2% -> 3%
where the time goes in v14:
time: 111 us
  starting transfers between devices  61.5 us (55%)
  waiting for transfers between devices  23.2 us (21%)
  blocking collectives  15.9 us (14%)
  Pallas kernels  6.76 us (6%)
  local copies, waits for them, and re-layouts  2.9 us (3%)
    ppermute x5, starting transfers between devices, swap_b(): return lax.ppermute(x, 'pair', SWAP_B)  19.4 us
    all_to_all x1, blocking collectives, body(): parts = lax.all_to_all(sum_z(parts), ('pair', 'x'), 0, 0)  15.9 us
    ppermute x3, starting transfers between devices, swap_cores(): return lax.ppermute(x, 'core', SWAP_CORES)  15.8 us
    ppermute x4, starting transfers between devices, swap_a(): return lax.ppermute(x, 'pair', SWAP_A)  12.4 us
    ppermute x5, waiting for transfers between devices, swap_b(): return lax.ppermute(x, 'pair', SWAP_B)  10.6 us
    all_to_all x1, starting transfers between devices, body(): parts = lax.all_to_all(summed, 'z', 0, 0)  10 us
    all_to_all x1, waiting for transfers between devices, body(): parts = lax.all_to_all(summed, 'z', 0, 0)  8.06 us
    all_to_all x1, starting transfers between devices, body(): mine = lax.all_to_all(copies, ('z', 'x'), 0, 0)  3.89 us
  transfers between devices with their start and end apart: 14, of which 6 were waited for; matrix products, arithmetic and copies ran while one was open for 1% of the time, Pallas kernels for 3%

profile of v14, /device:TPU:1, one launch (start us, length us, event | category | flops | bytes accessed | tf_op | source)
XLA Modules:
  0.0 110.6 jit_solution(16185301928960263154)
XLA Ops:
  0.0 0.0 copy-start
  0.0 0.0 copy-start.3
  0.0 4.2 %collective-permute-start = (bf16[896,256]{1,0:T(8,128)(2,1)}, bf16[896,256]{1,0:T(8,128)(2,1)S(1)}, u32[]{:S(2)}, u32[]{:S(2)}) collective-permute-start(bf16[896,256]{1,0:T(8,128)(2,1)} %refs_0_.3), channel_id=1, source_target_pairs={{0,1},{1,0},{2,3},{3,2},{4,5},{5,4},{6,7},{7,6},{8,9},{9,8},{10,11... | collective-permute-start | bytes 1376264 | tf_op jit(solution)/shard_map/ppermute | solution.py:258
  4.2 1.1 fusion
  5.2 4.9 %collective-permute-start.2 = (bf16[448,256]{1,0:T(8,128)(2,1)S(1)}, bf16[448,256]{1,0:T(8,128)(2,1)S(1)}, u32[]{:S(2)}, u32[]{:S(2)}) collective-permute-start(bf16[448,256]{1,0:T(8,128)(2,1)S(1)} %get-tuple-element.41), channel_id=1, source_target_pairs={{0,7},{1,2},{2,1},{3,4},{4,3},{5,6},{6,5},{7,0},{8,15},{9,10},{10,... | collective-permute-start | bytes 688136 | tf_op jit(solution)/shard_map/ppermute | solution.py:261
  10.1 0.0 copy-start.7
  10.1 0.0 copy-start.4
  10.2 0.0 copy-start.5
  10.2 0.0 copy-start.6
  10.2 2.1 %collective-permute-start.1 = (bf16[448,256]{1,0:T(8,128)(2,1)S(1)}, bf16[448,256]{1,0:T(8,128)(2,1)S(1)}, u32[]{:S(2)}, u32[]{:S(2)}) collective-permute-start(bf16[448,256]{1,0:T(8,128)(2,1)S(1)} %get-tuple-element.42), channel_id=1, source_target_pairs={{0,7},{1,2},{2,1},{3,4},{4,3},{5,6},{6,5},{7,0},{8,15},{9,10},{10,... | collective-permute-start | bytes 688136 | tf_op jit(solution)/shard_map/ppermute | solution.py:261
  12.2 0.0 collective-permute-done.refs_1_.refs_0_
  12.2 7.3 %collective-permute-start.5 = (bf16[896,256]{1,0:T(8,128)(2,1)S(1)}, bf16[896,256]{1,0:T(8,128)(2,1)S(1)}, u32[]{:S(2)}, u32[]{:S(2)}) collective-permute-start(bf16[896,256]{1,0:T(8,128)(2,1)S(1)} %collective-permute-done.refs_1_.refs_0_), channel_id=1, source_target_pairs={{0,7},{1,2},{2,1},{3,4},{4,3},{5,6},{6,5},{7,0},{8,15},{9,10},{10,... | collective-permute-start | bytes 1376264 | tf_op jit(solution)/shard_map/ppermute | solution.py:261
  19.5 0.0 copy-done.3
  19.5 0.0 copy-done.7
  19.6 0.0 copy-done.4
  19.6 0.0 copy-done.5
  19.6 0.0 copy-done.6
  19.6 0.7 tables.1
  20.3 0.0 collective-permute-done.2.refs_3_.refs_2_
  20.3 1.9 %collective-permute-start.4 = (bf16[448,256]{1,0:T(8,128)(2,1)S(1)}, bf16[448,256]{1,0:T(8,128)(2,1)S(1)}, u32[]{:S(2)}, u32[]{:S(2)}) collective-permute-start(bf16[448,256]{1,0:T(8,128)(2,1)S(1)} %collective-permute-done.2.refs_3_.refs_2_), channel_id=1, source_target_pairs={{0,1},{1,0},{2,3},{3,2},{4,5},{5,4},{6,7},{7,6},{8,9},{9,8},{10,11... | collective-permute-start | bytes 688136 | tf_op jit(solution)/shard_map/ppermute | solution.py:258
  22.2 0.0 collective-permute-done.1.refs_2_.refs_1_
  22.3 3.4 %collective-permute-start.3 = (bf16[448,256]{1,0:T(8,128)(2,1)S(1)}, bf16[448,256]{1,0:T(8,128)(2,1)S(1)}, u32[]{:S(2)}, u32[]{:S(2)}) collective-permute-start(bf16[448,256]{1,0:T(8,128)(2,1)S(1)} %collective-permute-done.1.refs_2_.refs_1_), channel_id=1, source_target_pairs={{0,1},{1,0},{2,3},{3,2},{4,5},{5,4},{6,7},{7,6},{8,9},{9,8},{10,11... | collective-permute-start | bytes 688136 | tf_op jit(solution)/shard_map/ppermute | solution.py:258
  25.6 0.0 copy-done
  25.6 0.6 coulomb_pairs.2
  26.3 4.7 %collective-permute-start.6 = (bf16[3,2,128,128]{3,2,1,0:T(8,128)(2,1)S(1)}, bf16[3,2,128,128]{3,2,1,0:T(8,128)(2,1)S(1)}, u32[]{:S(2)}, u32[]{:S(2)}) collective-permute-start(bf16[3,2,128,128]{3,2,1,0:T(8,128)(2,1)S(1)} %get-tuple-element.28), channel_id=1, source_target_pairs={{0,8},{8,0},{1,9},{9,1},{2,10},{10,2},{3,11},{11,3},{4,12},{12,4},... | collective-permute-start | bytes 589832 | tf_op jit(solution)/shard_map/ppermute | solution.py:264
  31.0 0.0 collective-permute-done.4.refs_4_
  31.0 1.4 %collective-permute-done.3.refs_3_ = bf16[448,256]{1,0:T(8,128)(2,1)S(1)} collective-permute-done((bf16[448,256]{1,0:T(8,128)(2,1)S(1)}, bf16[448,256]{1,0:T(8,128)(2,1)S(1)}, u32[]{:S(2)}, u32[]{:S(2)}) %collective-permute-start.3) | collective-permute-done | bytes 229408 | tf_op jit(solution)/shard_map/ppermute | solution.py:258
  32.4 0.0 collective-permute-done.5.refs_5_
  32.4 0.5 coulomb_pairs.3
  32.9 4.7 %collective-permute-start.7 = (bf16[2,2,128,128]{3,2,1,0:T(8,128)(2,1)S(1)}, bf16[2,2,128,128]{3,2,1,0:T(8,128)(2,1)S(1)}, u32[]{:S(2)}, u32[]{:S(2)}) collective-permute-start(bf16[2,2,128,128]{3,2,1,0:T(8,128)(2,1)S(1)} %get-tuple-element.29), channel_id=1, source_target_pairs={{0,8},{8,0},{1,9},{9,1},{2,10},{10,2},{3,11},{11,3},{4,12},{12,4},... | collective-permute-start | bytes 393224 | tf_op jit(solution)/shard_map/ppermute | solution.py:264
  37.6 0.0 collective-permute-done.6.refs_2_
  37.6 1.0 collective-permute-done.7.refs_3_
  38.6 0.8 sum_cores.1
  39.3 10.0 %all-to-all-start = ((bf16[8,160,128]{2,1,0:T(8,128)(2,1)}), bf16[8,160,128]{2,1,0:T(8,128)(2,1)S(1)}, u32[]{:S(2)}, u32[]{:S(2)}) async-start(bf16[8,160,128]{2,1,0:T(8,128)(2,1)} %sum_cores.1), calls=%async_computation | async-start | bytes 655360 | tf_op jit(solution)/shard_map/all_to_all | solution.py:287
  49.4 2.6 %collective-permute-start.9 = (bf16[896,256]{1,0:T(8,128)(2,1)S(1)}, bf16[896,256]{1,0:T(8,128)(2,1)S(1)}, u32[]{:S(2)}, u32[]{:S(2)}) collective-permute-start(bf16[896,256]{1,0:T(8,128)(2,1)S(1)} %get-tuple-element.31.refs_4_), channel_id=1, source_target_pairs={{0,7},{1,2},{2,1},{3,4},{4,3},{5,6},{6,5},{7,0},{8,15},{9,10},{10,... | collective-permute-start | bytes 1376264 | tf_op jit(solution)/shard_map/ppermute | solution.py:261
  52.0 3.0 %collective-permute-start.8 = (bf16[896,256]{1,0:T(8,128)(2,1)S(1)}, bf16[896,256]{1,0:T(8,128)(2,1)}, u32[]{:S(2)}, u32[]{:S(2)}) collective-permute-start(bf16[896,256]{1,0:T(8,128)(2,1)S(1)} %collective-permute-done.5.refs_5_), channel_id=1, source_target_pairs={{0,1},{1,0},{2,3},{3,2},{4,5},{5,4},{6,7},{7,6},{8,9},{9,8},{10,11... | collective-permute-start | bytes 1376264 | tf_op jit(solution)/shard_map/ppermute | solution.py:258
  54.9 8.1 %all-to-all-done.parts_ref = bf16[8,160,128]{2,1,0:T(8,128)(2,1)S(1)} async-done(((bf16[8,160,128]{2,1,0:T(8,128)(2,1)}), bf16[8,160,128]{2,1,0:T(8,128)(2,1)S(1)}, u32[]{:S(2)}, u32[]{:S(2)}) %all-to-all-start) | async-done | bytes 327712 | tf_op jit(solution)/shard_map/all_to_all | solution.py:287
  63.0 0.1 sum_z.1
  63.1 15.9 %all_to_all.15.parts_ref = bf16[32,16,128]{2,1,0:T(8,128)(2,1)S(1)} all-to-all(bf16[32,16,128]{2,1,0:T(8,128)(2,1)S(1)} %sum_z.1), channel_id=1, replica_groups=mesh['x'=4,'z'=8,'core'=2,'pair'=8] {'pair','x'}, dimensions={0} | all-to-all | bytes 262144 | tf_op jit(solution)/shard_map/all_to_all | solution.py:288
  79.0 0.9 amplitude_copies.1
  79.9 0.0 collective-permute-done.9.refs_7_
  79.9 0.0 collective-permute-done.8.refs_6_
  79.9 3.9 %all-to-all-start.2 = ((bf16[32,64,128]{2,1,0:T(8,128)(2,1)}), bf16[32,64,128]{2,1,0:T(8,128)(2,1)S(1)}, u32[]{:S(2)}, u32[]{:S(2)}) async-start(bf16[32,64,128]{2,1,0:T(8,128)(2,1)} %amplitude_copies.1), calls=%async_computation.2 | async-start | bytes 1048576 | tf_op jit(solution)/shard_map/all_to_all | solution.py:293
  83.8 2.6 %collective-permute-start.10 = (bf16[896,256]{1,0:T(8,128)(2,1)}, bf16[896,256]{1,0:T(8,128)(2,1)S(1)}, u32[]{:S(2)}, u32[]{:S(2)}) collective-permute-start(bf16[896,256]{1,0:T(8,128)(2,1)} %collective-permute-done.8.refs_6_), channel_id=1, source_target_pairs={{0,7},{1,2},{2,1},{3,4},{4,3},{5,6},{6,5},{7,0},{8,15},{9,10},{10,... | collective-permute-start | bytes 1376264 | tf_op jit(solution)/shard_map/ppermute | solution.py:261
  86.4 10.6 %collective-permute-done.10.refs_8_ = bf16[896,256]{1,0:T(8,128)(2,1)S(1)} collective-permute-done((bf16[896,256]{1,0:T(8,128)(2,1)}, bf16[896,256]{1,0:T(8,128)(2,1)S(1)}, u32[]{:S(2)}, u32[]{:S(2)}) %collective-permute-start.10) | collective-permute-done | bytes 458784 | tf_op jit(solution)/shard_map/ppermute | solution.py:261
  97.0 0.0 copy-start.1
  97.0 0.8 copy-done.1
  97.8 0.7 all-to-all-done.2.refs_9_
  98.4 6.4 %collective-permute-start.11 = (bf16[32,64,128]{2,1,0:T(8,128)(2,1)S(1)}, bf16[32,64,128]{2,1,0:T(8,128)(2,1)S(1)}, u32[]{:S(2)}, u32[]{:S(2)}) collective-permute-start(bf16[32,64,128]{2,1,0:T(8,128)(2,1)S(1)} %all-to-all-done.2.refs_9_), channel_id=1, source_target_pairs={{0,8},{8,0},{1,9},{9,1},{2,10},{10,2},{3,11},{11,3},{4,12},{12,4},... | collective-permute-start | bytes 1572872 | tf_op jit(solution)/shard_map/ppermute | solution.py:264
  104.9 1.5 %collective-permute-done.11.refs_10_ = bf16[32,64,128]{2,1,0:T(8,128)(2,1)S(1)} collective-permute-done((bf16[32,64,128]{2,1,0:T(8,128)(2,1)S(1)}, bf16[32,64,128]{2,1,0:T(8,128)(2,1)S(1)}, u32[]{:S(2)}, u32[]{:S(2)}) %collective-permute-start.11) | collective-permute-done | bytes 524320 | tf_op jit(solution)/shard_map/ppermute | solution.py:264
  106.4 0.0 copy-start.2
  106.4 1.0 copy-done.2
  107.4 3.2 %gamma_rows.1 = bf16[896,256]{1,0:T(8,128)(2,1)} custom-call(bf16[896,256]{1,0:T(8,128)(2,1)S(1)} %copy-done, bf16[896,256]{1,0:T(8,128)(2,1)S(1)} %collective-permute-done.refs_1_.refs_0_, bf16[448,256]{1,0:T(8,128)(2,1)S(1)} %collective-permute-done.1.refs_2_.refs_1_, bf16[448,256]{1,0:T(8,128)(2,1)S(1)} %collective-permute-done.2.refs_3_.refs_2_, ...), custom_call_target="tpu_custom_call" | custom-call | tf_op jit(solution)/shard_map/gamma_rows/pallas_call | solution.py:245
Async XLA Ops:
  0.0 25.6 %copy-start = (bf16[896,256]{1,0:T(8,128)(2,1)S(1)}, bf16[896,256]{1,0:T(8,128)(2,1)}, u32[]{:S(2)}) copy-start(bf16[896,256]{1,0:T(8,128)(2,1)} %refs_0_.3) | copy-start | bytes 1376260
  0.0 19.5 %copy-start.3 = (f32[20096]{0:T(1024)S(1)}, f32[20096]{0:T(1024)}, u32[]{:S(2)}) copy-start(f32[20096]{0:T(1024)} %param.8) | copy-start | bytes 241156
  0.0 12.2 %collective-permute-start = (bf16[896,256]{1,0:T(8,128)(2,1)}, bf16[896,256]{1,0:T(8,128)(2,1)S(1)}, u32[]{:S(2)}, u32[]{:S(2)}) collective-permute-start(bf16[896,256]{1,0:T(8,128)(2,1)} %refs_0_.3), channel_id=1, source_target_pairs={{0,1},{1,0},{2,3},{3,2},{4,5},{5,4},{6,7},{7,6},{8,9},{9,8},{10,11... | collective-permute-start | bytes 1376264 | tf_op jit(solution)/shard_map/ppermute | solution.py:258
  5.2 15.1 %collective-permute-start.2 = (bf16[448,256]{1,0:T(8,128)(2,1)S(1)}, bf16[448,256]{1,0:T(8,128)(2,1)S(1)}, u32[]{:S(2)}, u32[]{:S(2)}) collective-permute-start(bf16[448,256]{1,0:T(8,128)(2,1)S(1)} %get-tuple-element.41), channel_id=1, source_target_pairs={{0,7},{1,2},{2,1},{3,4},{4,3},{5,6},{6,5},{7,0},{8,15},{9,10},{10,... | collective-permute-start | bytes 688136 | tf_op jit(solution)/shard_map/ppermute | solution.py:261
  10.1 9.4 %copy-start.7 = (s32[16]{0:T(128)S(1)}, s32[16]{0:T(128)}, u32[]{:S(2)}) copy-start(s32[16]{0:T(128)} %exponent.1) | copy-start | bytes 196
  10.1 9.4 %copy-start.4 = (f32[64]{0:T(128)S(1)}, f32[64]{0:T(128)}, u32[]{:S(2)}) copy-start(f32[64]{0:T(128)} %occupied.1) | copy-start | bytes 772
  10.2 9.4 %copy-start.5 = (s32[16]{0:T(128)S(1)}, s32[16]{0:T(128)}, u32[]{:S(2)}) copy-start(s32[16]{0:T(128)} %occupied_of.1) | copy-start | bytes 196
  10.2 9.4 %copy-start.6 = (s32[16]{0:T(128)S(1)}, s32[16]{0:T(128)}, u32[]{:S(2)}) copy-start(s32[16]{0:T(128)} %virtual_of.1) | copy-start | bytes 196
  10.2 12.1 %collective-permute-start.1 = (bf16[448,256]{1,0:T(8,128)(2,1)S(1)}, bf16[448,256]{1,0:T(8,128)(2,1)S(1)}, u32[]{:S(2)}, u32[]{:S(2)}) collective-permute-start(bf16[448,256]{1,0:T(8,128)(2,1)S(1)} %get-tuple-element.42), channel_id=1, source_target_pairs={{0,7},{1,2},{2,1},{3,4},{4,3},{5,6},{6,5},{7,0},{8,15},{9,10},{10,... | collective-permute-start | bytes 688136 | tf_op jit(solution)/shard_map/ppermute | solution.py:261
  12.2 20.2 %collective-permute-start.5 = (bf16[896,256]{1,0:T(8,128)(2,1)S(1)}, bf16[896,256]{1,0:T(8,128)(2,1)S(1)}, u32[]{:S(2)}, u32[]{:S(2)}) collective-permute-start(bf16[896,256]{1,0:T(8,128)(2,1)S(1)} %collective-permute-done.refs_1_.refs_0_), channel_id=1, source_target_pairs={{0,7},{1,2},{2,1},{3,4},{4,3},{5,6},{6,5},{7,0},{8,15},{9,10},{10,... | collective-permute-start | bytes 1376264 | tf_op jit(solution)/shard_map/ppermute | solution.py:261
  20.3 10.7 %collective-permute-start.4 = (bf16[448,256]{1,0:T(8,128)(2,1)S(1)}, bf16[448,256]{1,0:T(8,128)(2,1)S(1)}, u32[]{:S(2)}, u32[]{:S(2)}) collective-permute-start(bf16[448,256]{1,0:T(8,128)(2,1)S(1)} %collective-permute-done.2.refs_3_.refs_2_), channel_id=1, source_target_pairs={{0,1},{1,0},{2,3},{3,2},{4,5},{5,4},{6,7},{7,6},{8,9},{9,8},{10,11... | collective-permute-start | bytes 688136 | tf_op jit(solution)/shard_map/ppermute | solution.py:258
  22.3 10.1 %collective-permute-start.3 = (bf16[448,256]{1,0:T(8,128)(2,1)S(1)}, bf16[448,256]{1,0:T(8,128)(2,1)S(1)}, u32[]{:S(2)}, u32[]{:S(2)}) collective-permute-start(bf16[448,256]{1,0:T(8,128)(2,1)S(1)} %collective-permute-done.1.refs_2_.refs_1_), channel_id=1, source_target_pairs={{0,1},{1,0},{2,3},{3,2},{4,5},{5,4},{6,7},{7,6},{8,9},{9,8},{10,11... | collective-permute-start | bytes 688136 | tf_op jit(solution)/shard_map/ppermute | solution.py:258
  26.3 11.3 %collective-permute-start.6 = (bf16[3,2,128,128]{3,2,1,0:T(8,128)(2,1)S(1)}, bf16[3,2,128,128]{3,2,1,0:T(8,128)(2,1)S(1)}, u32[]{:S(2)}, u32[]{:S(2)}) collective-permute-start(bf16[3,2,128,128]{3,2,1,0:T(8,128)(2,1)S(1)} %get-tuple-element.28), channel_id=1, source_target_pairs={{0,8},{8,0},{1,9},{9,1},{2,10},{10,2},{3,11},{11,3},{4,12},{12,4},... | collective-permute-start | bytes 589832 | tf_op jit(solution)/shard_map/ppermute | solution.py:264
  32.9 5.6 %collective-permute-start.7 = (bf16[2,2,128,128]{3,2,1,0:T(8,128)(2,1)S(1)}, bf16[2,2,128,128]{3,2,1,0:T(8,128)(2,1)S(1)}, u32[]{:S(2)}, u32[]{:S(2)}) collective-permute-start(bf16[2,2,128,128]{3,2,1,0:T(8,128)(2,1)S(1)} %get-tuple-element.29), channel_id=1, source_target_pairs={{0,8},{8,0},{1,9},{9,1},{2,10},{10,2},{3,11},{11,3},{4,12},{12,4},... | collective-permute-start | bytes 393224 | tf_op jit(solution)/shard_map/ppermute | solution.py:264
  39.3 23.7 %all-to-all-start = ((bf16[8,160,128]{2,1,0:T(8,128)(2,1)}), bf16[8,160,128]{2,1,0:T(8,128)(2,1)S(1)}, u32[]{:S(2)}, u32[]{:S(2)}) async-start(bf16[8,160,128]{2,1,0:T(8,128)(2,1)} %sum_cores.1), calls=%async_computation | async-start | bytes 655360 | tf_op jit(solution)/shard_map/all_to_all | solution.py:287
  49.4 30.5 %collective-permute-start.9 = (bf16[896,256]{1,0:T(8,128)(2,1)S(1)}, bf16[896,256]{1,0:T(8,128)(2,1)S(1)}, u32[]{:S(2)}, u32[]{:S(2)}) collective-permute-start(bf16[896,256]{1,0:T(8,128)(2,1)S(1)} %get-tuple-element.31.refs_4_), channel_id=1, source_target_pairs={{0,7},{1,2},{2,1},{3,4},{4,3},{5,6},{6,5},{7,0},{8,15},{9,10},{10,... | collective-permute-start | bytes 1376264 | tf_op jit(solution)/shard_map/ppermute | solution.py:261
  52.0 27.9 %collective-permute-start.8 = (bf16[896,256]{1,0:T(8,128)(2,1)S(1)}, bf16[896,256]{1,0:T(8,128)(2,1)}, u32[]{:S(2)}, u32[]{:S(2)}) collective-permute-start(bf16[896,256]{1,0:T(8,128)(2,1)S(1)} %collective-permute-done.5.refs_5_), channel_id=1, source_target_pairs={{0,1},{1,0},{2,3},{3,2},{4,5},{5,4},{6,7},{7,6},{8,9},{9,8},{10,11... | collective-permute-start | bytes 1376264 | tf_op jit(solution)/shard_map/ppermute | solution.py:258
  79.9 18.6 %all-to-all-start.2 = ((bf16[32,64,128]{2,1,0:T(8,128)(2,1)}), bf16[32,64,128]{2,1,0:T(8,128)(2,1)S(1)}, u32[]{:S(2)}, u32[]{:S(2)}) async-start(bf16[32,64,128]{2,1,0:T(8,128)(2,1)} %amplitude_copies.1), calls=%async_computation.2 | async-start | bytes 1048576 | tf_op jit(solution)/shard_map/all_to_all | solution.py:293
  83.8 13.2 %collective-permute-start.10 = (bf16[896,256]{1,0:T(8,128)(2,1)}, bf16[896,256]{1,0:T(8,128)(2,1)S(1)}, u32[]{:S(2)}, u32[]{:S(2)}) collective-permute-start(bf16[896,256]{1,0:T(8,128)(2,1)} %collective-permute-done.8.refs_6_), channel_id=1, source_target_pairs={{0,7},{1,2},{2,1},{3,4},{4,3},{5,6},{6,5},{7,0},{8,15},{9,10},{10,... | collective-permute-start | bytes 1376264 | tf_op jit(solution)/shard_map/ppermute | solution.py:261
  97.0 0.8 copy-start.1
  98.4 7.9 %collective-permute-start.11 = (bf16[32,64,128]{2,1,0:T(8,128)(2,1)S(1)}, bf16[32,64,128]{2,1,0:T(8,128)(2,1)S(1)}, u32[]{:S(2)}, u32[]{:S(2)}) collective-permute-start(bf16[32,64,128]{2,1,0:T(8,128)(2,1)S(1)} %all-to-all-done.2.refs_9_), channel_id=1, source_target_pairs={{0,8},{8,0},{1,9},{9,1},{2,10},{10,2},{3,11},{11,3},{4,12},{12,4},... | collective-permute-start | bytes 1572872 | tf_op jit(solution)/shard_map/ppermute | solution.py:264
  106.4 1.0 copy-start.2

commit v15 on v14

--- a/solution.py
+++ b/solution.py
@@ -267,14 +267,12 @@
     block = {0: [three_index]}
     block["A", 1] = [swap_a(three_index)]
     block["B", 1] = [swap_b(three_index[:half]), swap_b(three_index[half:])]
-    denominator, scales = tables(*energies)
-    block["B", 1][1], denominator, scales = lax.optimization_barrier(
-        (block["B", 1][1], denominator, scales)
-    )
     block["B", 2] = [swap_b(block["A", 1][0])]
     block["A", 2] = [swap_a(part) for part in block["B", 1]]
 
     early, other_early = coulomb_pairs(block, EARLY)
+    denominator, scales = tables(*energies)
+    other_early, denominator, scales = lax.optimization_barrier((other_early, denominator, scales))
     got_early = swap_cores(other_early)
     late, other_late, joined = coulomb_pairs(block, LATE, ("A", 2))
     got_late = swap_cores(other_late)
@@ -289,10 +287,10 @@
     copies = amplitude_copies(parts, denominator)
 
     copies, a3, b3 = lax.optimization_barrier((copies, a3, b3))
-    b4 = swap_b(a3)
+    b4 = [swap_b(a3[:half]), swap_a(b3[half:])]
     mine = lax.all_to_all(copies, ("z", "x"), 0, 0)
     mine, b4 = lax.optimization_barrier((mine, b4))
-    block.update({("B", 2): [b2], ("A", 2): [a2], ("A", 3): [a3], ("B", 3): [b3], ("B", 4): [b4]})
+    block.update({("B", 2): [b2], ("A", 2): [a2], ("A", 3): [a3], ("B", 3): [b3], ("B", 4): b4})
     return gamma_rows(block, mine, swap_cores(mine), scales)
 
 

time: 111 us -> 111 us (level)
  waiting for transfers between devices: 23.2 us -> 19.8 us
  starting transfers between devices: 61.5 us -> 64.1 us
    ppermute x5, waiting for transfers between devices: 10.6 us -> 3.96 us  [swap_b(): return lax.ppermute(x, 'pair', SWAP_B)]
    ppermute x4 -> x5, starting transfers between devices: 12.4 us -> 15.1 us  [swap_a(): return lax.ppermute(x, 'pair', SWAP_A)]
    all_to_all x1, waiting for transfers between devices: 0.66 us -> 2.93 us  [body(): mine = lax.all_to_all(copies, ('z', 'x'), 0, 0)]
    ppermute x4 -> x5, waiting for transfers between devices: 1.4 us -> 2.41 us  [swap_a(): return lax.ppermute(x, 'pair', SWAP_A)]
  transfers between devices with their start and end apart: 14 -> 15, of which waited for: 6 -> 6; matrix products, arithmetic and copies ran while one was open for 1% -> 1% of each run, Pallas kernels for 3% -> 3%
where the time goes in v15:
time: 111 us; the launch traced here: 110 us
  starting transfers between devices  64.1 us (58%)
  waiting for transfers between devices  19.8 us (18%)
  blocking collectives  15.9 us (14%)
  Pallas kernels  7.54 us (7%)
  local copies, waits for them, and re-layouts  2.77 us (2%)
    ppermute x5, starting transfers between devices, swap_b(): return lax.ppermute(x, 'pair', SWAP_B)  18.7 us
    ppermute x3, starting transfers between devices, swap_cores(): return lax.ppermute(x, 'core', SWAP_CORES)  16.4 us
    all_to_all x1, blocking collectives, body(): parts = lax.all_to_all(sum_z(parts), ('pair', 'x'), 0, 0)  15.9 us
    ppermute x5, starting transfers between devices, swap_a(): return lax.ppermute(x, 'pair', SWAP_A)  15.1 us
    all_to_all x1, starting transfers between devices, body(): parts = lax.all_to_all(summed, 'z', 0, 0)  10 us
    all_to_all x1, waiting for transfers between devices, body(): parts = lax.all_to_all(summed, 'z', 0, 0)  8.06 us
    ppermute x5, waiting for transfers between devices, swap_b(): return lax.ppermute(x, 'pair', SWAP_B)  3.96 us
    all_to_all x1, starting transfers between devices, body(): mine = lax.all_to_all(copies, ('z', 'x'), 0, 0)  3.89 us
  transfers between devices with their start and end apart: 15, of which 6 were waited for; matrix products, arithmetic and copies ran while one was open for 1% of the time, Pallas kernels for 3%

profile of v15, /device:TPU:1, one launch (start us, length us, event | category | flops | bytes accessed | tf_op | source)
XLA Modules:
  0.0 110.5 jit_solution(11417736193172541585)
XLA Ops:
  0.0 0.0 copy-start
  0.0 0.0 copy-start.3
  0.0 4.2 %collective-permute-start = (bf16[896,256]{1,0:T(8,128)(2,1)}, bf16[896,256]{1,0:T(8,128)(2,1)S(1)}, u32[]{:S(2)}, u32[]{:S(2)}) collective-permute-start(bf16[896,256]{1,0:T(8,128)(2,1)} %refs_0_.3), channel_id=1, source_target_pairs={{0,1},{1,0},{2,3},{3,2},{4,5},{5,4},{6,7},{7,6},{8,9},{9,8},{10,11... | collective-permute-start | bytes 1376264 | tf_op jit(solution)/shard_map/ppermute | solution.py:258
  4.2 1.1 fusion
  5.2 4.9 %collective-permute-start.2 = (bf16[448,256]{1,0:T(8,128)(2,1)S(1)}, bf16[448,256]{1,0:T(8,128)(2,1)S(1)}, u32[]{:S(2)}, u32[]{:S(2)}) collective-permute-start(bf16[448,256]{1,0:T(8,128)(2,1)S(1)} %get-tuple-element.43), channel_id=1, source_target_pairs={{0,7},{1,2},{2,1},{3,4},{4,3},{5,6},{6,5},{7,0},{8,15},{9,10},{10,... | collective-permute-start | bytes 688136 | tf_op jit(solution)/shard_map/ppermute | solution.py:261
  10.1 0.0 copy-start.7
  10.1 0.0 copy-start.4
  10.2 0.0 copy-start.5
  10.2 0.0 copy-start.6
  10.2 2.1 %collective-permute-start.1 = (bf16[448,256]{1,0:T(8,128)(2,1)S(1)}, bf16[448,256]{1,0:T(8,128)(2,1)S(1)}, u32[]{:S(2)}, u32[]{:S(2)}) collective-permute-start(bf16[448,256]{1,0:T(8,128)(2,1)S(1)} %get-tuple-element.44), channel_id=1, source_target_pairs={{0,7},{1,2},{2,1},{3,4},{4,3},{5,6},{6,5},{7,0},{8,15},{9,10},{10,... | collective-permute-start | bytes 688136 | tf_op jit(solution)/shard_map/ppermute | solution.py:261
  12.2 0.0 collective-permute-done.refs_1_.refs_0_
  12.2 7.3 %collective-permute-start.5 = (bf16[896,256]{1,0:T(8,128)(2,1)S(1)}, bf16[896,256]{1,0:T(8,128)(2,1)S(1)}, u32[]{:S(2)}, u32[]{:S(2)}) collective-permute-start(bf16[896,256]{1,0:T(8,128)(2,1)S(1)} %collective-permute-done.refs_1_.refs_0_), channel_id=1, source_target_pairs={{0,7},{1,2},{2,1},{3,4},{4,3},{5,6},{6,5},{7,0},{8,15},{9,10},{10,... | collective-permute-start | bytes 1376264 | tf_op jit(solution)/shard_map/ppermute | solution.py:261
  19.5 0.0 collective-permute-done.2.refs_3_.refs_2_
  19.5 1.9 %collective-permute-start.4 = (bf16[448,256]{1,0:T(8,128)(2,1)S(1)}, bf16[448,256]{1,0:T(8,128)(2,1)S(1)}, u32[]{:S(2)}, u32[]{:S(2)}) collective-permute-start(bf16[448,256]{1,0:T(8,128)(2,1)S(1)} %collective-permute-done.2.refs_3_.refs_2_), channel_id=1, source_target_pairs={{0,1},{1,0},{2,3},{3,2},{4,5},{5,4},{6,7},{7,6},{8,9},{9,8},{10,11... | collective-permute-start | bytes 688136 | tf_op jit(solution)/shard_map/ppermute | solution.py:258
  21.5 0.0 collective-permute-done.1.refs_2_.refs_1_
  21.5 3.4 %collective-permute-start.3 = (bf16[448,256]{1,0:T(8,128)(2,1)S(1)}, bf16[448,256]{1,0:T(8,128)(2,1)S(1)}, u32[]{:S(2)}, u32[]{:S(2)}) collective-permute-start(bf16[448,256]{1,0:T(8,128)(2,1)S(1)} %collective-permute-done.1.refs_2_.refs_1_), channel_id=1, source_target_pairs={{0,1},{1,0},{2,3},{3,2},{4,5},{5,4},{6,7},{7,6},{8,9},{9,8},{10,11... | collective-permute-start | bytes 688136 | tf_op jit(solution)/shard_map/ppermute | solution.py:258
  24.9 0.0 copy-done.3
  24.9 0.0 copy-done.7
  24.9 0.0 copy-done.4
  24.9 0.0 copy-done.5
  24.9 0.0 copy-done.6
  24.9 0.7 tables.1
  25.6 0.0 copy-done
  25.6 0.6 coulomb_pairs.2
  26.3 5.5 %collective-permute-start.6 = (bf16[3,2,128,128]{3,2,1,0:T(8,128)(2,1)S(1)}, bf16[3,2,128,128]{3,2,1,0:T(8,128)(2,1)S(1)}, u32[]{:S(2)}, u32[]{:S(2)}) collective-permute-start(bf16[3,2,128,128]{3,2,1,0:T(8,128)(2,1)S(1)} %get-tuple-element.29), channel_id=1, source_target_pairs={{0,8},{8,0},{1,9},{9,1},{2,10},{10,2},{3,11},{11,3},{4,12},{12,4},... | collective-permute-start | bytes 589832 | tf_op jit(solution)/shard_map/ppermute | solution.py:264
  31.8 0.0 collective-permute-done.4.refs_4_
  31.8 0.0 collective-permute-done.3.refs_3_
  31.8 0.0 collective-permute-done.5.refs_5_
  31.8 1.3 %coulomb_pairs.3 = (f32[2,2,128,128]{3,2,1,0:T(8,128)S(1)}, bf16[2,2,128,128]{3,2,1,0:T(8,128)(2,1)S(1)}, bf16[896,256]{1,0:T(8,128)(2,1)}) custom-call(bf16[896,256]{1,0:T(8,128)(2,1)S(1)} %collective-permute-done.refs_1_.refs_0_, bf16[448,256]{1,0:T(8,128)(2,1)S(1)} %collective-permute-done.1.refs_2_.refs_1_, ...), custom_call_target="tpu_custom_call" | custom-call | tf_op jit(solution)/shard_map/coulomb_pairs/pallas_call | solution.py:129
  33.1 4.5 %collective-permute-start.7 = (bf16[2,2,128,128]{3,2,1,0:T(8,128)(2,1)S(1)}, bf16[2,2,128,128]{3,2,1,0:T(8,128)(2,1)S(1)}, u32[]{:S(2)}, u32[]{:S(2)}) collective-permute-start(bf16[2,2,128,128]{3,2,1,0:T(8,128)(2,1)S(1)} %get-tuple-element.30), channel_id=1, source_target_pairs={{0,8},{8,0},{1,9},{9,1},{2,10},{10,2},{3,11},{11,3},{4,12},{12,4},... | collective-permute-start | bytes 393224 | tf_op jit(solution)/shard_map/ppermute | solution.py:264
  37.6 0.0 collective-permute-done.6.refs_2_
  37.6 1.0 collective-permute-done.7.refs_3_
  38.6 0.8 sum_cores.1
  39.4 10.0 %all-to-all-start = ((bf16[8,160,128]{2,1,0:T(8,128)(2,1)}), bf16[8,160,128]{2,1,0:T(8,128)(2,1)S(1)}, u32[]{:S(2)}, u32[]{:S(2)}) async-start(bf16[8,160,128]{2,1,0:T(8,128)(2,1)} %sum_cores.1), calls=%async_computation | async-start | bytes 655360 | tf_op jit(solution)/shard_map/all_to_all | solution.py:285
  49.4 2.6 %collective-permute-start.9 = (bf16[896,256]{1,0:T(8,128)(2,1)}, bf16[896,256]{1,0:T(8,128)(2,1)S(1)}, u32[]{:S(2)}, u32[]{:S(2)}) collective-permute-start(bf16[896,256]{1,0:T(8,128)(2,1)} %get-tuple-element.32.refs_4_), channel_id=1, source_target_pairs={{0,7},{1,2},{2,1},{3,4},{4,3},{5,6},{6,5},{7,0},{8,15},{9,10},{10,... | collective-permute-start | bytes 1376264 | tf_op jit(solution)/shard_map/ppermute | solution.py:261
  52.0 3.0 %collective-permute-start.8 = (bf16[896,256]{1,0:T(8,128)(2,1)S(1)}, bf16[896,256]{1,0:T(8,128)(2,1)S(1)}, u32[]{:S(2)}, u32[]{:S(2)}) collective-permute-start(bf16[896,256]{1,0:T(8,128)(2,1)S(1)} %collective-permute-done.5.refs_5_), channel_id=1, source_target_pairs={{0,1},{1,0},{2,3},{3,2},{4,5},{5,4},{6,7},{7,6},{8,9},{9,8},{10,11... | collective-permute-start | bytes 1376264 | tf_op jit(solution)/shard_map/ppermute | solution.py:258
  54.9 8.1 %all-to-all-done.parts_ref = bf16[8,160,128]{2,1,0:T(8,128)(2,1)S(1)} async-done(((bf16[8,160,128]{2,1,0:T(8,128)(2,1)}), bf16[8,160,128]{2,1,0:T(8,128)(2,1)S(1)}, u32[]{:S(2)}, u32[]{:S(2)}) %all-to-all-start) | async-done | bytes 327712 | tf_op jit(solution)/shard_map/all_to_all | solution.py:285
  63.0 0.1 sum_z.1
  63.1 15.9 %all_to_all.15.parts_ref = bf16[32,16,128]{2,1,0:T(8,128)(2,1)S(1)} all-to-all(bf16[32,16,128]{2,1,0:T(8,128)(2,1)S(1)} %sum_z.1), channel_id=1, replica_groups=mesh['x'=4,'z'=8,'core'=2,'pair'=8] {'pair','x'}, dimensions={0} | all-to-all | bytes 262144 | tf_op jit(solution)/shard_map/all_to_all | solution.py:286
  79.0 0.9 amplitude_copies.1
  79.8 0.0 collective-permute-done.9.refs_7_
  79.9 0.0 collective-permute-done.8.refs_6_
  79.9 3.9 %all-to-all-start.2 = ((bf16[32,64,128]{2,1,0:T(8,128)(2,1)}), bf16[32,64,128]{2,1,0:T(8,128)(2,1)S(1)}, u32[]{:S(2)}, u32[]{:S(2)}) async-start(bf16[32,64,128]{2,1,0:T(8,128)(2,1)} %amplitude_copies.1), calls=%async_computation.2 | async-start | bytes 1048576 | tf_op jit(solution)/shard_map/all_to_all | solution.py:291
  83.8 2.7 %collective-permute-start.11 = (bf16[448,256]{1,0:T(8,128)(2,1)S(1)}, bf16[448,256]{1,0:T(8,128)(2,1)S(1)}, u32[]{:S(2)}, u32[]{:S(2)}) collective-permute-start(bf16[448,256]{1,0:T(8,128)(2,1)S(1)} %slice.15), channel_id=1, source_target_pairs={{0,1},{1,0},{2,3},{3,2},{4,5},{5,4},{6,7},{7,6},{8,9},{9,8},{10,11... | collective-permute-start | bytes 688136 | tf_op jit(solution)/shard_map/ppermute | solution.py:258
  86.5 1.9 %collective-permute-start.10 = (bf16[448,256]{1,0:T(8,128)(2,1)S(1)}, bf16[448,256]{1,0:T(8,128)(2,1)S(1)}, u32[]{:S(2)}, u32[]{:S(2)}) collective-permute-start(bf16[448,256]{1,0:T(8,128)(2,1)S(1)} %slice.14), channel_id=1, source_target_pairs={{0,7},{1,2},{2,1},{3,4},{4,3},{5,6},{6,5},{7,0},{8,15},{9,10},{10,... | collective-permute-start | bytes 688136 | tf_op jit(solution)/shard_map/ppermute | solution.py:261
  88.5 2.4 %collective-permute-done.11.refs_9_ = bf16[448,256]{1,0:T(8,128)(2,1)S(1)} collective-permute-done((bf16[448,256]{1,0:T(8,128)(2,1)S(1)}, bf16[448,256]{1,0:T(8,128)(2,1)S(1)}, u32[]{:S(2)}, u32[]{:S(2)}) %collective-permute-start.11) | collective-permute-done | bytes 229408 | tf_op jit(solution)/shard_map/ppermute | solution.py:258
  90.9 3.9 %collective-permute-done.10.refs_8_ = bf16[448,256]{1,0:T(8,128)(2,1)S(1)} collective-permute-done((bf16[448,256]{1,0:T(8,128)(2,1)S(1)}, bf16[448,256]{1,0:T(8,128)(2,1)S(1)}, u32[]{:S(2)}, u32[]{:S(2)}) %collective-permute-start.10) | collective-permute-done | bytes 229408 | tf_op jit(solution)/shard_map/ppermute | solution.py:261
  94.8 0.0 copy-start.1
  94.8 0.7 copy-done.1
  95.5 2.9 %all-to-all-done.2.refs_10_ = bf16[32,64,128]{2,1,0:T(8,128)(2,1)S(1)} async-done(((bf16[32,64,128]{2,1,0:T(8,128)(2,1)}), bf16[32,64,128]{2,1,0:T(8,128)(2,1)S(1)}, u32[]{:S(2)}, u32[]{:S(2)}) %all-to-all-start.2) | async-done | bytes 524320 | tf_op jit(solution)/shard_map/all_to_all | solution.py:291
  98.4 6.4 %collective-permute-start.12 = (bf16[32,64,128]{2,1,0:T(8,128)(2,1)S(1)}, bf16[32,64,128]{2,1,0:T(8,128)(2,1)S(1)}, u32[]{:S(2)}, u32[]{:S(2)}) collective-permute-start(bf16[32,64,128]{2,1,0:T(8,128)(2,1)S(1)} %all-to-all-done.2.refs_10_), channel_id=1, source_target_pairs={{0,8},{8,0},{1,9},{9,1},{2,10},{10,2},{3,11},{11,3},{4,12},{12,4},... | collective-permute-start | bytes 1572872 | tf_op jit(solution)/shard_map/ppermute | solution.py:264
  104.9 1.5 %collective-permute-done.12.refs_11_ = bf16[32,64,128]{2,1,0:T(8,128)(2,1)S(1)} collective-permute-done((bf16[32,64,128]{2,1,0:T(8,128)(2,1)S(1)}, bf16[32,64,128]{2,1,0:T(8,128)(2,1)S(1)}, u32[]{:S(2)}, u32[]{:S(2)}) %collective-permute-start.12) | collective-permute-done | bytes 524320 | tf_op jit(solution)/shard_map/ppermute | solution.py:264
  106.4 0.0 copy-start.2
  106.4 0.9 copy-done.2
  107.3 3.2 %gamma_rows.1 = bf16[896,256]{1,0:T(8,128)(2,1)} custom-call(bf16[896,256]{1,0:T(8,128)(2,1)S(1)} %copy-done, bf16[896,256]{1,0:T(8,128)(2,1)S(1)} %collective-permute-done.refs_1_.refs_0_, bf16[448,256]{1,0:T(8,128)(2,1)S(1)} %collective-permute-done.1.refs_2_.refs_1_, bf16[448,256]{1,0:T(8,128)(2,1)S(1)} %collective-permute-done.2.refs_3_.refs_2_, ...), custom_call_target="tpu_custom_call" | custom-call | tf_op jit(solution)/shard_map/gamma_rows/pallas_call | solution.py:245
  (2 shorter events, 0.0 us)
Async XLA Ops:
  0.0 25.6 %copy-start = (bf16[896,256]{1,0:T(8,128)(2,1)S(1)}, bf16[896,256]{1,0:T(8,128)(2,1)}, u32[]{:S(2)}) copy-start(bf16[896,256]{1,0:T(8,128)(2,1)} %refs_0_.3) | copy-start | bytes 1376260
  0.0 24.9 %copy-start.3 = (f32[20096]{0:T(1024)S(1)}, f32[20096]{0:T(1024)}, u32[]{:S(2)}) copy-start(f32[20096]{0:T(1024)} %param.8) | copy-start | bytes 241156
  0.0 12.2 %collective-permute-start = (bf16[896,256]{1,0:T(8,128)(2,1)}, bf16[896,256]{1,0:T(8,128)(2,1)S(1)}, u32[]{:S(2)}, u32[]{:S(2)}) collective-permute-start(bf16[896,256]{1,0:T(8,128)(2,1)} %refs_0_.3), channel_id=1, source_target_pairs={{0,1},{1,0},{2,3},{3,2},{4,5},{5,4},{6,7},{7,6},{8,9},{9,8},{10,11... | collective-permute-start | bytes 1376264 | tf_op jit(solution)/shard_map/ppermute | solution.py:258
  5.2 14.3 %collective-permute-start.2 = (bf16[448,256]{1,0:T(8,128)(2,1)S(1)}, bf16[448,256]{1,0:T(8,128)(2,1)S(1)}, u32[]{:S(2)}, u32[]{:S(2)}) collective-permute-start(bf16[448,256]{1,0:T(8,128)(2,1)S(1)} %get-tuple-element.43), channel_id=1, source_target_pairs={{0,7},{1,2},{2,1},{3,4},{4,3},{5,6},{6,5},{7,0},{8,15},{9,10},{10,... | collective-permute-start | bytes 688136 | tf_op jit(solution)/shard_map/ppermute | solution.py:261
  10.1 14.7 %copy-start.7 = (s32[16]{0:T(128)S(1)}, s32[16]{0:T(128)}, u32[]{:S(2)}) copy-start(s32[16]{0:T(128)} %exponent.1) | copy-start | bytes 196
  10.1 14.7 %copy-start.4 = (f32[64]{0:T(128)S(1)}, f32[64]{0:T(128)}, u32[]{:S(2)}) copy-start(f32[64]{0:T(128)} %occupied.1) | copy-start | bytes 772
  10.2 14.7 %copy-start.5 = (s32[16]{0:T(128)S(1)}, s32[16]{0:T(128)}, u32[]{:S(2)}) copy-start(s32[16]{0:T(128)} %occupied_of.1) | copy-start | bytes 196
  10.2 14.7 %copy-start.6 = (s32[16]{0:T(128)S(1)}, s32[16]{0:T(128)}, u32[]{:S(2)}) copy-start(s32[16]{0:T(128)} %virtual_of.1) | copy-start | bytes 196
  10.2 11.3 %collective-permute-start.1 = (bf16[448,256]{1,0:T(8,128)(2,1)S(1)}, bf16[448,256]{1,0:T(8,128)(2,1)S(1)}, u32[]{:S(2)}, u32[]{:S(2)}) collective-permute-start(bf16[448,256]{1,0:T(8,128)(2,1)S(1)} %get-tuple-element.44), channel_id=1, source_target_pairs={{0,7},{1,2},{2,1},{3,4},{4,3},{5,6},{6,5},{7,0},{8,15},{9,10},{10,... | collective-permute-start | bytes 688136 | tf_op jit(solution)/shard_map/ppermute | solution.py:261
  12.2 19.5 %collective-permute-start.5 = (bf16[896,256]{1,0:T(8,128)(2,1)S(1)}, bf16[896,256]{1,0:T(8,128)(2,1)S(1)}, u32[]{:S(2)}, u32[]{:S(2)}) collective-permute-start(bf16[896,256]{1,0:T(8,128)(2,1)S(1)} %collective-permute-done.refs_1_.refs_0_), channel_id=1, source_target_pairs={{0,7},{1,2},{2,1},{3,4},{4,3},{5,6},{6,5},{7,0},{8,15},{9,10},{10,... | collective-permute-start | bytes 1376264 | tf_op jit(solution)/shard_map/ppermute | solution.py:261
  19.5 12.2 %collective-permute-start.4 = (bf16[448,256]{1,0:T(8,128)(2,1)S(1)}, bf16[448,256]{1,0:T(8,128)(2,1)S(1)}, u32[]{:S(2)}, u32[]{:S(2)}) collective-permute-start(bf16[448,256]{1,0:T(8,128)(2,1)S(1)} %collective-permute-done.2.refs_3_.refs_2_), channel_id=1, source_target_pairs={{0,1},{1,0},{2,3},{3,2},{4,5},{5,4},{6,7},{7,6},{8,9},{9,8},{10,11... | collective-permute-start | bytes 688136 | tf_op jit(solution)/shard_map/ppermute | solution.py:258
  21.5 10.3 %collective-permute-start.3 = (bf16[448,256]{1,0:T(8,128)(2,1)S(1)}, bf16[448,256]{1,0:T(8,128)(2,1)S(1)}, u32[]{:S(2)}, u32[]{:S(2)}) collective-permute-start(bf16[448,256]{1,0:T(8,128)(2,1)S(1)} %collective-permute-done.1.refs_2_.refs_1_), channel_id=1, source_target_pairs={{0,1},{1,0},{2,3},{3,2},{4,5},{5,4},{6,7},{7,6},{8,9},{9,8},{10,11... | collective-permute-start | bytes 688136 | tf_op jit(solution)/shard_map/ppermute | solution.py:258
  26.3 11.3 %collective-permute-start.6 = (bf16[3,2,128,128]{3,2,1,0:T(8,128)(2,1)S(1)}, bf16[3,2,128,128]{3,2,1,0:T(8,128)(2,1)S(1)}, u32[]{:S(2)}, u32[]{:S(2)}) collective-permute-start(bf16[3,2,128,128]{3,2,1,0:T(8,128)(2,1)S(1)} %get-tuple-element.29), channel_id=1, source_target_pairs={{0,8},{8,0},{1,9},{9,1},{2,10},{10,2},{3,11},{11,3},{4,12},{12,4},... | collective-permute-start | bytes 589832 | tf_op jit(solution)/shard_map/ppermute | solution.py:264
  33.1 5.5 %collective-permute-start.7 = (bf16[2,2,128,128]{3,2,1,0:T(8,128)(2,1)S(1)}, bf16[2,2,128,128]{3,2,1,0:T(8,128)(2,1)S(1)}, u32[]{:S(2)}, u32[]{:S(2)}) collective-permute-start(bf16[2,2,128,128]{3,2,1,0:T(8,128)(2,1)S(1)} %get-tuple-element.30), channel_id=1, source_target_pairs={{0,8},{8,0},{1,9},{9,1},{2,10},{10,2},{3,11},{11,3},{4,12},{12,4},... | collective-permute-start | bytes 393224 | tf_op jit(solution)/shard_map/ppermute | solution.py:264
  39.4 23.6 %all-to-all-start = ((bf16[8,160,128]{2,1,0:T(8,128)(2,1)}), bf16[8,160,128]{2,1,0:T(8,128)(2,1)S(1)}, u32[]{:S(2)}, u32[]{:S(2)}) async-start(bf16[8,160,128]{2,1,0:T(8,128)(2,1)} %sum_cores.1), calls=%async_computation | async-start | bytes 655360 | tf_op jit(solution)/shard_map/all_to_all | solution.py:285
  49.4 30.5 %collective-permute-start.9 = (bf16[896,256]{1,0:T(8,128)(2,1)}, bf16[896,256]{1,0:T(8,128)(2,1)S(1)}, u32[]{:S(2)}, u32[]{:S(2)}) collective-permute-start(bf16[896,256]{1,0:T(8,128)(2,1)} %get-tuple-element.32.refs_4_), channel_id=1, source_target_pairs={{0,7},{1,2},{2,1},{3,4},{4,3},{5,6},{6,5},{7,0},{8,15},{9,10},{10,... | collective-permute-start | bytes 1376264 | tf_op jit(solution)/shard_map/ppermute | solution.py:261
  52.0 27.9 %collective-permute-start.8 = (bf16[896,256]{1,0:T(8,128)(2,1)S(1)}, bf16[896,256]{1,0:T(8,128)(2,1)S(1)}, u32[]{:S(2)}, u32[]{:S(2)}) collective-permute-start(bf16[896,256]{1,0:T(8,128)(2,1)S(1)} %collective-permute-done.5.refs_5_), channel_id=1, source_target_pairs={{0,1},{1,0},{2,3},{3,2},{4,5},{5,4},{6,7},{7,6},{8,9},{9,8},{10,11... | collective-permute-start | bytes 1376264 | tf_op jit(solution)/shard_map/ppermute | solution.py:258
  79.9 18.6 %all-to-all-start.2 = ((bf16[32,64,128]{2,1,0:T(8,128)(2,1)}), bf16[32,64,128]{2,1,0:T(8,128)(2,1)S(1)}, u32[]{:S(2)}, u32[]{:S(2)}) async-start(bf16[32,64,128]{2,1,0:T(8,128)(2,1)} %amplitude_copies.1), calls=%async_computation.2 | async-start | bytes 1048576 | tf_op jit(solution)/shard_map/all_to_all | solution.py:291
  83.8 7.1 %collective-permute-start.11 = (bf16[448,256]{1,0:T(8,128)(2,1)S(1)}, bf16[448,256]{1,0:T(8,128)(2,1)S(1)}, u32[]{:S(2)}, u32[]{:S(2)}) collective-permute-start(bf16[448,256]{1,0:T(8,128)(2,1)S(1)} %slice.15), channel_id=1, source_target_pairs={{0,1},{1,0},{2,3},{3,2},{4,5},{5,4},{6,7},{7,6},{8,9},{9,8},{10,11... | collective-permute-start | bytes 688136 | tf_op jit(solution)/shard_map/ppermute | solution.py:258
  86.5 8.3 %collective-permute-start.10 = (bf16[448,256]{1,0:T(8,128)(2,1)S(1)}, bf16[448,256]{1,0:T(8,128)(2,1)S(1)}, u32[]{:S(2)}, u32[]{:S(2)}) collective-permute-start(bf16[448,256]{1,0:T(8,128)(2,1)S(1)} %slice.14), channel_id=1, source_target_pairs={{0,7},{1,2},{2,1},{3,4},{4,3},{5,6},{6,5},{7,0},{8,15},{9,10},{10,... | collective-permute-start | bytes 688136 | tf_op jit(solution)/shard_map/ppermute | solution.py:261
  94.8 0.7 copy-start.1
  98.4 7.9 %collective-permute-start.12 = (bf16[32,64,128]{2,1,0:T(8,128)(2,1)S(1)}, bf16[32,64,128]{2,1,0:T(8,128)(2,1)S(1)}, u32[]{:S(2)}, u32[]{:S(2)}) collective-permute-start(bf16[32,64,128]{2,1,0:T(8,128)(2,1)S(1)} %all-to-all-done.2.refs_10_), channel_id=1, source_target_pairs={{0,8},{8,0},{1,9},{9,1},{2,10},{10,2},{3,11},{11,3},{4,12},{12,4},... | collective-permute-start | bytes 1572872 | tf_op jit(solution)/shard_map/ppermute | solution.py:264
  106.4 0.9 copy-start.2

commit v16 on v15

--- a/solution.py
+++ b/solution.py
@@ -20,9 +20,11 @@
 GETS = tuple((PAIRS[k][0] - d, PAIRS[k][1] - d) for d, pairs in SENDS for k in pairs)
 ORDER = tuple((r, False) if c == 0 else (c, True) for r, c in GETS)
 ROWS = 224
+FETCHED = (("A", 3),)
 VMEM_LIMIT = 12 * 1024 * 1024
 bf16, f32 = jnp.bfloat16, jnp.float32
 in_vmem = pl.BlockSpec(memory_space=pltpu.VMEM)
+anywhere = pl.BlockSpec(memory_space=pl.ANY)
 in_smem = pl.BlockSpec(memory_space=pltpu.SMEM)
 
 
@@ -82,7 +84,7 @@
     )(occupied_energy, virtual_energy.reshape(VT, TS), tile_occupied, tile_virtual, tile_exponent)
 
 
-def coulomb_pairs(blocks, pairs, joined=None):
+def coulomb_pairs(blocks, pairs):
     names = [
         n for n in HELD if n in {held_name(d, parity) for pair in pairs for d in pair for parity in (0, 1)}
     ]
@@ -99,7 +101,7 @@
             parts[n] = mine if count == most else [
                 mine[0].at[i * height : (i + 1) * height] for i in range(most)
             ]
-        own, other, *whole = refs[sum(counts) :]
+        own, other = refs[sum(counts) :]
         core = lax.axis_index("core")
         me = lax.axis_index("pair")
         for parity in (0, 1):
@@ -118,14 +120,8 @@
                         for h in (0, 1):
                             out[k, h] = total[:, h * TS : (h + 1) * TS].astype(out.dtype)
 
-        for ref in whole:
-            for i, part in enumerate(parts[joined]):
-                ref[i * height : (i + 1) * height] = part[...]
-
     shape = (len(pairs), 2, TS, TS)
     out_shape = [jax.ShapeDtypeStruct(shape, f32), jax.ShapeDtypeStruct(shape, bf16)]
-    if joined is not None:
-        out_shape.append(jax.ShapeDtypeStruct((rows, WIDTH), bf16))
     return pl.pallas_call(
         kernel,
         out_shape=out_shape,
@@ -213,7 +209,14 @@
         for count in counts:
             block.append(given[:count])
             given = given[count:]
-        own, other, scale, out, matrix = refs[sum(counts) :]
+        own, other, scale, out, matrix, held, arrived = refs[sum(counts) :]
+        fetches = []
+        for k, name in enumerate(FETCHED):
+            i = HELD.index(name)
+            fetches.append(pltpu.make_async_copy(block[i][0], held.at[k], arrived.at[k]))
+            block[i] = [held.at[k]]
+        for fetch in fetches:
+            fetch.start()
         core = lax.axis_index("core")
         even = lax.rem(lax.axis_index("pair"), 2) == 0
         for pair in range(0, len(ORDER), 2):
@@ -233,6 +236,8 @@
                             tile = tiles[h] * scale[pl.ds(2 * i + part, 1)]
                             matrix[held, place, h * TS : (h + 1) * TS] = tile.astype(bf16)
 
+        for fetch in fetches:
+            fetch.wait()
         for start in range(0, rows, ROWS):
             total = None
             for i, parts in enumerate(block):
@@ -245,9 +250,14 @@
     return pl.pallas_call(
         kernel,
         out_shape=jax.ShapeDtypeStruct((rows, width), bf16),
-        in_specs=[in_vmem] * (sum(counts) + 3),
+        in_specs=[anywhere if n in FETCHED else in_vmem for n in HELD for _ in blocks[n]]
+        + [in_vmem] * 3,
         out_specs=in_vmem,
-        scratch_shapes=[pltpu.VMEM((len(HELD), WIDTH, WIDTH), bf16)],
+        scratch_shapes=[
+            pltpu.VMEM((len(HELD), WIDTH, WIDTH), bf16),
+            pltpu.VMEM((len(FETCHED), rows, width), bf16),
+            pltpu.SemaphoreType.DMA((len(FETCHED),)),
+        ],
         compiler_params=pltpu.CompilerParams(vmem_limit_bytes=VMEM_LIMIT),
         name="gamma_rows",
     )(*[part for n in HELD for part in blocks[n]], mine, theirs, scales)
@@ -274,14 +284,12 @@
     denominator, scales = tables(*energies)
     other_early, denominator, scales = lax.optimization_barrier((other_early, denominator, scales))
     got_early = swap_cores(other_early)
-    late, other_late, joined = coulomb_pairs(block, LATE, ("A", 2))
+    late, other_late = coulomb_pairs(block, LATE)
     got_late = swap_cores(other_late)
     summed = sum_cores((early, late), (got_early, got_late))
-    block["A", 2] = [joined]
-
-    b2, a2 = block["B", 2][0], joined
-    summed, b2, a2 = lax.optimization_barrier((summed, b2, a2))
-    a3, b3 = swap_a(b2), swap_b(a2)
+
+    summed, b2, a2 = lax.optimization_barrier((summed, block["B", 2], block["A", 2]))
+    a3, b3 = swap_a(b2[0]), swap_b(jnp.concatenate(a2))
     parts = lax.all_to_all(summed, "z", 0, 0)
     parts = lax.all_to_all(sum_z(parts), ("pair", "x"), 0, 0)
     copies = amplitude_copies(parts, denominator)
@@ -290,7 +298,7 @@
     b4 = [swap_b(a3[:half]), swap_a(b3[half:])]
     mine = lax.all_to_all(copies, ("z", "x"), 0, 0)
     mine, b4 = lax.optimization_barrier((mine, b4))
-    block.update({("B", 2): [b2], ("A", 2): [a2], ("A", 3): [a3], ("B", 3): [b3], ("B", 4): b4})
+    block.update({("B", 2): b2, ("A", 2): a2, ("A", 3): [a3], ("B", 3): [b3], ("B", 4): b4})
     return gamma_rows(block, mine, swap_cores(mine), scales)
 
 

time: 111 us -> 110 us (level)
  waiting for transfers between devices: 19.8 us -> 18.1 us
  transfers between devices with their start and end apart: 15 -> 15, of which waited for: 6 -> 6; matrix products, arithmetic and copies ran while one was open for 1% -> 3% of each run, Pallas kernels for 3% -> 3%
where the time goes in v16:
time: 110 us
  starting transfers between devices  64.2 us (58%)
  waiting for transfers between devices  18.1 us (16%)
  blocking collectives  15.9 us (14%)
  Pallas kernels  6.69 us (6%)
  local copies, waits for them, and re-layouts  3.71 us (3%)
    ppermute x5, starting transfers between devices, swap_b(): return lax.ppermute(x, 'pair', SWAP_B)  18.7 us
    ppermute x3, starting transfers between devices, swap_cores(): return lax.ppermute(x, 'core', SWAP_CORES)  16.4 us
    all_to_all x1, blocking collectives, body(): parts = lax.all_to_all(sum_z(parts), ('pair', 'x'), 0, 0)  15.9 us
    ppermute x5, starting transfers between devices, swap_a(): return lax.ppermute(x, 'pair', SWAP_A)  15.1 us
    all_to_all x1, starting transfers between devices, body(): parts = lax.all_to_all(summed, 'z', 0, 0)  10 us
    all_to_all x1, waiting for transfers between devices, body(): parts = lax.all_to_all(summed, 'z', 0, 0)  7.26 us
    ppermute x5, waiting for transfers between devices, swap_b(): return lax.ppermute(x, 'pair', SWAP_B)  4.25 us
    all_to_all x1, starting transfers between devices, body(): mine = lax.all_to_all(copies, ('z', 'x'), 0, 0)  3.89 us
  transfers between devices with their start and end apart: 15, of which 6 were waited for; matrix products, arithmetic and copies ran while one was open for 3% of the time, Pallas kernels for 3%

profile of v16, /device:TPU:1, one launch (start us, length us, event | category | flops | bytes accessed | tf_op | source)
XLA Modules:
  0.0 109.6 jit_solution(9280432684952996184)
XLA Ops:
  0.0 0.0 copy-start
  0.0 0.0 copy-start.3
  0.0 4.2 %collective-permute-start = (bf16[896,256]{1,0:T(8,128)(2,1)}, bf16[896,256]{1,0:T(8,128)(2,1)S(1)}, u32[]{:S(2)}, u32[]{:S(2)}) collective-permute-start(bf16[896,256]{1,0:T(8,128)(2,1)} %refs_0_.3), channel_id=1, source_target_pairs={{0,1},{1,0},{2,3},{3,2},{4,5},{5,4},{6,7},{7,6},{8,9},{9,8},{10,11... | collective-permute-start | bytes 1376264 | tf_op jit(solution)/shard_map/ppermute | solution.py:268
  4.2 1.1 fusion
  5.2 4.9 %collective-permute-start.2 = (bf16[448,256]{1,0:T(8,128)(2,1)S(1)}, bf16[448,256]{1,0:T(8,128)(2,1)S(1)}, u32[]{:S(2)}, u32[]{:S(2)}) collective-permute-start(bf16[448,256]{1,0:T(8,128)(2,1)S(1)} %get-tuple-element.43), channel_id=1, source_target_pairs={{0,7},{1,2},{2,1},{3,4},{4,3},{5,6},{6,5},{7,0},{8,15},{9,10},{10,... | collective-permute-start | bytes 688136 | tf_op jit(solution)/shard_map/ppermute | solution.py:271
  10.1 0.0 copy-start.7
  10.1 0.0 copy-start.4
  10.2 0.0 copy-start.5
  10.2 0.0 copy-start.6
  10.2 2.1 %collective-permute-start.1 = (bf16[448,256]{1,0:T(8,128)(2,1)S(1)}, bf16[448,256]{1,0:T(8,128)(2,1)S(1)}, u32[]{:S(2)}, u32[]{:S(2)}) collective-permute-start(bf16[448,256]{1,0:T(8,128)(2,1)S(1)} %get-tuple-element.44), channel_id=1, source_target_pairs={{0,7},{1,2},{2,1},{3,4},{4,3},{5,6},{6,5},{7,0},{8,15},{9,10},{10,... | collective-permute-start | bytes 688136 | tf_op jit(solution)/shard_map/ppermute | solution.py:271
  12.2 0.0 collective-permute-done.refs_1_.refs_0_
  12.2 7.3 %collective-permute-start.5 = (bf16[896,256]{1,0:T(8,128)(2,1)S(1)}, bf16[896,256]{1,0:T(8,128)(2,1)S(1)}, u32[]{:S(2)}, u32[]{:S(2)}) collective-permute-start(bf16[896,256]{1,0:T(8,128)(2,1)S(1)} %collective-permute-done.refs_1_.refs_0_), channel_id=1, source_target_pairs={{0,7},{1,2},{2,1},{3,4},{4,3},{5,6},{6,5},{7,0},{8,15},{9,10},{10,... | collective-permute-start | bytes 1376264 | tf_op jit(solution)/shard_map/ppermute | solution.py:271
  19.5 0.0 collective-permute-done.2.refs_3_.refs_2_
  19.5 1.9 %collective-permute-start.4 = (bf16[448,256]{1,0:T(8,128)(2,1)S(1)}, bf16[448,256]{1,0:T(8,128)(2,1)S(1)}, u32[]{:S(2)}, u32[]{:S(2)}) collective-permute-start(bf16[448,256]{1,0:T(8,128)(2,1)S(1)} %collective-permute-done.2.refs_3_.refs_2_), channel_id=1, source_target_pairs={{0,1},{1,0},{2,3},{3,2},{4,5},{5,4},{6,7},{7,6},{8,9},{9,8},{10,11... | collective-permute-start | bytes 688136 | tf_op jit(solution)/shard_map/ppermute | solution.py:268
  21.5 0.0 collective-permute-done.1.refs_2_.refs_1_
  21.5 3.4 %collective-permute-start.3 = (bf16[448,256]{1,0:T(8,128)(2,1)S(1)}, bf16[448,256]{1,0:T(8,128)(2,1)S(1)}, u32[]{:S(2)}, u32[]{:S(2)}) collective-permute-start(bf16[448,256]{1,0:T(8,128)(2,1)S(1)} %collective-permute-done.1.refs_2_.refs_1_), channel_id=1, source_target_pairs={{0,1},{1,0},{2,3},{3,2},{4,5},{5,4},{6,7},{7,6},{8,9},{9,8},{10,11... | collective-permute-start | bytes 688136 | tf_op jit(solution)/shard_map/ppermute | solution.py:268
  24.9 0.0 copy-done.3
  24.9 0.0 copy-done.7
  24.9 0.0 copy-done.4
  24.9 0.0 copy-done.5
  24.9 0.0 copy-done.6
  24.9 0.7 tables.1
  25.6 0.0 copy-done
  25.6 0.6 coulomb_pairs.2
  26.3 5.5 %collective-permute-start.6 = (bf16[3,2,128,128]{3,2,1,0:T(8,128)(2,1)S(1)}, bf16[3,2,128,128]{3,2,1,0:T(8,128)(2,1)S(1)}, u32[]{:S(2)}, u32[]{:S(2)}) collective-permute-start(bf16[3,2,128,128]{3,2,1,0:T(8,128)(2,1)S(1)} %get-tuple-element.29), channel_id=1, source_target_pairs={{0,8},{8,0},{1,9},{9,1},{2,10},{10,2},{3,11},{11,3},{4,12},{12,4},... | collective-permute-start | bytes 589832 | tf_op jit(solution)/shard_map/ppermute | solution.py:274
  31.8 0.0 collective-permute-done.4.refs_4_.refs_5_
  31.8 0.0 collective-permute-done.3.refs_3_.refs_4_
  31.8 0.0 collective-permute-done.5.refs_5_.refs_6_
  31.8 0.5 coulomb_pairs.3
  32.3 4.5 %collective-permute-start.7 = (bf16[2,2,128,128]{3,2,1,0:T(8,128)(2,1)S(1)}, bf16[2,2,128,128]{3,2,1,0:T(8,128)(2,1)S(1)}, u32[]{:S(2)}, u32[]{:S(2)}) collective-permute-start(bf16[2,2,128,128]{3,2,1,0:T(8,128)(2,1)S(1)} %get-tuple-element.30), channel_id=1, source_target_pairs={{0,8},{8,0},{1,9},{9,1},{2,10},{10,2},{3,11},{11,3},{4,12},{12,4},... | collective-permute-start | bytes 393224 | tf_op jit(solution)/shard_map/ppermute | solution.py:274
  36.8 0.0 collective-permute-done.6.refs_2_
  36.8 1.0 collective-permute-done.7.refs_3_
  37.8 0.8 sum_cores.1
  38.6 10.0 %all-to-all-start = ((bf16[8,160,128]{2,1,0:T(8,128)(2,1)}), bf16[8,160,128]{2,1,0:T(8,128)(2,1)S(1)}, u32[]{:S(2)}, u32[]{:S(2)}) async-start(bf16[8,160,128]{2,1,0:T(8,128)(2,1)} %sum_cores.1), calls=%async_computation | async-start | bytes 655360 | tf_op jit(solution)/shard_map/all_to_all | solution.py:293
  48.6 0.8 pad_maximum_fusion
  49.4 2.6 %collective-permute-start.9 = (bf16[896,256]{1,0:T(8,128)(2,1)}, bf16[896,256]{1,0:T(8,128)(2,1)S(1)}, u32[]{:S(2)}, u32[]{:S(2)}) collective-permute-start(bf16[896,256]{1,0:T(8,128)(2,1)} %pad_maximum_fusion), channel_id=1, source_target_pairs={{0,7},{1,2},{2,1},{3,4},{4,3},{5,6},{6,5},{7,0},{8,15},{9,10},{10,... | collective-permute-start | bytes 1376264 | tf_op jit(solution)/shard_map/ppermute | solution.py:271
  52.0 3.0 %collective-permute-start.8 = (bf16[896,256]{1,0:T(8,128)(2,1)S(1)}, bf16[896,256]{1,0:T(8,128)(2,1)}, u32[]{:S(2)}, u32[]{:S(2)}) collective-permute-start(bf16[896,256]{1,0:T(8,128)(2,1)S(1)} %collective-permute-done.5.refs_5_.refs_6_), channel_id=1, source_target_pairs={{0,1},{1,0},{2,3},{3,2},{4,5},{5,4},{6,7},{7,6},{8,9},{9,8},{10,11... | collective-permute-start | bytes 1376264 | tf_op jit(solution)/shard_map/ppermute | solution.py:268
  55.0 7.3 %all-to-all-done.parts_ref = bf16[8,160,128]{2,1,0:T(8,128)(2,1)S(1)} async-done(((bf16[8,160,128]{2,1,0:T(8,128)(2,1)}), bf16[8,160,128]{2,1,0:T(8,128)(2,1)S(1)}, u32[]{:S(2)}, u32[]{:S(2)}) %all-to-all-start) | async-done | bytes 327712 | tf_op jit(solution)/shard_map/all_to_all | solution.py:293
  62.2 0.1 sum_z.1
  62.3 15.9 %all_to_all.15.parts_ref = bf16[32,16,128]{2,1,0:T(8,128)(2,1)S(1)} all-to-all(bf16[32,16,128]{2,1,0:T(8,128)(2,1)S(1)} %sum_z.1), channel_id=1, replica_groups=mesh['x'=4,'z'=8,'core'=2,'pair'=8] {'pair','x'}, dimensions={0} | all-to-all | bytes 262144 | tf_op jit(solution)/shard_map/all_to_all | solution.py:294
  78.2 0.9 amplitude_copies.1
  79.1 0.0 collective-permute-done.9.refs_8_
  79.1 0.0 collective-permute-done.8.refs_7_
  79.1 3.9 %all-to-all-start.2 = ((bf16[32,64,128]{2,1,0:T(8,128)(2,1)}), bf16[32,64,128]{2,1,0:T(8,128)(2,1)S(1)}, u32[]{:S(2)}, u32[]{:S(2)}) async-start(bf16[32,64,128]{2,1,0:T(8,128)(2,1)} %amplitude_copies.1), calls=%async_computation.2 | async-start | bytes 1048576 | tf_op jit(solution)/shard_map/all_to_all | solution.py:299
  83.0 1.0 slice.14
  84.0 2.7 %collective-permute-start.11 = (bf16[448,256]{1,0:T(8,128)(2,1)S(1)}, bf16[448,256]{1,0:T(8,128)(2,1)S(1)}, u32[]{:S(2)}, u32[]{:S(2)}) collective-permute-start(bf16[448,256]{1,0:T(8,128)(2,1)S(1)} %slice.15), channel_id=1, source_target_pairs={{0,1},{1,0},{2,3},{3,2},{4,5},{5,4},{6,7},{7,6},{8,9},{9,8},{10,11... | collective-permute-start | bytes 688136 | tf_op jit(solution)/shard_map/ppermute | solution.py:268
  86.7 1.9 %collective-permute-start.10 = (bf16[448,256]{1,0:T(8,128)(2,1)S(1)}, bf16[448,256]{1,0:T(8,128)(2,1)S(1)}, u32[]{:S(2)}, u32[]{:S(2)}) collective-permute-start(bf16[448,256]{1,0:T(8,128)(2,1)S(1)} %slice.14), channel_id=1, source_target_pairs={{0,7},{1,2},{2,1},{3,4},{4,3},{5,6},{6,5},{7,0},{8,15},{9,10},{10,... | collective-permute-start | bytes 688136 | tf_op jit(solution)/shard_map/ppermute | solution.py:271
  88.6 2.1 %collective-permute-done.11.refs_10_ = bf16[448,256]{1,0:T(8,128)(2,1)S(1)} collective-permute-done((bf16[448,256]{1,0:T(8,128)(2,1)S(1)}, bf16[448,256]{1,0:T(8,128)(2,1)S(1)}, u32[]{:S(2)}, u32[]{:S(2)}) %collective-permute-start.11) | collective-permute-done | bytes 229408 | tf_op jit(solution)/shard_map/ppermute | solution.py:268
  90.7 4.2 %collective-permute-done.10.refs_9_ = bf16[448,256]{1,0:T(8,128)(2,1)S(1)} collective-permute-done((bf16[448,256]{1,0:T(8,128)(2,1)S(1)}, bf16[448,256]{1,0:T(8,128)(2,1)S(1)}, u32[]{:S(2)}, u32[]{:S(2)}) %collective-permute-start.10) | collective-permute-done | bytes 229408 | tf_op jit(solution)/shard_map/ppermute | solution.py:271
  95.0 0.0 copy-start.1
  95.0 0.7 copy-done.1
  95.6 2.0 %all-to-all-done.2.refs_11_ = bf16[32,64,128]{2,1,0:T(8,128)(2,1)S(1)} async-done(((bf16[32,64,128]{2,1,0:T(8,128)(2,1)}), bf16[32,64,128]{2,1,0:T(8,128)(2,1)S(1)}, u32[]{:S(2)}, u32[]{:S(2)}) %all-to-all-start.2) | async-done | bytes 524320 | tf_op jit(solution)/shard_map/all_to_all | solution.py:299
  97.6 6.4 %collective-permute-start.12 = (bf16[32,64,128]{2,1,0:T(8,128)(2,1)S(1)}, bf16[32,64,128]{2,1,0:T(8,128)(2,1)S(1)}, u32[]{:S(2)}, u32[]{:S(2)}) collective-permute-start(bf16[32,64,128]{2,1,0:T(8,128)(2,1)S(1)} %all-to-all-done.2.refs_11_), channel_id=1, source_target_pairs={{0,8},{8,0},{1,9},{9,1},{2,10},{10,2},{3,11},{11,3},{4,12},{12,4},... | collective-permute-start | bytes 1572872 | tf_op jit(solution)/shard_map/ppermute | solution.py:274
  104.1 1.5 %collective-permute-done.12.refs_12_ = bf16[32,64,128]{2,1,0:T(8,128)(2,1)S(1)} collective-permute-done((bf16[32,64,128]{2,1,0:T(8,128)(2,1)S(1)}, bf16[32,64,128]{2,1,0:T(8,128)(2,1)S(1)}, u32[]{:S(2)}, u32[]{:S(2)}) %collective-permute-start.12) | collective-permute-done | bytes 524320 | tf_op jit(solution)/shard_map/ppermute | solution.py:274
  105.6 0.0 copy-start.2
  105.6 0.9 copy-done.2
  106.5 3.1 %gamma_rows.1 = bf16[896,256]{1,0:T(8,128)(2,1)} custom-call(bf16[896,256]{1,0:T(8,128)(2,1)S(1)} %copy-done, bf16[896,256]{1,0:T(8,128)(2,1)S(1)} %collective-permute-done.refs_1_.refs_0_, bf16[448,256]{1,0:T(8,128)(2,1)S(1)} %collective-permute-done.1.refs_2_.refs_1_, bf16[448,256]{1,0:T(8,128)(2,1)S(1)} %collective-permute-done.2.refs_3_.refs_2_, ...), custom_call_target="tpu_custom_call" | custom-call | tf_op jit(solution)/shard_map/gamma_rows/pallas_call | solution.py:250
  (1 shorter events, 0.0 us)
Async XLA Ops:
  0.0 25.6 %copy-start = (bf16[896,256]{1,0:T(8,128)(2,1)S(1)}, bf16[896,256]{1,0:T(8,128)(2,1)}, u32[]{:S(2)}) copy-start(bf16[896,256]{1,0:T(8,128)(2,1)} %refs_0_.3) | copy-start | bytes 1376260
  0.0 24.9 %copy-start.3 = (f32[20096]{0:T(1024)S(1)}, f32[20096]{0:T(1024)}, u32[]{:S(2)}) copy-start(f32[20096]{0:T(1024)} %param.8) | copy-start | bytes 241156
  0.0 12.2 %collective-permute-start = (bf16[896,256]{1,0:T(8,128)(2,1)}, bf16[896,256]{1,0:T(8,128)(2,1)S(1)}, u32[]{:S(2)}, u32[]{:S(2)}) collective-permute-start(bf16[896,256]{1,0:T(8,128)(2,1)} %refs_0_.3), channel_id=1, source_target_pairs={{0,1},{1,0},{2,3},{3,2},{4,5},{5,4},{6,7},{7,6},{8,9},{9,8},{10,11... | collective-permute-start | bytes 1376264 | tf_op jit(solution)/shard_map/ppermute | solution.py:268
  5.2 14.3 %collective-permute-start.2 = (bf16[448,256]{1,0:T(8,128)(2,1)S(1)}, bf16[448,256]{1,0:T(8,128)(2,1)S(1)}, u32[]{:S(2)}, u32[]{:S(2)}) collective-permute-start(bf16[448,256]{1,0:T(8,128)(2,1)S(1)} %get-tuple-element.43), channel_id=1, source_target_pairs={{0,7},{1,2},{2,1},{3,4},{4,3},{5,6},{6,5},{7,0},{8,15},{9,10},{10,... | collective-permute-start | bytes 688136 | tf_op jit(solution)/shard_map/ppermute | solution.py:271
  10.1 14.7 %copy-start.7 = (s32[16]{0:T(128)S(1)}, s32[16]{0:T(128)}, u32[]{:S(2)}) copy-start(s32[16]{0:T(128)} %exponent.1) | copy-start | bytes 196
  10.1 14.7 %copy-start.4 = (f32[64]{0:T(128)S(1)}, f32[64]{0:T(128)}, u32[]{:S(2)}) copy-start(f32[64]{0:T(128)} %occupied.1) | copy-start | bytes 772
  10.2 14.7 %copy-start.5 = (s32[16]{0:T(128)S(1)}, s32[16]{0:T(128)}, u32[]{:S(2)}) copy-start(s32[16]{0:T(128)} %occupied_of.1) | copy-start | bytes 196
  10.2 14.7 %copy-start.6 = (s32[16]{0:T(128)S(1)}, s32[16]{0:T(128)}, u32[]{:S(2)}) copy-start(s32[16]{0:T(128)} %virtual_of.1) | copy-start | bytes 196
  10.2 11.3 %collective-permute-start.1 = (bf16[448,256]{1,0:T(8,128)(2,1)S(1)}, bf16[448,256]{1,0:T(8,128)(2,1)S(1)}, u32[]{:S(2)}, u32[]{:S(2)}) collective-permute-start(bf16[448,256]{1,0:T(8,128)(2,1)S(1)} %get-tuple-element.44), channel_id=1, source_target_pairs={{0,7},{1,2},{2,1},{3,4},{4,3},{5,6},{6,5},{7,0},{8,15},{9,10},{10,... | collective-permute-start | bytes 688136 | tf_op jit(solution)/shard_map/ppermute | solution.py:271
  12.2 19.5 %collective-permute-start.5 = (bf16[896,256]{1,0:T(8,128)(2,1)S(1)}, bf16[896,256]{1,0:T(8,128)(2,1)S(1)}, u32[]{:S(2)}, u32[]{:S(2)}) collective-permute-start(bf16[896,256]{1,0:T(8,128)(2,1)S(1)} %collective-permute-done.refs_1_.refs_0_), channel_id=1, source_target_pairs={{0,7},{1,2},{2,1},{3,4},{4,3},{5,6},{6,5},{7,0},{8,15},{9,10},{10,... | collective-permute-start | bytes 1376264 | tf_op jit(solution)/shard_map/ppermute | solution.py:271
  19.5 12.2 %collective-permute-start.4 = (bf16[448,256]{1,0:T(8,128)(2,1)S(1)}, bf16[448,256]{1,0:T(8,128)(2,1)S(1)}, u32[]{:S(2)}, u32[]{:S(2)}) collective-permute-start(bf16[448,256]{1,0:T(8,128)(2,1)S(1)} %collective-permute-done.2.refs_3_.refs_2_), channel_id=1, source_target_pairs={{0,1},{1,0},{2,3},{3,2},{4,5},{5,4},{6,7},{7,6},{8,9},{9,8},{10,11... | collective-permute-start | bytes 688136 | tf_op jit(solution)/shard_map/ppermute | solution.py:268
  21.5 10.3 %collective-permute-start.3 = (bf16[448,256]{1,0:T(8,128)(2,1)S(1)}, bf16[448,256]{1,0:T(8,128)(2,1)S(1)}, u32[]{:S(2)}, u32[]{:S(2)}) collective-permute-start(bf16[448,256]{1,0:T(8,128)(2,1)S(1)} %collective-permute-done.1.refs_2_.refs_1_), channel_id=1, source_target_pairs={{0,1},{1,0},{2,3},{3,2},{4,5},{5,4},{6,7},{7,6},{8,9},{9,8},{10,11... | collective-permute-start | bytes 688136 | tf_op jit(solution)/shard_map/ppermute | solution.py:268
  26.3 10.6 %collective-permute-start.6 = (bf16[3,2,128,128]{3,2,1,0:T(8,128)(2,1)S(1)}, bf16[3,2,128,128]{3,2,1,0:T(8,128)(2,1)S(1)}, u32[]{:S(2)}, u32[]{:S(2)}) collective-permute-start(bf16[3,2,128,128]{3,2,1,0:T(8,128)(2,1)S(1)} %get-tuple-element.29), channel_id=1, source_target_pairs={{0,8},{8,0},{1,9},{9,1},{2,10},{10,2},{3,11},{11,3},{4,12},{12,4},... | collective-permute-start | bytes 589832 | tf_op jit(solution)/shard_map/ppermute | solution.py:274
  32.3 5.5 %collective-permute-start.7 = (bf16[2,2,128,128]{3,2,1,0:T(8,128)(2,1)S(1)}, bf16[2,2,128,128]{3,2,1,0:T(8,128)(2,1)S(1)}, u32[]{:S(2)}, u32[]{:S(2)}) collective-permute-start(bf16[2,2,128,128]{3,2,1,0:T(8,128)(2,1)S(1)} %get-tuple-element.30), channel_id=1, source_target_pairs={{0,8},{8,0},{1,9},{9,1},{2,10},{10,2},{3,11},{11,3},{4,12},{12,4},... | collective-permute-start | bytes 393224 | tf_op jit(solution)/shard_map/ppermute | solution.py:274
  38.6 23.6 %all-to-all-start = ((bf16[8,160,128]{2,1,0:T(8,128)(2,1)}), bf16[8,160,128]{2,1,0:T(8,128)(2,1)S(1)}, u32[]{:S(2)}, u32[]{:S(2)}) async-start(bf16[8,160,128]{2,1,0:T(8,128)(2,1)} %sum_cores.1), calls=%async_computation | async-start | bytes 655360 | tf_op jit(solution)/shard_map/all_to_all | solution.py:293
  49.4 29.7 %collective-permute-start.9 = (bf16[896,256]{1,0:T(8,128)(2,1)}, bf16[896,256]{1,0:T(8,128)(2,1)S(1)}, u32[]{:S(2)}, u32[]{:S(2)}) collective-permute-start(bf16[896,256]{1,0:T(8,128)(2,1)} %pad_maximum_fusion), channel_id=1, source_target_pairs={{0,7},{1,2},{2,1},{3,4},{4,3},{5,6},{6,5},{7,0},{8,15},{9,10},{10,... | collective-permute-start | bytes 1376264 | tf_op jit(solution)/shard_map/ppermute | solution.py:271
  52.0 27.1 %collective-permute-start.8 = (bf16[896,256]{1,0:T(8,128)(2,1)S(1)}, bf16[896,256]{1,0:T(8,128)(2,1)}, u32[]{:S(2)}, u32[]{:S(2)}) collective-permute-start(bf16[896,256]{1,0:T(8,128)(2,1)S(1)} %collective-permute-done.5.refs_5_.refs_6_), channel_id=1, source_target_pairs={{0,1},{1,0},{2,3},{3,2},{4,5},{5,4},{6,7},{7,6},{8,9},{9,8},{10,11... | collective-permute-start | bytes 1376264 | tf_op jit(solution)/shard_map/ppermute | solution.py:268
  79.1 18.6 %all-to-all-start.2 = ((bf16[32,64,128]{2,1,0:T(8,128)(2,1)}), bf16[32,64,128]{2,1,0:T(8,128)(2,1)S(1)}, u32[]{:S(2)}, u32[]{:S(2)}) async-start(bf16[32,64,128]{2,1,0:T(8,128)(2,1)} %amplitude_copies.1), calls=%async_computation.2 | async-start | bytes 1048576 | tf_op jit(solution)/shard_map/all_to_all | solution.py:299
  84.0 6.8 %collective-permute-start.11 = (bf16[448,256]{1,0:T(8,128)(2,1)S(1)}, bf16[448,256]{1,0:T(8,128)(2,1)S(1)}, u32[]{:S(2)}, u32[]{:S(2)}) collective-permute-start(bf16[448,256]{1,0:T(8,128)(2,1)S(1)} %slice.15), channel_id=1, source_target_pairs={{0,1},{1,0},{2,3},{3,2},{4,5},{5,4},{6,7},{7,6},{8,9},{9,8},{10,11... | collective-permute-start | bytes 688136 | tf_op jit(solution)/shard_map/ppermute | solution.py:268
  86.7 8.3 %collective-permute-start.10 = (bf16[448,256]{1,0:T(8,128)(2,1)S(1)}, bf16[448,256]{1,0:T(8,128)(2,1)S(1)}, u32[]{:S(2)}, u32[]{:S(2)}) collective-permute-start(bf16[448,256]{1,0:T(8,128)(2,1)S(1)} %slice.14), channel_id=1, source_target_pairs={{0,7},{1,2},{2,1},{3,4},{4,3},{5,6},{6,5},{7,0},{8,15},{9,10},{10,... | collective-permute-start | bytes 688136 | tf_op jit(solution)/shard_map/ppermute | solution.py:271
  95.0 0.7 copy-start.1
  97.6 7.9 %collective-permute-start.12 = (bf16[32,64,128]{2,1,0:T(8,128)(2,1)S(1)}, bf16[32,64,128]{2,1,0:T(8,128)(2,1)S(1)}, u32[]{:S(2)}, u32[]{:S(2)}) collective-permute-start(bf16[32,64,128]{2,1,0:T(8,128)(2,1)S(1)} %all-to-all-done.2.refs_11_), channel_id=1, source_target_pairs={{0,8},{8,0},{1,9},{9,1},{2,10},{10,2},{3,11},{11,3},{4,12},{12,4},... | collective-permute-start | bytes 1572872 | tf_op jit(solution)/shard_map/ppermute | solution.py:274
  105.6 0.9 copy-start.2

commit v17 on v16

--- a/solution.py
+++ b/solution.py
@@ -20,7 +20,8 @@
 GETS = tuple((PAIRS[k][0] - d, PAIRS[k][1] - d) for d, pairs in SENDS for k in pairs)
 ORDER = tuple((r, False) if c == 0 else (c, True) for r, c in GETS)
 ROWS = 224
-FETCHED = (("A", 3),)
+FETCHED = (("A", 3), ("B", 3))
+PARKED = (("A", 1), ("B", 1))
 VMEM_LIMIT = 12 * 1024 * 1024
 bf16, f32 = jnp.bfloat16, jnp.float32
 in_vmem = pl.BlockSpec(memory_space=pltpu.VMEM)
@@ -199,7 +200,7 @@
     )(parts, denominator)
 
 
-def gamma_rows(blocks, mine, theirs, scales):
+def gamma_rows(blocks, parked, mine, theirs, scales):
     rows, width = blocks[0][0].shape
     counts = [len(blocks[n]) for n in HELD]
 
@@ -209,8 +210,10 @@
         for count in counts:
             block.append(given[:count])
             given = given[count:]
-        own, other, scale, out, matrix, held, arrived = refs[sum(counts) :]
+        parked_ref, own, other, scale, out, matrix, held, arrived, sums = refs[sum(counts) :]
         fetches = []
+        for k, name in enumerate(PARKED):
+            block[HELD.index(name)] = [parked_ref.at[k * rows : (k + 1) * rows]]
         for k, name in enumerate(FETCHED):
             i = HELD.index(name)
             fetches.append(pltpu.make_async_copy(block[i][0], held.at[k], arrived.at[k]))
@@ -236,31 +239,39 @@
                             tile = tiles[h] * scale[pl.ds(2 * i + part, 1)]
                             matrix[held, place, h * TS : (h + 1) * TS] = tile.astype(bf16)
 
+        def product(indices, start):
+            total = None
+            for i in indices:
+                part, offset = divmod(start, rows // len(block[i]))
+                left = block[i][part][offset : offset + ROWS]
+                term = jnp.dot(left, matrix[i], preferred_element_type=f32)
+                total = term if total is None else total + term
+            return total
+
+        last = [i for i, name in enumerate(HELD) if name in FETCHED]
+        for start in range(0, rows, ROWS):
+            sums[start : start + ROWS] = product([i for i in range(len(HELD)) if i not in last], start)
         for fetch in fetches:
             fetch.wait()
         for start in range(0, rows, ROWS):
-            total = None
-            for i, parts in enumerate(block):
-                part, offset = divmod(start, rows // len(parts))
-                left = parts[part][offset : offset + ROWS]
-                term = jnp.dot(left, matrix[i], preferred_element_type=f32)
-                total = term if total is None else total + term
+            total = sums[start : start + ROWS] + product(last, start)
             out[start : start + ROWS] = total.astype(bf16)
 
     return pl.pallas_call(
         kernel,
         out_shape=jax.ShapeDtypeStruct((rows, width), bf16),
         in_specs=[anywhere if n in FETCHED else in_vmem for n in HELD for _ in blocks[n]]
-        + [in_vmem] * 3,
+        + [in_vmem] * 4,
         out_specs=in_vmem,
         scratch_shapes=[
             pltpu.VMEM((len(HELD), WIDTH, WIDTH), bf16),
             pltpu.VMEM((len(FETCHED), rows, width), bf16),
             pltpu.SemaphoreType.DMA((len(FETCHED),)),
+            pltpu.VMEM((rows, width), f32),
         ],
         compiler_params=pltpu.CompilerParams(vmem_limit_bytes=VMEM_LIMIT),
         name="gamma_rows",
-    )(*[part for n in HELD for part in blocks[n]], mine, theirs, scales)
+    )(*[part for n in HELD for part in blocks[n]], parked, mine, theirs, scales)
 
 
 def body(three_index, *energies):
@@ -288,9 +299,13 @@
     got_late = swap_cores(other_late)
     summed = sum_cores((early, late), (got_early, got_late))
 
-    summed, b2, a2 = lax.optimization_barrier((summed, block["B", 2], block["A", 2]))
+    summed, b2, a2, a1, b1 = lax.optimization_barrier(
+        (summed, block["B", 2], block["A", 2], block["A", 1], block["B", 1])
+    )
+    parked = jnp.concatenate(a1 + b1)
     a3, b3 = swap_a(b2[0]), swap_b(jnp.concatenate(a2))
     parts = lax.all_to_all(summed, "z", 0, 0)
+    parts, parked = lax.optimization_barrier((parts, parked))
     parts = lax.all_to_all(sum_z(parts), ("pair", "x"), 0, 0)
     copies = amplitude_copies(parts, denominator)
 
@@ -298,8 +313,8 @@
     b4 = [swap_b(a3[:half]), swap_a(b3[half:])]
     mine = lax.all_to_all(copies, ("z", "x"), 0, 0)
     mine, b4 = lax.optimization_barrier((mine, b4))
-    block.update({("B", 2): b2, ("A", 2): a2, ("A", 3): [a3], ("B", 3): [b3], ("B", 4): b4})
-    return gamma_rows(block, mine, swap_cores(mine), scales)
+    block.update({("A", 1): [], ("B", 1): [], ("B", 2): b2, ("A", 2): a2, ("A", 3): [a3], ("B", 3): [b3], ("B", 4): b4})
+    return gamma_rows(block, parked, mine, swap_cores(mine), scales)
 
 
 def solution(mesh):

time: 110 us -> 111 us (level)
    unnamed x16 -> x12, local copies, waits for them, and re-layouts: 1.66 us -> 0.02 us
  transfers between devices with their start and end apart: 15 -> 15, of which waited for: 6 -> 7; matrix products, arithmetic and copies ran while one was open for 3% -> 4% of each run, Pallas kernels for 3% -> 3%
where the time goes in v17:
time: 111 us; the launch traced here: 110 us
  starting transfers between devices  64.1 us (58%)
  waiting for transfers between devices  18.1 us (16%)
  blocking collectives  15.9 us (14%)
  Pallas kernels  7.76 us (7%)
  local copies, waits for them, and re-layouts  3.01 us (3%)
    ppermute x5, starting transfers between devices, swap_b(): return lax.ppermute(x, 'pair', SWAP_B)  18.7 us
    ppermute x3, starting transfers between devices, swap_cores(): return lax.ppermute(x, 'core', SWAP_CORES)  16.2 us
    all_to_all x1, blocking collectives, body(): parts = lax.all_to_all(sum_z(parts), ('pair', 'x'), 0, 0)  15.9 us
    ppermute x5, starting transfers between devices, swap_a(): return lax.ppermute(x, 'pair', SWAP_A)  15.2 us
    all_to_all x1, starting transfers between devices, body(): parts = lax.all_to_all(summed, 'z', 0, 0)  10 us
    all_to_all x1, waiting for transfers between devices, body(): parts = lax.all_to_all(summed, 'z', 0, 0)  7.3 us
    ppermute x5, waiting for transfers between devices, swap_b(): return lax.ppermute(x, 'pair', SWAP_B)  3.96 us
    all_to_all x1, starting transfers between devices, body(): mine = lax.all_to_all(copies, ('z', 'x'), 0, 0)  3.89 us
  transfers between devices with their start and end apart: 15, of which 7 were waited for; matrix products, arithmetic and copies ran while one was open for 4% of the time, Pallas kernels for 3%

profile of v17, /device:TPU:1, one launch (start us, length us, event | category | flops | bytes accessed | tf_op | source)
XLA Modules:
  0.0 109.9 jit_solution(9784548178614034615)
XLA Ops:
  0.0 0.0 copy-start
  0.0 0.0 copy-start.5
  0.0 0.0 copy-start.4
  0.0 0.0 copy-start.3
  0.0 0.0 copy-start.1
  0.0 0.0 copy-start.2
  0.0 4.2 %collective-permute-start = (bf16[896,256]{1,0:T(8,128)(2,1)}, bf16[896,256]{1,0:T(8,128)(2,1)S(1)}, u32[]{:S(2)}, u32[]{:S(2)}) collective-permute-start(bf16[896,256]{1,0:T(8,128)(2,1)} %refs_0_.3), channel_id=1, source_target_pairs={{0,1},{1,0},{2,3},{3,2},{4,5},{5,4},{6,7},{7,6},{8,9},{9,8},{10,11... | collective-permute-start | bytes 1376264 | tf_op jit(solution)/shard_map/ppermute | solution.py:279
  4.2 1.1 fusion
  5.3 4.9 %collective-permute-start.2 = (bf16[448,256]{1,0:T(8,128)(2,1)S(1)}, bf16[448,256]{1,0:T(8,128)(2,1)S(1)}, u32[]{:S(2)}, u32[]{:S(2)}) collective-permute-start(bf16[448,256]{1,0:T(8,128)(2,1)S(1)} %get-tuple-element.53), channel_id=1, source_target_pairs={{0,7},{1,2},{2,1},{3,4},{4,3},{5,6},{6,5},{7,0},{8,15},{9,10},{10,... | collective-permute-start | bytes 688136 | tf_op jit(solution)/shard_map/ppermute | solution.py:282
  10.2 1.9 %collective-permute-start.1 = (bf16[448,256]{1,0:T(8,128)(2,1)S(1)}, bf16[448,256]{1,0:T(8,128)(2,1)S(1)}, u32[]{:S(2)}, u32[]{:S(2)}) collective-permute-start(bf16[448,256]{1,0:T(8,128)(2,1)S(1)} %get-tuple-element.54), channel_id=1, source_target_pairs={{0,7},{1,2},{2,1},{3,4},{4,3},{5,6},{6,5},{7,0},{8,15},{9,10},{10,... | collective-permute-start | bytes 688136 | tf_op jit(solution)/shard_map/ppermute | solution.py:282
  12.1 0.0 collective-permute-done.refs_1_.refs_0_
  12.1 7.5 %collective-permute-start.5 = (bf16[896,256]{1,0:T(8,128)(2,1)S(1)}, bf16[896,256]{1,0:T(8,128)(2,1)S(1)}, u32[]{:S(2)}, u32[]{:S(2)}) collective-permute-start(bf16[896,256]{1,0:T(8,128)(2,1)S(1)} %collective-permute-done.refs_1_.refs_0_), channel_id=1, source_target_pairs={{0,7},{1,2},{2,1},{3,4},{4,3},{5,6},{6,5},{7,0},{8,15},{9,10},{10,... | collective-permute-start | bytes 1376264 | tf_op jit(solution)/shard_map/ppermute | solution.py:282
  19.6 0.0 collective-permute-done.2.refs_3_.refs_2_
  19.6 1.9 %collective-permute-start.4 = (bf16[448,256]{1,0:T(8,128)(2,1)S(1)}, bf16[448,256]{1,0:T(8,128)(2,1)S(1)}, u32[]{:S(2)}, u32[]{:S(2)}) collective-permute-start(bf16[448,256]{1,0:T(8,128)(2,1)S(1)} %collective-permute-done.2.refs_3_.refs_2_), channel_id=1, source_target_pairs={{0,1},{1,0},{2,3},{3,2},{4,5},{5,4},{6,7},{7,6},{8,9},{9,8},{10,11... | collective-permute-start | bytes 688136 | tf_op jit(solution)/shard_map/ppermute | solution.py:279
  21.5 0.0 collective-permute-done.1.refs_2_.refs_1_
  21.5 3.4 %collective-permute-start.3 = (bf16[448,256]{1,0:T(8,128)(2,1)S(1)}, bf16[448,256]{1,0:T(8,128)(2,1)S(1)}, u32[]{:S(2)}, u32[]{:S(2)}) collective-permute-start(bf16[448,256]{1,0:T(8,128)(2,1)S(1)} %collective-permute-done.1.refs_2_.refs_1_), channel_id=1, source_target_pairs={{0,1},{1,0},{2,3},{3,2},{4,5},{5,4},{6,7},{7,6},{8,9},{9,8},{10,11... | collective-permute-start | bytes 688136 | tf_op jit(solution)/shard_map/ppermute | solution.py:279
  24.9 0.0 copy-done.5
  24.9 0.0 copy-done.4
  24.9 0.0 copy-done.3
  24.9 0.0 copy-done.1
  24.9 0.0 copy-done.2
  25.0 0.7 tables.1
  25.7 0.0 copy-done
  25.7 0.6 coulomb_pairs.2
  26.3 5.2 %collective-permute-start.6 = (bf16[3,2,128,128]{3,2,1,0:T(8,128)(2,1)S(1)}, bf16[3,2,128,128]{3,2,1,0:T(8,128)(2,1)S(1)}, u32[]{:S(2)}, u32[]{:S(2)}) collective-permute-start(bf16[3,2,128,128]{3,2,1,0:T(8,128)(2,1)S(1)} %get-tuple-element.34), channel_id=1, source_target_pairs={{0,8},{8,0},{1,9},{9,1},{2,10},{10,2},{3,11},{11,3},{4,12},{12,4},... | collective-permute-start | bytes 589832 | tf_op jit(solution)/shard_map/ppermute | solution.py:285
  31.5 0.0 collective-permute-done.4.refs_4_.refs_2_
  31.5 0.2 collective-permute-done.3.refs_3_.refs_1_
  31.7 0.0 collective-permute-done.5.refs_5_.refs_3_
  31.7 0.5 coulomb_pairs.3
  32.2 4.7 %collective-permute-start.7 = (bf16[2,2,128,128]{3,2,1,0:T(8,128)(2,1)S(1)}, bf16[2,2,128,128]{3,2,1,0:T(8,128)(2,1)S(1)}, u32[]{:S(2)}, u32[]{:S(2)}) collective-permute-start(bf16[2,2,128,128]{3,2,1,0:T(8,128)(2,1)S(1)} %get-tuple-element.35), channel_id=1, source_target_pairs={{0,8},{8,0},{1,9},{9,1},{2,10},{10,2},{3,11},{11,3},{4,12},{12,4},... | collective-permute-start | bytes 393224 | tf_op jit(solution)/shard_map/ppermute | solution.py:285
  36.8 0.0 collective-permute-done.6.refs_2_
  36.8 1.0 collective-permute-done.7.refs_3_
  37.8 0.8 sum_cores.1
  38.6 10.0 %all-to-all-start = ((bf16[8,160,128]{2,1,0:T(8,128)(2,1)}), bf16[8,160,128]{2,1,0:T(8,128)(2,1)}, u32[]{:S(2)}, u32[]{:S(2)}) async-start(bf16[8,160,128]{2,1,0:T(8,128)(2,1)} %sum_cores.1), calls=%async_computation | async-start | bytes 655360 | tf_op jit(solution)/shard_map/all_to_all | solution.py:307
  48.6 0.8 pad_maximum_fusion.1
  49.4 2.6 %collective-permute-start.9 = (bf16[896,256]{1,0:T(8,128)(2,1)}, bf16[896,256]{1,0:T(8,128)(2,1)}, u32[]{:S(2)}, u32[]{:S(2)}) collective-permute-start(bf16[896,256]{1,0:T(8,128)(2,1)} %pad_maximum_fusion.1), channel_id=1, source_target_pairs={{0,7},{1,2},{2,1},{3,4},{4,3},{5,6},{6,5},{7,0},{8,15},{9,10},{10,... | collective-permute-start | bytes 1376264 | tf_op jit(solution)/shard_map/ppermute | solution.py:282
  52.0 3.0 %collective-permute-start.8 = (bf16[896,256]{1,0:T(8,128)(2,1)S(1)}, bf16[896,256]{1,0:T(8,128)(2,1)}, u32[]{:S(2)}, u32[]{:S(2)}) collective-permute-start(bf16[896,256]{1,0:T(8,128)(2,1)S(1)} %collective-permute-done.5.refs_5_.refs_3_), channel_id=1, source_target_pairs={{0,1},{1,0},{2,3},{3,2},{4,5},{5,4},{6,7},{7,6},{8,9},{9,8},{10,11... | collective-permute-start | bytes 1376264 | tf_op jit(solution)/shard_map/ppermute | solution.py:279
  55.0 0.1 pad_maximum_fusion.refs_8_
  55.1 7.3 %all-to-all-done.parts_ref = bf16[8,160,128]{2,1,0:T(8,128)(2,1)} async-done(((bf16[8,160,128]{2,1,0:T(8,128)(2,1)}), bf16[8,160,128]{2,1,0:T(8,128)(2,1)}, u32[]{:S(2)}, u32[]{:S(2)}) %all-to-all-start) | async-done | bytes 327712 | tf_op jit(solution)/shard_map/all_to_all | solution.py:307
  62.4 1.0 sum_z.1
  63.4 15.9 %all_to_all.15.parts_ref = bf16[32,16,128]{2,1,0:T(8,128)(2,1)S(1)} all-to-all(bf16[32,16,128]{2,1,0:T(8,128)(2,1)S(1)} %sum_z.1), channel_id=1, replica_groups=mesh['x'=4,'z'=8,'core'=2,'pair'=8] {'pair','x'}, dimensions={0} | all-to-all | bytes 262144 | tf_op jit(solution)/shard_map/all_to_all | solution.py:309
  79.3 0.9 amplitude_copies.1
  80.2 0.0 collective-permute-done.9.refs_5_
  80.2 0.0 collective-permute-done.8.refs_4_
  80.2 3.9 %all-to-all-start.2 = ((bf16[32,64,128]{2,1,0:T(8,128)(2,1)}), bf16[32,64,128]{2,1,0:T(8,128)(2,1)S(1)}, u32[]{:S(2)}, u32[]{:S(2)}) async-start(bf16[32,64,128]{2,1,0:T(8,128)(2,1)} %amplitude_copies.1), calls=%async_computation.2 | async-start | bytes 1048576 | tf_op jit(solution)/shard_map/all_to_all | solution.py:314
  84.1 1.0 slice.14
  85.1 1.0 slice.15
  86.0 2.7 %collective-permute-start.11 = (bf16[448,256]{1,0:T(8,128)(2,1)S(1)}, bf16[448,256]{1,0:T(8,128)(2,1)S(1)}, u32[]{:S(2)}, u32[]{:S(2)}) collective-permute-start(bf16[448,256]{1,0:T(8,128)(2,1)S(1)} %slice.15), channel_id=1, source_target_pairs={{0,1},{1,0},{2,3},{3,2},{4,5},{5,4},{6,7},{7,6},{8,9},{9,8},{10,11... | collective-permute-start | bytes 688136 | tf_op jit(solution)/shard_map/ppermute | solution.py:279
  88.8 1.9 %collective-permute-start.10 = (bf16[448,256]{1,0:T(8,128)(2,1)S(1)}, bf16[448,256]{1,0:T(8,128)(2,1)S(1)}, u32[]{:S(2)}, u32[]{:S(2)}) collective-permute-start(bf16[448,256]{1,0:T(8,128)(2,1)S(1)} %slice.14), channel_id=1, source_target_pairs={{0,7},{1,2},{2,1},{3,4},{4,3},{5,6},{6,5},{7,0},{8,15},{9,10},{10,... | collective-permute-start | bytes 688136 | tf_op jit(solution)/shard_map/ppermute | solution.py:282
  90.7 2.4 %collective-permute-done.11.refs_7_ = bf16[448,256]{1,0:T(8,128)(2,1)S(1)} collective-permute-done((bf16[448,256]{1,0:T(8,128)(2,1)S(1)}, bf16[448,256]{1,0:T(8,128)(2,1)S(1)}, u32[]{:S(2)}, u32[]{:S(2)}) %collective-permute-start.11) | collective-permute-done | bytes 229408 | tf_op jit(solution)/shard_map/ppermute | solution.py:279
  93.1 3.9 %collective-permute-done.10.refs_6_ = bf16[448,256]{1,0:T(8,128)(2,1)S(1)} collective-permute-done((bf16[448,256]{1,0:T(8,128)(2,1)S(1)}, bf16[448,256]{1,0:T(8,128)(2,1)S(1)}, u32[]{:S(2)}, u32[]{:S(2)}) %collective-permute-start.10) | collective-permute-done | bytes 229408 | tf_op jit(solution)/shard_map/ppermute | solution.py:282
  97.0 1.8 %all-to-all-done.2.refs_9_ = bf16[32,64,128]{2,1,0:T(8,128)(2,1)S(1)} async-done(((bf16[32,64,128]{2,1,0:T(8,128)(2,1)}), bf16[32,64,128]{2,1,0:T(8,128)(2,1)S(1)}, u32[]{:S(2)}, u32[]{:S(2)}) %all-to-all-start.2) | async-done | bytes 524320 | tf_op jit(solution)/shard_map/all_to_all | solution.py:314
  98.8 6.4 %collective-permute-start.12 = (bf16[32,64,128]{2,1,0:T(8,128)(2,1)S(1)}, bf16[32,64,128]{2,1,0:T(8,128)(2,1)S(1)}, u32[]{:S(2)}, u32[]{:S(2)}) collective-permute-start(bf16[32,64,128]{2,1,0:T(8,128)(2,1)S(1)} %all-to-all-done.2.refs_9_), channel_id=1, source_target_pairs={{0,8},{8,0},{1,9},{9,1},{2,10},{10,2},{3,11},{11,3},{4,12},{12,4},... | collective-permute-start | bytes 1572872 | tf_op jit(solution)/shard_map/ppermute | solution.py:285
  105.2 1.5 %collective-permute-done.12.refs_10_ = bf16[32,64,128]{2,1,0:T(8,128)(2,1)S(1)} collective-permute-done((bf16[32,64,128]{2,1,0:T(8,128)(2,1)S(1)}, bf16[32,64,128]{2,1,0:T(8,128)(2,1)S(1)}, u32[]{:S(2)}, u32[]{:S(2)}) %collective-permute-start.12) | collective-permute-done | bytes 524320 | tf_op jit(solution)/shard_map/ppermute | solution.py:285
  106.7 3.2 %gamma_rows.1 = bf16[896,256]{1,0:T(8,128)(2,1)} custom-call(bf16[896,256]{1,0:T(8,128)(2,1)S(1)} %copy-done, bf16[448,256]{1,0:T(8,128)(2,1)S(1)} %collective-permute-done.3.refs_3_.refs_1_, bf16[448,256]{1,0:T(8,128)(2,1)S(1)} %collective-permute-done.4.refs_4_.refs_2_, bf16[896,256]{1,0:T(8,128)(2,1)S(1)} %collective-permute-done.5.refs_5_.refs_3_, ...), custom_call_target="tpu_custom_call" | custom-call | tf_op jit(solution)/shard_map/gamma_rows/pallas_call | solution.py:260
Async XLA Ops:
  0.0 25.7 %copy-start = (bf16[896,256]{1,0:T(8,128)(2,1)S(1)}, bf16[896,256]{1,0:T(8,128)(2,1)}, u32[]{:S(2)}) copy-start(bf16[896,256]{1,0:T(8,128)(2,1)} %refs_0_.3) | copy-start | bytes 1376260
  0.0 24.9 %copy-start.5 = (s32[16]{0:T(128)S(1)}, s32[16]{0:T(128)}, u32[]{:S(2)}) copy-start(s32[16]{0:T(128)} %exponent.1) | copy-start | bytes 196
  0.0 24.9 %copy-start.4 = (s32[16]{0:T(128)S(1)}, s32[16]{0:T(128)}, u32[]{:S(2)}) copy-start(s32[16]{0:T(128)} %virtual_of.1) | copy-start | bytes 196
  0.0 24.9 %copy-start.3 = (s32[16]{0:T(128)S(1)}, s32[16]{0:T(128)}, u32[]{:S(2)}) copy-start(s32[16]{0:T(128)} %occupied_of.1) | copy-start | bytes 196
  0.0 24.9 %copy-start.1 = (f32[20096]{0:T(1024)S(1)}, f32[20096]{0:T(1024)}, u32[]{:S(2)}) copy-start(f32[20096]{0:T(1024)} %param.8) | copy-start | bytes 241156
  0.0 24.9 %copy-start.2 = (f32[64]{0:T(128)S(1)}, f32[64]{0:T(128)}, u32[]{:S(2)}) copy-start(f32[64]{0:T(128)} %occupied.1) | copy-start | bytes 772
  0.0 12.1 %collective-permute-start = (bf16[896,256]{1,0:T(8,128)(2,1)}, bf16[896,256]{1,0:T(8,128)(2,1)S(1)}, u32[]{:S(2)}, u32[]{:S(2)}) collective-permute-start(bf16[896,256]{1,0:T(8,128)(2,1)} %refs_0_.3), channel_id=1, source_target_pairs={{0,1},{1,0},{2,3},{3,2},{4,5},{5,4},{6,7},{7,6},{8,9},{9,8},{10,11... | collective-permute-start | bytes 1376264 | tf_op jit(solution)/shard_map/ppermute | solution.py:279
  5.3 14.3 %collective-permute-start.2 = (bf16[448,256]{1,0:T(8,128)(2,1)S(1)}, bf16[448,256]{1,0:T(8,128)(2,1)S(1)}, u32[]{:S(2)}, u32[]{:S(2)}) collective-permute-start(bf16[448,256]{1,0:T(8,128)(2,1)S(1)} %get-tuple-element.53), channel_id=1, source_target_pairs={{0,7},{1,2},{2,1},{3,4},{4,3},{5,6},{6,5},{7,0},{8,15},{9,10},{10,... | collective-permute-start | bytes 688136 | tf_op jit(solution)/shard_map/ppermute | solution.py:282
  10.2 11.4 %collective-permute-start.1 = (bf16[448,256]{1,0:T(8,128)(2,1)S(1)}, bf16[448,256]{1,0:T(8,128)(2,1)S(1)}, u32[]{:S(2)}, u32[]{:S(2)}) collective-permute-start(bf16[448,256]{1,0:T(8,128)(2,1)S(1)} %get-tuple-element.54), channel_id=1, source_target_pairs={{0,7},{1,2},{2,1},{3,4},{4,3},{5,6},{6,5},{7,0},{8,15},{9,10},{10,... | collective-permute-start | bytes 688136 | tf_op jit(solution)/shard_map/ppermute | solution.py:282
  12.1 19.6 %collective-permute-start.5 = (bf16[896,256]{1,0:T(8,128)(2,1)S(1)}, bf16[896,256]{1,0:T(8,128)(2,1)S(1)}, u32[]{:S(2)}, u32[]{:S(2)}) collective-permute-start(bf16[896,256]{1,0:T(8,128)(2,1)S(1)} %collective-permute-done.refs_1_.refs_0_), channel_id=1, source_target_pairs={{0,7},{1,2},{2,1},{3,4},{4,3},{5,6},{6,5},{7,0},{8,15},{9,10},{10,... | collective-permute-start | bytes 1376264 | tf_op jit(solution)/shard_map/ppermute | solution.py:282
  19.6 11.9 %collective-permute-start.4 = (bf16[448,256]{1,0:T(8,128)(2,1)S(1)}, bf16[448,256]{1,0:T(8,128)(2,1)S(1)}, u32[]{:S(2)}, u32[]{:S(2)}) collective-permute-start(bf16[448,256]{1,0:T(8,128)(2,1)S(1)} %collective-permute-done.2.refs_3_.refs_2_), channel_id=1, source_target_pairs={{0,1},{1,0},{2,3},{3,2},{4,5},{5,4},{6,7},{7,6},{8,9},{9,8},{10,11... | collective-permute-start | bytes 688136 | tf_op jit(solution)/shard_map/ppermute | solution.py:279
  21.5 10.1 %collective-permute-start.3 = (bf16[448,256]{1,0:T(8,128)(2,1)S(1)}, bf16[448,256]{1,0:T(8,128)(2,1)S(1)}, u32[]{:S(2)}, u32[]{:S(2)}) collective-permute-start(bf16[448,256]{1,0:T(8,128)(2,1)S(1)} %collective-permute-done.1.refs_2_.refs_1_), channel_id=1, source_target_pairs={{0,1},{1,0},{2,3},{3,2},{4,5},{5,4},{6,7},{7,6},{8,9},{9,8},{10,11... | collective-permute-start | bytes 688136 | tf_op jit(solution)/shard_map/ppermute | solution.py:279
  26.3 10.5 %collective-permute-start.6 = (bf16[3,2,128,128]{3,2,1,0:T(8,128)(2,1)S(1)}, bf16[3,2,128,128]{3,2,1,0:T(8,128)(2,1)S(1)}, u32[]{:S(2)}, u32[]{:S(2)}) collective-permute-start(bf16[3,2,128,128]{3,2,1,0:T(8,128)(2,1)S(1)} %get-tuple-element.34), channel_id=1, source_target_pairs={{0,8},{8,0},{1,9},{9,1},{2,10},{10,2},{3,11},{11,3},{4,12},{12,4},... | collective-permute-start | bytes 589832 | tf_op jit(solution)/shard_map/ppermute | solution.py:285
  32.2 5.6 %collective-permute-start.7 = (bf16[2,2,128,128]{3,2,1,0:T(8,128)(2,1)S(1)}, bf16[2,2,128,128]{3,2,1,0:T(8,128)(2,1)S(1)}, u32[]{:S(2)}, u32[]{:S(2)}) collective-permute-start(bf16[2,2,128,128]{3,2,1,0:T(8,128)(2,1)S(1)} %get-tuple-element.35), channel_id=1, source_target_pairs={{0,8},{8,0},{1,9},{9,1},{2,10},{10,2},{3,11},{11,3},{4,12},{12,4},... | collective-permute-start | bytes 393224 | tf_op jit(solution)/shard_map/ppermute | solution.py:285
  38.6 23.8 %all-to-all-start = ((bf16[8,160,128]{2,1,0:T(8,128)(2,1)}), bf16[8,160,128]{2,1,0:T(8,128)(2,1)}, u32[]{:S(2)}, u32[]{:S(2)}) async-start(bf16[8,160,128]{2,1,0:T(8,128)(2,1)} %sum_cores.1), calls=%async_computation | async-start | bytes 655360 | tf_op jit(solution)/shard_map/all_to_all | solution.py:307
  49.4 30.8 %collective-permute-start.9 = (bf16[896,256]{1,0:T(8,128)(2,1)}, bf16[896,256]{1,0:T(8,128)(2,1)}, u32[]{:S(2)}, u32[]{:S(2)}) collective-permute-start(bf16[896,256]{1,0:T(8,128)(2,1)} %pad_maximum_fusion.1), channel_id=1, source_target_pairs={{0,7},{1,2},{2,1},{3,4},{4,3},{5,6},{6,5},{7,0},{8,15},{9,10},{10,... | collective-permute-start | bytes 1376264 | tf_op jit(solution)/shard_map/ppermute | solution.py:282
  52.0 28.2 %collective-permute-start.8 = (bf16[896,256]{1,0:T(8,128)(2,1)S(1)}, bf16[896,256]{1,0:T(8,128)(2,1)}, u32[]{:S(2)}, u32[]{:S(2)}) collective-permute-start(bf16[896,256]{1,0:T(8,128)(2,1)S(1)} %collective-permute-done.5.refs_5_.refs_3_), channel_id=1, source_target_pairs={{0,1},{1,0},{2,3},{3,2},{4,5},{5,4},{6,7},{7,6},{8,9},{9,8},{10,11... | collective-permute-start | bytes 1376264 | tf_op jit(solution)/shard_map/ppermute | solution.py:279
  80.2 18.6 %all-to-all-start.2 = ((bf16[32,64,128]{2,1,0:T(8,128)(2,1)}), bf16[32,64,128]{2,1,0:T(8,128)(2,1)S(1)}, u32[]{:S(2)}, u32[]{:S(2)}) async-start(bf16[32,64,128]{2,1,0:T(8,128)(2,1)} %amplitude_copies.1), calls=%async_computation.2 | async-start | bytes 1048576 | tf_op jit(solution)/shard_map/all_to_all | solution.py:314
  86.0 7.1 %collective-permute-start.11 = (bf16[448,256]{1,0:T(8,128)(2,1)S(1)}, bf16[448,256]{1,0:T(8,128)(2,1)S(1)}, u32[]{:S(2)}, u32[]{:S(2)}) collective-permute-start(bf16[448,256]{1,0:T(8,128)(2,1)S(1)} %slice.15), channel_id=1, source_target_pairs={{0,1},{1,0},{2,3},{3,2},{4,5},{5,4},{6,7},{7,6},{8,9},{9,8},{10,11... | collective-permute-start | bytes 688136 | tf_op jit(solution)/shard_map/ppermute | solution.py:279
  88.8 8.3 %collective-permute-start.10 = (bf16[448,256]{1,0:T(8,128)(2,1)S(1)}, bf16[448,256]{1,0:T(8,128)(2,1)S(1)}, u32[]{:S(2)}, u32[]{:S(2)}) collective-permute-start(bf16[448,256]{1,0:T(8,128)(2,1)S(1)} %slice.14), channel_id=1, source_target_pairs={{0,7},{1,2},{2,1},{3,4},{4,3},{5,6},{6,5},{7,0},{8,15},{9,10},{10,... | collective-permute-start | bytes 688136 | tf_op jit(solution)/shard_map/ppermute | solution.py:282
  98.8 7.9 %collective-permute-start.12 = (bf16[32,64,128]{2,1,0:T(8,128)(2,1)S(1)}, bf16[32,64,128]{2,1,0:T(8,128)(2,1)S(1)}, u32[]{:S(2)}, u32[]{:S(2)}) collective-permute-start(bf16[32,64,128]{2,1,0:T(8,128)(2,1)S(1)} %all-to-all-done.2.refs_9_), channel_id=1, source_target_pairs={{0,8},{8,0},{1,9},{9,1},{2,10},{10,2},{3,11},{11,3},{4,12},{12,4},... | collective-permute-start | bytes 1572872 | tf_op jit(solution)/shard_map/ppermute | solution.py:285

commit v18 on v16

--- a/solution.py
+++ b/solution.py
@@ -61,7 +61,7 @@
 
         lane = lax.broadcasted_iota(jnp.int32, (PIECE, TS), 1)
         chosen = lane == first + lax.broadcasted_iota(jnp.int32, (PIECE, TS), 0)
-        for k, (r, c) in enumerate(GETS):
+        for k, (r, c) in enumerate(PAIRS):
             row, column = tile_of(r, core), tile_of(c, half)
             of_row = jnp.sum(jnp.where(chosen, energy(row), 0.0), axis=1, keepdims=True)
             level = jnp.full((PIECE, TS), scale(row) * scale(column), f32)
@@ -74,7 +74,7 @@
     return pl.pallas_call(
         kernel,
         out_shape=(
-            jax.ShapeDtypeStruct((len(GETS) * PIECE, TS), f32),
+            jax.ShapeDtypeStruct((len(PAIRS) * PIECE, TS), f32),
             jax.ShapeDtypeStruct((2 * len(ORDER), TS), f32),
         ),
         in_specs=[in_smem, in_vmem, in_smem, in_smem, in_smem],
@@ -133,22 +133,18 @@
 
 
 def sum_cores(own, received):
-    pairs = sum(a.shape[0] for a in own)
-    rows = WIDTH // NZ
+    count = sum(a.shape[0] for a in own)
 
     def kernel(*refs):
-        out = refs[-1]
-        n = 0
+        parts = []
         for mine, theirs in zip(refs[: len(own)], refs[len(own) : -1]):
-            count = mine.shape[0]
-            total = (mine[...] + theirs[...].astype(f32)).astype(bf16).reshape(count, NZ, rows, TS)
-            for k in range(count):
-                out[:, (n + k) * rows : (n + k + 1) * rows] = total[k]
-            n += count
-
-    return pl.pallas_call(
-        kernel,
-        out_shape=jax.ShapeDtypeStruct((NZ, pairs * rows, TS), bf16),
+            total = (mine[...] + theirs[...].astype(f32)).reshape(-1, NXZ, PIECE, TS)
+            parts += [total[k] for k in range(total.shape[0])]
+        refs[-1][...] = jnp.concatenate(parts, axis=1).astype(bf16)
+
+    return pl.pallas_call(
+        kernel,
+        out_shape=jax.ShapeDtypeStruct((NXZ, count * PIECE, TS), bf16),
         in_specs=[in_vmem] * (2 * len(own)),
         out_specs=in_vmem,
         compiler_params=pltpu.CompilerParams(vmem_limit_bytes=VMEM_LIMIT),
@@ -156,47 +152,41 @@
     )(*own, *received)
 
 
-def sum_z(parts):
-    def kernel(parts_ref, out):
+def amplitude_sends(parts, denominator):
+    def kernel(parts_ref, denominator_ref, out):
         me = lax.axis_index("pair")
-        total = jnp.sum(parts_ref[...].astype(f32), axis=0).reshape(len(PAIRS), NX, PIECE, TS)
+        total = jnp.sum(parts_ref[...].astype(f32), axis=0) / denominator_ref[...]
         out[...] = jnp.zeros_like(out)
         for d, (first, second) in SENDS:
-            both = jnp.concatenate([total[first], total[second]], axis=1)
-            out[pl.ds(NX * lax.rem(me + d + NPAIR, NPAIR), NX)] = both.astype(bf16)
-
-    return pl.pallas_call(
-        kernel,
-        out_shape=jax.ShapeDtypeStruct((NPAIR * NX, 2 * PIECE, TS), bf16),
+            both = total[first * PIECE : (second + 1) * PIECE]
+            out[lax.rem(me + d + NPAIR, NPAIR)] = both.astype(bf16)
+
+    return pl.pallas_call(
+        kernel,
+        out_shape=jax.ShapeDtypeStruct((NPAIR, 2 * PIECE, TS), bf16),
+        in_specs=[in_vmem] * 2,
+        out_specs=in_vmem,
+        compiler_params=pltpu.CompilerParams(vmem_limit_bytes=VMEM_LIMIT),
+        name="amplitude_sends",
+    )(parts, denominator)
+
+
+def amplitude_copies(received):
+    rows = len(GETS) * PIECE
+
+    def kernel(received_ref, out):
+        me = lax.axis_index("pair")
+        pieces = [received_ref[lax.rem(me - d + NPAIR, NPAIR)] for d, _ in SENDS]
+        out[...] = jnp.broadcast_to(jnp.concatenate(pieces)[None], out.shape)
+
+    return pl.pallas_call(
+        kernel,
+        out_shape=jax.ShapeDtypeStruct((NXZ, rows, TS), bf16),
         in_specs=[in_vmem],
         out_specs=in_vmem,
         compiler_params=pltpu.CompilerParams(vmem_limit_bytes=VMEM_LIMIT),
-        name="sum_z",
-    )(parts)
-
-
-def amplitude_copies(parts, denominator):
-    rows = len(GETS) * PIECE
-
-    def kernel(parts_ref, denominator_ref, out):
-        me = lax.axis_index("pair")
-        total = jnp.concatenate(
-            [
-                jnp.sum(parts_ref[pl.ds(NX * lax.rem(me - d + NPAIR, NPAIR), NX)].astype(f32), axis=0)
-                for d, _ in SENDS
-            ]
-        )
-        amplitude = (total / denominator_ref[...]).astype(bf16)
-        out[...] = jnp.broadcast_to(amplitude[None], out.shape)
-
-    return pl.pallas_call(
-        kernel,
-        out_shape=jax.ShapeDtypeStruct((NXZ, rows, TS), bf16),
-        in_specs=[in_vmem] * 2,
-        out_specs=in_vmem,
-        compiler_params=pltpu.CompilerParams(vmem_limit_bytes=VMEM_LIMIT),
         name="amplitude_copies",
-    )(parts, denominator)
+    )(received)
 
 
 def gamma_rows(blocks, mine, theirs, scales):
@@ -209,7 +199,7 @@
         for count in counts:
             block.append(given[:count])
             given = given[count:]
-        own, other, scale, out, matrix, held, arrived = refs[sum(counts) :]
+        own, other, scale, out, matrix, held, arrived, sums = refs[sum(counts) :]
         fetches = []
         for k, name in enumerate(FETCHED):
             i = HELD.index(name)
@@ -236,15 +226,22 @@
                             tile = tiles[h] * scale[pl.ds(2 * i + part, 1)]
                             matrix[held, place, h * TS : (h + 1) * TS] = tile.astype(bf16)
 
+        def product(indices, start):
+            total = None
+            for i in indices:
+                part, offset = divmod(start, rows // len(block[i]))
+                left = block[i][part][offset : offset + ROWS]
+                term = jnp.dot(left, matrix[i], preferred_element_type=f32)
+                total = term if total is None else total + term
+            return total
+
+        last = [i for i, name in enumerate(HELD) if name in FETCHED]
+        for start in range(0, rows, ROWS):
+            sums[start : start + ROWS] = product([i for i in range(len(HELD)) if i not in last], start)
         for fetch in fetches:
             fetch.wait()
         for start in range(0, rows, ROWS):
-            total = None
-            for i, parts in enumerate(block):
-                part, offset = divmod(start, rows // len(parts))
-                left = parts[part][offset : offset + ROWS]
-                term = jnp.dot(left, matrix[i], preferred_element_type=f32)
-                total = term if total is None else total + term
+            total = sums[start : start + ROWS] + product(last, start)
             out[start : start + ROWS] = total.astype(bf16)
 
     return pl.pallas_call(
@@ -257,6 +254,7 @@
             pltpu.VMEM((len(HELD), WIDTH, WIDTH), bf16),
             pltpu.VMEM((len(FETCHED), rows, width), bf16),
             pltpu.SemaphoreType.DMA((len(FETCHED),)),
+            pltpu.VMEM((rows, width), f32),
         ],
         compiler_params=pltpu.CompilerParams(vmem_limit_bytes=VMEM_LIMIT),
         name="gamma_rows",
@@ -290,9 +288,9 @@
 
     summed, b2, a2 = lax.optimization_barrier((summed, block["B", 2], block["A", 2]))
     a3, b3 = swap_a(b2[0]), swap_b(jnp.concatenate(a2))
-    parts = lax.all_to_all(summed, "z", 0, 0)
-    parts = lax.all_to_all(sum_z(parts), ("pair", "x"), 0, 0)
-    copies = amplitude_copies(parts, denominator)
+    parts = lax.all_to_all(summed, ("z", "x"), 0, 0)
+    received = lax.all_to_all(amplitude_sends(parts, denominator), "pair", 0, 0)
+    copies = amplitude_copies(received)
 
     copies, a3, b3 = lax.optimization_barrier((copies, a3, b3))
     b4 = [swap_b(a3[:half]), swap_a(b3[half:])]

time: 110 us -> 108 us (0.982)
  blocking collectives: 15.9 us -> 10.6 us
  starting transfers between devices: 64.2 us -> 69 us
  waiting for transfers between devices: 18.1 us -> 16.4 us
    all_to_all x1, blocking collectives: 15.9 us -> 10.6 us  [body(): received = lax.all_to_all(amplitude_sends(parts, denominator), 'pair', 0, 0)]
    all_to_all x1, starting transfers between devices: 10 us -> 12.9 us  [body(): parts = lax.all_to_all(summed, ('z', 'x'), 0, 0)]
    all_to_all x1, starting transfers between devices: 3.89 us -> 5.25 us  [body(): mine = lax.all_to_all(copies, ('z', 'x'), 0, 0)]
where the time goes in v18:
time: 108 us; the launch traced here: 107 us
  starting transfers between devices  69 us (64%)
  waiting for transfers between devices  16.4 us (15%)
  blocking collectives  10.6 us (10%)
  Pallas kernels  6.41 us (6%)
  local copies, waits for them, and re-layouts  3.71 us (3%)
    ppermute x5, starting transfers between devices, swap_b(): return lax.ppermute(x, 'pair', SWAP_B)  18.8 us
    ppermute x3, starting transfers between devices, swap_cores(): return lax.ppermute(x, 'core', SWAP_CORES)  16.5 us
    ppermute x5, starting transfers between devices, swap_a(): return lax.ppermute(x, 'pair', SWAP_A)  15.6 us
    all_to_all x1, starting transfers between devices, body(): parts = lax.all_to_all(summed, ('z', 'x'), 0, 0)  12.9 us
    all_to_all x1, blocking collectives, body(): received = lax.all_to_all(amplitude_sends(parts, denominator), 'pair', 0, 0)  10.6 us
    all_to_all x1, waiting for transfers between devices, body(): parts = lax.all_to_all(summed, ('z', 'x'), 0, 0)  6.39 us
    all_to_all x1, starting transfers between devices, body(): mine = lax.all_to_all(copies, ('z', 'x'), 0, 0)  5.25 us
    ppermute x5, waiting for transfers between devices, swap_b(): return lax.ppermute(x, 'pair', SWAP_B)  4.47 us
  transfers between devices with their start and end apart: 15, of which 6 were waited for; matrix products, arithmetic and copies ran while one was open for 3% of the time, Pallas kernels for 3%

profile of v18, /device:TPU:1, one launch (start us, length us, event | category | flops | bytes accessed | tf_op | source)
XLA Modules:
  0.0 107.2 jit_solution(2432297161232397100)
XLA Ops:
  0.0 0.0 copy-start
  0.0 0.0 copy-start.3
  0.0 4.2 %collective-permute-start = (bf16[896,256]{1,0:T(8,128)(2,1)}, bf16[896,256]{1,0:T(8,128)(2,1)S(1)}, u32[]{:S(2)}, u32[]{:S(2)}) collective-permute-start(bf16[896,256]{1,0:T(8,128)(2,1)} %refs_0_.3), channel_id=1, source_target_pairs={{0,1},{1,0},{2,3},{3,2},{4,5},{5,4},{6,7},{7,6},{8,9},{9,8},{10,11... | collective-permute-start | bytes 1376264 | tf_op jit(solution)/shard_map/ppermute | solution.py:266
  4.2 1.1 %fusion = (bf16[448,256]{1,0:T(8,128)(2,1)S(1)}, bf16[448,256]{1,0:T(8,128)(2,1)S(1)}) fusion(bf16[896,256]{1,0:T(8,128)(2,1)} %refs_0_.3), kind=kLoop, calls=%fused_computation.1 | loop fusion | bytes 917504 | tf_op jit(solution)/shard_map/slice | solution.py:277
  5.2 4.9 %collective-permute-start.2 = (bf16[448,256]{1,0:T(8,128)(2,1)S(1)}, bf16[448,256]{1,0:T(8,128)(2,1)S(1)}, u32[]{:S(2)}, u32[]{:S(2)}) collective-permute-start(bf16[448,256]{1,0:T(8,128)(2,1)S(1)} %get-tuple-element.43), channel_id=1, source_target_pairs={{0,7},{1,2},{2,1},{3,4},{4,3},{5,6},{6,5},{7,0},{8,15},{9,10},{10,... | collective-permute-start | bytes 688136 | tf_op jit(solution)/shard_map/ppermute | solution.py:269
  10.1 0.0 copy-start.7
  10.1 0.0 copy-start.4
  10.2 0.0 copy-start.5
  10.2 0.0 copy-start.6
  10.2 2.1 %collective-permute-start.1 = (bf16[448,256]{1,0:T(8,128)(2,1)S(1)}, bf16[448,256]{1,0:T(8,128)(2,1)S(1)}, u32[]{:S(2)}, u32[]{:S(2)}) collective-permute-start(bf16[448,256]{1,0:T(8,128)(2,1)S(1)} %get-tuple-element.44), channel_id=1, source_target_pairs={{0,7},{1,2},{2,1},{3,4},{4,3},{5,6},{6,5},{7,0},{8,15},{9,10},{10,... | collective-permute-start | bytes 688136 | tf_op jit(solution)/shard_map/ppermute | solution.py:269
  12.2 0.0 collective-permute-done.refs_1_.refs_0_
  12.2 7.3 %collective-permute-start.5 = (bf16[896,256]{1,0:T(8,128)(2,1)S(1)}, bf16[896,256]{1,0:T(8,128)(2,1)S(1)}, u32[]{:S(2)}, u32[]{:S(2)}) collective-permute-start(bf16[896,256]{1,0:T(8,128)(2,1)S(1)} %collective-permute-done.refs_1_.refs_0_), channel_id=1, source_target_pairs={{0,7},{1,2},{2,1},{3,4},{4,3},{5,6},{6,5},{7,0},{8,15},{9,10},{10,... | collective-permute-start | bytes 1376264 | tf_op jit(solution)/shard_map/ppermute | solution.py:269
  19.5 0.0 collective-permute-done.2.refs_3_.refs_2_
  19.5 1.9 %collective-permute-start.4 = (bf16[448,256]{1,0:T(8,128)(2,1)S(1)}, bf16[448,256]{1,0:T(8,128)(2,1)S(1)}, u32[]{:S(2)}, u32[]{:S(2)}) collective-permute-start(bf16[448,256]{1,0:T(8,128)(2,1)S(1)} %collective-permute-done.2.refs_3_.refs_2_), channel_id=1, source_target_pairs={{0,1},{1,0},{2,3},{3,2},{4,5},{5,4},{6,7},{7,6},{8,9},{9,8},{10,11... | collective-permute-start | bytes 688136 | tf_op jit(solution)/shard_map/ppermute | solution.py:266
  21.5 0.0 collective-permute-done.1.refs_2_.refs_1_
  21.5 3.4 %collective-permute-start.3 = (bf16[448,256]{1,0:T(8,128)(2,1)S(1)}, bf16[448,256]{1,0:T(8,128)(2,1)S(1)}, u32[]{:S(2)}, u32[]{:S(2)}) collective-permute-start(bf16[448,256]{1,0:T(8,128)(2,1)S(1)} %collective-permute-done.1.refs_2_.refs_1_), channel_id=1, source_target_pairs={{0,1},{1,0},{2,3},{3,2},{4,5},{5,4},{6,7},{7,6},{8,9},{9,8},{10,11... | collective-permute-start | bytes 688136 | tf_op jit(solution)/shard_map/ppermute | solution.py:266
  24.9 0.0 copy-done.3
  24.9 0.0 copy-done.7
  24.9 0.0 copy-done.4
  24.9 0.0 copy-done.5
  24.9 0.0 copy-done.6
  24.9 0.7 tables.1
  25.6 0.0 copy-done
  25.6 0.6 coulomb_pairs.2
  26.3 5.5 %collective-permute-start.6 = (bf16[3,2,128,128]{3,2,1,0:T(8,128)(2,1)S(1)}, bf16[3,2,128,128]{3,2,1,0:T(8,128)(2,1)S(1)}, u32[]{:S(2)}, u32[]{:S(2)}) collective-permute-start(bf16[3,2,128,128]{3,2,1,0:T(8,128)(2,1)S(1)} %get-tuple-element.29), channel_id=1, source_target_pairs={{0,8},{8,0},{1,9},{9,1},{2,10},{10,2},{3,11},{11,3},{4,12},{12,4},... | collective-permute-start | bytes 589832 | tf_op jit(solution)/shard_map/ppermute | solution.py:272
  31.8 0.0 collective-permute-done.4.refs_4_.refs_5_
  31.8 0.0 collective-permute-done.3.refs_3_.refs_4_
  31.8 0.0 collective-permute-done.5.refs_5_.refs_6_
  31.8 0.5 coulomb_pairs.3
  32.3 4.5 %collective-permute-start.7 = (bf16[2,2,128,128]{3,2,1,0:T(8,128)(2,1)S(1)}, bf16[2,2,128,128]{3,2,1,0:T(8,128)(2,1)S(1)}, u32[]{:S(2)}, u32[]{:S(2)}) collective-permute-start(bf16[2,2,128,128]{3,2,1,0:T(8,128)(2,1)S(1)} %get-tuple-element.30), channel_id=1, source_target_pairs={{0,8},{8,0},{1,9},{9,1},{2,10},{10,2},{3,11},{11,3},{4,12},{12,4},... | collective-permute-start | bytes 393224 | tf_op jit(solution)/shard_map/ppermute | solution.py:272
  36.8 0.0 collective-permute-done.6.refs_2_
  36.8 1.0 collective-permute-done.7.refs_3_
  37.8 0.8 sum_cores.1
  38.6 12.9 %all-to-all-start = ((bf16[32,40,128]{2,1,0:T(8,128)(2,1)}), bf16[32,40,128]{2,1,0:T(8,128)(2,1)S(1)}, u32[]{:S(2)}, u32[]{:S(2)}) async-start(bf16[32,40,128]{2,1,0:T(8,128)(2,1)} %sum_cores.1), calls=%async_computation | async-start | bytes 655360 | tf_op jit(solution)/shard_map/all_to_all | solution.py:291
  51.4 0.8 pad_maximum_fusion
  52.2 2.6 %collective-permute-start.9 = (bf16[896,256]{1,0:T(8,128)(2,1)}, bf16[896,256]{1,0:T(8,128)(2,1)S(1)}, u32[]{:S(2)}, u32[]{:S(2)}) collective-permute-start(bf16[896,256]{1,0:T(8,128)(2,1)} %pad_maximum_fusion), channel_id=1, source_target_pairs={{0,7},{1,2},{2,1},{3,4},{4,3},{5,6},{6,5},{7,0},{8,15},{9,10},{10,... | collective-permute-start | bytes 1376264 | tf_op jit(solution)/shard_map/ppermute | solution.py:269
  54.8 3.0 %collective-permute-start.8 = (bf16[896,256]{1,0:T(8,128)(2,1)S(1)}, bf16[896,256]{1,0:T(8,128)(2,1)}, u32[]{:S(2)}, u32[]{:S(2)}) collective-permute-start(bf16[896,256]{1,0:T(8,128)(2,1)S(1)} %collective-permute-done.5.refs_5_.refs_6_), channel_id=1, source_target_pairs={{0,1},{1,0},{2,3},{3,2},{4,5},{5,4},{6,7},{7,6},{8,9},{9,8},{10,11... | collective-permute-start | bytes 1376264 | tf_op jit(solution)/shard_map/ppermute | solution.py:266
  57.8 6.4 %all-to-all-done.parts_ref = bf16[32,40,128]{2,1,0:T(8,128)(2,1)S(1)} async-done(((bf16[32,40,128]{2,1,0:T(8,128)(2,1)}), bf16[32,40,128]{2,1,0:T(8,128)(2,1)S(1)}, u32[]{:S(2)}, u32[]{:S(2)}) %all-to-all-start) | async-done | bytes 327712 | tf_op jit(solution)/shard_map/all_to_all | solution.py:291
  64.3 10.6 %all_to_all.15.received_ref = bf16[8,16,128]{2,1,0:T(8,128)(2,1)S(1)} all-to-all(bf16[8,16,128]{2,1,0:T(8,128)(2,1)S(1)} %amplitude_sends.1), channel_id=1, replica_groups=mesh['x'=4,'z'=8,'core'=2,'pair'=8] {'pair'}, dimensions={0} | all-to-all | bytes 65536 | tf_op jit(solution)/shard_map/all_to_all | solution.py:292
  74.8 0.9 amplitude_copies.1
  75.8 0.0 collective-permute-done.9.refs_8_
  75.8 0.0 collective-permute-done.8.refs_7_
  75.8 5.3 %all-to-all-start.2 = ((bf16[32,64,128]{2,1,0:T(8,128)(2,1)}), bf16[32,64,128]{2,1,0:T(8,128)(2,1)S(1)}, u32[]{:S(2)}, u32[]{:S(2)}) async-start(bf16[32,64,128]{2,1,0:T(8,128)(2,1)} %amplitude_copies.1), calls=%async_computation.2 | async-start | bytes 1048576 | tf_op jit(solution)/shard_map/all_to_all | solution.py:297
  81.0 1.0 slice.14
  82.0 3.1 %collective-permute-start.11 = (bf16[448,256]{1,0:T(8,128)(2,1)S(1)}, bf16[448,256]{1,0:T(8,128)(2,1)S(1)}, u32[]{:S(2)}, u32[]{:S(2)}) collective-permute-start(bf16[448,256]{1,0:T(8,128)(2,1)S(1)} %slice.15), channel_id=1, source_target_pairs={{0,1},{1,0},{2,3},{3,2},{4,5},{5,4},{6,7},{7,6},{8,9},{9,8},{10,11... | collective-permute-start | bytes 688136 | tf_op jit(solution)/shard_map/ppermute | solution.py:266
  85.2 2.0 %collective-permute-start.10 = (bf16[448,256]{1,0:T(8,128)(2,1)S(1)}, bf16[448,256]{1,0:T(8,128)(2,1)S(1)}, u32[]{:S(2)}, u32[]{:S(2)}) collective-permute-start(bf16[448,256]{1,0:T(8,128)(2,1)S(1)} %slice.14), channel_id=1, source_target_pairs={{0,7},{1,2},{2,1},{3,4},{4,3},{5,6},{6,5},{7,0},{8,15},{9,10},{10,... | collective-permute-start | bytes 688136 | tf_op jit(solution)/shard_map/ppermute | solution.py:269
  87.2 1.8 %collective-permute-done.11.refs_10_ = bf16[448,256]{1,0:T(8,128)(2,1)S(1)} collective-permute-done((bf16[448,256]{1,0:T(8,128)(2,1)S(1)}, bf16[448,256]{1,0:T(8,128)(2,1)S(1)}, u32[]{:S(2)}, u32[]{:S(2)}) %collective-permute-start.11) | collective-permute-done | bytes 229408 | tf_op jit(solution)/shard_map/ppermute | solution.py:266
  89.0 4.5 %collective-permute-done.10.refs_9_ = bf16[448,256]{1,0:T(8,128)(2,1)S(1)} collective-permute-done((bf16[448,256]{1,0:T(8,128)(2,1)S(1)}, bf16[448,256]{1,0:T(8,128)(2,1)S(1)}, u32[]{:S(2)}, u32[]{:S(2)}) %collective-permute-start.10) | collective-permute-done | bytes 229408 | tf_op jit(solution)/shard_map/ppermute | solution.py:269
  93.4 0.0 copy-start.1
  93.4 0.7 copy-done.1
  94.1 1.3 %all-to-all-done.2.refs_11_ = bf16[32,64,128]{2,1,0:T(8,128)(2,1)S(1)} async-done(((bf16[32,64,128]{2,1,0:T(8,128)(2,1)}), bf16[32,64,128]{2,1,0:T(8,128)(2,1)S(1)}, u32[]{:S(2)}, u32[]{:S(2)}) %all-to-all-start.2) | async-done | bytes 524320 | tf_op jit(solution)/shard_map/all_to_all | solution.py:297
  95.4 6.5 %collective-permute-start.12 = (bf16[32,64,128]{2,1,0:T(8,128)(2,1)S(1)}, bf16[32,64,128]{2,1,0:T(8,128)(2,1)S(1)}, u32[]{:S(2)}, u32[]{:S(2)}) collective-permute-start(bf16[32,64,128]{2,1,0:T(8,128)(2,1)S(1)} %all-to-all-done.2.refs_11_), channel_id=1, source_target_pairs={{0,8},{8,0},{1,9},{9,1},{2,10},{10,2},{3,11},{11,3},{4,12},{12,4},... | collective-permute-start | bytes 1572872 | tf_op jit(solution)/shard_map/ppermute | solution.py:272
  101.9 1.5 %collective-permute-done.12.refs_12_ = bf16[32,64,128]{2,1,0:T(8,128)(2,1)S(1)} collective-permute-done((bf16[32,64,128]{2,1,0:T(8,128)(2,1)S(1)}, bf16[32,64,128]{2,1,0:T(8,128)(2,1)S(1)}, u32[]{:S(2)}, u32[]{:S(2)}) %collective-permute-start.12) | collective-permute-done | bytes 524320 | tf_op jit(solution)/shard_map/ppermute | solution.py:272
  103.4 0.0 copy-start.2
  103.4 0.9 copy-done.2
  104.4 2.8 %gamma_rows.1 = bf16[896,256]{1,0:T(8,128)(2,1)} custom-call(bf16[896,256]{1,0:T(8,128)(2,1)S(1)} %copy-done, bf16[896,256]{1,0:T(8,128)(2,1)S(1)} %collective-permute-done.refs_1_.refs_0_, bf16[448,256]{1,0:T(8,128)(2,1)S(1)} %collective-permute-done.1.refs_2_.refs_1_, bf16[448,256]{1,0:T(8,128)(2,1)S(1)} %collective-permute-done.2.refs_3_.refs_2_, ...), custom_call_target="tpu_custom_call" | custom-call | tf_op jit(solution)/shard_map/gamma_rows/pallas_call | solution.py:247
  (2 shorter events, 0.1 us)
Async XLA Ops:
  0.0 25.6 %copy-start = (bf16[896,256]{1,0:T(8,128)(2,1)S(1)}, bf16[896,256]{1,0:T(8,128)(2,1)}, u32[]{:S(2)}) copy-start(bf16[896,256]{1,0:T(8,128)(2,1)} %refs_0_.3) | copy-start | bytes 1376260
  0.0 24.9 %copy-start.3 = (f32[20096]{0:T(1024)S(1)}, f32[20096]{0:T(1024)}, u32[]{:S(2)}) copy-start(f32[20096]{0:T(1024)} %param.8) | copy-start | bytes 241156
  0.0 12.2 %collective-permute-start = (bf16[896,256]{1,0:T(8,128)(2,1)}, bf16[896,256]{1,0:T(8,128)(2,1)S(1)}, u32[]{:S(2)}, u32[]{:S(2)}) collective-permute-start(bf16[896,256]{1,0:T(8,128)(2,1)} %refs_0_.3), channel_id=1, source_target_pairs={{0,1},{1,0},{2,3},{3,2},{4,5},{5,4},{6,7},{7,6},{8,9},{9,8},{10,11... | collective-permute-start | bytes 1376264 | tf_op jit(solution)/shard_map/ppermute | solution.py:266
  5.2 14.3 %collective-permute-start.2 = (bf16[448,256]{1,0:T(8,128)(2,1)S(1)}, bf16[448,256]{1,0:T(8,128)(2,1)S(1)}, u32[]{:S(2)}, u32[]{:S(2)}) collective-permute-start(bf16[448,256]{1,0:T(8,128)(2,1)S(1)} %get-tuple-element.43), channel_id=1, source_target_pairs={{0,7},{1,2},{2,1},{3,4},{4,3},{5,6},{6,5},{7,0},{8,15},{9,10},{10,... | collective-permute-start | bytes 688136 | tf_op jit(solution)/shard_map/ppermute | solution.py:269
  10.1 14.7 %copy-start.7 = (s32[16]{0:T(128)S(1)}, s32[16]{0:T(128)}, u32[]{:S(2)}) copy-start(s32[16]{0:T(128)} %exponent.1) | copy-start | bytes 196
  10.1 14.7 %copy-start.4 = (f32[64]{0:T(128)S(1)}, f32[64]{0:T(128)}, u32[]{:S(2)}) copy-start(f32[64]{0:T(128)} %occupied.1) | copy-start | bytes 772
  10.2 14.7 %copy-start.5 = (s32[16]{0:T(128)S(1)}, s32[16]{0:T(128)}, u32[]{:S(2)}) copy-start(s32[16]{0:T(128)} %occupied_of.1) | copy-start | bytes 196
  10.2 14.7 %copy-start.6 = (s32[16]{0:T(128)S(1)}, s32[16]{0:T(128)}, u32[]{:S(2)}) copy-start(s32[16]{0:T(128)} %virtual_of.1) | copy-start | bytes 196
  10.2 11.3 %collective-permute-start.1 = (bf16[448,256]{1,0:T(8,128)(2,1)S(1)}, bf16[448,256]{1,0:T(8,128)(2,1)S(1)}, u32[]{:S(2)}, u32[]{:S(2)}) collective-permute-start(bf16[448,256]{1,0:T(8,128)(2,1)S(1)} %get-tuple-element.44), channel_id=1, source_target_pairs={{0,7},{1,2},{2,1},{3,4},{4,3},{5,6},{6,5},{7,0},{8,15},{9,10},{10,... | collective-permute-start | bytes 688136 | tf_op jit(solution)/shard_map/ppermute | solution.py:269
  12.2 19.5 %collective-permute-start.5 = (bf16[896,256]{1,0:T(8,128)(2,1)S(1)}, bf16[896,256]{1,0:T(8,128)(2,1)S(1)}, u32[]{:S(2)}, u32[]{:S(2)}) collective-permute-start(bf16[896,256]{1,0:T(8,128)(2,1)S(1)} %collective-permute-done.refs_1_.refs_0_), channel_id=1, source_target_pairs={{0,7},{1,2},{2,1},{3,4},{4,3},{5,6},{6,5},{7,0},{8,15},{9,10},{10,... | collective-permute-start | bytes 1376264 | tf_op jit(solution)/shard_map/ppermute | solution.py:269
  19.5 12.2 %collective-permute-start.4 = (bf16[448,256]{1,0:T(8,128)(2,1)S(1)}, bf16[448,256]{1,0:T(8,128)(2,1)S(1)}, u32[]{:S(2)}, u32[]{:S(2)}) collective-permute-start(bf16[448,256]{1,0:T(8,128)(2,1)S(1)} %collective-permute-done.2.refs_3_.refs_2_), channel_id=1, source_target_pairs={{0,1},{1,0},{2,3},{3,2},{4,5},{5,4},{6,7},{7,6},{8,9},{9,8},{10,11... | collective-permute-start | bytes 688136 | tf_op jit(solution)/shard_map/ppermute | solution.py:266
  21.5 10.3 %collective-permute-start.3 = (bf16[448,256]{1,0:T(8,128)(2,1)S(1)}, bf16[448,256]{1,0:T(8,128)(2,1)S(1)}, u32[]{:S(2)}, u32[]{:S(2)}) collective-permute-start(bf16[448,256]{1,0:T(8,128)(2,1)S(1)} %collective-permute-done.1.refs_2_.refs_1_), channel_id=1, source_target_pairs={{0,1},{1,0},{2,3},{3,2},{4,5},{5,4},{6,7},{7,6},{8,9},{9,8},{10,11... | collective-permute-start | bytes 688136 | tf_op jit(solution)/shard_map/ppermute | solution.py:266
  26.3 10.6 %collective-permute-start.6 = (bf16[3,2,128,128]{3,2,1,0:T(8,128)(2,1)S(1)}, bf16[3,2,128,128]{3,2,1,0:T(8,128)(2,1)S(1)}, u32[]{:S(2)}, u32[]{:S(2)}) collective-permute-start(bf16[3,2,128,128]{3,2,1,0:T(8,128)(2,1)S(1)} %get-tuple-element.29), channel_id=1, source_target_pairs={{0,8},{8,0},{1,9},{9,1},{2,10},{10,2},{3,11},{11,3},{4,12},{12,4},... | collective-permute-start | bytes 589832 | tf_op jit(solution)/shard_map/ppermute | solution.py:272
  32.3 5.5 %collective-permute-start.7 = (bf16[2,2,128,128]{3,2,1,0:T(8,128)(2,1)S(1)}, bf16[2,2,128,128]{3,2,1,0:T(8,128)(2,1)S(1)}, u32[]{:S(2)}, u32[]{:S(2)}) collective-permute-start(bf16[2,2,128,128]{3,2,1,0:T(8,128)(2,1)S(1)} %get-tuple-element.30), channel_id=1, source_target_pairs={{0,8},{8,0},{1,9},{9,1},{2,10},{10,2},{3,11},{11,3},{4,12},{12,4},... | collective-permute-start | bytes 393224 | tf_op jit(solution)/shard_map/ppermute | solution.py:272
  38.6 25.6 %all-to-all-start = ((bf16[32,40,128]{2,1,0:T(8,128)(2,1)}), bf16[32,40,128]{2,1,0:T(8,128)(2,1)S(1)}, u32[]{:S(2)}, u32[]{:S(2)}) async-start(bf16[32,40,128]{2,1,0:T(8,128)(2,1)} %sum_cores.1), calls=%async_computation | async-start | bytes 655360 | tf_op jit(solution)/shard_map/all_to_all | solution.py:291
  52.2 23.5 %collective-permute-start.9 = (bf16[896,256]{1,0:T(8,128)(2,1)}, bf16[896,256]{1,0:T(8,128)(2,1)S(1)}, u32[]{:S(2)}, u32[]{:S(2)}) collective-permute-start(bf16[896,256]{1,0:T(8,128)(2,1)} %pad_maximum_fusion), channel_id=1, source_target_pairs={{0,7},{1,2},{2,1},{3,4},{4,3},{5,6},{6,5},{7,0},{8,15},{9,10},{10,... | collective-permute-start | bytes 1376264 | tf_op jit(solution)/shard_map/ppermute | solution.py:269
  54.8 20.9 %collective-permute-start.8 = (bf16[896,256]{1,0:T(8,128)(2,1)S(1)}, bf16[896,256]{1,0:T(8,128)(2,1)}, u32[]{:S(2)}, u32[]{:S(2)}) collective-permute-start(bf16[896,256]{1,0:T(8,128)(2,1)S(1)} %collective-permute-done.5.refs_5_.refs_6_), channel_id=1, source_target_pairs={{0,1},{1,0},{2,3},{3,2},{4,5},{5,4},{6,7},{7,6},{8,9},{9,8},{10,11... | collective-permute-start | bytes 1376264 | tf_op jit(solution)/shard_map/ppermute | solution.py:266
  75.8 19.6 %all-to-all-start.2 = ((bf16[32,64,128]{2,1,0:T(8,128)(2,1)}), bf16[32,64,128]{2,1,0:T(8,128)(2,1)S(1)}, u32[]{:S(2)}, u32[]{:S(2)}) async-start(bf16[32,64,128]{2,1,0:T(8,128)(2,1)} %amplitude_copies.1), calls=%async_computation.2 | async-start | bytes 1048576 | tf_op jit(solution)/shard_map/all_to_all | solution.py:297
  82.0 7.0 %collective-permute-start.11 = (bf16[448,256]{1,0:T(8,128)(2,1)S(1)}, bf16[448,256]{1,0:T(8,128)(2,1)S(1)}, u32[]{:S(2)}, u32[]{:S(2)}) collective-permute-start(bf16[448,256]{1,0:T(8,128)(2,1)S(1)} %slice.15), channel_id=1, source_target_pairs={{0,1},{1,0},{2,3},{3,2},{4,5},{5,4},{6,7},{7,6},{8,9},{9,8},{10,11... | collective-permute-start | bytes 688136 | tf_op jit(solution)/shard_map/ppermute | solution.py:266
  85.2 8.3 %collective-permute-start.10 = (bf16[448,256]{1,0:T(8,128)(2,1)S(1)}, bf16[448,256]{1,0:T(8,128)(2,1)S(1)}, u32[]{:S(2)}, u32[]{:S(2)}) collective-permute-start(bf16[448,256]{1,0:T(8,128)(2,1)S(1)} %slice.14), channel_id=1, source_target_pairs={{0,7},{1,2},{2,1},{3,4},{4,3},{5,6},{6,5},{7,0},{8,15},{9,10},{10,... | collective-permute-start | bytes 688136 | tf_op jit(solution)/shard_map/ppermute | solution.py:269
  93.4 0.7 copy-start.1
  95.4 8.0 %collective-permute-start.12 = (bf16[32,64,128]{2,1,0:T(8,128)(2,1)S(1)}, bf16[32,64,128]{2,1,0:T(8,128)(2,1)S(1)}, u32[]{:S(2)}, u32[]{:S(2)}) collective-permute-start(bf16[32,64,128]{2,1,0:T(8,128)(2,1)S(1)} %all-to-all-done.2.refs_11_), channel_id=1, source_target_pairs={{0,8},{8,0},{1,9},{9,1},{2,10},{10,2},{3,11},{11,3},{4,12},{12,4},... | collective-permute-start | bytes 1572872 | tf_op jit(solution)/shard_map/ppermute | solution.py:272
  103.4 0.9 copy-start.2

commit v19 on v18

--- a/solution.py
+++ b/solution.py
@@ -20,7 +20,6 @@
 GETS = tuple((PAIRS[k][0] - d, PAIRS[k][1] - d) for d, pairs in SENDS for k in pairs)
 ORDER = tuple((r, False) if c == 0 else (c, True) for r, c in GETS)
 ROWS = 224
-FETCHED = (("A", 3),)
 VMEM_LIMIT = 12 * 1024 * 1024
 bf16, f32 = jnp.bfloat16, jnp.float32
 in_vmem = pl.BlockSpec(memory_space=pltpu.VMEM)
@@ -189,7 +188,47 @@
     )(received)
 
 
-def gamma_rows(blocks, mine, theirs, scales):
+def lay_out(source, part, scale, matrix):
+    even = lax.rem(lax.axis_index("pair"), 2) == 0
+    place = pl.ds(pl.multiple_of(part * TS, TS), TS)
+    for pair in range(0, len(ORDER), 2):
+        both = source[:, pair * PIECE : (pair + 2) * PIECE].astype(f32)
+        for k in (0, 1):
+            i = pair + k
+            q, transposed = ORDER[i]
+            held = jnp.where(even, HELD.index(held_name(q, 0)), HELD.index(held_name(q, 1)))
+            tiles = both[:, k * PIECE : (k + 1) * PIECE].reshape(2, TS, TS)
+            for h in (0, 1):
+                if transposed:
+                    tile = tiles[h].T * scale[2 * i + h : 2 * i + h + 1]
+                    matrix[held, h * TS : (h + 1) * TS, place] = tile.astype(bf16)
+                else:
+                    tile = tiles[h] * scale[pl.ds(2 * i + part, 1)]
+                    matrix[held, place, h * TS : (h + 1) * TS] = tile.astype(bf16)
+
+
+def own_half(mine, scales, far):
+    def kernel(mine_ref, scale, far_ref, matrix, near, arrived):
+        fetch = pltpu.make_async_copy(far_ref, near, arrived)
+        fetch.start()
+        lay_out(mine_ref, lax.axis_index("core"), scale, matrix)
+        fetch.wait()
+
+    return pl.pallas_call(
+        kernel,
+        out_shape=(
+            jax.ShapeDtypeStruct((len(HELD), WIDTH, WIDTH), bf16),
+            jax.ShapeDtypeStruct(far.shape, far.dtype),
+        ),
+        in_specs=[in_vmem, in_vmem, anywhere],
+        out_specs=(in_vmem, in_vmem),
+        scratch_shapes=[pltpu.SemaphoreType.DMA],
+        compiler_params=pltpu.CompilerParams(vmem_limit_bytes=VMEM_LIMIT),
+        name="own_half",
+    )(mine, scales, far)
+
+
+def gamma_rows(blocks, half, theirs, scales):
     rows, width = blocks[0][0].shape
     counts = [len(blocks[n]) for n in HELD]
 
@@ -199,66 +238,29 @@
         for count in counts:
             block.append(given[:count])
             given = given[count:]
-        own, other, scale, out, matrix, held, arrived, sums = refs[sum(counts) :]
-        fetches = []
-        for k, name in enumerate(FETCHED):
-            i = HELD.index(name)
-            fetches.append(pltpu.make_async_copy(block[i][0], held.at[k], arrived.at[k]))
-            block[i] = [held.at[k]]
-        for fetch in fetches:
-            fetch.start()
-        core = lax.axis_index("core")
-        even = lax.rem(lax.axis_index("pair"), 2) == 0
-        for pair in range(0, len(ORDER), 2):
-            for part, source in ((core, own), (1 - core, other)):
-                place = pl.ds(pl.multiple_of(part * TS, TS), TS)
-                both = source[:, pair * PIECE : (pair + 2) * PIECE].astype(f32)
-                for k in (0, 1):
-                    i = pair + k
-                    q, transposed = ORDER[i]
-                    held = jnp.where(even, HELD.index(held_name(q, 0)), HELD.index(held_name(q, 1)))
-                    tiles = both[:, k * PIECE : (k + 1) * PIECE].reshape(2, TS, TS)
-                    for h in (0, 1):
-                        if transposed:
-                            tile = tiles[h].T * scale[2 * i + h : 2 * i + h + 1]
-                            matrix[held, h * TS : (h + 1) * TS, place] = tile.astype(bf16)
-                        else:
-                            tile = tiles[h] * scale[pl.ds(2 * i + part, 1)]
-                            matrix[held, place, h * TS : (h + 1) * TS] = tile.astype(bf16)
-
-        def product(indices, start):
+        _, other, scale, out, matrix = refs[sum(counts) :]
+        lay_out(other, 1 - lax.axis_index("core"), scale, matrix)
+        for start in range(0, rows, ROWS):
             total = None
-            for i in indices:
-                part, offset = divmod(start, rows // len(block[i]))
-                left = block[i][part][offset : offset + ROWS]
+            for i, parts in enumerate(block):
+                part, offset = divmod(start, rows // len(parts))
+                left = parts[part][offset : offset + ROWS]
                 term = jnp.dot(left, matrix[i], preferred_element_type=f32)
                 total = term if total is None else total + term
-            return total
-
-        last = [i for i, name in enumerate(HELD) if name in FETCHED]
-        for start in range(0, rows, ROWS):
-            sums[start : start + ROWS] = product([i for i in range(len(HELD)) if i not in last], start)
-        for fetch in fetches:
-            fetch.wait()
-        for start in range(0, rows, ROWS):
-            total = sums[start : start + ROWS] + product(last, start)
             out[start : start + ROWS] = total.astype(bf16)
 
     return pl.pallas_call(
         kernel,
-        out_shape=jax.ShapeDtypeStruct((rows, width), bf16),
-        in_specs=[anywhere if n in FETCHED else in_vmem for n in HELD for _ in blocks[n]]
-        + [in_vmem] * 3,
-        out_specs=in_vmem,
-        scratch_shapes=[
-            pltpu.VMEM((len(HELD), WIDTH, WIDTH), bf16),
-            pltpu.VMEM((len(FETCHED), rows, width), bf16),
-            pltpu.SemaphoreType.DMA((len(FETCHED),)),
-            pltpu.VMEM((rows, width), f32),
-        ],
+        out_shape=(
+            jax.ShapeDtypeStruct((rows, width), bf16),
+            jax.ShapeDtypeStruct(half.shape, half.dtype),
+        ),
+        in_specs=[in_vmem] * (sum(counts) + 3),
+        out_specs=(in_vmem, in_vmem),
+        input_output_aliases={sum(counts): 1},
         compiler_params=pltpu.CompilerParams(vmem_limit_bytes=VMEM_LIMIT),
         name="gamma_rows",
-    )(*[part for n in HELD for part in blocks[n]], mine, theirs, scales)
+    )(*[part for n in HELD for part in blocks[n]], half, theirs, scales)[0]
 
 
 def body(three_index, *energies):
@@ -297,7 +299,10 @@
     mine = lax.all_to_all(copies, ("z", "x"), 0, 0)
     mine, b4 = lax.optimization_barrier((mine, b4))
     block.update({("B", 2): b2, ("A", 2): a2, ("A", 3): [a3], ("B", 3): [b3], ("B", 4): b4})
-    return gamma_rows(block, mine, swap_cores(mine), scales)
+    theirs = swap_cores(mine)
+    half, a3 = own_half(mine, scales, a3)
+    block["A", 3] = [a3]
+    return gamma_rows(block, half, theirs, scales)
 
 
 def solution(mesh):

time: 108 us -> 106 us (0.981)
  waiting for transfers between devices: 16.4 us -> 15.3 us
    pallas_call x1 -> x2, Pallas kernels: 2.79 us -> 3.17 us  [the longest x1 2.11 us: gamma_rows(): pl.pallas_call(kernel, out_shape=(jax.ShapeDtypeStruct((rows, width), bf1...]
  transfers between devices with their start and end apart: 15 -> 15, of which waited for: 6 -> 6; matrix products, arithmetic and copies ran while one was open for 3% -> 3% of each run, Pallas kernels for 3% -> 4%
where the time goes in v19:
time: 106 us
  starting transfers between devices  69.1 us (65%)
  waiting for transfers between devices  15.3 us (14%)
  blocking collectives  10.6 us (10%)
  Pallas kernels  6.78 us (6%)
  local copies, waits for them, and re-layouts  2.78 us (3%)
    ppermute x5, starting transfers between devices, swap_b(): return lax.ppermute(x, 'pair', SWAP_B)  18.8 us
    ppermute x3, starting transfers between devices, swap_cores(): return lax.ppermute(x, 'core', SWAP_CORES)  16.7 us
    ppermute x5, starting transfers between devices, swap_a(): return lax.ppermute(x, 'pair', SWAP_A)  15.6 us
    all_to_all x1, starting transfers between devices, body(): parts = lax.all_to_all(summed, ('z', 'x'), 0, 0)  12.9 us
    all_to_all x1, blocking collectives, body(): received = lax.all_to_all(amplitude_sends(parts, denominator), 'pair', 0, 0)  10.6 us
    all_to_all x1, waiting for transfers between devices, body(): parts = lax.all_to_all(summed, ('z', 'x'), 0, 0)  6.39 us
    all_to_all x1, starting transfers between devices, body(): mine = lax.all_to_all(copies, ('z', 'x'), 0, 0)  5.25 us
    ppermute x5, waiting for transfers between devices, swap_b(): return lax.ppermute(x, 'pair', SWAP_B)  4.47 us
  transfers between devices with their start and end apart: 15, of which 6 were waited for; matrix products, arithmetic and copies ran while one was open for 3% of the time, Pallas kernels for 4%

profile of v19, /device:TPU:1, one launch (start us, length us, event | category | flops | bytes accessed | tf_op | source)
XLA Modules:
  0.0 105.7 jit_solution(3438509483725556598)
XLA Ops:
  0.0 0.0 copy-start
  0.0 0.0 copy-start.3
  0.0 4.2 %collective-permute-start = (bf16[896,256]{1,0:T(8,128)(2,1)}, bf16[896,256]{1,0:T(8,128)(2,1)S(1)}, u32[]{:S(2)}, u32[]{:S(2)}) collective-permute-start(bf16[896,256]{1,0:T(8,128)(2,1)} %refs_0_.3), channel_id=1, source_target_pairs={{0,1},{1,0},{2,3},{3,2},{4,5},{5,4},{6,7},{7,6},{8,9},{9,8},{10,11... | collective-permute-start | bytes 1376264 | tf_op jit(solution)/shard_map/ppermute | solution.py:268
  4.2 1.1 %fusion = (bf16[448,256]{1,0:T(8,128)(2,1)S(1)}, bf16[448,256]{1,0:T(8,128)(2,1)S(1)}) fusion(bf16[896,256]{1,0:T(8,128)(2,1)} %refs_0_.3), kind=kLoop, calls=%fused_computation.1 | loop fusion | bytes 917504 | tf_op jit(solution)/shard_map/slice | solution.py:279
  5.2 4.9 %collective-permute-start.2 = (bf16[448,256]{1,0:T(8,128)(2,1)S(1)}, bf16[448,256]{1,0:T(8,128)(2,1)S(1)}, u32[]{:S(2)}, u32[]{:S(2)}) collective-permute-start(bf16[448,256]{1,0:T(8,128)(2,1)S(1)} %get-tuple-element.49), channel_id=1, source_target_pairs={{0,7},{1,2},{2,1},{3,4},{4,3},{5,6},{6,5},{7,0},{8,15},{9,10},{10,... | collective-permute-start | bytes 688136 | tf_op jit(solution)/shard_map/ppermute | solution.py:271
  10.1 0.0 copy-start.7
  10.1 0.0 copy-start.4
  10.2 0.0 copy-start.5
  10.2 0.0 copy-start.6
  10.2 2.1 %collective-permute-start.1 = (bf16[448,256]{1,0:T(8,128)(2,1)S(1)}, bf16[448,256]{1,0:T(8,128)(2,1)S(1)}, u32[]{:S(2)}, u32[]{:S(2)}) collective-permute-start(bf16[448,256]{1,0:T(8,128)(2,1)S(1)} %get-tuple-element.50), channel_id=1, source_target_pairs={{0,7},{1,2},{2,1},{3,4},{4,3},{5,6},{6,5},{7,0},{8,15},{9,10},{10,... | collective-permute-start | bytes 688136 | tf_op jit(solution)/shard_map/ppermute | solution.py:271
  12.2 0.0 collective-permute-done.refs_1_.refs_0_
  12.2 7.3 %collective-permute-start.5 = (bf16[896,256]{1,0:T(8,128)(2,1)S(1)}, bf16[896,256]{1,0:T(8,128)(2,1)S(1)}, u32[]{:S(2)}, u32[]{:S(2)}) collective-permute-start(bf16[896,256]{1,0:T(8,128)(2,1)S(1)} %collective-permute-done.refs_1_.refs_0_), channel_id=1, source_target_pairs={{0,7},{1,2},{2,1},{3,4},{4,3},{5,6},{6,5},{7,0},{8,15},{9,10},{10,... | collective-permute-start | bytes 1376264 | tf_op jit(solution)/shard_map/ppermute | solution.py:271
  19.5 0.0 collective-permute-done.2.refs_3_.refs_2_
  19.5 1.9 %collective-permute-start.4 = (bf16[448,256]{1,0:T(8,128)(2,1)S(1)}, bf16[448,256]{1,0:T(8,128)(2,1)S(1)}, u32[]{:S(2)}, u32[]{:S(2)}) collective-permute-start(bf16[448,256]{1,0:T(8,128)(2,1)S(1)} %collective-permute-done.2.refs_3_.refs_2_), channel_id=1, source_target_pairs={{0,1},{1,0},{2,3},{3,2},{4,5},{5,4},{6,7},{7,6},{8,9},{9,8},{10,11... | collective-permute-start | bytes 688136 | tf_op jit(solution)/shard_map/ppermute | solution.py:268
  21.5 0.0 collective-permute-done.1.refs_2_.refs_1_
  21.5 3.4 %collective-permute-start.3 = (bf16[448,256]{1,0:T(8,128)(2,1)S(1)}, bf16[448,256]{1,0:T(8,128)(2,1)S(1)}, u32[]{:S(2)}, u32[]{:S(2)}) collective-permute-start(bf16[448,256]{1,0:T(8,128)(2,1)S(1)} %collective-permute-done.1.refs_2_.refs_1_), channel_id=1, source_target_pairs={{0,1},{1,0},{2,3},{3,2},{4,5},{5,4},{6,7},{7,6},{8,9},{9,8},{10,11... | collective-permute-start | bytes 688136 | tf_op jit(solution)/shard_map/ppermute | solution.py:268
  24.9 0.0 copy-done.3
  24.9 0.0 copy-done.7
  24.9 0.0 copy-done.4
  24.9 0.0 copy-done.5
  24.9 0.0 copy-done.6
  24.9 0.7 tables.1
  25.6 0.0 copy-done
  25.6 0.6 coulomb_pairs.2
  26.3 5.5 %collective-permute-start.6 = (bf16[3,2,128,128]{3,2,1,0:T(8,128)(2,1)S(1)}, bf16[3,2,128,128]{3,2,1,0:T(8,128)(2,1)S(1)}, u32[]{:S(2)}, u32[]{:S(2)}) collective-permute-start(bf16[3,2,128,128]{3,2,1,0:T(8,128)(2,1)S(1)} %get-tuple-element.32), channel_id=1, source_target_pairs={{0,8},{8,0},{1,9},{9,1},{2,10},{10,2},{3,11},{11,3},{4,12},{12,4},... | collective-permute-start | bytes 589832 | tf_op jit(solution)/shard_map/ppermute | solution.py:274
  31.8 0.0 collective-permute-done.4.refs_4_.refs_5_
  31.8 0.0 collective-permute-done.3.refs_3_.refs_4_
  31.8 0.0 collective-permute-done.5.refs_5_.refs_6_
  31.8 0.5 coulomb_pairs.3
  32.3 4.5 %collective-permute-start.7 = (bf16[2,2,128,128]{3,2,1,0:T(8,128)(2,1)S(1)}, bf16[2,2,128,128]{3,2,1,0:T(8,128)(2,1)S(1)}, u32[]{:S(2)}, u32[]{:S(2)}) collective-permute-start(bf16[2,2,128,128]{3,2,1,0:T(8,128)(2,1)S(1)} %get-tuple-element.33), channel_id=1, source_target_pairs={{0,8},{8,0},{1,9},{9,1},{2,10},{10,2},{3,11},{11,3},{4,12},{12,4},... | collective-permute-start | bytes 393224 | tf_op jit(solution)/shard_map/ppermute | solution.py:274
  36.8 0.0 collective-permute-done.6.refs_2_
  36.8 1.0 collective-permute-done.7.refs_3_
  37.8 0.8 sum_cores.1
  38.6 12.9 %all-to-all-start = ((bf16[32,40,128]{2,1,0:T(8,128)(2,1)}), bf16[32,40,128]{2,1,0:T(8,128)(2,1)S(1)}, u32[]{:S(2)}, u32[]{:S(2)}) async-start(bf16[32,40,128]{2,1,0:T(8,128)(2,1)} %sum_cores.1), calls=%async_computation | async-start | bytes 655360 | tf_op jit(solution)/shard_map/all_to_all | solution.py:293
  51.4 0.8 pad_maximum_fusion
  52.2 2.6 %collective-permute-start.9 = (bf16[896,256]{1,0:T(8,128)(2,1)}, bf16[896,256]{1,0:T(8,128)(2,1)S(1)}, u32[]{:S(2)}, u32[]{:S(2)}) collective-permute-start(bf16[896,256]{1,0:T(8,128)(2,1)} %pad_maximum_fusion), channel_id=1, source_target_pairs={{0,7},{1,2},{2,1},{3,4},{4,3},{5,6},{6,5},{7,0},{8,15},{9,10},{10,... | collective-permute-start | bytes 1376264 | tf_op jit(solution)/shard_map/ppermute | solution.py:271
  54.8 3.0 %collective-permute-start.8 = (bf16[896,256]{1,0:T(8,128)(2,1)S(1)}, bf16[896,256]{1,0:T(8,128)(2,1)}, u32[]{:S(2)}, u32[]{:S(2)}) collective-permute-start(bf16[896,256]{1,0:T(8,128)(2,1)S(1)} %collective-permute-done.5.refs_5_.refs_6_), channel_id=1, source_target_pairs={{0,1},{1,0},{2,3},{3,2},{4,5},{5,4},{6,7},{7,6},{8,9},{9,8},{10,11... | collective-permute-start | bytes 1376264 | tf_op jit(solution)/shard_map/ppermute | solution.py:268
  57.8 6.4 %all-to-all-done.parts_ref = bf16[32,40,128]{2,1,0:T(8,128)(2,1)S(1)} async-done(((bf16[32,40,128]{2,1,0:T(8,128)(2,1)}), bf16[32,40,128]{2,1,0:T(8,128)(2,1)S(1)}, u32[]{:S(2)}, u32[]{:S(2)}) %all-to-all-start) | async-done | bytes 327712 | tf_op jit(solution)/shard_map/all_to_all | solution.py:293
  64.3 10.6 %all_to_all.15.received_ref = bf16[8,16,128]{2,1,0:T(8,128)(2,1)S(1)} all-to-all(bf16[8,16,128]{2,1,0:T(8,128)(2,1)S(1)} %amplitude_sends.1), channel_id=1, replica_groups=mesh['x'=4,'z'=8,'core'=2,'pair'=8] {'pair'}, dimensions={0} | all-to-all | bytes 65536 | tf_op jit(solution)/shard_map/all_to_all | solution.py:294
  74.8 0.9 amplitude_copies.1
  75.8 0.0 collective-permute-done.9.refs_8_
  75.8 0.0 collective-permute-done.8.far_ref
  75.8 5.3 %all-to-all-start.2 = ((bf16[32,64,128]{2,1,0:T(8,128)(2,1)}), bf16[32,64,128]{2,1,0:T(8,128)(2,1)S(1)}, u32[]{:S(2)}, u32[]{:S(2)}) async-start(bf16[32,64,128]{2,1,0:T(8,128)(2,1)} %amplitude_copies.1), calls=%async_computation.2 | async-start | bytes 1048576 | tf_op jit(solution)/shard_map/all_to_all | solution.py:299
  81.0 1.0 slice.14
  82.0 3.1 %collective-permute-start.11 = (bf16[448,256]{1,0:T(8,128)(2,1)S(1)}, bf16[448,256]{1,0:T(8,128)(2,1)S(1)}, u32[]{:S(2)}, u32[]{:S(2)}) collective-permute-start(bf16[448,256]{1,0:T(8,128)(2,1)S(1)} %slice.15), channel_id=1, source_target_pairs={{0,1},{1,0},{2,3},{3,2},{4,5},{5,4},{6,7},{7,6},{8,9},{9,8},{10,11... | collective-permute-start | bytes 688136 | tf_op jit(solution)/shard_map/ppermute | solution.py:268
  85.2 2.0 %collective-permute-start.10 = (bf16[448,256]{1,0:T(8,128)(2,1)S(1)}, bf16[448,256]{1,0:T(8,128)(2,1)S(1)}, u32[]{:S(2)}, u32[]{:S(2)}) collective-permute-start(bf16[448,256]{1,0:T(8,128)(2,1)S(1)} %slice.14), channel_id=1, source_target_pairs={{0,7},{1,2},{2,1},{3,4},{4,3},{5,6},{6,5},{7,0},{8,15},{9,10},{10,... | collective-permute-start | bytes 688136 | tf_op jit(solution)/shard_map/ppermute | solution.py:271
  87.2 1.8 %collective-permute-done.11.refs_10_ = bf16[448,256]{1,0:T(8,128)(2,1)S(1)} collective-permute-done((bf16[448,256]{1,0:T(8,128)(2,1)S(1)}, bf16[448,256]{1,0:T(8,128)(2,1)S(1)}, u32[]{:S(2)}, u32[]{:S(2)}) %collective-permute-start.11) | collective-permute-done | bytes 229408 | tf_op jit(solution)/shard_map/ppermute | solution.py:268
  89.0 4.5 %collective-permute-done.10.refs_9_ = bf16[448,256]{1,0:T(8,128)(2,1)S(1)} collective-permute-done((bf16[448,256]{1,0:T(8,128)(2,1)S(1)}, bf16[448,256]{1,0:T(8,128)(2,1)S(1)}, u32[]{:S(2)}, u32[]{:S(2)}) %collective-permute-start.10) | collective-permute-done | bytes 229408 | tf_op jit(solution)/shard_map/ppermute | solution.py:271
  93.5 0.0 copy-start.1
  93.5 0.7 copy-done.1
  94.1 1.3 %all-to-all-done.2.mine_ref = bf16[32,64,128]{2,1,0:T(8,128)(2,1)S(1)} async-done(((bf16[32,64,128]{2,1,0:T(8,128)(2,1)}), bf16[32,64,128]{2,1,0:T(8,128)(2,1)S(1)}, u32[]{:S(2)}, u32[]{:S(2)}) %all-to-all-start.2) | async-done | bytes 524320 | tf_op jit(solution)/shard_map/all_to_all | solution.py:299
  95.4 0.0 copy-start.2
  95.4 6.7 %collective-permute-start.12 = (bf16[32,64,128]{2,1,0:T(8,128)(2,1)S(1)}, bf16[32,64,128]{2,1,0:T(8,128)(2,1)S(1)}, u32[]{:S(2)}, u32[]{:S(2)}) collective-permute-start(bf16[32,64,128]{2,1,0:T(8,128)(2,1)S(1)} %all-to-all-done.2.mine_ref), channel_id=1, source_target_pairs={{0,8},{8,0},{1,9},{9,1},{2,10},{10,2},{3,11},{11,3},{4,12},{12,4},... | collective-permute-start | bytes 1572872 | tf_op jit(solution)/shard_map/ppermute | solution.py:274
  102.1 1.1 own_half.1
  103.1 0.5 collective-permute-done.12.refs_12_
  103.6 0.0 copy-done.2
  103.6 2.1 %gamma_rows.1 = (bf16[896,256]{1,0:T(8,128)(2,1)}, bf16[8,256,256]{2,1,0:T(8,128)(2,1)S(1)}) custom-call(bf16[896,256]{1,0:T(8,128)(2,1)S(1)} %copy-done, bf16[896,256]{1,0:T(8,128)(2,1)S(1)} %collective-permute-done.refs_1_.refs_0_, bf16[448,256]{1,0:T(8,128)(2,1)S(1)} %collective-permute-done.1.refs_2_.refs_1_, ...), custom_call_target="tpu_custom_call", output_to_operand_aliasing={{1}: (11, {})} | custom-call | tf_op jit(solution)/shard_map/gamma_rows/pallas_call | solution.py:252
  (2 shorter events, 0.1 us)
Async XLA Ops:
  0.0 25.6 %copy-start = (bf16[896,256]{1,0:T(8,128)(2,1)S(1)}, bf16[896,256]{1,0:T(8,128)(2,1)}, u32[]{:S(2)}) copy-start(bf16[896,256]{1,0:T(8,128)(2,1)} %refs_0_.3) | copy-start | bytes 1376260
  0.0 24.9 %copy-start.3 = (f32[20096]{0:T(1024)S(1)}, f32[20096]{0:T(1024)}, u32[]{:S(2)}) copy-start(f32[20096]{0:T(1024)} %param.8) | copy-start | bytes 241156
  0.0 12.2 %collective-permute-start = (bf16[896,256]{1,0:T(8,128)(2,1)}, bf16[896,256]{1,0:T(8,128)(2,1)S(1)}, u32[]{:S(2)}, u32[]{:S(2)}) collective-permute-start(bf16[896,256]{1,0:T(8,128)(2,1)} %refs_0_.3), channel_id=1, source_target_pairs={{0,1},{1,0},{2,3},{3,2},{4,5},{5,4},{6,7},{7,6},{8,9},{9,8},{10,11... | collective-permute-start | bytes 1376264 | tf_op jit(solution)/shard_map/ppermute | solution.py:268
  5.2 14.3 %collective-permute-start.2 = (bf16[448,256]{1,0:T(8,128)(2,1)S(1)}, bf16[448,256]{1,0:T(8,128)(2,1)S(1)}, u32[]{:S(2)}, u32[]{:S(2)}) collective-permute-start(bf16[448,256]{1,0:T(8,128)(2,1)S(1)} %get-tuple-element.49), channel_id=1, source_target_pairs={{0,7},{1,2},{2,1},{3,4},{4,3},{5,6},{6,5},{7,0},{8,15},{9,10},{10,... | collective-permute-start | bytes 688136 | tf_op jit(solution)/shard_map/ppermute | solution.py:271
  10.1 14.7 %copy-start.7 = (s32[16]{0:T(128)S(1)}, s32[16]{0:T(128)}, u32[]{:S(2)}) copy-start(s32[16]{0:T(128)} %exponent.1) | copy-start | bytes 196
  10.1 14.7 %copy-start.4 = (f32[64]{0:T(128)S(1)}, f32[64]{0:T(128)}, u32[]{:S(2)}) copy-start(f32[64]{0:T(128)} %occupied.1) | copy-start | bytes 772
  10.2 14.7 %copy-start.5 = (s32[16]{0:T(128)S(1)}, s32[16]{0:T(128)}, u32[]{:S(2)}) copy-start(s32[16]{0:T(128)} %occupied_of.1) | copy-start | bytes 196
  10.2 14.7 %copy-start.6 = (s32[16]{0:T(128)S(1)}, s32[16]{0:T(128)}, u32[]{:S(2)}) copy-start(s32[16]{0:T(128)} %virtual_of.1) | copy-start | bytes 196
  10.2 11.3 %collective-permute-start.1 = (bf16[448,256]{1,0:T(8,128)(2,1)S(1)}, bf16[448,256]{1,0:T(8,128)(2,1)S(1)}, u32[]{:S(2)}, u32[]{:S(2)}) collective-permute-start(bf16[448,256]{1,0:T(8,128)(2,1)S(1)} %get-tuple-element.50), channel_id=1, source_target_pairs={{0,7},{1,2},{2,1},{3,4},{4,3},{5,6},{6,5},{7,0},{8,15},{9,10},{10,... | collective-permute-start | bytes 688136 | tf_op jit(solution)/shard_map/ppermute | solution.py:271
  12.2 19.5 %collective-permute-start.5 = (bf16[896,256]{1,0:T(8,128)(2,1)S(1)}, bf16[896,256]{1,0:T(8,128)(2,1)S(1)}, u32[]{:S(2)}, u32[]{:S(2)}) collective-permute-start(bf16[896,256]{1,0:T(8,128)(2,1)S(1)} %collective-permute-done.refs_1_.refs_0_), channel_id=1, source_target_pairs={{0,7},{1,2},{2,1},{3,4},{4,3},{5,6},{6,5},{7,0},{8,15},{9,10},{10,... | collective-permute-start | bytes 1376264 | tf_op jit(solution)/shard_map/ppermute | solution.py:271
  19.5 12.2 %collective-permute-start.4 = (bf16[448,256]{1,0:T(8,128)(2,1)S(1)}, bf16[448,256]{1,0:T(8,128)(2,1)S(1)}, u32[]{:S(2)}, u32[]{:S(2)}) collective-permute-start(bf16[448,256]{1,0:T(8,128)(2,1)S(1)} %collective-permute-done.2.refs_3_.refs_2_), channel_id=1, source_target_pairs={{0,1},{1,0},{2,3},{3,2},{4,5},{5,4},{6,7},{7,6},{8,9},{9,8},{10,11... | collective-permute-start | bytes 688136 | tf_op jit(solution)/shard_map/ppermute | solution.py:268
  21.5 10.3 %collective-permute-start.3 = (bf16[448,256]{1,0:T(8,128)(2,1)S(1)}, bf16[448,256]{1,0:T(8,128)(2,1)S(1)}, u32[]{:S(2)}, u32[]{:S(2)}) collective-permute-start(bf16[448,256]{1,0:T(8,128)(2,1)S(1)} %collective-permute-done.1.refs_2_.refs_1_), channel_id=1, source_target_pairs={{0,1},{1,0},{2,3},{3,2},{4,5},{5,4},{6,7},{7,6},{8,9},{9,8},{10,11... | collective-permute-start | bytes 688136 | tf_op jit(solution)/shard_map/ppermute | solution.py:268
  26.3 10.6 %collective-permute-start.6 = (bf16[3,2,128,128]{3,2,1,0:T(8,128)(2,1)S(1)}, bf16[3,2,128,128]{3,2,1,0:T(8,128)(2,1)S(1)}, u32[]{:S(2)}, u32[]{:S(2)}) collective-permute-start(bf16[3,2,128,128]{3,2,1,0:T(8,128)(2,1)S(1)} %get-tuple-element.32), channel_id=1, source_target_pairs={{0,8},{8,0},{1,9},{9,1},{2,10},{10,2},{3,11},{11,3},{4,12},{12,4},... | collective-permute-start | bytes 589832 | tf_op jit(solution)/shard_map/ppermute | solution.py:274
  32.3 5.5 %collective-permute-start.7 = (bf16[2,2,128,128]{3,2,1,0:T(8,128)(2,1)S(1)}, bf16[2,2,128,128]{3,2,1,0:T(8,128)(2,1)S(1)}, u32[]{:S(2)}, u32[]{:S(2)}) collective-permute-start(bf16[2,2,128,128]{3,2,1,0:T(8,128)(2,1)S(1)} %get-tuple-element.33), channel_id=1, source_target_pairs={{0,8},{8,0},{1,9},{9,1},{2,10},{10,2},{3,11},{11,3},{4,12},{12,4},... | collective-permute-start | bytes 393224 | tf_op jit(solution)/shard_map/ppermute | solution.py:274
  38.6 25.6 %all-to-all-start = ((bf16[32,40,128]{2,1,0:T(8,128)(2,1)}), bf16[32,40,128]{2,1,0:T(8,128)(2,1)S(1)}, u32[]{:S(2)}, u32[]{:S(2)}) async-start(bf16[32,40,128]{2,1,0:T(8,128)(2,1)} %sum_cores.1), calls=%async_computation | async-start | bytes 655360 | tf_op jit(solution)/shard_map/all_to_all | solution.py:293
  52.2 23.5 %collective-permute-start.9 = (bf16[896,256]{1,0:T(8,128)(2,1)}, bf16[896,256]{1,0:T(8,128)(2,1)S(1)}, u32[]{:S(2)}, u32[]{:S(2)}) collective-permute-start(bf16[896,256]{1,0:T(8,128)(2,1)} %pad_maximum_fusion), channel_id=1, source_target_pairs={{0,7},{1,2},{2,1},{3,4},{4,3},{5,6},{6,5},{7,0},{8,15},{9,10},{10,... | collective-permute-start | bytes 1376264 | tf_op jit(solution)/shard_map/ppermute | solution.py:271
  54.8 21.0 %collective-permute-start.8 = (bf16[896,256]{1,0:T(8,128)(2,1)S(1)}, bf16[896,256]{1,0:T(8,128)(2,1)}, u32[]{:S(2)}, u32[]{:S(2)}) collective-permute-start(bf16[896,256]{1,0:T(8,128)(2,1)S(1)} %collective-permute-done.5.refs_5_.refs_6_), channel_id=1, source_target_pairs={{0,1},{1,0},{2,3},{3,2},{4,5},{5,4},{6,7},{7,6},{8,9},{9,8},{10,11... | collective-permute-start | bytes 1376264 | tf_op jit(solution)/shard_map/ppermute | solution.py:268
  75.8 19.6 %all-to-all-start.2 = ((bf16[32,64,128]{2,1,0:T(8,128)(2,1)}), bf16[32,64,128]{2,1,0:T(8,128)(2,1)S(1)}, u32[]{:S(2)}, u32[]{:S(2)}) async-start(bf16[32,64,128]{2,1,0:T(8,128)(2,1)} %amplitude_copies.1), calls=%async_computation.2 | async-start | bytes 1048576 | tf_op jit(solution)/shard_map/all_to_all | solution.py:299
  82.0 7.0 %collective-permute-start.11 = (bf16[448,256]{1,0:T(8,128)(2,1)S(1)}, bf16[448,256]{1,0:T(8,128)(2,1)S(1)}, u32[]{:S(2)}, u32[]{:S(2)}) collective-permute-start(bf16[448,256]{1,0:T(8,128)(2,1)S(1)} %slice.15), channel_id=1, source_target_pairs={{0,1},{1,0},{2,3},{3,2},{4,5},{5,4},{6,7},{7,6},{8,9},{9,8},{10,11... | collective-permute-start | bytes 688136 | tf_op jit(solution)/shard_map/ppermute | solution.py:268
  85.2 8.3 %collective-permute-start.10 = (bf16[448,256]{1,0:T(8,128)(2,1)S(1)}, bf16[448,256]{1,0:T(8,128)(2,1)S(1)}, u32[]{:S(2)}, u32[]{:S(2)}) collective-permute-start(bf16[448,256]{1,0:T(8,128)(2,1)S(1)} %slice.14), channel_id=1, source_target_pairs={{0,7},{1,2},{2,1},{3,4},{4,3},{5,6},{6,5},{7,0},{8,15},{9,10},{10,... | collective-permute-start | bytes 688136 | tf_op jit(solution)/shard_map/ppermute | solution.py:271
  93.5 0.7 copy-start.1
  95.4 8.2 %copy-start.2 = (bf16[448,256]{1,0:T(8,128)(2,1)S(1)}, bf16[448,256]{1,0:T(8,128)(2,1)}, u32[]{:S(2)}) copy-start(bf16[448,256]{1,0:T(8,128)(2,1)} %copy-done.1) | copy-start | bytes 688132
  95.4 8.2 %collective-permute-start.12 = (bf16[32,64,128]{2,1,0:T(8,128)(2,1)S(1)}, bf16[32,64,128]{2,1,0:T(8,128)(2,1)S(1)}, u32[]{:S(2)}, u32[]{:S(2)}) collective-permute-start(bf16[32,64,128]{2,1,0:T(8,128)(2,1)S(1)} %all-to-all-done.2.mine_ref), channel_id=1, source_target_pairs={{0,8},{8,0},{1,9},{9,1},{2,10},{10,2},{3,11},{11,3},{4,12},{12,4},... | collective-permute-start | bytes 1572872 | tf_op jit(solution)/shard_map/ppermute | solution.py:274

commit v20 on v19

--- a/solution.py
+++ b/solution.py
@@ -208,24 +208,33 @@
 
 
 def own_half(mine, scales, far):
-    def kernel(mine_ref, scale, far_ref, matrix, near, arrived):
-        fetch = pltpu.make_async_copy(far_ref, near, arrived)
-        fetch.start()
+    def kernel(mine_ref, scale, *refs):
+        sources, (matrix, near, arrived) = refs[: len(far)], refs[len(far) :]
+        fetches = []
+        start = 0
+        for k, source in enumerate(sources):
+            place = near.at[start : start + source.shape[0]]
+            fetches.append(pltpu.make_async_copy(source, place, arrived.at[k]))
+            start += source.shape[0]
+        for fetch in fetches:
+            fetch.start()
         lay_out(mine_ref, lax.axis_index("core"), scale, matrix)
-        fetch.wait()
-
+        for fetch in fetches:
+            fetch.wait()
+
+    rows = sum(part.shape[0] for part in far)
     return pl.pallas_call(
         kernel,
         out_shape=(
             jax.ShapeDtypeStruct((len(HELD), WIDTH, WIDTH), bf16),
-            jax.ShapeDtypeStruct(far.shape, far.dtype),
+            jax.ShapeDtypeStruct((rows, WIDTH), bf16),
         ),
-        in_specs=[in_vmem, in_vmem, anywhere],
+        in_specs=[in_vmem, in_vmem] + [anywhere] * len(far),
         out_specs=(in_vmem, in_vmem),
-        scratch_shapes=[pltpu.SemaphoreType.DMA],
+        scratch_shapes=[pltpu.SemaphoreType.DMA((len(far),))],
         compiler_params=pltpu.CompilerParams(vmem_limit_bytes=VMEM_LIMIT),
         name="own_half",
-    )(mine, scales, far)
+    )(mine, scales, *far)
 
 
 def gamma_rows(blocks, half, theirs, scales):
@@ -289,20 +298,20 @@
     summed = sum_cores((early, late), (got_early, got_late))
 
     summed, b2, a2 = lax.optimization_barrier((summed, block["B", 2], block["A", 2]))
-    a3, b3 = swap_a(b2[0]), swap_b(jnp.concatenate(a2))
+    a3, b3 = swap_a(b2[0]), [swap_b(part) for part in a2]
     parts = lax.all_to_all(summed, ("z", "x"), 0, 0)
     received = lax.all_to_all(amplitude_sends(parts, denominator), "pair", 0, 0)
     copies = amplitude_copies(received)
 
     copies, a3, b3 = lax.optimization_barrier((copies, a3, b3))
-    b4 = [swap_b(a3[:half]), swap_a(b3[half:])]
+    b4 = [swap_b(a3[:half]), swap_a(b3[1])]
     mine = lax.all_to_all(copies, ("z", "x"), 0, 0)
     mine, b4 = lax.optimization_barrier((mine, b4))
-    block.update({("B", 2): b2, ("A", 2): a2, ("A", 3): [a3], ("B", 3): [b3], ("B", 4): b4})
+    block.update({("B", 2): b2, ("A", 2): a2, ("A", 3): [a3], ("B", 3): b3, ("B", 4): b4})
     theirs = swap_cores(mine)
-    half, a3 = own_half(mine, scales, a3)
-    block["A", 3] = [a3]
-    return gamma_rows(block, half, theirs, scales)
+    own, near = own_half(mine, scales, b3)
+    block["B", 3] = [near]
+    return gamma_rows(block, own, theirs, scales)
 
 
 def solution(mesh):

time: 106 us -> 107 us (level)
  starting transfers between devices: 69.1 us -> 72.6 us
  waiting for transfers between devices: 15.3 us -> 12.7 us
    ppermute x5 -> x6, starting transfers between devices: 18.8 us -> 22.9 us  [swap_b(): return lax.ppermute(x, 'pair', SWAP_B)]
    all_to_all x1, waiting for transfers between devices: 6.39 us -> 4.32 us  [body(): parts = lax.all_to_all(summed, ('z', 'x'), 0, 0)]
    ppermute x5, starting transfers between devices: 15.6 us -> 13.7 us  [swap_a(): return lax.ppermute(x, 'pair', SWAP_A)]
    all_to_all x1, waiting for transfers between devices: 1.26 us -> 3.04 us  [body(): mine = lax.all_to_all(copies, ('z', 'x'), 0, 0)]
    ppermute x5, waiting for transfers between devices: 1.81 us -> 0.52 us  [swap_a(): return lax.ppermute(x, 'pair', SWAP_A)]
    ppermute x3, starting transfers between devices: 16.7 us -> 17.8 us  [swap_cores(): return lax.ppermute(x, 'core', SWAP_CORES)]
    ppermute x5 -> x6, waiting for transfers between devices: 4.47 us -> 3.72 us  [swap_b(): return lax.ppermute(x, 'pair', SWAP_B)]
  transfers between devices with their start and end apart: 15 -> 16, of which waited for: 6 -> 6; matrix products, arithmetic and copies ran while one was open for 3% -> 1% of each run, Pallas kernels for 4% -> 4%
where the time goes in v20:
time: 107 us; the launch traced here: 106 us
  starting transfers between devices  72.6 us (68%)
  waiting for transfers between devices  12.7 us (12%)
  blocking collectives  10.6 us (10%)
  Pallas kernels  6.99 us (7%)
  local copies, waits for them, and re-layouts  2.52 us (2%)
    ppermute x6, starting transfers between devices, swap_b(): return lax.ppermute(x, 'pair', SWAP_B)  22.9 us
    ppermute x3, starting transfers between devices, swap_cores(): return lax.ppermute(x, 'core', SWAP_CORES)  17.8 us
    ppermute x5, starting transfers between devices, swap_a(): return lax.ppermute(x, 'pair', SWAP_A)  13.7 us
    all_to_all x1, starting transfers between devices, body(): parts = lax.all_to_all(summed, ('z', 'x'), 0, 0)  12.9 us
    all_to_all x1, blocking collectives, body(): received = lax.all_to_all(amplitude_sends(parts, denominator), 'pair', 0, 0)  10.6 us
    all_to_all x1, starting transfers between devices, body(): mine = lax.all_to_all(copies, ('z', 'x'), 0, 0)  5.37 us
    all_to_all x1, waiting for transfers between devices, body(): parts = lax.all_to_all(summed, ('z', 'x'), 0, 0)  4.32 us
    ppermute x6, waiting for transfers between devices, swap_b(): return lax.ppermute(x, 'pair', SWAP_B)  3.72 us
  transfers between devices with their start and end apart: 16, of which 6 were waited for; matrix products, arithmetic and copies ran while one was open for 1% of the time, Pallas kernels for 4%

profile of v20, /device:TPU:1, one launch (start us, length us, event | category | flops | bytes accessed | tf_op | source)
XLA Modules:
  0.0 105.8 jit_solution(2928698131317925327)
XLA Ops:
  0.0 0.0 copy-start
  0.0 0.0 copy-start.5
  0.0 4.2 %collective-permute-start = (bf16[896,256]{1,0:T(8,128)(2,1)}, bf16[896,256]{1,0:T(8,128)(2,1)S(1)}, u32[]{:S(2)}, u32[]{:S(2)}) collective-permute-start(bf16[896,256]{1,0:T(8,128)(2,1)} %refs_0_.3), channel_id=1, source_target_pairs={{0,1},{1,0},{2,3},{3,2},{4,5},{5,4},{6,7},{7,6},{8,9},{9,8},{10,11... | collective-permute-start | bytes 1376264 | tf_op jit(solution)/shard_map/ppermute | solution.py:277
  4.2 1.1 %fusion = (bf16[448,256]{1,0:T(8,128)(2,1)S(1)}, bf16[448,256]{1,0:T(8,128)(2,1)S(1)}) fusion(bf16[896,256]{1,0:T(8,128)(2,1)} %refs_0_.3), kind=kLoop, calls=%fused_computation | loop fusion | bytes 917504 | tf_op jit(solution)/shard_map/slice | solution.py:288
  5.2 4.9 %collective-permute-start.2 = (bf16[448,256]{1,0:T(8,128)(2,1)S(1)}, bf16[448,256]{1,0:T(8,128)(2,1)S(1)}, u32[]{:S(2)}, u32[]{:S(2)}) collective-permute-start(bf16[448,256]{1,0:T(8,128)(2,1)S(1)} %get-tuple-element.51), channel_id=1, source_target_pairs={{0,7},{1,2},{2,1},{3,4},{4,3},{5,6},{6,5},{7,0},{8,15},{9,10},{10,... | collective-permute-start | bytes 688136 | tf_op jit(solution)/shard_map/ppermute | solution.py:280
  10.1 0.0 copy-start.9
  10.1 0.0 copy-start.6
  10.2 0.0 copy-start.7
  10.2 0.0 copy-start.8
  10.2 2.1 %collective-permute-start.1 = (bf16[448,256]{1,0:T(8,128)(2,1)S(1)}, bf16[448,256]{1,0:T(8,128)(2,1)S(1)}, u32[]{:S(2)}, u32[]{:S(2)}) collective-permute-start(bf16[448,256]{1,0:T(8,128)(2,1)S(1)} %get-tuple-element.52), channel_id=1, source_target_pairs={{0,7},{1,2},{2,1},{3,4},{4,3},{5,6},{6,5},{7,0},{8,15},{9,10},{10,... | collective-permute-start | bytes 688136 | tf_op jit(solution)/shard_map/ppermute | solution.py:280
  12.2 0.0 collective-permute-done.refs_1_.refs_0_
  12.2 7.3 %collective-permute-start.5 = (bf16[896,256]{1,0:T(8,128)(2,1)S(1)}, bf16[896,256]{1,0:T(8,128)(2,1)S(1)}, u32[]{:S(2)}, u32[]{:S(2)}) collective-permute-start(bf16[896,256]{1,0:T(8,128)(2,1)S(1)} %collective-permute-done.refs_1_.refs_0_), channel_id=1, source_target_pairs={{0,7},{1,2},{2,1},{3,4},{4,3},{5,6},{6,5},{7,0},{8,15},{9,10},{10,... | collective-permute-start | bytes 1376264 | tf_op jit(solution)/shard_map/ppermute | solution.py:280
  19.5 0.0 collective-permute-done.2.refs_3_.refs_2_
  19.5 1.9 %collective-permute-start.4 = (bf16[448,256]{1,0:T(8,128)(2,1)S(1)}, bf16[448,256]{1,0:T(8,128)(2,1)S(1)}, u32[]{:S(2)}, u32[]{:S(2)}) collective-permute-start(bf16[448,256]{1,0:T(8,128)(2,1)S(1)} %collective-permute-done.2.refs_3_.refs_2_), channel_id=1, source_target_pairs={{0,1},{1,0},{2,3},{3,2},{4,5},{5,4},{6,7},{7,6},{8,9},{9,8},{10,11... | collective-permute-start | bytes 688136 | tf_op jit(solution)/shard_map/ppermute | solution.py:277
  21.5 0.0 collective-permute-done.1.refs_2_.refs_1_
  21.5 3.4 %collective-permute-start.3 = (bf16[448,256]{1,0:T(8,128)(2,1)S(1)}, bf16[448,256]{1,0:T(8,128)(2,1)S(1)}, u32[]{:S(2)}, u32[]{:S(2)}) collective-permute-start(bf16[448,256]{1,0:T(8,128)(2,1)S(1)} %collective-permute-done.1.refs_2_.refs_1_), channel_id=1, source_target_pairs={{0,1},{1,0},{2,3},{3,2},{4,5},{5,4},{6,7},{7,6},{8,9},{9,8},{10,11... | collective-permute-start | bytes 688136 | tf_op jit(solution)/shard_map/ppermute | solution.py:277
  24.9 0.0 copy-done.5
  24.9 0.0 copy-done.9
  24.9 0.0 copy-done.6
  24.9 0.0 copy-done.7
  24.9 0.0 copy-done.8
  24.9 0.7 tables.1
  25.6 0.0 copy-done
  25.6 0.6 coulomb_pairs.2
  26.3 5.5 %collective-permute-start.6 = (bf16[3,2,128,128]{3,2,1,0:T(8,128)(2,1)S(1)}, bf16[3,2,128,128]{3,2,1,0:T(8,128)(2,1)S(1)}, u32[]{:S(2)}, u32[]{:S(2)}) collective-permute-start(bf16[3,2,128,128]{3,2,1,0:T(8,128)(2,1)S(1)} %get-tuple-element.33), channel_id=1, source_target_pairs={{0,8},{8,0},{1,9},{9,1},{2,10},{10,2},{3,11},{11,3},{4,12},{12,4},... | collective-permute-start | bytes 589832 | tf_op jit(solution)/shard_map/ppermute | solution.py:283
  31.8 0.0 collective-permute-done.4.refs_4_.refs_5_
  31.8 0.0 collective-permute-done.3.refs_3_.refs_4_
  31.8 0.0 collective-permute-done.5.refs_5_.refs_6_
  31.8 0.5 coulomb_pairs.3
  32.3 4.5 %collective-permute-start.7 = (bf16[2,2,128,128]{3,2,1,0:T(8,128)(2,1)S(1)}, bf16[2,2,128,128]{3,2,1,0:T(8,128)(2,1)S(1)}, u32[]{:S(2)}, u32[]{:S(2)}) collective-permute-start(bf16[2,2,128,128]{3,2,1,0:T(8,128)(2,1)S(1)} %get-tuple-element.34), channel_id=1, source_target_pairs={{0,8},{8,0},{1,9},{9,1},{2,10},{10,2},{3,11},{11,3},{4,12},{12,4},... | collective-permute-start | bytes 393224 | tf_op jit(solution)/shard_map/ppermute | solution.py:283
  36.8 0.0 collective-permute-done.6.refs_2_
  36.8 1.0 collective-permute-done.7.refs_3_
  37.8 0.8 sum_cores.1
  38.6 12.9 %all-to-all-start = ((bf16[32,40,128]{2,1,0:T(8,128)(2,1)}), bf16[32,40,128]{2,1,0:T(8,128)(2,1)S(1)}, u32[]{:S(2)}, u32[]{:S(2)}) async-start(bf16[32,40,128]{2,1,0:T(8,128)(2,1)} %sum_cores.1), calls=%async_computation | async-start | bytes 655360 | tf_op jit(solution)/shard_map/all_to_all | solution.py:302
  51.4 1.9 %collective-permute-start.8 = (bf16[896,256]{1,0:T(8,128)(2,1)S(1)}, bf16[896,256]{1,0:T(8,128)(2,1)S(1)}, u32[]{:S(2)}, u32[]{:S(2)}) collective-permute-start(bf16[896,256]{1,0:T(8,128)(2,1)S(1)} %collective-permute-done.5.refs_5_.refs_6_), channel_id=1, source_target_pairs={{0,1},{1,0},{2,3},{3,2},{4,5},{5,4},{6,7},{7,6},{8,9},{9,8},{10,11... | collective-permute-start | bytes 1376264 | tf_op jit(solution)/shard_map/ppermute | solution.py:277
  53.4 4.0 %collective-permute-start.9 = (bf16[448,256]{1,0:T(8,128)(2,1)S(1)}, bf16[448,256]{1,0:T(8,128)(2,1)S(1)}, u32[]{:S(2)}, u32[]{:S(2)}) collective-permute-start(bf16[448,256]{1,0:T(8,128)(2,1)S(1)} %collective-permute-done.3.refs_3_.refs_4_), channel_id=1, source_target_pairs={{0,7},{1,2},{2,1},{3,4},{4,3},{5,6},{6,5},{7,0},{8,15},{9,10},{10,... | collective-permute-start | bytes 688136 | tf_op jit(solution)/shard_map/ppermute | solution.py:280
  57.4 2.5 %collective-permute-start.10 = (bf16[448,256]{1,0:T(8,128)(2,1)S(1)}, bf16[448,256]{1,0:T(8,128)(2,1)}, u32[]{:S(2)}, u32[]{:S(2)}) collective-permute-start(bf16[448,256]{1,0:T(8,128)(2,1)S(1)} %collective-permute-done.4.refs_4_.refs_5_), channel_id=1, source_target_pairs={{0,7},{1,2},{2,1},{3,4},{4,3},{5,6},{6,5},{7,0},{8,15},{9,10},{10,... | collective-permute-start | bytes 688136 | tf_op jit(solution)/shard_map/ppermute | solution.py:280
  59.9 4.3 %all-to-all-done.parts_ref = bf16[32,40,128]{2,1,0:T(8,128)(2,1)S(1)} async-done(((bf16[32,40,128]{2,1,0:T(8,128)(2,1)}), bf16[32,40,128]{2,1,0:T(8,128)(2,1)S(1)}, u32[]{:S(2)}, u32[]{:S(2)}) %all-to-all-start) | async-done | bytes 327712 | tf_op jit(solution)/shard_map/all_to_all | solution.py:302
  64.2 10.6 %all_to_all.15.received_ref = bf16[8,16,128]{2,1,0:T(8,128)(2,1)S(1)} all-to-all(bf16[8,16,128]{2,1,0:T(8,128)(2,1)S(1)} %amplitude_sends.1), channel_id=1, replica_groups=mesh['x'=4,'z'=8,'core'=2,'pair'=8] {'pair'}, dimensions={0} | all-to-all | bytes 65536 | tf_op jit(solution)/shard_map/all_to_all | solution.py:303
  74.8 0.9 amplitude_copies.1
  75.7 0.0 collective-permute-done.9.refs_0_
  75.7 0.0 collective-permute-done.10.refs_1_
  75.7 0.0 collective-permute-done.8.refs_7_
  75.7 5.4 %all-to-all-start.2 = ((bf16[32,64,128]{2,1,0:T(8,128)(2,1)}), bf16[32,64,128]{2,1,0:T(8,128)(2,1)S(1)}, u32[]{:S(2)}, u32[]{:S(2)}) async-start(bf16[32,64,128]{2,1,0:T(8,128)(2,1)} %amplitude_copies.1), calls=%async_computation.2 | async-start | bytes 1048576 | tf_op jit(solution)/shard_map/all_to_all | solution.py:308
  81.2 2.2 %collective-permute-start.11 = (bf16[448,256]{1,0:T(8,128)(2,1)S(1)}, bf16[448,256]{1,0:T(8,128)(2,1)S(1)}, u32[]{:S(2)}, u32[]{:S(2)}) collective-permute-start(bf16[448,256]{1,0:T(8,128)(2,1)S(1)} %slice.11), channel_id=1, source_target_pairs={{0,7},{1,2},{2,1},{3,4},{4,3},{5,6},{6,5},{7,0},{8,15},{9,10},{10,... | collective-permute-start | bytes 688136 | tf_op jit(solution)/shard_map/ppermute | solution.py:280
  83.3 2.4 %collective-permute-start.12 = (bf16[448,256]{1,0:T(8,128)(2,1)}, bf16[448,256]{1,0:T(8,128)(2,1)S(1)}, u32[]{:S(2)}, u32[]{:S(2)}) collective-permute-start(bf16[448,256]{1,0:T(8,128)(2,1)} %collective-permute-done.10.refs_1_), channel_id=1, source_target_pairs={{0,1},{1,0},{2,3},{3,2},{4,5},{5,4},{6,7},{7,6},{8,9},{9,8},{10,11... | collective-permute-start | bytes 688136 | tf_op jit(solution)/shard_map/ppermute | solution.py:277
  85.7 3.7 %collective-permute-done.11.refs_9_ = bf16[448,256]{1,0:T(8,128)(2,1)S(1)} collective-permute-done((bf16[448,256]{1,0:T(8,128)(2,1)S(1)}, bf16[448,256]{1,0:T(8,128)(2,1)S(1)}, u32[]{:S(2)}, u32[]{:S(2)}) %collective-permute-start.11) | collective-permute-done | bytes 229408 | tf_op jit(solution)/shard_map/ppermute | solution.py:280
  89.4 0.0 copy-start.1
  89.4 0.7 copy-done.1
  90.1 0.5 collective-permute-done.12.refs_10_
  90.6 0.0 copy-start.3
  90.6 0.7 copy-done.3
  91.3 3.0 %all-to-all-done.2.mine_ref = bf16[32,64,128]{2,1,0:T(8,128)(2,1)S(1)} async-done(((bf16[32,64,128]{2,1,0:T(8,128)(2,1)}), bf16[32,64,128]{2,1,0:T(8,128)(2,1)S(1)}, u32[]{:S(2)}, u32[]{:S(2)}) %all-to-all-start.2) | async-done | bytes 524320 | tf_op jit(solution)/shard_map/all_to_all | solution.py:308
  94.4 0.0 copy-start.2
  94.4 0.0 copy-start.4
  94.4 7.8 %collective-permute-start.13 = (bf16[32,64,128]{2,1,0:T(8,128)(2,1)S(1)}, bf16[32,64,128]{2,1,0:T(8,128)(2,1)S(1)}, u32[]{:S(2)}, u32[]{:S(2)}) collective-permute-start(bf16[32,64,128]{2,1,0:T(8,128)(2,1)S(1)} %all-to-all-done.2.mine_ref), channel_id=1, source_target_pairs={{0,8},{8,0},{1,9},{9,1},{2,10},{10,2},{3,11},{11,3},{4,12},{12,4},... | collective-permute-start | bytes 1572872 | tf_op jit(solution)/shard_map/ppermute | solution.py:283
  102.2 1.3 %own_half.1 = (bf16[8,256,256]{2,1,0:T(8,128)(2,1)S(1)}, bf16[896,256]{1,0:T(8,128)(2,1)S(1)}) custom-call(bf16[32,64,128]{2,1,0:T(8,128)(2,1)S(1)} %all-to-all-done.2.mine_ref, f32[16,128]{1,0:T(8,128)S(1)} %get-tuple-element.44.scale.refs_13_, bf16[448,256]{1,0:T(8,128)(2,1)S(1)} %collective-permute-done.9.refs_0_, ...), custom_call_target="tpu_custom_call" | custom-call | tf_op jit(solution)/shard_map/own_half/pallas_call | solution.py:226
  103.5 0.2 collective-permute-done.13.refs_12_
  103.7 0.0 copy-done.2
  103.7 0.0 copy-done.4
  103.7 2.1 %gamma_rows.1 = (bf16[896,256]{1,0:T(8,128)(2,1)}, bf16[8,256,256]{2,1,0:T(8,128)(2,1)S(1)}) custom-call(bf16[896,256]{1,0:T(8,128)(2,1)S(1)} %copy-done, bf16[896,256]{1,0:T(8,128)(2,1)S(1)} %collective-permute-done.refs_1_.refs_0_, bf16[448,256]{1,0:T(8,128)(2,1)S(1)} %collective-permute-done.1.refs_2_.refs_1_, ...), custom_call_target="tpu_custom_call", output_to_operand_aliasing={{1}: (11, {})} | custom-call | tf_op jit(solution)/shard_map/gamma_rows/pallas_call | solution.py:261
  (2 shorter events, 0.1 us)
Async XLA Ops:
  0.0 25.6 %copy-start = (bf16[896,256]{1,0:T(8,128)(2,1)S(1)}, bf16[896,256]{1,0:T(8,128)(2,1)}, u32[]{:S(2)}) copy-start(bf16[896,256]{1,0:T(8,128)(2,1)} %refs_0_.3) | copy-start | bytes 1376260
  0.0 24.9 %copy-start.5 = (f32[20096]{0:T(1024)S(1)}, f32[20096]{0:T(1024)}, u32[]{:S(2)}) copy-start(f32[20096]{0:T(1024)} %param.8) | copy-start | bytes 241156
  0.0 12.2 %collective-permute-start = (bf16[896,256]{1,0:T(8,128)(2,1)}, bf16[896,256]{1,0:T(8,128)(2,1)S(1)}, u32[]{:S(2)}, u32[]{:S(2)}) collective-permute-start(bf16[896,256]{1,0:T(8,128)(2,1)} %refs_0_.3), channel_id=1, source_target_pairs={{0,1},{1,0},{2,3},{3,2},{4,5},{5,4},{6,7},{7,6},{8,9},{9,8},{10,11... | collective-permute-start | bytes 1376264 | tf_op jit(solution)/shard_map/ppermute | solution.py:277
  5.2 14.3 %collective-permute-start.2 = (bf16[448,256]{1,0:T(8,128)(2,1)S(1)}, bf16[448,256]{1,0:T(8,128)(2,1)S(1)}, u32[]{:S(2)}, u32[]{:S(2)}) collective-permute-start(bf16[448,256]{1,0:T(8,128)(2,1)S(1)} %get-tuple-element.51), channel_id=1, source_target_pairs={{0,7},{1,2},{2,1},{3,4},{4,3},{5,6},{6,5},{7,0},{8,15},{9,10},{10,... | collective-permute-start | bytes 688136 | tf_op jit(solution)/shard_map/ppermute | solution.py:280
  10.1 14.7 %copy-start.9 = (s32[16]{0:T(128)S(1)}, s32[16]{0:T(128)}, u32[]{:S(2)}) copy-start(s32[16]{0:T(128)} %exponent.1) | copy-start | bytes 196
  10.1 14.7 %copy-start.6 = (f32[64]{0:T(128)S(1)}, f32[64]{0:T(128)}, u32[]{:S(2)}) copy-start(f32[64]{0:T(128)} %occupied.1) | copy-start | bytes 772
  10.2 14.7 %copy-start.7 = (s32[16]{0:T(128)S(1)}, s32[16]{0:T(128)}, u32[]{:S(2)}) copy-start(s32[16]{0:T(128)} %occupied_of.1) | copy-start | bytes 196
  10.2 14.7 %copy-start.8 = (s32[16]{0:T(128)S(1)}, s32[16]{0:T(128)}, u32[]{:S(2)}) copy-start(s32[16]{0:T(128)} %virtual_of.1) | copy-start | bytes 196
  10.2 11.3 %collective-permute-start.1 = (bf16[448,256]{1,0:T(8,128)(2,1)S(1)}, bf16[448,256]{1,0:T(8,128)(2,1)S(1)}, u32[]{:S(2)}, u32[]{:S(2)}) collective-permute-start(bf16[448,256]{1,0:T(8,128)(2,1)S(1)} %get-tuple-element.52), channel_id=1, source_target_pairs={{0,7},{1,2},{2,1},{3,4},{4,3},{5,6},{6,5},{7,0},{8,15},{9,10},{10,... | collective-permute-start | bytes 688136 | tf_op jit(solution)/shard_map/ppermute | solution.py:280
  12.2 19.5 %collective-permute-start.5 = (bf16[896,256]{1,0:T(8,128)(2,1)S(1)}, bf16[896,256]{1,0:T(8,128)(2,1)S(1)}, u32[]{:S(2)}, u32[]{:S(2)}) collective-permute-start(bf16[896,256]{1,0:T(8,128)(2,1)S(1)} %collective-permute-done.refs_1_.refs_0_), channel_id=1, source_target_pairs={{0,7},{1,2},{2,1},{3,4},{4,3},{5,6},{6,5},{7,0},{8,15},{9,10},{10,... | collective-permute-start | bytes 1376264 | tf_op jit(solution)/shard_map/ppermute | solution.py:280
  19.5 12.2 %collective-permute-start.4 = (bf16[448,256]{1,0:T(8,128)(2,1)S(1)}, bf16[448,256]{1,0:T(8,128)(2,1)S(1)}, u32[]{:S(2)}, u32[]{:S(2)}) collective-permute-start(bf16[448,256]{1,0:T(8,128)(2,1)S(1)} %collective-permute-done.2.refs_3_.refs_2_), channel_id=1, source_target_pairs={{0,1},{1,0},{2,3},{3,2},{4,5},{5,4},{6,7},{7,6},{8,9},{9,8},{10,11... | collective-permute-start | bytes 688136 | tf_op jit(solution)/shard_map/ppermute | solution.py:277
  21.5 10.3 %collective-permute-start.3 = (bf16[448,256]{1,0:T(8,128)(2,1)S(1)}, bf16[448,256]{1,0:T(8,128)(2,1)S(1)}, u32[]{:S(2)}, u32[]{:S(2)}) collective-permute-start(bf16[448,256]{1,0:T(8,128)(2,1)S(1)} %collective-permute-done.1.refs_2_.refs_1_), channel_id=1, source_target_pairs={{0,1},{1,0},{2,3},{3,2},{4,5},{5,4},{6,7},{7,6},{8,9},{9,8},{10,11... | collective-permute-start | bytes 688136 | tf_op jit(solution)/shard_map/ppermute | solution.py:277
  26.3 10.6 %collective-permute-start.6 = (bf16[3,2,128,128]{3,2,1,0:T(8,128)(2,1)S(1)}, bf16[3,2,128,128]{3,2,1,0:T(8,128)(2,1)S(1)}, u32[]{:S(2)}, u32[]{:S(2)}) collective-permute-start(bf16[3,2,128,128]{3,2,1,0:T(8,128)(2,1)S(1)} %get-tuple-element.33), channel_id=1, source_target_pairs={{0,8},{8,0},{1,9},{9,1},{2,10},{10,2},{3,11},{11,3},{4,12},{12,4},... | collective-permute-start | bytes 589832 | tf_op jit(solution)/shard_map/ppermute | solution.py:283
  32.3 5.5 %collective-permute-start.7 = (bf16[2,2,128,128]{3,2,1,0:T(8,128)(2,1)S(1)}, bf16[2,2,128,128]{3,2,1,0:T(8,128)(2,1)S(1)}, u32[]{:S(2)}, u32[]{:S(2)}) collective-permute-start(bf16[2,2,128,128]{3,2,1,0:T(8,128)(2,1)S(1)} %get-tuple-element.34), channel_id=1, source_target_pairs={{0,8},{8,0},{1,9},{9,1},{2,10},{10,2},{3,11},{11,3},{4,12},{12,4},... | collective-permute-start | bytes 393224 | tf_op jit(solution)/shard_map/ppermute | solution.py:283
  38.6 25.6 %all-to-all-start = ((bf16[32,40,128]{2,1,0:T(8,128)(2,1)}), bf16[32,40,128]{2,1,0:T(8,128)(2,1)S(1)}, u32[]{:S(2)}, u32[]{:S(2)}) async-start(bf16[32,40,128]{2,1,0:T(8,128)(2,1)} %sum_cores.1), calls=%async_computation | async-start | bytes 655360 | tf_op jit(solution)/shard_map/all_to_all | solution.py:302
  51.4 24.3 %collective-permute-start.8 = (bf16[896,256]{1,0:T(8,128)(2,1)S(1)}, bf16[896,256]{1,0:T(8,128)(2,1)S(1)}, u32[]{:S(2)}, u32[]{:S(2)}) collective-permute-start(bf16[896,256]{1,0:T(8,128)(2,1)S(1)} %collective-permute-done.5.refs_5_.refs_6_), channel_id=1, source_target_pairs={{0,1},{1,0},{2,3},{3,2},{4,5},{5,4},{6,7},{7,6},{8,9},{9,8},{10,11... | collective-permute-start | bytes 1376264 | tf_op jit(solution)/shard_map/ppermute | solution.py:277
  53.4 22.4 %collective-permute-start.9 = (bf16[448,256]{1,0:T(8,128)(2,1)S(1)}, bf16[448,256]{1,0:T(8,128)(2,1)S(1)}, u32[]{:S(2)}, u32[]{:S(2)}) collective-permute-start(bf16[448,256]{1,0:T(8,128)(2,1)S(1)} %collective-permute-done.3.refs_3_.refs_4_), channel_id=1, source_target_pairs={{0,7},{1,2},{2,1},{3,4},{4,3},{5,6},{6,5},{7,0},{8,15},{9,10},{10,... | collective-permute-start | bytes 688136 | tf_op jit(solution)/shard_map/ppermute | solution.py:280
  57.4 18.3 %collective-permute-start.10 = (bf16[448,256]{1,0:T(8,128)(2,1)S(1)}, bf16[448,256]{1,0:T(8,128)(2,1)}, u32[]{:S(2)}, u32[]{:S(2)}) collective-permute-start(bf16[448,256]{1,0:T(8,128)(2,1)S(1)} %collective-permute-done.4.refs_4_.refs_5_), channel_id=1, source_target_pairs={{0,7},{1,2},{2,1},{3,4},{4,3},{5,6},{6,5},{7,0},{8,15},{9,10},{10,... | collective-permute-start | bytes 688136 | tf_op jit(solution)/shard_map/ppermute | solution.py:280
  75.7 18.6 %all-to-all-start.2 = ((bf16[32,64,128]{2,1,0:T(8,128)(2,1)}), bf16[32,64,128]{2,1,0:T(8,128)(2,1)S(1)}, u32[]{:S(2)}, u32[]{:S(2)}) async-start(bf16[32,64,128]{2,1,0:T(8,128)(2,1)} %amplitude_copies.1), calls=%async_computation.2 | async-start | bytes 1048576 | tf_op jit(solution)/shard_map/all_to_all | solution.py:308
  81.2 8.3 %collective-permute-start.11 = (bf16[448,256]{1,0:T(8,128)(2,1)S(1)}, bf16[448,256]{1,0:T(8,128)(2,1)S(1)}, u32[]{:S(2)}, u32[]{:S(2)}) collective-permute-start(bf16[448,256]{1,0:T(8,128)(2,1)S(1)} %slice.11), channel_id=1, source_target_pairs={{0,7},{1,2},{2,1},{3,4},{4,3},{5,6},{6,5},{7,0},{8,15},{9,10},{10,... | collective-permute-start | bytes 688136 | tf_op jit(solution)/shard_map/ppermute | solution.py:280
  83.3 7.3 %collective-permute-start.12 = (bf16[448,256]{1,0:T(8,128)(2,1)}, bf16[448,256]{1,0:T(8,128)(2,1)S(1)}, u32[]{:S(2)}, u32[]{:S(2)}) collective-permute-start(bf16[448,256]{1,0:T(8,128)(2,1)} %collective-permute-done.10.refs_1_), channel_id=1, source_target_pairs={{0,1},{1,0},{2,3},{3,2},{4,5},{5,4},{6,7},{7,6},{8,9},{9,8},{10,11... | collective-permute-start | bytes 688136 | tf_op jit(solution)/shard_map/ppermute | solution.py:277
  89.4 0.7 copy-start.1
  90.6 0.7 copy-start.3
  94.4 9.3 %copy-start.2 = (bf16[448,256]{1,0:T(8,128)(2,1)S(1)}, bf16[448,256]{1,0:T(8,128)(2,1)}, u32[]{:S(2)}) copy-start(bf16[448,256]{1,0:T(8,128)(2,1)} %copy-done.1) | copy-start | bytes 688132
  94.4 9.3 %copy-start.4 = (bf16[448,256]{1,0:T(8,128)(2,1)S(1)}, bf16[448,256]{1,0:T(8,128)(2,1)}, u32[]{:S(2)}) copy-start(bf16[448,256]{1,0:T(8,128)(2,1)} %copy-done.3) | copy-start | bytes 688132
  94.4 9.3 %collective-permute-start.13 = (bf16[32,64,128]{2,1,0:T(8,128)(2,1)S(1)}, bf16[32,64,128]{2,1,0:T(8,128)(2,1)S(1)}, u32[]{:S(2)}, u32[]{:S(2)}) collective-permute-start(bf16[32,64,128]{2,1,0:T(8,128)(2,1)S(1)} %all-to-all-done.2.mine_ref), channel_id=1, source_target_pairs={{0,8},{8,0},{1,9},{9,1},{2,10},{10,2},{3,11},{11,3},{4,12},{12,4},... | collective-permute-start | bytes 1572872 | tf_op jit(solution)/shard_map/ppermute | solution.py:283

commit v21 on v20

--- a/solution.py
+++ b/solution.py
@@ -19,7 +19,7 @@
 SENDS = ((0, (0, 1)), (1, (1, 2)), (-1, (2, 3)), (2, (3, 4)))
 GETS = tuple((PAIRS[k][0] - d, PAIRS[k][1] - d) for d, pairs in SENDS for k in pairs)
 ORDER = tuple((r, False) if c == 0 else (c, True) for r, c in GETS)
-ROWS = 224
+ROWS = 448
 VMEM_LIMIT = 12 * 1024 * 1024
 bf16, f32 = jnp.bfloat16, jnp.float32
 in_vmem = pl.BlockSpec(memory_space=pltpu.VMEM)

time: 107 us -> 107 us (level)
  no operation moved by 1% of the time
where the time goes in v21:
time: 107 us; the launch traced here: 106 us
  starting transfers between devices  72.6 us (68%)
  waiting for transfers between devices  12.7 us (12%)
  blocking collectives  10.6 us (10%)
  Pallas kernels  6.98 us (7%)
  local copies, waits for them, and re-layouts  2.52 us (2%)
    ppermute x6, starting transfers between devices, swap_b(): return lax.ppermute(x, 'pair', SWAP_B)  22.9 us
    ppermute x3, starting transfers between devices, swap_cores(): return lax.ppermute(x, 'core', SWAP_CORES)  17.8 us
    ppermute x5, starting transfers between devices, swap_a(): return lax.ppermute(x, 'pair', SWAP_A)  13.7 us
    all_to_all x1, starting transfers between devices, body(): parts = lax.all_to_all(summed, ('z', 'x'), 0, 0)  12.9 us
    all_to_all x1, blocking collectives, body(): received = lax.all_to_all(amplitude_sends(parts, denominator), 'pair', 0, 0)  10.6 us
    all_to_all x1, starting transfers between devices, body(): mine = lax.all_to_all(copies, ('z', 'x'), 0, 0)  5.37 us
    all_to_all x1, waiting for transfers between devices, body(): parts = lax.all_to_all(summed, ('z', 'x'), 0, 0)  4.32 us
    ppermute x6, waiting for transfers between devices, swap_b(): return lax.ppermute(x, 'pair', SWAP_B)  3.72 us
  transfers between devices with their start and end apart: 16, of which 6 were waited for; matrix products, arithmetic and copies ran while one was open for 1% of the time, Pallas kernels for 4%

profile of v21, /device:TPU:1, one launch (start us, length us, event | category | flops | bytes accessed | tf_op | source)
XLA Modules:
  0.0 105.8 jit_solution(11905998669114557726)
XLA Ops:
  0.0 0.0 copy-start
  0.0 0.0 copy-start.5
  0.0 4.2 %collective-permute-start = (bf16[896,256]{1,0:T(8,128)(2,1)}, bf16[896,256]{1,0:T(8,128)(2,1)S(1)}, u32[]{:S(2)}, u32[]{:S(2)}) collective-permute-start(bf16[896,256]{1,0:T(8,128)(2,1)} %refs_0_.3), channel_id=1, source_target_pairs={{0,1},{1,0},{2,3},{3,2},{4,5},{5,4},{6,7},{7,6},{8,9},{9,8},{10,11... | collective-permute-start | bytes 1376264 | tf_op jit(solution)/shard_map/ppermute | solution.py:277
  4.2 1.1 %fusion = (bf16[448,256]{1,0:T(8,128)(2,1)S(1)}, bf16[448,256]{1,0:T(8,128)(2,1)S(1)}) fusion(bf16[896,256]{1,0:T(8,128)(2,1)} %refs_0_.3), kind=kLoop, calls=%fused_computation | loop fusion | bytes 917504 | tf_op jit(solution)/shard_map/slice | solution.py:288
  5.2 4.9 %collective-permute-start.2 = (bf16[448,256]{1,0:T(8,128)(2,1)S(1)}, bf16[448,256]{1,0:T(8,128)(2,1)S(1)}, u32[]{:S(2)}, u32[]{:S(2)}) collective-permute-start(bf16[448,256]{1,0:T(8,128)(2,1)S(1)} %get-tuple-element.51), channel_id=1, source_target_pairs={{0,7},{1,2},{2,1},{3,4},{4,3},{5,6},{6,5},{7,0},{8,15},{9,10},{10,... | collective-permute-start | bytes 688136 | tf_op jit(solution)/shard_map/ppermute | solution.py:280
  10.1 0.0 copy-start.9
  10.1 0.0 copy-start.6
  10.2 0.0 copy-start.7
  10.2 0.0 copy-start.8
  10.2 2.1 %collective-permute-start.1 = (bf16[448,256]{1,0:T(8,128)(2,1)S(1)}, bf16[448,256]{1,0:T(8,128)(2,1)S(1)}, u32[]{:S(2)}, u32[]{:S(2)}) collective-permute-start(bf16[448,256]{1,0:T(8,128)(2,1)S(1)} %get-tuple-element.52), channel_id=1, source_target_pairs={{0,7},{1,2},{2,1},{3,4},{4,3},{5,6},{6,5},{7,0},{8,15},{9,10},{10,... | collective-permute-start | bytes 688136 | tf_op jit(solution)/shard_map/ppermute | solution.py:280
  12.2 0.0 collective-permute-done.refs_1_.refs_0_
  12.2 7.3 %collective-permute-start.5 = (bf16[896,256]{1,0:T(8,128)(2,1)S(1)}, bf16[896,256]{1,0:T(8,128)(2,1)S(1)}, u32[]{:S(2)}, u32[]{:S(2)}) collective-permute-start(bf16[896,256]{1,0:T(8,128)(2,1)S(1)} %collective-permute-done.refs_1_.refs_0_), channel_id=1, source_target_pairs={{0,7},{1,2},{2,1},{3,4},{4,3},{5,6},{6,5},{7,0},{8,15},{9,10},{10,... | collective-permute-start | bytes 1376264 | tf_op jit(solution)/shard_map/ppermute | solution.py:280
  19.5 0.0 collective-permute-done.2.refs_3_.refs_2_
  19.5 1.9 %collective-permute-start.4 = (bf16[448,256]{1,0:T(8,128)(2,1)S(1)}, bf16[448,256]{1,0:T(8,128)(2,1)S(1)}, u32[]{:S(2)}, u32[]{:S(2)}) collective-permute-start(bf16[448,256]{1,0:T(8,128)(2,1)S(1)} %collective-permute-done.2.refs_3_.refs_2_), channel_id=1, source_target_pairs={{0,1},{1,0},{2,3},{3,2},{4,5},{5,4},{6,7},{7,6},{8,9},{9,8},{10,11... | collective-permute-start | bytes 688136 | tf_op jit(solution)/shard_map/ppermute | solution.py:277
  21.5 0.0 collective-permute-done.1.refs_2_.refs_1_
  21.5 3.4 %collective-permute-start.3 = (bf16[448,256]{1,0:T(8,128)(2,1)S(1)}, bf16[448,256]{1,0:T(8,128)(2,1)S(1)}, u32[]{:S(2)}, u32[]{:S(2)}) collective-permute-start(bf16[448,256]{1,0:T(8,128)(2,1)S(1)} %collective-permute-done.1.refs_2_.refs_1_), channel_id=1, source_target_pairs={{0,1},{1,0},{2,3},{3,2},{4,5},{5,4},{6,7},{7,6},{8,9},{9,8},{10,11... | collective-permute-start | bytes 688136 | tf_op jit(solution)/shard_map/ppermute | solution.py:277
  24.9 0.0 copy-done.5
  24.9 0.0 copy-done.9
  24.9 0.0 copy-done.6
  24.9 0.0 copy-done.7
  24.9 0.0 copy-done.8
  24.9 0.7 tables.1
  25.6 0.0 copy-done
  25.6 0.6 coulomb_pairs.2
  26.3 5.5 %collective-permute-start.6 = (bf16[3,2,128,128]{3,2,1,0:T(8,128)(2,1)S(1)}, bf16[3,2,128,128]{3,2,1,0:T(8,128)(2,1)S(1)}, u32[]{:S(2)}, u32[]{:S(2)}) collective-permute-start(bf16[3,2,128,128]{3,2,1,0:T(8,128)(2,1)S(1)} %get-tuple-element.33), channel_id=1, source_target_pairs={{0,8},{8,0},{1,9},{9,1},{2,10},{10,2},{3,11},{11,3},{4,12},{12,4},... | collective-permute-start | bytes 589832 | tf_op jit(solution)/shard_map/ppermute | solution.py:283
  31.8 0.0 collective-permute-done.4.refs_4_.refs_5_
  31.8 0.0 collective-permute-done.3.refs_3_.refs_4_
  31.8 0.0 collective-permute-done.5.refs_5_.refs_6_
  31.8 0.5 coulomb_pairs.3
  32.3 4.5 %collective-permute-start.7 = (bf16[2,2,128,128]{3,2,1,0:T(8,128)(2,1)S(1)}, bf16[2,2,128,128]{3,2,1,0:T(8,128)(2,1)S(1)}, u32[]{:S(2)}, u32[]{:S(2)}) collective-permute-start(bf16[2,2,128,128]{3,2,1,0:T(8,128)(2,1)S(1)} %get-tuple-element.34), channel_id=1, source_target_pairs={{0,8},{8,0},{1,9},{9,1},{2,10},{10,2},{3,11},{11,3},{4,12},{12,4},... | collective-permute-start | bytes 393224 | tf_op jit(solution)/shard_map/ppermute | solution.py:283
  36.8 0.0 collective-permute-done.6.refs_2_
  36.8 1.0 collective-permute-done.7.refs_3_
  37.8 0.8 sum_cores.1
  38.6 12.9 %all-to-all-start = ((bf16[32,40,128]{2,1,0:T(8,128)(2,1)}), bf16[32,40,128]{2,1,0:T(8,128)(2,1)S(1)}, u32[]{:S(2)}, u32[]{:S(2)}) async-start(bf16[32,40,128]{2,1,0:T(8,128)(2,1)} %sum_cores.1), calls=%async_computation | async-start | bytes 655360 | tf_op jit(solution)/shard_map/all_to_all | solution.py:302
  51.4 1.9 %collective-permute-start.8 = (bf16[896,256]{1,0:T(8,128)(2,1)S(1)}, bf16[896,256]{1,0:T(8,128)(2,1)S(1)}, u32[]{:S(2)}, u32[]{:S(2)}) collective-permute-start(bf16[896,256]{1,0:T(8,128)(2,1)S(1)} %collective-permute-done.5.refs_5_.refs_6_), channel_id=1, source_target_pairs={{0,1},{1,0},{2,3},{3,2},{4,5},{5,4},{6,7},{7,6},{8,9},{9,8},{10,11... | collective-permute-start | bytes 1376264 | tf_op jit(solution)/shard_map/ppermute | solution.py:277
  53.4 4.0 %collective-permute-start.9 = (bf16[448,256]{1,0:T(8,128)(2,1)S(1)}, bf16[448,256]{1,0:T(8,128)(2,1)S(1)}, u32[]{:S(2)}, u32[]{:S(2)}) collective-permute-start(bf16[448,256]{1,0:T(8,128)(2,1)S(1)} %collective-permute-done.3.refs_3_.refs_4_), channel_id=1, source_target_pairs={{0,7},{1,2},{2,1},{3,4},{4,3},{5,6},{6,5},{7,0},{8,15},{9,10},{10,... | collective-permute-start | bytes 688136 | tf_op jit(solution)/shard_map/ppermute | solution.py:280
  57.4 2.5 %collective-permute-start.10 = (bf16[448,256]{1,0:T(8,128)(2,1)S(1)}, bf16[448,256]{1,0:T(8,128)(2,1)}, u32[]{:S(2)}, u32[]{:S(2)}) collective-permute-start(bf16[448,256]{1,0:T(8,128)(2,1)S(1)} %collective-permute-done.4.refs_4_.refs_5_), channel_id=1, source_target_pairs={{0,7},{1,2},{2,1},{3,4},{4,3},{5,6},{6,5},{7,0},{8,15},{9,10},{10,... | collective-permute-start | bytes 688136 | tf_op jit(solution)/shard_map/ppermute | solution.py:280
  59.9 4.3 %all-to-all-done.parts_ref = bf16[32,40,128]{2,1,0:T(8,128)(2,1)S(1)} async-done(((bf16[32,40,128]{2,1,0:T(8,128)(2,1)}), bf16[32,40,128]{2,1,0:T(8,128)(2,1)S(1)}, u32[]{:S(2)}, u32[]{:S(2)}) %all-to-all-start) | async-done | bytes 327712 | tf_op jit(solution)/shard_map/all_to_all | solution.py:302
  64.2 10.6 %all_to_all.15.received_ref = bf16[8,16,128]{2,1,0:T(8,128)(2,1)S(1)} all-to-all(bf16[8,16,128]{2,1,0:T(8,128)(2,1)S(1)} %amplitude_sends.1), channel_id=1, replica_groups=mesh['x'=4,'z'=8,'core'=2,'pair'=8] {'pair'}, dimensions={0} | all-to-all | bytes 65536 | tf_op jit(solution)/shard_map/all_to_all | solution.py:303
  74.8 0.9 amplitude_copies.1
  75.7 0.0 collective-permute-done.9.refs_0_
  75.7 0.0 collective-permute-done.10.refs_1_
  75.7 0.0 collective-permute-done.8.refs_7_
  75.7 5.4 %all-to-all-start.2 = ((bf16[32,64,128]{2,1,0:T(8,128)(2,1)}), bf16[32,64,128]{2,1,0:T(8,128)(2,1)S(1)}, u32[]{:S(2)}, u32[]{:S(2)}) async-start(bf16[32,64,128]{2,1,0:T(8,128)(2,1)} %amplitude_copies.1), calls=%async_computation.2 | async-start | bytes 1048576 | tf_op jit(solution)/shard_map/all_to_all | solution.py:308
  81.2 2.2 %collective-permute-start.11 = (bf16[448,256]{1,0:T(8,128)(2,1)S(1)}, bf16[448,256]{1,0:T(8,128)(2,1)S(1)}, u32[]{:S(2)}, u32[]{:S(2)}) collective-permute-start(bf16[448,256]{1,0:T(8,128)(2,1)S(1)} %slice.11), channel_id=1, source_target_pairs={{0,7},{1,2},{2,1},{3,4},{4,3},{5,6},{6,5},{7,0},{8,15},{9,10},{10,... | collective-permute-start | bytes 688136 | tf_op jit(solution)/shard_map/ppermute | solution.py:280
  83.3 2.4 %collective-permute-start.12 = (bf16[448,256]{1,0:T(8,128)(2,1)}, bf16[448,256]{1,0:T(8,128)(2,1)S(1)}, u32[]{:S(2)}, u32[]{:S(2)}) collective-permute-start(bf16[448,256]{1,0:T(8,128)(2,1)} %collective-permute-done.10.refs_1_), channel_id=1, source_target_pairs={{0,1},{1,0},{2,3},{3,2},{4,5},{5,4},{6,7},{7,6},{8,9},{9,8},{10,11... | collective-permute-start | bytes 688136 | tf_op jit(solution)/shard_map/ppermute | solution.py:277
  85.7 3.7 %collective-permute-done.11.refs_9_ = bf16[448,256]{1,0:T(8,128)(2,1)S(1)} collective-permute-done((bf16[448,256]{1,0:T(8,128)(2,1)S(1)}, bf16[448,256]{1,0:T(8,128)(2,1)S(1)}, u32[]{:S(2)}, u32[]{:S(2)}) %collective-permute-start.11) | collective-permute-done | bytes 229408 | tf_op jit(solution)/shard_map/ppermute | solution.py:280
  89.4 0.0 copy-start.1
  89.4 0.7 copy-done.1
  90.1 0.5 collective-permute-done.12.refs_10_
  90.6 0.0 copy-start.3
  90.6 0.7 copy-done.3
  91.3 3.0 %all-to-all-done.2.mine_ref = bf16[32,64,128]{2,1,0:T(8,128)(2,1)S(1)} async-done(((bf16[32,64,128]{2,1,0:T(8,128)(2,1)}), bf16[32,64,128]{2,1,0:T(8,128)(2,1)S(1)}, u32[]{:S(2)}, u32[]{:S(2)}) %all-to-all-start.2) | async-done | bytes 524320 | tf_op jit(solution)/shard_map/all_to_all | solution.py:308
  94.4 0.0 copy-start.2
  94.4 0.0 copy-start.4
  94.4 7.8 %collective-permute-start.13 = (bf16[32,64,128]{2,1,0:T(8,128)(2,1)S(1)}, bf16[32,64,128]{2,1,0:T(8,128)(2,1)S(1)}, u32[]{:S(2)}, u32[]{:S(2)}) collective-permute-start(bf16[32,64,128]{2,1,0:T(8,128)(2,1)S(1)} %all-to-all-done.2.mine_ref), channel_id=1, source_target_pairs={{0,8},{8,0},{1,9},{9,1},{2,10},{10,2},{3,11},{11,3},{4,12},{12,4},... | collective-permute-start | bytes 1572872 | tf_op jit(solution)/shard_map/ppermute | solution.py:283
  102.2 1.3 %own_half.1 = (bf16[8,256,256]{2,1,0:T(8,128)(2,1)S(1)}, bf16[896,256]{1,0:T(8,128)(2,1)S(1)}) custom-call(bf16[32,64,128]{2,1,0:T(8,128)(2,1)S(1)} %all-to-all-done.2.mine_ref, f32[16,128]{1,0:T(8,128)S(1)} %get-tuple-element.44.scale.refs_13_, bf16[448,256]{1,0:T(8,128)(2,1)S(1)} %collective-permute-done.9.refs_0_, ...), custom_call_target="tpu_custom_call" | custom-call | tf_op jit(solution)/shard_map/own_half/pallas_call | solution.py:226
  103.5 0.2 collective-permute-done.13.refs_12_
  103.7 0.0 copy-done.2
  103.7 0.0 copy-done.4
  103.7 2.1 %gamma_rows.1 = (bf16[896,256]{1,0:T(8,128)(2,1)}, bf16[8,256,256]{2,1,0:T(8,128)(2,1)S(1)}) custom-call(bf16[896,256]{1,0:T(8,128)(2,1)S(1)} %copy-done, bf16[896,256]{1,0:T(8,128)(2,1)S(1)} %collective-permute-done.refs_1_.refs_0_, bf16[448,256]{1,0:T(8,128)(2,1)S(1)} %collective-permute-done.1.refs_2_.refs_1_, ...), custom_call_target="tpu_custom_call", output_to_operand_aliasing={{1}: (11, {})} | custom-call | tf_op jit(solution)/shard_map/gamma_rows/pallas_call | solution.py:261
  (2 shorter events, 0.1 us)
Async XLA Ops:
  0.0 25.6 %copy-start = (bf16[896,256]{1,0:T(8,128)(2,1)S(1)}, bf16[896,256]{1,0:T(8,128)(2,1)}, u32[]{:S(2)}) copy-start(bf16[896,256]{1,0:T(8,128)(2,1)} %refs_0_.3) | copy-start | bytes 1376260
  0.0 24.9 %copy-start.5 = (f32[20096]{0:T(1024)S(1)}, f32[20096]{0:T(1024)}, u32[]{:S(2)}) copy-start(f32[20096]{0:T(1024)} %param.8) | copy-start | bytes 241156
  0.0 12.2 %collective-permute-start = (bf16[896,256]{1,0:T(8,128)(2,1)}, bf16[896,256]{1,0:T(8,128)(2,1)S(1)}, u32[]{:S(2)}, u32[]{:S(2)}) collective-permute-start(bf16[896,256]{1,0:T(8,128)(2,1)} %refs_0_.3), channel_id=1, source_target_pairs={{0,1},{1,0},{2,3},{3,2},{4,5},{5,4},{6,7},{7,6},{8,9},{9,8},{10,11... | collective-permute-start | bytes 1376264 | tf_op jit(solution)/shard_map/ppermute | solution.py:277
  5.2 14.3 %collective-permute-start.2 = (bf16[448,256]{1,0:T(8,128)(2,1)S(1)}, bf16[448,256]{1,0:T(8,128)(2,1)S(1)}, u32[]{:S(2)}, u32[]{:S(2)}) collective-permute-start(bf16[448,256]{1,0:T(8,128)(2,1)S(1)} %get-tuple-element.51), channel_id=1, source_target_pairs={{0,7},{1,2},{2,1},{3,4},{4,3},{5,6},{6,5},{7,0},{8,15},{9,10},{10,... | collective-permute-start | bytes 688136 | tf_op jit(solution)/shard_map/ppermute | solution.py:280
  10.1 14.7 %copy-start.9 = (s32[16]{0:T(128)S(1)}, s32[16]{0:T(128)}, u32[]{:S(2)}) copy-start(s32[16]{0:T(128)} %exponent.1) | copy-start | bytes 196
  10.1 14.7 %copy-start.6 = (f32[64]{0:T(128)S(1)}, f32[64]{0:T(128)}, u32[]{:S(2)}) copy-start(f32[64]{0:T(128)} %occupied.1) | copy-start | bytes 772
  10.2 14.7 %copy-start.7 = (s32[16]{0:T(128)S(1)}, s32[16]{0:T(128)}, u32[]{:S(2)}) copy-start(s32[16]{0:T(128)} %occupied_of.1) | copy-start | bytes 196
  10.2 14.7 %copy-start.8 = (s32[16]{0:T(128)S(1)}, s32[16]{0:T(128)}, u32[]{:S(2)}) copy-start(s32[16]{0:T(128)} %virtual_of.1) | copy-start | bytes 196
  10.2 11.3 %collective-permute-start.1 = (bf16[448,256]{1,0:T(8,128)(2,1)S(1)}, bf16[448,256]{1,0:T(8,128)(2,1)S(1)}, u32[]{:S(2)}, u32[]{:S(2)}) collective-permute-start(bf16[448,256]{1,0:T(8,128)(2,1)S(1)} %get-tuple-element.52), channel_id=1, source_target_pairs={{0,7},{1,2},{2,1},{3,4},{4,3},{5,6},{6,5},{7,0},{8,15},{9,10},{10,... | collective-permute-start | bytes 688136 | tf_op jit(solution)/shard_map/ppermute | solution.py:280
  12.2 19.5 %collective-permute-start.5 = (bf16[896,256]{1,0:T(8,128)(2,1)S(1)}, bf16[896,256]{1,0:T(8,128)(2,1)S(1)}, u32[]{:S(2)}, u32[]{:S(2)}) collective-permute-start(bf16[896,256]{1,0:T(8,128)(2,1)S(1)} %collective-permute-done.refs_1_.refs_0_), channel_id=1, source_target_pairs={{0,7},{1,2},{2,1},{3,4},{4,3},{5,6},{6,5},{7,0},{8,15},{9,10},{10,... | collective-permute-start | bytes 1376264 | tf_op jit(solution)/shard_map/ppermute | solution.py:280
  19.5 12.2 %collective-permute-start.4 = (bf16[448,256]{1,0:T(8,128)(2,1)S(1)}, bf16[448,256]{1,0:T(8,128)(2,1)S(1)}, u32[]{:S(2)}, u32[]{:S(2)}) collective-permute-start(bf16[448,256]{1,0:T(8,128)(2,1)S(1)} %collective-permute-done.2.refs_3_.refs_2_), channel_id=1, source_target_pairs={{0,1},{1,0},{2,3},{3,2},{4,5},{5,4},{6,7},{7,6},{8,9},{9,8},{10,11... | collective-permute-start | bytes 688136 | tf_op jit(solution)/shard_map/ppermute | solution.py:277
  21.5 10.3 %collective-permute-start.3 = (bf16[448,256]{1,0:T(8,128)(2,1)S(1)}, bf16[448,256]{1,0:T(8,128)(2,1)S(1)}, u32[]{:S(2)}, u32[]{:S(2)}) collective-permute-start(bf16[448,256]{1,0:T(8,128)(2,1)S(1)} %collective-permute-done.1.refs_2_.refs_1_), channel_id=1, source_target_pairs={{0,1},{1,0},{2,3},{3,2},{4,5},{5,4},{6,7},{7,6},{8,9},{9,8},{10,11... | collective-permute-start | bytes 688136 | tf_op jit(solution)/shard_map/ppermute | solution.py:277
  26.3 10.6 %collective-permute-start.6 = (bf16[3,2,128,128]{3,2,1,0:T(8,128)(2,1)S(1)}, bf16[3,2,128,128]{3,2,1,0:T(8,128)(2,1)S(1)}, u32[]{:S(2)}, u32[]{:S(2)}) collective-permute-start(bf16[3,2,128,128]{3,2,1,0:T(8,128)(2,1)S(1)} %get-tuple-element.33), channel_id=1, source_target_pairs={{0,8},{8,0},{1,9},{9,1},{2,10},{10,2},{3,11},{11,3},{4,12},{12,4},... | collective-permute-start | bytes 589832 | tf_op jit(solution)/shard_map/ppermute | solution.py:283
  32.3 5.5 %collective-permute-start.7 = (bf16[2,2,128,128]{3,2,1,0:T(8,128)(2,1)S(1)}, bf16[2,2,128,128]{3,2,1,0:T(8,128)(2,1)S(1)}, u32[]{:S(2)}, u32[]{:S(2)}) collective-permute-start(bf16[2,2,128,128]{3,2,1,0:T(8,128)(2,1)S(1)} %get-tuple-element.34), channel_id=1, source_target_pairs={{0,8},{8,0},{1,9},{9,1},{2,10},{10,2},{3,11},{11,3},{4,12},{12,4},... | collective-permute-start | bytes 393224 | tf_op jit(solution)/shard_map/ppermute | solution.py:283
  38.6 25.6 %all-to-all-start = ((bf16[32,40,128]{2,1,0:T(8,128)(2,1)}), bf16[32,40,128]{2,1,0:T(8,128)(2,1)S(1)}, u32[]{:S(2)}, u32[]{:S(2)}) async-start(bf16[32,40,128]{2,1,0:T(8,128)(2,1)} %sum_cores.1), calls=%async_computation | async-start | bytes 655360 | tf_op jit(solution)/shard_map/all_to_all | solution.py:302
  51.4 24.3 %collective-permute-start.8 = (bf16[896,256]{1,0:T(8,128)(2,1)S(1)}, bf16[896,256]{1,0:T(8,128)(2,1)S(1)}, u32[]{:S(2)}, u32[]{:S(2)}) collective-permute-start(bf16[896,256]{1,0:T(8,128)(2,1)S(1)} %collective-permute-done.5.refs_5_.refs_6_), channel_id=1, source_target_pairs={{0,1},{1,0},{2,3},{3,2},{4,5},{5,4},{6,7},{7,6},{8,9},{9,8},{10,11... | collective-permute-start | bytes 1376264 | tf_op jit(solution)/shard_map/ppermute | solution.py:277
  53.4 22.4 %collective-permute-start.9 = (bf16[448,256]{1,0:T(8,128)(2,1)S(1)}, bf16[448,256]{1,0:T(8,128)(2,1)S(1)}, u32[]{:S(2)}, u32[]{:S(2)}) collective-permute-start(bf16[448,256]{1,0:T(8,128)(2,1)S(1)} %collective-permute-done.3.refs_3_.refs_4_), channel_id=1, source_target_pairs={{0,7},{1,2},{2,1},{3,4},{4,3},{5,6},{6,5},{7,0},{8,15},{9,10},{10,... | collective-permute-start | bytes 688136 | tf_op jit(solution)/shard_map/ppermute | solution.py:280
  57.4 18.3 %collective-permute-start.10 = (bf16[448,256]{1,0:T(8,128)(2,1)S(1)}, bf16[448,256]{1,0:T(8,128)(2,1)}, u32[]{:S(2)}, u32[]{:S(2)}) collective-permute-start(bf16[448,256]{1,0:T(8,128)(2,1)S(1)} %collective-permute-done.4.refs_4_.refs_5_), channel_id=1, source_target_pairs={{0,7},{1,2},{2,1},{3,4},{4,3},{5,6},{6,5},{7,0},{8,15},{9,10},{10,... | collective-permute-start | bytes 688136 | tf_op jit(solution)/shard_map/ppermute | solution.py:280
  75.7 18.6 %all-to-all-start.2 = ((bf16[32,64,128]{2,1,0:T(8,128)(2,1)}), bf16[32,64,128]{2,1,0:T(8,128)(2,1)S(1)}, u32[]{:S(2)}, u32[]{:S(2)}) async-start(bf16[32,64,128]{2,1,0:T(8,128)(2,1)} %amplitude_copies.1), calls=%async_computation.2 | async-start | bytes 1048576 | tf_op jit(solution)/shard_map/all_to_all | solution.py:308
  81.2 8.3 %collective-permute-start.11 = (bf16[448,256]{1,0:T(8,128)(2,1)S(1)}, bf16[448,256]{1,0:T(8,128)(2,1)S(1)}, u32[]{:S(2)}, u32[]{:S(2)}) collective-permute-start(bf16[448,256]{1,0:T(8,128)(2,1)S(1)} %slice.11), channel_id=1, source_target_pairs={{0,7},{1,2},{2,1},{3,4},{4,3},{5,6},{6,5},{7,0},{8,15},{9,10},{10,... | collective-permute-start | bytes 688136 | tf_op jit(solution)/shard_map/ppermute | solution.py:280
  83.3 7.3 %collective-permute-start.12 = (bf16[448,256]{1,0:T(8,128)(2,1)}, bf16[448,256]{1,0:T(8,128)(2,1)S(1)}, u32[]{:S(2)}, u32[]{:S(2)}) collective-permute-start(bf16[448,256]{1,0:T(8,128)(2,1)} %collective-permute-done.10.refs_1_), channel_id=1, source_target_pairs={{0,1},{1,0},{2,3},{3,2},{4,5},{5,4},{6,7},{7,6},{8,9},{9,8},{10,11... | collective-permute-start | bytes 688136 | tf_op jit(solution)/shard_map/ppermute | solution.py:277
  89.4 0.7 copy-start.1
  90.6 0.7 copy-start.3
  94.4 9.3 %copy-start.2 = (bf16[448,256]{1,0:T(8,128)(2,1)S(1)}, bf16[448,256]{1,0:T(8,128)(2,1)}, u32[]{:S(2)}) copy-start(bf16[448,256]{1,0:T(8,128)(2,1)} %copy-done.1) | copy-start | bytes 688132
  94.4 9.3 %copy-start.4 = (bf16[448,256]{1,0:T(8,128)(2,1)S(1)}, bf16[448,256]{1,0:T(8,128)(2,1)}, u32[]{:S(2)}) copy-start(bf16[448,256]{1,0:T(8,128)(2,1)} %copy-done.3) | copy-start | bytes 688132
  94.4 9.3 %collective-permute-start.13 = (bf16[32,64,128]{2,1,0:T(8,128)(2,1)S(1)}, bf16[32,64,128]{2,1,0:T(8,128)(2,1)S(1)}, u32[]{:S(2)}, u32[]{:S(2)}) collective-permute-start(bf16[32,64,128]{2,1,0:T(8,128)(2,1)S(1)} %all-to-all-done.2.mine_ref), channel_id=1, source_target_pairs={{0,8},{8,0},{1,9},{9,1},{2,10},{10,2},{3,11},{11,3},{4,12},{12,4},... | collective-permute-start | bytes 1572872 | tf_op jit(solution)/shard_map/ppermute | solution.py:283

commit v22 on v20

--- a/solution.py
+++ b/solution.py
@@ -286,7 +286,8 @@
     block = {0: [three_index]}
     block["A", 1] = [swap_a(three_index)]
     block["B", 1] = [swap_b(three_index[:half]), swap_b(three_index[half:])]
-    block["B", 2] = [swap_b(block["A", 1][0])]
+    a1 = block["A", 1][0]
+    block["B", 2] = [swap_b(a1[:half]), swap_b(a1[half:])]
     block["A", 2] = [swap_a(part) for part in block["B", 1]]
 
     early, other_early = coulomb_pairs(block, EARLY)
@@ -298,16 +299,16 @@
     summed = sum_cores((early, late), (got_early, got_late))
 
     summed, b2, a2 = lax.optimization_barrier((summed, block["B", 2], block["A", 2]))
-    a3, b3 = swap_a(b2[0]), [swap_b(part) for part in a2]
+    a3, b3 = [swap_a(part) for part in b2], [swap_b(part) for part in a2]
     parts = lax.all_to_all(summed, ("z", "x"), 0, 0)
     received = lax.all_to_all(amplitude_sends(parts, denominator), "pair", 0, 0)
     copies = amplitude_copies(received)
 
     copies, a3, b3 = lax.optimization_barrier((copies, a3, b3))
-    b4 = [swap_b(a3[:half]), swap_a(b3[1])]
+    b4 = [swap_b(a3[0]), swap_a(b3[1])]
     mine = lax.all_to_all(copies, ("z", "x"), 0, 0)
     mine, b4 = lax.optimization_barrier((mine, b4))
-    block.update({("B", 2): b2, ("A", 2): a2, ("A", 3): [a3], ("B", 3): b3, ("B", 4): b4})
+    block.update({("B", 2): b2, ("A", 2): a2, ("A", 3): a3, ("B", 3): b3, ("B", 4): b4})
     theirs = swap_cores(mine)
     own, near = own_half(mine, scales, b3)
     block["B", 3] = [near]

time: 107 us -> 114 us (1.065)
  starting transfers between devices: 72.6 us -> 76.1 us
  waiting for transfers between devices: 12.7 us -> 15.8 us
  blocking collectives: 10.6 us -> 11.8 us
    ppermute x6 -> x7, waiting for transfers between devices: 3.72 us -> 10.3 us  [swap_b(): return lax.ppermute(x, 'pair', SWAP_B)]
    all_to_all x1, waiting for transfers between devices: 4.32 us -> 0.95 us  [body(): parts = lax.all_to_all(summed, ('z', 'x'), 0, 0)]
    all_to_all x1, starting transfers between devices: 5.37 us -> 8.29 us  [body(): mine = lax.all_to_all(copies, ('z', 'x'), 0, 0)]
    ppermute x5 -> x6, starting transfers between devices: 13.7 us -> 15.6 us  [swap_a(): return lax.ppermute(x, 'pair', SWAP_A)]
    all_to_all x1, starting transfers between devices: 12.9 us -> 11.3 us  [body(): parts = lax.all_to_all(summed, ('z', 'x'), 0, 0)]
    all_to_all x1, blocking collectives: 10.6 us -> 11.8 us  [body(): received = lax.all_to_all(amplitude_sends(parts, denominator), 'pair', 0, 0)]
    ppermute x6 -> x7, starting transfers between devices: 22.9 us -> 22.1 us  [swap_b(): return lax.ppermute(x, 'pair', SWAP_B)]
  transfers between devices with their start and end apart: 16 -> 18, of which waited for: 6 -> 8; matrix products, arithmetic and copies ran while one was open for 1% -> 1% of each run, Pallas kernels for 4% -> 4%
where the time goes in v22:
time: 114 us
  starting transfers between devices  76.1 us (67%)
  waiting for transfers between devices  15.8 us (14%)
  blocking collectives  11.8 us (10%)
  Pallas kernels  7 us (6%)
  local copies, waits for them, and re-layouts  2.56 us (2%)
    ppermute x7, starting transfers between devices, swap_b(): return lax.ppermute(x, 'pair', SWAP_B)  22.1 us
    ppermute x3, starting transfers between devices, swap_cores(): return lax.ppermute(x, 'core', SWAP_CORES)  18.8 us
    ppermute x6, starting transfers between devices, swap_a(): return lax.ppermute(x, 'pair', SWAP_A)  15.6 us
    all_to_all x1, blocking collectives, body(): received = lax.all_to_all(amplitude_sends(parts, denominator), 'pair', 0, 0)  11.8 us
    all_to_all x1, starting transfers between devices, body(): parts = lax.all_to_all(summed, ('z', 'x'), 0, 0)  11.3 us
    ppermute x7, waiting for transfers between devices, swap_b(): return lax.ppermute(x, 'pair', SWAP_B)  10.3 us
    all_to_all x1, starting transfers between devices, body(): mine = lax.all_to_all(copies, ('z', 'x'), 0, 0)  8.29 us
    all_to_all x1, waiting for transfers between devices, body(): mine = lax.all_to_all(copies, ('z', 'x'), 0, 0)  2.93 us
  transfers between devices with their start and end apart: 18, of which 8 were waited for; matrix products, arithmetic and copies ran while one was open for 1% of the time, Pallas kernels for 4%

profile of v22, /device:TPU:1, one launch (start us, length us, event | category | flops | bytes accessed | tf_op | source)
XLA Modules:
  0.0 113.6 jit_solution(6923511644641848038)
XLA Ops:
  0.0 4.0 %collective-permute-start = (bf16[896,256]{1,0:T(8,128)(2,1)}, bf16[896,256]{1,0:T(8,128)(2,1)S(1)}, u32[]{:S(2)}, u32[]{:S(2)}) collective-permute-start(bf16[896,256]{1,0:T(8,128)(2,1)} %refs_0_.3), channel_id=1, source_target_pairs={{0,1},{1,0},{2,3},{3,2},{4,5},{5,4},{6,7},{7,6},{8,9},{9,8},{10,11... | collective-permute-start | bytes 1376264 | tf_op jit(solution)/shard_map/ppermute | solution.py:277
  4.0 1.1 fusion.1
  5.1 4.9 %collective-permute-start.2 = (bf16[448,256]{1,0:T(8,128)(2,1)S(1)}, bf16[448,256]{1,0:T(8,128)(2,1)S(1)}, u32[]{:S(2)}, u32[]{:S(2)}) collective-permute-start(bf16[448,256]{1,0:T(8,128)(2,1)S(1)} %get-tuple-element.57), channel_id=1, source_target_pairs={{0,7},{1,2},{2,1},{3,4},{4,3},{5,6},{6,5},{7,0},{8,15},{9,10},{10,... | collective-permute-start | bytes 688136 | tf_op jit(solution)/shard_map/ppermute | solution.py:280
  10.0 0.0 copy-start.5
  10.0 0.0 copy-start
  10.0 2.1 %collective-permute-start.1 = (bf16[448,256]{1,0:T(8,128)(2,1)S(1)}, bf16[448,256]{1,0:T(8,128)(2,1)S(1)}, u32[]{:S(2)}, u32[]{:S(2)}) collective-permute-start(bf16[448,256]{1,0:T(8,128)(2,1)S(1)} %get-tuple-element.58), channel_id=1, source_target_pairs={{0,7},{1,2},{2,1},{3,4},{4,3},{5,6},{6,5},{7,0},{8,15},{9,10},{10,... | collective-permute-start | bytes 688136 | tf_op jit(solution)/shard_map/ppermute | solution.py:280
  12.1 1.3 %collective-permute-done.2.refs_3_.refs_2_ = bf16[448,256]{1,0:T(8,128)(2,1)S(1)} collective-permute-done((bf16[448,256]{1,0:T(8,128)(2,1)S(1)}, bf16[448,256]{1,0:T(8,128)(2,1)S(1)}, u32[]{:S(2)}, u32[]{:S(2)}) %collective-permute-start.2) | collective-permute-done | bytes 229408 | tf_op jit(solution)/shard_map/ppermute | solution.py:280
  13.4 1.9 %collective-permute-start.4 = (bf16[448,256]{1,0:T(8,128)(2,1)S(1)}, bf16[448,256]{1,0:T(8,128)(2,1)S(1)}, u32[]{:S(2)}, u32[]{:S(2)}) collective-permute-start(bf16[448,256]{1,0:T(8,128)(2,1)S(1)} %collective-permute-done.2.refs_3_.refs_2_), channel_id=1, source_target_pairs={{0,1},{1,0},{2,3},{3,2},{4,5},{5,4},{6,7},{7,6},{8,9},{9,8},{10,11... | collective-permute-start | bytes 688136 | tf_op jit(solution)/shard_map/ppermute | solution.py:277
  15.3 5.4 %collective-permute-done.1.refs_2_.refs_1_ = bf16[448,256]{1,0:T(8,128)(2,1)S(1)} collective-permute-done((bf16[448,256]{1,0:T(8,128)(2,1)S(1)}, bf16[448,256]{1,0:T(8,128)(2,1)S(1)}, u32[]{:S(2)}, u32[]{:S(2)}) %collective-permute-start.1) | collective-permute-done | bytes 229408 | tf_op jit(solution)/shard_map/ppermute | solution.py:280
  20.7 1.9 %collective-permute-start.3 = (bf16[448,256]{1,0:T(8,128)(2,1)S(1)}, bf16[448,256]{1,0:T(8,128)(2,1)S(1)}, u32[]{:S(2)}, u32[]{:S(2)}) collective-permute-start(bf16[448,256]{1,0:T(8,128)(2,1)S(1)} %collective-permute-done.1.refs_2_.refs_1_), channel_id=1, source_target_pairs={{0,1},{1,0},{2,3},{3,2},{4,5},{5,4},{6,7},{7,6},{8,9},{9,8},{10,11... | collective-permute-start | bytes 688136 | tf_op jit(solution)/shard_map/ppermute | solution.py:277
  22.6 0.0 collective-permute-done.refs_1_.refs_0_
  22.7 3.3 %collective-permute-start.6 = (bf16[448,256]{1,0:T(8,128)(2,1)S(1)}, bf16[448,256]{1,0:T(8,128)(2,1)S(1)}, u32[]{:S(2)}, u32[]{:S(2)}) collective-permute-start(bf16[448,256]{1,0:T(8,128)(2,1)S(1)} %get-tuple-element.55), channel_id=1, source_target_pairs={{0,7},{1,2},{2,1},{3,4},{4,3},{5,6},{6,5},{7,0},{8,15},{9,10},{10,... | collective-permute-start | bytes 688136 | tf_op jit(solution)/shard_map/ppermute | solution.py:280
  25.9 0.0 copy-start.9
  25.9 0.0 copy-start.6
  25.9 0.0 copy-start.7
  26.0 0.0 copy-start.8
  26.0 3.4 %collective-permute-start.5 = (bf16[448,256]{1,0:T(8,128)(2,1)S(1)}, bf16[448,256]{1,0:T(8,128)(2,1)S(1)}, u32[]{:S(2)}, u32[]{:S(2)}) collective-permute-start(bf16[448,256]{1,0:T(8,128)(2,1)S(1)} %get-tuple-element.56), channel_id=1, source_target_pairs={{0,7},{1,2},{2,1},{3,4},{4,3},{5,6},{6,5},{7,0},{8,15},{9,10},{10,... | collective-permute-start | bytes 688136 | tf_op jit(solution)/shard_map/ppermute | solution.py:280
  29.3 0.0 copy-done.5
  29.4 0.0 copy-done.9
  29.4 0.0 copy-done.6
  29.4 0.0 copy-done.7
  29.4 0.0 copy-done.8
  29.4 0.7 tables.1
  30.1 0.0 copy-done
  30.1 0.6 coulomb_pairs.2
  30.7 7.0 %collective-permute-start.7 = (bf16[3,2,128,128]{3,2,1,0:T(8,128)(2,1)S(1)}, bf16[3,2,128,128]{3,2,1,0:T(8,128)(2,1)S(1)}, u32[]{:S(2)}, u32[]{:S(2)}) collective-permute-start(bf16[3,2,128,128]{3,2,1,0:T(8,128)(2,1)S(1)} %get-tuple-element.35), channel_id=1, source_target_pairs={{0,8},{8,0},{1,9},{9,1},{2,10},{10,2},{3,11},{11,3},{4,12},{12,4},... | collective-permute-start | bytes 589832 | tf_op jit(solution)/shard_map/ppermute | solution.py:283
  37.8 0.0 collective-permute-done.4.refs_4_.refs_5_
  37.8 0.0 collective-permute-done.3.refs_3_.refs_4_
  37.8 0.0 collective-permute-done.6.refs_6_.refs_7_
  37.8 0.0 collective-permute-done.5.refs_5_.refs_6_
  37.8 0.5 coulomb_pairs.3
  38.3 3.8 %collective-permute-start.8 = (bf16[2,2,128,128]{3,2,1,0:T(8,128)(2,1)S(1)}, bf16[2,2,128,128]{3,2,1,0:T(8,128)(2,1)S(1)}, u32[]{:S(2)}, u32[]{:S(2)}) collective-permute-start(bf16[2,2,128,128]{3,2,1,0:T(8,128)(2,1)S(1)} %get-tuple-element.36), channel_id=1, source_target_pairs={{0,8},{8,0},{1,9},{9,1},{2,10},{10,2},{3,11},{11,3},{4,12},{12,4},... | collective-permute-start | bytes 393224 | tf_op jit(solution)/shard_map/ppermute | solution.py:283
  42.1 0.0 collective-permute-done.7.refs_2_
  42.1 1.0 collective-permute-done.8.refs_3_
  43.1 0.8 sum_cores.1
  43.8 11.3 %all-to-all-start = ((bf16[32,40,128]{2,1,0:T(8,128)(2,1)}), bf16[32,40,128]{2,1,0:T(8,128)(2,1)S(1)}, u32[]{:S(2)}, u32[]{:S(2)}) async-start(bf16[32,40,128]{2,1,0:T(8,128)(2,1)} %sum_cores.1), calls=%async_computation | async-start | bytes 655360 | tf_op jit(solution)/shard_map/all_to_all | solution.py:303
  55.1 4.1 %collective-permute-start.11 = (bf16[448,256]{1,0:T(8,128)(2,1)S(1)}, bf16[448,256]{1,0:T(8,128)(2,1)S(1)}, u32[]{:S(2)}, u32[]{:S(2)}) collective-permute-start(bf16[448,256]{1,0:T(8,128)(2,1)S(1)} %collective-permute-done.3.refs_3_.refs_4_), channel_id=1, source_target_pairs={{0,7},{1,2},{2,1},{3,4},{4,3},{5,6},{6,5},{7,0},{8,15},{9,10},{10,... | collective-permute-start | bytes 688136 | tf_op jit(solution)/shard_map/ppermute | solution.py:280
  59.2 2.4 %collective-permute-start.12 = (bf16[448,256]{1,0:T(8,128)(2,1)S(1)}, bf16[448,256]{1,0:T(8,128)(2,1)}, u32[]{:S(2)}, u32[]{:S(2)}) collective-permute-start(bf16[448,256]{1,0:T(8,128)(2,1)S(1)} %collective-permute-done.4.refs_4_.refs_5_), channel_id=1, source_target_pairs={{0,7},{1,2},{2,1},{3,4},{4,3},{5,6},{6,5},{7,0},{8,15},{9,10},{10,... | collective-permute-start | bytes 688136 | tf_op jit(solution)/shard_map/ppermute | solution.py:280
  61.6 1.9 %collective-permute-start.9 = (bf16[448,256]{1,0:T(8,128)(2,1)S(1)}, bf16[448,256]{1,0:T(8,128)(2,1)S(1)}, u32[]{:S(2)}, u32[]{:S(2)}) collective-permute-start(bf16[448,256]{1,0:T(8,128)(2,1)S(1)} %collective-permute-done.5.refs_5_.refs_6_), channel_id=1, source_target_pairs={{0,1},{1,0},{2,3},{3,2},{4,5},{5,4},{6,7},{7,6},{8,9},{9,8},{10,11... | collective-permute-start | bytes 688136 | tf_op jit(solution)/shard_map/ppermute | solution.py:277
  63.6 3.4 %collective-permute-start.10 = (bf16[448,256]{1,0:T(8,128)(2,1)S(1)}, bf16[448,256]{1,0:T(8,128)(2,1)S(1)}, u32[]{:S(2)}, u32[]{:S(2)}) collective-permute-start(bf16[448,256]{1,0:T(8,128)(2,1)S(1)} %collective-permute-done.6.refs_6_.refs_7_), channel_id=1, source_target_pairs={{0,1},{1,0},{2,3},{3,2},{4,5},{5,4},{6,7},{7,6},{8,9},{9,8},{10,11... | collective-permute-start | bytes 688136 | tf_op jit(solution)/shard_map/ppermute | solution.py:277
  66.9 0.9 all-to-all-done.parts_ref
  67.9 11.8 %all_to_all.15.received_ref = bf16[8,16,128]{2,1,0:T(8,128)(2,1)S(1)} all-to-all(bf16[8,16,128]{2,1,0:T(8,128)(2,1)S(1)} %amplitude_sends.1), channel_id=1, replica_groups=mesh['x'=4,'z'=8,'core'=2,'pair'=8] {'pair'}, dimensions={0} | all-to-all | bytes 65536 | tf_op jit(solution)/shard_map/all_to_all | solution.py:304
  79.7 0.9 amplitude_copies.1
  80.6 0.0 collective-permute-done.11.refs_0_
  80.6 0.0 collective-permute-done.12.refs_1_
  80.6 0.0 collective-permute-done.9.refs_8_
  80.6 0.0 collective-permute-done.10.refs_9_
  80.6 8.3 %all-to-all-start.2 = ((bf16[32,64,128]{2,1,0:T(8,128)(2,1)}), bf16[32,64,128]{2,1,0:T(8,128)(2,1)S(1)}, u32[]{:S(2)}, u32[]{:S(2)}) async-start(bf16[32,64,128]{2,1,0:T(8,128)(2,1)} %amplitude_copies.1), calls=%async_computation.2 | async-start | bytes 1048576 | tf_op jit(solution)/shard_map/all_to_all | solution.py:309
  88.9 2.1 %collective-permute-start.13 = (bf16[448,256]{1,0:T(8,128)(2,1)S(1)}, bf16[448,256]{1,0:T(8,128)(2,1)S(1)}, u32[]{:S(2)}, u32[]{:S(2)}) collective-permute-start(bf16[448,256]{1,0:T(8,128)(2,1)S(1)} %collective-permute-done.9.refs_8_), channel_id=1, source_target_pairs={{0,7},{1,2},{2,1},{3,4},{4,3},{5,6},{6,5},{7,0},{8,15},{9,10},{10,... | collective-permute-start | bytes 688136 | tf_op jit(solution)/shard_map/ppermute | solution.py:280
  91.0 2.5 %collective-permute-start.14 = (bf16[448,256]{1,0:T(8,128)(2,1)}, bf16[448,256]{1,0:T(8,128)(2,1)S(1)}, u32[]{:S(2)}, u32[]{:S(2)}) collective-permute-start(bf16[448,256]{1,0:T(8,128)(2,1)} %collective-permute-done.12.refs_1_), channel_id=1, source_target_pairs={{0,1},{1,0},{2,3},{3,2},{4,5},{5,4},{6,7},{7,6},{8,9},{9,8},{10,11... | collective-permute-start | bytes 688136 | tf_op jit(solution)/shard_map/ppermute | solution.py:277
  93.5 3.6 %collective-permute-done.13.refs_11_ = bf16[448,256]{1,0:T(8,128)(2,1)S(1)} collective-permute-done((bf16[448,256]{1,0:T(8,128)(2,1)S(1)}, bf16[448,256]{1,0:T(8,128)(2,1)S(1)}, u32[]{:S(2)}, u32[]{:S(2)}) %collective-permute-start.13) | collective-permute-done | bytes 229408 | tf_op jit(solution)/shard_map/ppermute | solution.py:280
  97.2 0.0 copy-start.1
  97.2 0.7 copy-done.1
  97.8 0.4 collective-permute-done.14.refs_12_
  98.3 0.0 copy-start.3
  98.3 0.7 copy-done.3
  99.0 2.9 %all-to-all-done.2.mine_ref = bf16[32,64,128]{2,1,0:T(8,128)(2,1)S(1)} async-done(((bf16[32,64,128]{2,1,0:T(8,128)(2,1)}), bf16[32,64,128]{2,1,0:T(8,128)(2,1)S(1)}, u32[]{:S(2)}, u32[]{:S(2)}) %all-to-all-start.2) | async-done | bytes 524320 | tf_op jit(solution)/shard_map/all_to_all | solution.py:309
  101.9 0.0 copy-start.2
  101.9 8.0 %collective-permute-start.15 = (bf16[32,64,128]{2,1,0:T(8,128)(2,1)S(1)}, bf16[32,64,128]{2,1,0:T(8,128)(2,1)S(1)}, u32[]{:S(2)}, u32[]{:S(2)}) collective-permute-start(bf16[32,64,128]{2,1,0:T(8,128)(2,1)S(1)} %all-to-all-done.2.mine_ref), channel_id=1, source_target_pairs={{0,8},{8,0},{1,9},{9,1},{2,10},{10,2},{3,11},{11,3},{4,12},{12,4},... | collective-permute-start | bytes 1572872 | tf_op jit(solution)/shard_map/ppermute | solution.py:283
  110.0 1.3 %own_half.1 = (bf16[8,256,256]{2,1,0:T(8,128)(2,1)S(1)}, bf16[896,256]{1,0:T(8,128)(2,1)S(1)}) custom-call(bf16[32,64,128]{2,1,0:T(8,128)(2,1)S(1)} %all-to-all-done.2.mine_ref, f32[16,128]{1,0:T(8,128)S(1)} %get-tuple-element.48.scale.refs_15_, bf16[448,256]{1,0:T(8,128)(2,1)S(1)} %collective-permute-done.11.refs_0_, ...), custom_call_target="tpu_custom_call" | custom-call | tf_op jit(solution)/shard_map/own_half/pallas_call | solution.py:226
  111.3 0.2 collective-permute-done.15.refs_14_
  111.5 0.0 copy-done.2
  111.5 0.0 copy-done.4
  111.5 2.1 %gamma_rows.1 = (bf16[896,256]{1,0:T(8,128)(2,1)}, bf16[8,256,256]{2,1,0:T(8,128)(2,1)S(1)}) custom-call(bf16[896,256]{1,0:T(8,128)(2,1)S(1)} %copy-done, bf16[896,256]{1,0:T(8,128)(2,1)S(1)} %collective-permute-done.refs_1_.refs_0_, bf16[448,256]{1,0:T(8,128)(2,1)S(1)} %collective-permute-done.1.refs_2_.refs_1_, ...), custom_call_target="tpu_custom_call", output_to_operand_aliasing={{1}: (13, {})} | custom-call | tf_op jit(solution)/shard_map/gamma_rows/pallas_call | solution.py:261
  (3 shorter events, 0.1 us)
Async XLA Ops:
  0.0 22.6 %collective-permute-start = (bf16[896,256]{1,0:T(8,128)(2,1)}, bf16[896,256]{1,0:T(8,128)(2,1)S(1)}, u32[]{:S(2)}, u32[]{:S(2)}) collective-permute-start(bf16[896,256]{1,0:T(8,128)(2,1)} %refs_0_.3), channel_id=1, source_target_pairs={{0,1},{1,0},{2,3},{3,2},{4,5},{5,4},{6,7},{7,6},{8,9},{9,8},{10,11... | collective-permute-start | bytes 1376264 | tf_op jit(solution)/shard_map/ppermute | solution.py:277
  5.1 8.3 %collective-permute-start.2 = (bf16[448,256]{1,0:T(8,128)(2,1)S(1)}, bf16[448,256]{1,0:T(8,128)(2,1)S(1)}, u32[]{:S(2)}, u32[]{:S(2)}) collective-permute-start(bf16[448,256]{1,0:T(8,128)(2,1)S(1)} %get-tuple-element.57), channel_id=1, source_target_pairs={{0,7},{1,2},{2,1},{3,4},{4,3},{5,6},{6,5},{7,0},{8,15},{9,10},{10,... | collective-permute-start | bytes 688136 | tf_op jit(solution)/shard_map/ppermute | solution.py:280
  10.0 19.4 %copy-start.5 = (f32[20096]{0:T(1024)S(1)}, f32[20096]{0:T(1024)}, u32[]{:S(2)}) copy-start(f32[20096]{0:T(1024)} %param.8) | copy-start | bytes 241156
  10.0 20.1 %copy-start = (bf16[896,256]{1,0:T(8,128)(2,1)S(1)}, bf16[896,256]{1,0:T(8,128)(2,1)}, u32[]{:S(2)}) copy-start(bf16[896,256]{1,0:T(8,128)(2,1)} %refs_0_.3) | copy-start | bytes 1376260
  10.0 10.7 %collective-permute-start.1 = (bf16[448,256]{1,0:T(8,128)(2,1)S(1)}, bf16[448,256]{1,0:T(8,128)(2,1)S(1)}, u32[]{:S(2)}, u32[]{:S(2)}) collective-permute-start(bf16[448,256]{1,0:T(8,128)(2,1)S(1)} %get-tuple-element.58), channel_id=1, source_target_pairs={{0,7},{1,2},{2,1},{3,4},{4,3},{5,6},{6,5},{7,0},{8,15},{9,10},{10,... | collective-permute-start | bytes 688136 | tf_op jit(solution)/shard_map/ppermute | solution.py:280
  13.4 24.4 %collective-permute-start.4 = (bf16[448,256]{1,0:T(8,128)(2,1)S(1)}, bf16[448,256]{1,0:T(8,128)(2,1)S(1)}, u32[]{:S(2)}, u32[]{:S(2)}) collective-permute-start(bf16[448,256]{1,0:T(8,128)(2,1)S(1)} %collective-permute-done.2.refs_3_.refs_2_), channel_id=1, source_target_pairs={{0,1},{1,0},{2,3},{3,2},{4,5},{5,4},{6,7},{7,6},{8,9},{9,8},{10,11... | collective-permute-start | bytes 688136 | tf_op jit(solution)/shard_map/ppermute | solution.py:277
  20.7 17.1 %collective-permute-start.3 = (bf16[448,256]{1,0:T(8,128)(2,1)S(1)}, bf16[448,256]{1,0:T(8,128)(2,1)S(1)}, u32[]{:S(2)}, u32[]{:S(2)}) collective-permute-start(bf16[448,256]{1,0:T(8,128)(2,1)S(1)} %collective-permute-done.1.refs_2_.refs_1_), channel_id=1, source_target_pairs={{0,1},{1,0},{2,3},{3,2},{4,5},{5,4},{6,7},{7,6},{8,9},{9,8},{10,11... | collective-permute-start | bytes 688136 | tf_op jit(solution)/shard_map/ppermute | solution.py:277
  22.7 15.1 %collective-permute-start.6 = (bf16[448,256]{1,0:T(8,128)(2,1)S(1)}, bf16[448,256]{1,0:T(8,128)(2,1)S(1)}, u32[]{:S(2)}, u32[]{:S(2)}) collective-permute-start(bf16[448,256]{1,0:T(8,128)(2,1)S(1)} %get-tuple-element.55), channel_id=1, source_target_pairs={{0,7},{1,2},{2,1},{3,4},{4,3},{5,6},{6,5},{7,0},{8,15},{9,10},{10,... | collective-permute-start | bytes 688136 | tf_op jit(solution)/shard_map/ppermute | solution.py:280
  25.9 3.4 %copy-start.9 = (s32[16]{0:T(128)S(1)}, s32[16]{0:T(128)}, u32[]{:S(2)}) copy-start(s32[16]{0:T(128)} %exponent.1) | copy-start | bytes 196
  25.9 3.4 %copy-start.6 = (f32[64]{0:T(128)S(1)}, f32[64]{0:T(128)}, u32[]{:S(2)}) copy-start(f32[64]{0:T(128)} %occupied.1) | copy-start | bytes 772
  25.9 3.4 %copy-start.7 = (s32[16]{0:T(128)S(1)}, s32[16]{0:T(128)}, u32[]{:S(2)}) copy-start(s32[16]{0:T(128)} %occupied_of.1) | copy-start | bytes 196
  26.0 3.4 %copy-start.8 = (s32[16]{0:T(128)S(1)}, s32[16]{0:T(128)}, u32[]{:S(2)}) copy-start(s32[16]{0:T(128)} %virtual_of.1) | copy-start | bytes 196
  26.0 11.8 %collective-permute-start.5 = (bf16[448,256]{1,0:T(8,128)(2,1)S(1)}, bf16[448,256]{1,0:T(8,128)(2,1)S(1)}, u32[]{:S(2)}, u32[]{:S(2)}) collective-permute-start(bf16[448,256]{1,0:T(8,128)(2,1)S(1)} %get-tuple-element.56), channel_id=1, source_target_pairs={{0,7},{1,2},{2,1},{3,4},{4,3},{5,6},{6,5},{7,0},{8,15},{9,10},{10,... | collective-permute-start | bytes 688136 | tf_op jit(solution)/shard_map/ppermute | solution.py:280
  30.7 11.3 %collective-permute-start.7 = (bf16[3,2,128,128]{3,2,1,0:T(8,128)(2,1)S(1)}, bf16[3,2,128,128]{3,2,1,0:T(8,128)(2,1)S(1)}, u32[]{:S(2)}, u32[]{:S(2)}) collective-permute-start(bf16[3,2,128,128]{3,2,1,0:T(8,128)(2,1)S(1)} %get-tuple-element.35), channel_id=1, source_target_pairs={{0,8},{8,0},{1,9},{9,1},{2,10},{10,2},{3,11},{11,3},{4,12},{12,4},... | collective-permute-start | bytes 589832 | tf_op jit(solution)/shard_map/ppermute | solution.py:283
  38.3 4.8 %collective-permute-start.8 = (bf16[2,2,128,128]{3,2,1,0:T(8,128)(2,1)S(1)}, bf16[2,2,128,128]{3,2,1,0:T(8,128)(2,1)S(1)}, u32[]{:S(2)}, u32[]{:S(2)}) collective-permute-start(bf16[2,2,128,128]{3,2,1,0:T(8,128)(2,1)S(1)} %get-tuple-element.36), channel_id=1, source_target_pairs={{0,8},{8,0},{1,9},{9,1},{2,10},{10,2},{3,11},{11,3},{4,12},{12,4},... | collective-permute-start | bytes 393224 | tf_op jit(solution)/shard_map/ppermute | solution.py:283
  43.8 24.1 %all-to-all-start = ((bf16[32,40,128]{2,1,0:T(8,128)(2,1)}), bf16[32,40,128]{2,1,0:T(8,128)(2,1)S(1)}, u32[]{:S(2)}, u32[]{:S(2)}) async-start(bf16[32,40,128]{2,1,0:T(8,128)(2,1)} %sum_cores.1), calls=%async_computation | async-start | bytes 655360 | tf_op jit(solution)/shard_map/all_to_all | solution.py:303
  55.1 25.5 %collective-permute-start.11 = (bf16[448,256]{1,0:T(8,128)(2,1)S(1)}, bf16[448,256]{1,0:T(8,128)(2,1)S(1)}, u32[]{:S(2)}, u32[]{:S(2)}) collective-permute-start(bf16[448,256]{1,0:T(8,128)(2,1)S(1)} %collective-permute-done.3.refs_3_.refs_4_), channel_id=1, source_target_pairs={{0,7},{1,2},{2,1},{3,4},{4,3},{5,6},{6,5},{7,0},{8,15},{9,10},{10,... | collective-permute-start | bytes 688136 | tf_op jit(solution)/shard_map/ppermute | solution.py:280
  59.2 21.4 %collective-permute-start.12 = (bf16[448,256]{1,0:T(8,128)(2,1)S(1)}, bf16[448,256]{1,0:T(8,128)(2,1)}, u32[]{:S(2)}, u32[]{:S(2)}) collective-permute-start(bf16[448,256]{1,0:T(8,128)(2,1)S(1)} %collective-permute-done.4.refs_4_.refs_5_), channel_id=1, source_target_pairs={{0,7},{1,2},{2,1},{3,4},{4,3},{5,6},{6,5},{7,0},{8,15},{9,10},{10,... | collective-permute-start | bytes 688136 | tf_op jit(solution)/shard_map/ppermute | solution.py:280
  61.6 19.0 %collective-permute-start.9 = (bf16[448,256]{1,0:T(8,128)(2,1)S(1)}, bf16[448,256]{1,0:T(8,128)(2,1)S(1)}, u32[]{:S(2)}, u32[]{:S(2)}) collective-permute-start(bf16[448,256]{1,0:T(8,128)(2,1)S(1)} %collective-permute-done.5.refs_5_.refs_6_), channel_id=1, source_target_pairs={{0,1},{1,0},{2,3},{3,2},{4,5},{5,4},{6,7},{7,6},{8,9},{9,8},{10,11... | collective-permute-start | bytes 688136 | tf_op jit(solution)/shard_map/ppermute | solution.py:277
  63.6 17.1 %collective-permute-start.10 = (bf16[448,256]{1,0:T(8,128)(2,1)S(1)}, bf16[448,256]{1,0:T(8,128)(2,1)S(1)}, u32[]{:S(2)}, u32[]{:S(2)}) collective-permute-start(bf16[448,256]{1,0:T(8,128)(2,1)S(1)} %collective-permute-done.6.refs_6_.refs_7_), channel_id=1, source_target_pairs={{0,1},{1,0},{2,3},{3,2},{4,5},{5,4},{6,7},{7,6},{8,9},{9,8},{10,11... | collective-permute-start | bytes 688136 | tf_op jit(solution)/shard_map/ppermute | solution.py:277
  80.6 21.3 %all-to-all-start.2 = ((bf16[32,64,128]{2,1,0:T(8,128)(2,1)}), bf16[32,64,128]{2,1,0:T(8,128)(2,1)S(1)}, u32[]{:S(2)}, u32[]{:S(2)}) async-start(bf16[32,64,128]{2,1,0:T(8,128)(2,1)} %amplitude_copies.1), calls=%async_computation.2 | async-start | bytes 1048576 | tf_op jit(solution)/shard_map/all_to_all | solution.py:309
  88.9 8.2 %collective-permute-start.13 = (bf16[448,256]{1,0:T(8,128)(2,1)S(1)}, bf16[448,256]{1,0:T(8,128)(2,1)S(1)}, u32[]{:S(2)}, u32[]{:S(2)}) collective-permute-start(bf16[448,256]{1,0:T(8,128)(2,1)S(1)} %collective-permute-done.9.refs_8_), channel_id=1, source_target_pairs={{0,7},{1,2},{2,1},{3,4},{4,3},{5,6},{6,5},{7,0},{8,15},{9,10},{10,... | collective-permute-start | bytes 688136 | tf_op jit(solution)/shard_map/ppermute | solution.py:280
  91.0 7.3 %collective-permute-start.14 = (bf16[448,256]{1,0:T(8,128)(2,1)}, bf16[448,256]{1,0:T(8,128)(2,1)S(1)}, u32[]{:S(2)}, u32[]{:S(2)}) collective-permute-start(bf16[448,256]{1,0:T(8,128)(2,1)} %collective-permute-done.12.refs_1_), channel_id=1, source_target_pairs={{0,1},{1,0},{2,3},{3,2},{4,5},{5,4},{6,7},{7,6},{8,9},{9,8},{10,11... | collective-permute-start | bytes 688136 | tf_op jit(solution)/shard_map/ppermute | solution.py:277
  97.2 0.7 copy-start.1
  98.3 0.7 copy-start.3
  101.9 9.6 %copy-start.2 = (bf16[448,256]{1,0:T(8,128)(2,1)S(1)}, bf16[448,256]{1,0:T(8,128)(2,1)}, u32[]{:S(2)}) copy-start(bf16[448,256]{1,0:T(8,128)(2,1)} %copy-done.1) | copy-start | bytes 688132
  101.9 9.6 %copy-start.4 = (bf16[448,256]{1,0:T(8,128)(2,1)S(1)}, bf16[448,256]{1,0:T(8,128)(2,1)}, u32[]{:S(2)}) copy-start(bf16[448,256]{1,0:T(8,128)(2,1)} %copy-done.3) | copy-start | bytes 688132
  101.9 9.6 %collective-permute-start.15 = (bf16[32,64,128]{2,1,0:T(8,128)(2,1)S(1)}, bf16[32,64,128]{2,1,0:T(8,128)(2,1)S(1)}, u32[]{:S(2)}, u32[]{:S(2)}) collective-permute-start(bf16[32,64,128]{2,1,0:T(8,128)(2,1)S(1)} %all-to-all-done.2.mine_ref), channel_id=1, source_target_pairs={{0,8},{8,0},{1,9},{9,1},{2,10},{10,2},{3,11},{11,3},{4,12},{12,4},... | collective-permute-start | bytes 1572872 | tf_op jit(solution)/shard_map/ppermute | solution.py:283

commit v23 on v20

--- a/solution.py
+++ b/solution.py
@@ -247,7 +247,8 @@
         for count in counts:
             block.append(given[:count])
             given = given[count:]
-        _, other, scale, out, matrix = refs[sum(counts) :]
+        _, other, scale, out, matrix, held, sent = refs[sum(counts) :]
+        sends = []
         lay_out(other, 1 - lax.axis_index("core"), scale, matrix)
         for start in range(0, rows, ROWS):
             total = None
@@ -256,7 +257,12 @@
                 left = parts[part][offset : offset + ROWS]
                 term = jnp.dot(left, matrix[i], preferred_element_type=f32)
                 total = term if total is None else total + term
-            out[start : start + ROWS] = total.astype(bf16)
+            here = slice(start, start + ROWS)
+            held[here] = total.astype(bf16)
+            sends.append(pltpu.make_async_copy(held.at[here], out.at[here], sent.at[len(sends)]))
+            sends[-1].start()
+        for send in sends:
+            send.wait()
 
     return pl.pallas_call(
         kernel,
@@ -265,7 +271,11 @@
             jax.ShapeDtypeStruct(half.shape, half.dtype),
         ),
         in_specs=[in_vmem] * (sum(counts) + 3),
-        out_specs=(in_vmem, in_vmem),
+        out_specs=(anywhere, in_vmem),
+        scratch_shapes=[
+            pltpu.VMEM((rows, width), bf16),
+            pltpu.SemaphoreType.DMA((rows // ROWS,)),
+        ],
         input_output_aliases={sum(counts): 1},
         compiler_params=pltpu.CompilerParams(vmem_limit_bytes=VMEM_LIMIT),
         name="gamma_rows",

time: 107 us -> 106 us (level)
  no operation moved by 1% of the time
where the time goes in v23:
time: 106 us
  starting transfers between devices  72.6 us (68%)
  waiting for transfers between devices  12.7 us (12%)
  blocking collectives  10.6 us (10%)
  Pallas kernels  6.94 us (7%)
  local copies, waits for them, and re-layouts  2.52 us (2%)
    ppermute x6, starting transfers between devices, swap_b(): return lax.ppermute(x, 'pair', SWAP_B)  22.9 us
    ppermute x3, starting transfers between devices, swap_cores(): return lax.ppermute(x, 'core', SWAP_CORES)  17.8 us
    ppermute x5, starting transfers between devices, swap_a(): return lax.ppermute(x, 'pair', SWAP_A)  13.7 us
    all_to_all x1, starting transfers between devices, body(): parts = lax.all_to_all(summed, ('z', 'x'), 0, 0)  12.9 us
    all_to_all x1, blocking collectives, body(): received = lax.all_to_all(amplitude_sends(parts, denominator), 'pair', 0, 0)  10.6 us
    all_to_all x1, starting transfers between devices, body(): mine = lax.all_to_all(copies, ('z', 'x'), 0, 0)  5.37 us
    all_to_all x1, waiting for transfers between devices, body(): parts = lax.all_to_all(summed, ('z', 'x'), 0, 0)  4.32 us
    ppermute x6, waiting for transfers between devices, swap_b(): return lax.ppermute(x, 'pair', SWAP_B)  3.72 us
  transfers between devices with their start and end apart: 16, of which 6 were waited for; matrix products, arithmetic and copies ran while one was open for 1% of the time, Pallas kernels for 4%

profile of v23, /device:TPU:1, one launch (start us, length us, event | category | flops | bytes accessed | tf_op | source)
XLA Modules:
  0.0 105.7 jit_solution(15347791499684352006)
XLA Ops:
  0.0 0.0 copy-start
  0.0 0.0 copy-start.5
  0.0 4.2 %collective-permute-start = (bf16[896,256]{1,0:T(8,128)(2,1)}, bf16[896,256]{1,0:T(8,128)(2,1)S(1)}, u32[]{:S(2)}, u32[]{:S(2)}) collective-permute-start(bf16[896,256]{1,0:T(8,128)(2,1)} %refs_0_.3), channel_id=1, source_target_pairs={{0,1},{1,0},{2,3},{3,2},{4,5},{5,4},{6,7},{7,6},{8,9},{9,8},{10,11... | collective-permute-start | bytes 1376264 | tf_op jit(solution)/shard_map/ppermute | solution.py:287
  4.2 1.1 %fusion = (bf16[448,256]{1,0:T(8,128)(2,1)S(1)}, bf16[448,256]{1,0:T(8,128)(2,1)S(1)}) fusion(bf16[896,256]{1,0:T(8,128)(2,1)} %refs_0_.3), kind=kLoop, calls=%fused_computation | loop fusion | bytes 917504 | tf_op jit(solution)/shard_map/slice | solution.py:298
  5.2 4.9 %collective-permute-start.2 = (bf16[448,256]{1,0:T(8,128)(2,1)S(1)}, bf16[448,256]{1,0:T(8,128)(2,1)S(1)}, u32[]{:S(2)}, u32[]{:S(2)}) collective-permute-start(bf16[448,256]{1,0:T(8,128)(2,1)S(1)} %get-tuple-element.51), channel_id=1, source_target_pairs={{0,7},{1,2},{2,1},{3,4},{4,3},{5,6},{6,5},{7,0},{8,15},{9,10},{10,... | collective-permute-start | bytes 688136 | tf_op jit(solution)/shard_map/ppermute | solution.py:290
  10.1 0.0 copy-start.9
  10.1 0.0 copy-start.6
  10.2 0.0 copy-start.7
  10.2 0.0 copy-start.8
  10.2 2.1 %collective-permute-start.1 = (bf16[448,256]{1,0:T(8,128)(2,1)S(1)}, bf16[448,256]{1,0:T(8,128)(2,1)S(1)}, u32[]{:S(2)}, u32[]{:S(2)}) collective-permute-start(bf16[448,256]{1,0:T(8,128)(2,1)S(1)} %get-tuple-element.52), channel_id=1, source_target_pairs={{0,7},{1,2},{2,1},{3,4},{4,3},{5,6},{6,5},{7,0},{8,15},{9,10},{10,... | collective-permute-start | bytes 688136 | tf_op jit(solution)/shard_map/ppermute | solution.py:290
  12.2 0.0 collective-permute-done.refs_1_.refs_0_
  12.2 7.3 %collective-permute-start.5 = (bf16[896,256]{1,0:T(8,128)(2,1)S(1)}, bf16[896,256]{1,0:T(8,128)(2,1)S(1)}, u32[]{:S(2)}, u32[]{:S(2)}) collective-permute-start(bf16[896,256]{1,0:T(8,128)(2,1)S(1)} %collective-permute-done.refs_1_.refs_0_), channel_id=1, source_target_pairs={{0,7},{1,2},{2,1},{3,4},{4,3},{5,6},{6,5},{7,0},{8,15},{9,10},{10,... | collective-permute-start | bytes 1376264 | tf_op jit(solution)/shard_map/ppermute | solution.py:290
  19.5 0.0 collective-permute-done.2.refs_3_.refs_2_
  19.5 1.9 %collective-permute-start.4 = (bf16[448,256]{1,0:T(8,128)(2,1)S(1)}, bf16[448,256]{1,0:T(8,128)(2,1)S(1)}, u32[]{:S(2)}, u32[]{:S(2)}) collective-permute-start(bf16[448,256]{1,0:T(8,128)(2,1)S(1)} %collective-permute-done.2.refs_3_.refs_2_), channel_id=1, source_target_pairs={{0,1},{1,0},{2,3},{3,2},{4,5},{5,4},{6,7},{7,6},{8,9},{9,8},{10,11... | collective-permute-start | bytes 688136 | tf_op jit(solution)/shard_map/ppermute | solution.py:287
  21.5 0.0 collective-permute-done.1.refs_2_.refs_1_
  21.5 3.4 %collective-permute-start.3 = (bf16[448,256]{1,0:T(8,128)(2,1)S(1)}, bf16[448,256]{1,0:T(8,128)(2,1)S(1)}, u32[]{:S(2)}, u32[]{:S(2)}) collective-permute-start(bf16[448,256]{1,0:T(8,128)(2,1)S(1)} %collective-permute-done.1.refs_2_.refs_1_), channel_id=1, source_target_pairs={{0,1},{1,0},{2,3},{3,2},{4,5},{5,4},{6,7},{7,6},{8,9},{9,8},{10,11... | collective-permute-start | bytes 688136 | tf_op jit(solution)/shard_map/ppermute | solution.py:287
  24.9 0.0 copy-done.5
  24.9 0.0 copy-done.9
  24.9 0.0 copy-done.6
  24.9 0.0 copy-done.7
  24.9 0.0 copy-done.8
  24.9 0.7 tables.1
  25.6 0.0 copy-done
  25.6 0.6 coulomb_pairs.2
  26.3 5.5 %collective-permute-start.6 = (bf16[3,2,128,128]{3,2,1,0:T(8,128)(2,1)S(1)}, bf16[3,2,128,128]{3,2,1,0:T(8,128)(2,1)S(1)}, u32[]{:S(2)}, u32[]{:S(2)}) collective-permute-start(bf16[3,2,128,128]{3,2,1,0:T(8,128)(2,1)S(1)} %get-tuple-element.33), channel_id=1, source_target_pairs={{0,8},{8,0},{1,9},{9,1},{2,10},{10,2},{3,11},{11,3},{4,12},{12,4},... | collective-permute-start | bytes 589832 | tf_op jit(solution)/shard_map/ppermute | solution.py:293
  31.8 0.0 collective-permute-done.4.refs_4_.refs_5_
  31.8 0.0 collective-permute-done.3.refs_3_.refs_4_
  31.8 0.0 collective-permute-done.5.refs_5_.refs_6_
  31.8 0.5 coulomb_pairs.3
  32.3 4.5 %collective-permute-start.7 = (bf16[2,2,128,128]{3,2,1,0:T(8,128)(2,1)S(1)}, bf16[2,2,128,128]{3,2,1,0:T(8,128)(2,1)S(1)}, u32[]{:S(2)}, u32[]{:S(2)}) collective-permute-start(bf16[2,2,128,128]{3,2,1,0:T(8,128)(2,1)S(1)} %get-tuple-element.34), channel_id=1, source_target_pairs={{0,8},{8,0},{1,9},{9,1},{2,10},{10,2},{3,11},{11,3},{4,12},{12,4},... | collective-permute-start | bytes 393224 | tf_op jit(solution)/shard_map/ppermute | solution.py:293
  36.8 0.0 collective-permute-done.6.refs_2_
  36.8 1.0 collective-permute-done.7.refs_3_
  37.8 0.8 sum_cores.1
  38.6 12.9 %all-to-all-start = ((bf16[32,40,128]{2,1,0:T(8,128)(2,1)}), bf16[32,40,128]{2,1,0:T(8,128)(2,1)S(1)}, u32[]{:S(2)}, u32[]{:S(2)}) async-start(bf16[32,40,128]{2,1,0:T(8,128)(2,1)} %sum_cores.1), calls=%async_computation | async-start | bytes 655360 | tf_op jit(solution)/shard_map/all_to_all | solution.py:312
  51.4 1.9 %collective-permute-start.8 = (bf16[896,256]{1,0:T(8,128)(2,1)S(1)}, bf16[896,256]{1,0:T(8,128)(2,1)S(1)}, u32[]{:S(2)}, u32[]{:S(2)}) collective-permute-start(bf16[896,256]{1,0:T(8,128)(2,1)S(1)} %collective-permute-done.5.refs_5_.refs_6_), channel_id=1, source_target_pairs={{0,1},{1,0},{2,3},{3,2},{4,5},{5,4},{6,7},{7,6},{8,9},{9,8},{10,11... | collective-permute-start | bytes 1376264 | tf_op jit(solution)/shard_map/ppermute | solution.py:287
  53.4 4.0 %collective-permute-start.9 = (bf16[448,256]{1,0:T(8,128)(2,1)S(1)}, bf16[448,256]{1,0:T(8,128)(2,1)S(1)}, u32[]{:S(2)}, u32[]{:S(2)}) collective-permute-start(bf16[448,256]{1,0:T(8,128)(2,1)S(1)} %collective-permute-done.3.refs_3_.refs_4_), channel_id=1, source_target_pairs={{0,7},{1,2},{2,1},{3,4},{4,3},{5,6},{6,5},{7,0},{8,15},{9,10},{10,... | collective-permute-start | bytes 688136 | tf_op jit(solution)/shard_map/ppermute | solution.py:290
  57.4 2.5 %collective-permute-start.10 = (bf16[448,256]{1,0:T(8,128)(2,1)S(1)}, bf16[448,256]{1,0:T(8,128)(2,1)}, u32[]{:S(2)}, u32[]{:S(2)}) collective-permute-start(bf16[448,256]{1,0:T(8,128)(2,1)S(1)} %collective-permute-done.4.refs_4_.refs_5_), channel_id=1, source_target_pairs={{0,7},{1,2},{2,1},{3,4},{4,3},{5,6},{6,5},{7,0},{8,15},{9,10},{10,... | collective-permute-start | bytes 688136 | tf_op jit(solution)/shard_map/ppermute | solution.py:290
  59.9 4.3 %all-to-all-done.parts_ref = bf16[32,40,128]{2,1,0:T(8,128)(2,1)S(1)} async-done(((bf16[32,40,128]{2,1,0:T(8,128)(2,1)}), bf16[32,40,128]{2,1,0:T(8,128)(2,1)S(1)}, u32[]{:S(2)}, u32[]{:S(2)}) %all-to-all-start) | async-done | bytes 327712 | tf_op jit(solution)/shard_map/all_to_all | solution.py:312
  64.2 10.6 %all_to_all.15.received_ref = bf16[8,16,128]{2,1,0:T(8,128)(2,1)S(1)} all-to-all(bf16[8,16,128]{2,1,0:T(8,128)(2,1)S(1)} %amplitude_sends.1), channel_id=1, replica_groups=mesh['x'=4,'z'=8,'core'=2,'pair'=8] {'pair'}, dimensions={0} | all-to-all | bytes 65536 | tf_op jit(solution)/shard_map/all_to_all | solution.py:313
  74.8 0.9 amplitude_copies.1
  75.7 0.0 collective-permute-done.9.refs_0_
  75.7 0.0 collective-permute-done.10.refs_1_
  75.7 0.0 collective-permute-done.8.refs_7_
  75.7 5.4 %all-to-all-start.2 = ((bf16[32,64,128]{2,1,0:T(8,128)(2,1)}), bf16[32,64,128]{2,1,0:T(8,128)(2,1)S(1)}, u32[]{:S(2)}, u32[]{:S(2)}) async-start(bf16[32,64,128]{2,1,0:T(8,128)(2,1)} %amplitude_copies.1), calls=%async_computation.2 | async-start | bytes 1048576 | tf_op jit(solution)/shard_map/all_to_all | solution.py:318
  81.2 2.2 %collective-permute-start.11 = (bf16[448,256]{1,0:T(8,128)(2,1)S(1)}, bf16[448,256]{1,0:T(8,128)(2,1)S(1)}, u32[]{:S(2)}, u32[]{:S(2)}) collective-permute-start(bf16[448,256]{1,0:T(8,128)(2,1)S(1)} %slice.11), channel_id=1, source_target_pairs={{0,7},{1,2},{2,1},{3,4},{4,3},{5,6},{6,5},{7,0},{8,15},{9,10},{10,... | collective-permute-start | bytes 688136 | tf_op jit(solution)/shard_map/ppermute | solution.py:290
  83.3 2.4 %collective-permute-start.12 = (bf16[448,256]{1,0:T(8,128)(2,1)}, bf16[448,256]{1,0:T(8,128)(2,1)S(1)}, u32[]{:S(2)}, u32[]{:S(2)}) collective-permute-start(bf16[448,256]{1,0:T(8,128)(2,1)} %collective-permute-done.10.refs_1_), channel_id=1, source_target_pairs={{0,1},{1,0},{2,3},{3,2},{4,5},{5,4},{6,7},{7,6},{8,9},{9,8},{10,11... | collective-permute-start | bytes 688136 | tf_op jit(solution)/shard_map/ppermute | solution.py:287
  85.7 3.7 %collective-permute-done.11.refs_9_ = bf16[448,256]{1,0:T(8,128)(2,1)S(1)} collective-permute-done((bf16[448,256]{1,0:T(8,128)(2,1)S(1)}, bf16[448,256]{1,0:T(8,128)(2,1)S(1)}, u32[]{:S(2)}, u32[]{:S(2)}) %collective-permute-start.11) | collective-permute-done | bytes 229408 | tf_op jit(solution)/shard_map/ppermute | solution.py:290
  89.4 0.0 copy-start.1
  89.4 0.7 copy-done.1
  90.1 0.5 collective-permute-done.12.refs_10_
  90.6 0.0 copy-start.3
  90.6 0.7 copy-done.3
  91.3 3.0 %all-to-all-done.2.mine_ref = bf16[32,64,128]{2,1,0:T(8,128)(2,1)S(1)} async-done(((bf16[32,64,128]{2,1,0:T(8,128)(2,1)}), bf16[32,64,128]{2,1,0:T(8,128)(2,1)S(1)}, u32[]{:S(2)}, u32[]{:S(2)}) %all-to-all-start.2) | async-done | bytes 524320 | tf_op jit(solution)/shard_map/all_to_all | solution.py:318
  94.4 0.0 copy-start.2
  94.4 0.0 copy-start.4
  94.4 7.8 %collective-permute-start.13 = (bf16[32,64,128]{2,1,0:T(8,128)(2,1)S(1)}, bf16[32,64,128]{2,1,0:T(8,128)(2,1)S(1)}, u32[]{:S(2)}, u32[]{:S(2)}) collective-permute-start(bf16[32,64,128]{2,1,0:T(8,128)(2,1)S(1)} %all-to-all-done.2.mine_ref), channel_id=1, source_target_pairs={{0,8},{8,0},{1,9},{9,1},{2,10},{10,2},{3,11},{11,3},{4,12},{12,4},... | collective-permute-start | bytes 1572872 | tf_op jit(solution)/shard_map/ppermute | solution.py:293
  102.2 1.3 %own_half.1 = (bf16[8,256,256]{2,1,0:T(8,128)(2,1)S(1)}, bf16[896,256]{1,0:T(8,128)(2,1)S(1)}) custom-call(bf16[32,64,128]{2,1,0:T(8,128)(2,1)S(1)} %all-to-all-done.2.mine_ref, f32[16,128]{1,0:T(8,128)S(1)} %get-tuple-element.44.scale.refs_13_, bf16[448,256]{1,0:T(8,128)(2,1)S(1)} %collective-permute-done.9.refs_0_, ...), custom_call_target="tpu_custom_call" | custom-call | tf_op jit(solution)/shard_map/own_half/pallas_call | solution.py:226
  103.5 0.2 collective-permute-done.13.refs_12_
  103.7 0.0 copy-done.2
  103.7 0.0 copy-done.4
  103.7 2.0 %gamma_rows.1 = (bf16[896,256]{1,0:T(8,128)(2,1)}, bf16[8,256,256]{2,1,0:T(8,128)(2,1)S(1)}) custom-call(bf16[896,256]{1,0:T(8,128)(2,1)S(1)} %copy-done, bf16[896,256]{1,0:T(8,128)(2,1)S(1)} %collective-permute-done.refs_1_.refs_0_, bf16[448,256]{1,0:T(8,128)(2,1)S(1)} %collective-permute-done.1.refs_2_.refs_1_, ...), custom_call_target="tpu_custom_call", output_to_operand_aliasing={{1}: (11, {})} | custom-call | tf_op jit(solution)/shard_map/gamma_rows/pallas_call | solution.py:267
  (2 shorter events, 0.1 us)
Async XLA Ops:
  0.0 25.6 %copy-start = (bf16[896,256]{1,0:T(8,128)(2,1)S(1)}, bf16[896,256]{1,0:T(8,128)(2,1)}, u32[]{:S(2)}) copy-start(bf16[896,256]{1,0:T(8,128)(2,1)} %refs_0_.3) | copy-start | bytes 1376260
  0.0 24.9 %copy-start.5 = (f32[20096]{0:T(1024)S(1)}, f32[20096]{0:T(1024)}, u32[]{:S(2)}) copy-start(f32[20096]{0:T(1024)} %param.8) | copy-start | bytes 241156
  0.0 12.2 %collective-permute-start = (bf16[896,256]{1,0:T(8,128)(2,1)}, bf16[896,256]{1,0:T(8,128)(2,1)S(1)}, u32[]{:S(2)}, u32[]{:S(2)}) collective-permute-start(bf16[896,256]{1,0:T(8,128)(2,1)} %refs_0_.3), channel_id=1, source_target_pairs={{0,1},{1,0},{2,3},{3,2},{4,5},{5,4},{6,7},{7,6},{8,9},{9,8},{10,11... | collective-permute-start | bytes 1376264 | tf_op jit(solution)/shard_map/ppermute | solution.py:287
  5.2 14.3 %collective-permute-start.2 = (bf16[448,256]{1,0:T(8,128)(2,1)S(1)}, bf16[448,256]{1,0:T(8,128)(2,1)S(1)}, u32[]{:S(2)}, u32[]{:S(2)}) collective-permute-start(bf16[448,256]{1,0:T(8,128)(2,1)S(1)} %get-tuple-element.51), channel_id=1, source_target_pairs={{0,7},{1,2},{2,1},{3,4},{4,3},{5,6},{6,5},{7,0},{8,15},{9,10},{10,... | collective-permute-start | bytes 688136 | tf_op jit(solution)/shard_map/ppermute | solution.py:290
  10.1 14.7 %copy-start.9 = (s32[16]{0:T(128)S(1)}, s32[16]{0:T(128)}, u32[]{:S(2)}) copy-start(s32[16]{0:T(128)} %exponent.1) | copy-start | bytes 196
  10.1 14.7 %copy-start.6 = (f32[64]{0:T(128)S(1)}, f32[64]{0:T(128)}, u32[]{:S(2)}) copy-start(f32[64]{0:T(128)} %occupied.1) | copy-start | bytes 772
  10.2 14.7 %copy-start.7 = (s32[16]{0:T(128)S(1)}, s32[16]{0:T(128)}, u32[]{:S(2)}) copy-start(s32[16]{0:T(128)} %occupied_of.1) | copy-start | bytes 196
  10.2 14.7 %copy-start.8 = (s32[16]{0:T(128)S(1)}, s32[16]{0:T(128)}, u32[]{:S(2)}) copy-start(s32[16]{0:T(128)} %virtual_of.1) | copy-start | bytes 196
  10.2 11.3 %collective-permute-start.1 = (bf16[448,256]{1,0:T(8,128)(2,1)S(1)}, bf16[448,256]{1,0:T(8,128)(2,1)S(1)}, u32[]{:S(2)}, u32[]{:S(2)}) collective-permute-start(bf16[448,256]{1,0:T(8,128)(2,1)S(1)} %get-tuple-element.52), channel_id=1, source_target_pairs={{0,7},{1,2},{2,1},{3,4},{4,3},{5,6},{6,5},{7,0},{8,15},{9,10},{10,... | collective-permute-start | bytes 688136 | tf_op jit(solution)/shard_map/ppermute | solution.py:290
  12.2 19.5 %collective-permute-start.5 = (bf16[896,256]{1,0:T(8,128)(2,1)S(1)}, bf16[896,256]{1,0:T(8,128)(2,1)S(1)}, u32[]{:S(2)}, u32[]{:S(2)}) collective-permute-start(bf16[896,256]{1,0:T(8,128)(2,1)S(1)} %collective-permute-done.refs_1_.refs_0_), channel_id=1, source_target_pairs={{0,7},{1,2},{2,1},{3,4},{4,3},{5,6},{6,5},{7,0},{8,15},{9,10},{10,... | collective-permute-start | bytes 1376264 | tf_op jit(solution)/shard_map/ppermute | solution.py:290
  19.5 12.2 %collective-permute-start.4 = (bf16[448,256]{1,0:T(8,128)(2,1)S(1)}, bf16[448,256]{1,0:T(8,128)(2,1)S(1)}, u32[]{:S(2)}, u32[]{:S(2)}) collective-permute-start(bf16[448,256]{1,0:T(8,128)(2,1)S(1)} %collective-permute-done.2.refs_3_.refs_2_), channel_id=1, source_target_pairs={{0,1},{1,0},{2,3},{3,2},{4,5},{5,4},{6,7},{7,6},{8,9},{9,8},{10,11... | collective-permute-start | bytes 688136 | tf_op jit(solution)/shard_map/ppermute | solution.py:287
  21.5 10.3 %collective-permute-start.3 = (bf16[448,256]{1,0:T(8,128)(2,1)S(1)}, bf16[448,256]{1,0:T(8,128)(2,1)S(1)}, u32[]{:S(2)}, u32[]{:S(2)}) collective-permute-start(bf16[448,256]{1,0:T(8,128)(2,1)S(1)} %collective-permute-done.1.refs_2_.refs_1_), channel_id=1, source_target_pairs={{0,1},{1,0},{2,3},{3,2},{4,5},{5,4},{6,7},{7,6},{8,9},{9,8},{10,11... | collective-permute-start | bytes 688136 | tf_op jit(solution)/shard_map/ppermute | solution.py:287
  26.3 10.6 %collective-permute-start.6 = (bf16[3,2,128,128]{3,2,1,0:T(8,128)(2,1)S(1)}, bf16[3,2,128,128]{3,2,1,0:T(8,128)(2,1)S(1)}, u32[]{:S(2)}, u32[]{:S(2)}) collective-permute-start(bf16[3,2,128,128]{3,2,1,0:T(8,128)(2,1)S(1)} %get-tuple-element.33), channel_id=1, source_target_pairs={{0,8},{8,0},{1,9},{9,1},{2,10},{10,2},{3,11},{11,3},{4,12},{12,4},... | collective-permute-start | bytes 589832 | tf_op jit(solution)/shard_map/ppermute | solution.py:293
  32.3 5.5 %collective-permute-start.7 = (bf16[2,2,128,128]{3,2,1,0:T(8,128)(2,1)S(1)}, bf16[2,2,128,128]{3,2,1,0:T(8,128)(2,1)S(1)}, u32[]{:S(2)}, u32[]{:S(2)}) collective-permute-start(bf16[2,2,128,128]{3,2,1,0:T(8,128)(2,1)S(1)} %get-tuple-element.34), channel_id=1, source_target_pairs={{0,8},{8,0},{1,9},{9,1},{2,10},{10,2},{3,11},{11,3},{4,12},{12,4},... | collective-permute-start | bytes 393224 | tf_op jit(solution)/shard_map/ppermute | solution.py:293
  38.6 25.6 %all-to-all-start = ((bf16[32,40,128]{2,1,0:T(8,128)(2,1)}), bf16[32,40,128]{2,1,0:T(8,128)(2,1)S(1)}, u32[]{:S(2)}, u32[]{:S(2)}) async-start(bf16[32,40,128]{2,1,0:T(8,128)(2,1)} %sum_cores.1), calls=%async_computation | async-start | bytes 655360 | tf_op jit(solution)/shard_map/all_to_all | solution.py:312
  51.4 24.3 %collective-permute-start.8 = (bf16[896,256]{1,0:T(8,128)(2,1)S(1)}, bf16[896,256]{1,0:T(8,128)(2,1)S(1)}, u32[]{:S(2)}, u32[]{:S(2)}) collective-permute-start(bf16[896,256]{1,0:T(8,128)(2,1)S(1)} %collective-permute-done.5.refs_5_.refs_6_), channel_id=1, source_target_pairs={{0,1},{1,0},{2,3},{3,2},{4,5},{5,4},{6,7},{7,6},{8,9},{9,8},{10,11... | collective-permute-start | bytes 1376264 | tf_op jit(solution)/shard_map/ppermute | solution.py:287
  53.4 22.4 %collective-permute-start.9 = (bf16[448,256]{1,0:T(8,128)(2,1)S(1)}, bf16[448,256]{1,0:T(8,128)(2,1)S(1)}, u32[]{:S(2)}, u32[]{:S(2)}) collective-permute-start(bf16[448,256]{1,0:T(8,128)(2,1)S(1)} %collective-permute-done.3.refs_3_.refs_4_), channel_id=1, source_target_pairs={{0,7},{1,2},{2,1},{3,4},{4,3},{5,6},{6,5},{7,0},{8,15},{9,10},{10,... | collective-permute-start | bytes 688136 | tf_op jit(solution)/shard_map/ppermute | solution.py:290
  57.4 18.3 %collective-permute-start.10 = (bf16[448,256]{1,0:T(8,128)(2,1)S(1)}, bf16[448,256]{1,0:T(8,128)(2,1)}, u32[]{:S(2)}, u32[]{:S(2)}) collective-permute-start(bf16[448,256]{1,0:T(8,128)(2,1)S(1)} %collective-permute-done.4.refs_4_.refs_5_), channel_id=1, source_target_pairs={{0,7},{1,2},{2,1},{3,4},{4,3},{5,6},{6,5},{7,0},{8,15},{9,10},{10,... | collective-permute-start | bytes 688136 | tf_op jit(solution)/shard_map/ppermute | solution.py:290
  75.7 18.6 %all-to-all-start.2 = ((bf16[32,64,128]{2,1,0:T(8,128)(2,1)}), bf16[32,64,128]{2,1,0:T(8,128)(2,1)S(1)}, u32[]{:S(2)}, u32[]{:S(2)}) async-start(bf16[32,64,128]{2,1,0:T(8,128)(2,1)} %amplitude_copies.1), calls=%async_computation.2 | async-start | bytes 1048576 | tf_op jit(solution)/shard_map/all_to_all | solution.py:318
  81.2 8.3 %collective-permute-start.11 = (bf16[448,256]{1,0:T(8,128)(2,1)S(1)}, bf16[448,256]{1,0:T(8,128)(2,1)S(1)}, u32[]{:S(2)}, u32[]{:S(2)}) collective-permute-start(bf16[448,256]{1,0:T(8,128)(2,1)S(1)} %slice.11), channel_id=1, source_target_pairs={{0,7},{1,2},{2,1},{3,4},{4,3},{5,6},{6,5},{7,0},{8,15},{9,10},{10,... | collective-permute-start | bytes 688136 | tf_op jit(solution)/shard_map/ppermute | solution.py:290
  83.3 7.3 %collective-permute-start.12 = (bf16[448,256]{1,0:T(8,128)(2,1)}, bf16[448,256]{1,0:T(8,128)(2,1)S(1)}, u32[]{:S(2)}, u32[]{:S(2)}) collective-permute-start(bf16[448,256]{1,0:T(8,128)(2,1)} %collective-permute-done.10.refs_1_), channel_id=1, source_target_pairs={{0,1},{1,0},{2,3},{3,2},{4,5},{5,4},{6,7},{7,6},{8,9},{9,8},{10,11... | collective-permute-start | bytes 688136 | tf_op jit(solution)/shard_map/ppermute | solution.py:287
  89.4 0.7 copy-start.1
  90.6 0.7 copy-start.3
  94.4 9.3 %copy-start.2 = (bf16[448,256]{1,0:T(8,128)(2,1)S(1)}, bf16[448,256]{1,0:T(8,128)(2,1)}, u32[]{:S(2)}) copy-start(bf16[448,256]{1,0:T(8,128)(2,1)} %copy-done.1) | copy-start | bytes 688132
  94.4 9.3 %copy-start.4 = (bf16[448,256]{1,0:T(8,128)(2,1)S(1)}, bf16[448,256]{1,0:T(8,128)(2,1)}, u32[]{:S(2)}) copy-start(bf16[448,256]{1,0:T(8,128)(2,1)} %copy-done.3) | copy-start | bytes 688132
  94.4 9.3 %collective-permute-start.13 = (bf16[32,64,128]{2,1,0:T(8,128)(2,1)S(1)}, bf16[32,64,128]{2,1,0:T(8,128)(2,1)S(1)}, u32[]{:S(2)}, u32[]{:S(2)}) collective-permute-start(bf16[32,64,128]{2,1,0:T(8,128)(2,1)S(1)} %all-to-all-done.2.mine_ref), channel_id=1, source_target_pairs={{0,8},{8,0},{1,9},{9,1},{2,10},{10,2},{3,11},{11,3},{4,12},{12,4},... | collective-permute-start | bytes 1572872 | tf_op jit(solution)/shard_map/ppermute | solution.py:293

commit v24 on v23

--- a/solution.py
+++ b/solution.py
@@ -308,15 +308,16 @@
     summed = sum_cores((early, late), (got_early, got_late))
 
     summed, b2, a2 = lax.optimization_barrier((summed, block["B", 2], block["A", 2]))
-    a3, b3 = swap_a(b2[0]), [swap_b(part) for part in a2]
+    a3, b3 = swap_a(b2[0]), [None, swap_b(a2[1])]
     parts = lax.all_to_all(summed, ("z", "x"), 0, 0)
     received = lax.all_to_all(amplitude_sends(parts, denominator), "pair", 0, 0)
     copies = amplitude_copies(received)
 
-    copies, a3, b3 = lax.optimization_barrier((copies, a3, b3))
+    copies, a3, b3[1], a2 = lax.optimization_barrier((copies, a3, b3[1], a2))
+    b3[0] = swap_b(a2[0])
     b4 = [swap_b(a3[:half]), swap_a(b3[1])]
     mine = lax.all_to_all(copies, ("z", "x"), 0, 0)
-    mine, b4 = lax.optimization_barrier((mine, b4))
+    mine, b4, b3 = lax.optimization_barrier((mine, b4, b3))
     block.update({("B", 2): b2, ("A", 2): a2, ("A", 3): [a3], ("B", 3): b3, ("B", 4): b4})
     theirs = swap_cores(mine)
     own, near = own_half(mine, scales, b3)

time: 106 us -> 106 us (level)
  local copies, waits for them, and re-layouts: 2.52 us -> 4.16 us
  waiting for transfers between devices: 12.7 us -> 11.5 us
    all_to_all x1, waiting for transfers between devices: 3.04 us -> 0.01 us  [body(): mine = lax.all_to_all(copies, ('z', 'x'), 0, 0)]
    all_to_all x1, waiting for transfers between devices: 4.32 us -> 6.79 us  [body(): parts = lax.all_to_all(summed, ('z', 'x'), 0, 0)]
    ppermute x6, starting transfers between devices: 22.9 us -> 24.7 us  [swap_b(): return lax.ppermute(x, 'pair', SWAP_B)]
    unnamed x20 -> x24, local copies, waits for them, and re-layouts: 1.43 us -> 3.06 us
    ppermute x3, starting transfers between devices: 17.8 us -> 16.7 us  [swap_cores(): return lax.ppermute(x, 'core', SWAP_CORES)]
  transfers between devices with their start and end apart: 16 -> 16, of which waited for: 6 -> 4; matrix products, arithmetic and copies ran while one was open for 1% -> 1% of each run, Pallas kernels for 4% -> 3%
where the time goes in v24:
time: 106 us; the launch traced here: 105 us
  starting transfers between devices  72.3 us (68%)
  waiting for transfers between devices  11.5 us (11%)
  blocking collectives  10.6 us (10%)
  Pallas kernels  6.44 us (6%)
  local copies, waits for them, and re-layouts  4.16 us (4%)
    ppermute x6, starting transfers between devices, swap_b(): return lax.ppermute(x, 'pair', SWAP_B)  24.7 us
    ppermute x3, starting transfers between devices, swap_cores(): return lax.ppermute(x, 'core', SWAP_CORES)  16.7 us
    ppermute x5, starting transfers between devices, swap_a(): return lax.ppermute(x, 'pair', SWAP_A)  13.3 us
    all_to_all x1, starting transfers between devices, body(): parts = lax.all_to_all(summed, ('z', 'x'), 0, 0)  12.9 us
    all_to_all x1, blocking collectives, body(): received = lax.all_to_all(amplitude_sends(parts, denominator), 'pair', 0, 0)  10.6 us
    all_to_all x1, waiting for transfers between devices, body(): parts = lax.all_to_all(summed, ('z', 'x'), 0, 0)  6.79 us
    all_to_all x1, starting transfers between devices, body(): mine = lax.all_to_all(copies, ('z', 'x'), 0, 0)  4.76 us
    unnamed x24, local copies, waits for them, and re-layouts  3.06 us
  transfers between devices with their start and end apart: 16, of which 4 were waited for; matrix products, arithmetic and copies ran while one was open for 1% of the time, Pallas kernels for 3%

profile of v24, /device:TPU:1, one launch (start us, length us, event | category | flops | bytes accessed | tf_op | source)
XLA Modules:
  0.0 105.4 jit_solution(14119001384169709349)
XLA Ops:
  0.0 0.0 copy-start
  0.0 0.0 copy-start.7
  0.0 4.2 %collective-permute-start = (bf16[896,256]{1,0:T(8,128)(2,1)}, bf16[896,256]{1,0:T(8,128)(2,1)S(1)}, u32[]{:S(2)}, u32[]{:S(2)}) collective-permute-start(bf16[896,256]{1,0:T(8,128)(2,1)} %refs_0_.3), channel_id=1, source_target_pairs={{0,1},{1,0},{2,3},{3,2},{4,5},{5,4},{6,7},{7,6},{8,9},{9,8},{10,11... | collective-permute-start | bytes 1376264 | tf_op jit(solution)/shard_map/ppermute | solution.py:287
  4.2 1.1 %fusion = (bf16[448,256]{1,0:T(8,128)(2,1)S(1)}, bf16[448,256]{1,0:T(8,128)(2,1)S(1)}) fusion(bf16[896,256]{1,0:T(8,128)(2,1)} %refs_0_.3), kind=kLoop, calls=%fused_computation | loop fusion | bytes 917504 | tf_op jit(solution)/shard_map/slice | solution.py:298
  5.2 4.9 %collective-permute-start.2 = (bf16[448,256]{1,0:T(8,128)(2,1)S(1)}, bf16[448,256]{1,0:T(8,128)(2,1)S(1)}, u32[]{:S(2)}, u32[]{:S(2)}) collective-permute-start(bf16[448,256]{1,0:T(8,128)(2,1)S(1)} %get-tuple-element.57), channel_id=1, source_target_pairs={{0,7},{1,2},{2,1},{3,4},{4,3},{5,6},{6,5},{7,0},{8,15},{9,10},{10,... | collective-permute-start | bytes 688136 | tf_op jit(solution)/shard_map/ppermute | solution.py:290
  10.1 0.0 copy-start.11
  10.1 0.0 copy-start.8
  10.2 0.0 copy-start.9
  10.2 0.0 copy-start.10
  10.2 2.1 %collective-permute-start.1 = (bf16[448,256]{1,0:T(8,128)(2,1)S(1)}, bf16[448,256]{1,0:T(8,128)(2,1)S(1)}, u32[]{:S(2)}, u32[]{:S(2)}) collective-permute-start(bf16[448,256]{1,0:T(8,128)(2,1)S(1)} %get-tuple-element.58), channel_id=1, source_target_pairs={{0,7},{1,2},{2,1},{3,4},{4,3},{5,6},{6,5},{7,0},{8,15},{9,10},{10,... | collective-permute-start | bytes 688136 | tf_op jit(solution)/shard_map/ppermute | solution.py:290
  12.2 0.0 collective-permute-done.refs_1_.refs_0_
  12.2 7.3 %collective-permute-start.5 = (bf16[896,256]{1,0:T(8,128)(2,1)S(1)}, bf16[896,256]{1,0:T(8,128)(2,1)S(1)}, u32[]{:S(2)}, u32[]{:S(2)}) collective-permute-start(bf16[896,256]{1,0:T(8,128)(2,1)S(1)} %collective-permute-done.refs_1_.refs_0_), channel_id=1, source_target_pairs={{0,7},{1,2},{2,1},{3,4},{4,3},{5,6},{6,5},{7,0},{8,15},{9,10},{10,... | collective-permute-start | bytes 1376264 | tf_op jit(solution)/shard_map/ppermute | solution.py:290
  19.5 0.0 collective-permute-done.2.refs_3_.refs_2_
  19.5 1.9 %collective-permute-start.4 = (bf16[448,256]{1,0:T(8,128)(2,1)S(1)}, bf16[448,256]{1,0:T(8,128)(2,1)S(1)}, u32[]{:S(2)}, u32[]{:S(2)}) collective-permute-start(bf16[448,256]{1,0:T(8,128)(2,1)S(1)} %collective-permute-done.2.refs_3_.refs_2_), channel_id=1, source_target_pairs={{0,1},{1,0},{2,3},{3,2},{4,5},{5,4},{6,7},{7,6},{8,9},{9,8},{10,11... | collective-permute-start | bytes 688136 | tf_op jit(solution)/shard_map/ppermute | solution.py:287
  21.5 0.0 collective-permute-done.1.refs_2_.refs_1_
  21.5 3.4 %collective-permute-start.3 = (bf16[448,256]{1,0:T(8,128)(2,1)S(1)}, bf16[448,256]{1,0:T(8,128)(2,1)S(1)}, u32[]{:S(2)}, u32[]{:S(2)}) collective-permute-start(bf16[448,256]{1,0:T(8,128)(2,1)S(1)} %collective-permute-done.1.refs_2_.refs_1_), channel_id=1, source_target_pairs={{0,1},{1,0},{2,3},{3,2},{4,5},{5,4},{6,7},{7,6},{8,9},{9,8},{10,11... | collective-permute-start | bytes 688136 | tf_op jit(solution)/shard_map/ppermute | solution.py:287
  24.9 0.0 copy-done.7
  24.9 0.0 copy-done.11
  24.9 0.0 copy-done.8
  24.9 0.0 copy-done.9
  24.9 0.0 copy-done.10
  24.9 0.7 tables.1
  25.6 0.0 copy-done
  25.6 0.6 coulomb_pairs.2
  26.3 5.5 %collective-permute-start.6 = (bf16[3,2,128,128]{3,2,1,0:T(8,128)(2,1)S(1)}, bf16[3,2,128,128]{3,2,1,0:T(8,128)(2,1)S(1)}, u32[]{:S(2)}, u32[]{:S(2)}) collective-permute-start(bf16[3,2,128,128]{3,2,1,0:T(8,128)(2,1)S(1)} %get-tuple-element.36), channel_id=1, source_target_pairs={{0,8},{8,0},{1,9},{9,1},{2,10},{10,2},{3,11},{11,3},{4,12},{12,4},... | collective-permute-start | bytes 589832 | tf_op jit(solution)/shard_map/ppermute | solution.py:293
  31.8 0.0 collective-permute-done.4.refs_4_.refs_5_
  31.8 0.0 collective-permute-done.3.refs_3_.refs_4_
  31.8 0.0 collective-permute-done.5.refs_5_.refs_6_
  31.8 0.5 coulomb_pairs.3
  32.3 4.5 %collective-permute-start.7 = (bf16[2,2,128,128]{3,2,1,0:T(8,128)(2,1)S(1)}, bf16[2,2,128,128]{3,2,1,0:T(8,128)(2,1)S(1)}, u32[]{:S(2)}, u32[]{:S(2)}) collective-permute-start(bf16[2,2,128,128]{3,2,1,0:T(8,128)(2,1)S(1)} %get-tuple-element.37), channel_id=1, source_target_pairs={{0,8},{8,0},{1,9},{9,1},{2,10},{10,2},{3,11},{11,3},{4,12},{12,4},... | collective-permute-start | bytes 393224 | tf_op jit(solution)/shard_map/ppermute | solution.py:293
  36.8 0.0 collective-permute-done.6.refs_2_
  36.8 1.0 collective-permute-done.7.refs_3_
  37.8 0.8 sum_cores.1
  38.6 12.9 %all-to-all-start = ((bf16[32,40,128]{2,1,0:T(8,128)(2,1)}), bf16[32,40,128]{2,1,0:T(8,128)(2,1)S(1)}, u32[]{:S(2)}, u32[]{:S(2)}) async-start(bf16[32,40,128]{2,1,0:T(8,128)(2,1)} %sum_cores.1), calls=%async_computation | async-start | bytes 655360 | tf_op jit(solution)/shard_map/all_to_all | solution.py:312
  51.4 1.9 %collective-permute-start.8 = (bf16[896,256]{1,0:T(8,128)(2,1)S(1)}, bf16[896,256]{1,0:T(8,128)(2,1)S(1)}, u32[]{:S(2)}, u32[]{:S(2)}) collective-permute-start(bf16[896,256]{1,0:T(8,128)(2,1)S(1)} %collective-permute-done.5.refs_5_.refs_6_), channel_id=1, source_target_pairs={{0,1},{1,0},{2,3},{3,2},{4,5},{5,4},{6,7},{7,6},{8,9},{9,8},{10,11... | collective-permute-start | bytes 1376264 | tf_op jit(solution)/shard_map/ppermute | solution.py:287
  53.4 4.0 %collective-permute-start.9 = (bf16[448,256]{1,0:T(8,128)(2,1)S(1)}, bf16[448,256]{1,0:T(8,128)(2,1)S(1)}, u32[]{:S(2)}, u32[]{:S(2)}) collective-permute-start(bf16[448,256]{1,0:T(8,128)(2,1)S(1)} %collective-permute-done.4.refs_4_.refs_5_), channel_id=1, source_target_pairs={{0,7},{1,2},{2,1},{3,4},{4,3},{5,6},{6,5},{7,0},{8,15},{9,10},{10,... | collective-permute-start | bytes 688136 | tf_op jit(solution)/shard_map/ppermute | solution.py:290
  57.4 6.8 %all-to-all-done.parts_ref = bf16[32,40,128]{2,1,0:T(8,128)(2,1)S(1)} async-done(((bf16[32,40,128]{2,1,0:T(8,128)(2,1)}), bf16[32,40,128]{2,1,0:T(8,128)(2,1)S(1)}, u32[]{:S(2)}, u32[]{:S(2)}) %all-to-all-start) | async-done | bytes 327712 | tf_op jit(solution)/shard_map/all_to_all | solution.py:312
  64.2 10.6 %all_to_all.15.received_ref = bf16[8,16,128]{2,1,0:T(8,128)(2,1)S(1)} all-to-all(bf16[8,16,128]{2,1,0:T(8,128)(2,1)S(1)} %amplitude_sends.1), channel_id=1, replica_groups=mesh['x'=4,'z'=8,'core'=2,'pair'=8] {'pair'}, dimensions={0} | all-to-all | bytes 65536 | tf_op jit(solution)/shard_map/all_to_all | solution.py:313
  74.8 0.9 amplitude_copies.1
  75.7 0.0 collective-permute-done.9.refs_1_
  75.7 0.0 collective-permute-done.8.refs_7_
  75.7 4.8 %all-to-all-start.2 = ((bf16[32,64,128]{2,1,0:T(8,128)(2,1)}), bf16[32,64,128]{2,1,0:T(8,128)(2,1)S(1)}, u32[]{:S(2)}, u32[]{:S(2)}) async-start(bf16[32,64,128]{2,1,0:T(8,128)(2,1)} %amplitude_copies.1), calls=%async_computation.2 | async-start | bytes 1048576 | tf_op jit(solution)/shard_map/all_to_all | solution.py:319
  80.5 2.0 %collective-permute-start.10 = (bf16[448,256]{1,0:T(8,128)(2,1)S(1)}, bf16[448,256]{1,0:T(8,128)(2,1)S(1)}, u32[]{:S(2)}, u32[]{:S(2)}) collective-permute-start(bf16[448,256]{1,0:T(8,128)(2,1)S(1)} %slice.11), channel_id=1, source_target_pairs={{0,7},{1,2},{2,1},{3,4},{4,3},{5,6},{6,5},{7,0},{8,15},{9,10},{10,... | collective-permute-start | bytes 688136 | tf_op jit(solution)/shard_map/ppermute | solution.py:290
  82.6 4.5 %collective-permute-start.12 = (bf16[448,256]{1,0:T(8,128)(2,1)S(1)}, bf16[448,256]{1,0:T(8,128)(2,1)S(1)}, u32[]{:S(2)}, u32[]{:S(2)}) collective-permute-start(bf16[448,256]{1,0:T(8,128)(2,1)S(1)} %collective-permute-done.3.refs_3_.refs_4_), channel_id=1, source_target_pairs={{0,7},{1,2},{2,1},{3,4},{4,3},{5,6},{6,5},{7,0},{8,15},{9,10},{10,... | collective-permute-start | bytes 688136 | tf_op jit(solution)/shard_map/ppermute | solution.py:290
  87.0 1.9 %collective-permute-start.11 = (bf16[448,256]{1,0:T(8,128)(2,1)S(1)}, bf16[448,256]{1,0:T(8,128)(2,1)S(1)}, u32[]{:S(2)}, u32[]{:S(2)}) collective-permute-start(bf16[448,256]{1,0:T(8,128)(2,1)S(1)} %collective-permute-done.9.refs_1_), channel_id=1, source_target_pairs={{0,1},{1,0},{2,3},{3,2},{4,5},{5,4},{6,7},{7,6},{8,9},{9,8},{10,11... | collective-permute-start | bytes 688136 | tf_op jit(solution)/shard_map/ppermute | solution.py:287
  89.0 0.0 collective-permute-done.10.refs_9_
  89.0 0.0 copy-start.1
  89.0 0.7 copy-done.1
  89.7 2.9 %collective-permute-done.12.refs_0_ = bf16[448,256]{1,0:T(8,128)(2,1)S(1)} collective-permute-done((bf16[448,256]{1,0:T(8,128)(2,1)S(1)}, bf16[448,256]{1,0:T(8,128)(2,1)S(1)}, u32[]{:S(2)}, u32[]{:S(2)}) %collective-permute-start.12) | collective-permute-done | bytes 229408 | tf_op jit(solution)/shard_map/ppermute | solution.py:290
  92.6 0.7 copy-done.5
  93.3 0.8 collective-permute-done.11.refs_10_
  94.1 0.0 copy-start.3
  94.1 0.7 copy-done.3
  94.8 0.0 all-to-all-done.2.mine_ref
  94.8 0.0 copy-start.2
  94.8 0.0 copy-start.4
  94.8 6.7 %collective-permute-start.13 = (bf16[32,64,128]{2,1,0:T(8,128)(2,1)S(1)}, bf16[32,64,128]{2,1,0:T(8,128)(2,1)S(1)}, u32[]{:S(2)}, u32[]{:S(2)}) collective-permute-start(bf16[32,64,128]{2,1,0:T(8,128)(2,1)S(1)} %all-to-all-done.2.mine_ref), channel_id=1, source_target_pairs={{0,8},{8,0},{1,9},{9,1},{2,10},{10,2},{3,11},{11,3},{4,12},{12,4},... | collective-permute-start | bytes 1572872 | tf_op jit(solution)/shard_map/ppermute | solution.py:293
  101.5 0.0 copy-start.6
  101.5 0.9 copy-done.6
  102.5 0.8 own_half.1
  103.3 0.0 collective-permute-done.13.refs_12_
  103.3 0.0 copy-done.2
  103.3 0.0 copy-done.4
  103.3 2.1 %gamma_rows.1 = (bf16[896,256]{1,0:T(8,128)(2,1)}, bf16[8,256,256]{2,1,0:T(8,128)(2,1)S(1)}) custom-call(bf16[896,256]{1,0:T(8,128)(2,1)S(1)} %copy-done, bf16[896,256]{1,0:T(8,128)(2,1)S(1)} %collective-permute-done.refs_1_.refs_0_, bf16[448,256]{1,0:T(8,128)(2,1)S(1)} %collective-permute-done.1.refs_2_.refs_1_, ...), custom_call_target="tpu_custom_call", output_to_operand_aliasing={{1}: (11, {})} | custom-call | tf_op jit(solution)/shard_map/gamma_rows/pallas_call | solution.py:267
  (3 shorter events, 0.1 us)
Async XLA Ops:
  0.0 25.6 %copy-start = (bf16[896,256]{1,0:T(8,128)(2,1)S(1)}, bf16[896,256]{1,0:T(8,128)(2,1)}, u32[]{:S(2)}) copy-start(bf16[896,256]{1,0:T(8,128)(2,1)} %refs_0_.3) | copy-start | bytes 1376260
  0.0 24.9 %copy-start.7 = (f32[20096]{0:T(1024)S(1)}, f32[20096]{0:T(1024)}, u32[]{:S(2)}) copy-start(f32[20096]{0:T(1024)} %param.8) | copy-start | bytes 241156
  0.0 12.2 %collective-permute-start = (bf16[896,256]{1,0:T(8,128)(2,1)}, bf16[896,256]{1,0:T(8,128)(2,1)S(1)}, u32[]{:S(2)}, u32[]{:S(2)}) collective-permute-start(bf16[896,256]{1,0:T(8,128)(2,1)} %refs_0_.3), channel_id=1, source_target_pairs={{0,1},{1,0},{2,3},{3,2},{4,5},{5,4},{6,7},{7,6},{8,9},{9,8},{10,11... | collective-permute-start | bytes 1376264 | tf_op jit(solution)/shard_map/ppermute | solution.py:287
  5.2 14.3 %collective-permute-start.2 = (bf16[448,256]{1,0:T(8,128)(2,1)S(1)}, bf16[448,256]{1,0:T(8,128)(2,1)S(1)}, u32[]{:S(2)}, u32[]{:S(2)}) collective-permute-start(bf16[448,256]{1,0:T(8,128)(2,1)S(1)} %get-tuple-element.57), channel_id=1, source_target_pairs={{0,7},{1,2},{2,1},{3,4},{4,3},{5,6},{6,5},{7,0},{8,15},{9,10},{10,... | collective-permute-start | bytes 688136 | tf_op jit(solution)/shard_map/ppermute | solution.py:290
  10.1 14.7 %copy-start.11 = (s32[16]{0:T(128)S(1)}, s32[16]{0:T(128)}, u32[]{:S(2)}) copy-start(s32[16]{0:T(128)} %exponent.1) | copy-start | bytes 196
  10.1 14.7 %copy-start.8 = (f32[64]{0:T(128)S(1)}, f32[64]{0:T(128)}, u32[]{:S(2)}) copy-start(f32[64]{0:T(128)} %occupied.1) | copy-start | bytes 772
  10.2 14.7 %copy-start.9 = (s32[16]{0:T(128)S(1)}, s32[16]{0:T(128)}, u32[]{:S(2)}) copy-start(s32[16]{0:T(128)} %occupied_of.1) | copy-start | bytes 196
  10.2 14.7 %copy-start.10 = (s32[16]{0:T(128)S(1)}, s32[16]{0:T(128)}, u32[]{:S(2)}) copy-start(s32[16]{0:T(128)} %virtual_of.1) | copy-start | bytes 196
  10.2 11.3 %collective-permute-start.1 = (bf16[448,256]{1,0:T(8,128)(2,1)S(1)}, bf16[448,256]{1,0:T(8,128)(2,1)S(1)}, u32[]{:S(2)}, u32[]{:S(2)}) collective-permute-start(bf16[448,256]{1,0:T(8,128)(2,1)S(1)} %get-tuple-element.58), channel_id=1, source_target_pairs={{0,7},{1,2},{2,1},{3,4},{4,3},{5,6},{6,5},{7,0},{8,15},{9,10},{10,... | collective-permute-start | bytes 688136 | tf_op jit(solution)/shard_map/ppermute | solution.py:290
  12.2 19.5 %collective-permute-start.5 = (bf16[896,256]{1,0:T(8,128)(2,1)S(1)}, bf16[896,256]{1,0:T(8,128)(2,1)S(1)}, u32[]{:S(2)}, u32[]{:S(2)}) collective-permute-start(bf16[896,256]{1,0:T(8,128)(2,1)S(1)} %collective-permute-done.refs_1_.refs_0_), channel_id=1, source_target_pairs={{0,7},{1,2},{2,1},{3,4},{4,3},{5,6},{6,5},{7,0},{8,15},{9,10},{10,... | collective-permute-start | bytes 1376264 | tf_op jit(solution)/shard_map/ppermute | solution.py:290
  19.5 12.2 %collective-permute-start.4 = (bf16[448,256]{1,0:T(8,128)(2,1)S(1)}, bf16[448,256]{1,0:T(8,128)(2,1)S(1)}, u32[]{:S(2)}, u32[]{:S(2)}) collective-permute-start(bf16[448,256]{1,0:T(8,128)(2,1)S(1)} %collective-permute-done.2.refs_3_.refs_2_), channel_id=1, source_target_pairs={{0,1},{1,0},{2,3},{3,2},{4,5},{5,4},{6,7},{7,6},{8,9},{9,8},{10,11... | collective-permute-start | bytes 688136 | tf_op jit(solution)/shard_map/ppermute | solution.py:287
  21.5 10.3 %collective-permute-start.3 = (bf16[448,256]{1,0:T(8,128)(2,1)S(1)}, bf16[448,256]{1,0:T(8,128)(2,1)S(1)}, u32[]{:S(2)}, u32[]{:S(2)}) collective-permute-start(bf16[448,256]{1,0:T(8,128)(2,1)S(1)} %collective-permute-done.1.refs_2_.refs_1_), channel_id=1, source_target_pairs={{0,1},{1,0},{2,3},{3,2},{4,5},{5,4},{6,7},{7,6},{8,9},{9,8},{10,11... | collective-permute-start | bytes 688136 | tf_op jit(solution)/shard_map/ppermute | solution.py:287
  26.3 10.6 %collective-permute-start.6 = (bf16[3,2,128,128]{3,2,1,0:T(8,128)(2,1)S(1)}, bf16[3,2,128,128]{3,2,1,0:T(8,128)(2,1)S(1)}, u32[]{:S(2)}, u32[]{:S(2)}) collective-permute-start(bf16[3,2,128,128]{3,2,1,0:T(8,128)(2,1)S(1)} %get-tuple-element.36), channel_id=1, source_target_pairs={{0,8},{8,0},{1,9},{9,1},{2,10},{10,2},{3,11},{11,3},{4,12},{12,4},... | collective-permute-start | bytes 589832 | tf_op jit(solution)/shard_map/ppermute | solution.py:293
  32.3 5.5 %collective-permute-start.7 = (bf16[2,2,128,128]{3,2,1,0:T(8,128)(2,1)S(1)}, bf16[2,2,128,128]{3,2,1,0:T(8,128)(2,1)S(1)}, u32[]{:S(2)}, u32[]{:S(2)}) collective-permute-start(bf16[2,2,128,128]{3,2,1,0:T(8,128)(2,1)S(1)} %get-tuple-element.37), channel_id=1, source_target_pairs={{0,8},{8,0},{1,9},{9,1},{2,10},{10,2},{3,11},{11,3},{4,12},{12,4},... | collective-permute-start | bytes 393224 | tf_op jit(solution)/shard_map/ppermute | solution.py:293
  38.6 25.6 %all-to-all-start = ((bf16[32,40,128]{2,1,0:T(8,128)(2,1)}), bf16[32,40,128]{2,1,0:T(8,128)(2,1)S(1)}, u32[]{:S(2)}, u32[]{:S(2)}) async-start(bf16[32,40,128]{2,1,0:T(8,128)(2,1)} %sum_cores.1), calls=%async_computation | async-start | bytes 655360 | tf_op jit(solution)/shard_map/all_to_all | solution.py:312
  51.4 24.3 %collective-permute-start.8 = (bf16[896,256]{1,0:T(8,128)(2,1)S(1)}, bf16[896,256]{1,0:T(8,128)(2,1)S(1)}, u32[]{:S(2)}, u32[]{:S(2)}) collective-permute-start(bf16[896,256]{1,0:T(8,128)(2,1)S(1)} %collective-permute-done.5.refs_5_.refs_6_), channel_id=1, source_target_pairs={{0,1},{1,0},{2,3},{3,2},{4,5},{5,4},{6,7},{7,6},{8,9},{9,8},{10,11... | collective-permute-start | bytes 1376264 | tf_op jit(solution)/shard_map/ppermute | solution.py:287
  53.4 22.4 %collective-permute-start.9 = (bf16[448,256]{1,0:T(8,128)(2,1)S(1)}, bf16[448,256]{1,0:T(8,128)(2,1)S(1)}, u32[]{:S(2)}, u32[]{:S(2)}) collective-permute-start(bf16[448,256]{1,0:T(8,128)(2,1)S(1)} %collective-permute-done.4.refs_4_.refs_5_), channel_id=1, source_target_pairs={{0,7},{1,2},{2,1},{3,4},{4,3},{5,6},{6,5},{7,0},{8,15},{9,10},{10,... | collective-permute-start | bytes 688136 | tf_op jit(solution)/shard_map/ppermute | solution.py:290
  75.7 19.1 %all-to-all-start.2 = ((bf16[32,64,128]{2,1,0:T(8,128)(2,1)}), bf16[32,64,128]{2,1,0:T(8,128)(2,1)S(1)}, u32[]{:S(2)}, u32[]{:S(2)}) async-start(bf16[32,64,128]{2,1,0:T(8,128)(2,1)} %amplitude_copies.1), calls=%async_computation.2 | async-start | bytes 1048576 | tf_op jit(solution)/shard_map/all_to_all | solution.py:319
  80.5 8.4 %collective-permute-start.10 = (bf16[448,256]{1,0:T(8,128)(2,1)S(1)}, bf16[448,256]{1,0:T(8,128)(2,1)S(1)}, u32[]{:S(2)}, u32[]{:S(2)}) collective-permute-start(bf16[448,256]{1,0:T(8,128)(2,1)S(1)} %slice.11), channel_id=1, source_target_pairs={{0,7},{1,2},{2,1},{3,4},{4,3},{5,6},{6,5},{7,0},{8,15},{9,10},{10,... | collective-permute-start | bytes 688136 | tf_op jit(solution)/shard_map/ppermute | solution.py:290
  82.6 10.0 %collective-permute-start.12 = (bf16[448,256]{1,0:T(8,128)(2,1)S(1)}, bf16[448,256]{1,0:T(8,128)(2,1)S(1)}, u32[]{:S(2)}, u32[]{:S(2)}) collective-permute-start(bf16[448,256]{1,0:T(8,128)(2,1)S(1)} %collective-permute-done.3.refs_3_.refs_4_), channel_id=1, source_target_pairs={{0,7},{1,2},{2,1},{3,4},{4,3},{5,6},{6,5},{7,0},{8,15},{9,10},{10,... | collective-permute-start | bytes 688136 | tf_op jit(solution)/shard_map/ppermute | solution.py:290
  87.0 7.1 %collective-permute-start.11 = (bf16[448,256]{1,0:T(8,128)(2,1)S(1)}, bf16[448,256]{1,0:T(8,128)(2,1)S(1)}, u32[]{:S(2)}, u32[]{:S(2)}) collective-permute-start(bf16[448,256]{1,0:T(8,128)(2,1)S(1)} %collective-permute-done.9.refs_1_), channel_id=1, source_target_pairs={{0,1},{1,0},{2,3},{3,2},{4,5},{5,4},{6,7},{7,6},{8,9},{9,8},{10,11... | collective-permute-start | bytes 688136 | tf_op jit(solution)/shard_map/ppermute | solution.py:287
  89.0 0.7 copy-start.1
  92.6 0.7 copy-start.5
  94.1 0.7 copy-start.3
  94.8 8.5 %copy-start.2 = (bf16[448,256]{1,0:T(8,128)(2,1)S(1)}, bf16[448,256]{1,0:T(8,128)(2,1)}, u32[]{:S(2)}) copy-start(bf16[448,256]{1,0:T(8,128)(2,1)} %copy-done.1) | copy-start | bytes 688132
  94.8 8.5 %copy-start.4 = (bf16[448,256]{1,0:T(8,128)(2,1)S(1)}, bf16[448,256]{1,0:T(8,128)(2,1)}, u32[]{:S(2)}) copy-start(bf16[448,256]{1,0:T(8,128)(2,1)} %copy-done.3) | copy-start | bytes 688132
  94.8 8.5 %collective-permute-start.13 = (bf16[32,64,128]{2,1,0:T(8,128)(2,1)S(1)}, bf16[32,64,128]{2,1,0:T(8,128)(2,1)S(1)}, u32[]{:S(2)}, u32[]{:S(2)}) collective-permute-start(bf16[32,64,128]{2,1,0:T(8,128)(2,1)S(1)} %all-to-all-done.2.mine_ref), channel_id=1, source_target_pairs={{0,8},{8,0},{1,9},{9,1},{2,10},{10,2},{3,11},{11,3},{4,12},{12,4},... | collective-permute-start | bytes 1572872 | tf_op jit(solution)/shard_map/ppermute | solution.py:293
  101.5 0.9 copy-start.6
